TPU v7x, 128 devices: a whole 4x4x4 slice. The times are simulated.
128 devices in a mesh: seq: 16 (over x_hi, z, core), wshard: 8 (over y, x_lo).
Axes of the slice: x: 4 (x_hi: 2, x_lo: 2; x = x_hi * 2 + x_lo), y: 4, z: 4, core: 2. Of those that a mesh axis runs over, the one named last changes fastest.
Arguments:
- tokens: bfloat16 [8, 3584, 1024], P('wshard', 'seq'), may hold values from -6 to 6
- routes: int32 [8, 3584, 8], P('wshard', 'seq'), may hold values from 0 to 31, all different within a row; in each aligned block of 224 rows (0 to 223, 224 to 447, ..., all dimensions but the last counted through in order) at most 70 rows name the same one
- cont_lengths: int32 [8, 6], P('wshard'), may hold values from 1 to 384, 1536 in all within a row
- norm_attn: bfloat16 [1024], P(('seq', 'wshard')), may hold values from 0.3984375 to 1.59375
- w_qkv: bfloat16 [1024, 2048], P(('seq', 'wshard')), may hold values from -0.1875 to 0.1875
- w_out: bfloat16 [1024, 1024], P(('seq', 'wshard')), may hold values from -1.5 to 1.5
- w_router: bfloat16 [1024, 32], P(('seq', 'wshard')), may hold values from -0.09375 to 0.09375
- norm_ffn: bfloat16 [1024], P(('seq', 'wshard')), may hold values from 0.3984375 to 1.59375
- w_gate_up: bfloat16 [32, 1024, 1024], P('seq', 'wshard'), may hold values from -0.1875 to 0.1875
- w_down: bfloat16 [32, 512, 1024], P('seq', 'wshard'), may hold values from -0.75 to 0.75
- cotangent: bfloat16 [8, 3584, 1024], P('wshard', 'seq'), may hold values from -6 to 6
Outputs:
- output: bfloat16 [8, 3584, 1024], P('wshard', 'seq')
- grad_input: float32 [8, 3584, 1024], P('wshard', 'seq')
- grad_norm_attn: float32 [1024], P(('seq', 'wshard'))
- grad_qkv: float32 [1024, 2048], P(('seq', 'wshard'))
- grad_out: float32 [1024, 1024], P(('seq', 'wshard'))
- grad_router: float32 [1024, 32], P(('seq', 'wshard'))
- grad_norm_ffn: float32 [1024], P(('seq', 'wshard'))
- grad_gate_up: float32 [32, 1024, 1024], P('seq', 'wshard')
- grad_down: float32 [32, 512, 1024], P('seq', 'wshard')
Inputs may be any that keep to these rules, and one draw needn't show every extreme that they name: `routes`: each row names 8 different experts; in each aligned block of 224 rows (the rows of one device) no expert is named by more than 70 rows, and in some block one expert is named by exactly 70 rows. `cont_lengths`: A group's 6 lengths sum to 1536; the longest is exactly 384.
All inputs are finite; a program needn't handle non-finite values.
Results may differ from a plain program's by a relative error of at most 0.023.
Values may be sent and summed in bfloat16 or wider, within the bound.
No kernel may reach another device: no remote copies, remote signals or barrier semaphores. Data moves between devices by JAX's collectives and lax.ppermute only.
A program may use at most 128 MiB of HBM per device.

v0:
```python
import jax
import jax.numpy as jnp
from jax import lax
from jax.sharding import PartitionSpec as P

HEADS = 16
KV_HEADS = 8
HEAD_DIM = 64
EXPERTS = 32
TOPK = 8
FF = 512
PROMPT = 2048
GROUP = 3584


norm_eps = 1e-06
rope_base = 10000.0
masked_score = -1e30


def rms_norm(values, gain):
    return values * lax.rsqrt(jnp.mean(values * values, axis=-1, keepdims=True) + norm_eps) * gain


def rotary_tables(position):
    half_dim = HEAD_DIM // 2
    inverse = rope_base ** (-(jnp.arange(half_dim, dtype=jnp.float32) * 2.0) / HEAD_DIM)
    angles = position[:, None] * inverse[None, :]
    cosine = jnp.cos(angles)
    sine_table = jnp.sin(angles)
    return (
        jnp.concatenate([cosine, cosine], axis=-1),
        jnp.concatenate([sine_table, sine_table], axis=-1),
    )


def rotate(values, cosine, sine_table):
    half_dim = values.shape[-1] // 2
    turned = jnp.concatenate([-values[..., half_dim:], values[..., :half_dim]], axis=-1)
    return values * cosine[:, None, :] + turned * sine_table[:, None, :]


def group_layout(lengths):
    places = jnp.arange(GROUP, dtype=jnp.int32)
    ends = jnp.cumsum(lengths)
    starts = ends - lengths
    offset_in = places - PROMPT
    segment_id = jnp.sum((offset_in[:, None] >= ends[None, :]).astype(jnp.int32), axis=1)
    segment_hot = segment_id[:, None] == jnp.arange(lengths.shape[0], dtype=jnp.int32)[None, :]
    begin = jnp.sum(jnp.where(segment_hot, starts[None, :], 0), axis=1)
    inside = offset_in >= 0
    position = jnp.where(inside, PROMPT + offset_in - begin, places)
    segment = jnp.where(inside, segment_id, -1)
    return (places, position, segment)


def allowed_mask(query_places, query_segment, places, segment):
    causal = places[None, :] <= query_places[:, None]
    same_doc = (segment[None, :] < 0) | (segment[None, :] == query_segment[:, None])
    return causal & same_doc


def swiglu(projected_rows):
    return jax.nn.silu(projected_rows[..., :FF]) * projected_rows[..., FF:]


def local(
    tokens,
    routes,
    cont_lengths,
    norm_attn,
    w_qkv,
    w_out,
    w_router,
    norm_ffn,
    w_gate_up,
    w_down,
    cotangent,
):
    seq_count = lax.axis_size("seq")
    seq_index = lax.axis_index("seq")
    tok_dev = tokens.shape[1]
    model_width = tokens.shape[2]
    query_width = HEADS * HEAD_DIM
    kv_width = KV_HEADS * HEAD_DIM
    head_share = HEADS // KV_HEADS
    local_heads = HEADS // seq_count
    capacity = max(2, tok_dev * TOPK * 5 // (4 * EXPERTS))
    block_rows = min(512, GROUP)
    block_count = GROUP // block_rows
    score_scale = HEAD_DIM ** (-0.5)
    attn_params = (
        lax.all_gather(norm_attn, ("seq", "wshard"), axis=0, tiled=True),
        lax.all_gather(w_qkv, ("seq", "wshard"), axis=0, tiled=True),
        lax.all_gather(w_out, ("seq", "wshard"), axis=0, tiled=True),
        lax.all_gather(w_router, ("seq", "wshard"), axis=0, tiled=True),
        lax.all_gather(norm_ffn, ("seq", "wshard"), axis=0, tiled=True),
    )
    expert_params = (
        lax.all_gather(w_gate_up, "wshard", axis=1, tiled=True),
        lax.all_gather(w_down, "wshard", axis=1, tiled=True),
    )
    gain_attn = attn_params[0].astype(jnp.float32)
    weight_qkv = attn_params[1]
    weight_out = attn_params[2]
    weight_router = attn_params[3]
    gain_ffn = attn_params[4].astype(jnp.float32)
    weight_gate_up = expert_params[0]
    weight_down = expert_params[1]
    places, position, segment = group_layout(cont_lengths[0])
    local_position = lax.dynamic_slice_in_dim(position, seq_index * tok_dev, tok_dev, 0)
    cosine, sine_table = rotary_tables(local_position.astype(jnp.float32))
    inputs = tokens[0].astype(jnp.float32)
    normed = rms_norm(inputs, gain_attn).astype(jnp.bfloat16)
    projected = jnp.dot(normed, weight_qkv, preferred_element_type=jnp.float32)
    queries = projected[:, :query_width].reshape(tok_dev, HEADS, HEAD_DIM)
    keys_part = projected[:, query_width : query_width + kv_width].reshape(
        tok_dev, KV_HEADS, HEAD_DIM
    )
    values_part = projected[:, query_width + kv_width :].reshape(tok_dev, KV_HEADS, HEAD_DIM)

    def embed(query_part, key_part):
        return (rotate(query_part, cosine, sine_table), rotate(key_part, cosine, sine_table))

    (queries_turned, keys_turned), rope_pull = jax.vjp(embed, queries, keys_part)
    stacked = jnp.stack(
        [
            queries_turned,
            jnp.repeat(keys_turned, head_share, axis=1),
            jnp.repeat(values_part, head_share, axis=1),
        ],
        axis=2,
    ).astype(jnp.bfloat16)
    by_heads = lax.all_to_all(stacked, "seq", split_axis=1, concat_axis=0, tiled=True)
    head_queries = by_heads[:, :, 0]
    head_keys = by_heads[:, :, 1]
    head_values = by_heads[:, :, 2]

    def block_scores(query_block, offset):
        query_places = offset + jnp.arange(block_rows, dtype=jnp.int32)
        query_segment = lax.dynamic_slice_in_dim(segment, offset, block_rows, 0)
        raw_scores = (
            jnp.einsum("qhd,khd->hqk", query_block, head_keys, preferred_element_type=jnp.float32)
            * score_scale
        )
        allowed = allowed_mask(query_places, query_segment, places, segment)
        return jnp.where(allowed[None], raw_scores, masked_score)

    def forward_block(offset):
        query_block = lax.dynamic_slice_in_dim(head_queries, offset, block_rows, 0)
        scores = block_scores(query_block, offset)
        peak_score = jnp.max(scores, axis=-1, keepdims=True)
        exponent = jnp.exp(scores - peak_score)
        row_total = jnp.sum(exponent, axis=-1, keepdims=True)
        weights = (exponent / row_total).astype(jnp.bfloat16)
        block_out = jnp.einsum(
            "hqk,khd->qhd", weights, head_values, preferred_element_type=jnp.float32
        )
        return (block_out.astype(jnp.bfloat16), peak_score, row_total)

    offsets = jnp.arange(block_count, dtype=jnp.int32) * block_rows
    attended, peaks, totals = lax.map(forward_block, offsets)
    attended = attended.reshape(GROUP, local_heads, HEAD_DIM)
    token_attended = lax.all_to_all(attended, "seq", split_axis=0, concat_axis=1, tiled=True)
    attended_rows = token_attended.reshape(tok_dev, query_width)
    hidden = inputs + jnp.dot(attended_rows, weight_out, preferred_element_type=jnp.float32)
    normed_ffn = rms_norm(hidden, gain_ffn).astype(jnp.bfloat16)
    logits = jnp.dot(normed_ffn, weight_router, preferred_element_type=jnp.float32)
    expert_ids = routes[0]
    chosen = jnp.take_along_axis(logits, expert_ids, axis=1)
    gate_weights = jax.nn.softmax(chosen, axis=-1)
    expert_flat = expert_ids.reshape(-1)
    expert_range = jnp.arange(EXPERTS, dtype=jnp.int32)
    expert_hot = (expert_flat[:, None] == expert_range[None, :]).astype(jnp.int32)
    slot_rank = jnp.sum((jnp.cumsum(expert_hot, axis=0) - 1) * expert_hot, axis=1)
    slot_index = expert_flat * capacity + slot_rank
    slot_owner = (
        jnp.full((EXPERTS * capacity,), tok_dev * TOPK, jnp.int32)
        .at[slot_index]
        .set(jnp.arange(tok_dev * TOPK, dtype=jnp.int32))
    )
    padded = jnp.concatenate([normed_ffn, jnp.zeros((1, model_width), jnp.bfloat16)], axis=0)
    outgoing = padded[slot_owner // TOPK].reshape(EXPERTS, capacity, model_width)
    arrived = lax.all_to_all(outgoing, "seq", split_axis=0, concat_axis=1, tiled=True)
    mixed_rows = jnp.einsum(
        "erd,edf->erf", arrived, weight_gate_up, preferred_element_type=jnp.float32
    )
    activated, swiglu_pull = jax.vjp(swiglu, mixed_rows)
    activated = activated.astype(jnp.bfloat16)
    returned = jnp.einsum(
        "erf,efd->erd", activated, weight_down, preferred_element_type=jnp.float32
    ).astype(jnp.bfloat16)
    came_back = lax.all_to_all(returned, "seq", split_axis=1, concat_axis=0, tiled=True)
    picked = (
        came_back.reshape(EXPERTS * capacity, model_width)[slot_index]
        .reshape(tok_dev, TOPK, model_width)
        .astype(jnp.float32)
    )
    output = (hidden + jnp.sum(gate_weights[..., None] * picked, axis=1)).astype(jnp.bfloat16)
    attn_params = (
        lax.all_gather(norm_attn, ("seq", "wshard"), axis=0, tiled=True),
        lax.all_gather(w_qkv, ("seq", "wshard"), axis=0, tiled=True),
        lax.all_gather(w_out, ("seq", "wshard"), axis=0, tiled=True),
        lax.all_gather(w_router, ("seq", "wshard"), axis=0, tiled=True),
        lax.all_gather(norm_ffn, ("seq", "wshard"), axis=0, tiled=True),
    )
    expert_params = (
        lax.all_gather(w_gate_up, "wshard", axis=1, tiled=True),
        lax.all_gather(w_down, "wshard", axis=1, tiled=True),
    )
    gain_attn = attn_params[0].astype(jnp.float32)
    weight_qkv = attn_params[1]
    weight_out = attn_params[2]
    weight_router = attn_params[3]
    gain_ffn = attn_params[4].astype(jnp.float32)
    weight_gate_up = expert_params[0]
    weight_down = expert_params[1]
    upstream = cotangent[0].astype(jnp.float32)
    gate_grad = jnp.sum(upstream[:, None, :] * picked, axis=-1)
    chosen_grad = gate_weights * (
        gate_grad - jnp.sum(gate_weights * gate_grad, axis=-1, keepdims=True)
    )
    logit_grad = jnp.sum(
        jnp.where(
            expert_ids[:, :, None] == expert_range[None, None, :], chosen_grad[:, :, None], 0.0
        ),
        axis=1,
    ).astype(jnp.bfloat16)
    picked_grad = (
        (gate_weights[..., None] * upstream[:, None, :])
        .reshape(tok_dev * TOPK, model_width)
        .astype(jnp.bfloat16)
    )
    padded_grad = jnp.concatenate([picked_grad, jnp.zeros((1, model_width), jnp.bfloat16)], axis=0)
    outgoing_grad = padded_grad[slot_owner].reshape(EXPERTS, capacity, model_width)
    arrived_grad = lax.all_to_all(outgoing_grad, "seq", split_axis=0, concat_axis=1, tiled=True)
    act_grad = jnp.einsum(
        "erd,efd->erf", arrived_grad, weight_down, preferred_element_type=jnp.float32
    )
    grad_down = jnp.einsum(
        "erf,erd->efd", activated, arrived_grad, preferred_element_type=jnp.float32
    )
    mixed_grad = swiglu_pull(act_grad)[0].astype(jnp.bfloat16)
    grad_gate_up = jnp.einsum(
        "erd,erf->edf", arrived, mixed_grad, preferred_element_type=jnp.float32
    )
    rows_grad = jnp.einsum(
        "erf,edf->erd", mixed_grad, weight_gate_up, preferred_element_type=jnp.float32
    ).astype(jnp.bfloat16)
    back_grad = lax.all_to_all(rows_grad, "seq", split_axis=1, concat_axis=0, tiled=True)
    routed_grad = (
        back_grad.reshape(EXPERTS * capacity, model_width)[slot_index]
        .reshape(tok_dev, TOPK, model_width)
        .astype(jnp.float32)
    )
    normed_ffn_grad = jnp.sum(routed_grad, axis=1) + jnp.einsum(
        "te,de->td", logit_grad, weight_router, preferred_element_type=jnp.float32
    )
    grad_router = jnp.einsum(
        "td,te->de", normed_ffn, logit_grad, preferred_element_type=jnp.float32
    )
    norm_ffn_pull = jax.vjp(rms_norm, hidden, gain_ffn)[1]
    hidden_part, grad_norm_ffn = norm_ffn_pull(normed_ffn_grad)
    hidden_grad = upstream + hidden_part
    branch_grad = hidden_grad.astype(jnp.bfloat16)
    grad_out = jnp.einsum(
        "tq,td->qd", attended_rows, branch_grad, preferred_element_type=jnp.float32
    )
    attended_grad = (
        jnp.einsum("td,qd->tq", branch_grad, weight_out, preferred_element_type=jnp.float32)
        .astype(jnp.bfloat16)
        .reshape(tok_dev, HEADS, HEAD_DIM)
    )
    head_grad = lax.all_to_all(attended_grad, "seq", split_axis=1, concat_axis=0, tiled=True)

    def backward_block(running, block_item):
        keys_grad, values_grad = running
        offset, peak_score, row_total = block_item
        query_block = lax.dynamic_slice_in_dim(head_queries, offset, block_rows, 0)
        output_grad = lax.dynamic_slice_in_dim(head_grad, offset, block_rows, 0)
        scores = block_scores(query_block, offset)
        weights = jnp.exp(scores - peak_score) / row_total
        weights_grad = jnp.einsum(
            "qhd,khd->hqk", output_grad, head_values, preferred_element_type=jnp.float32
        )
        inner_sum = jnp.sum(weights * weights_grad, axis=-1, keepdims=True)
        scores_grad = (weights * (weights_grad - inner_sum)).astype(jnp.bfloat16)
        query_grad = (
            jnp.einsum("hqk,khd->qhd", scores_grad, head_keys, preferred_element_type=jnp.float32)
            * score_scale
        )
        keys_grad = (
            keys_grad
            + jnp.einsum(
                "hqk,qhd->khd", scores_grad, query_block, preferred_element_type=jnp.float32
            )
            * score_scale
        )
        values_grad = values_grad + jnp.einsum(
            "hqk,qhd->khd",
            weights.astype(jnp.bfloat16),
            output_grad,
            preferred_element_type=jnp.float32,
        )
        return ((keys_grad, values_grad), query_grad)

    zero_heads = jnp.zeros((GROUP, local_heads, HEAD_DIM), jnp.float32)
    (keys_grad, values_grad), query_grad = lax.scan(
        backward_block, (zero_heads, zero_heads), (offsets, peaks, totals)
    )
    query_grad = query_grad.reshape(GROUP, local_heads, HEAD_DIM)
    stacked_grad = jnp.stack([query_grad, keys_grad, values_grad], axis=2).astype(jnp.bfloat16)
    token_grad = lax.all_to_all(
        stacked_grad, "seq", split_axis=0, concat_axis=1, tiled=True
    ).astype(jnp.float32)
    keys_sum = jnp.sum(token_grad[:, :, 1].reshape(tok_dev, KV_HEADS, head_share, HEAD_DIM), axis=2)
    values_sum = jnp.sum(
        token_grad[:, :, 2].reshape(tok_dev, KV_HEADS, head_share, HEAD_DIM), axis=2
    )
    query_back, keys_back = rope_pull((token_grad[:, :, 0], keys_sum))
    projected_grad = jnp.concatenate(
        [
            query_back.reshape(tok_dev, query_width),
            keys_back.reshape(tok_dev, kv_width),
            values_sum.reshape(tok_dev, kv_width),
        ],
        axis=1,
    ).astype(jnp.bfloat16)
    grad_qkv = jnp.einsum("td,tf->df", normed, projected_grad, preferred_element_type=jnp.float32)
    normed_grad = jnp.einsum(
        "tf,df->td", projected_grad, weight_qkv, preferred_element_type=jnp.float32
    )
    norm_attn_pull = jax.vjp(rms_norm, inputs, gain_attn)[1]
    input_part, grad_norm_attn = norm_attn_pull(normed_grad)
    grad_input = hidden_grad + input_part
    attn_grads = (
        lax.psum_scatter(grad_norm_attn, ("seq", "wshard"), scatter_dimension=0, tiled=True),
        lax.psum_scatter(grad_qkv, ("seq", "wshard"), scatter_dimension=0, tiled=True),
        lax.psum_scatter(grad_out, ("seq", "wshard"), scatter_dimension=0, tiled=True),
        lax.psum_scatter(grad_router, ("seq", "wshard"), scatter_dimension=0, tiled=True),
        lax.psum_scatter(grad_norm_ffn, ("seq", "wshard"), scatter_dimension=0, tiled=True),
    )
    expert_grads = (
        lax.psum_scatter(
            grad_gate_up.astype(jnp.bfloat16), "wshard", scatter_dimension=1, tiled=True
        ).astype(jnp.float32),
        lax.psum_scatter(
            grad_down.astype(jnp.bfloat16), "wshard", scatter_dimension=1, tiled=True
        ).astype(jnp.float32),
    )
    return (
        output[None],
        grad_input[None],
        attn_grads[0],
        attn_grads[1],
        attn_grads[2],
        attn_grads[3],
        attn_grads[4],
        expert_grads[0],
        expert_grads[1],
    )


def solution(mesh):
    return jax.shard_map(
        local,
        mesh=mesh,
        in_specs=(
            P("wshard", "seq", None),
            P("wshard", "seq", None),
            P("wshard", None),
            P(("seq", "wshard")),
            P(("seq", "wshard"), None),
            P(("seq", "wshard"), None),
            P(("seq", "wshard"), None),
            P(("seq", "wshard")),
            P("seq", "wshard", None),
            P("seq", "wshard", None),
            P("wshard", "seq", None),
        ),
        out_specs=(
            P("wshard", "seq", None),
            P("wshard", "seq", None),
            P(("seq", "wshard")),
            P(("seq", "wshard"), None),
            P(("seq", "wshard"), None),
            P(("seq", "wshard"), None),
            P(("seq", "wshard")),
            P("seq", "wshard", None),
            P("seq", "wshard", None),
        ),
        check_vma=False,
    )
```

profile of v0, /device:TPU:0, one launch (start us, length us, event | category | flops | bytes accessed | tf_op | source)
XLA Modules:
  0.0 2781.9 jit_solution(12732559854793601514)
XLA Ops:
  12.6 68.2 %all-reduce.14 = (bf16[1024]{0:T(1024)(128)(2,1)S(1)}, bf16[1024]{0:T(1024)(128)(2,1)}) all-reduce(bf16[1024]{0:T(1024)(128)(2,1)S(1)} %dynamic-update-slice, bf16[1024]{0:T(1024)(128)(2,1)S(1)} %dynamic-update-slice.1), channel_id=1, replica_groups=mesh['seq'=16,'wshard'=8] {'seq','wshard'}, use_global_device_ids=true, to_apply=%add.8 | all-reduce | flops 2048 | bytes 8192
  84.2 232.0 %all-gather.5.cloned.1.call-done = bf16[1024,2048]{1,0:T(8,128)(2,1)} async-done(((bf16[8,2048]{1,0:T(8,128)(2,1)}), bf16[1024,2048]{1,0:T(8,128)(2,1)}) %all-gather.5.cloned.1.call-update) | async-done | bytes 4194320 | tf_op jit(solution)/shard_map/all_gather | solution.py:94
  332.2 9.1 reduce-window.11
  342.3 7.7 scatter_custom_fusion
  361.9 72.5 %while.30 = (s32[]{:T(128)}, bf16[7,512,1,64]{1,3,2,0:T(8,128)(2,1)}, f32[7,1,512,1]{2,3,1,0:T(1,128)}, f32[7,1,512,1]{2,3,1,0:T(1,128)}, s32[7]{0:T(128)S(1)}, ...) while((s32[]{:T(128)}, ...), condition=%wide.region_7.8_spmd.clone, body=%wide.region_4.7_spmd.clone.sunk | while | flops 491817984 | bytes 23136944 | solution.py:162
  442.9 20.8 reduce.12
  471.3 317.3 %all_gather.32 = bf16[1024,32]{1,0:T(8,128)(2,1)S(1)} all-gather(bf16[8,32]{1,0:T(8,128)(2,1)S(1)} %copy-done.49), channel_id=1, replica_groups=mesh['seq'=16,'wshard'=8] {'seq','wshard'}, dimensions={0}, use_global_device_ids=true | all-gather | bytes 66048 | tf_op jit(solution)/shard_map/all_gather | solution.py:96
  800.7 14.1 gather_fusion.4
  818.8 13.5 gather_fusion.2
  844.1 8.1 gather_fusion
  859.4 46.8 %all-to-all-done.4 = bf16[32,70,1024]{2,1,0:T(8,128)(2,1)} async-done(((bf16[32,70,1024]{2,1,0:T(8,128)(2,1)}), bf16[32,70,1024]{2,1,0:T(8,128)(2,1)}, u32[]{:S(2)}, u32[]{:S(2)}) %all-to-all-start.4) | async-done | bytes 4587552 | tf_op jit(solution)/shard_map/all_to_all | solution.py:236
  906.2 13.4 all-to-all-start.2
  925.4 7.5 all_to_all.109
  932.9 83.4 %all-to-all-done.2 = bf16[32,70,1024]{2,1,0:T(8,128)(2,1)} async-done(((bf16[32,70,1024]{2,1,0:T(8,128)(2,1)}), bf16[32,70,1024]{2,1,0:T(8,128)(2,1)}, u32[]{:S(2)}, u32[]{:S(2)}) %all-to-all-start.2) | async-done | bytes 4587552 | tf_op jit(solution)/shard_map/all_to_all | solution.py:184
  1028.7 12.1 fusion.99
  1040.8 13.4 fusion.59
  1056.8 16.8 copy.120
  1085.7 83.7 %all-to-all-done.3 = bf16[2,1120,1024]{2,0,1:T(2,128)(2,1)} async-done(((bf16[2,1120,1024]{2,0,1:T(2,128)(2,1)}), bf16[2,1120,1024]{2,0,1:T(2,128)(2,1)}, u32[]{:S(2)}, u32[]{:S(2)}) %all-to-all-start.3) | async-done | bytes 4587552 | tf_op jit(solution)/shard_map/all_to_all | solution.py:193
  1182.6 11.8 gather_fusion.1
  1201.4 11.7 convolution_convert_fusion.2
  1213.2 11.9 convolution_convert_fusion.1
  1225.1 23.0 copy.124
  1248.1 59.2 %all_to_all.126 = bf16[2,1120,1024]{2,0,1:T(2,128)(2,1)S(1)} all-to-all(bf16[2,1120,1024]{2,0,1:T(2,128)(2,1)S(1)} %copy.124), channel_id=1, replica_groups=mesh['seq'=16,'wshard'=8] {'seq'}, dimensions={1} | all-to-all | bytes 9175040 | tf_op jit(solution)/shard_map/all_to_all | solution.py:250
  1318.4 11.7 gather_fusion.3
  1348.6 8.2 all-to-all-done.6
  1360.9 200.2 %while.31 = (s32[]{:T(128)}, f32[3584,1,64]{0,2,1:T(8,128)S(1)}, f32[3584,1,64]{0,2,1:T(8,128)S(1)}, bf16[7,512,1,64]{1,3,2,0:T(8,128)(2,1)}, s32[7]{0:T(128)S(1...) while((s32[]{:T(128)}, f32[3584,1,64]{0,2,1:T(8,128)S(1)}, ...), condition=%wide.region_23.24_spmd.clone, body=%wide.region_21.23_spmd.clone.sunk | while | flops 1201278464 | bytes 75233016 | solution.py:308
  1366.3 7.4 multiply_reduce_fusion.6
  1537.8 7.4 multiply_reduce_fusion.6
  1573.0 27.1 all_to_all.127
  1630.8 64.6 %all-reduce.13 = (f32[1024]{0:T(1024)S(1)}, f32[1024]{0:T(1024)S(1)}) all-reduce(f32[1024]{0:T(1024)S(1)} %get-tuple-element.203, f32[1024]{0:T(1024)S(1)} %copy-done.44), channel_id=2, replica_groups=mesh['seq'=16,'wshard'=8] {'seq','wshard'}, use_global_device_ids=true, to_apply=%region_28.29.clone | all-reduce | flops 2048 | bytes 16384
  1699.9 425.2 %reduce-scatter.7.cloned.1.call-done = f32[8,1024]{1,0:T(8,128)} async-done(((f32[1024,1024]{1,0:T(8,128)}), f32[8,1024]{1,0:T(8,128)}) %reduce-scatter.7.cloned.1.call-update) | async-done | bytes 32784 | tf_op jit(solution)/shard_map/reduce_scatter | solution.py:339
  2125.1 649.8 %reduce-scatter.5.cloned.1.call-done = f32[8,2048]{1,0:T(8,128)} async-done(((f32[1024,2048]{1,0:T(8,128)}), f32[8,2048]{1,0:T(8,128)}) %reduce-scatter.5.cloned.1.call-update) | async-done | bytes 65552 | tf_op jit(solution)/shard_map/reduce_scatter | solution.py:338
  (427 shorter events, 451.6 us)
Async XLA Ops:
  7.2 309.0 %all-gather.5.cloned.1.call-start = ((), (), s32[]{:S(2)}) async-start(), calls=%async_computation.12 | async-start | bytes 4227072 | tf_op jit(solution)/shard_map/all_gather | solution.py:94
  7.9 788.9 %all-gather.7.cloned.1.call-start = ((), (), s32[]{:S(2)}) async-start(), calls=%async_computation.13 | async-start | bytes 2113536 | tf_op jit(solution)/shard_map/all_gather | solution.py:95
  8.7 1020.1 %all-gather.9.cloned.1.call-start = ((), (), s32[]{:S(2)}) async-start(), calls=%async_computation.14 | async-start | bytes 4718592 | tf_op jit(solution)/shard_map/all_gather | solution.py:100
  80.8 238.9 %copy-start.30 = (f32[1024]{0:T(1024)}, f32[1024]{0:T(1024)S(1)}, u32[]{:S(2)}) copy-start(f32[1024]{0:T(1024)S(1)} %convert_element_type.146) | copy-start | bytes 12292
  82.0 237.8 %copy-start.40 = (f32[224]{0:T(256)}, f32[224]{0:T(256)S(1)}, u32[]{:S(2)}) copy-start(f32[224]{0:T(256)S(1)} %fusion.86) | copy-start | bytes 2692
  83.7 236.1 %copy-start.32 = (s32[3584]{0:T(1024)}, s32[3584]{0:T(1024)S(1)}, u32[]{:S(2)}) copy-start(s32[3584]{0:T(1024)S(1)} %convert_reduce_fusion.1) | copy-start | bytes 43012
  84.1 238.5 %copy-start.23 = (f32[224,64]{0,1:T(8,128)}, f32[224,64]{0,1:T(8,128)S(1)}, u32[]{:S(2)}) copy-start(f32[224,64]{0,1:T(8,128)S(1)} %get-tuple-element.286) | copy-start | bytes 172036
  84.2 238.5 %copy-start.25 = (f32[224,64]{0,1:T(8,128)}, f32[224,64]{0,1:T(8,128)S(1)}, u32[]{:S(2)}) copy-start(f32[224,64]{0,1:T(8,128)S(1)} %get-tuple-element.285) | copy-start | bytes 172036
  323.4 18.3 copy-start.34
  323.4 26.6 copy-start.33
  324.6 31.5 %all-to-all-start = ((bf16[224,16,3,64]{0,3,2,1:T(8,128)(2,1)}), bf16[224,16,3,64]{0,3,2,1:T(8,128)(2,1)S(1)}, u32[]{:S(2)}, u32[]{:S(2)}) async-start(bf16[224,16,3,64]{0,3,2,1:T(8,128)(2,1)} %copy.106), calls=%async_computation | async-start | bytes 3145728 | tf_op jit(solution)/shard_map/all_to_all | solution.py:134
  434.5 32.1 %copy-start.1 = (bf16[3584,1,64]{0,2,1:T(8,128)(2,1)}, bf16[3584,1,64]{0,2,1:T(8,128)(2,1)S(1)}, u32[]{:S(2)}) copy-start(bf16[3584,1,64]{0,2,1:T(8,128)(2,1)S(1)} %get-tuple-element.533) | copy-start | bytes 1376260
  434.5 32.1 %copy-start.3 = (bf16[3584,1,64]{0,2,1:T(8,128)(2,1)}, bf16[3584,1,64]{0,2,1:T(8,128)(2,1)S(1)}, u32[]{:S(2)}) copy-start(bf16[3584,1,64]{0,2,1:T(8,128)(2,1)S(1)} %get-tuple-element.534) | copy-start | bytes 1376260
  434.5 32.1 %copy-start.16 = (s32[3584]{0:T(1024)}, s32[3584]{0:T(1024)S(1)}, u32[]{:S(2)}) copy-start(s32[3584]{0:T(1024)S(1)} %get-tuple-element.540) | copy-start | bytes 43012
  434.5 32.1 %copy-start.52 = (s32[7]{0:T(128)}, s32[7]{0:T(128)S(1)}, u32[]{:S(2)}) copy-start(s32[7]{0:T(128)S(1)} %get-tuple-element.562) | copy-start | bytes 88
  435.3 35.7 %copy-start.50 = (bf16[1024]{0:T(1024)(128)(2,1)S(1)}, bf16[1024]{0:T(1024)(128)(2,1)}, u32[]{:S(2)}) copy-start(bf16[1024]{0:T(1024)(128)(2,1)} %get-tuple-element.250) | copy-start | bytes 6148
  435.3 36.0 %copy-start.49 = (bf16[8,32]{1,0:T(8,128)(2,1)S(1)}, bf16[8,32]{1,0:T(8,128)(2,1)}, u32[]{:S(2)}) copy-start(bf16[8,32]{1,0:T(8,128)(2,1)} %param.21) | copy-start | bytes 1540
  466.6 330.2 %copy-start.9 = (bf16[1,224,1024]{2,1,0:T(8,128)(2,1)S(1)}, bf16[1,224,1024]{2,1,0:T(8,128)(2,1)}, u32[]{:S(2)}) copy-start(bf16[1,224,1024]{2,1,0:T(8,128)(2,1)} %param.15) | copy-start | bytes 1376260
  466.6 323.2 %all-to-all-start.1 = ((bf16[16,2,7168]{2,1,0:T(2,128)(2,1)}), bf16[16,2,7168]{2,1,0:T(2,128)(2,1)S(1)}, u32[]{:S(2)}, u32[]{:S(2)}) async-start(bf16[16,2,7168]{2,1,0:T(2,128)(2,1)} %reshape.649), calls=%async_computation.1 | async-start | bytes 917504 | tf_op jit(solution)/shard_map/all_to_all | solution.py:164
  471.0 328.9 %copy-start.35 = (f32[1024]{0:T(1024)}, f32[1024]{0:T(1024)S(1)}, u32[]{:S(2)}) copy-start(f32[1024]{0:T(1024)S(1)} %convert_element_type.149) | copy-start | bytes 12292
  839.5 66.7 %all-to-all-start.4 = ((bf16[32,70,1024]{2,1,0:T(8,128)(2,1)}), bf16[32,70,1024]{2,1,0:T(8,128)(2,1)}, u32[]{:S(2)}, u32[]{:S(2)}) async-start(bf16[32,70,1024]{2,1,0:T(8,128)(2,1)} %reshape.572), calls=%async_computation.4 | async-start | bytes 9437184 | tf_op jit(solution)/shard_map/all_to_all | solution.py:236
  906.2 110.1 %all-to-all-start.2 = ((bf16[32,70,1024]{2,1,0:T(8,128)(2,1)}), bf16[32,70,1024]{2,1,0:T(8,128)(2,1)}, u32[]{:S(2)}, u32[]{:S(2)}) async-start(bf16[32,70,1024]{2,1,0:T(8,128)(2,1)} %reshape.570), calls=%async_computation.2 | async-start | bytes 9437184 | tf_op jit(solution)/shard_map/all_to_all | solution.py:184
  919.6 121.2 %all-gather.11.cloned.1.call-start = ((), (), s32[]{:S(2)}) async-start(), calls=%async_computation.15 | async-start | bytes 2359296 | tf_op jit(solution)/shard_map/all_gather | solution.py:101
  1073.6 95.8 %all-to-all-start.3 = ((bf16[2,1120,1024]{2,0,1:T(2,128)(2,1)}), bf16[2,1120,1024]{2,0,1:T(2,128)(2,1)}, u32[]{:S(2)}, u32[]{:S(2)}) async-start(bf16[2,1120,1024]{2,0,1:T(2,128)(2,1)} %copy.120), calls=%async_computation.3 | async-start | bytes 9175040 | tf_op jit(solution)/shard_map/all_to_all | solution.py:193
  1078.2 545.5 %reduce-scatter.11.cloned.1.call-start = ((), (), s32[]{:S(2)}) async-start(), calls=%async_computation.19 | async-start | bytes 2359296 | tf_op jit(solution)/shard_map/reduce_scatter | solution.py:347
  1085.5 540.0 %all-reduce.17.cloned.1.call-start = ((), (), s32[]{:S(2)}) async-start(), calls=%async_computation.20 | async-start | bytes 1048576
  1201.4 496.4 %reduce-scatter.9.cloned.1.call-start = ((), (), s32[]{:S(2)}) async-start(), calls=%async_computation.18 | async-start | bytes 4718592 | tf_op jit(solution)/shard_map/reduce_scatter | solution.py:344
  1340.2 16.6 all-to-all-start.6
  1344.4 780.6 %reduce-scatter.7.cloned.1.call-start = ((), (), s32[]{:S(2)}) async-start(), calls=%async_computation.17 | async-start | bytes 4227072 | tf_op jit(solution)/shard_map/reduce_scatter | solution.py:339
  1348.6 1426.2 %reduce-scatter.5.cloned.1.call-start = ((), (), s32[]{:S(2)}) async-start(), calls=%async_computation.16 | async-start | bytes 8454144 | tf_op jit(solution)/shard_map/reduce_scatter | solution.py:338
  1626.8 69.7 %copy-start.46 = (f32[224]{0:T(256)S(1)}, f32[224]{0:T(256)}, u32[]{:S(2)}) copy-start(f32[224]{0:T(256)} %copy-done.45) | copy-start | bytes 2692
  1626.8 69.7 %copy-start.8 = (f32[224,1024]{1,0:T(8,128)S(1)}, f32[224,1024]{1,0:T(8,128)}, u32[]{:S(2)}) copy-start(f32[224,1024]{1,0:T(8,128)} %copy-done.7) | copy-start | bytes 2752516
  (44 other events, 246.3 us)
Sparse Core Ops, SparseCore 0:
  9.7 306.3 all-gather.4
  317.8 308.7 all-gather.6
  628.3 91.2 all-gather.8
  921.8 86.2 all-gather.10
  1085.6 82.8 reduce-scatter.10
  1201.5 178.7 all-reduce.16
  1382.8 90.4 reduce-scatter.8
  1476.3 648.6 reduce-scatter.6
  2128.0 646.7 reduce-scatter.4
where the time goes:
time: 2790 us; the launch traced here: 2780 us
  waiting for transfers between devices  1540 us (55%)
  blocking collectives  536 us (19%)
  local copies, waits for them, and re-layouts  256 us (9%)
  matrix products  242 us (9%)
  other arithmetic  127 us (5%)
  starting transfers between devices  38.9 us (1%)
    reduce_scatter x1, waiting for transfers between devices, local(): lax.psum_scatter(grad_qkv, ('seq', 'wshard'), scatter_dimension=0, tiled=...  650 us
    reduce_scatter x1, waiting for transfers between devices, local(): lax.psum_scatter(grad_out, ('seq', 'wshard'), scatter_dimension=0, tiled=...  425 us
    all_gather x1, blocking collectives, local(): lax.all_gather(w_router, ('seq', 'wshard'), axis=0, tiled=True)  317 us
    all_gather x1, waiting for transfers between devices, local(): lax.all_gather(w_qkv, ('seq', 'wshard'), axis=0, tiled=True)  232 us
    unnamed x2, blocking collectives  133 us
    all_to_all x1, waiting for transfers between devices, local(): lax.all_to_all(returned, 'seq', split_axis=1, concat_axis=0, tiled=True)  83.7 us
    all_to_all x1, waiting for transfers between devices, local(): lax.all_to_all(outgoing, 'seq', split_axis=0, concat_axis=1, tiled=True)  83.4 us
    dot_general x14, matrix products, block_scores(): jnp.einsum('qhd,khd->hqk', query_block, head_keys, preferred_element_type...  73.7 us
  transfers between devices with their start and end apart: 15, of which 8 were waited for; matrix products, arithmetic and copies ran while one was open for 20% of the time, Pallas kernels for 0%

commit v1 on v0

v1 whole, which is shorter than its diff:
```python
import jax
import jax.numpy as jnp
from jax import lax
from jax.sharding import PartitionSpec as P

HEADS = 16
KV_HEADS = 8
HEAD_DIM = 64
EXPERTS = 32
TOPK = 8
FF = 512
PROMPT = 2048
GROUP = 3584
TOK = 224
WIDTH = 1024
SLOTS = 72
N_SEQ = 16

norm_eps = 1e-06
rope_base = 10000.0
masked_score = -1e30
BOTH = ("seq", "wshard")
f32 = jnp.float32
bf16 = jnp.bfloat16


def place_of(x, z, core):
    return x * 8 + z * 2 + core


def shift_perm(a, b):
    return [
        (place_of(x, z, c), place_of(x ^ a, (z + b) % 4, c))
        for x in range(2)
        for z in range(4)
        for c in range(2)
    ]


CORE_PERM = [(i, i ^ 1) for i in range(16)]
CHIPS = [(a, b) for a in range(2) for b in range(4)]


def relative_places(seq_index):
    x, z, c = seq_index // 8, (seq_index // 2) % 4, seq_index % 2
    r = jnp.arange(16, dtype=jnp.int32)
    a, b, k = r // 8, (r // 2) % 4, r % 2
    forward = (a ^ x) * 8 + ((z - b) % 4) * 2 + (k ^ c)
    inverse = (a ^ x) * 8 + ((z - b) % 4) * 2 + (k ^ c)
    return forward, inverse


def seq_gather(rows):
    parts = []
    for a, b in CHIPS:
        got = rows if (a, b) == (0, 0) else lax.ppermute(rows, "seq", shift_perm(a, b))
        parts.append(got)
        parts.append(lax.ppermute(got, "seq", CORE_PERM))
    return jnp.stack(parts)


def seq_scatter_sum(blocks):
    paired = blocks.reshape(8, 2, *blocks.shape[1:])
    mine = paired[:, 0]
    other = lax.ppermute(paired[:, 1], "seq", CORE_PERM)
    chip = (mine.astype(f32) + other.astype(f32)).astype(bf16)
    total = chip[0].astype(f32)
    for i, (a, b) in enumerate(CHIPS):
        if i == 0:
            continue
        total = total + lax.ppermute(chip[i], "seq", shift_perm(a, -b)).astype(f32)
    return total


def inverse_rms(values):
    return lax.rsqrt(jnp.mean(values * values, axis=-1, keepdims=True) + norm_eps)


def rms_pull(values, scale, gain, grad):
    scaled = grad * gain
    return scale * scaled - values * (scale * scale * scale) * jnp.mean(
        scaled * values, axis=-1, keepdims=True
    )


def group_layout(lengths):
    places = jnp.arange(GROUP, dtype=jnp.int32)
    ends = jnp.cumsum(lengths)
    starts = ends - lengths
    offset_in = places - PROMPT
    segment_id = jnp.sum((offset_in[:, None] >= ends[None, :]).astype(jnp.int32), axis=1)
    segment_hot = segment_id[:, None] == jnp.arange(lengths.shape[0], dtype=jnp.int32)[None, :]
    begin = jnp.sum(jnp.where(segment_hot, starts[None, :], 0), axis=1)
    inside = offset_in >= 0
    position = jnp.where(inside, PROMPT + offset_in - begin, places)
    segment = jnp.where(inside, segment_id, -1)
    return (places, position, segment)


def rotary_tables(position):
    half_dim = HEAD_DIM // 2
    inverse = rope_base ** (-(jnp.arange(half_dim, dtype=f32) * 2.0) / HEAD_DIM)
    angles = position[:, None] * inverse[None, :]
    cosine, sine = jnp.cos(angles), jnp.sin(angles)
    return (
        jnp.concatenate([cosine, cosine], axis=-1),
        jnp.concatenate([sine, sine], axis=-1),
    )


def turn(values):
    half_dim = HEAD_DIM // 2
    return jnp.concatenate([-values[..., half_dim:], values[..., :half_dim]], axis=-1)


def turn_back(values):
    half_dim = HEAD_DIM // 2
    return jnp.concatenate([values[..., half_dim:], -values[..., :half_dim]], axis=-1)


def allowed_mask(query_places, query_segment, places, segment):
    causal = places[None, :] <= query_places[:, None]
    same_doc = (segment[None, :] < 0) | (segment[None, :] == query_segment[:, None])
    return causal & same_doc


def attention_forward(q, k, v, places, segment):
    rows = 512
    def block(offset):
        qb = lax.dynamic_slice_in_dim(q, offset, rows, 0)
        query_segment = lax.dynamic_slice_in_dim(segment, offset, rows, 0)
        raw = jnp.einsum("qd,kd->qk", qb, k, preferred_element_type=f32) * HEAD_DIM**-0.5
        allowed = allowed_mask(offset + jnp.arange(rows), query_segment, places, segment)
        scores = jnp.where(allowed, raw, masked_score)
        peak = jnp.max(scores, axis=-1, keepdims=True)
        exponent = jnp.exp(scores - peak)
        total = jnp.sum(exponent, axis=-1, keepdims=True)
        weights = (exponent / total).astype(bf16)
        out = jnp.einsum("qk,kd->qd", weights, v, preferred_element_type=f32)
        return out, peak, total

    offsets = jnp.arange(GROUP // rows, dtype=jnp.int32) * rows
    out, peak, total = lax.map(block, offsets)
    return out.reshape(GROUP, HEAD_DIM), (peak, total)


def attention_backward(q, k, v, attended, stats, grad, places, segment):
    rows = 512
    def block(running, item):
        keys_grad, values_grad = running
        offset, peak, total = item
        qb = lax.dynamic_slice_in_dim(q, offset, rows, 0)
        gb = lax.dynamic_slice_in_dim(grad, offset, rows, 0)
        query_segment = lax.dynamic_slice_in_dim(segment, offset, rows, 0)
        raw = jnp.einsum("qd,kd->qk", qb, k, preferred_element_type=f32) * HEAD_DIM**-0.5
        allowed = allowed_mask(offset + jnp.arange(rows), query_segment, places, segment)
        scores = jnp.where(allowed, raw, masked_score)
        weights = jnp.exp(scores - peak) / total
        wgrad = jnp.einsum("qd,kd->qk", gb, v, preferred_element_type=f32)
        inner = jnp.sum(weights * wgrad, axis=-1, keepdims=True)
        sgrad = (weights * (wgrad - inner)).astype(bf16)
        qgrad = jnp.einsum("qk,kd->qd", sgrad, k, preferred_element_type=f32) * HEAD_DIM**-0.5
        keys_grad = keys_grad + jnp.einsum(
            "qk,qd->kd", sgrad, qb, preferred_element_type=f32
        ) * HEAD_DIM**-0.5
        values_grad = values_grad + jnp.einsum(
            "qk,qd->kd", weights.astype(bf16), gb, preferred_element_type=f32
        )
        return (keys_grad, values_grad), qgrad

    zero = jnp.zeros((GROUP, HEAD_DIM), f32)
    offsets = jnp.arange(GROUP // rows, dtype=jnp.int32) * rows
    (keys_grad, values_grad), qgrad = lax.scan(block, (zero, zero), (offsets, *stats))
    return qgrad.reshape(GROUP, HEAD_DIM), keys_grad, values_grad


def local(
    tokens,
    routes,
    cont_lengths,
    norm_attn,
    w_qkv,
    w_out,
    w_router,
    norm_ffn,
    w_gate_up,
    w_down,
    cotangent,
):
    seq_index = lax.axis_index("seq")
    relative, inverse = relative_places(seq_index)
    rows = tokens[0]
    query_width = HEADS * HEAD_DIM
    kv_width = KV_HEADS * HEAD_DIM

    rows_all = seq_gather(rows)
    head_cols = jnp.concatenate(
        [
            w_qkv[:, :query_width].reshape(8, HEADS, HEAD_DIM),
            jnp.repeat(w_qkv[:, query_width : query_width + kv_width].reshape(8, KV_HEADS, HEAD_DIM), 2, axis=1),
            jnp.repeat(w_qkv[:, query_width + kv_width :].reshape(8, KV_HEADS, HEAD_DIM), 2, axis=1),
            jnp.broadcast_to(norm_attn[:, None, None], (8, HEADS, HEAD_DIM)),
        ],
        axis=2,
    ).transpose(1, 0, 2)
    head_cols = jnp.broadcast_to(head_cols[:, None], (HEADS, 8, 8, 256)).reshape(128, 8, 256)
    head_weights = lax.all_to_all(head_cols, BOTH, 0, 0, tiled=True).reshape(WIDTH, 256)
    weight_head = head_weights[:, :192]
    gain_attn = head_weights[:, 192].astype(f32)

    shared = jnp.concatenate(
        [w_out, w_router, norm_ffn[:, None], jnp.zeros((8, 95), bf16)], axis=1
    )
    shared = lax.all_gather(shared, "wshard", axis=0, tiled=True)
    shared = lax.all_gather(shared, "seq", axis=0, tiled=True)
    weight_out = shared[:, :WIDTH]
    weight_router = shared[:, WIDTH : WIDTH + EXPERTS]
    gain_ffn = shared[:, WIDTH + EXPERTS].astype(f32)

    expert_rows = jnp.concatenate([w_gate_up, w_down], axis=1)
    experts = lax.all_gather(expert_rows, "wshard", axis=0).transpose(1, 0, 2, 3)
    weight_gate_up = experts[:, :, :128].reshape(2, WIDTH, 2 * FF)
    weight_down = experts[:, :, 128:].reshape(2, FF, WIDTH)

    routes_all = jnp.take(lax.all_gather(routes[0], "seq", axis=0), relative, axis=0)
    places, position, segment = group_layout(cont_lengths[0])
    cosine, sine = rotary_tables(position.astype(f32))

    inputs_all = rows_all.astype(f32)
    normed_all = (inputs_all * inverse_rms(inputs_all) * gain_attn).astype(bf16)
    projected = jnp.einsum("btd,df->btf", normed_all, weight_head, preferred_element_type=f32)
    projected = jnp.take(projected, inverse, axis=0).reshape(GROUP, 192)
    q, k, v = projected[:, :64], projected[:, 64:128], projected[:, 128:]
    q = (q * cosine + turn(q) * sine).astype(bf16)
    k = (k * cosine + turn(k) * sine).astype(bf16)
    v = v.astype(bf16)

    attended_head, stats = attention_forward(q, k, v, places, segment)
    attended = lax.all_to_all(
        attended_head.astype(bf16).reshape(16, TOK, HEAD_DIM), "seq", 0, 0, tiled=True
    )
    attended = attended.transpose(1, 0, 2).reshape(TOK, query_width)
    inputs = rows.astype(f32)
    hidden = inputs + jnp.dot(attended, weight_out, preferred_element_type=f32)
    hidden_scale = inverse_rms(hidden)
    normed_ffn = (hidden * hidden_scale * gain_ffn).astype(bf16)

    grad_all = seq_gather(cotangent[0])
    ffn_all = seq_gather(normed_ffn)
    expert_range = jnp.arange(EXPERTS, dtype=jnp.int32)
    chosen = jnp.any(routes_all[..., None] == expert_range, axis=2)
    logits = jnp.einsum("btd,de->bte", ffn_all, weight_router, preferred_element_type=f32)
    peak = jnp.max(jnp.where(chosen, logits, -jnp.inf), axis=-1, keepdims=True)
    raised = jnp.where(chosen, jnp.exp(logits - peak), 0.0)
    gates_all = raised / jnp.sum(raised, axis=-1, keepdims=True)
    gates = gates_all[0]
    chosen_own = lax.dynamic_slice_in_dim(chosen, seq_index * 2, 2, 2).transpose(0, 2, 1)
    gates_own = lax.dynamic_slice_in_dim(gates_all, seq_index * 2, 2, 2).transpose(0, 2, 1)
    rank = jnp.cumsum(chosen_own.astype(jnp.int32), axis=2) - 1
    slot = jnp.arange(SLOTS, dtype=jnp.int32)
    picks = chosen_own[:, :, None, :] & (rank[:, :, None, :] == slot[None, None, :, None])
    slot_gates = jnp.sum(jnp.where(picks, gates_own[:, :, None, :], 0.0), axis=3)
    slot_gates = slot_gates.transpose(1, 0, 2).reshape(2, 16 * SLOTS, 1)
    picks = picks.astype(bf16)

    expert_in = jnp.einsum(
        "best,btd->ebsd", picks, ffn_all, preferred_element_type=f32
    ).astype(bf16).reshape(2, 16 * SLOTS, WIDTH)
    expert_grad = jnp.einsum(
        "best,btd->ebsd", picks, grad_all, preferred_element_type=f32
    ).reshape(2, 16 * SLOTS, WIDTH)
    returned_grad = (slot_gates * expert_grad).astype(bf16)
    mixed = jnp.einsum("erd,edf->erf", expert_in, weight_gate_up, preferred_element_type=f32)
    gate_part, up_part = mixed[..., :FF], mixed[..., FF:]
    sigma = jax.nn.sigmoid(gate_part)
    silu = gate_part * sigma
    activated = (silu * up_part).astype(bf16)
    returned = jnp.einsum(
        "erf,efd->erd", activated, weight_down, preferred_element_type=f32
    ).astype(bf16).astype(f32)
    gate_grad = jnp.sum(returned * expert_grad, axis=-1).reshape(2, 16, SLOTS)
    act_grad = jnp.einsum("erd,efd->erf", returned_grad, weight_down, preferred_element_type=f32)
    mixed_grad = jnp.concatenate(
        [act_grad * up_part * (sigma + silu * (1.0 - sigma)), act_grad * silu], axis=-1
    ).astype(bf16)
    rows_grad = jnp.einsum(
        "erf,edf->erd", mixed_grad, weight_gate_up, preferred_element_type=f32
    ).astype(bf16)
    grad_down = jnp.einsum("erf,erd->efd", activated, returned_grad, preferred_element_type=f32)
    grad_gate_up = jnp.einsum("erd,erf->edf", expert_in, mixed_grad, preferred_element_type=f32)

    routed_part = jnp.einsum(
        "best,ebsd->btd",
        picks,
        rows_grad.reshape(2, 16, SLOTS, WIDTH),
        preferred_element_type=f32,
    ).astype(bf16)
    token_gate_grad = jnp.sum(
        picks.astype(f32) * gate_grad.transpose(1, 0, 2)[..., None], axis=2
    )
    gate_grad_own = lax.all_to_all(
        jnp.take(token_gate_grad, inverse, axis=0), "seq", 0, 0, tiled=True
    ).reshape(EXPERTS, TOK).T
    routed_grad = seq_scatter_sum(routed_part)

    expert_grads = jnp.concatenate(
        [grad_gate_up.reshape(2, 8, 128, 1024), grad_down.reshape(2, 8, 64, 1024)], axis=2
    ).astype(bf16).reshape(2, 8 * 192, 1024)
    expert_grads = lax.psum_scatter(
        expert_grads, "wshard", scatter_dimension=1, tiled=True
    ).astype(f32)

    chosen_grad = gates * (gate_grad_own - jnp.sum(gates * gate_grad_own, axis=-1, keepdims=True))
    logit_grad = chosen_grad.astype(bf16)
    normed_ffn_grad = routed_grad + jnp.einsum(
        "te,de->td", logit_grad, weight_router, preferred_element_type=f32
    )
    grad_router = jnp.einsum("td,te->de", normed_ffn, logit_grad, preferred_element_type=f32)
    upstream = cotangent[0].astype(f32)
    grad_norm_ffn = jnp.sum(normed_ffn_grad * hidden * hidden_scale, axis=0)
    hidden_grad = upstream + rms_pull(hidden, hidden_scale, gain_ffn, normed_ffn_grad)
    branch_grad = hidden_grad.astype(bf16)
    attended_grad = jnp.einsum(
        "td,qd->tq", branch_grad, weight_out, preferred_element_type=f32
    ).astype(bf16)
    head_grad = lax.all_to_all(
        attended_grad.reshape(TOK, HEADS, HEAD_DIM).transpose(1, 0, 2), "seq", 0, 0, tiled=True
    ).reshape(GROUP, HEAD_DIM)

    grad_out = jnp.einsum("tq,td->qd", attended, branch_grad, preferred_element_type=f32)
    shared_grads = jnp.concatenate(
        [grad_out, grad_router, grad_norm_ffn[:, None], jnp.zeros((WIDTH, 95), f32)], axis=1
    ).astype(bf16)
    shared_grads = jnp.sum(
        lax.all_to_all(shared_grads.reshape(128, 8, 1152), BOTH, 0, 0, tiled=True).astype(f32),
        axis=0,
    )

    moved_part = jnp.einsum(
        "best,ebsd->btd",
        picks,
        (slot_gates * returned).astype(bf16).reshape(2, 16, SLOTS, WIDTH),
        preferred_element_type=f32,
    ).astype(bf16)
    output = (hidden + seq_scatter_sum(moved_part)).astype(bf16)

    dq, dk, dv = attention_backward(q, k, v, attended_head, stats, head_grad, places, segment)
    dq = dq.astype(bf16).astype(f32)
    dk = dk.astype(bf16).astype(f32)
    projected_grad = jnp.concatenate(
        [dq * cosine + turn_back(dq * sine), dk * cosine + turn_back(dk * sine), dv], axis=1
    ).astype(bf16)
    projected_grad = jnp.take(projected_grad.reshape(16, TOK, 192), relative, axis=0)
    normed_part = jnp.einsum(
        "btf,df->btd", projected_grad, weight_head, preferred_element_type=f32
    ).astype(bf16)
    normed_grad = seq_scatter_sum(normed_part)
    grad_head = jnp.einsum(
        "btd,btf->df", normed_all, projected_grad, preferred_element_type=f32
    ).astype(bf16)
    grad_heads = jnp.sum(
        lax.all_to_all(grad_head.reshape(128, 8, 192), BOTH, 0, 0, tiled=True)
        .reshape(16, 8, 8, 192)
        .astype(f32),
        axis=1,
    ).transpose(1, 0, 2)
    grad_qkv = jnp.concatenate(
        [
            grad_heads[:, :, :64].reshape(8, query_width),
            jnp.sum(grad_heads[:, :, 64:128].reshape(8, KV_HEADS, 2, 64), axis=2).reshape(8, kv_width),
            jnp.sum(grad_heads[:, :, 128:].reshape(8, KV_HEADS, 2, 64), axis=2).reshape(8, kv_width),
        ],
        axis=1,
    )
    grad_norm_attn = jnp.sum(grad_qkv * w_qkv.astype(f32), axis=1) / norm_attn.astype(f32)
    grad_input = hidden_grad + rms_pull(inputs, inverse_rms(inputs), gain_attn, normed_grad)
    return (
        output[None],
        grad_input[None],
        grad_norm_attn,
        grad_qkv,
        shared_grads[:, :WIDTH],
        shared_grads[:, WIDTH : WIDTH + EXPERTS],
        shared_grads[:, WIDTH + EXPERTS],
        expert_grads[:, :128],
        expert_grads[:, 128:],
    )


def solution(mesh):
    return jax.shard_map(
        local,
        mesh=mesh,
        in_specs=(
            P("wshard", "seq", None),
            P("wshard", "seq", None),
            P("wshard", None),
            P(BOTH),
            P(BOTH, None),
            P(BOTH, None),
            P(BOTH, None),
            P(BOTH),
            P("seq", "wshard", None),
            P("seq", "wshard", None),
            P("wshard", "seq", None),
        ),
        out_specs=(
            P("wshard", "seq", None),
            P("wshard", "seq", None),
            P(BOTH),
            P(BOTH, None),
            P(BOTH, None),
            P(BOTH, None),
            P(BOTH),
            P("seq", "wshard", None),
            P("seq", "wshard", None),
        ),
        check_vma=False,
    )
```

time: 2790 us -> 1050 us (0.38)
  waiting for transfers between devices: 1540 us -> 179 us
  blocking collectives: 536 us -> 55.9 us
  starting transfers between devices: 38.9 us -> 165 us
  local copies, waits for them, and re-layouts: 256 us -> 204 us
    reduce_scatter x4 -> x1, waiting for transfers between devices: 1070 us -> 0.01 us  [local(): lax.psum_scatter(expert_grads, 'wshard', scatter_dimension=1, tiled=True)]
    all_gather x1 -> x2, blocking collectives: 317 us -> 55.9 us  [the longest x1 30.9 us: local(): shared = lax.all_gather(shared, 'wshard', axis=0, tiled=True)]
    all_gather x4 -> x2, waiting for transfers between devices: 232 us -> 0.02 us  [the longest x1 0.02 us: local(): lax.all_gather(expert_rows, 'wshard', axis=0).transpose(1, 0, 2, 3)]
    all_to_all x6, waiting for transfers between devices: 228 us -> 2.96 us  [the longest x1 2.81 us: local(): lax.all_to_all(attended_grad.reshape(TOK, HEADS, HEAD_DIM).transpose(1, 0...]
    ppermute x0 -> x69, waiting for transfers between devices: none -> 176 us  [the longest x21 101 us: seq_gather(): lax.ppermute(rows, 'seq', shift_perm(a, b))]
    unnamed x2 -> x0, blocking collectives: 133 us -> none
    ppermute x0 -> x69, starting transfers between devices: none -> 125 us  [the longest x21 77.5 us: seq_scatter_sum(): total = total + lax.ppermute(chip[i], 'seq', shift_perm(a, -b)).astype(f32)]
    all_to_all x2 -> x0, blocking collectives: 86.2 us -> none  [the longest x1 59.2 us: local(): lax.all_to_all(rows_grad, 'seq', split_axis=1, concat_axis=0, tiled=True)]
  transfers between devices with their start and end apart: 15 -> 78, of which waited for: 8 -> 22; matrix products, arithmetic and copies ran while one was open for 20% -> 46% of each run, Pallas kernels for 0% -> 0%
where the time goes in v1:
time: 1050 us; the launch traced here: 1040 us
  matrix products  249 us (24%)
  local copies, waits for them, and re-layouts  204 us (19%)
  waiting for transfers between devices  179 us (17%)
  starting transfers between devices  165 us (16%)
  other arithmetic  134 us (13%)
  blocking collectives  55.9 us (5%)
  loops' own time  40.4 us (4%)
  between operations  15.4 us (1%)
    ppermute x21, waiting for transfers between devices, seq_gather(): lax.ppermute(rows, 'seq', shift_perm(a, b))  101 us
    ppermute x21, starting transfers between devices, seq_scatter_sum(): total = total + lax.ppermute(chip[i], 'seq', shift_perm(a, -b)).astype(f32)  77.5 us
    ppermute x21, waiting for transfers between devices, seq_scatter_sum(): total = total + lax.ppermute(chip[i], 'seq', shift_perm(a, -b)).astype(f32)  74.4 us
    unnamed x170, local copies, waits for them, and re-layouts  71.6 us
    dot_general x14, matrix products, block(): jnp.einsum('qd,kd->qk', qb, k, preferred_element_type=f32)  70.4 us
    convert_element_type x7, other arithmetic, block(): sgrad = (weights * (wgrad - inner)).astype(bf16)  47.2 us
    ppermute x21, starting transfers between devices, seq_gather(): lax.ppermute(rows, 'seq', shift_perm(a, b))  43.3 us
    all_gather x1, blocking collectives, local(): shared = lax.all_gather(shared, 'wshard', axis=0, tiled=True)  30.9 us
  transfers between devices with their start and end apart: 78, of which 22 were waited for; matrix products, arithmetic and copies ran while one was open for 46% of the time, Pallas kernels for 0%

profile of v1, /device:TPU:0, one launch (start us, length us, event | category | flops | bytes accessed | tf_op | source)
XLA Modules:
  0.0 1043.4 jit_solution(12948576964759663565)
XLA Ops:
  8.8 30.9 %all_gather.15 = bf16[64,1152]{1,0:T(8,128)(2,1)} all-gather(bf16[8,1152]{1,0:T(8,128)(2,1)S(1)} %concatenate.69), channel_id=1, replica_groups=mesh['seq'=16,'wshard'=8] {'wshard'}, dimensions={0}, use_global_device_ids=true | all-gather | bytes 165888 | tf_op jit(solution)/shard_map/all_gather | solution.py:214
  64.9 25.0 %all_gather.17 = s32[16,224,8]{1,2,0:T(8,128)S(1)} all-gather(s32[1,224,8]{1,2,0:T(8,128)} %param.16), channel_id=1, replica_groups=mesh['seq'=16,'wshard'=8] {'seq'}, dimensions={0}, use_global_device_ids=true | all-gather | bytes 121856 | tf_op jit(solution)/shard_map/all_gather | solution.py:225
  101.4 12.3 %collective-permute-done.39 = bf16[224,1024]{1,0:T(8,128)(2,1)} collective-permute-done((bf16[224,1024]{1,0:T(8,128)(2,1)}, bf16[224,1024]{1,0:T(8,128)(2,1)}, u32[]{:S(2)}, u32[]{:S(2)}) %collective-permute-start.39) | collective-permute-done | bytes 458784 | tf_op jit(solution)/shard_map/ppermute | solution.py:56
  130.5 10.5 %collective-permute-done.9 = bf16[224,1024]{1,0:T(8,128)(2,1)} collective-permute-done((bf16[224,1024]{1,0:T(8,128)(2,1)S(1)}, bf16[224,1024]{1,0:T(8,128)(2,1)}, u32[]{:S(2)}, u32[]{:S(2)}) %collective-permute-start.9) | collective-permute-done | bytes 458784 | tf_op jit(solution)/shard_map/ppermute | solution.py:56
  143.7 14.2 %collective-permute-done.11 = bf16[224,1024]{1,0:T(8,128)(2,1)S(1)} collective-permute-done((bf16[224,1024]{1,0:T(8,128)(2,1)S(1)}, bf16[224,1024]{1,0:T(8,128)(2,1)S(1)}, u32[]{:S(2)}, u32[]{:S(2)}) %collective-permute-start.11) | collective-permute-done | bytes 458784 | tf_op jit(solution)/shard_map/ppermute | solution.py:56
  160.1 13.6 %collective-permute-done.13 = bf16[224,1024]{1,0:T(8,128)(2,1)S(1)} collective-permute-done((bf16[224,1024]{1,0:T(8,128)(2,1)S(1)}, bf16[224,1024]{1,0:T(8,128)(2,1)S(1)}, u32[]{:S(2)}, u32[]{:S(2)}) %collective-permute-start.13) | collective-permute-done | bytes 458784 | tf_op jit(solution)/shard_map/ppermute | solution.py:56
  203.8 79.3 %while.30 = (s32[]{:T(128)}, bf16[7,512,64]{1,2,0:T(8,128)(2,1)S(1)}, f32[7,512,1]{1,2,0:T(1,128)}, f32[7,512,1]{1,2,0:T(1,128)}, s32[7]{0:T(128)S(1)}, /*index=...) while((s32[]{:T(128)}, ...), condition=%wide.region_7.8_spmd.clone, body=%wide.region_4.7_spmd.clone.sunk | while | flops 491785216 | bytes 24185012 | solution.py:143
  289.1 7.6 all-to-all-start.1
  308.0 11.6 %collective-permute-done.49 = bf16[224,1024]{1,0:T(8,128)(2,1)S(1)} collective-permute-done((bf16[224,1024]{1,0:T(8,128)(2,1)}, bf16[224,1024]{1,0:T(8,128)(2,1)S(1)}, u32[]{:S(2)}, u32[]{:S(2)}) %collective-permute-start.49) | collective-permute-done | bytes 458784 | tf_op jit(solution)/shard_map/ppermute | solution.py:56
  319.6 7.9 collective-permute-done.51
  384.5 9.8 collective-permute-done.26
  394.3 8.4 collective-permute-done.28
  426.6 12.5 %copy.379 = bf16[8,2,192,1024]{2,0,3,1:T(8,128)(2,1)} copy(bf16[8,2,192,1024]{3,2,1,0:T(8,128)(2,1)} %bitcast.431) | data formatting | bytes 12582912 | tf_op jit(solution)/shard_map/all_gather | solution.py:221
  447.6 7.3 reshape.508
  454.9 8.1 fusion.174
  474.6 10.2 fusion.30
  492.6 9.7 multiply_convert_fusion.2
  561.2 22.2 %collective-permute-done.54 = bf16[224,1024]{1,0:T(8,128)(2,1)S(1)} collective-permute-done((bf16[224,1024]{1,0:T(8,128)(2,1)}, bf16[224,1024]{1,0:T(8,128)(2,1)S(1)}, u32[]{:S(2)}, u32[]{:S(2)}) %collective-permute-start.54) | collective-permute-done | bytes 458784 | tf_op jit(solution)/shard_map/ppermute | solution.py:71
  590.4 11.0 %fusion.52 = bf16[2,1024,1024]{2,1,0:T(8,128)(2,1)} fusion(bf16[2,1152,1024]{2,1,0:T(8,128)(2,1)} %bitcast.436, bf16[2,1152,512]{1,2,0:T(8,128)(2,1)} %get-tuple-element.430, bf16[2,1152,512]{1,2,0:T(8,128)(2,1)} %get-tuple-element.429), kind=kOutput, calls=%fused_computation.96 | convolution fusion | flops 4843372544 | bytes 13631488 | tf_op jit(solution)/shard_map/erd,erf->edf/dot_general | solution.py:290
  620.6 9.4 collective-permute-done.35
  630.0 9.5 collective-permute-done.36
  672.1 206.7 %while.31 = (s32[]{:T(128)}, f32[3584,64]{0,1:T(8,128)S(1)}, f32[3584,64]{0,1:T(8,128)S(1)}, bf16[7,512,64]{1,2,0:T(8,128)(2,1)}, s32[7]{0:T(128)S(1)}, /*index=...) while((s32[]{:T(128)}, f32[3584,64]{0,1:T(8,128)S(1)}, ...), condition=%wide.region_22.23_spmd.clone, body=%wide.region_20.22_spmd.clone.sunk | while | flops 1201278464 | bytes 79165240 | solution.py:173
  678.4 7.1 multiply_reduce_fusion.7
  708.0 7.1 multiply_reduce_fusion.7
  826.0 7.1 multiply_reduce_fusion.7
  855.5 7.1 multiply_reduce_fusion.7
  915.9 7.5 all-to-all-start.4
  936.9 9.6 all-to-all-start.5
  965.3 18.1 %collective-permute-done.62 = bf16[224,1024]{1,0:T(8,128)(2,1)} collective-permute-done((bf16[224,1024]{1,0:T(8,128)(2,1)}, bf16[224,1024]{1,0:T(8,128)(2,1)}, u32[]{:S(2)}, u32[]{:S(2)}) %collective-permute-start.62) | collective-permute-done | bytes 458784 | tf_op jit(solution)/shard_map/ppermute | solution.py:71
  983.4 15.7 %collective-permute-start.67 = (bf16[224,1024]{1,0:T(8,128)(2,1)}, bf16[224,1024]{1,0:T(8,128)(2,1)}, u32[]{:S(2)}, u32[]{:S(2)}) collective-permute-start(bf16[224,1024]{1,0:T(8,128)(2,1)} %get-tuple-element.433), channel_id=1, source_target_pairs={{0,96},{8,104},{16,112},{24,120},{32,64},{40,72},{48,80},{56,88},{... | collective-permute-start | bytes 1376264 | tf_op jit(solution)/shard_map/ppermute | solution.py:71
  999.1 18.7 %collective-permute-start.68 = (bf16[224,1024]{1,0:T(8,128)(2,1)}, bf16[224,1024]{1,0:T(8,128)(2,1)}, u32[]{:S(2)}, u32[]{:S(2)}) collective-permute-start(bf16[224,1024]{1,0:T(8,128)(2,1)} %get-tuple-element.432), channel_id=1, source_target_pairs={{0,80},{8,88},{16,96},{24,104},{32,112},{40,120},{48,64},{56,72},{... | collective-permute-start | bytes 1376264 | tf_op jit(solution)/shard_map/ppermute | solution.py:71
  1020.7 8.0 collective-permute-done.68
  (655 shorter events, 629.8 us)
Async XLA Ops:
  7.2 332.8 %all-gather.4.cloned.1.call-start = ((), (), s32[]{:S(2)}) async-start(), calls=%async_computation.7 | async-start | bytes 2506752 | tf_op jit(solution)/shard_map/all_gather | solution.py:215
  39.7 59.9 %collective-permute-start.1 = (bf16[224,1024]{1,0:T(8,128)(2,1)}, bf16[224,1024]{1,0:T(8,128)(2,1)S(1)}, u32[]{:S(2)}, u32[]{:S(2)}) collective-permute-start(bf16[224,1024]{1,0:T(8,128)(2,1)} %bitcast.423), channel_id=1, source_target_pairs={{0,16},{8,24},{16,32},{24,40},{32,48},{40,56},{48,0},{56,8},{64,80... | collective-permute-start | bytes 1376264 | tf_op jit(solution)/shard_map/ppermute | solution.py:56
  41.7 55.7 %collective-permute-start = (bf16[224,1024]{1,0:T(8,128)(2,1)}, bf16[224,1024]{1,0:T(8,128)(2,1)}, u32[]{:S(2)}, u32[]{:S(2)}) collective-permute-start(bf16[224,1024]{1,0:T(8,128)(2,1)} %bitcast.424), channel_id=1, source_target_pairs={{0,8},{8,0},{16,24},{24,16},{32,40},{40,32},{48,56},{56,48},{64,72... | collective-permute-start | bytes 1376264 | tf_op jit(solution)/shard_map/ppermute | solution.py:58
  41.7 74.1 %collective-permute-start.3 = (bf16[224,1024]{1,0:T(8,128)(2,1)}, bf16[224,1024]{1,0:T(8,128)(2,1)S(1)}, u32[]{:S(2)}, u32[]{:S(2)}) collective-permute-start(bf16[224,1024]{1,0:T(8,128)(2,1)} %bitcast.425), channel_id=1, source_target_pairs={{0,32},{8,40},{16,48},{24,56},{32,0},{40,8},{48,16},{56,24},{64,96... | collective-permute-start | bytes 1376264 | tf_op jit(solution)/shard_map/ppermute | solution.py:56
  45.3 76.7 %collective-permute-start.5 = (bf16[224,1024]{1,0:T(8,128)(2,1)}, bf16[224,1024]{1,0:T(8,128)(2,1)S(1)}, u32[]{:S(2)}, u32[]{:S(2)}) collective-permute-start(bf16[224,1024]{1,0:T(8,128)(2,1)} %bitcast.426), channel_id=1, source_target_pairs={{0,48},{8,56},{16,0},{24,8},{32,16},{40,24},{48,32},{56,40},{64,11... | collective-permute-start | bytes 1376264 | tf_op jit(solution)/shard_map/ppermute | solution.py:56
  46.3 79.8 %collective-permute-start.7 = (bf16[224,1024]{1,0:T(8,128)(2,1)}, bf16[224,1024]{1,0:T(8,128)(2,1)S(1)}, u32[]{:S(2)}, u32[]{:S(2)}) collective-permute-start(bf16[224,1024]{1,0:T(8,128)(2,1)} %bitcast.427), channel_id=1, source_target_pairs={{0,64},{8,72},{16,80},{24,88},{32,96},{40,104},{48,112},{56,120},{... | collective-permute-start | bytes 1376264 | tf_op jit(solution)/shard_map/ppermute | solution.py:56
  52.7 62.9 %all-to-all-start = ((bf16[128,8,256]{2,1,0:T(8,128)(2,1)}), bf16[128,8,256]{2,1,0:T(8,128)(2,1)S(1)}, u32[]{:S(2)}, u32[]{:S(2)}) async-start(bf16[128,8,256]{2,1,0:T(8,128)(2,1)} %bitcast.21), calls=%async_computation | async-start | bytes 1048576 | tf_op jit(solution)/shard_map/all_to_all | solution.py:207
  58.3 368.3 %all-gather.6.cloned.1.call-start = ((), (), s32[]{:S(2)}) async-start(), calls=%async_computation.9 | async-start | bytes 7077888 | tf_op jit(solution)/shard_map/all_gather | solution.py:221
  115.8 42.1 %collective-permute-start.11 = (bf16[224,1024]{1,0:T(8,128)(2,1)S(1)}, bf16[224,1024]{1,0:T(8,128)(2,1)S(1)}, u32[]{:S(2)}, u32[]{:S(2)}) collective-permute-start(bf16[224,1024]{1,0:T(8,128)(2,1)S(1)} %bitcast.429), channel_id=1, source_target_pairs={{0,96},{8,104},{16,112},{24,120},{32,64},{40,72},{48,80},{56,88},{... | collective-permute-start | bytes 1376264 | tf_op jit(solution)/shard_map/ppermute | solution.py:56
  122.0 51.8 %collective-permute-start.13 = (bf16[224,1024]{1,0:T(8,128)(2,1)S(1)}, bf16[224,1024]{1,0:T(8,128)(2,1)S(1)}, u32[]{:S(2)}, u32[]{:S(2)}) collective-permute-start(bf16[224,1024]{1,0:T(8,128)(2,1)S(1)} %bitcast.430), channel_id=1, source_target_pairs={{0,112},{8,120},{16,64},{24,72},{32,80},{40,88},{48,96},{56,104},{... | collective-permute-start | bytes 1376264 | tf_op jit(solution)/shard_map/ppermute | solution.py:56
  126.1 170.5 %collective-permute-start.41 = (bf16[224,1024]{1,0:T(8,128)(2,1)}, bf16[224,1024]{1,0:T(8,128)(2,1)}, u32[]{:S(2)}, u32[]{:S(2)}) collective-permute-start(bf16[224,1024]{1,0:T(8,128)(2,1)} %bitcast.73), channel_id=1, source_target_pairs={{0,32},{8,40},{16,48},{24,56},{32,0},{40,8},{48,16},{56,24},{64,96... | collective-permute-start | bytes 1376264 | tf_op jit(solution)/shard_map/ppermute | solution.py:56
  141.0 161.5 %collective-permute-start.43 = (bf16[224,1024]{1,0:T(8,128)(2,1)}, bf16[224,1024]{1,0:T(8,128)(2,1)}, u32[]{:S(2)}, u32[]{:S(2)}) collective-permute-start(bf16[224,1024]{1,0:T(8,128)(2,1)} %bitcast.73), channel_id=1, source_target_pairs={{0,48},{8,56},{16,0},{24,8},{32,16},{40,24},{48,32},{56,40},{64,11... | collective-permute-start | bytes 1376264 | tf_op jit(solution)/shard_map/ppermute | solution.py:56
  158.0 149.5 %collective-permute-start.45 = (bf16[224,1024]{1,0:T(8,128)(2,1)}, bf16[224,1024]{1,0:T(8,128)(2,1)}, u32[]{:S(2)}, u32[]{:S(2)}) collective-permute-start(bf16[224,1024]{1,0:T(8,128)(2,1)} %bitcast.73), channel_id=1, source_target_pairs={{0,64},{8,72},{16,80},{24,88},{32,96},{40,104},{48,112},{56,120},{... | collective-permute-start | bytes 1376264 | tf_op jit(solution)/shard_map/ppermute | solution.py:56
  173.8 134.2 %collective-permute-start.47 = (bf16[224,1024]{1,0:T(8,128)(2,1)}, bf16[224,1024]{1,0:T(8,128)(2,1)}, u32[]{:S(2)}, u32[]{:S(2)}) collective-permute-start(bf16[224,1024]{1,0:T(8,128)(2,1)} %bitcast.73), channel_id=1, source_target_pairs={{0,80},{8,88},{16,96},{24,104},{32,112},{40,120},{48,64},{56,72},{... | collective-permute-start | bytes 1376264 | tf_op jit(solution)/shard_map/ppermute | solution.py:56
  179.3 124.4 %collective-permute-start.40 = (bf16[224,1024]{1,0:T(8,128)(2,1)}, bf16[224,1024]{1,0:T(8,128)(2,1)}, u32[]{:S(2)}, u32[]{:S(2)}) collective-permute-start(bf16[224,1024]{1,0:T(8,128)(2,1)} %collective-permute-done.39), channel_id=1, source_target_pairs={{0,8},{8,0},{16,24},{24,16},{32,40},{40,32},{48,56},{56,48},{64,72... | collective-permute-start | bytes 1376264 | tf_op jit(solution)/shard_map/ppermute | solution.py:58
  289.1 52.1 %all-to-all-start.1 = ((bf16[16,224,64]{1,2,0:T(8,128)(2,1)}), bf16[16,224,64]{1,2,0:T(8,128)(2,1)S(1)}, u32[]{:S(2)}, u32[]{:S(2)}) async-start(bf16[16,224,64]{1,2,0:T(8,128)(2,1)} %copy.369), calls=%async_computation.1 | async-start | bytes 1048576 | tf_op jit(solution)/shard_map/all_to_all | solution.py:239
  541.5 41.9 %collective-permute-start.54 = (bf16[224,1024]{1,0:T(8,128)(2,1)}, bf16[224,1024]{1,0:T(8,128)(2,1)S(1)}, u32[]{:S(2)}, u32[]{:S(2)}) collective-permute-start(bf16[224,1024]{1,0:T(8,128)(2,1)} %get-tuple-element.438), channel_id=1, source_target_pairs={{0,48},{8,56},{16,0},{24,8},{32,16},{40,24},{48,32},{56,40},{64,11... | collective-permute-start | bytes 1376264 | tf_op jit(solution)/shard_map/ppermute | solution.py:71
  543.3 40.1 %collective-permute-start.55 = (bf16[224,1024]{1,0:T(8,128)(2,1)}, bf16[224,1024]{1,0:T(8,128)(2,1)}, u32[]{:S(2)}, u32[]{:S(2)}) collective-permute-start(bf16[224,1024]{1,0:T(8,128)(2,1)} %get-tuple-element.444), channel_id=1, source_target_pairs={{0,32},{8,40},{16,48},{24,56},{32,0},{40,8},{48,16},{56,24},{64,96... | collective-permute-start | bytes 1376264 | tf_op jit(solution)/shard_map/ppermute | solution.py:71
  548.8 52.6 %all-to-all-start.2 = ((f32[16,2,224]{2,1,0:T(2,128)}), f32[16,2,224]{2,1,0:T(2,128)S(1)}, u32[]{:S(2)}, u32[]{:S(2)}) async-start(f32[16,2,224]{2,1,0:T(2,128)} %broadcast_select_fusion.5), calls=%async_computation.2 | async-start | bytes 65536 | tf_op jit(solution)/shard_map/all_to_all | solution.py:301
  552.3 51.5 %collective-permute-start.56 = (bf16[224,1024]{1,0:T(8,128)(2,1)}, bf16[224,1024]{1,0:T(8,128)(2,1)}, u32[]{:S(2)}, u32[]{:S(2)}) collective-permute-start(bf16[224,1024]{1,0:T(8,128)(2,1)} %get-tuple-element.443), channel_id=1, source_target_pairs={{0,16},{8,24},{16,32},{24,40},{32,48},{40,56},{48,0},{56,8},{64,80... | collective-permute-start | bytes 1376264 | tf_op jit(solution)/shard_map/ppermute | solution.py:71
  554.4 51.1 %collective-permute-start.57 = (bf16[224,1024]{1,0:T(8,128)(2,1)}, bf16[224,1024]{1,0:T(8,128)(2,1)}, u32[]{:S(2)}, u32[]{:S(2)}) collective-permute-start(bf16[224,1024]{1,0:T(8,128)(2,1)} %get-tuple-element.442), channel_id=1, source_target_pairs={{0,64},{8,72},{16,80},{24,88},{32,96},{40,104},{48,112},{56,120},{... | collective-permute-start | bytes 1376264 | tf_op jit(solution)/shard_map/ppermute | solution.py:71
  557.1 51.4 %collective-permute-start.58 = (bf16[224,1024]{1,0:T(8,128)(2,1)}, bf16[224,1024]{1,0:T(8,128)(2,1)}, u32[]{:S(2)}, u32[]{:S(2)}) collective-permute-start(bf16[224,1024]{1,0:T(8,128)(2,1)} %get-tuple-element.441), channel_id=1, source_target_pairs={{0,112},{8,120},{16,64},{24,72},{32,80},{40,88},{48,96},{56,104},{... | collective-permute-start | bytes 1376264 | tf_op jit(solution)/shard_map/ppermute | solution.py:71
  612.8 31.9 %collective-permute-start.37 = (bf16[224,1024]{1,0:T(8,128)(2,1)}, bf16[224,1024]{1,0:T(8,128)(2,1)S(1)}, u32[]{:S(2)}, u32[]{:S(2)}) collective-permute-start(bf16[224,1024]{1,0:T(8,128)(2,1)} %get-tuple-element.446), channel_id=1, source_target_pairs={{0,80},{8,88},{16,96},{24,104},{32,112},{40,120},{48,64},{56,72},{... | collective-permute-start | bytes 1376264 | tf_op jit(solution)/shard_map/ppermute | solution.py:71
  656.6 376.1 %reduce-scatter.2.cloned.1.call-start = ((), (), s32[]{:S(2)}) async-start(), calls=%async_computation.8 | async-start | bytes 7077888 | tf_op jit(solution)/shard_map/reduce_scatter | solution.py:309
  910.6 36.1 %collective-permute-start.61 = (bf16[8,224,1024]{2,1,0:T(8,128)(2,1)}, bf16[8,224,1024]{2,1,0:T(8,128)(2,1)}, u32[]{:S(2)}, u32[]{:S(2)}) collective-permute-start(bf16[8,224,1024]{2,1,0:T(8,128)(2,1)} %slice_bitcast_fusion), channel_id=1, source_target_pairs={{0,8},{8,0},{16,24},{24,16},{32,40},{40,32},{48,56},{56,48},{64,72... | collective-permute-start | bytes 11010056 | tf_op jit(solution)/shard_map/ppermute | solution.py:65
  936.9 81.5 %all-to-all-start.5 = ((bf16[128,8,1152]{2,1,0:T(8,128)(2,1)}), bf16[128,8,1152]{2,1,0:T(8,128)(2,1)S(1)}, u32[]{:S(2)}, u32[]{:S(2)}) async-start(bf16[128,8,1152]{2,1,0:T(8,128)(2,1)} %copy.415), calls=%async_computation.5 | async-start | bytes 4718592 | tf_op jit(solution)/shard_map/all_to_all | solution.py:335
  958.2 40.9 %collective-permute-start.63 = (bf16[224,1024]{1,0:T(8,128)(2,1)}, bf16[224,1024]{1,0:T(8,128)(2,1)}, u32[]{:S(2)}, u32[]{:S(2)}) collective-permute-start(bf16[224,1024]{1,0:T(8,128)(2,1)} %get-tuple-element.437), channel_id=1, source_target_pairs={{0,32},{8,40},{16,48},{24,56},{32,0},{40,8},{48,16},{56,24},{64,96... | collective-permute-start | bytes 1376264 | tf_op jit(solution)/shard_map/ppermute | solution.py:71
  959.0 61.6 %collective-permute-start.64 = (bf16[224,1024]{1,0:T(8,128)(2,1)}, bf16[224,1024]{1,0:T(8,128)(2,1)}, u32[]{:S(2)}, u32[]{:S(2)}) collective-permute-start(bf16[224,1024]{1,0:T(8,128)(2,1)} %get-tuple-element.436), channel_id=1, source_target_pairs={{0,16},{8,24},{16,32},{24,40},{32,48},{40,56},{48,0},{56,8},{64,80... | collective-permute-start | bytes 1376264 | tf_op jit(solution)/shard_map/ppermute | solution.py:71
  960.2 60.4 %collective-permute-start.65 = (bf16[224,1024]{1,0:T(8,128)(2,1)}, bf16[224,1024]{1,0:T(8,128)(2,1)}, u32[]{:S(2)}, u32[]{:S(2)}) collective-permute-start(bf16[224,1024]{1,0:T(8,128)(2,1)} %get-tuple-element.435), channel_id=1, source_target_pairs={{0,64},{8,72},{16,80},{24,88},{32,96},{40,104},{48,112},{56,120},{... | collective-permute-start | bytes 1376264 | tf_op jit(solution)/shard_map/ppermute | solution.py:71
  963.2 57.4 %collective-permute-start.66 = (bf16[224,1024]{1,0:T(8,128)(2,1)}, bf16[224,1024]{1,0:T(8,128)(2,1)}, u32[]{:S(2)}, u32[]{:S(2)}) collective-permute-start(bf16[224,1024]{1,0:T(8,128)(2,1)} %get-tuple-element.434), channel_id=1, source_target_pairs={{0,112},{8,120},{16,64},{24,72},{32,80},{40,88},{48,96},{56,104},{... | collective-permute-start | bytes 1376264 | tf_op jit(solution)/shard_map/ppermute | solution.py:71
  983.4 37.3 %collective-permute-start.67 = (bf16[224,1024]{1,0:T(8,128)(2,1)}, bf16[224,1024]{1,0:T(8,128)(2,1)}, u32[]{:S(2)}, u32[]{:S(2)}) collective-permute-start(bf16[224,1024]{1,0:T(8,128)(2,1)} %get-tuple-element.433), channel_id=1, source_target_pairs={{0,96},{8,104},{16,112},{24,120},{32,64},{40,72},{48,80},{56,88},{... | collective-permute-start | bytes 1376264 | tf_op jit(solution)/shard_map/ppermute | solution.py:71
  999.1 29.5 %collective-permute-start.68 = (bf16[224,1024]{1,0:T(8,128)(2,1)}, bf16[224,1024]{1,0:T(8,128)(2,1)}, u32[]{:S(2)}, u32[]{:S(2)}) collective-permute-start(bf16[224,1024]{1,0:T(8,128)(2,1)} %get-tuple-element.432), channel_id=1, source_target_pairs={{0,80},{8,88},{16,96},{24,104},{32,112},{40,120},{48,64},{56,72},{... | collective-permute-start | bytes 1376264 | tf_op jit(solution)/shard_map/ppermute | solution.py:71
  (127 other events, 2414.6 us)
Sparse Core Ops, SparseCore 0:
  39.8 57.5 all-gather.3
  99.0 177.3 all-gather.5
  666.3 131.5 reduce-scatter.1

commit v2 on v1

v2 whole, which is shorter than its diff:
```python
import jax
import jax.numpy as jnp
from jax import lax
from jax.experimental import pallas as pl
from jax.experimental.pallas import tpu as pltpu
from jax.sharding import PartitionSpec as P

HEADS = 16
KV_HEADS = 8
HEAD_DIM = 64
EXPERTS = 32
FF = 512
PROMPT = 2048
GROUP = 3584
TOK = 224
HALF = TOK // 2
WIDTH = 1024
SLOTS = 72
STEP_ROWS = 4 * SLOTS
ALL_ROWS = 16 * SLOTS
BLOCK = 512

norm_eps = 1e-06
rope_base = 10000.0
masked_score = -1e30
BOTH = ("seq", "wshard")
NT = (((1,), (1,)), ((), ()))
TN = (((0,), (0,)), ((), ()))
f32 = jnp.float32
bf16 = jnp.bfloat16
i32 = jnp.int32


def place_of(x, z, core):
    return x * 8 + z * 2 + core


def shift_perm(a, b):
    return [
        (place_of(x, z, c), place_of(x ^ a, (z + b) % 4, c))
        for x in range(2)
        for z in range(4)
        for c in range(2)
    ]


CORE_PERM = [(i, i ^ 1) for i in range(16)]


def send(rows, a, b):
    return lax.ppermute(rows, "seq", shift_perm(a, b))


def swap_cores(rows):
    return lax.ppermute(rows, "seq", CORE_PERM)


def relative_places(seq_index):
    x, z, c = seq_index // 8, (seq_index // 2) % 4, seq_index % 2
    r = jnp.arange(16, dtype=i32)
    a, b, k = r // 8, (r // 2) % 4, r % 2
    return (a ^ x) * 8 + ((z - b) % 4) * 2 + (k ^ c)


def seq_gather(rows):
    near = [rows, send(rows, 0, 1), send(rows, 0, 2), send(rows, 0, 3)]
    across = send(rows, 1, 0)
    mine_near = jnp.stack(near)
    tops = [send(near[b][:HALF], 1, 0) for b in (1, 2, 3)]
    bottoms = [send(across[HALF:], 0, b) for b in (1, 2, 3)]
    far = [across] + [jnp.concatenate([t, u], axis=0) for t, u in zip(tops, bottoms)]
    mine_far = jnp.stack(far)
    return (mine_near, swap_cores(mine_near)), (mine_far, swap_cores(mine_far))


def add_low(*terms):
    return sum([t.astype(f32) for t in terms]).astype(bf16)


def seq_scatter_sum(near, far):
    near_other = swap_cores(near[1])
    far_other = swap_cores(far[1])
    own_near = [(near[0][b], near_other[b]) for b in range(4)]
    own_far = [(far[0][b], far_other[b]) for b in range(4)]
    low = slice(HALF, TOK)
    top = slice(0, HALF)
    near_low = [send(add_low(own_near[b][0][low], own_near[b][1][low]), 0, -b) for b in (1, 2, 3)]
    tops_far = add_low(far[0][:, top], far_other[:, top])
    tops_got = send(tops_far, 1, 0)
    far_low = [send(add_low(own_far[b][0][low], own_far[b][1][low]), 0, -b) for b in (1, 2, 3)]
    crossed = send(add_low(own_far[0][0][low], own_far[0][1][low], *far_low), 1, 0)
    tops = [
        send(add_low(own_near[b][0][top], own_near[b][1][top], tops_got[b]), 0, -b)
        for b in (1, 2, 3)
    ]
    own = [own_near[0][0].astype(f32), own_near[0][1].astype(f32)]
    upper = sum([t.astype(f32) for t in tops], own[0][top] + own[1][top] + tops_got[0].astype(f32))
    lower = sum([t.astype(f32) for t in near_low], own[0][low] + own[1][low] + crossed.astype(f32))
    return jnp.concatenate([upper, lower], axis=0)


def inverse_rms(values):
    return lax.rsqrt(jnp.mean(values * values, axis=-1, keepdims=True) + norm_eps)


def rms_pull(values, scale, gain, grad):
    scaled = grad * gain
    return scale * scaled - values * (scale * scale * scale) * jnp.mean(
        scaled * values, axis=-1, keepdims=True
    )


def group_layout(lengths):
    places = jnp.arange(GROUP, dtype=i32)
    ends = jnp.cumsum(lengths)
    starts = ends - lengths
    offset_in = places - PROMPT
    segment_id = jnp.sum((offset_in[:, None] >= ends[None, :]).astype(i32), axis=1)
    segment_hot = segment_id[:, None] == jnp.arange(lengths.shape[0], dtype=i32)[None, :]
    begin = jnp.sum(jnp.where(segment_hot, starts[None, :], 0), axis=1)
    inside = offset_in >= 0
    position = jnp.where(inside, PROMPT + offset_in - begin, places)
    return position, jnp.where(inside, PROMPT + begin, 0)


def rotary_tables(position):
    half_dim = HEAD_DIM // 2
    inverse = rope_base ** (-(jnp.arange(half_dim, dtype=f32) * 2.0) / HEAD_DIM)
    angles = position[:, None] * inverse[None, :]
    cosine, sine = jnp.cos(angles), jnp.sin(angles)
    return (
        jnp.concatenate([cosine, cosine], axis=-1),
        jnp.concatenate([sine, sine], axis=-1),
    )


def turn(values):
    half_dim = HEAD_DIM // 2
    return jnp.concatenate([-values[:, half_dim:], values[:, :half_dim]], axis=-1)


def turn_back(values):
    half_dim = HEAD_DIM // 2
    return jnp.concatenate([values[:, half_dim:], -values[:, :half_dim]], axis=-1)


def project_kernel(places, mine, other, w, gain, cosine, sine, *refs):
    del places
    normed_ref, q_ref, k_ref, v_ref = refs[-4:]
    rows = jnp.where(pl.program_id(1) == 0, mine[0], other[0])
    values = rows.astype(f32)
    normed = (values * inverse_rms(values) * gain[...]).astype(bf16)
    normed_ref[0] = normed
    projected = jnp.dot(normed, w[...], preferred_element_type=f32)
    c, s = cosine[...], sine[...]
    q, k, v = projected[:, :64], projected[:, 64:128], projected[:, 128:192]
    q_ref[...] = ((q * c + turn(q) * s).astype(bf16).astype(f32) * HEAD_DIM**-0.5).astype(bf16)
    k_ref[...] = (k * c + turn(k) * s).astype(bf16)
    v_ref[...] = v.astype(bf16)


def project(places, gathered, w, gain, cosine, sine, before):
    chip = pl.BlockSpec((1, TOK, WIDTH), lambda j, k, p: (j, 0, 0))
    whole = lambda shape: pl.BlockSpec(shape, lambda j, k, p: (0,) * len(shape))
    at = pl.BlockSpec((TOK, HEAD_DIM), lambda j, k, p: (p[2 * j + k], 0))
    table = jax.ShapeDtypeStruct((GROUP, HEAD_DIM), bf16)
    return pl.pallas_call(
        project_kernel,
        grid_spec=pltpu.PrefetchScalarGridSpec(
            num_scalar_prefetch=1,
            grid=(4, 2),
            in_specs=[chip, chip, whole((WIDTH, 256)), whole((1, WIDTH)), at, at]
            + [pl.BlockSpec(memory_space=pl.ANY)] * len(before),
            out_specs=[pl.BlockSpec((1, TOK, WIDTH), lambda j, k, p: (2 * j + k, 0, 0)), at, at, at],
        ),
        out_shape=[jax.ShapeDtypeStruct((8, TOK, WIDTH), bf16), table, table, table],
        input_output_aliases={7 + i: 1 + i for i in range(len(before))},
        compiler_params=pltpu.CompilerParams(vmem_limit_bytes=32 << 20),
        cost_estimate=pl.CostEstimate(
            flops=2 * 8 * TOK * WIDTH * 256, bytes_accessed=10 << 20, transcendentals=0
        ),
    )(places, *gathered, w, gain, cosine, sine, *before)


def project_back_kernel(places, normed, dq, dk, dv, w, cosine, sine, *refs):
    del places
    mine, other, grad = refs[-3:]
    first = (pl.program_id(0) == 0) & (pl.program_id(1) == 0)

    @pl.when(first)
    def _():
        grad[...] = jnp.zeros_like(grad) if len(refs) == 3 else refs[0][...]

    c, s = cosine[...], sine[...]
    q = dq[...].astype(bf16).astype(f32)
    k = dk[...].astype(bf16).astype(f32)
    projected = jnp.concatenate(
        [q * c + turn_back(q * s), k * c + turn_back(k * s), dv[...], jnp.zeros_like(q)], axis=1
    ).astype(bf16)
    grad[...] += lax.dot_general(normed[0], projected, TN, preferred_element_type=f32)
    part = lax.dot_general(projected, w[...], NT, preferred_element_type=f32).astype(bf16)

    @pl.when(pl.program_id(1) == 0)
    def _():
        mine[0] = part

    @pl.when(pl.program_id(1) == 1)
    def _():
        other[0] = part


def project_back(places, normed, grads, w, cosine, sine, before):
    chip = pl.BlockSpec((1, TOK, WIDTH), lambda j, k, p: (j, 0, 0))
    whole = lambda shape: pl.BlockSpec(shape, lambda j, k, p: (0,) * len(shape))
    at = pl.BlockSpec((TOK, HEAD_DIM), lambda j, k, p: (p[2 * j + k], 0))
    part = jax.ShapeDtypeStruct((4, TOK, WIDTH), bf16)
    return pl.pallas_call(
        project_back_kernel,
        grid_spec=pltpu.PrefetchScalarGridSpec(
            num_scalar_prefetch=1,
            grid=(4, 2),
            in_specs=[
                pl.BlockSpec((1, TOK, WIDTH), lambda j, k, p: (2 * j + k, 0, 0)),
                at,
                at,
                at,
                whole((WIDTH, 256)),
                at,
                at,
            ]
            + [whole((WIDTH, 256))] * len(before),
            out_specs=[chip, chip, whole((WIDTH, 256))],
        ),
        out_shape=[part, part, jax.ShapeDtypeStruct((WIDTH, 256), f32)],
        compiler_params=pltpu.CompilerParams(vmem_limit_bytes=32 << 20),
        cost_estimate=pl.CostEstimate(
            flops=4 * 8 * TOK * WIDTH * 256, bytes_accessed=12 << 20, transcendentals=0
        ),
    )(places, normed, *grads, w, cosine, sine, *before)


def tile_mask(scores, key_start, query_start, begin):
    keys = key_start + lax.broadcasted_iota(i32, scores.shape, 0)
    queries = query_start + lax.broadcasted_iota(i32, scores.shape, 1)
    return jnp.where((keys <= queries) & (keys >= begin), scores, masked_score)


def key_ranges(i):
    first = PROMPT // BLOCK
    return jnp.where(i > first, i - 1, i), jnp.minimum(i, first)


def attend_kernel(q_ref, k_ref, v_ref, begin_ref, o_ref, ot_ref, lse_ref, vt):
    i = pl.program_id(0)

    @pl.when(i == 0)
    def _():
        vt[...] = v_ref[...].T

    q = q_ref[...]
    begin = begin_ref[...]

    def tile(j, carry, masked):
        peak, total, out = carry
        start = pl.multiple_of(j * BLOCK, BLOCK)
        at = pl.ds(start, BLOCK)
        s = lax.dot_general(k_ref[at, :], q, NT, preferred_element_type=f32)
        if masked:
            s = tile_mask(s, start, i * BLOCK, begin)
        higher = jnp.maximum(peak, jnp.max(s, axis=0, keepdims=True))
        p = jnp.exp(s - higher)
        fade = jnp.exp(peak - higher)
        total = total * fade + jnp.sum(p, axis=0, keepdims=True)
        out = out * fade + jnp.dot(vt[:, at], p.astype(bf16), preferred_element_type=f32)
        return higher, total, out

    carry = (
        jnp.full((1, BLOCK), masked_score, f32),
        jnp.zeros((1, BLOCK), f32),
        jnp.zeros((HEAD_DIM, BLOCK), f32),
    )
    carry = tile(i, carry, True)
    window, shared = key_ranges(i)
    carry = lax.fori_loop(window, i, lambda j, c: tile(j, c, True), carry)
    peak, total, out = lax.fori_loop(0, shared, lambda j, c: tile(j, c, False), carry)
    out = out * (1.0 / total)
    ot_ref[...] = out
    o_ref[...] = out.T.astype(bf16)
    lse_ref[...] = peak + jnp.log(total)


def attend(q, k, v, begin):
    whole = pl.BlockSpec((GROUP, HEAD_DIM), lambda i: (0, 0))
    rows = pl.BlockSpec((BLOCK, HEAD_DIM), lambda i: (i, 0))
    cols = lambda n: pl.BlockSpec((n, BLOCK), lambda i: (0, i))
    return pl.pallas_call(
        attend_kernel,
        grid=(GROUP // BLOCK,),
        in_specs=[rows, whole, whole, cols(1)],
        out_specs=[rows, cols(HEAD_DIM), cols(1)],
        out_shape=[
            jax.ShapeDtypeStruct((GROUP, HEAD_DIM), bf16),
            jax.ShapeDtypeStruct((HEAD_DIM, GROUP), f32),
            jax.ShapeDtypeStruct((1, GROUP), f32),
        ],
        scratch_shapes=[pltpu.VMEM((HEAD_DIM, GROUP), bf16)],
        compiler_params=pltpu.CompilerParams(vmem_limit_bytes=32 << 20),
        cost_estimate=pl.CostEstimate(
            flops=2 * 27 * BLOCK * BLOCK * 512, bytes_accessed=4 << 20, transcendentals=27 * BLOCK * BLOCK
        ),
    )(q, k, v, begin)


def attend_back_kernel(
    q_ref, k_ref, v_ref, g_ref, ot_ref, lse_ref, begin_ref, dq_ref, dk_ref, dv_ref, kt
):
    i = pl.program_id(0)

    @pl.when(i == 0)
    def _():
        dk_ref[...] = jnp.zeros_like(dk_ref)
        dv_ref[...] = jnp.zeros_like(dv_ref)
        kt[...] = k_ref[...].T

    q = q_ref[...]
    g = g_ref[...]
    begin = begin_ref[...]
    lse = lse_ref[...]
    inner = jnp.sum(g.T.astype(f32) * ot_ref[...], axis=0, keepdims=True)

    def tile(j, dq, masked):
        start = pl.multiple_of(j * BLOCK, BLOCK)
        at = pl.ds(start, BLOCK)
        s = lax.dot_general(k_ref[at, :], q, NT, preferred_element_type=f32)
        if masked:
            s = tile_mask(s, start, i * BLOCK, begin)
        p = jnp.exp(s - lse)
        dp = lax.dot_general(v_ref[at, :], g, NT, preferred_element_type=f32)
        ds = (p * (dp - inner)).astype(bf16)
        dv_ref[at, :] += jnp.dot(p.astype(bf16), g, preferred_element_type=f32)
        dk_ref[at, :] += jnp.dot(ds, q, preferred_element_type=f32)
        return dq + jnp.dot(kt[:, at], ds, preferred_element_type=f32)

    dq = tile(i, jnp.zeros((HEAD_DIM, BLOCK), f32), True)
    window, shared = key_ranges(i)
    dq = lax.fori_loop(window, i, lambda j, c: tile(j, c, True), dq)
    dq = lax.fori_loop(0, shared, lambda j, c: tile(j, c, False), dq)
    dq_ref[...] = dq.T * HEAD_DIM**-0.5


def attend_back(q, k, v, g, ot, lse, begin):
    whole = pl.BlockSpec((GROUP, HEAD_DIM), lambda i: (0, 0))
    rows = pl.BlockSpec((BLOCK, HEAD_DIM), lambda i: (i, 0))
    cols = lambda n: pl.BlockSpec((n, BLOCK), lambda i: (0, i))
    out = jax.ShapeDtypeStruct((GROUP, HEAD_DIM), f32)
    return pl.pallas_call(
        attend_back_kernel,
        grid=(GROUP // BLOCK,),
        in_specs=[rows, whole, whole, rows, cols(HEAD_DIM), cols(1), cols(1)],
        out_specs=[rows, whole, whole],
        out_shape=[out, out, out],
        scratch_shapes=[pltpu.VMEM((HEAD_DIM, GROUP), bf16)],
        compiler_params=pltpu.CompilerParams(vmem_limit_bytes=48 << 20),
        cost_estimate=pl.CostEstimate(
            flops=5 * 27 * BLOCK * BLOCK * 512, bytes_accessed=8 << 20, transcendentals=27 * BLOCK * BLOCK
        ),
    )(q, k, v, g, ot, lse, begin)


def experts_kernel(
    own_ref, ffn_mine, ffn_other, g_mine, g_other, w_ref, router_ref, chosen_ref, slots_ref, slot_cols_ref, *refs
):
    routed_mine, routed_other, moved_mine, moved_other, gate_grad_ref = refs[-9:-4]
    x_ref, dh_ref, act_ref, dy_ref = refs[-4:]
    own = own_ref[0]
    expert_rows = lax.broadcasted_iota(i32, (EXPERTS, TOK), 0)
    slot_rows = lax.broadcasted_iota(i32, (SLOTS, TOK), 0)
    gate_rows = [[], []]
    picks = [[], []]
    picked_rows = [[], []]
    picked_grads = [[], []]
    blocks = [(ffn_mine, g_mine, 0), (ffn_other, g_other, 0), (ffn_mine, g_mine, 1), (ffn_other, g_other, 1)]
    for b, (rows_ref, grads_ref, n) in enumerate(blocks):
        rows, grads = rows_ref[n], grads_ref[n]
        chosen = chosen_ref[b] > 0
        logits = lax.dot_general(router_ref[...], rows, NT, preferred_element_type=f32)
        peak = jnp.max(jnp.where(chosen, logits, masked_score), axis=0, keepdims=True)
        raised = jnp.where(chosen, jnp.exp(jnp.minimum(logits - peak, 0.0)), 0.0)
        gates = raised / jnp.sum(raised, axis=0, keepdims=True)
        for e in range(2):
            gate_rows[e].append(
                jnp.sum(jnp.where(expert_rows == own + e, gates, 0.0), axis=0, keepdims=True)
            )
            pick = (slots_ref[b, e : e + 1, :] == slot_rows).astype(f32)
            picks[e].append(pick)
            low = pick.astype(bf16)
            picked_rows[e].append(jnp.dot(low, rows, preferred_element_type=f32))
            picked_grads[e].append(jnp.dot(low, grads, preferred_element_type=f32))
    moved, routed = [], []
    for e in range(2):
        w_gate_up = w_ref[:, e, :128, :].reshape(WIDTH, 2 * FF)
        w_down = w_ref[:, e, 128:, :].reshape(FF, WIDTH)
        x = jnp.concatenate(picked_rows[e], axis=0).astype(bf16)
        gate = jnp.concatenate(
            [jnp.sum(p * r, axis=1, keepdims=True) for p, r in zip(picks[e], gate_rows[e])], axis=0
        )
        grads = jnp.concatenate(picked_grads[e], axis=0)
        dy = (gate * grads).astype(bf16)
        mixed = jnp.dot(x, w_gate_up, preferred_element_type=f32)
        dact = lax.dot_general(dy, w_down, NT, preferred_element_type=f32)
        gate_part, up_part = mixed[:, :FF], mixed[:, FF:]
        sigma = 1.0 / (1.0 + jnp.exp(-gate_part))
        silu = gate_part * sigma
        act = (silu * up_part).astype(bf16)
        dh = jnp.concatenate(
            [dact * up_part * (sigma + silu * (1.0 - sigma)), dact * silu], axis=1
        ).astype(bf16)
        x_ref[e] = x
        dy_ref[e] = dy
        act_ref[e] = act
        dh_ref[e] = dh
        returned = jnp.dot(act, w_down, preferred_element_type=f32).astype(bf16).astype(f32)
        dgate = jnp.sum(returned * grads, axis=1, keepdims=True)
        for b in range(4):
            gate_grad_ref[b, e : e + 1, :] = jnp.sum(
                picks[e][b] * dgate[b * SLOTS : (b + 1) * SLOTS], axis=0, keepdims=True
            )
        moved.append(gate * returned)
        routed.append(lax.dot_general(dh, w_gate_up, NT, preferred_element_type=f32))
    columns = lax.broadcasted_iota(i32, (TOK, 2 * SLOTS), 1)
    outs = [(routed_mine, moved_mine, 0), (routed_other, moved_other, 0), (routed_mine, moved_mine, 1), (routed_other, moved_other, 1)]
    for b, (routed_ref, moved_ref, n) in enumerate(outs):
        first, second = slot_cols_ref[b, :, 0:1], slot_cols_ref[b, :, 1:2]
        back = ((columns == first) | ((columns == second + SLOTS) & (second >= 0))).astype(f32).astype(bf16)
        at = slice(b * SLOTS, (b + 1) * SLOTS)
        for terms, ref in ((routed, routed_ref), (moved, moved_ref)):
            joined = jnp.concatenate([terms[0][at], terms[1][at]], axis=0).astype(bf16)
            ref[n] = jnp.dot(back, joined, preferred_element_type=f32).astype(bf16)


def run_experts(half, own, ffn, grads, weights, router, chosen, slots, slot_cols, before):
    pair = pl.BlockSpec((2, TOK, WIDTH), lambda i, o: (i, 0, 0))
    whole = lambda shape: pl.BlockSpec(shape, lambda i, o: (0,) * len(shape))
    four = lambda *shape: pl.BlockSpec((4, *shape), lambda i, o: (i + 2 * half, 0, 0))
    kept = lambda n: pl.BlockSpec((2, STEP_ROWS, n), lambda i, o: (0, i + 2 * half, 0))
    part = jax.ShapeDtypeStruct((4, TOK, WIDTH), bf16)
    keep = lambda n: jax.ShapeDtypeStruct((2, ALL_ROWS, n), bf16)
    return pl.pallas_call(
        experts_kernel,
        grid_spec=pltpu.PrefetchScalarGridSpec(
            num_scalar_prefetch=1,
            grid=(2,),
            in_specs=[
                pair,
                pair,
                pair,
                pair,
                whole((8, 2, 192, 1024)),
                whole((EXPERTS, WIDTH)),
                four(EXPERTS, TOK),
                four(2, TOK),
                four(TOK, 2),
            ]
            + [pl.BlockSpec(memory_space=pl.ANY)] * len(before),
            out_specs=[
                pair,
                pair,
                pair,
                pair,
                pl.BlockSpec((4, 2, TOK), lambda i, o: (i, 0, 0)),
                kept(WIDTH),
                kept(2 * FF),
                kept(FF),
                kept(WIDTH),
            ],
        ),
        out_shape=[
            part,
            part,
            part,
            part,
            jax.ShapeDtypeStruct((8, 2, TOK), f32),
            keep(WIDTH),
            keep(2 * FF),
            keep(FF),
            keep(WIDTH),
        ],
        input_output_aliases={10 + i: 5 + i for i in range(len(before))},
        compiler_params=pltpu.CompilerParams(vmem_limit_bytes=60 << 20),
        cost_estimate=pl.CostEstimate(
            flops=14 << 30, bytes_accessed=24 << 20, transcendentals=8 * SLOTS * 2 * FF
        ),
    )(own, *ffn, *grads, weights, router, chosen, slots, slot_cols, *before)


def expert_grads_kernel(x_ref, dh_ref, act_ref, dy_ref, out_ref):
    up = lax.dot_general(x_ref[0], dh_ref[0], TN, preferred_element_type=f32)
    down = lax.dot_general(act_ref[0], dy_ref[0], TN, preferred_element_type=f32)
    out_ref[:, 0, :128, :] = up.astype(bf16).reshape(2, 128, 2 * FF)
    out_ref[:, 0, 128:, :] = down.astype(bf16).reshape(2, 64, WIDTH)


def expert_weight_grads(x, dh, act, dy):
    return pl.pallas_call(
        expert_grads_kernel,
        grid=(2, 4),
        in_specs=[
            pl.BlockSpec((1, ALL_ROWS, 256), lambda e, i: (e, 0, i)),
            pl.BlockSpec((1, ALL_ROWS, 2 * FF), lambda e, i: (e, 0, 0)),
            pl.BlockSpec((1, ALL_ROWS, 128), lambda e, i: (e, 0, i)),
            pl.BlockSpec((1, ALL_ROWS, WIDTH), lambda e, i: (e, 0, 0)),
        ],
        out_specs=pl.BlockSpec((2, 1, 192, 1024), lambda e, i: (i, e, 0, 0)),
        out_shape=jax.ShapeDtypeStruct((8, 2, 192, 1024), bf16),
        compiler_params=pltpu.CompilerParams(vmem_limit_bytes=48 << 20),
        cost_estimate=pl.CostEstimate(flops=8 << 30, bytes_accessed=14 << 20, transcendentals=0),
    )(x, dh, act, dy)


def local(
    tokens,
    routes,
    cont_lengths,
    norm_attn,
    w_qkv,
    w_out,
    w_router,
    norm_ffn,
    w_gate_up,
    w_down,
    cotangent,
):
    seq_index = lax.axis_index("seq")
    places = relative_places(seq_index)
    rows = tokens[0]
    query_width = HEADS * HEAD_DIM
    kv_width = KV_HEADS * HEAD_DIM

    rows_all = seq_gather(rows)
    kv_heads = lambda start: jnp.repeat(
        w_qkv[:, start : start + kv_width].reshape(8, KV_HEADS, HEAD_DIM), 2, axis=1
    )
    head_cols = jnp.concatenate(
        [
            w_qkv[:, :query_width].reshape(8, HEADS, HEAD_DIM),
            kv_heads(query_width),
            kv_heads(query_width + kv_width),
            jnp.broadcast_to(norm_attn[:, None, None], (8, HEADS, HEAD_DIM)),
        ],
        axis=2,
    ).transpose(1, 0, 2)
    head_cols = jnp.broadcast_to(head_cols[:, None], (HEADS, 8, 8, 256)).reshape(128, 8, 256)
    head_weights = lax.all_to_all(head_cols, BOTH, 0, 0, tiled=True).reshape(WIDTH, 256)
    gain_attn = head_weights[:, 192].astype(f32)[None]
    head_weights = jnp.where(jnp.arange(256)[None] < 192, head_weights, 0.0).astype(bf16)

    routes_t = jnp.broadcast_to(routes[0].T[None], (16, 8, TOK))
    routes_all = jnp.take(lax.all_to_all(routes_t, "seq", 0, 0, tiled=True), places, axis=0)

    shared = jnp.concatenate(
        [w_out, w_router, norm_ffn[:, None], jnp.zeros((8, 95), bf16)], axis=1
    )
    shared = lax.all_to_all(
        jnp.broadcast_to(shared[None], (128, 8, 1152)), BOTH, 0, 0, tiled=True
    ).reshape(WIDTH, 1152)
    weight_out = shared[:, :WIDTH]
    weight_router = shared[:, WIDTH : WIDTH + EXPERTS]
    gain_ffn = shared[:, WIDTH + EXPERTS].astype(f32)

    expert_rows = jnp.concatenate([w_gate_up, w_down], axis=1)
    experts = lax.all_to_all(
        jnp.broadcast_to(expert_rows[None], (8, 2, 192, 1024)), "wshard", 0, 0, tiled=True
    )

    position, begin = group_layout(cont_lengths[0])
    begin = begin[None]
    cosine, sine = rotary_tables(position.astype(f32))

    expert_range = jnp.arange(EXPERTS, dtype=i32)
    chosen = jnp.any(routes_all[:, None] == expert_range[None, :, None, None], axis=2)
    own_first = seq_index * 2
    chosen_own = jnp.any(
        routes_all[:, None] == (own_first + jnp.arange(2, dtype=i32))[None, :, None, None], axis=2
    )
    upto = (jnp.arange(TOK)[:, None] <= jnp.arange(TOK)[None, :]).astype(bf16)
    rank = jnp.einsum("bet,tu->beu", chosen_own.astype(bf16), upto, preferred_element_type=f32)
    slots = jnp.where(chosen_own, rank.astype(i32) - 1, -1)
    slot_cols = slots.transpose(0, 2, 1)
    chosen = chosen.astype(f32)

    normed_near, *qkv = project(places[:8], rows_all[0], head_weights, gain_attn, cosine, sine, ())
    normed_far, q, k, v = project(places[8:], rows_all[1], head_weights, gain_attn, cosine, sine, qkv)
    attended_head, attended_t, lse = attend(q, k, v, begin)
    attended = lax.all_to_all(attended_head.reshape(16, TOK, HEAD_DIM), "seq", 0, 0, tiled=True)
    attended = attended.transpose(1, 0, 2).reshape(TOK, query_width)
    inputs = rows.astype(f32)
    hidden = inputs + jnp.dot(attended, weight_out, preferred_element_type=f32)
    hidden_scale = inverse_rms(hidden)
    normed_ffn = (hidden * hidden_scale * gain_ffn).astype(bf16)

    grad_all = seq_gather(cotangent[0])
    ffn_all = seq_gather(normed_ffn)
    router_t = weight_router.T
    own = own_first[None]
    near = run_experts(
        0, own, ffn_all[0], grad_all[0], experts, router_t, chosen, slots, slot_cols, ()
    )
    far = run_experts(
        1, own, ffn_all[1], grad_all[1], experts, router_t, chosen, slots, slot_cols, near[5:]
    )
    routed_grad = seq_scatter_sum(near[:2], far[:2])
    token_gate_grad = jnp.take(jnp.concatenate([near[4], far[4]], axis=0), places, axis=0)
    gate_grad = lax.all_to_all(token_gate_grad, "seq", 0, 0, tiled=True).reshape(EXPERTS, TOK).T
    expert_grads = lax.all_to_all(expert_weight_grads(*far[5:]), "wshard", 0, 0, tiled=True)
    expert_grads = jnp.sum(expert_grads.astype(f32), axis=0)

    chosen_here = jnp.any(routes[0][:, :, None] == expert_range, axis=1)
    logits = jnp.dot(normed_ffn, weight_router, preferred_element_type=f32)
    peak = jnp.max(jnp.where(chosen_here, logits, -jnp.inf), axis=-1, keepdims=True)
    raised = jnp.where(chosen_here, jnp.exp(logits - peak), 0.0)
    gates = raised / jnp.sum(raised, axis=-1, keepdims=True)
    chosen_grad = gates * (gate_grad - jnp.sum(gates * gate_grad, axis=-1, keepdims=True))
    logit_grad = chosen_grad.astype(bf16)
    normed_ffn_grad = routed_grad + jnp.einsum(
        "te,de->td", logit_grad, weight_router, preferred_element_type=f32
    )
    upstream = cotangent[0].astype(f32)
    hidden_grad = upstream + rms_pull(hidden, hidden_scale, gain_ffn, normed_ffn_grad)
    branch_grad = hidden_grad.astype(bf16)
    attended_grad = jnp.einsum(
        "td,qd->tq", branch_grad, weight_out, preferred_element_type=f32
    ).astype(bf16)
    head_grad = lax.all_to_all(
        attended_grad.reshape(TOK, HEADS, HEAD_DIM).transpose(1, 0, 2), "seq", 0, 0, tiled=True
    ).reshape(GROUP, HEAD_DIM)

    grad_router = jnp.einsum("td,te->de", normed_ffn, logit_grad, preferred_element_type=f32)
    grad_norm_ffn = jnp.sum(normed_ffn_grad * hidden * hidden_scale, axis=0)
    grad_out = jnp.einsum("tq,td->qd", attended, branch_grad, preferred_element_type=f32)
    shared_grads = jnp.concatenate(
        [grad_out, grad_router, grad_norm_ffn[:, None], jnp.zeros((WIDTH, 95), f32)], axis=1
    ).astype(bf16)
    shared_grads = jnp.sum(
        lax.all_to_all(shared_grads.reshape(128, 8, 1152), BOTH, 0, 0, tiled=True).astype(f32),
        axis=0,
    )
    output = (hidden + seq_scatter_sum(near[2:4], far[2:4])).astype(bf16)

    grads = attend_back(q, k, v, head_grad, attended_t, lse, begin)
    *near_part, grad_head = project_back(
        places[:8], normed_near, grads, head_weights, cosine, sine, ()
    )
    *far_part, grad_head = project_back(
        places[8:], normed_far, grads, head_weights, cosine, sine, (grad_head,)
    )
    normed_grad = seq_scatter_sum(near_part, far_part)
    grad_heads = jnp.sum(
        lax.all_to_all(grad_head.astype(bf16).reshape(128, 8, 256), BOTH, 0, 0, tiled=True)
        .reshape(16, 8, 8, 256)
        .astype(f32),
        axis=1,
    ).transpose(1, 0, 2)
    kv_sum = lambda start: jnp.sum(
        grad_heads[:, :, start : start + HEAD_DIM].reshape(8, KV_HEADS, 2, HEAD_DIM), axis=2
    ).reshape(8, kv_width)
    grad_qkv = jnp.concatenate(
        [grad_heads[:, :, :HEAD_DIM].reshape(8, query_width), kv_sum(HEAD_DIM), kv_sum(2 * HEAD_DIM)],
        axis=1,
    )
    grad_norm_attn = jnp.sum(grad_qkv * w_qkv.astype(f32), axis=1) / norm_attn.astype(f32)
    grad_input = hidden_grad + rms_pull(inputs, inverse_rms(inputs), gain_attn, normed_grad)
    return (
        output[None],
        grad_input[None],
        grad_norm_attn,
        grad_qkv,
        shared_grads[:, :WIDTH],
        shared_grads[:, WIDTH : WIDTH + EXPERTS],
        shared_grads[:, WIDTH + EXPERTS],
        expert_grads[:, :128],
        expert_grads[:, 128:],
    )


def solution(mesh):
    return jax.shard_map(
        local,
        mesh=mesh,
        in_specs=(
            P("wshard", "seq", None),
            P("wshard", "seq", None),
            P("wshard", None),
            P(BOTH),
            P(BOTH, None),
            P(BOTH, None),
            P(BOTH, None),
            P(BOTH),
            P("seq", "wshard", None),
            P("seq", "wshard", None),
            P("wshard", "seq", None),
        ),
        out_specs=(
            P("wshard", "seq", None),
            P("wshard", "seq", None),
            P(BOTH),
            P(BOTH, None),
            P(BOTH, None),
            P(BOTH, None),
            P(BOTH),
            P("seq", "wshard", None),
            P("seq", "wshard", None),
        ),
        check_vma=False,
    )
```

time: 1050 us -> 741 us (0.71)
  matrix products: 249 us -> 13 us
  Pallas kernels: 0 us -> 136 us
  local copies, waits for them, and re-layouts: 204 us -> 72 us
  waiting for transfers between devices: 179 us -> 255 us
  other arithmetic: 134 us -> 83.2 us
  loops' own time: 40.4 us -> 0 us
  blocking collectives: 55.9 us -> 17.2 us
  between operations: 15.4 us -> 2.07 us
  starting transfers between devices: 165 us -> 154 us
    dot_general x63 -> x2, matrix products: 240 us -> 1.5 us  [the longest x1 1.36 us: local(): logits = jnp.dot(normed_ffn, weight_router, preferred_element_type=f32)]
    pallas_call x0 -> x9, Pallas kernels: none -> 136 us  [the longest x2 44.8 us: run_experts(): pl.pallas_call(experts_kernel, grid_spec=pltpu.PrefetchScalarGridSpec(num...]
    all_gather x2 -> x0, blocking collectives: 55.9 us -> none  [the longest x1 30.9 us: local(): shared = lax.all_gather(shared, 'wshard', axis=0, tiled=True)]
    unnamed x170 -> x122, local copies, waits for them, and re-layouts: 71.6 us -> 24.9 us
    another operation x2 -> x0, loops' own time: 40.4 us -> none  [the longest x1 25.6 us: attention_forward(): out, peak, total = lax.map(block, offsets)]
    convert_element_type x16 -> x22, other arithmetic: 70.6 us -> 31.1 us  [the longest x12 19.7 us: add_low(): return sum([t.astype(f32) for t in terms]).astype(bf16)]
    ppermute x69 -> x75, waiting for transfers between devices: 176 us -> 213 us  [the longest x63 212 us: send(): return lax.ppermute(rows, 'seq', shift_perm(a, b))]
    ppermute x69 -> x75, starting transfers between devices: 125 us -> 98.2 us  [the longest x63 95.8 us: send(): return lax.ppermute(rows, 'seq', shift_perm(a, b))]
  transfers between devices with their start and end apart: 78 -> 84, of which waited for: 22 -> 32; matrix products, arithmetic and copies ran while one was open for 46% -> 18% of each run, Pallas kernels for 0% -> 10%
where the time goes in v2:
time: 741 us; the launch traced here: 732 us
  waiting for transfers between devices  255 us (34%)
  starting transfers between devices  154 us (21%)
  Pallas kernels  136 us (18%)
  other arithmetic  83.2 us (11%)
  local copies, waits for them, and re-layouts  72 us (10%)
  blocking collectives  17.2 us (2%)
  matrix products  13 us (2%)
    ppermute x63, waiting for transfers between devices, send(): return lax.ppermute(rows, 'seq', shift_perm(a, b))  212 us
    ppermute x63, starting transfers between devices, send(): return lax.ppermute(rows, 'seq', shift_perm(a, b))  95.8 us
    pallas_call x2, Pallas kernels, run_experts(): pl.pallas_call(experts_kernel, grid_spec=pltpu.PrefetchScalarGridSpec(num...  44.8 us
    pallas_call x1, Pallas kernels, attend_back(): pl.pallas_call(attend_back_kernel, grid=(GROUP // BLOCK,), in_specs=[rows...  26.1 us
    unnamed x122, local copies, waits for them, and re-layouts  24.9 us
    pallas_call x1, Pallas kernels, attend(): pl.pallas_call(attend_kernel, grid=(GROUP // BLOCK,), in_specs=[rows, who...  19.7 us
    convert_element_type x12, other arithmetic, add_low(): return sum([t.astype(f32) for t in terms]).astype(bf16)  19.7 us
    all_to_all x1, blocking collectives, local(): lax.all_to_all(attended_grad.reshape(TOK, HEADS, HEAD_DIM).transpose(1, 0...  17.2 us
  transfers between devices with their start and end apart: 84, of which 32 were waited for; matrix products, arithmetic and copies ran while one was open for 18% of the time, Pallas kernels for 10%

profile of v2, /device:TPU:0, one launch (start us, length us, event | category | flops | bytes accessed | tf_op | source)
XLA Modules:
  0.0 731.8 jit_solution(16302279821057788255)
XLA Ops:
  17.0 8.2 %multiply_sine_fusion = (f32[3584,32]{1,0:T(8,128)}, f32[3584,32]{1,0:T(8,128)}) fusion(f32[32]{0:T(128)S(1)} %multiply_power_fusion, f32[3584]{0:T(1024)S(1)} %get-tuple-element.133), kind=kLoop, calls=%fused_computation.6 | loop fusion | flops 114688 | bytes 931968 | tf_op jit(solution)/shard_map/sin | solution.py:130
  45.8 8.5 %all-to-all-start = ((bf16[128,8,256]{2,1,0:T(8,128)(2,1)}), bf16[128,8,256]{2,1,0:T(8,128)(2,1)S(1)}, u32[]{:S(2)}, u32[]{:S(2)}) async-start(bf16[128,8,256]{2,1,0:T(8,128)(2,1)} %bitcast.8), calls=%async_computation | async-start | bytes 1048576 | tf_op jit(solution)/shard_map/all_to_all | solution.py:553
  56.1 11.7 %all-to-all-done = bf16[128,8,256]{2,1,0:T(8,128)(2,1)S(1)} async-done(((bf16[128,8,256]{2,1,0:T(8,128)(2,1)}), bf16[128,8,256]{2,1,0:T(8,128)(2,1)S(1)}, u32[]{:S(2)}, u32[]{:S(2)}) %all-to-all-start) | async-done | bytes 524320 | tf_op jit(solution)/shard_map/all_to_all | solution.py:553
  69.4 5.9 all-to-all-start.2
  75.3 4.3 pad_maximum_fusion.1
  79.9 8.6 %shard_map.178 = (bf16[8,224,1024]{2,1,0:T(8,128)(2,1)S(1)}, bf16[3584,64]{1,0:T(8,128)(2,1)S(1)}, bf16[3584,64]{1,0:T(8,128)(2,1)S(1)}, bf16[3584,64]{1,0:T(8,128)(2,1)S(1)}) custom-call(s32[8]{0:T(128)S(1)} %get-tuple-element.138.places, bf16[4,224,1024]{2,1,0:T(8,128)(2,1)} %pad_maximum_fusion.3.mine, ...), custom_call_target="tpu_custom_call" | custom-call | flops 939524096 | bytes 10485760 | tf_op jit(solution)/shard_map/pallas_call | solution.py:167
  90.3 8.6 %shard_map.179 = (bf16[8,224,1024]{2,1,0:T(8,128)(2,1)S(1)}, bf16[3584,64]{1,0:T(8,128)(2,1)S(1)}, bf16[3584,64]{1,0:T(8,128)(2,1)S(1)}, bf16[3584,64]{1,0:T(8,128)(2,1)S(1)}) custom-call(s32[8]{0:T(128)S(1)} %get-tuple-element.139.places, bf16[4,224,1024]{2,1,0:T(8,128)(2,1)} %pad_maximum_fusion.mine, ...), custom_call_target="tpu_custom_call", output_to_operand_aliasing={{1}: (7, {}), {2}: (8, {}), {3}: (9, {})} | custom-call | flops 939524096 | bytes 10485760 | tf_op jit(solution)/shard_map/pallas_call | solution.py:167
  100.8 19.7 %shard_map.180 = (bf16[3584,64]{1,0:T(8,128)(2,1)S(1)}, f32[64,3584]{1,0:T(8,128)S(1)}, f32[1,3584]{1,0:T(1,128)S(1)}) custom-call(bf16[3584,64]{1,0:T(8,128)(2,1)S(1)} %get-tuple-element.50.q_ref, bf16[3584,64]{1,0:T(8,128)(2,1)S(1)} %get-tuple-element.51.k_ref, bf16[3584,64]{1,0:T(8,128)(2,1)S(1)} %get-tuple-element.52.v_ref, ...), custom_call_target="tpu_custom_call" | custom-call | flops 7247757312 | bytes 4194304 | tf_op jit(solution)/shard_map/pallas_call | solution.py:296
  124.6 6.8 all-to-all-start.1
  133.6 10.4 %all-to-all-done.1 = bf16[16,224,64]{1,2,0:T(8,128)(2,1)} async-done(((bf16[16,224,64]{1,2,0:T(8,128)(2,1)}), bf16[16,224,64]{1,2,0:T(8,128)(2,1)}, u32[]{:S(2)}, u32[]{:S(2)}) %all-to-all-start.1) | async-done | bytes 458784 | tf_op jit(solution)/shard_map/all_to_all | solution.py:594
  143.9 4.7 broadcast_in_dim.151
  148.6 4.7 all-to-all-start.3
  167.3 65.1 %collective-permute-done.29 = bf16[224,1024]{1,0:T(8,128)(2,1)} collective-permute-done((bf16[224,1024]{1,0:T(8,128)(2,1)}, bf16[224,1024]{1,0:T(8,128)(2,1)}, u32[]{:S(2)}, u32[]{:S(2)}) %collective-permute-start.29) | collective-permute-done | bytes 458784 | tf_op jit(solution)/shard_map/ppermute | solution.py:51
  284.9 6.5 collective-permute-done.26
  304.3 22.3 %shard_map.181 = (bf16[4,224,1024]{2,1,0:T(8,128)(2,1)}, bf16[4,224,1024]{2,1,0:T(8,128)(2,1)}, bf16[4,224,1024]{2,1,0:T(8,128)(2,1)}, bf16[4,224,1024]{2,1,0:T(...) custom-call(s32[1]{0:T(128)} %bitcast.22.own_ref, ...), custom_call_target="tpu_custom_call" | custom-call | flops 15032385536 | bytes 25165824 | tf_op jit(solution)/shard_map/pallas_call | solution.py:448
  326.6 22.5 %shard_map.182 = (bf16[4,224,1024]{2,1,0:T(8,128)(2,1)}, bf16[4,224,1024]{2,1,0:T(8,128)(2,1)}, bf16[4,224,1024]{2,1,0:T(8,128)(2,1)}, bf16[4,224,1024]{2,1,0:T(...) custom-call(s32[1]{0:T(128)} %bitcast.22.own_ref, ...), custom_call_target="tpu_custom_call", output_to_operand_aliasing={{5}: (10, {}), {6}: (11, {}), {7}: (12, {}), {8}: (13, {})} | custom-call | flops 15032385536 | bytes 25165824 | tf_op jit(solution)/shard_map/pallas_call | solution.py:448
  381.0 3.7 collective-permute-start.42
  386.8 23.9 %collective-permute-done.51 = bf16[4,112,1024]{2,1,0:T(8,128)(2,1)S(1)} collective-permute-done((bf16[4,112,1024]{2,1,0:T(8,128)(2,1)S(1)}, bf16[4,112,1024]{2,1,0:T(8,128)(2,1)S(1)}, u32[]{:S(2)}, u32[]{:S(2)}) %collective-permute-start.51) | collective-permute-done | bytes 917536 | tf_op jit(solution)/shard_map/ppermute | solution.py:51
  447.1 4.8 collective-permute-done.41
  466.5 17.2 %all_to_all.50 = bf16[16,224,64]{1,2,0:T(8,128)(2,1)} all-to-all(bf16[16,224,64]{1,2,0:T(8,128)(2,1)} %bitcast.255), channel_id=1, replica_groups=mesh['seq'=16,'wshard'=8] {'seq'}, dimensions={0} | all-to-all | bytes 917504 | tf_op jit(solution)/shard_map/all_to_all | solution.py:633
  490.7 26.1 %shard_map.183 = (f32[3584,64]{1,0:T(8,128)}, f32[3584,64]{1,0:T(8,128)}, f32[3584,64]{1,0:T(8,128)}) custom-call(bf16[3584,64]{1,0:T(8,128)(2,1)S(1)} %get-tuple-element.50.q_ref, bf16[3584,64]{1,0:T(8,128)(2,1)S(1)} %copy-done.14, bf16[3584,64]{1,0:T(8,128)(2,1)S(1)} %copy-done.16, bf16[3584,64]{1,0:T(8,128)(2,1)S(1)} %bitcast.244, ...), custom_call_target="tpu_custom_call" | custom-call | flops 18119393280 | bytes 8388608 | tf_op jit(solution)/shard_map/pallas_call | solution.py:356
  521.4 6.2 shard_map.184
  530.0 6.2 shard_map.185
  539.6 7.5 %all-to-all-start.7 = ((bf16[128,8,256]{2,1,0:T(8,128)(2,1)}), bf16[128,8,256]{2,1,0:T(8,128)(2,1)}, u32[]{:S(2)}, u32[]{:S(2)}) async-start(bf16[128,8,256]{2,1,0:T(8,128)(2,1)} %convert_bitcast_fusion), calls=%async_computation.7 | async-start | bytes 1048576 | tf_op jit(solution)/shard_map/all_to_all | solution.py:658
  554.8 3.9 concatenate.87
  561.5 10.2 %all-to-all-start.8 = ((bf16[128,8,1152]{2,1,0:T(8,128)(2,1)}), bf16[128,8,1152]{2,1,0:T(8,128)(2,1)}, u32[]{:S(2)}, u32[]{:S(2)}) async-start(bf16[128,8,1152]{2,1,0:T(8,128)(2,1)} %copy.153), calls=%async_computation.8 | async-start | bytes 4718592 | tf_op jit(solution)/shard_map/all_to_all | solution.py:644
  571.7 15.6 %shard_map.186 = bf16[8,2,192,1024]{3,2,1,0:T(8,128)(2,1)} custom-call(bf16[2,1152,1024]{2,1,0:T(8,128)(2,1)} %get-tuple-element.81.x_ref, bf16[2,1152,1024]{2,1,0:T(8,128)(2,1)} %get-tuple-element.82.dh_ref, bf16[2,1152,512]{2,1,0:T(8,128)(2,1)S(1)} %copy-done.21, bf16[2,1152,1024]{2,1,0:T(8,128)(2,1)} %get-tuple-element.84.dy_ref), custom_call_target="tpu_custom_call" | custom-call | flops 8589934592 | bytes 14680064 | tf_op jit(solution)/shard_map/pallas_call | solution.py:504
  587.3 16.9 %all-to-all-done.8 = bf16[128,8,1152]{2,1,0:T(8,128)(2,1)} async-done(((bf16[128,8,1152]{2,1,0:T(8,128)(2,1)}), bf16[128,8,1152]{2,1,0:T(8,128)(2,1)}, u32[]{:S(2)}, u32[]{:S(2)}) %all-to-all-start.8) | async-done | bytes 2359328 | tf_op jit(solution)/shard_map/all_to_all | solution.py:644
  604.3 4.8 all-to-all-start.9
  623.4 3.9 collective-permute-done.68
  636.2 63.6 %collective-permute-done.64 = bf16[4,112,1024]{2,1,0:T(8,128)(2,1)S(1)} collective-permute-done((bf16[4,112,1024]{2,1,0:T(8,128)(2,1)S(1)}, bf16[4,112,1024]{2,1,0:T(8,128)(2,1)S(1)}, u32[]{:S(2)}, u32[]{:S(2)}) %collective-permute-start.64) | collective-permute-done | bytes 917536 | tf_op jit(solution)/shard_map/ppermute | solution.py:51
  714.3 4.4 convert_reduce_fusion
  (417 shorter events, 292.5 us)
Async XLA Ops:
  0.6 27.4 %collective-permute-start.1 = (bf16[224,1024]{1,0:T(8,128)(2,1)}, bf16[224,1024]{1,0:T(8,128)(2,1)S(1)}, u32[]{:S(2)}, u32[]{:S(2)}) collective-permute-start(bf16[224,1024]{1,0:T(8,128)(2,1)} %bitcast.248), channel_id=1, source_target_pairs={{0,16},{8,24},{16,32},{24,40},{32,48},{40,56},{48,0},{56,8},{64,80... | collective-permute-start | bytes 1376264 | tf_op jit(solution)/shard_map/ppermute | solution.py:51
  2.7 32.1 %collective-permute-start.4 = (bf16[224,1024]{1,0:T(8,128)(2,1)}, bf16[224,1024]{1,0:T(8,128)(2,1)S(1)}, u32[]{:S(2)}, u32[]{:S(2)}) collective-permute-start(bf16[224,1024]{1,0:T(8,128)(2,1)} %bitcast.249), channel_id=1, source_target_pairs={{0,32},{8,40},{16,48},{24,56},{32,0},{40,8},{48,16},{56,24},{64,96... | collective-permute-start | bytes 1376264 | tf_op jit(solution)/shard_map/ppermute | solution.py:51
  6.3 30.0 %collective-permute-start.7 = (bf16[224,1024]{1,0:T(8,128)(2,1)}, bf16[224,1024]{1,0:T(8,128)(2,1)S(1)}, u32[]{:S(2)}, u32[]{:S(2)}) collective-permute-start(bf16[224,1024]{1,0:T(8,128)(2,1)} %bitcast.250), channel_id=1, source_target_pairs={{0,48},{8,56},{16,0},{24,8},{32,16},{40,24},{48,32},{56,40},{64,11... | collective-permute-start | bytes 1376264 | tf_op jit(solution)/shard_map/ppermute | solution.py:51
  11.7 33.2 %all-to-all-start.4 = ((s32[16,8,224]{2,1,0:T(8,128)}), s32[16,8,224]{2,1,0:T(8,128)S(1)}, u32[]{:S(2)}, u32[]{:S(2)}) async-start(s32[16,8,224]{2,1,0:T(8,128)} %broadcast_in_dim.153), calls=%async_computation.4 | async-start | bytes 262144 | tf_op jit(solution)/shard_map/all_to_all | solution.py:558
  34.8 19.4 %collective-permute-start.9 = (bf16[112,1024]{1,0:T(8,128)(2,1)}, bf16[112,1024]{1,0:T(8,128)(2,1)S(1)}, u32[]{:S(2)}, u32[]{:S(2)}) collective-permute-start(bf16[112,1024]{1,0:T(8,128)(2,1)} %slice.687), channel_id=1, source_target_pairs={{0,48},{8,56},{16,0},{24,8},{32,16},{40,24},{48,32},{56,40},{64,11... | collective-permute-start | bytes 688136 | tf_op jit(solution)/shard_map/ppermute | solution.py:51
  39.1 40.8 %collective-permute-start.11 = (bf16[4,224,1024]{2,1,0:T(8,128)(2,1)}, bf16[4,224,1024]{2,1,0:T(8,128)(2,1)}, u32[]{:S(2)}, u32[]{:S(2)}) collective-permute-start(bf16[4,224,1024]{2,1,0:T(8,128)(2,1)} %pad_maximum_fusion.3.mine), channel_id=1, source_target_pairs={{0,8},{8,0},{16,24},{24,16},{32,40},{40,32},{48,56},{56,48},{64,72... | collective-permute-start | bytes 5505032 | tf_op jit(solution)/shard_map/ppermute | solution.py:55
  45.8 22.0 %all-to-all-start = ((bf16[128,8,256]{2,1,0:T(8,128)(2,1)}), bf16[128,8,256]{2,1,0:T(8,128)(2,1)S(1)}, u32[]{:S(2)}, u32[]{:S(2)}) async-start(bf16[128,8,256]{2,1,0:T(8,128)(2,1)} %bitcast.8), calls=%async_computation | async-start | bytes 1048576 | tf_op jit(solution)/shard_map/all_to_all | solution.py:553
  55.8 34.5 %collective-permute-start.10 = (bf16[4,224,1024]{2,1,0:T(8,128)(2,1)}, bf16[4,224,1024]{2,1,0:T(8,128)(2,1)}, u32[]{:S(2)}, u32[]{:S(2)}) collective-permute-start(bf16[4,224,1024]{2,1,0:T(8,128)(2,1)} %pad_maximum_fusion.mine), channel_id=1, source_target_pairs={{0,8},{8,0},{16,24},{24,16},{32,40},{40,32},{48,56},{56,48},{64,72... | collective-permute-start | bytes 5505032 | tf_op jit(solution)/shard_map/ppermute | solution.py:55
  69.4 55.3 %all-to-all-start.2 = ((bf16[128,8,1152]{2,1,0:T(8,128)(2,1)}), bf16[128,8,1152]{2,1,0:T(8,128)(2,1)}, u32[]{:S(2)}, u32[]{:S(2)}) async-start(bf16[128,8,1152]{2,1,0:T(8,128)(2,1)} %broadcast_in_dim.149), calls=%async_computation.2 | async-start | bytes 4718592 | tf_op jit(solution)/shard_map/all_to_all | solution.py:563
  124.6 19.3 %all-to-all-start.1 = ((bf16[16,224,64]{1,2,0:T(8,128)(2,1)}), bf16[16,224,64]{1,2,0:T(8,128)(2,1)}, u32[]{:S(2)}, u32[]{:S(2)}) async-start(bf16[16,224,64]{1,2,0:T(8,128)(2,1)} %copy.136), calls=%async_computation.1 | async-start | bytes 1048576 | tf_op jit(solution)/shard_map/all_to_all | solution.py:594
  148.6 155.7 %all-to-all-start.3 = ((bf16[8,2,192,1024]{3,2,1,0:T(8,128)(2,1)}), bf16[8,2,192,1024]{3,2,1,0:T(8,128)(2,1)}, u32[]{:S(2)}, u32[]{:S(2)}) async-start(bf16[8,2,192,1024]{3,2,1,0:T(8,128)(2,1)} %broadcast_in_dim.151), calls=%async_computation.3 | async-start | bytes 12582912 | tf_op jit(solution)/shard_map/all_to_all | solution.py:571
  153.4 83.2 %collective-permute-start.17 = (bf16[224,1024]{1,0:T(8,128)(2,1)}, bf16[224,1024]{1,0:T(8,128)(2,1)}, u32[]{:S(2)}, u32[]{:S(2)}) collective-permute-start(bf16[224,1024]{1,0:T(8,128)(2,1)} %bitcast.257), channel_id=1, source_target_pairs={{0,32},{8,40},{16,48},{24,56},{32,0},{40,8},{48,16},{56,24},{64,96... | collective-permute-start | bytes 1376264 | tf_op jit(solution)/shard_map/ppermute | solution.py:51
  155.8 83.1 %collective-permute-start.18 = (bf16[224,1024]{1,0:T(8,128)(2,1)}, bf16[224,1024]{1,0:T(8,128)(2,1)}, u32[]{:S(2)}, u32[]{:S(2)}) collective-permute-start(bf16[224,1024]{1,0:T(8,128)(2,1)} %bitcast.258), channel_id=1, source_target_pairs={{0,48},{8,56},{16,0},{24,8},{32,16},{40,24},{48,32},{56,40},{64,11... | collective-permute-start | bytes 1376264 | tf_op jit(solution)/shard_map/ppermute | solution.py:51
  156.6 75.8 %collective-permute-start.29 = (bf16[224,1024]{1,0:T(8,128)(2,1)}, bf16[224,1024]{1,0:T(8,128)(2,1)}, u32[]{:S(2)}, u32[]{:S(2)}) collective-permute-start(bf16[224,1024]{1,0:T(8,128)(2,1)} %bitcast.259), channel_id=1, source_target_pairs={{0,64},{8,72},{16,80},{24,88},{32,96},{40,104},{48,112},{56,120},{... | collective-permute-start | bytes 1376264 | tf_op jit(solution)/shard_map/ppermute | solution.py:51
  164.2 80.0 %collective-permute-start.12 = (bf16[224,1024]{1,0:T(8,128)(2,1)}, bf16[224,1024]{1,0:T(8,128)(2,1)S(1)}, u32[]{:S(2)}, u32[]{:S(2)}) collective-permute-start(bf16[224,1024]{1,0:T(8,128)(2,1)} %multiply_convert_fusion), channel_id=1, source_target_pairs={{0,16},{8,24},{16,32},{24,40},{32,48},{40,56},{48,0},{56,8},{64,80... | collective-permute-start | bytes 1376264 | tf_op jit(solution)/shard_map/ppermute | solution.py:51
  167.1 78.6 %collective-permute-start.13 = (bf16[224,1024]{1,0:T(8,128)(2,1)}, bf16[224,1024]{1,0:T(8,128)(2,1)S(1)}, u32[]{:S(2)}, u32[]{:S(2)}) collective-permute-start(bf16[224,1024]{1,0:T(8,128)(2,1)} %multiply_convert_fusion), channel_id=1, source_target_pairs={{0,32},{8,40},{16,48},{24,56},{32,0},{40,8},{48,16},{56,24},{64,96... | collective-permute-start | bytes 1376264 | tf_op jit(solution)/shard_map/ppermute | solution.py:51
  245.7 58.6 %collective-permute-start.19 = (bf16[4,224,1024]{2,1,0:T(8,128)(2,1)}, bf16[4,224,1024]{2,1,0:T(8,128)(2,1)}, u32[]{:S(2)}, u32[]{:S(2)}) collective-permute-start(bf16[4,224,1024]{2,1,0:T(8,128)(2,1)} %pad_maximum_fusion.5.g_mine), channel_id=1, source_target_pairs={{0,8},{8,0},{16,24},{24,16},{32,40},{40,32},{48,56},{56,48},{64,72... | collective-permute-start | bytes 5505032 | tf_op jit(solution)/shard_map/ppermute | solution.py:55
  251.5 52.8 %collective-permute-start.15 = (bf16[4,224,1024]{2,1,0:T(8,128)(2,1)}, bf16[4,224,1024]{2,1,0:T(8,128)(2,1)}, u32[]{:S(2)}, u32[]{:S(2)}) collective-permute-start(bf16[4,224,1024]{2,1,0:T(8,128)(2,1)} %pad_maximum_fusion.4.ffn_mine), channel_id=1, source_target_pairs={{0,8},{8,0},{16,24},{24,16},{32,40},{40,32},{48,56},{56,48},{64,72... | collective-permute-start | bytes 5505032 | tf_op jit(solution)/shard_map/ppermute | solution.py:55
  284.8 41.8 %collective-permute-start.36 = (bf16[4,224,1024]{2,1,0:T(8,128)(2,1)}, bf16[4,224,1024]{2,1,0:T(8,128)(2,1)}, u32[]{:S(2)}, u32[]{:S(2)}) collective-permute-start(bf16[4,224,1024]{2,1,0:T(8,128)(2,1)} %pad_maximum_fusion.7.g_mine), channel_id=1, source_target_pairs={{0,8},{8,0},{16,24},{24,16},{32,40},{40,32},{48,56},{56,48},{64,72... | collective-permute-start | bytes 5505032 | tf_op jit(solution)/shard_map/ppermute | solution.py:55
  294.2 32.4 %collective-permute-start.28 = (bf16[4,224,1024]{2,1,0:T(8,128)(2,1)}, bf16[4,224,1024]{2,1,0:T(8,128)(2,1)}, u32[]{:S(2)}, u32[]{:S(2)}) collective-permute-start(bf16[4,224,1024]{2,1,0:T(8,128)(2,1)} %pad_maximum_fusion.6.ffn_mine), channel_id=1, source_target_pairs={{0,8},{8,0},{16,24},{24,16},{32,40},{40,32},{48,56},{56,48},{64,72... | collective-permute-start | bytes 5505032 | tf_op jit(solution)/shard_map/ppermute | solution.py:55
  351.3 22.2 %collective-permute-start.20 = (bf16[4,224,1024]{2,1,0:T(8,128)(2,1)}, bf16[4,224,1024]{2,1,0:T(8,128)(2,1)}, u32[]{:S(2)}, u32[]{:S(2)}) collective-permute-start(bf16[4,224,1024]{2,1,0:T(8,128)(2,1)} %get-tuple-element.55), channel_id=1, source_target_pairs={{0,8},{8,0},{16,24},{24,16},{32,40},{40,32},{48,56},{56,48},{64,72... | collective-permute-start | bytes 5505032 | tf_op jit(solution)/shard_map/ppermute | solution.py:55
  351.9 25.6 %collective-permute-start.49 = (bf16[4,224,1024]{2,1,0:T(8,128)(2,1)}, bf16[4,224,1024]{2,1,0:T(8,128)(2,1)}, u32[]{:S(2)}, u32[]{:S(2)}) collective-permute-start(bf16[4,224,1024]{2,1,0:T(8,128)(2,1)} %get-tuple-element.63), channel_id=1, source_target_pairs={{0,8},{8,0},{16,24},{24,16},{32,40},{40,32},{48,56},{56,48},{64,72... | collective-permute-start | bytes 5505032 | tf_op jit(solution)/shard_map/ppermute | solution.py:55
  367.1 53.7 %collective-permute-start.38 = (bf16[4,112,1024]{2,1,0:T(8,128)(2,1)S(1)}, bf16[4,112,1024]{2,1,0:T(8,128)(2,1)S(1)}, u32[]{:S(2)}, u32[]{:S(2)}) collective-permute-start(bf16[4,112,1024]{2,1,0:T(8,128)(2,1)S(1)} %add_convert_fusion.2), channel_id=1, source_target_pairs={{0,64},{8,72},{16,80},{24,88},{32,96},{40,104},{48,112},{56,120},{... | collective-permute-start | bytes 2752520 | tf_op jit(solution)/shard_map/ppermute | solution.py:51
  373.5 37.2 %collective-permute-start.51 = (bf16[4,112,1024]{2,1,0:T(8,128)(2,1)S(1)}, bf16[4,112,1024]{2,1,0:T(8,128)(2,1)S(1)}, u32[]{:S(2)}, u32[]{:S(2)}) collective-permute-start(bf16[4,112,1024]{2,1,0:T(8,128)(2,1)S(1)} %add_convert_fusion.1), channel_id=1, source_target_pairs={{0,64},{8,72},{16,80},{24,88},{32,96},{40,104},{48,112},{56,120},{... | collective-permute-start | bytes 2752520 | tf_op jit(solution)/shard_map/ppermute | solution.py:51
  381.0 32.4 %collective-permute-start.42 = (bf16[112,1024]{1,0:T(8,128)(2,1)S(1)}, bf16[112,1024]{1,0:T(8,128)(2,1)S(1)}, u32[]{:S(2)}, u32[]{:S(2)}) collective-permute-start(bf16[112,1024]{1,0:T(8,128)(2,1)S(1)} %get-tuple-element.117), channel_id=1, source_target_pairs={{0,48},{8,56},{16,0},{24,8},{32,16},{40,24},{48,32},{56,40},{64,11... | collective-permute-start | bytes 688136 | tf_op jit(solution)/shard_map/ppermute | solution.py:51
  384.7 30.8 %collective-permute-start.43 = (bf16[112,1024]{1,0:T(8,128)(2,1)S(1)}, bf16[112,1024]{1,0:T(8,128)(2,1)S(1)}, u32[]{:S(2)}, u32[]{:S(2)}) collective-permute-start(bf16[112,1024]{1,0:T(8,128)(2,1)S(1)} %get-tuple-element.119), channel_id=1, source_target_pairs={{0,32},{8,40},{16,48},{24,56},{32,0},{40,8},{48,16},{56,24},{64,96... | collective-permute-start | bytes 688136 | tf_op jit(solution)/shard_map/ppermute | solution.py:51
  385.2 30.3 %collective-permute-start.44 = (bf16[112,1024]{1,0:T(8,128)(2,1)S(1)}, bf16[112,1024]{1,0:T(8,128)(2,1)S(1)}, u32[]{:S(2)}, u32[]{:S(2)}) collective-permute-start(bf16[112,1024]{1,0:T(8,128)(2,1)S(1)} %get-tuple-element.118), channel_id=1, source_target_pairs={{0,16},{8,24},{16,32},{24,40},{32,48},{40,56},{48,0},{56,8},{64,80... | collective-permute-start | bytes 688136 | tf_op jit(solution)/shard_map/ppermute | solution.py:51
  539.6 21.9 %all-to-all-start.7 = ((bf16[128,8,256]{2,1,0:T(8,128)(2,1)}), bf16[128,8,256]{2,1,0:T(8,128)(2,1)}, u32[]{:S(2)}, u32[]{:S(2)}) async-start(bf16[128,8,256]{2,1,0:T(8,128)(2,1)} %convert_bitcast_fusion), calls=%async_computation.7 | async-start | bytes 1048576 | tf_op jit(solution)/shard_map/all_to_all | solution.py:658
  561.5 42.7 %all-to-all-start.8 = ((bf16[128,8,1152]{2,1,0:T(8,128)(2,1)}), bf16[128,8,1152]{2,1,0:T(8,128)(2,1)}, u32[]{:S(2)}, u32[]{:S(2)}) async-start(bf16[128,8,1152]{2,1,0:T(8,128)(2,1)} %copy.153), calls=%async_computation.8 | async-start | bytes 4718592 | tf_op jit(solution)/shard_map/all_to_all | solution.py:644
  604.3 110.0 %all-to-all-start.9 = ((bf16[8,2,192,1024]{3,2,1,0:T(8,128)(2,1)}), bf16[8,2,192,1024]{3,2,1,0:T(8,128)(2,1)}, u32[]{:S(2)}, u32[]{:S(2)}) async-start(bf16[8,2,192,1024]{3,2,1,0:T(8,128)(2,1)} %shard_map.186), calls=%async_computation.9 | async-start | bytes 12582912 | tf_op jit(solution)/shard_map/all_to_all | solution.py:614
  615.1 84.7 %collective-permute-start.64 = (bf16[4,112,1024]{2,1,0:T(8,128)(2,1)S(1)}, bf16[4,112,1024]{2,1,0:T(8,128)(2,1)S(1)}, u32[]{:S(2)}, u32[]{:S(2)}) collective-permute-start(bf16[4,112,1024]{2,1,0:T(8,128)(2,1)S(1)} %add_convert_fusion), channel_id=1, source_target_pairs={{0,64},{8,72},{16,80},{24,88},{32,96},{40,104},{48,112},{56,120},{... | collective-permute-start | bytes 2752520 | tf_op jit(solution)/shard_map/ppermute | solution.py:51
  634.1 77.6 %collective-permute-start.71 = (bf16[112,1024]{1,0:T(8,128)(2,1)S(1)}, bf16[112,1024]{1,0:T(8,128)(2,1)S(1)}, u32[]{:S(2)}, u32[]{:S(2)}) collective-permute-start(bf16[112,1024]{1,0:T(8,128)(2,1)S(1)} %fusion.52), channel_id=1, source_target_pairs={{0,64},{8,72},{16,80},{24,88},{32,96},{40,104},{48,112},{56,120},{... | collective-permute-start | bytes 688136 | tf_op jit(solution)/shard_map/ppermute | solution.py:51
  (112 other events, 1340.3 us)

commit v3 on v2

--- a/solution.py
+++ b/solution.py
@@ -13,7 +13,6 @@
 PROMPT = 2048
 GROUP = 3584
 TOK = 224
-HALF = TOK // 2
 WIDTH = 1024
 SLOTS = 72
 STEP_ROWS = 4 * SLOTS
@@ -63,40 +62,43 @@
 
 
 def seq_gather(rows):
-    near = [rows, send(rows, 0, 1), send(rows, 0, 2), send(rows, 0, 3)]
     across = send(rows, 1, 0)
-    mine_near = jnp.stack(near)
-    tops = [send(near[b][:HALF], 1, 0) for b in (1, 2, 3)]
-    bottoms = [send(across[HALF:], 0, b) for b in (1, 2, 3)]
-    far = [across] + [jnp.concatenate([t, u], axis=0) for t, u in zip(tops, bottoms)]
-    mine_far = jnp.stack(far)
-    return (mine_near, swap_cores(mine_near)), (mine_far, swap_cores(mine_far))
+    near = jnp.stack([rows] + [send(rows, 0, b) for b in (1, 2, 3)])
+    far = jnp.stack([across] + [send(across, 0, b) for b in (1, 2, 3)])
+    return (near, swap_cores(near)), (far, swap_cores(far))
 
 
 def add_low(*terms):
     return sum([t.astype(f32) for t in terms]).astype(bf16)
 
 
-def seq_scatter_sum(near, far):
-    near_other = swap_cores(near[1])
-    far_other = swap_cores(far[1])
-    own_near = [(near[0][b], near_other[b]) for b in range(4)]
-    own_far = [(far[0][b], far_other[b]) for b in range(4)]
-    low = slice(HALF, TOK)
-    top = slice(0, HALF)
-    near_low = [send(add_low(own_near[b][0][low], own_near[b][1][low]), 0, -b) for b in (1, 2, 3)]
-    tops_far = add_low(far[0][:, top], far_other[:, top])
-    tops_got = send(tops_far, 1, 0)
-    far_low = [send(add_low(own_far[b][0][low], own_far[b][1][low]), 0, -b) for b in (1, 2, 3)]
-    crossed = send(add_low(own_far[0][0][low], own_far[0][1][low], *far_low), 1, 0)
-    tops = [
-        send(add_low(own_near[b][0][top], own_near[b][1][top], tops_got[b]), 0, -b)
-        for b in (1, 2, 3)
-    ]
-    own = [own_near[0][0].astype(f32), own_near[0][1].astype(f32)]
-    upper = sum([t.astype(f32) for t in tops], own[0][top] + own[1][top] + tops_got[0].astype(f32))
-    lower = sum([t.astype(f32) for t in near_low], own[0][low] + own[1][low] + crossed.astype(f32))
-    return jnp.concatenate([upper, lower], axis=0)
+def seq_gather_by_x(rows):
+    near = jnp.stack([rows] + [send(rows, 0, b) for b in (1, 2, 3)])
+    far = send(near, 1, 0)
+    return (near, swap_cores(near)), (far, swap_cores(far))
+
+
+def seq_sum_by_x(near, far):
+    got = swap_cores(far[1])
+    crossed = send(add_low(far[0], got), 1, 0)
+    got = swap_cores(near[1])
+    parts = [add_low(near[0][b], got[b], crossed[b]) for b in range(4)]
+    return sum([t.astype(f32) for t in [parts[0]] + [send(parts[b], 0, -b) for b in (1, 2, 3)]])
+
+
+def sum_along_z(mine, other):
+    got = swap_cores(other)
+    parts = [add_low(mine[b], got[b]) for b in range(4)]
+    return [parts[0]] + [send(parts[b], 0, -b) for b in (1, 2, 3)]
+
+
+def sum_across(near_terms, far_terms):
+    crossed = send(add_low(*far_terms), 1, 0)
+    return sum([t.astype(f32) for t in near_terms]) + crossed.astype(f32)
+
+
+def tie(*values):
+    return lax.optimization_barrier(values)
 
 
 def inverse_rms(values):
@@ -398,8 +400,8 @@
             picked_grads[e].append(jnp.dot(low, grads, preferred_element_type=f32))
     moved, routed = [], []
     for e in range(2):
-        w_gate_up = w_ref[:, e, :128, :].reshape(WIDTH, 2 * FF)
-        w_down = w_ref[:, e, 128:, :].reshape(FF, WIDTH)
+        w_gate_up = w_ref[e, :, :128, :].reshape(WIDTH, 2 * FF)
+        w_down = w_ref[e, :, 128:, :].reshape(FF, WIDTH)
         x = jnp.concatenate(picked_rows[e], axis=0).astype(bf16)
         gate = jnp.concatenate(
             [jnp.sum(p * r, axis=1, keepdims=True) for p, r in zip(picks[e], gate_rows[e])], axis=0
@@ -455,7 +457,7 @@
                 pair,
                 pair,
                 pair,
-                whole((8, 2, 192, 1024)),
+                whole((2, 8, 192, 1024)),
                 whole((EXPERTS, WIDTH)),
                 four(EXPERTS, TOK),
                 four(2, TOK),
@@ -496,8 +498,8 @@
 def expert_grads_kernel(x_ref, dh_ref, act_ref, dy_ref, out_ref):
     up = lax.dot_general(x_ref[0], dh_ref[0], TN, preferred_element_type=f32)
     down = lax.dot_general(act_ref[0], dy_ref[0], TN, preferred_element_type=f32)
-    out_ref[:, 0, :128, :] = up.astype(bf16).reshape(2, 128, 2 * FF)
-    out_ref[:, 0, 128:, :] = down.astype(bf16).reshape(2, 64, WIDTH)
+    out_ref[0, :, :128, :] = up.astype(bf16).reshape(2, 128, 2 * FF)
+    out_ref[0, :, 128:, :] = down.astype(bf16).reshape(2, 64, WIDTH)
 
 
 def expert_weight_grads(x, dh, act, dy):
@@ -510,8 +512,8 @@
             pl.BlockSpec((1, ALL_ROWS, 128), lambda e, i: (e, 0, i)),
             pl.BlockSpec((1, ALL_ROWS, WIDTH), lambda e, i: (e, 0, 0)),
         ],
-        out_specs=pl.BlockSpec((2, 1, 192, 1024), lambda e, i: (i, e, 0, 0)),
-        out_shape=jax.ShapeDtypeStruct((8, 2, 192, 1024), bf16),
+        out_specs=pl.BlockSpec((1, 2, 192, 1024), lambda e, i: (e, i, 0, 0)),
+        out_shape=jax.ShapeDtypeStruct((2, 8, 192, 1024), bf16),
         compiler_params=pltpu.CompilerParams(vmem_limit_bytes=48 << 20),
         cost_estimate=pl.CostEstimate(flops=8 << 30, bytes_accessed=14 << 20, transcendentals=0),
     )(x, dh, act, dy)
@@ -536,7 +538,7 @@
     query_width = HEADS * HEAD_DIM
     kv_width = KV_HEADS * HEAD_DIM
 
-    rows_all = seq_gather(rows)
+    rows_near, rows_far = seq_gather(rows)
     kv_heads = lambda start: jnp.repeat(
         w_qkv[:, start : start + kv_width].reshape(8, KV_HEADS, HEAD_DIM), 2, axis=1
     )
@@ -554,27 +556,37 @@
     gain_attn = head_weights[:, 192].astype(f32)[None]
     head_weights = jnp.where(jnp.arange(256)[None] < 192, head_weights, 0.0).astype(bf16)
 
-    routes_t = jnp.broadcast_to(routes[0].T[None], (16, 8, TOK))
-    routes_all = jnp.take(lax.all_to_all(routes_t, "seq", 0, 0, tiled=True), places, axis=0)
+    expert_rows = jnp.concatenate([w_gate_up, w_down], axis=1)
+    experts = lax.all_gather(expert_rows, "wshard", axis=1, tiled=True).reshape(2, 8, 192, 1024)
+
+    position, begin = group_layout(cont_lengths[0])
+    begin = begin[None]
+    cosine, sine = rotary_tables(position.astype(f32))
+
+    normed_near, *qkv = project(places[:8], rows_near, head_weights, gain_attn, cosine, sine, ())
+    rows_far, normed_near = tie(rows_far, normed_near)
 
     shared = jnp.concatenate(
         [w_out, w_router, norm_ffn[:, None], jnp.zeros((8, 95), bf16)], axis=1
     )
+    shared, _ = tie(shared, head_weights)
     shared = lax.all_to_all(
-        jnp.broadcast_to(shared[None], (128, 8, 1152)), BOTH, 0, 0, tiled=True
-    ).reshape(WIDTH, 1152)
+        jnp.broadcast_to(shared[None], (8, 8, 1152)), "wshard", 0, 0, tiled=True
+    ).reshape(64, 1152)
+    shared, _ = tie(shared, normed_near)
+    in_order = lambda halves: jnp.concatenate(
+        [jnp.stack(pair, axis=1).reshape(8, *pair[0].shape[1:]) for pair in halves], axis=0
+    )
+    shared = jnp.take(in_order(seq_gather_by_x(shared)), places, axis=0).reshape(WIDTH, 1152)
     weight_out = shared[:, :WIDTH]
     weight_router = shared[:, WIDTH : WIDTH + EXPERTS]
     gain_ffn = shared[:, WIDTH + EXPERTS].astype(f32)
-
-    expert_rows = jnp.concatenate([w_gate_up, w_down], axis=1)
-    experts = lax.all_to_all(
-        jnp.broadcast_to(expert_rows[None], (8, 2, 192, 1024)), "wshard", 0, 0, tiled=True
-    )
-
-    position, begin = group_layout(cont_lengths[0])
-    begin = begin[None]
-    cosine, sine = rotary_tables(position.astype(f32))
+    routes_rows = jnp.pad(routes[0].T.astype(bf16), ((0, 8), (0, WIDTH - TOK)))
+    upstream_rows, _ = tie(jnp.concatenate([cotangent[0], routes_rows], axis=0), rows_far[1])
+    grad_near, grad_far = seq_gather_by_x(upstream_rows)
+    routes_all = in_order(
+        [tuple(t[:, TOK : TOK + 8, :TOK] for t in half) for half in (grad_near, grad_far)]
+    ).astype(i32)
 
     expert_range = jnp.arange(EXPERTS, dtype=i32)
     chosen = jnp.any(routes_all[:, None] == expert_range[None, :, None, None], axis=2)
@@ -588,8 +600,7 @@
     slot_cols = slots.transpose(0, 2, 1)
     chosen = chosen.astype(f32)
 
-    normed_near, *qkv = project(places[:8], rows_all[0], head_weights, gain_attn, cosine, sine, ())
-    normed_far, q, k, v = project(places[8:], rows_all[1], head_weights, gain_attn, cosine, sine, qkv)
+    normed_far, q, k, v = project(places[8:], rows_far, head_weights, gain_attn, cosine, sine, qkv)
     attended_head, attended_t, lse = attend(q, k, v, begin)
     attended = lax.all_to_all(attended_head.reshape(16, TOK, HEAD_DIM), "seq", 0, 0, tiled=True)
     attended = attended.transpose(1, 0, 2).reshape(TOK, query_width)
@@ -597,22 +608,32 @@
     hidden = inputs + jnp.dot(attended, weight_out, preferred_element_type=f32)
     hidden_scale = inverse_rms(hidden)
     normed_ffn = (hidden * hidden_scale * gain_ffn).astype(bf16)
-
-    grad_all = seq_gather(cotangent[0])
-    ffn_all = seq_gather(normed_ffn)
+    normed_ffn, grad_near, grad_far, chosen, slots, slot_cols = tie(
+        normed_ffn, grad_near, grad_far, chosen, slots, slot_cols
+    )
+
+    ffn_near, ffn_far = seq_gather(normed_ffn)
     router_t = weight_router.T
     own = own_first[None]
     near = run_experts(
-        0, own, ffn_all[0], grad_all[0], experts, router_t, chosen, slots, slot_cols, ()
-    )
+        0, own, ffn_near, grad_near, experts, router_t, chosen, slots, slot_cols, ()
+    )
+    near_terms = sum_along_z(near[0], near[1])
     far = run_experts(
-        1, own, ffn_all[1], grad_all[1], experts, router_t, chosen, slots, slot_cols, near[5:]
-    )
-    routed_grad = seq_scatter_sum(near[:2], far[:2])
+        1, own, ffn_far, grad_far, experts, router_t, chosen, slots, slot_cols, near[5:]
+    )
+    far, near_terms = tie(far, near_terms)
+    far_terms = sum_along_z(far[0], far[1])
+    expert_grads = expert_weight_grads(*far[5:])
+    routed_grad = sum_across(near_terms, far_terms)
     token_gate_grad = jnp.take(jnp.concatenate([near[4], far[4]], axis=0), places, axis=0)
     gate_grad = lax.all_to_all(token_gate_grad, "seq", 0, 0, tiled=True).reshape(EXPERTS, TOK).T
-    expert_grads = lax.all_to_all(expert_weight_grads(*far[5:]), "wshard", 0, 0, tiled=True)
-    expert_grads = jnp.sum(expert_grads.astype(f32), axis=0)
+    routed_grad, gate_grad, expert_grads, near, far = tie(
+        routed_grad, gate_grad, expert_grads, near, far
+    )
+    expert_grads = lax.psum_scatter(
+        expert_grads.reshape(2, 8 * 192, 1024), "wshard", scatter_dimension=1, tiled=True
+    ).astype(f32)
 
     chosen_here = jnp.any(routes[0][:, :, None] == expert_range, axis=1)
     logits = jnp.dot(normed_ffn, weight_router, preferred_element_type=f32)
@@ -640,26 +661,29 @@
     shared_grads = jnp.concatenate(
         [grad_out, grad_router, grad_norm_ffn[:, None], jnp.zeros((WIDTH, 95), f32)], axis=1
     ).astype(bf16)
+    moved = seq_sum_by_x(near[2:4], far[2:4])
+    head_grad, shared_grads = tie(head_grad, shared_grads)
     shared_grads = jnp.sum(
         lax.all_to_all(shared_grads.reshape(128, 8, 1152), BOTH, 0, 0, tiled=True).astype(f32),
         axis=0,
     )
-    output = (hidden + seq_scatter_sum(near[2:4], far[2:4])).astype(bf16)
-
     grads = attend_back(q, k, v, head_grad, attended_t, lse, begin)
+    grads, moved = tie(grads, moved)
+    output = (hidden + moved).astype(bf16)
     *near_part, grad_head = project_back(
         places[:8], normed_near, grads, head_weights, cosine, sine, ()
     )
+    near_terms = sum_along_z(*near_part)
     *far_part, grad_head = project_back(
         places[8:], normed_far, grads, head_weights, cosine, sine, (grad_head,)
     )
-    normed_grad = seq_scatter_sum(near_part, far_part)
-    grad_heads = jnp.sum(
-        lax.all_to_all(grad_head.astype(bf16).reshape(128, 8, 256), BOTH, 0, 0, tiled=True)
-        .reshape(16, 8, 8, 256)
-        .astype(f32),
-        axis=1,
-    ).transpose(1, 0, 2)
+    far_terms = sum_along_z(*far_part)
+    grad_heads = lax.all_to_all(
+        grad_head.astype(bf16).reshape(128, 8, 256), BOTH, 0, 0, tiled=True
+    )
+    grad_heads, far_terms = tie(grad_heads, far_terms)
+    normed_grad = sum_across(near_terms, far_terms)
+    grad_heads = jnp.sum(grad_heads.reshape(16, 8, 8, 256).astype(f32), axis=1).transpose(1, 0, 2)
     kv_sum = lambda start: jnp.sum(
         grad_heads[:, :, start : start + HEAD_DIM].reshape(8, KV_HEADS, 2, HEAD_DIM), axis=2
     ).reshape(8, kv_width)

time: 741 us -> 688 us (0.928)
  waiting for transfers between devices: 255 us -> 219 us
  starting transfers between devices: 154 us -> 130 us
  blocking collectives: 17.2 us -> 0 us
  between operations: 2.07 us -> 15.4 us
  local copies, waits for them, and re-layouts: 72 us -> 81.7 us
    ppermute x63 -> x40, waiting for transfers between devices: 212 us -> 143 us  [send(): return lax.ppermute(rows, 'seq', shift_perm(a, b))]
    all_to_all x4 -> x2, waiting for transfers between devices: 0.01 us -> 65.9 us  [the longest x1 65.9 us: local(): lax.all_to_all(attended_grad.reshape(TOK, HEADS, HEAD_DIM).transpose(1, 0...]
    all_to_all x1 -> x0, blocking collectives: 17.2 us -> none  [local(): lax.all_to_all(attended_grad.reshape(TOK, HEADS, HEAD_DIM).transpose(1, 0...]
    all_to_all x1, waiting for transfers between devices: 16.9 us -> 0.01 us  [local(): lax.all_to_all(shared_grads.reshape(128, 8, 1152), BOTH, 0, 0, tiled=True)]
    ppermute x63 -> x40, starting transfers between devices: 95.8 us -> 80.1 us  [send(): return lax.ppermute(rows, 'seq', shift_perm(a, b))]
    all_to_all x1, waiting for transfers between devices: 11.7 us -> 0.01 us  [local(): lax.all_to_all(head_cols, BOTH, 0, 0, tiled=True).reshape(WIDTH, 256)]
    all_to_all x4 -> x2, starting transfers between devices: 19 us -> 8.73 us  [the longest x1 4.5 us: local(): lax.all_to_all(jnp.broadcast_to(shared[None], (8, 8, 1152)), 'wshard', 0,...]
    slice x12 -> x0, local copies, waits for them, and re-layouts: 9.36 us -> none  [the longest x9 6.03 us: seq_gather(): tops = [send(near[b][:HALF], 1, 0) for b in (1, 2, 3)]]
  transfers between devices with their start and end apart: 84 -> 63, of which waited for: 32 -> 24; matrix products, arithmetic and copies ran while one was open for 18% -> 22% of each run, Pallas kernels for 10% -> 20%
where the time goes in v3:
time: 688 us; the launch traced here: 677 us
  waiting for transfers between devices  219 us (32%)
  Pallas kernels  135 us (20%)
  starting transfers between devices  130 us (19%)
  other arithmetic  84 us (12%)
  local copies, waits for them, and re-layouts  81.7 us (12%)
  between operations  15.4 us (2%)
  matrix products  10.7 us (2%)
    ppermute x40, waiting for transfers between devices, send(): return lax.ppermute(rows, 'seq', shift_perm(a, b))  143 us
    ppermute x40, starting transfers between devices, send(): return lax.ppermute(rows, 'seq', shift_perm(a, b))  80.1 us
    all_to_all x1, waiting for transfers between devices, local(): lax.all_to_all(attended_grad.reshape(TOK, HEADS, HEAD_DIM).transpose(1, 0...  65.9 us
    pallas_call x2, Pallas kernels, run_experts(): pl.pallas_call(experts_kernel, grid_spec=pltpu.PrefetchScalarGridSpec(num...  42.8 us
    unnamed x130, local copies, waits for them, and re-layouts  28.8 us
    pallas_call x1, Pallas kernels, attend_back(): pl.pallas_call(attend_back_kernel, grid=(GROUP // BLOCK,), in_specs=[rows...  26 us
    convert_element_type x8, other arithmetic, add_low(): return sum([t.astype(f32) for t in terms]).astype(bf16)  23.3 us
    pallas_call x1, Pallas kernels, attend(): pl.pallas_call(attend_kernel, grid=(GROUP // BLOCK,), in_specs=[rows, who...  19.6 us
  transfers between devices with their start and end apart: 63, of which 24 were waited for; matrix products, arithmetic and copies ran while one was open for 22% of the time, Pallas kernels for 20%

profile of v3, /device:TPU:0, one launch (start us, length us, event | category | flops | bytes accessed | tf_op | source)
XLA Modules:
  0.0 676.8 jit_solution(12949807084531611899)
XLA Ops:
  19.1 7.4 %all-to-all-start = ((bf16[128,8,256]{2,1,0:T(8,128)(2,1)}), bf16[128,8,256]{2,1,0:T(8,128)(2,1)S(1)}, u32[]{:S(2)}, u32[]{:S(2)}) async-start(bf16[128,8,256]{2,1,0:T(8,128)(2,1)} %bitcast.11), calls=%async_computation | async-start | bytes 1048576 | tf_op jit(solution)/shard_map/all_to_all | solution.py:555
  32.2 8.8 %collective-permute-done.7 = bf16[224,1024]{1,0:T(8,128)(2,1)S(1)} collective-permute-done((bf16[224,1024]{1,0:T(8,128)(2,1)}, bf16[224,1024]{1,0:T(8,128)(2,1)S(1)}, u32[]{:S(2)}, u32[]{:S(2)}) %collective-permute-start.7) | collective-permute-done | bytes 458784 | tf_op jit(solution)/shard_map/ppermute | solution.py:50
  46.2 13.0 %collective-permute-done.3 = bf16[224,1024]{1,0:T(8,128)(2,1)S(1)} collective-permute-done((bf16[224,1024]{1,0:T(8,128)(2,1)S(1)}, bf16[224,1024]{1,0:T(8,128)(2,1)S(1)}, u32[]{:S(2)}, u32[]{:S(2)}) %collective-permute-start.3) | collective-permute-done | bytes 458784 | tf_op jit(solution)/shard_map/ppermute | solution.py:50
  64.1 8.2 %multiply_sine_fusion = (f32[3584,32]{1,0:T(8,128)}, f32[3584,32]{1,0:T(8,128)}) fusion(f32[32]{0:T(128)S(1)} %multiply_power_fusion, f32[3584]{0:T(1024)S(1)} %get-tuple-element.208), kind=kLoop, calls=%fused_computation.6 | loop fusion | flops 114688 | bytes 931968 | tf_op jit(solution)/shard_map/sin | solution.py:132
  72.7 5.4 pad_maximum_fusion.4
  78.8 4.5 all-to-all-start.2
  85.1 8.5 %shard_map.178 = (bf16[8,224,1024]{2,1,0:T(8,128)(2,1)S(1)}, bf16[3584,64]{1,0:T(8,128)(2,1)S(1)}, bf16[3584,64]{1,0:T(8,128)(2,1)S(1)}, bf16[3584,64]{1,0:T(8,128)(2,1)S(1)}) custom-call(s32[8]{0:T(128)S(1)} %get-tuple-element.213.places, bf16[4,224,1024]{2,1,0:T(8,128)(2,1)} %pad_maximum_fusion.3.mine, bf16[4,224,1024]{2,1,0:T(8,128)(2,1)} %collective-permute-done.8.other, ...), custom_call_target="tpu_custom_call" | custom-call | flops 939524096 | bytes 10485760 | tf_op jit(solution)/shard_map/pallas_call | solution.py:169
  118.0 4.4 collective-permute-done.16
  122.4 9.4 %collective-permute-done.15 = bf16[240,1024]{1,0:T(8,128)(2,1)} collective-permute-done((bf16[240,1024]{1,0:T(8,128)(2,1)}, bf16[240,1024]{1,0:T(8,128)(2,1)}, u32[]{:S(2)}, u32[]{:S(2)}) %collective-permute-start.15) | collective-permute-done | bytes 491552 | tf_op jit(solution)/shard_map/ppermute | solution.py:50
  137.0 8.5 %shard_map.179 = (bf16[8,224,1024]{2,1,0:T(8,128)(2,1)S(1)}, bf16[3584,64]{1,0:T(8,128)(2,1)S(1)}, bf16[3584,64]{1,0:T(8,128)(2,1)S(1)}, bf16[3584,64]{1,0:T(8,128)(2,1)S(1)}) custom-call(s32[8]{0:T(128)S(1)} %get-tuple-element.214.places, bf16[4,224,1024]{2,1,0:T(8,128)(2,1)} %pad_maximum_fusion.2.mine, ...), custom_call_target="tpu_custom_call", output_to_operand_aliasing={{1}: (7, {}), {2}: (8, {}), {3}: (9, {})} | custom-call | flops 939524096 | bytes 10485760 | tf_op jit(solution)/shard_map/pallas_call | solution.py:169
  146.4 19.6 %shard_map.180 = (bf16[3584,64]{1,0:T(8,128)(2,1)S(1)}, f32[64,3584]{1,0:T(8,128)S(1)}, f32[1,3584]{1,0:T(1,128)S(1)}) custom-call(bf16[3584,64]{1,0:T(8,128)(2,1)S(1)} %get-tuple-element.98.q_ref, bf16[3584,64]{1,0:T(8,128)(2,1)S(1)} %get-tuple-element.99.k_ref, bf16[3584,64]{1,0:T(8,128)(2,1)S(1)} %get-tuple-element.100.v_ref, ...), custom_call_target="tpu_custom_call" | custom-call | flops 7247757312 | bytes 4194304 | tf_op jit(solution)/shard_map/pallas_call | solution.py:298
  170.2 10.6 %all-to-all-start.1 = ((bf16[16,224,64]{1,2,0:T(8,128)(2,1)}), bf16[16,224,64]{1,2,0:T(8,128)(2,1)}, u32[]{:S(2)}, u32[]{:S(2)}) async-start(bf16[16,224,64]{1,2,0:T(8,128)(2,1)} %copy.121), calls=%async_computation.1 | async-start | bytes 1048576 | tf_op jit(solution)/shard_map/all_to_all | solution.py:605
  194.6 22.3 %collective-permute-done.19.g_mine = bf16[4,240,1024]{2,1,0:T(8,128)(2,1)} collective-permute-done((bf16[4,240,1024]{2,1,0:T(8,128)(2,1)}, bf16[4,240,1024]{2,1,0:T(8,128)(2,1)}, u32[]{:S(2)}, u32[]{:S(2)}) %collective-permute-start.19) | collective-permute-done | bytes 1966112 | tf_op jit(solution)/shard_map/ppermute | solution.py:50
  220.2 4.4 all-to-all-done.1
  243.2 18.6 %collective-permute-done.28 = bf16[224,1024]{1,0:T(8,128)(2,1)S(1)} collective-permute-done((bf16[224,1024]{1,0:T(8,128)(2,1)}, bf16[224,1024]{1,0:T(8,128)(2,1)S(1)}, u32[]{:S(2)}, u32[]{:S(2)}) %collective-permute-start.28) | collective-permute-done | bytes 458784 | tf_op jit(solution)/shard_map/ppermute | solution.py:50
  272.6 10.0 %collective-permute-done.21 = bf16[224,1024]{1,0:T(8,128)(2,1)} collective-permute-done((bf16[224,1024]{1,0:T(8,128)(2,1)}, bf16[224,1024]{1,0:T(8,128)(2,1)}, u32[]{:S(2)}, u32[]{:S(2)}) %collective-permute-start.21) | collective-permute-done | bytes 458784 | tf_op jit(solution)/shard_map/ppermute | solution.py:50
  285.3 21.4 %shard_map.181 = (bf16[4,224,1024]{2,1,0:T(8,128)(2,1)}, bf16[4,224,1024]{2,1,0:T(8,128)(2,1)}, bf16[4,224,1024]{2,1,0:T(8,128)(2,1)}, bf16[4,224,1024]{2,1,0:T(...) custom-call(s32[1]{0:T(128)} %bitcast.36.own_ref, ...), custom_call_target="tpu_custom_call" | custom-call | flops 15032385536 | bytes 25165824 | tf_op jit(solution)/shard_map/pallas_call | solution.py:450
  309.1 5.4 copy.144.refs_0_
  329.7 21.4 %shard_map.182 = (bf16[4,224,1024]{2,1,0:T(8,128)(2,1)}, bf16[4,224,1024]{2,1,0:T(8,128)(2,1)}, bf16[4,224,1024]{2,1,0:T(8,128)(2,1)}, bf16[4,224,1024]{2,1,0:T(...) custom-call(s32[1]{0:T(128)} %bitcast.36.own_ref, ...), custom_call_target="tpu_custom_call", output_to_operand_aliasing={{5}: (10, {}), {6}: (11, {}), {7}: (12, {}), {8}: (13, {})} | custom-call | flops 15032385536 | bytes 25165824 | tf_op jit(solution)/shard_map/pallas_call | solution.py:450
  367.7 6.0 collective-permute-done.37
  373.6 9.3 %collective-permute-done.36 = bf16[224,1024]{1,0:T(8,128)(2,1)} collective-permute-done((bf16[224,1024]{1,0:T(8,128)(2,1)}, bf16[224,1024]{1,0:T(8,128)(2,1)}, u32[]{:S(2)}, u32[]{:S(2)}) %collective-permute-start.36) | collective-permute-done | bytes 458784 | tf_op jit(solution)/shard_map/ppermute | solution.py:50
  386.8 15.6 %shard_map.183 = bf16[2,8,192,1024]{3,2,1,0:T(8,128)(2,1)} custom-call(bf16[2,1152,1024]{2,1,0:T(8,128)(2,1)} %get-tuple-element.137.x_ref, bf16[2,1152,1024]{2,1,0:T(8,128)(2,1)} %get-tuple-element.138.dh_ref, bf16[2,1152,512]{2,1,0:T(8,128)(2,1)S(1)} %copy-done.10, bf16[2,1152,1024]{2,1,0:T(8,128)(2,1)} %get-tuple-element.140.dy_ref), custom_call_target="tpu_custom_call" | custom-call | flops 8589934592 | bytes 14680064 | tf_op jit(solution)/shard_map/pallas_call | solution.py:506
  430.9 12.4 %concatenate.53 = bf16[1024,1152]{0,1:T(8,128)(2,1)} concatenate(bf16[1024,1024]{0,1:T(8,128)(2,1)} %convolution_convert_fusion, bf16[1024,32]{0,1:T(8,128)(2,1)S(1)} %convolution_convert_fusion.1, bf16[1024,1]{0,1:T(2,128)(2,1)S(1)} %broadcast_in_dim.154, bf16[1024,95]{0,1:T(8,128)(2,1)} %broadcast_in_dim.155), dimensions={1} | concatenate | bytes 4718592 | tf_op jit(solution)/shard_map/concatenate | solution.py:661
  443.3 65.9 %all-to-all-done.4 = bf16[16,224,64]{1,2,0:T(8,128)(2,1)} async-done(((bf16[16,224,64]{1,2,0:T(8,128)(2,1)}), bf16[16,224,64]{1,2,0:T(8,128)(2,1)}, u32[]{:S(2)}, u32[]{:S(2)}) %all-to-all-start.4) | async-done | bytes 458784 | tf_op jit(solution)/shard_map/all_to_all | solution.py:654
  515.8 8.6 %all-to-all-start.6 = ((bf16[128,8,1152]{2,1,0:T(8,128)(2,1)}), bf16[128,8,1152]{2,1,0:T(8,128)(2,1)}, u32[]{:S(2)}, u32[]{:S(2)}) async-start(bf16[128,8,1152]{2,1,0:T(8,128)(2,1)} %bitcast.168), calls=%async_computation.6 | async-start | bytes 4718592 | tf_op jit(solution)/shard_map/all_to_all | solution.py:667
  533.1 26.0 %shard_map.184 = (f32[3584,64]{1,0:T(8,128)}, f32[3584,64]{1,0:T(8,128)}, f32[3584,64]{1,0:T(8,128)}) custom-call(bf16[3584,64]{1,0:T(8,128)(2,1)S(1)} %get-tuple-element.98.q_ref, bf16[3584,64]{1,0:T(8,128)(2,1)S(1)} %copy-done.18, bf16[3584,64]{1,0:T(8,128)(2,1)S(1)} %copy-done.22, bf16[3584,64]{1,0:T(8,128)(2,1)S(1)} %bitcast.164, ...), custom_call_target="tpu_custom_call" | custom-call | flops 18119393280 | bytes 8388608 | tf_op jit(solution)/shard_map/pallas_call | solution.py:358
  559.1 12.4 %collective-permute-done.43 = bf16[224,1024]{1,0:T(8,128)(2,1)S(1)} collective-permute-done((bf16[224,1024]{1,0:T(8,128)(2,1)S(1)}, bf16[224,1024]{1,0:T(8,128)(2,1)S(1)}, u32[]{:S(2)}, u32[]{:S(2)}) %collective-permute-start.43) | collective-permute-done | bytes 458784 | tf_op jit(solution)/shard_map/ppermute | solution.py:50
  577.3 7.1 %shard_map.185 = (bf16[4,224,1024]{2,1,0:T(8,128)(2,1)S(1)}, bf16[4,224,1024]{2,1,0:T(8,128)(2,1)}, f32[1024,256]{1,0:T(8,128)S(1)}) custom-call(s32[8]{0:T(128)S(1)} %get-tuple-element.213.places, bf16[8,224,1024]{2,1,0:T(8,128)(2,1)S(1)} %copy-done.9, f32[3584,64]{1,0:T(8,128)S(1)} %copy-done.3, f32[3584,64]{1,0:T(8,128)S(1)} %copy-done.4, ...), custom_call_target="tpu_custom_call" | custom-call | flops 1879048192 | bytes 12582912 | tf_op jit(solution)/shard_map/pallas_call | solution.py:219
  585.6 7.2 %shard_map.186 = (bf16[4,224,1024]{2,1,0:T(8,128)(2,1)S(1)}, bf16[4,224,1024]{2,1,0:T(8,128)(2,1)}, f32[1024,256]{1,0:T(8,128)S(1)}) custom-call(s32[8]{0:T(128)S(1)} %get-tuple-element.214.places, bf16[8,224,1024]{2,1,0:T(8,128)(2,1)S(1)} %copy-done.7, f32[3584,64]{1,0:T(8,128)S(1)} %copy-done.3, f32[3584,64]{1,0:T(8,128)S(1)} %copy-done.4, ...), custom_call_target="tpu_custom_call" | custom-call | flops 1879048192 | bytes 12582912 | tf_op jit(solution)/shard_map/pallas_call | solution.py:219
  599.6 8.0 %all-to-all-start.5 = ((bf16[128,8,256]{2,1,0:T(8,128)(2,1)}), bf16[128,8,256]{2,1,0:T(8,128)(2,1)S(1)}, u32[]{:S(2)}, u32[]{:S(2)}) async-start(bf16[128,8,256]{2,1,0:T(8,128)(2,1)} %convert_bitcast_fusion), calls=%async_computation.5 | async-start | bytes 1048576 | tf_op jit(solution)/shard_map/all_to_all | solution.py:681
  622.4 4.4 collective-permute-done.50
  627.5 21.9 %collective-permute-start.46 = (bf16[224,1024]{1,0:T(8,128)(2,1)}, bf16[224,1024]{1,0:T(8,128)(2,1)}, u32[]{:S(2)}, u32[]{:S(2)}) collective-permute-start(bf16[224,1024]{1,0:T(8,128)(2,1)} %get-tuple-element.187), channel_id=1, source_target_pairs={{0,48},{8,56},{16,0},{24,8},{32,16},{40,24},{48,32},{56,40},{64,11... | collective-permute-start | bytes 1376264 | tf_op jit(solution)/shard_map/ppermute | solution.py:50
  (365 shorter events, 244.9 us)
Async XLA Ops:
  10.4 30.6 %collective-permute-start.7 = (bf16[224,1024]{1,0:T(8,128)(2,1)}, bf16[224,1024]{1,0:T(8,128)(2,1)S(1)}, u32[]{:S(2)}, u32[]{:S(2)}) collective-permute-start(bf16[224,1024]{1,0:T(8,128)(2,1)} %bitcast.178), channel_id=1, source_target_pairs={{0,48},{8,56},{16,0},{24,8},{32,16},{40,24},{48,32},{56,40},{64,11... | collective-permute-start | bytes 1376264 | tf_op jit(solution)/shard_map/ppermute | solution.py:50
  14.4 26.6 %collective-permute-start.6 = (bf16[224,1024]{1,0:T(8,128)(2,1)}, bf16[224,1024]{1,0:T(8,128)(2,1)S(1)}, u32[]{:S(2)}, u32[]{:S(2)}) collective-permute-start(bf16[224,1024]{1,0:T(8,128)(2,1)} %bitcast.179), channel_id=1, source_target_pairs={{0,32},{8,40},{16,48},{24,56},{32,0},{40,8},{48,16},{56,24},{64,96... | collective-permute-start | bytes 1376264 | tf_op jit(solution)/shard_map/ppermute | solution.py:50
  14.4 30.3 %collective-permute-start.5 = (bf16[224,1024]{1,0:T(8,128)(2,1)}, bf16[224,1024]{1,0:T(8,128)(2,1)S(1)}, u32[]{:S(2)}, u32[]{:S(2)}) collective-permute-start(bf16[224,1024]{1,0:T(8,128)(2,1)} %bitcast.180), channel_id=1, source_target_pairs={{0,16},{8,24},{16,32},{24,40},{32,48},{40,56},{48,0},{56,8},{64,80... | collective-permute-start | bytes 1376264 | tf_op jit(solution)/shard_map/ppermute | solution.py:50
  19.1 59.0 %all-to-all-start = ((bf16[128,8,256]{2,1,0:T(8,128)(2,1)}), bf16[128,8,256]{2,1,0:T(8,128)(2,1)S(1)}, u32[]{:S(2)}, u32[]{:S(2)}) async-start(bf16[128,8,256]{2,1,0:T(8,128)(2,1)} %bitcast.11), calls=%async_computation | async-start | bytes 1048576 | tf_op jit(solution)/shard_map/all_to_all | solution.py:555
  26.6 258.8 %all-gather.2.cloned.1.call-start = ((), (), s32[]{:S(2)}) async-start(), calls=%async_computation.8 | async-start | bytes 7077888 | tf_op jit(solution)/shard_map/all_gather | solution.py:560
  29.0 30.2 %collective-permute-start.3 = (bf16[224,1024]{1,0:T(8,128)(2,1)S(1)}, bf16[224,1024]{1,0:T(8,128)(2,1)S(1)}, u32[]{:S(2)}, u32[]{:S(2)}) collective-permute-start(bf16[224,1024]{1,0:T(8,128)(2,1)S(1)} %collective-permute-done), channel_id=1, source_target_pairs={{0,48},{8,56},{16,0},{24,8},{32,16},{40,24},{48,32},{56,40},{64,11... | collective-permute-start | bytes 1376264 | tf_op jit(solution)/shard_map/ppermute | solution.py:50
  31.9 27.3 %collective-permute-start.2 = (bf16[224,1024]{1,0:T(8,128)(2,1)S(1)}, bf16[224,1024]{1,0:T(8,128)(2,1)S(1)}, u32[]{:S(2)}, u32[]{:S(2)}) collective-permute-start(bf16[224,1024]{1,0:T(8,128)(2,1)S(1)} %collective-permute-done), channel_id=1, source_target_pairs={{0,32},{8,40},{16,48},{24,56},{32,0},{40,8},{48,16},{56,24},{64,96... | collective-permute-start | bytes 1376264 | tf_op jit(solution)/shard_map/ppermute | solution.py:50
  46.2 37.3 %collective-permute-start.8 = (bf16[4,224,1024]{2,1,0:T(8,128)(2,1)}, bf16[4,224,1024]{2,1,0:T(8,128)(2,1)}, u32[]{:S(2)}, u32[]{:S(2)}) collective-permute-start(bf16[4,224,1024]{2,1,0:T(8,128)(2,1)} %pad_maximum_fusion.3.mine), channel_id=1, source_target_pairs={{0,8},{8,0},{16,24},{24,16},{32,40},{40,32},{48,56},{56,48},{64,72... | collective-permute-start | bytes 5505032 | tf_op jit(solution)/shard_map/ppermute | solution.py:54
  64.1 33.2 %collective-permute-start.4 = (bf16[4,224,1024]{2,1,0:T(8,128)(2,1)}, bf16[4,224,1024]{2,1,0:T(8,128)(2,1)}, u32[]{:S(2)}, u32[]{:S(2)}) collective-permute-start(bf16[4,224,1024]{2,1,0:T(8,128)(2,1)} %pad_maximum_fusion.2.mine), channel_id=1, source_target_pairs={{0,8},{8,0},{16,24},{24,16},{32,40},{40,32},{48,56},{56,48},{64,72... | collective-permute-start | bytes 5505032 | tf_op jit(solution)/shard_map/ppermute | solution.py:54
  105.6 26.2 %collective-permute-start.15 = (bf16[240,1024]{1,0:T(8,128)(2,1)}, bf16[240,1024]{1,0:T(8,128)(2,1)}, u32[]{:S(2)}, u32[]{:S(2)}) collective-permute-start(bf16[240,1024]{1,0:T(8,128)(2,1)} %fusion.26), channel_id=1, source_target_pairs={{0,16},{8,24},{16,32},{24,40},{32,48},{40,56},{48,0},{56,8},{64,80... | collective-permute-start | bytes 1474568 | tf_op jit(solution)/shard_map/ppermute | solution.py:50
  114.1 31.7 %collective-permute-start.13 = (bf16[4,64,1152]{2,1,0:T(8,128)(2,1)}, bf16[4,64,1152]{2,1,0:T(8,128)(2,1)}, u32[]{:S(2)}, u32[]{:S(2)}) collective-permute-start(bf16[4,64,1152]{2,1,0:T(8,128)(2,1)} %get-tuple-element.202), channel_id=1, source_target_pairs={{0,64},{8,72},{16,80},{24,88},{32,96},{40,104},{48,112},{56,120},{... | collective-permute-start | bytes 1769480 | tf_op jit(solution)/shard_map/ppermute | solution.py:50
  135.0 82.0 %collective-permute-start.19 = (bf16[4,240,1024]{2,1,0:T(8,128)(2,1)}, bf16[4,240,1024]{2,1,0:T(8,128)(2,1)}, u32[]{:S(2)}, u32[]{:S(2)}) collective-permute-start(bf16[4,240,1024]{2,1,0:T(8,128)(2,1)} %pad_maximum_fusion.1.g_mine), channel_id=1, source_target_pairs={{0,64},{8,72},{16,80},{24,88},{32,96},{40,104},{48,112},{56,120},{... | collective-permute-start | bytes 5898248 | tf_op jit(solution)/shard_map/ppermute | solution.py:50
  145.6 36.3 %collective-permute-start.12 = (bf16[4,64,1152]{2,1,0:T(8,128)(2,1)}, bf16[4,64,1152]{2,1,0:T(8,128)(2,1)}, u32[]{:S(2)}, u32[]{:S(2)}) collective-permute-start(bf16[4,64,1152]{2,1,0:T(8,128)(2,1)} %get-tuple-element.202), channel_id=1, source_target_pairs={{0,8},{8,0},{16,24},{24,16},{32,40},{40,32},{48,56},{56,48},{64,72... | collective-permute-start | bytes 1769480 | tf_op jit(solution)/shard_map/ppermute | solution.py:54
  145.9 37.4 %collective-permute-start.14 = (bf16[4,64,1152]{2,1,0:T(8,128)(2,1)}, bf16[4,64,1152]{2,1,0:T(8,128)(2,1)}, u32[]{:S(2)}, u32[]{:S(2)}) collective-permute-start(bf16[4,64,1152]{2,1,0:T(8,128)(2,1)} %collective-permute-done.13), channel_id=1, source_target_pairs={{0,8},{8,0},{16,24},{24,16},{32,40},{40,32},{48,56},{56,48},{64,72... | collective-permute-start | bytes 1769480 | tf_op jit(solution)/shard_map/ppermute | solution.py:54
  170.2 54.5 %all-to-all-start.1 = ((bf16[16,224,64]{1,2,0:T(8,128)(2,1)}), bf16[16,224,64]{1,2,0:T(8,128)(2,1)}, u32[]{:S(2)}, u32[]{:S(2)}) async-start(bf16[16,224,64]{1,2,0:T(8,128)(2,1)} %copy.121), calls=%async_computation.1 | async-start | bytes 1048576 | tf_op jit(solution)/shard_map/all_to_all | solution.py:605
  180.8 48.4 %collective-permute-start.18 = (bf16[4,240,1024]{2,1,0:T(8,128)(2,1)}, bf16[4,240,1024]{2,1,0:T(8,128)(2,1)}, u32[]{:S(2)}, u32[]{:S(2)}) collective-permute-start(bf16[4,240,1024]{2,1,0:T(8,128)(2,1)} %pad_maximum_fusion.1.g_mine), channel_id=1, source_target_pairs={{0,8},{8,0},{16,24},{24,16},{32,40},{40,32},{48,56},{56,48},{64,72... | collective-permute-start | bytes 5898248 | tf_op jit(solution)/shard_map/ppermute | solution.py:54
  324.3 26.8 %collective-permute-start.31 = (bf16[224,1024]{1,0:T(8,128)(2,1)}, bf16[224,1024]{1,0:T(8,128)(2,1)S(1)}, u32[]{:S(2)}, u32[]{:S(2)}) collective-permute-start(bf16[224,1024]{1,0:T(8,128)(2,1)} %get-tuple-element.199), channel_id=1, source_target_pairs={{0,48},{8,56},{16,0},{24,8},{32,16},{40,24},{48,32},{56,40},{64,11... | collective-permute-start | bytes 1376264 | tf_op jit(solution)/shard_map/ppermute | solution.py:50
  364.1 38.3 %all-to-all-start.3 = ((f32[16,2,224]{2,1,0:T(2,128)}), f32[16,2,224]{2,1,0:T(2,128)S(1)}, u32[]{:S(2)}, u32[]{:S(2)}) async-start(f32[16,2,224]{2,1,0:T(2,128)} %broadcast_select_fusion.2), calls=%async_computation.3 | async-start | bytes 65536 | tf_op jit(solution)/shard_map/all_to_all | solution.py:630
  367.6 298.9 %reduce-scatter.2.cloned.1.call-start = ((), (), s32[]{:S(2)}) async-start(), calls=%async_computation.9 | async-start | bytes 7077888 | tf_op jit(solution)/shard_map/reduce_scatter | solution.py:634
  406.8 117.6 %collective-permute-start.39 = (bf16[4,224,1024]{2,1,0:T(8,128)(2,1)}, bf16[4,224,1024]{2,1,0:T(8,128)(2,1)}, u32[]{:S(2)}, u32[]{:S(2)}) collective-permute-start(bf16[4,224,1024]{2,1,0:T(8,128)(2,1)} %get-tuple-element.154), channel_id=1, source_target_pairs={{0,8},{8,0},{16,24},{24,16},{32,40},{40,32},{48,56},{56,48},{64,72... | collective-permute-start | bytes 5505032 | tf_op jit(solution)/shard_map/ppermute | solution.py:54
  413.0 111.4 %collective-permute-start.41 = (bf16[4,224,1024]{2,1,0:T(8,128)(2,1)}, bf16[4,224,1024]{2,1,0:T(8,128)(2,1)}, u32[]{:S(2)}, u32[]{:S(2)}) collective-permute-start(bf16[4,224,1024]{2,1,0:T(8,128)(2,1)} %add_convert_fusion), channel_id=1, source_target_pairs={{0,64},{8,72},{16,80},{24,88},{32,96},{40,104},{48,112},{56,120},{... | collective-permute-start | bytes 5505032 | tf_op jit(solution)/shard_map/ppermute | solution.py:50
  421.3 87.9 %all-to-all-start.4 = ((bf16[16,224,64]{1,2,0:T(8,128)(2,1)}), bf16[16,224,64]{1,2,0:T(8,128)(2,1)}, u32[]{:S(2)}, u32[]{:S(2)}) async-start(bf16[16,224,64]{1,2,0:T(8,128)(2,1)} %bitcast.182), calls=%async_computation.4 | async-start | bytes 1048576 | tf_op jit(solution)/shard_map/all_to_all | solution.py:654
  515.8 79.0 %all-to-all-start.6 = ((bf16[128,8,1152]{2,1,0:T(8,128)(2,1)}), bf16[128,8,1152]{2,1,0:T(8,128)(2,1)}, u32[]{:S(2)}, u32[]{:S(2)}) async-start(bf16[128,8,1152]{2,1,0:T(8,128)(2,1)} %bitcast.168), calls=%async_computation.6 | async-start | bytes 4718592 | tf_op jit(solution)/shard_map/all_to_all | solution.py:667
  527.6 31.5 %collective-permute-start.44 = (bf16[224,1024]{1,0:T(8,128)(2,1)S(1)}, bf16[224,1024]{1,0:T(8,128)(2,1)S(1)}, u32[]{:S(2)}, u32[]{:S(2)}) collective-permute-start(bf16[224,1024]{1,0:T(8,128)(2,1)S(1)} %get-tuple-element.185), channel_id=1, source_target_pairs={{0,16},{8,24},{16,32},{24,40},{32,48},{40,56},{48,0},{56,8},{64,80... | collective-permute-start | bytes 1376264 | tf_op jit(solution)/shard_map/ppermute | solution.py:50
  528.7 42.9 %collective-permute-start.43 = (bf16[224,1024]{1,0:T(8,128)(2,1)S(1)}, bf16[224,1024]{1,0:T(8,128)(2,1)S(1)}, u32[]{:S(2)}, u32[]{:S(2)}) collective-permute-start(bf16[224,1024]{1,0:T(8,128)(2,1)S(1)} %get-tuple-element.186), channel_id=1, source_target_pairs={{0,32},{8,40},{16,48},{24,56},{32,0},{40,8},{48,16},{56,24},{64,96... | collective-permute-start | bytes 1376264 | tf_op jit(solution)/shard_map/ppermute | solution.py:50
  531.9 39.7 %collective-permute-start.42 = (bf16[224,1024]{1,0:T(8,128)(2,1)S(1)}, bf16[224,1024]{1,0:T(8,128)(2,1)S(1)}, u32[]{:S(2)}, u32[]{:S(2)}) collective-permute-start(bf16[224,1024]{1,0:T(8,128)(2,1)S(1)} %get-tuple-element.184), channel_id=1, source_target_pairs={{0,48},{8,56},{16,0},{24,8},{32,16},{40,24},{48,32},{56,40},{64,11... | collective-permute-start | bytes 1376264 | tf_op jit(solution)/shard_map/ppermute | solution.py:50
  599.6 49.8 %all-to-all-start.5 = ((bf16[128,8,256]{2,1,0:T(8,128)(2,1)}), bf16[128,8,256]{2,1,0:T(8,128)(2,1)S(1)}, u32[]{:S(2)}, u32[]{:S(2)}) async-start(bf16[128,8,256]{2,1,0:T(8,128)(2,1)} %convert_bitcast_fusion), calls=%async_computation.5 | async-start | bytes 1048576 | tf_op jit(solution)/shard_map/all_to_all | solution.py:681
  613.7 35.7 %collective-permute-start.51 = (bf16[224,1024]{1,0:T(8,128)(2,1)}, bf16[224,1024]{1,0:T(8,128)(2,1)}, u32[]{:S(2)}, u32[]{:S(2)}) collective-permute-start(bf16[224,1024]{1,0:T(8,128)(2,1)} %get-tuple-element.191), channel_id=1, source_target_pairs={{0,32},{8,40},{16,48},{24,56},{32,0},{40,8},{48,16},{56,24},{64,96... | collective-permute-start | bytes 1376264 | tf_op jit(solution)/shard_map/ppermute | solution.py:50
  614.0 35.4 %collective-permute-start.52 = (bf16[224,1024]{1,0:T(8,128)(2,1)}, bf16[224,1024]{1,0:T(8,128)(2,1)}, u32[]{:S(2)}, u32[]{:S(2)}) collective-permute-start(bf16[224,1024]{1,0:T(8,128)(2,1)} %get-tuple-element.190), channel_id=1, source_target_pairs={{0,16},{8,24},{16,32},{24,40},{32,48},{40,56},{48,0},{56,8},{64,80... | collective-permute-start | bytes 1376264 | tf_op jit(solution)/shard_map/ppermute | solution.py:50
  618.8 37.8 %collective-permute-start.48 = (bf16[224,1024]{1,0:T(8,128)(2,1)}, bf16[224,1024]{1,0:T(8,128)(2,1)}, u32[]{:S(2)}, u32[]{:S(2)}) collective-permute-start(bf16[224,1024]{1,0:T(8,128)(2,1)} %get-tuple-element.188), channel_id=1, source_target_pairs={{0,16},{8,24},{16,32},{24,40},{32,48},{40,56},{48,0},{56,8},{64,80... | collective-permute-start | bytes 1376264 | tf_op jit(solution)/shard_map/ppermute | solution.py:50
  620.8 38.1 %collective-permute-start.47 = (bf16[224,1024]{1,0:T(8,128)(2,1)}, bf16[224,1024]{1,0:T(8,128)(2,1)}, u32[]{:S(2)}, u32[]{:S(2)}) collective-permute-start(bf16[224,1024]{1,0:T(8,128)(2,1)} %get-tuple-element.189), channel_id=1, source_target_pairs={{0,32},{8,40},{16,48},{24,56},{32,0},{40,8},{48,16},{56,24},{64,96... | collective-permute-start | bytes 1376264 | tf_op jit(solution)/shard_map/ppermute | solution.py:50
  627.5 31.5 %collective-permute-start.46 = (bf16[224,1024]{1,0:T(8,128)(2,1)}, bf16[224,1024]{1,0:T(8,128)(2,1)}, u32[]{:S(2)}, u32[]{:S(2)}) collective-permute-start(bf16[224,1024]{1,0:T(8,128)(2,1)} %get-tuple-element.187), channel_id=1, source_target_pairs={{0,48},{8,56},{16,0},{24,8},{32,16},{40,24},{48,32},{56,40},{64,11... | collective-permute-start | bytes 1376264 | tf_op jit(solution)/shard_map/ppermute | solution.py:50
  (93 other events, 1035.4 us)
Sparse Core Ops, SparseCore 0:
  29.0 170.8 all-gather.1
  405.4 200.9 reduce-scatter.1

commit v4 on v3

--- a/solution.py
+++ b/solution.py
@@ -57,44 +57,44 @@
 def relative_places(seq_index):
     x, z, c = seq_index // 8, (seq_index // 2) % 4, seq_index % 2
     r = jnp.arange(16, dtype=i32)
-    a, b, k = r // 8, (r // 2) % 4, r % 2
-    return (a ^ x) * 8 + ((z - b) % 4) * 2 + (k ^ c)
+    a, i, k = r // 8, (r // 2) % 4, r % 2
+    shift = i ^ (i // 2)
+    behind = (z - i) % 4
+    places = (a ^ x) * 8 + ((z - shift) % 4) * 2 + (k ^ c)
+    return places, (a ^ x) * 8 + (behind ^ (behind // 2)) * 2 + (k ^ c)
+
+
+def gather_near(rows):
+    return [rows] + [send(rows, 0, b) for b in (1, 3, 2)], send(rows, 1, 0)
+
+
+def both_cores(parts):
+    mine = jnp.stack(parts)
+    return mine, swap_cores(mine)
+
+
+def gather_far(across):
+    return both_cores([across] + [send(across, 0, b) for b in (1, 3, 2)])
 
 
 def seq_gather(rows):
-    across = send(rows, 1, 0)
-    near = jnp.stack([rows] + [send(rows, 0, b) for b in (1, 2, 3)])
-    far = jnp.stack([across] + [send(across, 0, b) for b in (1, 2, 3)])
-    return (near, swap_cores(near)), (far, swap_cores(far))
+    near, across = gather_near(rows)
+    return both_cores(near), gather_far(across)
 
 
 def add_low(*terms):
     return sum([t.astype(f32) for t in terms]).astype(bf16)
 
 
-def seq_gather_by_x(rows):
-    near = jnp.stack([rows] + [send(rows, 0, b) for b in (1, 2, 3)])
-    far = send(near, 1, 0)
-    return (near, swap_cores(near)), (far, swap_cores(far))
-
-
-def seq_sum_by_x(near, far):
-    got = swap_cores(far[1])
-    crossed = send(add_low(far[0], got), 1, 0)
-    got = swap_cores(near[1])
-    parts = [add_low(near[0][b], got[b], crossed[b]) for b in range(4)]
-    return sum([t.astype(f32) for t in [parts[0]] + [send(parts[b], 0, -b) for b in (1, 2, 3)]])
-
-
 def sum_along_z(mine, other):
     got = swap_cores(other)
-    parts = [add_low(mine[b], got[b]) for b in range(4)]
-    return [parts[0]] + [send(parts[b], 0, -b) for b in (1, 2, 3)]
-
-
-def sum_across(near_terms, far_terms):
-    crossed = send(add_low(*far_terms), 1, 0)
-    return sum([t.astype(f32) for t in near_terms]) + crossed.astype(f32)
+    parts = [add_low(mine[i], got[i]) for i in range(4)]
+    return [parts[0]] + [send(parts[i], 0, -b) for i, b in ((1, 1), (2, 3), (3, 2))]
+
+
+def send_w(rows, a, b):
+    pairs = [(y * 2 + x, ((y + b) % 4) * 2 + (x ^ a)) for y in range(4) for x in range(2)]
+    return lax.ppermute(rows, "wshard", pairs)
 
 
 def tie(*values):
@@ -369,12 +369,31 @@
     )(q, k, v, g, ot, lse, begin)
 
 
+SHARDS = [(0, 0, 0), (0, 1, 1), (1, 0, 2), (1, 1, 3), (2, 0, 6), (2, 1, 7), (3, None, 4), (4, None, 5)]
+N_SHARDS = 5
+
+
 def experts_kernel(
-    own_ref, ffn_mine, ffn_other, g_mine, g_other, w_ref, router_ref, chosen_ref, slots_ref, slot_cols_ref, *refs
+    own_ref, ffn_mine, ffn_other, g_mine, g_other, router_ref, chosen_ref, slots_ref, slot_cols_ref, *refs
 ):
-    routed_mine, routed_other, moved_mine, moved_other, gate_grad_ref = refs[-9:-4]
-    x_ref, dh_ref, act_ref, dy_ref = refs[-4:]
+    shards = refs[:N_SHARDS]
+    routed_mine, routed_other, gate_grad_ref, moved_mine, moved_other = refs[-11:-6]
+    x_ref, dh_ref, act_ref, dy_ref, w_ref, sem = refs[-6:]
     own = own_ref[0]
+
+    @pl.when(pl.program_id(0) == 0)
+    def _():
+        copies = []
+        for n, (shard, a, r) in enumerate(SHARDS):
+            source = shards[shard] if a is None else shards[shard].at[a]
+            for e in range(2):
+                place = own_ref[1 + r]
+                copies.append(pltpu.make_async_copy(source.at[e], w_ref.at[e, place], sem.at[n, e]))
+        for copy in copies:
+            copy.start()
+        for copy in copies:
+            copy.wait()
+
     expert_rows = lax.broadcasted_iota(i32, (EXPERTS, TOK), 0)
     slot_rows = lax.broadcasted_iota(i32, (SLOTS, TOK), 0)
     gate_rows = [[], []]
@@ -442,6 +461,7 @@
 
 def run_experts(half, own, ffn, grads, weights, router, chosen, slots, slot_cols, before):
     pair = pl.BlockSpec((2, TOK, WIDTH), lambda i, o: (i, 0, 0))
+    pair_of_all = pl.BlockSpec((2, TOK, WIDTH), lambda i, o: (i + 2 * half, 0, 0))
     whole = lambda shape: pl.BlockSpec(shape, lambda i, o: (0,) * len(shape))
     four = lambda *shape: pl.BlockSpec((4, *shape), lambda i, o: (i + 2 * half, 0, 0))
     kept = lambda n: pl.BlockSpec((2, STEP_ROWS, n), lambda i, o: (0, i + 2 * half, 0))
@@ -457,66 +477,166 @@
                 pair,
                 pair,
                 pair,
-                whole((2, 8, 192, 1024)),
                 whole((EXPERTS, WIDTH)),
                 four(EXPERTS, TOK),
                 four(2, TOK),
                 four(TOK, 2),
             ]
-            + [pl.BlockSpec(memory_space=pl.ANY)] * len(before),
+            + [pl.BlockSpec(memory_space=pl.ANY)] * (N_SHARDS + len(before)),
             out_specs=[
                 pair,
                 pair,
-                pair,
-                pair,
                 pl.BlockSpec((4, 2, TOK), lambda i, o: (i, 0, 0)),
+                pair_of_all,
+                pair_of_all,
                 kept(WIDTH),
                 kept(2 * FF),
                 kept(FF),
                 kept(WIDTH),
             ],
+            scratch_shapes=[
+                pltpu.VMEM((2, 8, 192, 1024), bf16),
+                pltpu.SemaphoreType.DMA((8, 2)),
+            ],
         ),
         out_shape=[
             part,
             part,
-            part,
-            part,
             jax.ShapeDtypeStruct((8, 2, TOK), f32),
+            jax.ShapeDtypeStruct((8, TOK, WIDTH), bf16),
+            jax.ShapeDtypeStruct((8, TOK, WIDTH), bf16),
             keep(WIDTH),
             keep(2 * FF),
             keep(FF),
             keep(WIDTH),
         ],
-        input_output_aliases={10 + i: 5 + i for i in range(len(before))},
+        input_output_aliases={9 + N_SHARDS + i: 3 + i for i in range(len(before))},
         compiler_params=pltpu.CompilerParams(vmem_limit_bytes=60 << 20),
         cost_estimate=pl.CostEstimate(
             flops=14 << 30, bytes_accessed=24 << 20, transcendentals=8 * SLOTS * 2 * FF
         ),
-    )(own, *ffn, *grads, weights, router, chosen, slots, slot_cols, *before)
-
-
-def expert_grads_kernel(x_ref, dh_ref, act_ref, dy_ref, out_ref):
+    )(own, *ffn, *grads, router, chosen, slots, slot_cols, *weights, *before)
+
+
+def expert_grads_kernel(order, x_ref, dh_ref, act_ref, dy_ref, out_ref):
+    del order
     up = lax.dot_general(x_ref[0], dh_ref[0], TN, preferred_element_type=f32)
     down = lax.dot_general(act_ref[0], dy_ref[0], TN, preferred_element_type=f32)
-    out_ref[0, :, :128, :] = up.astype(bf16).reshape(2, 128, 2 * FF)
-    out_ref[0, :, 128:, :] = down.astype(bf16).reshape(2, 64, WIDTH)
-
-
-def expert_weight_grads(x, dh, act, dy):
+    out_ref[0, :, 0, :128, :] = up.astype(bf16).reshape(2, 128, 2 * FF)
+    out_ref[0, :, 0, 128:, :] = down.astype(bf16).reshape(2, 64, WIDTH)
+
+
+def expert_weight_grads(order, x, dh, act, dy):
     return pl.pallas_call(
         expert_grads_kernel,
-        grid=(2, 4),
-        in_specs=[
-            pl.BlockSpec((1, ALL_ROWS, 256), lambda e, i: (e, 0, i)),
-            pl.BlockSpec((1, ALL_ROWS, 2 * FF), lambda e, i: (e, 0, 0)),
-            pl.BlockSpec((1, ALL_ROWS, 128), lambda e, i: (e, 0, i)),
-            pl.BlockSpec((1, ALL_ROWS, WIDTH), lambda e, i: (e, 0, 0)),
-        ],
-        out_specs=pl.BlockSpec((1, 2, 192, 1024), lambda e, i: (e, i, 0, 0)),
-        out_shape=jax.ShapeDtypeStruct((2, 8, 192, 1024), bf16),
+        grid_spec=pltpu.PrefetchScalarGridSpec(
+            num_scalar_prefetch=1,
+            grid=(2, 4),
+            in_specs=[
+                pl.BlockSpec((1, ALL_ROWS, 256), lambda e, i, o: (e, 0, i)),
+                pl.BlockSpec((1, ALL_ROWS, 2 * FF), lambda e, i, o: (e, 0, 0)),
+                pl.BlockSpec((1, ALL_ROWS, 128), lambda e, i, o: (e, 0, i)),
+                pl.BlockSpec((1, ALL_ROWS, WIDTH), lambda e, i, o: (e, 0, 0)),
+            ],
+            out_specs=pl.BlockSpec((1, 2, 1, 192, 1024), lambda e, i, o: (o[i], 0, e, 0, 0)),
+        ),
+        out_shape=jax.ShapeDtypeStruct((4, 2, 2, 192, 1024), bf16),
         compiler_params=pltpu.CompilerParams(vmem_limit_bytes=48 << 20),
         cost_estimate=pl.CostEstimate(flops=8 << 30, bytes_accessed=14 << 20, transcendentals=0),
-    )(x, dh, act, dy)
+    )(order, x, dh, act, dy)
+
+
+def hidden_kernel(att_ref, w_ref, rows_ref, gain_ref, hidden_ref, normed_ref, att_rows_ref):
+    att = jnp.concatenate([att_ref[h] for h in range(HEADS)], axis=1)
+    att_rows_ref[...] = att
+    hidden = rows_ref[...].astype(f32) + jnp.dot(att, w_ref[:, :WIDTH], preferred_element_type=f32)
+    hidden_ref[...] = hidden
+    normed_ref[...] = (hidden * inverse_rms(hidden) * gain_ref[...]).astype(bf16)
+
+
+def hidden_of(attended, shared, rows, gain):
+    return pl.pallas_call(
+        hidden_kernel,
+        out_shape=[
+            jax.ShapeDtypeStruct((TOK, WIDTH), f32),
+            jax.ShapeDtypeStruct((TOK, WIDTH), bf16),
+            jax.ShapeDtypeStruct((TOK, WIDTH), bf16),
+        ],
+        compiler_params=pltpu.CompilerParams(vmem_limit_bytes=32 << 20),
+        cost_estimate=pl.CostEstimate(
+            flops=2 * TOK * WIDTH * WIDTH, bytes_accessed=5 << 20, transcendentals=0
+        ),
+    )(attended, shared, rows, gain)
+
+
+def hidden_back_kernel(
+    t0, t1, t2, t3, crossed, hidden_ref, normed_ref, gate_grad_ref, chosen_ref, router_ref, g_ref, gain_ref,
+    w_ref, hidden_grad_ref, branch_ref, logit_ref, scaled_ref, att_ref
+):
+    chosen = chosen_ref[...] > 0
+    logits = lax.dot_general(router_ref[...], normed_ref[...], NT, preferred_element_type=f32)
+    peak = jnp.max(jnp.where(chosen, logits, masked_score), axis=0, keepdims=True)
+    raised = jnp.where(chosen, jnp.exp(jnp.minimum(logits - peak, 0.0)), 0.0)
+    gates = raised / jnp.sum(raised, axis=0, keepdims=True)
+    gate_grad = gate_grad_ref[...]
+    logit_grad = gates * (gate_grad - jnp.sum(gates * gate_grad, axis=0, keepdims=True))
+    logit_grad = logit_grad.astype(bf16)
+    logit_ref[...] = logit_grad
+    normed_grad = lax.dot_general(logit_grad, router_ref[...], TN, preferred_element_type=f32)
+    for term in (t0, t1, t2, t3, crossed):
+        normed_grad = normed_grad + term[...].astype(f32)
+    hidden = hidden_ref[...]
+    scale = inverse_rms(hidden)
+    scaled_ref[...] = (normed_grad * hidden * scale).astype(bf16)
+    hidden_grad = g_ref[...].astype(f32) + rms_pull(hidden, scale, gain_ref[...], normed_grad)
+    hidden_grad_ref[...] = hidden_grad
+    branch = hidden_grad.astype(bf16)
+    branch_ref[...] = branch
+    att = lax.dot_general(branch, w_ref[:, :WIDTH], NT, preferred_element_type=f32).astype(bf16)
+    for h in range(HEADS):
+        att_ref[h] = att[:, h * HEAD_DIM : (h + 1) * HEAD_DIM]
+
+
+def hidden_back(terms, crossed, hidden, normed, gate_grad, chosen, router_t, g, gain, shared):
+    wide = lambda t: jax.ShapeDtypeStruct((TOK, WIDTH), t)
+    return pl.pallas_call(
+        hidden_back_kernel,
+        out_shape=[
+            wide(f32),
+            wide(bf16),
+            jax.ShapeDtypeStruct((EXPERTS, TOK), bf16),
+            wide(bf16),
+            jax.ShapeDtypeStruct((HEADS, TOK, HEAD_DIM), bf16),
+        ],
+        compiler_params=pltpu.CompilerParams(vmem_limit_bytes=32 << 20),
+        cost_estimate=pl.CostEstimate(
+            flops=2 * TOK * WIDTH * WIDTH, bytes_accessed=8 << 20, transcendentals=0
+        ),
+    )(*terms, crossed, hidden, normed, gate_grad, chosen, router_t, g, gain, shared)
+
+
+def shared_grads_kernel(att_ref, branch_ref, normed_ref, logit_ref, scaled_ref, out_ref):
+    out_ref[:, :WIDTH] = lax.dot_general(
+        att_ref[...], branch_ref[...], TN, preferred_element_type=f32
+    ).astype(bf16)
+    over_tokens = (((0,), (1,)), ((), ()))
+    logit = jnp.concatenate([logit_ref[...], jnp.zeros((96, TOK), bf16)], axis=0)
+    ones = (lax.broadcasted_iota(i32, (128, TOK), 0) == EXPERTS).astype(f32).astype(bf16)
+    out_ref[:, WIDTH:] = (
+        lax.dot_general(normed_ref[...], logit, over_tokens, preferred_element_type=f32)
+        + lax.dot_general(scaled_ref[...], ones, over_tokens, preferred_element_type=f32)
+    ).astype(bf16)
+
+
+def shared_weight_grads(att, branch, normed, logit_grad, scaled):
+    return pl.pallas_call(
+        shared_grads_kernel,
+        out_shape=jax.ShapeDtypeStruct((WIDTH, 1152), bf16),
+        compiler_params=pltpu.CompilerParams(vmem_limit_bytes=32 << 20),
+        cost_estimate=pl.CostEstimate(
+            flops=2 * TOK * WIDTH * 1280, bytes_accessed=5 << 20, transcendentals=0
+        ),
+    )(att, branch, normed, logit_grad, scaled)
 
 
 def local(
@@ -533,12 +653,14 @@
     cotangent,
 ):
     seq_index = lax.axis_index("seq")
-    places = relative_places(seq_index)
+    places, blocks = relative_places(seq_index)
     rows = tokens[0]
     query_width = HEADS * HEAD_DIM
     kv_width = KV_HEADS * HEAD_DIM
 
-    rows_near, rows_far = seq_gather(rows)
+    position, begin = group_layout(cont_lengths[0])
+    begin = begin[None]
+    cosine, sine = rotary_tables(position.astype(f32))
     kv_heads = lambda start: jnp.repeat(
         w_qkv[:, start : start + kv_width].reshape(8, KV_HEADS, HEAD_DIM), 2, axis=1
     )
@@ -556,16 +678,19 @@
     gain_attn = head_weights[:, 192].astype(f32)[None]
     head_weights = jnp.where(jnp.arange(256)[None] < 192, head_weights, 0.0).astype(bf16)
 
+    rows_near, rows_across = gather_near(rows)
+    rows_near, cosine, sine, head_weights = tie(rows_near, cosine, sine, head_weights)
+    rows_near = both_cores(rows_near)
+    rows_far = [rows_across] + [send(rows_across, 0, b) for b in (1, 3, 2)]
+
+    w_index = lax.axis_index("wshard")
+    own_y, own_x = w_index // 2, w_index % 2
     expert_rows = jnp.concatenate([w_gate_up, w_down], axis=1)
-    experts = lax.all_gather(expert_rows, "wshard", axis=1, tiled=True).reshape(2, 8, 192, 1024)
-
-    position, begin = group_layout(cont_lengths[0])
-    begin = begin[None]
-    cosine, sine = rotary_tables(position.astype(f32))
+    expert_pair = jnp.stack([expert_rows, send_w(expert_rows, 1, 0)])
+    pair_before, pair_after = send_w(expert_pair, 0, 1), send_w(expert_pair, 0, -1)
+    w_places = [((own_y - b) % 4) * 2 + (own_x ^ a) for b in range(4) for a in range(2)]
 
     normed_near, *qkv = project(places[:8], rows_near, head_weights, gain_attn, cosine, sine, ())
-    rows_far, normed_near = tie(rows_far, normed_near)
-
     shared = jnp.concatenate(
         [w_out, w_router, norm_ffn[:, None], jnp.zeros((8, 95), bf16)], axis=1
     )
@@ -573,17 +698,35 @@
     shared = lax.all_to_all(
         jnp.broadcast_to(shared[None], (8, 8, 1152)), "wshard", 0, 0, tiled=True
     ).reshape(64, 1152)
-    shared, _ = tie(shared, normed_near)
+    rows_far, normed_near, pair_before, pair_after, shared = tie(
+        rows_far, normed_near, pair_before, pair_after, shared
+    )
+    rows_far = both_cores(rows_far)
+    experts = (
+        expert_pair,
+        pair_before,
+        pair_after,
+        send_w(pair_before[0], 0, 1),
+        send_w(pair_after[1], 0, -1),
+    )
+    normed_far, q, k, v = project(places[8:], rows_far, head_weights, gain_attn, cosine, sine, qkv)
+
+    shared = lax.all_to_all(
+        jnp.broadcast_to(shared[None], (16, 64, 1152)), "seq", 0, 0, tiled=True
+    ).reshape(WIDTH, 1152)
+    router_t = shared[:, WIDTH : WIDTH + EXPERTS].T
+    gain_ffn = shared[:, WIDTH + EXPERTS].astype(f32)[None]
+    routes_rows = jnp.pad(routes[0].T.astype(bf16), ((0, 8), (0, WIDTH - TOK)))
+    upstream_rows, _ = tie(jnp.concatenate([cotangent[0], routes_rows], axis=0), normed_far)
+    grad_near, grad_across = gather_near(upstream_rows)
+    attended_head, attended_t, lse = attend(q, k, v, begin)
+    attended_head, experts, shared, grad_near, grad_across = tie(
+        attended_head, experts, shared, grad_near, grad_across
+    )
+    grad_near, grad_far = both_cores(grad_near), gather_far(grad_across)
     in_order = lambda halves: jnp.concatenate(
         [jnp.stack(pair, axis=1).reshape(8, *pair[0].shape[1:]) for pair in halves], axis=0
     )
-    shared = jnp.take(in_order(seq_gather_by_x(shared)), places, axis=0).reshape(WIDTH, 1152)
-    weight_out = shared[:, :WIDTH]
-    weight_router = shared[:, WIDTH : WIDTH + EXPERTS]
-    gain_ffn = shared[:, WIDTH + EXPERTS].astype(f32)
-    routes_rows = jnp.pad(routes[0].T.astype(bf16), ((0, 8), (0, WIDTH - TOK)))
-    upstream_rows, _ = tie(jnp.concatenate([cotangent[0], routes_rows], axis=0), rows_far[1])
-    grad_near, grad_far = seq_gather_by_x(upstream_rows)
     routes_all = in_order(
         [tuple(t[:, TOK : TOK + 8, :TOK] for t in half) for half in (grad_near, grad_far)]
     ).astype(i32)
@@ -600,89 +743,77 @@
     slot_cols = slots.transpose(0, 2, 1)
     chosen = chosen.astype(f32)
 
-    normed_far, q, k, v = project(places[8:], rows_far, head_weights, gain_attn, cosine, sine, qkv)
-    attended_head, attended_t, lse = attend(q, k, v, begin)
     attended = lax.all_to_all(attended_head.reshape(16, TOK, HEAD_DIM), "seq", 0, 0, tiled=True)
-    attended = attended.transpose(1, 0, 2).reshape(TOK, query_width)
-    inputs = rows.astype(f32)
-    hidden = inputs + jnp.dot(attended, weight_out, preferred_element_type=f32)
-    hidden_scale = inverse_rms(hidden)
-    normed_ffn = (hidden * hidden_scale * gain_ffn).astype(bf16)
-    normed_ffn, grad_near, grad_far, chosen, slots, slot_cols = tie(
-        normed_ffn, grad_near, grad_far, chosen, slots, slot_cols
-    )
+    hidden, normed_ffn, attended = hidden_of(attended, shared, rows, gain_ffn)
+    normed_ffn, grad_near = tie(normed_ffn, grad_near)
 
     ffn_near, ffn_far = seq_gather(normed_ffn)
-    router_t = weight_router.T
-    own = own_first[None]
+    own = jnp.stack([own_first] + w_places)
     near = run_experts(
         0, own, ffn_near, grad_near, experts, router_t, chosen, slots, slot_cols, ()
     )
+    near, saved = near[:3], near[3:]
     near_terms = sum_along_z(near[0], near[1])
     far = run_experts(
-        1, own, ffn_far, grad_far, experts, router_t, chosen, slots, slot_cols, near[5:]
-    )
+        1, own, ffn_far, grad_far, experts, router_t, chosen, slots, slot_cols, saved
+    )
+    far, saved = far[:3], far[3:]
+    moved, saved = saved[:2], saved[2:]
     far, near_terms = tie(far, near_terms)
     far_terms = sum_along_z(far[0], far[1])
-    expert_grads = expert_weight_grads(*far[5:])
-    routed_grad = sum_across(near_terms, far_terms)
-    token_gate_grad = jnp.take(jnp.concatenate([near[4], far[4]], axis=0), places, axis=0)
-    gate_grad = lax.all_to_all(token_gate_grad, "seq", 0, 0, tiled=True).reshape(EXPERTS, TOK).T
-    routed_grad, gate_grad, expert_grads, near, far = tie(
-        routed_grad, gate_grad, expert_grads, near, far
-    )
-    expert_grads = lax.psum_scatter(
-        expert_grads.reshape(2, 8 * 192, 1024), "wshard", scatter_dimension=1, tiled=True
-    ).astype(f32)
-
-    chosen_here = jnp.any(routes[0][:, :, None] == expert_range, axis=1)
-    logits = jnp.dot(normed_ffn, weight_router, preferred_element_type=f32)
-    peak = jnp.max(jnp.where(chosen_here, logits, -jnp.inf), axis=-1, keepdims=True)
-    raised = jnp.where(chosen_here, jnp.exp(logits - peak), 0.0)
-    gates = raised / jnp.sum(raised, axis=-1, keepdims=True)
-    chosen_grad = gates * (gate_grad - jnp.sum(gates * gate_grad, axis=-1, keepdims=True))
-    logit_grad = chosen_grad.astype(bf16)
-    normed_ffn_grad = routed_grad + jnp.einsum(
-        "te,de->td", logit_grad, weight_router, preferred_element_type=f32
-    )
-    upstream = cotangent[0].astype(f32)
-    hidden_grad = upstream + rms_pull(hidden, hidden_scale, gain_ffn, normed_ffn_grad)
-    branch_grad = hidden_grad.astype(bf16)
-    attended_grad = jnp.einsum(
-        "td,qd->tq", branch_grad, weight_out, preferred_element_type=f32
-    ).astype(bf16)
-    head_grad = lax.all_to_all(
-        attended_grad.reshape(TOK, HEADS, HEAD_DIM).transpose(1, 0, 2), "seq", 0, 0, tiled=True
-    ).reshape(GROUP, HEAD_DIM)
-
-    grad_router = jnp.einsum("td,te->de", normed_ffn, logit_grad, preferred_element_type=f32)
-    grad_norm_ffn = jnp.sum(normed_ffn_grad * hidden * hidden_scale, axis=0)
-    grad_out = jnp.einsum("tq,td->qd", attended, branch_grad, preferred_element_type=f32)
-    shared_grads = jnp.concatenate(
-        [grad_out, grad_router, grad_norm_ffn[:, None], jnp.zeros((WIDTH, 95), f32)], axis=1
-    ).astype(bf16)
-    moved = seq_sum_by_x(near[2:4], far[2:4])
-    head_grad, shared_grads = tie(head_grad, shared_grads)
-    shared_grads = jnp.sum(
-        lax.all_to_all(shared_grads.reshape(128, 8, 1152), BOTH, 0, 0, tiled=True).astype(f32),
-        axis=0,
-    )
+    token_gate_grad = jnp.take(jnp.concatenate([near[2], far[2]], axis=0), blocks, axis=0)
+    gate_grad = lax.all_to_all(token_gate_grad, "seq", 0, 0, tiled=True).reshape(EXPERTS, TOK)
+    along = jnp.arange(4, dtype=i32)
+    expert_grads = expert_weight_grads((own_y - along) % 4, *saved)
+    far_terms, expert_grads = tie(far_terms, expert_grads)
+    crossed = send(add_low(*far_terms), 1, 0)
+    crossed, gate_grad, expert_grads, moved = tie(crossed, gate_grad, expert_grads, moved)
+
+    chosen_here = jnp.any(routes[0].T[None] == expert_range[:, None, None], axis=1).astype(f32)
+    hidden_grad, branch_grad, logit_grad, scaled_grad, attended_grad = hidden_back(
+        near_terms, crossed, hidden, normed_ffn, gate_grad, chosen_here, router_t, cotangent[0], gain_ffn, shared
+    )
+    head_grad = lax.all_to_all(attended_grad, "seq", 0, 0, tiled=True).reshape(GROUP, HEAD_DIM)
+    shared_grads = shared_weight_grads(attended, branch_grad, normed_ffn, logit_grad, scaled_grad)
+
+    far_down, far_up = send_w(expert_grads[2, 0], 0, -1), send_w(expert_grads[2, 1], 0, 1)
+    below = jnp.stack([add_low(expert_grads[1, 0], far_down), expert_grads[1, 1]])
+    above = jnp.stack([expert_grads[3, 0], add_low(expert_grads[3, 1], far_up)])
+    head_grad, shared_grads, below, above = tie(head_grad, shared_grads, below, above)
+    expert_terms = (expert_grads[0], send_w(below, 0, -1), send_w(above, 0, 1))
+
+    by_x = [t.reshape(2, 4, TOK, WIDTH).transpose(1, 0, 2, 3) for t in (moved[0], swap_cores(moved[1]))]
+    moved_parts = [add_low(by_x[0][i], by_x[1][i]) for i in range(4)]
+    moved_terms = [moved_parts[0]] + [
+        send(moved_parts[i], 0, -b) for i, b in ((1, 1), (2, 3), (3, 2))
+    ]
+    shared_grads = lax.all_to_all(shared_grads.reshape(128, 8, 1152), BOTH, 0, 0, tiled=True)
     grads = attend_back(q, k, v, head_grad, attended_t, lse, begin)
-    grads, moved = tie(grads, moved)
-    output = (hidden + moved).astype(bf16)
+    grads, moved_terms = tie(grads, moved_terms)
+    moved_crossed = send(add_low(*[t[1] for t in moved_terms]), 1, 0)
+    *far_part, grad_head = project_back(
+        places[8:], normed_far, grads, head_weights, cosine, sine, ()
+    )
+    far_part, expert_terms = tie(far_part, expert_terms)
+    far_terms = sum_along_z(*far_part)
     *near_part, grad_head = project_back(
-        places[:8], normed_near, grads, head_weights, cosine, sine, ()
-    )
+        places[:8], normed_near, grads, head_weights, cosine, sine, (grad_head,)
+    )
+    near_part, shared_grads, moved_crossed = tie(near_part, shared_grads, moved_crossed)
     near_terms = sum_along_z(*near_part)
-    *far_part, grad_head = project_back(
-        places[8:], normed_far, grads, head_weights, cosine, sine, (grad_head,)
-    )
-    far_terms = sum_along_z(*far_part)
     grad_heads = lax.all_to_all(
         grad_head.astype(bf16).reshape(128, 8, 256), BOTH, 0, 0, tiled=True
     )
     grad_heads, far_terms = tie(grad_heads, far_terms)
-    normed_grad = sum_across(near_terms, far_terms)
+    crossed = send(add_low(*far_terms), 1, 0)
+    expert_grads = add_low(*expert_terms)
+    kept = lax.dynamic_index_in_dim(expert_grads, own_x, 0, keepdims=False)
+    sent = lax.dynamic_index_in_dim(expert_grads, 1 - own_x, 0, keepdims=False)
+    expert_grads = kept.astype(f32) + send_w(sent, 1, 0).astype(f32)
+    total = lambda terms: sum([t.astype(f32) for t in terms])
+    output = (hidden + total([t[0] for t in moved_terms] + [moved_crossed])).astype(bf16)
+    normed_grad = total(near_terms + [crossed])
+    shared_grads = jnp.sum(shared_grads.astype(f32), axis=0)
     grad_heads = jnp.sum(grad_heads.reshape(16, 8, 8, 256).astype(f32), axis=1).transpose(1, 0, 2)
     kv_sum = lambda start: jnp.sum(
         grad_heads[:, :, start : start + HEAD_DIM].reshape(8, KV_HEADS, 2, HEAD_DIM), axis=2
@@ -692,6 +823,7 @@
         axis=1,
     )
     grad_norm_attn = jnp.sum(grad_qkv * w_qkv.astype(f32), axis=1) / norm_attn.astype(f32)
+    inputs = rows.astype(f32)
     grad_input = hidden_grad + rms_pull(inputs, inverse_rms(inputs), gain_attn, normed_grad)
     return (
         output[None],

time: 688 us -> 611 us (0.89)
  waiting for transfers between devices: 219 us -> 147 us
  between operations: 15.4 us -> 2.19 us
  Pallas kernels: 135 us -> 147 us
  other arithmetic: 84 us -> 72 us
  blocking collectives: 0 us -> 11.8 us
  local copies, waits for them, and re-layouts: 81.7 us -> 93.2 us
  matrix products: 10.7 us -> 0.15 us
    all_to_all x2, waiting for transfers between devices: 65.9 us -> 2.94 us  [the longest x1 2.94 us: local(): lax.all_to_all(attended_grad, 'seq', 0, 0, tiled=True)]
    ppermute x40 -> x39, waiting for transfers between devices: 143 us -> 119 us  [send(): return lax.ppermute(rows, 'seq', shift_perm(a, b))]
    unnamed x130 -> x181, local copies, waits for them, and re-layouts: 28.8 us -> 42.9 us
    another operation x6 -> x11, other arithmetic: 10.5 us -> 23.7 us  [the longest x6 15.6 us: both_cores(): mine = jnp.stack(parts)]
    ppermute x0 -> x10, starting transfers between devices: none -> 12.7 us  [send_w(): return lax.ppermute(rows, 'wshard', pairs)]
    all_to_all x0 -> x1, blocking collectives: none -> 11.8 us  [local(): lax.all_to_all(token_gate_grad, 'seq', 0, 0, tiled=True)]
    concatenate x1, local copies, waits for them, and re-layouts: 12.4 us -> 0.72 us  [local(): expert_rows = jnp.concatenate([w_gate_up, w_down], axis=1)]
    dot_general x6 -> x0, matrix products: 10.6 us -> none  [the longest x1 3.4 us: local(): jnp.einsum('tq,td->qd', attended, branch_grad, preferred_element_type=f32)]
  transfers between devices with their start and end apart: 63 -> 67, of which waited for: 24 -> 21; matrix products, arithmetic and copies ran while one was open for 22% -> 18% of each run, Pallas kernels for 20% -> 24%
where the time goes in v4:
time: 611 us; the launch traced here: 605 us
  waiting for transfers between devices  147 us (24%)
  Pallas kernels  147 us (24%)
  starting transfers between devices  131 us (21%)
  local copies, waits for them, and re-layouts  93.2 us (15%)
  other arithmetic  72 us (12%)
  blocking collectives  11.8 us (2%)
    ppermute x39, waiting for transfers between devices, send(): return lax.ppermute(rows, 'seq', shift_perm(a, b))  119 us
    ppermute x39, starting transfers between devices, send(): return lax.ppermute(rows, 'seq', shift_perm(a, b))  72.7 us
    pallas_call x2, Pallas kernels, run_experts(): pl.pallas_call(experts_kernel, grid_spec=pltpu.PrefetchScalarGridSpec(num...  47.2 us
    unnamed x181, local copies, waits for them, and re-layouts  42.9 us
    pallas_call x1, Pallas kernels, attend_back(): pl.pallas_call(attend_back_kernel, grid=(GROUP // BLOCK,), in_specs=[rows...  26.1 us
    pallas_call x1, Pallas kernels, attend(): pl.pallas_call(attend_kernel, grid=(GROUP // BLOCK,), in_specs=[rows, who...  19.7 us
    convert_element_type x8, other arithmetic, add_low(): return sum([t.astype(f32) for t in terms]).astype(bf16)  19.5 us
    pallas_call x2, Pallas kernels, project(): pl.pallas_call(project_kernel, grid_spec=pltpu.PrefetchScalarGridSpec(num...  17 us
  transfers between devices with their start and end apart: 67, of which 21 were waited for; matrix products, arithmetic and copies ran while one was open for 18% of the time, Pallas kernels for 24%

profile of v4, /device:TPU:0, one launch (start us, length us, event | category | flops | bytes accessed | tf_op | source)
XLA Modules:
  0.0 604.6 jit_solution(16118310865473232863)
XLA Ops:
  10.2 8.8 %all-to-all-start = ((bf16[128,8,256]{2,1,0:T(8,128)(2,1)}), bf16[128,8,256]{2,1,0:T(8,128)(2,1)S(1)}, u32[]{:S(2)}, u32[]{:S(2)}) async-start(bf16[128,8,256]{2,1,0:T(8,128)(2,1)} %bitcast.8), calls=%async_computation | async-start | bytes 1048576 | tf_op jit(solution)/shard_map/all_to_all | solution.py:677
  22.0 6.4 %multiply_sine_fusion = (f32[3584,32]{1,0:T(8,128)S(1)}, f32[3584,32]{1,0:T(8,128)S(1)}) fusion(f32[32]{0:T(128)S(1)} %multiply_power_fusion, f32[3584]{0:T(1024)S(1)} %get-tuple-element.284), kind=kLoop, calls=%fused_computation.7 | loop fusion | flops 114688 | bytes 931968 | tf_op jit(solution)/shard_map/sin | solution.py:132
  35.5 7.3 %collective-permute-done.8 = bf16[2,192,1024]{2,1,0:T(8,128)(2,1)} collective-permute-done((bf16[2,192,1024]{2,1,0:T(8,128)(2,1)}, bf16[2,192,1024]{2,1,0:T(8,128)(2,1)}, u32[]{:S(2)}, u32[]{:S(2)}) %collective-permute-start.8) | collective-permute-done | bytes 786464 | tf_op jit(solution)/shard_map/ppermute | solution.py:97
  51.2 10.7 %collective-permute-done = bf16[224,1024]{1,0:T(8,128)(2,1)} collective-permute-done((bf16[224,1024]{1,0:T(8,128)(2,1)S(1)}, bf16[224,1024]{1,0:T(8,128)(2,1)}, u32[]{:S(2)}, u32[]{:S(2)}) %collective-permute-start) | collective-permute-done | bytes 458784 | tf_op jit(solution)/shard_map/ppermute | solution.py:50
  74.4 8.5 %shard_map.178 = (bf16[8,224,1024]{2,1,0:T(8,128)(2,1)S(1)}, bf16[3584,64]{1,0:T(8,128)(2,1)S(1)}, bf16[3584,64]{1,0:T(8,128)(2,1)S(1)}, bf16[3584,64]{1,0:T(8,128)(2,1)S(1)}) custom-call(s32[8]{0:T(128)S(1)} %get-tuple-element.287.places, bf16[4,224,1024]{2,1,0:T(8,128)(2,1)} %pad_maximum_fusion.4.mine, bf16[4,224,1024]{2,1,0:T(8,128)(2,1)} %collective-permute-done.7.other, ...), custom_call_target="tpu_custom_call" | custom-call | flops 939524096 | bytes 10485760 | tf_op jit(solution)/shard_map/pallas_call | solution.py:169
  92.3 6.6 %all-to-all-start.2 = ((bf16[16,64,1152]{2,1,0:T(8,128)(2,1)}), bf16[16,64,1152]{2,1,0:T(8,128)(2,1)}, u32[]{:S(2)}, u32[]{:S(2)}) async-start(bf16[16,64,1152]{2,1,0:T(8,128)(2,1)} %broadcast_in_dim.115), calls=%async_computation.2 | async-start | bytes 4718592 | tf_op jit(solution)/shard_map/all_to_all | solution.py:714
  106.1 8.5 %shard_map.179 = (bf16[8,224,1024]{2,1,0:T(8,128)(2,1)S(1)}, bf16[3584,64]{1,0:T(8,128)(2,1)S(1)}, bf16[3584,64]{1,0:T(8,128)(2,1)S(1)}, bf16[3584,64]{1,0:T(8,128)(2,1)S(1)}) custom-call(s32[8]{0:T(128)S(1)} %get-tuple-element.288.places, bf16[4,224,1024]{2,1,0:T(8,128)(2,1)} %pad_maximum_fusion.5.mine, ...), custom_call_target="tpu_custom_call", output_to_operand_aliasing={{1}: (7, {}), {2}: (8, {}), {3}: (9, {})} | custom-call | flops 939524096 | bytes 10485760 | tf_op jit(solution)/shard_map/pallas_call | solution.py:169
  124.9 19.7 %shard_map.180 = (bf16[3584,64]{1,0:T(8,128)(2,1)S(1)}, f32[64,3584]{1,0:T(8,128)S(1)}, f32[1,3584]{1,0:T(1,128)S(1)}) custom-call(bf16[3584,64]{1,0:T(8,128)(2,1)S(1)} %get-tuple-element.145.q_ref, bf16[3584,64]{1,0:T(8,128)(2,1)S(1)} %get-tuple-element.146.k_ref, bf16[3584,64]{1,0:T(8,128)(2,1)S(1)} %get-tuple-element.147.v_ref, ...), custom_call_target="tpu_custom_call" | custom-call | flops 7247757312 | bytes 4194304 | tf_op jit(solution)/shard_map/pallas_call | solution.py:298
  158.3 10.6 %collective-permute-done.24 = bf16[240,1024]{1,0:T(8,128)(2,1)S(1)} collective-permute-done((bf16[240,1024]{1,0:T(8,128)(2,1)}, bf16[240,1024]{1,0:T(8,128)(2,1)S(1)}, u32[]{:S(2)}, u32[]{:S(2)}) %collective-permute-start.24) | collective-permute-done | bytes 491552 | tf_op jit(solution)/shard_map/ppermute | solution.py:50
  168.9 9.9 %collective-permute-done.25 = bf16[240,1024]{1,0:T(8,128)(2,1)S(1)} collective-permute-done((bf16[240,1024]{1,0:T(8,128)(2,1)}, bf16[240,1024]{1,0:T(8,128)(2,1)S(1)}, u32[]{:S(2)}, u32[]{:S(2)}) %collective-permute-start.25) | collective-permute-done | bytes 491552 | tf_op jit(solution)/shard_map/ppermute | solution.py:50
  185.6 5.5 all-to-all-start.3
  193.0 10.5 %all-to-all-done.3 = bf16[16,224,64]{1,2,0:T(8,128)(2,1)} async-done(((bf16[16,224,64]{1,2,0:T(8,128)(2,1)}), bf16[16,224,64]{1,2,0:T(8,128)(2,1)}, u32[]{:S(2)}, u32[]{:S(2)}) %all-to-all-start.3) | async-done | bytes 458784 | tf_op jit(solution)/shard_map/all_to_all | solution.py:746
  211.2 10.4 %collective-permute-start.28 = (bf16[224,1024]{1,0:T(8,128)(2,1)S(1)}, bf16[224,1024]{1,0:T(8,128)(2,1)}, u32[]{:S(2)}, u32[]{:S(2)}) collective-permute-start(bf16[224,1024]{1,0:T(8,128)(2,1)S(1)} %get-tuple-element.162.normed_ref), channel_id=1, source_target_pairs={{0,16},{8,24},{16,32},{24,40},{32,48},{40,56},{48,0},{56,8},{64,80... | collective-permute-start | bytes 1376264 | tf_op jit(solution)/shard_map/ppermute | solution.py:50
  229.7 5.4 collective-permute-done.28
  235.0 8.6 %collective-permute-done.29 = bf16[224,1024]{1,0:T(8,128)(2,1)} collective-permute-done((bf16[224,1024]{1,0:T(8,128)(2,1)S(1)}, bf16[224,1024]{1,0:T(8,128)(2,1)}, u32[]{:S(2)}, u32[]{:S(2)}) %collective-permute-start.29) | collective-permute-done | bytes 458784 | tf_op jit(solution)/shard_map/ppermute | solution.py:50
  266.1 23.6 %shard_map.182 = (bf16[4,224,1024]{2,1,0:T(8,128)(2,1)}, bf16[4,224,1024]{2,1,0:T(8,128)(2,1)}, f32[8,2,224]{2,1,0:T(2,128)}, bf16[8,224,1024]{2,1,0:T(8,128)(2,...) custom-call(s32[9]{0:T(128)} %stack.181.own_ref, ...), custom_call_target="tpu_custom_call" | custom-call | flops 15032385536 | bytes 25165824 | tf_op jit(solution)/shard_map/pallas_call | solution.py:470
  301.8 23.6 %shard_map.183 = (bf16[4,224,1024]{2,1,0:T(8,128)(2,1)}, bf16[4,224,1024]{2,1,0:T(8,128)(2,1)}, f32[8,2,224]{2,1,0:T(2,128)}, bf16[8,224,1024]{2,1,0:T(8,128)(2,...) custom-call(s32[9]{0:T(128)} %stack.181.own_ref, ...), custom_call_target="tpu_custom_call", output_to_operand_aliasing={{3}: (14, {}), {4}: (15, {}), {5}: (16, {}), {6}: (17, {}),... | custom-call | flops 15032385536 | bytes 25165824 | tf_op jit(solution)/shard_map/pallas_call | solution.py:470
  335.1 16.2 %shard_map.184 = bf16[4,2,2,192,1024]{4,3,2,1,0:T(8,128)(2,1)} custom-call(s32[4]{0:T(128)S(1)} %and_select_fusion.8.order, bf16[2,1152,1024]{2,1,0:T(8,128)(2,1)} %get-tuple-element.188.x_ref, bf16[2,1152,1024]{2,1,0:T(8,128)(2,1)} %get-tuple-element.189.dh_ref, bf16[2,1152,512]{2,1,0:T(8,128)(2,1)S(1)} %copy-done.58, ...), custom_call_target="tpu_custom_call" | custom-call | flops 8589934592 | bytes 14680064 | tf_op jit(solution)/shard_map/pallas_call | solution.py:530
  351.3 5.4 collective-permute-done.38
  359.6 11.8 %all_to_all.40 = f32[16,2,224]{2,1,0:T(2,128)S(1)} all-to-all(f32[16,2,224]{2,1,0:T(2,128)S(1)} %broadcast_select_fusion.1), channel_id=1, replica_groups=mesh['seq'=16,'wshard'=8] {'seq'}, dimensions={0} | all-to-all | bytes 57344 | tf_op jit(solution)/shard_map/all_to_all | solution.py:765
  378.0 4.3 shard_map.185
  388.0 4.7 all-to-all-start.5
  392.7 4.3 copy.152
  415.9 8.8 %all-to-all-start.6 = ((bf16[128,8,1152]{2,1,0:T(8,128)(2,1)}), bf16[128,8,1152]{2,1,0:T(8,128)(2,1)}, u32[]{:S(2)}, u32[]{:S(2)}) async-start(bf16[128,8,1152]{2,1,0:T(8,128)(2,1)} %bitcast.190), calls=%async_computation.6 | async-start | bytes 4718592 | tf_op jit(solution)/shard_map/all_to_all | solution.py:790
  435.8 26.1 %shard_map.187 = (f32[3584,64]{1,0:T(8,128)}, f32[3584,64]{1,0:T(8,128)}, f32[3584,64]{1,0:T(8,128)}) custom-call(bf16[3584,64]{1,0:T(8,128)(2,1)S(1)} %copy-done.34, bf16[3584,64]{1,0:T(8,128)(2,1)S(1)} %copy-done.38, bf16[3584,64]{1,0:T(8,128)(2,1)S(1)} %copy-done.42, bf16[3584,64]{1,0:T(8,128)(2,1)S(1)} %bitcast.199, f32[64,3584]{1,0:T(8,128)S(1)} %copy-done.60, ...), custom_call_target="tpu_custom_call" | custom-call | flops 18119393280 | bytes 8388608 | tf_op jit(solution)/shard_map/pallas_call | solution.py:358
  461.9 8.0 %collective-permute-done.44 = bf16[2,224,1024]{2,1,0:T(8,128)(2,1)S(1)} collective-permute-done((bf16[2,224,1024]{2,1,0:T(8,128)(2,1)}, bf16[2,224,1024]{2,1,0:T(8,128)(2,1)S(1)}, u32[]{:S(2)}, u32[]{:S(2)}) %collective-permute-start.44) | collective-permute-done | bytes 917536 | tf_op jit(solution)/shard_map/ppermute | solution.py:50
  470.0 25.6 %collective-permute-done.45 = bf16[2,224,1024]{2,1,0:T(8,128)(2,1)S(1)} collective-permute-done((bf16[2,224,1024]{2,1,0:T(8,128)(2,1)S(1)}, bf16[2,224,1024]{2,1,0:T(8,128)(2,1)S(1)}, u32[]{:S(2)}, u32[]{:S(2)}) %collective-permute-start.45) | collective-permute-done | bytes 917536 | tf_op jit(solution)/shard_map/ppermute | solution.py:50
  503.6 7.2 %shard_map.188 = (bf16[4,224,1024]{2,1,0:T(8,128)(2,1)S(1)}, bf16[4,224,1024]{2,1,0:T(8,128)(2,1)}, f32[1024,256]{1,0:T(8,128)S(1)}) custom-call(s32[8]{0:T(128)S(1)} %get-tuple-element.288.places, bf16[8,224,1024]{2,1,0:T(8,128)(2,1)S(1)} %copy-done.19, f32[3584,64]{1,0:T(8,128)S(1)} %copy-done.6, f32[3584,64]{1,0:T(8,128)S(1)} %copy-done.8, ...), custom_call_target="tpu_custom_call" | custom-call | flops 1879048192 | bytes 12582912 | tf_op jit(solution)/shard_map/pallas_call | solution.py:219
  522.3 6.2 %shard_map.189 = (bf16[4,224,1024]{2,1,0:T(8,128)(2,1)S(1)}, bf16[4,224,1024]{2,1,0:T(8,128)(2,1)S(1)}, f32[1024,256]{1,0:T(8,128)S(1)}) custom-call(s32[8]{0:T(128)S(1)} %get-tuple-element.287.places, bf16[8,224,1024]{2,1,0:T(8,128)(2,1)S(1)} %copy-done.13, f32[3584,64]{1,0:T(8,128)S(1)} %copy-done.7, f32[3584,64]{1,0:T(8,128)S(1)} %copy-done.9, ...), custom_call_target="tpu_custom_call" | custom-call | flops 1879048192 | bytes 12582912 | tf_op jit(solution)/shard_map/pallas_call | solution.py:219
  538.8 5.2 all-to-all-start.7
  566.3 12.6 %collective-permute-done.55 = bf16[224,1024]{1,0:T(8,128)(2,1)S(1)} collective-permute-done((bf16[224,1024]{1,0:T(8,128)(2,1)S(1)}, bf16[224,1024]{1,0:T(8,128)(2,1)S(1)}, u32[]{:S(2)}, u32[]{:S(2)}) %collective-permute-start.55) | collective-permute-done | bytes 458784 | tf_op jit(solution)/shard_map/ppermute | solution.py:50
  587.6 10.7 %collective-permute-done.49 = bf16[224,1024]{1,0:T(8,128)(2,1)} collective-permute-done((bf16[224,1024]{1,0:T(8,128)(2,1)}, bf16[224,1024]{1,0:T(8,128)(2,1)}, u32[]{:S(2)}, u32[]{:S(2)}) %collective-permute-start.49) | collective-permute-done | bytes 458784 | tf_op jit(solution)/shard_map/ppermute | solution.py:50
  (417 shorter events, 260.7 us)
Async XLA Ops:
  0.7 32.1 %collective-permute-start.4 = (bf16[224,1024]{1,0:T(8,128)(2,1)}, bf16[224,1024]{1,0:T(8,128)(2,1)}, u32[]{:S(2)}, u32[]{:S(2)}) collective-permute-start(bf16[224,1024]{1,0:T(8,128)(2,1)} %bitcast.191), channel_id=1, source_target_pairs={{0,16},{8,24},{16,32},{24,40},{32,48},{40,56},{48,0},{56,8},{64,80... | collective-permute-start | bytes 1376264 | tf_op jit(solution)/shard_map/ppermute | solution.py:50
  2.7 30.0 %collective-permute-start.5 = (bf16[224,1024]{1,0:T(8,128)(2,1)}, bf16[224,1024]{1,0:T(8,128)(2,1)}, u32[]{:S(2)}, u32[]{:S(2)}) collective-permute-start(bf16[224,1024]{1,0:T(8,128)(2,1)} %bitcast.192), channel_id=1, source_target_pairs={{0,48},{8,56},{16,0},{24,8},{32,16},{40,24},{48,32},{56,40},{64,11... | collective-permute-start | bytes 1376264 | tf_op jit(solution)/shard_map/ppermute | solution.py:50
  35.5 29.9 %collective-permute-start.7 = (bf16[4,224,1024]{2,1,0:T(8,128)(2,1)}, bf16[4,224,1024]{2,1,0:T(8,128)(2,1)}, u32[]{:S(2)}, u32[]{:S(2)}) collective-permute-start(bf16[4,224,1024]{2,1,0:T(8,128)(2,1)} %pad_maximum_fusion.4.mine), channel_id=1, source_target_pairs={{0,8},{8,0},{16,24},{24,16},{32,40},{40,32},{48,56},{56,48},{64,72... | collective-permute-start | bytes 5505032 | tf_op jit(solution)/shard_map/ppermute | solution.py:54
  45.5 42.1 %collective-permute-start.10 = (bf16[2,2,192,1024]{3,2,1,0:T(8,128)(2,1)}, bf16[2,2,192,1024]{3,2,1,0:T(8,128)(2,1)}, u32[]{:S(2)}, u32[]{:S(2)}) collective-permute-start(bf16[2,2,192,1024]{3,2,1,0:T(8,128)(2,1)} %pad_maximum_fusion.8.refs_0_), channel_id=1, source_target_pairs={{0,6},{1,7},{2,0},{3,1},{4,2},{5,3},{6,4},{7,5},{8,14},{9,15},{10,... | collective-permute-start | bytes 4718600 | tf_op jit(solution)/shard_map/ppermute | solution.py:97
  48.3 39.4 %collective-permute-start.9 = (bf16[2,2,192,1024]{3,2,1,0:T(8,128)(2,1)}, bf16[2,2,192,1024]{3,2,1,0:T(8,128)(2,1)}, u32[]{:S(2)}, u32[]{:S(2)}) collective-permute-start(bf16[2,2,192,1024]{3,2,1,0:T(8,128)(2,1)} %pad_maximum_fusion.8.refs_0_), channel_id=1, source_target_pairs={{0,2},{1,3},{2,4},{3,5},{4,6},{5,7},{6,0},{7,1},{8,10},{9,11},{10,... | collective-permute-start | bytes 4718600 | tf_op jit(solution)/shard_map/ppermute | solution.py:97
  92.3 54.2 %all-to-all-start.2 = ((bf16[16,64,1152]{2,1,0:T(8,128)(2,1)}), bf16[16,64,1152]{2,1,0:T(8,128)(2,1)}, u32[]{:S(2)}, u32[]{:S(2)}) async-start(bf16[16,64,1152]{2,1,0:T(8,128)(2,1)} %broadcast_in_dim.115), calls=%async_computation.2 | async-start | bytes 4718592 | tf_op jit(solution)/shard_map/all_to_all | solution.py:714
  102.6 43.9 %collective-permute-start.13 = (bf16[2,192,1024]{2,1,0:T(8,128)(2,1)S(1)}, bf16[2,192,1024]{2,1,0:T(8,128)(2,1)}, u32[]{:S(2)}, u32[]{:S(2)}) collective-permute-start(bf16[2,192,1024]{2,1,0:T(8,128)(2,1)S(1)} %slice_bitcast_fusion.5), channel_id=1, source_target_pairs={{0,6},{1,7},{2,0},{3,1},{4,2},{5,3},{6,4},{7,5},{8,14},{9,15},{10,... | collective-permute-start | bytes 2359304 | tf_op jit(solution)/shard_map/ppermute | solution.py:97
  116.5 30.0 %collective-permute-start.14 = (bf16[240,1024]{1,0:T(8,128)(2,1)S(1)}, bf16[240,1024]{1,0:T(8,128)(2,1)}, u32[]{:S(2)}, u32[]{:S(2)}) collective-permute-start(bf16[240,1024]{1,0:T(8,128)(2,1)S(1)} %fusion.22), channel_id=1, source_target_pairs={{0,16},{8,24},{16,32},{24,40},{32,48},{40,56},{48,0},{56,8},{64,80... | collective-permute-start | bytes 1474568 | tf_op jit(solution)/shard_map/ppermute | solution.py:50
  118.4 28.1 %collective-permute-start.15 = (bf16[240,1024]{1,0:T(8,128)(2,1)S(1)}, bf16[240,1024]{1,0:T(8,128)(2,1)}, u32[]{:S(2)}, u32[]{:S(2)}) collective-permute-start(bf16[240,1024]{1,0:T(8,128)(2,1)S(1)} %fusion.22), channel_id=1, source_target_pairs={{0,48},{8,56},{16,0},{24,8},{32,16},{40,24},{48,32},{56,40},{64,11... | collective-permute-start | bytes 1474568 | tf_op jit(solution)/shard_map/ppermute | solution.py:50
  119.7 30.3 %collective-permute-start.16 = (bf16[240,1024]{1,0:T(8,128)(2,1)S(1)}, bf16[240,1024]{1,0:T(8,128)(2,1)}, u32[]{:S(2)}, u32[]{:S(2)}) collective-permute-start(bf16[240,1024]{1,0:T(8,128)(2,1)S(1)} %fusion.22), channel_id=1, source_target_pairs={{0,32},{8,40},{16,48},{24,56},{32,0},{40,8},{48,16},{56,24},{64,96... | collective-permute-start | bytes 1474568 | tf_op jit(solution)/shard_map/ppermute | solution.py:50
  152.8 58.4 %collective-permute-start.18 = (bf16[4,240,1024]{2,1,0:T(8,128)(2,1)}, bf16[4,240,1024]{2,1,0:T(8,128)(2,1)}, u32[]{:S(2)}, u32[]{:S(2)}) collective-permute-start(bf16[4,240,1024]{2,1,0:T(8,128)(2,1)} %pad_maximum_fusion.g_mine), channel_id=1, source_target_pairs={{0,8},{8,0},{16,24},{24,16},{32,40},{40,32},{48,56},{56,48},{64,72... | collective-permute-start | bytes 5898248 | tf_op jit(solution)/shard_map/ppermute | solution.py:54
  183.3 70.0 %collective-permute-start.27 = (bf16[4,240,1024]{2,1,0:T(8,128)(2,1)}, bf16[4,240,1024]{2,1,0:T(8,128)(2,1)}, u32[]{:S(2)}, u32[]{:S(2)}) collective-permute-start(bf16[4,240,1024]{2,1,0:T(8,128)(2,1)} %pad_maximum_fusion.1.g_mine), channel_id=1, source_target_pairs={{0,8},{8,0},{16,24},{24,16},{32,40},{40,32},{48,56},{56,48},{64,72... | collective-permute-start | bytes 5898248 | tf_op jit(solution)/shard_map/ppermute | solution.py:54
  249.0 40.8 %collective-permute-start.20 = (bf16[224,1024]{1,0:T(8,128)(2,1)}, bf16[224,1024]{1,0:T(8,128)(2,1)}, u32[]{:S(2)}, u32[]{:S(2)}) collective-permute-start(bf16[224,1024]{1,0:T(8,128)(2,1)} %collective-permute-done.19), channel_id=1, source_target_pairs={{0,16},{8,24},{16,32},{24,40},{32,48},{40,56},{48,0},{56,8},{64,80... | collective-permute-start | bytes 1376264 | tf_op jit(solution)/shard_map/ppermute | solution.py:50
  250.2 39.6 %collective-permute-start.21 = (bf16[224,1024]{1,0:T(8,128)(2,1)}, bf16[224,1024]{1,0:T(8,128)(2,1)}, u32[]{:S(2)}, u32[]{:S(2)}) collective-permute-start(bf16[224,1024]{1,0:T(8,128)(2,1)} %collective-permute-done.19), channel_id=1, source_target_pairs={{0,48},{8,56},{16,0},{24,8},{32,16},{40,24},{48,32},{56,40},{64,11... | collective-permute-start | bytes 1376264 | tf_op jit(solution)/shard_map/ppermute | solution.py:50
  252.3 37.5 %collective-permute-start.22 = (bf16[224,1024]{1,0:T(8,128)(2,1)}, bf16[224,1024]{1,0:T(8,128)(2,1)}, u32[]{:S(2)}, u32[]{:S(2)}) collective-permute-start(bf16[224,1024]{1,0:T(8,128)(2,1)} %collective-permute-done.19), channel_id=1, source_target_pairs={{0,32},{8,40},{16,48},{24,56},{32,0},{40,8},{48,16},{56,24},{64,96... | collective-permute-start | bytes 1376264 | tf_op jit(solution)/shard_map/ppermute | solution.py:50
  295.6 29.8 %collective-permute-start.33 = (bf16[224,1024]{1,0:T(8,128)(2,1)}, bf16[224,1024]{1,0:T(8,128)(2,1)S(1)}, u32[]{:S(2)}, u32[]{:S(2)}) collective-permute-start(bf16[224,1024]{1,0:T(8,128)(2,1)} %get-tuple-element.277), channel_id=1, source_target_pairs={{0,48},{8,56},{16,0},{24,8},{32,16},{40,24},{48,32},{56,40},{64,11... | collective-permute-start | bytes 1376264 | tf_op jit(solution)/shard_map/ppermute | solution.py:50
  297.2 28.2 %collective-permute-start.34 = (bf16[224,1024]{1,0:T(8,128)(2,1)}, bf16[224,1024]{1,0:T(8,128)(2,1)}, u32[]{:S(2)}, u32[]{:S(2)}) collective-permute-start(bf16[224,1024]{1,0:T(8,128)(2,1)} %get-tuple-element.276), channel_id=1, source_target_pairs={{0,16},{8,24},{16,32},{24,40},{32,48},{40,56},{48,0},{56,8},{64,80... | collective-permute-start | bytes 1376264 | tf_op jit(solution)/shard_map/ppermute | solution.py:50
  371.5 53.2 %collective-permute-start.43 = (bf16[8,224,1024]{2,1,0:T(8,128)(2,1)}, bf16[8,224,1024]{2,1,0:T(8,128)(2,1)}, u32[]{:S(2)}, u32[]{:S(2)}) collective-permute-start(bf16[8,224,1024]{2,1,0:T(8,128)(2,1)} %get-tuple-element.216), channel_id=1, source_target_pairs={{0,8},{8,0},{16,24},{24,16},{32,40},{40,32},{48,56},{56,48},{64,72... | collective-permute-start | bytes 11010056 | tf_op jit(solution)/shard_map/ppermute | solution.py:54
  375.5 31.9 %collective-permute-start.41 = (bf16[2,192,1024]{2,1,0:T(8,128)(2,1)}, bf16[2,192,1024]{2,1,0:T(8,128)(2,1)}, u32[]{:S(2)}, u32[]{:S(2)}) collective-permute-start(bf16[2,192,1024]{2,1,0:T(8,128)(2,1)} %get-tuple-element.261), channel_id=1, source_target_pairs={{0,6},{1,7},{2,0},{3,1},{4,2},{5,3},{6,4},{7,5},{8,14},{9,15},{10,... | collective-permute-start | bytes 2359304 | tf_op jit(solution)/shard_map/ppermute | solution.py:97
  377.7 29.8 %collective-permute-start.42 = (bf16[2,192,1024]{2,1,0:T(8,128)(2,1)}, bf16[2,192,1024]{2,1,0:T(8,128)(2,1)}, u32[]{:S(2)}, u32[]{:S(2)}) collective-permute-start(bf16[2,192,1024]{2,1,0:T(8,128)(2,1)} %get-tuple-element.259), channel_id=1, source_target_pairs={{0,2},{1,3},{2,4},{3,5},{4,6},{5,7},{6,0},{7,1},{8,10},{9,11},{10,... | collective-permute-start | bytes 2359304 | tf_op jit(solution)/shard_map/ppermute | solution.py:97
  412.7 100.4 %collective-permute-start.52 = (bf16[2,2,192,1024]{3,2,1,0:T(8,128)(2,1)}, bf16[2,2,192,1024]{3,2,1,0:T(8,128)(2,1)}, u32[]{:S(2)}, u32[]{:S(2)}) collective-permute-start(bf16[2,2,192,1024]{3,2,1,0:T(8,128)(2,1)} %pad_maximum_fusion.9), channel_id=1, source_target_pairs={{0,6},{1,7},{2,0},{3,1},{4,2},{5,3},{6,4},{7,5},{8,14},{9,15},{10,... | collective-permute-start | bytes 4718600 | tf_op jit(solution)/shard_map/ppermute | solution.py:97
  415.9 97.1 %collective-permute-start.53 = (bf16[2,2,192,1024]{3,2,1,0:T(8,128)(2,1)}, bf16[2,2,192,1024]{3,2,1,0:T(8,128)(2,1)}, u32[]{:S(2)}, u32[]{:S(2)}) collective-permute-start(bf16[2,2,192,1024]{3,2,1,0:T(8,128)(2,1)} %pad_maximum_fusion.10), channel_id=1, source_target_pairs={{0,2},{1,3},{2,4},{3,5},{4,6},{5,7},{6,0},{7,1},{8,10},{9,11},{10,... | collective-permute-start | bytes 4718600 | tf_op jit(solution)/shard_map/ppermute | solution.py:97
  415.9 116.2 %all-to-all-start.6 = ((bf16[128,8,1152]{2,1,0:T(8,128)(2,1)}), bf16[128,8,1152]{2,1,0:T(8,128)(2,1)}, u32[]{:S(2)}, u32[]{:S(2)}) async-start(bf16[128,8,1152]{2,1,0:T(8,128)(2,1)} %bitcast.190), calls=%async_computation.6 | async-start | bytes 4718592 | tf_op jit(solution)/shard_map/all_to_all | solution.py:790
  430.8 39.2 %collective-permute-start.44 = (bf16[2,224,1024]{2,1,0:T(8,128)(2,1)}, bf16[2,224,1024]{2,1,0:T(8,128)(2,1)S(1)}, u32[]{:S(2)}, u32[]{:S(2)}) collective-permute-start(bf16[2,224,1024]{2,1,0:T(8,128)(2,1)} %get-tuple-element.256), channel_id=1, source_target_pairs={{0,48},{8,56},{16,0},{24,8},{32,16},{40,24},{48,32},{56,40},{64,11... | collective-permute-start | bytes 2752520 | tf_op jit(solution)/shard_map/ppermute | solution.py:50
  433.6 62.0 %collective-permute-start.45 = (bf16[2,224,1024]{2,1,0:T(8,128)(2,1)S(1)}, bf16[2,224,1024]{2,1,0:T(8,128)(2,1)S(1)}, u32[]{:S(2)}, u32[]{:S(2)}) collective-permute-start(bf16[2,224,1024]{2,1,0:T(8,128)(2,1)S(1)} %get-tuple-element.255), channel_id=1, source_target_pairs={{0,16},{8,24},{16,32},{24,40},{32,48},{40,56},{48,0},{56,8},{64,80... | collective-permute-start | bytes 2752520 | tf_op jit(solution)/shard_map/ppermute | solution.py:50
  433.6 62.0 %collective-permute-start.46 = (bf16[2,224,1024]{2,1,0:T(8,128)(2,1)S(1)}, bf16[2,224,1024]{2,1,0:T(8,128)(2,1)S(1)}, u32[]{:S(2)}, u32[]{:S(2)}) collective-permute-start(bf16[2,224,1024]{2,1,0:T(8,128)(2,1)S(1)} %get-tuple-element.254), channel_id=1, source_target_pairs={{0,32},{8,40},{16,48},{24,56},{32,0},{40,8},{48,16},{56,24},{64,96... | collective-permute-start | bytes 2752520 | tf_op jit(solution)/shard_map/ppermute | solution.py:50
  496.9 35.1 %collective-permute-start.47 = (bf16[224,1024]{1,0:T(8,128)(2,1)}, bf16[224,1024]{1,0:T(8,128)(2,1)S(1)}, u32[]{:S(2)}, u32[]{:S(2)}) collective-permute-start(bf16[224,1024]{1,0:T(8,128)(2,1)} %fusion.31), channel_id=1, source_target_pairs={{0,64},{8,72},{16,80},{24,88},{32,96},{40,104},{48,112},{56,120},{... | collective-permute-start | bytes 1376264 | tf_op jit(solution)/shard_map/ppermute | solution.py:50
  513.0 37.5 %collective-permute-start.54 = (bf16[4,224,1024]{2,1,0:T(8,128)(2,1)}, bf16[4,224,1024]{2,1,0:T(8,128)(2,1)}, u32[]{:S(2)}, u32[]{:S(2)}) collective-permute-start(bf16[4,224,1024]{2,1,0:T(8,128)(2,1)} %get-tuple-element.239), channel_id=1, source_target_pairs={{0,8},{8,0},{16,24},{24,16},{32,40},{40,32},{48,56},{56,48},{64,72... | collective-permute-start | bytes 5505032 | tf_op jit(solution)/shard_map/ppermute | solution.py:54
  532.0 29.6 %collective-permute-start.48 = (bf16[4,224,1024]{2,1,0:T(8,128)(2,1)}, bf16[4,224,1024]{2,1,0:T(8,128)(2,1)}, u32[]{:S(2)}, u32[]{:S(2)}) collective-permute-start(bf16[4,224,1024]{2,1,0:T(8,128)(2,1)} %copy-done.57), channel_id=1, source_target_pairs={{0,8},{8,0},{16,24},{24,16},{32,40},{40,32},{48,56},{56,48},{64,72... | collective-permute-start | bytes 5505032 | tf_op jit(solution)/shard_map/ppermute | solution.py:54
  538.8 41.0 %all-to-all-start.7 = ((bf16[128,8,256]{2,1,0:T(8,128)(2,1)}), bf16[128,8,256]{2,1,0:T(8,128)(2,1)S(1)}, u32[]{:S(2)}, u32[]{:S(2)}) async-start(bf16[128,8,256]{2,1,0:T(8,128)(2,1)} %convert_bitcast_fusion), calls=%async_computation.7 | async-start | bytes 1048576 | tf_op jit(solution)/shard_map/all_to_all | solution.py:804
  564.3 34.0 %collective-permute-start.49 = (bf16[224,1024]{1,0:T(8,128)(2,1)}, bf16[224,1024]{1,0:T(8,128)(2,1)}, u32[]{:S(2)}, u32[]{:S(2)}) collective-permute-start(bf16[224,1024]{1,0:T(8,128)(2,1)} %get-tuple-element.264), channel_id=1, source_target_pairs={{0,48},{8,56},{16,0},{24,8},{32,16},{40,24},{48,32},{56,40},{64,11... | collective-permute-start | bytes 1376264 | tf_op jit(solution)/shard_map/ppermute | solution.py:50
  565.5 35.6 %collective-permute-start.50 = (bf16[224,1024]{1,0:T(8,128)(2,1)}, bf16[224,1024]{1,0:T(8,128)(2,1)}, u32[]{:S(2)}, u32[]{:S(2)}) collective-permute-start(bf16[224,1024]{1,0:T(8,128)(2,1)} %get-tuple-element.266), channel_id=1, source_target_pairs={{0,16},{8,24},{16,32},{24,40},{32,48},{40,56},{48,0},{56,8},{64,80... | collective-permute-start | bytes 1376264 | tf_op jit(solution)/shard_map/ppermute | solution.py:50
  (124 other events, 1485.5 us)

commit v5 on v4

--- a/solution.py
+++ b/solution.py
@@ -18,6 +18,8 @@
 STEP_ROWS = 4 * SLOTS
 ALL_ROWS = 16 * SLOTS
 BLOCK = 512
+VMEM_LIMIT = 60 << 20
+PAY = TOK + 32
 
 norm_eps = 1e-06
 rope_base = 10000.0
@@ -74,12 +76,7 @@
 
 
 def gather_far(across):
-    return both_cores([across] + [send(across, 0, b) for b in (1, 3, 2)])
-
-
-def seq_gather(rows):
-    near, across = gather_near(rows)
-    return both_cores(near), gather_far(across)
+    return [across] + [send(across, 0, b) for b in (1, 3, 2)]
 
 
 def add_low(*terms):
@@ -177,7 +174,7 @@
         ),
         out_shape=[jax.ShapeDtypeStruct((8, TOK, WIDTH), bf16), table, table, table],
         input_output_aliases={7 + i: 1 + i for i in range(len(before))},
-        compiler_params=pltpu.CompilerParams(vmem_limit_bytes=32 << 20),
+        compiler_params=pltpu.CompilerParams(vmem_limit_bytes=VMEM_LIMIT),
         cost_estimate=pl.CostEstimate(
             flops=2 * 8 * TOK * WIDTH * 256, bytes_accessed=10 << 20, transcendentals=0
         ),
@@ -234,7 +231,7 @@
             out_specs=[chip, chip, whole((WIDTH, 256))],
         ),
         out_shape=[part, part, jax.ShapeDtypeStruct((WIDTH, 256), f32)],
-        compiler_params=pltpu.CompilerParams(vmem_limit_bytes=32 << 20),
+        compiler_params=pltpu.CompilerParams(vmem_limit_bytes=VMEM_LIMIT),
         cost_estimate=pl.CostEstimate(
             flops=4 * 8 * TOK * WIDTH * 256, bytes_accessed=12 << 20, transcendentals=0
         ),
@@ -262,10 +259,10 @@
     q = q_ref[...]
     begin = begin_ref[...]
 
-    def tile(j, carry, masked):
+    def tile(j, carry, masked, n=1):
         peak, total, out = carry
         start = pl.multiple_of(j * BLOCK, BLOCK)
-        at = pl.ds(start, BLOCK)
+        at = pl.ds(start, n * BLOCK)
         s = lax.dot_general(k_ref[at, :], q, NT, preferred_element_type=f32)
         if masked:
             s = tile_mask(s, start, i * BLOCK, begin)
@@ -284,38 +281,41 @@
     carry = tile(i, carry, True)
     window, shared = key_ranges(i)
     carry = lax.fori_loop(window, i, lambda j, c: tile(j, c, True), carry)
-    peak, total, out = lax.fori_loop(0, shared, lambda j, c: tile(j, c, False), carry)
-    out = out * (1.0 / total)
-    ot_ref[...] = out
-    o_ref[...] = out.T.astype(bf16)
+    pairs = shared // 2
+    carry = lax.fori_loop(0, pairs, lambda j, c: tile(2 * j, c, False, 2), carry)
+    peak, total, out = lax.fori_loop(2 * pairs, shared, lambda j, c: tile(j, c, False), carry)
+    ot_ref[:, pl.ds(pl.multiple_of(i * BLOCK, BLOCK), BLOCK)] = out * (1.0 / total)
     lse_ref[...] = peak + jnp.log(total)
 
+    @pl.when(i == GROUP // BLOCK - 1)
+    def _():
+        for b in range(16):
+            o_ref[b] = ot_ref[:, b * TOK : (b + 1) * TOK].astype(bf16)
+
 
 def attend(q, k, v, begin):
-    whole = pl.BlockSpec((GROUP, HEAD_DIM), lambda i: (0, 0))
+    whole = lambda *shape: pl.BlockSpec(shape, lambda i: (0,) * len(shape))
     rows = pl.BlockSpec((BLOCK, HEAD_DIM), lambda i: (i, 0))
     cols = lambda n: pl.BlockSpec((n, BLOCK), lambda i: (0, i))
     return pl.pallas_call(
         attend_kernel,
         grid=(GROUP // BLOCK,),
-        in_specs=[rows, whole, whole, cols(1)],
-        out_specs=[rows, cols(HEAD_DIM), cols(1)],
+        in_specs=[rows, whole(GROUP, HEAD_DIM), whole(GROUP, HEAD_DIM), cols(1)],
+        out_specs=[whole(16, HEAD_DIM, TOK), whole(HEAD_DIM, GROUP), cols(1)],
         out_shape=[
-            jax.ShapeDtypeStruct((GROUP, HEAD_DIM), bf16),
+            jax.ShapeDtypeStruct((16, HEAD_DIM, TOK), bf16),
             jax.ShapeDtypeStruct((HEAD_DIM, GROUP), f32),
             jax.ShapeDtypeStruct((1, GROUP), f32),
         ],
         scratch_shapes=[pltpu.VMEM((HEAD_DIM, GROUP), bf16)],
-        compiler_params=pltpu.CompilerParams(vmem_limit_bytes=32 << 20),
+        compiler_params=pltpu.CompilerParams(vmem_limit_bytes=VMEM_LIMIT),
         cost_estimate=pl.CostEstimate(
             flops=2 * 27 * BLOCK * BLOCK * 512, bytes_accessed=4 << 20, transcendentals=27 * BLOCK * BLOCK
         ),
     )(q, k, v, begin)
 
 
-def attend_back_kernel(
-    q_ref, k_ref, v_ref, g_ref, ot_ref, lse_ref, begin_ref, dq_ref, dk_ref, dv_ref, kt
-):
+def attend_back_kernel(q_ref, k_ref, v_ref, g_ref, ot_ref, lse_ref, begin_ref, dq_ref, dk_ref, dv_ref, kt, gt):
     i = pl.program_id(0)
 
     @pl.when(i == 0)
@@ -323,46 +323,50 @@
         dk_ref[...] = jnp.zeros_like(dk_ref)
         dv_ref[...] = jnp.zeros_like(dv_ref)
         kt[...] = k_ref[...].T
+        for b in range(16):
+            gt[:, b * TOK : (b + 1) * TOK] = g_ref[b]
 
     q = q_ref[...]
-    g = g_ref[...]
+    g = gt[:, pl.ds(pl.multiple_of(i * BLOCK, BLOCK), BLOCK)]
     begin = begin_ref[...]
     lse = lse_ref[...]
-    inner = jnp.sum(g.T.astype(f32) * ot_ref[...], axis=0, keepdims=True)
-
-    def tile(j, dq, masked):
+    inner = jnp.sum(g.astype(f32) * ot_ref[...], axis=0, keepdims=True)
+
+    def tile(j, dq, masked, n=1):
         start = pl.multiple_of(j * BLOCK, BLOCK)
-        at = pl.ds(start, BLOCK)
+        at = pl.ds(start, n * BLOCK)
         s = lax.dot_general(k_ref[at, :], q, NT, preferred_element_type=f32)
         if masked:
             s = tile_mask(s, start, i * BLOCK, begin)
         p = jnp.exp(s - lse)
-        dp = lax.dot_general(v_ref[at, :], g, NT, preferred_element_type=f32)
+        dp = jnp.dot(v_ref[at, :], g, preferred_element_type=f32)
         ds = (p * (dp - inner)).astype(bf16)
-        dv_ref[at, :] += jnp.dot(p.astype(bf16), g, preferred_element_type=f32)
+        dv_ref[at, :] += lax.dot_general(p.astype(bf16), g, NT, preferred_element_type=f32)
         dk_ref[at, :] += jnp.dot(ds, q, preferred_element_type=f32)
         return dq + jnp.dot(kt[:, at], ds, preferred_element_type=f32)
 
     dq = tile(i, jnp.zeros((HEAD_DIM, BLOCK), f32), True)
     window, shared = key_ranges(i)
     dq = lax.fori_loop(window, i, lambda j, c: tile(j, c, True), dq)
-    dq = lax.fori_loop(0, shared, lambda j, c: tile(j, c, False), dq)
+    pairs = shared // 2
+    dq = lax.fori_loop(0, pairs, lambda j, c: tile(2 * j, c, False, 2), dq)
+    dq = lax.fori_loop(2 * pairs, shared, lambda j, c: tile(j, c, False), dq)
     dq_ref[...] = dq.T * HEAD_DIM**-0.5
 
 
 def attend_back(q, k, v, g, ot, lse, begin):
-    whole = pl.BlockSpec((GROUP, HEAD_DIM), lambda i: (0, 0))
+    whole = lambda *shape: pl.BlockSpec(shape, lambda i: (0,) * len(shape))
     rows = pl.BlockSpec((BLOCK, HEAD_DIM), lambda i: (i, 0))
     cols = lambda n: pl.BlockSpec((n, BLOCK), lambda i: (0, i))
     out = jax.ShapeDtypeStruct((GROUP, HEAD_DIM), f32)
     return pl.pallas_call(
         attend_back_kernel,
         grid=(GROUP // BLOCK,),
-        in_specs=[rows, whole, whole, rows, cols(HEAD_DIM), cols(1), cols(1)],
-        out_specs=[rows, whole, whole],
+        in_specs=[rows, whole(GROUP, HEAD_DIM), whole(GROUP, HEAD_DIM), whole(16, HEAD_DIM, TOK), cols(HEAD_DIM), cols(1), cols(1)],
+        out_specs=[rows, whole(GROUP, HEAD_DIM), whole(GROUP, HEAD_DIM)],
         out_shape=[out, out, out],
-        scratch_shapes=[pltpu.VMEM((HEAD_DIM, GROUP), bf16)],
-        compiler_params=pltpu.CompilerParams(vmem_limit_bytes=48 << 20),
+        scratch_shapes=[pltpu.VMEM((HEAD_DIM, GROUP), bf16), pltpu.VMEM((HEAD_DIM, GROUP), bf16)],
+        compiler_params=pltpu.CompilerParams(vmem_limit_bytes=VMEM_LIMIT),
         cost_estimate=pl.CostEstimate(
             flops=5 * 27 * BLOCK * BLOCK * 512, bytes_accessed=8 << 20, transcendentals=27 * BLOCK * BLOCK
         ),
@@ -374,10 +378,10 @@
 
 
 def experts_kernel(
-    own_ref, ffn_mine, ffn_other, g_mine, g_other, router_ref, chosen_ref, slots_ref, slot_cols_ref, *refs
+    own_ref, ffn_mine, ffn_other, g_mine, g_other, routes_mine, routes_other, router_ref, *refs
 ):
     shards = refs[:N_SHARDS]
-    routed_mine, routed_other, gate_grad_ref, moved_mine, moved_other = refs[-11:-6]
+    routed_mine, routed_other, moved_mine, moved_other = refs[-10:-6]
     x_ref, dh_ref, act_ref, dy_ref, w_ref, sem = refs[-6:]
     own = own_ref[0]
 
@@ -395,15 +399,30 @@
             copy.wait()
 
     expert_rows = lax.broadcasted_iota(i32, (EXPERTS, TOK), 0)
-    slot_rows = lax.broadcasted_iota(i32, (SLOTS, TOK), 0)
+    slot_rows = lax.broadcasted_iota(i32, (SLOTS, TOK), 0).astype(f32)
+    upto = (
+        lax.broadcasted_iota(i32, (TOK, TOK), 0) <= lax.broadcasted_iota(i32, (TOK, TOK), 1)
+    ).astype(f32).astype(bf16)
+    slot_cols = []
+    gate_grads = [jnp.zeros((EXPERTS, WIDTH), f32) for _ in range(4)]
+    payload_rows = lax.broadcasted_iota(i32, (EXPERTS, WIDTH), 0)
     gate_rows = [[], []]
     picks = [[], []]
     picked_rows = [[], []]
     picked_grads = [[], []]
-    blocks = [(ffn_mine, g_mine, 0), (ffn_other, g_other, 0), (ffn_mine, g_mine, 1), (ffn_other, g_other, 1)]
-    for b, (rows_ref, grads_ref, n) in enumerate(blocks):
+    blocks = [(ffn_mine, g_mine, routes_mine, 0), (ffn_other, g_other, routes_other, 0)]
+    blocks = blocks + [(*refs_of[:3], 1) for refs_of in blocks]
+    for rows_ref, grads_ref, routes_ref, n in blocks:
         rows, grads = rows_ref[n], grads_ref[n]
-        chosen = chosen_ref[b] > 0
+        routes = routes_ref[n][:8, :TOK].astype(f32).astype(i32)
+        chosen = expert_rows == routes[0:1]
+        for j in range(1, 8):
+            chosen = chosen | (expert_rows == routes[j : j + 1])
+        named = [jnp.max((routes == own + e).astype(f32), axis=0, keepdims=True) for e in range(2)]
+        named = jnp.concatenate(named + [jnp.zeros((6, TOK), f32)], axis=0)
+        rank = jnp.dot(named.astype(bf16), upto, preferred_element_type=f32)
+        slots = jnp.where(named > 0, rank - 1.0, -1.0)
+        slot_cols.append(slots.T)
         logits = lax.dot_general(router_ref[...], rows, NT, preferred_element_type=f32)
         peak = jnp.max(jnp.where(chosen, logits, masked_score), axis=0, keepdims=True)
         raised = jnp.where(chosen, jnp.exp(jnp.minimum(logits - peak, 0.0)), 0.0)
@@ -412,7 +431,7 @@
             gate_rows[e].append(
                 jnp.sum(jnp.where(expert_rows == own + e, gates, 0.0), axis=0, keepdims=True)
             )
-            pick = (slots_ref[b, e : e + 1, :] == slot_rows).astype(f32)
+            pick = (slots[e : e + 1] == slot_rows).astype(f32)
             picks[e].append(pick)
             low = pick.astype(bf16)
             picked_rows[e].append(jnp.dot(low, rows, preferred_element_type=f32))
@@ -443,29 +462,35 @@
         returned = jnp.dot(act, w_down, preferred_element_type=f32).astype(bf16).astype(f32)
         dgate = jnp.sum(returned * grads, axis=1, keepdims=True)
         for b in range(4):
-            gate_grad_ref[b, e : e + 1, :] = jnp.sum(
+            grad = jnp.sum(
                 picks[e][b] * dgate[b * SLOTS : (b + 1) * SLOTS], axis=0, keepdims=True
             )
+            high = grad.astype(bf16).astype(f32)
+            gap = jnp.zeros((1, 256 - TOK), f32)
+            wide = jnp.concatenate([high, gap, grad - high, gap, jnp.zeros((1, WIDTH - 512), f32)], axis=1)
+            gate_grads[b] = gate_grads[b] + jnp.where(payload_rows == own + e, wide, 0.0)
         moved.append(gate * returned)
         routed.append(lax.dot_general(dh, w_gate_up, NT, preferred_element_type=f32))
-    columns = lax.broadcasted_iota(i32, (TOK, 2 * SLOTS), 1)
+    columns = lax.broadcasted_iota(i32, (TOK, 2 * SLOTS), 1).astype(f32)
     outs = [(routed_mine, moved_mine, 0), (routed_other, moved_other, 0), (routed_mine, moved_mine, 1), (routed_other, moved_other, 1)]
     for b, (routed_ref, moved_ref, n) in enumerate(outs):
-        first, second = slot_cols_ref[b, :, 0:1], slot_cols_ref[b, :, 1:2]
+        first, second = slot_cols[b][:, 0:1], slot_cols[b][:, 1:2]
         back = ((columns == first) | ((columns == second + SLOTS) & (second >= 0))).astype(f32).astype(bf16)
         at = slice(b * SLOTS, (b + 1) * SLOTS)
         for terms, ref in ((routed, routed_ref), (moved, moved_ref)):
             joined = jnp.concatenate([terms[0][at], terms[1][at]], axis=0).astype(bf16)
-            ref[n] = jnp.dot(back, joined, preferred_element_type=f32).astype(bf16)
-
-
-def run_experts(half, own, ffn, grads, weights, router, chosen, slots, slot_cols, before):
+            ref[n, :TOK, :] = jnp.dot(back, joined, preferred_element_type=f32).astype(bf16)
+        routed_ref[n, TOK:, :] = gate_grads[b].astype(bf16)
+
+
+def run_experts(half, own, ffn, grads, weights, router, before):
     pair = pl.BlockSpec((2, TOK, WIDTH), lambda i, o: (i, 0, 0))
     pair_of_all = pl.BlockSpec((2, TOK, WIDTH), lambda i, o: (i + 2 * half, 0, 0))
     whole = lambda shape: pl.BlockSpec(shape, lambda i, o: (0,) * len(shape))
-    four = lambda *shape: pl.BlockSpec((4, *shape), lambda i, o: (i + 2 * half, 0, 0))
+    routes = pl.BlockSpec((2, 16, 256), lambda i, o: (i, TOK // 16, 0))
+    summed = pl.BlockSpec((2, PAY, WIDTH), lambda i, o: (i, 0, 0))
     kept = lambda n: pl.BlockSpec((2, STEP_ROWS, n), lambda i, o: (0, i + 2 * half, 0))
-    part = jax.ShapeDtypeStruct((4, TOK, WIDTH), bf16)
+    part = jax.ShapeDtypeStruct((4, PAY, WIDTH), bf16)
     keep = lambda n: jax.ShapeDtypeStruct((2, ALL_ROWS, n), bf16)
     return pl.pallas_call(
         experts_kernel,
@@ -477,16 +502,14 @@
                 pair,
                 pair,
                 pair,
+                routes,
+                routes,
                 whole((EXPERTS, WIDTH)),
-                four(EXPERTS, TOK),
-                four(2, TOK),
-                four(TOK, 2),
             ]
             + [pl.BlockSpec(memory_space=pl.ANY)] * (N_SHARDS + len(before)),
             out_specs=[
-                pair,
-                pair,
-                pl.BlockSpec((4, 2, TOK), lambda i, o: (i, 0, 0)),
+                summed,
+                summed,
                 pair_of_all,
                 pair_of_all,
                 kept(WIDTH),
@@ -502,7 +525,6 @@
         out_shape=[
             part,
             part,
-            jax.ShapeDtypeStruct((8, 2, TOK), f32),
             jax.ShapeDtypeStruct((8, TOK, WIDTH), bf16),
             jax.ShapeDtypeStruct((8, TOK, WIDTH), bf16),
             keep(WIDTH),
@@ -510,12 +532,12 @@
             keep(FF),
             keep(WIDTH),
         ],
-        input_output_aliases={9 + N_SHARDS + i: 3 + i for i in range(len(before))},
-        compiler_params=pltpu.CompilerParams(vmem_limit_bytes=60 << 20),
+        input_output_aliases={8 + N_SHARDS + i: 2 + i for i in range(len(before))},
+        compiler_params=pltpu.CompilerParams(vmem_limit_bytes=VMEM_LIMIT),
         cost_estimate=pl.CostEstimate(
             flops=14 << 30, bytes_accessed=24 << 20, transcendentals=8 * SLOTS * 2 * FF
         ),
-    )(own, *ffn, *grads, router, chosen, slots, slot_cols, *weights, *before)
+    )(own, *ffn, *grads, *grads, router, *weights, *before)
 
 
 def expert_grads_kernel(order, x_ref, dh_ref, act_ref, dy_ref, out_ref):
@@ -541,15 +563,16 @@
             out_specs=pl.BlockSpec((1, 2, 1, 192, 1024), lambda e, i, o: (o[i], 0, e, 0, 0)),
         ),
         out_shape=jax.ShapeDtypeStruct((4, 2, 2, 192, 1024), bf16),
-        compiler_params=pltpu.CompilerParams(vmem_limit_bytes=48 << 20),
+        compiler_params=pltpu.CompilerParams(vmem_limit_bytes=VMEM_LIMIT),
         cost_estimate=pl.CostEstimate(flops=8 << 30, bytes_accessed=14 << 20, transcendentals=0),
     )(order, x, dh, act, dy)
 
 
-def hidden_kernel(att_ref, w_ref, rows_ref, gain_ref, hidden_ref, normed_ref, att_rows_ref):
-    att = jnp.concatenate([att_ref[h] for h in range(HEADS)], axis=1)
-    att_rows_ref[...] = att
-    hidden = rows_ref[...].astype(f32) + jnp.dot(att, w_ref[:, :WIDTH], preferred_element_type=f32)
+def hidden_kernel(att_ref, w_ref, rows_ref, gain_ref, hidden_ref, normed_ref):
+    att = att_ref[...].reshape(WIDTH, TOK)
+    hidden = rows_ref[...].astype(f32) + lax.dot_general(
+        att, w_ref[:, :WIDTH], TN, preferred_element_type=f32
+    )
     hidden_ref[...] = hidden
     normed_ref[...] = (hidden * inverse_rms(hidden) * gain_ref[...]).astype(bf16)
 
@@ -560,9 +583,8 @@
         out_shape=[
             jax.ShapeDtypeStruct((TOK, WIDTH), f32),
             jax.ShapeDtypeStruct((TOK, WIDTH), bf16),
-            jax.ShapeDtypeStruct((TOK, WIDTH), bf16),
         ],
-        compiler_params=pltpu.CompilerParams(vmem_limit_bytes=32 << 20),
+        compiler_params=pltpu.CompilerParams(vmem_limit_bytes=VMEM_LIMIT),
         cost_estimate=pl.CostEstimate(
             flops=2 * TOK * WIDTH * WIDTH, bytes_accessed=5 << 20, transcendentals=0
         ),
@@ -570,7 +592,7 @@
 
 
 def hidden_back_kernel(
-    t0, t1, t2, t3, crossed, hidden_ref, normed_ref, gate_grad_ref, chosen_ref, router_ref, g_ref, gain_ref,
+    t0, t1, t2, t3, crossed, hidden_ref, normed_ref, chosen_ref, router_ref, g_ref, gain_ref,
     w_ref, hidden_grad_ref, branch_ref, logit_ref, scaled_ref, att_ref
 ):
     chosen = chosen_ref[...] > 0
@@ -578,13 +600,16 @@
     peak = jnp.max(jnp.where(chosen, logits, masked_score), axis=0, keepdims=True)
     raised = jnp.where(chosen, jnp.exp(jnp.minimum(logits - peak, 0.0)), 0.0)
     gates = raised / jnp.sum(raised, axis=0, keepdims=True)
-    gate_grad = gate_grad_ref[...]
+    summed = t0[...].astype(f32)
+    for term in (t1, t2, t3, crossed):
+        summed = summed + term[...].astype(f32)
+    gate_grad = summed[TOK:, :TOK] + summed[TOK:, 256 : 256 + TOK]
     logit_grad = gates * (gate_grad - jnp.sum(gates * gate_grad, axis=0, keepdims=True))
     logit_grad = logit_grad.astype(bf16)
     logit_ref[...] = logit_grad
-    normed_grad = lax.dot_general(logit_grad, router_ref[...], TN, preferred_element_type=f32)
-    for term in (t0, t1, t2, t3, crossed):
-        normed_grad = normed_grad + term[...].astype(f32)
+    normed_grad = summed[:TOK] + lax.dot_general(
+        logit_grad, router_ref[...], TN, preferred_element_type=f32
+    )
     hidden = hidden_ref[...]
     scale = inverse_rms(hidden)
     scaled_ref[...] = (normed_grad * hidden * scale).astype(bf16)
@@ -592,12 +617,11 @@
     hidden_grad_ref[...] = hidden_grad
     branch = hidden_grad.astype(bf16)
     branch_ref[...] = branch
-    att = lax.dot_general(branch, w_ref[:, :WIDTH], NT, preferred_element_type=f32).astype(bf16)
-    for h in range(HEADS):
-        att_ref[h] = att[:, h * HEAD_DIM : (h + 1) * HEAD_DIM]
-
-
-def hidden_back(terms, crossed, hidden, normed, gate_grad, chosen, router_t, g, gain, shared):
+    att = lax.dot_general(w_ref[:, :WIDTH], branch, NT, preferred_element_type=f32)
+    att_ref[...] = att.astype(bf16).reshape(HEADS, HEAD_DIM, TOK)
+
+
+def hidden_back(terms, crossed, hidden, normed, chosen, router_t, g, gain, shared):
     wide = lambda t: jax.ShapeDtypeStruct((TOK, WIDTH), t)
     return pl.pallas_call(
         hidden_back_kernel,
@@ -606,19 +630,18 @@
             wide(bf16),
             jax.ShapeDtypeStruct((EXPERTS, TOK), bf16),
             wide(bf16),
-            jax.ShapeDtypeStruct((HEADS, TOK, HEAD_DIM), bf16),
+            jax.ShapeDtypeStruct((HEADS, HEAD_DIM, TOK), bf16),
         ],
-        compiler_params=pltpu.CompilerParams(vmem_limit_bytes=32 << 20),
+        compiler_params=pltpu.CompilerParams(vmem_limit_bytes=VMEM_LIMIT),
         cost_estimate=pl.CostEstimate(
             flops=2 * TOK * WIDTH * WIDTH, bytes_accessed=8 << 20, transcendentals=0
         ),
-    )(*terms, crossed, hidden, normed, gate_grad, chosen, router_t, g, gain, shared)
+    )(*terms, crossed, hidden, normed, chosen, router_t, g, gain, shared)
 
 
 def shared_grads_kernel(att_ref, branch_ref, normed_ref, logit_ref, scaled_ref, out_ref):
-    out_ref[:, :WIDTH] = lax.dot_general(
-        att_ref[...], branch_ref[...], TN, preferred_element_type=f32
-    ).astype(bf16)
+    att = att_ref[...].reshape(WIDTH, TOK)
+    out_ref[:, :WIDTH] = jnp.dot(att, branch_ref[...], preferred_element_type=f32).astype(bf16)
     over_tokens = (((0,), (1,)), ((), ()))
     logit = jnp.concatenate([logit_ref[...], jnp.zeros((96, TOK), bf16)], axis=0)
     ones = (lax.broadcasted_iota(i32, (128, TOK), 0) == EXPERTS).astype(f32).astype(bf16)
@@ -632,7 +655,7 @@
     return pl.pallas_call(
         shared_grads_kernel,
         out_shape=jax.ShapeDtypeStruct((WIDTH, 1152), bf16),
-        compiler_params=pltpu.CompilerParams(vmem_limit_bytes=32 << 20),
+        compiler_params=pltpu.CompilerParams(vmem_limit_bytes=VMEM_LIMIT),
         cost_estimate=pl.CostEstimate(
             flops=2 * TOK * WIDTH * 1280, bytes_accessed=5 << 20, transcendentals=0
         ),
@@ -679,9 +702,10 @@
     head_weights = jnp.where(jnp.arange(256)[None] < 192, head_weights, 0.0).astype(bf16)
 
     rows_near, rows_across = gather_near(rows)
-    rows_near, cosine, sine, head_weights = tie(rows_near, cosine, sine, head_weights)
-    rows_near = both_cores(rows_near)
-    rows_far = [rows_across] + [send(rows_across, 0, b) for b in (1, 3, 2)]
+    rows_near, _, cosine, sine, head_weights = tie(
+        rows_near, rows_across, cosine, sine, head_weights
+    )
+    rows_near, rows_far = both_cores(rows_near), gather_far(rows_across)
 
     w_index = lax.axis_index("wshard")
     own_y, own_x = w_index // 2, w_index % 2
@@ -698,17 +722,8 @@
     shared = lax.all_to_all(
         jnp.broadcast_to(shared[None], (8, 8, 1152)), "wshard", 0, 0, tiled=True
     ).reshape(64, 1152)
-    rows_far, normed_near, pair_before, pair_after, shared = tie(
-        rows_far, normed_near, pair_before, pair_after, shared
-    )
+    rows_far, normed_near, shared = tie(rows_far, normed_near, shared)
     rows_far = both_cores(rows_far)
-    experts = (
-        expert_pair,
-        pair_before,
-        pair_after,
-        send_w(pair_before[0], 0, 1),
-        send_w(pair_after[1], 0, -1),
-    )
     normed_far, q, k, v = project(places[8:], rows_far, head_weights, gain_attn, cosine, sine, qkv)
 
     shared = lax.all_to_all(
@@ -720,60 +735,51 @@
     upstream_rows, _ = tie(jnp.concatenate([cotangent[0], routes_rows], axis=0), normed_far)
     grad_near, grad_across = gather_near(upstream_rows)
     attended_head, attended_t, lse = attend(q, k, v, begin)
-    attended_head, experts, shared, grad_near, grad_across = tie(
-        attended_head, experts, shared, grad_near, grad_across
+    attended_head, shared, grad_near, grad_across, pair_before, pair_after = tie(
+        attended_head, shared, grad_near, grad_across, pair_before, pair_after
     )
     grad_near, grad_far = both_cores(grad_near), gather_far(grad_across)
-    in_order = lambda halves: jnp.concatenate(
-        [jnp.stack(pair, axis=1).reshape(8, *pair[0].shape[1:]) for pair in halves], axis=0
-    )
-    routes_all = in_order(
-        [tuple(t[:, TOK : TOK + 8, :TOK] for t in half) for half in (grad_near, grad_far)]
-    ).astype(i32)
-
-    expert_range = jnp.arange(EXPERTS, dtype=i32)
-    chosen = jnp.any(routes_all[:, None] == expert_range[None, :, None, None], axis=2)
-    own_first = seq_index * 2
-    chosen_own = jnp.any(
-        routes_all[:, None] == (own_first + jnp.arange(2, dtype=i32))[None, :, None, None], axis=2
-    )
-    upto = (jnp.arange(TOK)[:, None] <= jnp.arange(TOK)[None, :]).astype(bf16)
-    rank = jnp.einsum("bet,tu->beu", chosen_own.astype(bf16), upto, preferred_element_type=f32)
-    slots = jnp.where(chosen_own, rank.astype(i32) - 1, -1)
-    slot_cols = slots.transpose(0, 2, 1)
-    chosen = chosen.astype(f32)
-
-    attended = lax.all_to_all(attended_head.reshape(16, TOK, HEAD_DIM), "seq", 0, 0, tiled=True)
-    hidden, normed_ffn, attended = hidden_of(attended, shared, rows, gain_ffn)
-    normed_ffn, grad_near = tie(normed_ffn, grad_near)
-
-    ffn_near, ffn_far = seq_gather(normed_ffn)
-    own = jnp.stack([own_first] + w_places)
-    near = run_experts(
-        0, own, ffn_near, grad_near, experts, router_t, chosen, slots, slot_cols, ()
-    )
-    near, saved = near[:3], near[3:]
-    near_terms = sum_along_z(near[0], near[1])
-    far = run_experts(
-        1, own, ffn_far, grad_far, experts, router_t, chosen, slots, slot_cols, saved
-    )
-    far, saved = far[:3], far[3:]
-    moved, saved = saved[:2], saved[2:]
+    experts = (
+        expert_pair,
+        pair_before,
+        pair_after,
+        send_w(pair_before[0], 0, 1),
+        send_w(pair_after[1], 0, -1),
+    )
+    attended = lax.all_to_all(attended_head, "seq", 0, 0, tiled=True)
+    hidden, normed_ffn = hidden_of(attended, shared, rows, gain_ffn)
+    normed_ffn, grad_far, experts = tie(normed_ffn, grad_far, experts)
+    grad_far = both_cores(grad_far)
+
+    ffn_near, ffn_across = gather_near(normed_ffn)
+    ffn_near, _ = tie(ffn_near, ffn_across)
+    ffn_near, ffn_far = both_cores(ffn_near), gather_far(ffn_across)
+    own = jnp.stack([seq_index * 2] + w_places)
+    near = run_experts(0, own, ffn_near, grad_near, experts, router_t, ())
+    near_terms = sum_along_z(*near[:2])
+    ffn_far = both_cores(ffn_far)
+    far = run_experts(1, own, ffn_far, grad_far, experts, router_t, near[2:])
     far, near_terms = tie(far, near_terms)
-    far_terms = sum_along_z(far[0], far[1])
-    token_gate_grad = jnp.take(jnp.concatenate([near[2], far[2]], axis=0), blocks, axis=0)
-    gate_grad = lax.all_to_all(token_gate_grad, "seq", 0, 0, tiled=True).reshape(EXPERTS, TOK)
+    moved, saved = far[2:4], far[4:]
+    far_terms = sum_along_z(*far[:2])
     along = jnp.arange(4, dtype=i32)
     expert_grads = expert_weight_grads((own_y - along) % 4, *saved)
-    far_terms, expert_grads = tie(far_terms, expert_grads)
+    moved_other = swap_cores(moved[1])
+    far_terms, expert_grads, moved_other = tie(far_terms, expert_grads, moved_other)
     crossed = send(add_low(*far_terms), 1, 0)
-    crossed, gate_grad, expert_grads, moved = tie(crossed, gate_grad, expert_grads, moved)
-
+    by_x = [t.reshape(2, 4, TOK, WIDTH) for t in (moved[0], moved_other)]
+    moved_parts = [add_low(by_x[0][:, i], by_x[1][:, i]) for i in range(4)]
+    moved_terms = [moved_parts[0]] + [
+        send(moved_parts[i], 0, -b) for i, b in ((1, 1), (2, 3), (3, 2))
+    ]
+
+    expert_range = jnp.arange(EXPERTS, dtype=i32)
     chosen_here = jnp.any(routes[0].T[None] == expert_range[:, None, None], axis=1).astype(f32)
     hidden_grad, branch_grad, logit_grad, scaled_grad, attended_grad = hidden_back(
-        near_terms, crossed, hidden, normed_ffn, gate_grad, chosen_here, router_t, cotangent[0], gain_ffn, shared
-    )
-    head_grad = lax.all_to_all(attended_grad, "seq", 0, 0, tiled=True).reshape(GROUP, HEAD_DIM)
+        near_terms, crossed, hidden, normed_ffn, chosen_here, router_t, cotangent[0], gain_ffn, shared
+    )
+    branch_grad, expert_grads = tie(branch_grad, expert_grads)
+    head_grad = lax.all_to_all(attended_grad, "seq", 0, 0, tiled=True)
     shared_grads = shared_weight_grads(attended, branch_grad, normed_ffn, logit_grad, scaled_grad)
 
     far_down, far_up = send_w(expert_grads[2, 0], 0, -1), send_w(expert_grads[2, 1], 0, 1)
@@ -781,31 +787,28 @@
     above = jnp.stack([expert_grads[3, 0], add_low(expert_grads[3, 1], far_up)])
     head_grad, shared_grads, below, above = tie(head_grad, shared_grads, below, above)
     expert_terms = (expert_grads[0], send_w(below, 0, -1), send_w(above, 0, 1))
-
-    by_x = [t.reshape(2, 4, TOK, WIDTH).transpose(1, 0, 2, 3) for t in (moved[0], swap_cores(moved[1]))]
-    moved_parts = [add_low(by_x[0][i], by_x[1][i]) for i in range(4)]
-    moved_terms = [moved_parts[0]] + [
-        send(moved_parts[i], 0, -b) for i, b in ((1, 1), (2, 3), (3, 2))
-    ]
-    shared_grads = lax.all_to_all(shared_grads.reshape(128, 8, 1152), BOTH, 0, 0, tiled=True)
+    shared_grads = lax.all_to_all(
+        shared_grads.reshape(16, 8, 8, 1152), "wshard", 1, 1, tiled=True
+    )
     grads = attend_back(q, k, v, head_grad, attended_t, lse, begin)
-    grads, moved_terms = tie(grads, moved_terms)
+    grads, moved_terms, expert_terms = tie(grads, moved_terms, expert_terms)
     moved_crossed = send(add_low(*[t[1] for t in moved_terms]), 1, 0)
     *far_part, grad_head = project_back(
         places[8:], normed_far, grads, head_weights, cosine, sine, ()
     )
-    far_part, expert_terms = tie(far_part, expert_terms)
     far_terms = sum_along_z(*far_part)
     *near_part, grad_head = project_back(
         places[:8], normed_near, grads, head_weights, cosine, sine, (grad_head,)
     )
-    near_part, shared_grads, moved_crossed = tie(near_part, shared_grads, moved_crossed)
+    near_part, moved_crossed, shared_grads = tie(near_part, moved_crossed, shared_grads)
     near_terms = sum_along_z(*near_part)
+    shared_grads = jnp.sum(shared_grads.astype(f32), axis=1).astype(bf16)
+    shared_grads = lax.all_to_all(shared_grads, "seq", 0, 0, tiled=True)
     grad_heads = lax.all_to_all(
         grad_head.astype(bf16).reshape(128, 8, 256), BOTH, 0, 0, tiled=True
     )
-    grad_heads, far_terms = tie(grad_heads, far_terms)
     crossed = send(add_low(*far_terms), 1, 0)
+    crossed, grad_heads = tie(crossed, grad_heads)
     expert_grads = add_low(*expert_terms)
     kept = lax.dynamic_index_in_dim(expert_grads, own_x, 0, keepdims=False)
     sent = lax.dynamic_index_in_dim(expert_grads, 1 - own_x, 0, keepdims=False)

time: 611 us -> 575 us (0.941)
  local copies, waits for them, and re-layouts: 93.2 us -> 34.6 us
  Pallas kernels: 147 us -> 169 us
  waiting for transfers between devices: 147 us -> 169 us
  starting transfers between devices: 131 us -> 119 us
  blocking collectives: 11.8 us -> 0 us
    ppermute x39, waiting for transfers between devices: 119 us -> 73.1 us  [send(): return lax.ppermute(rows, 'seq', shift_perm(a, b))]
    all_to_all x3 -> x4, waiting for transfers between devices: 13.5 us -> 52.7 us  [the longest x1 28.2 us: local(): head_grad = lax.all_to_all(attended_grad, 'seq', 0, 0, tiled=True)]
    unnamed x181 -> x87, local copies, waits for them, and re-layouts: 42.9 us -> 7.96 us
    ppermute x10, waiting for transfers between devices: 7.33 us -> 27.5 us  [send_w(): return lax.ppermute(rows, 'wshard', pairs)]
    all_to_all x1 -> x0, blocking collectives: 11.8 us -> none  [local(): lax.all_to_all(token_gate_grad, 'seq', 0, 0, tiled=True)]
    pallas_call x2, Pallas kernels: 13.4 us -> 23.8 us  [project_back(): pl.pallas_call(project_back_kernel, grid_spec=pltpu.PrefetchScalarGridSpe...]
    ppermute x39, starting transfers between devices: 72.7 us -> 63 us  [send(): return lax.ppermute(rows, 'seq', shift_perm(a, b))]
    reshape x4 -> x1, local copies, waits for them, and re-layouts: 9.23 us -> 1.69 us  [local(): shared_grads.reshape(16, 8, 8, 1152)]
  transfers between devices with their start and end apart: 67 -> 68, of which waited for: 21 -> 22; matrix products, arithmetic and copies ran while one was open for 18% -> 15% of each run, Pallas kernels for 24% -> 29%
where the time goes in v5:
time: 575 us; the launch traced here: 564 us
  waiting for transfers between devices  169 us (29%)
  Pallas kernels  169 us (29%)
  starting transfers between devices  119 us (21%)
  other arithmetic  70.7 us (12%)
  local copies, waits for them, and re-layouts  34.6 us (6%)
    ppermute x39, waiting for transfers between devices, send(): return lax.ppermute(rows, 'seq', shift_perm(a, b))  73.1 us
    ppermute x39, starting transfers between devices, send(): return lax.ppermute(rows, 'seq', shift_perm(a, b))  63 us
    pallas_call x2, Pallas kernels, run_experts(): pl.pallas_call(experts_kernel, grid_spec=pltpu.PrefetchScalarGridSpec(num...  48.6 us
    all_to_all x1, waiting for transfers between devices, local(): head_grad = lax.all_to_all(attended_grad, 'seq', 0, 0, tiled=True)  28.2 us
    ppermute x10, waiting for transfers between devices, send_w(): return lax.ppermute(rows, 'wshard', pairs)  27.5 us
    pallas_call x1, Pallas kernels, attend_back(): pl.pallas_call(attend_back_kernel, grid=(GROUP // BLOCK,), in_specs=[rows...  27 us
    convert_element_type x8, other arithmetic, add_low(): return sum([t.astype(f32) for t in terms]).astype(bf16)  25.7 us
    pallas_call x2, Pallas kernels, project_back(): pl.pallas_call(project_back_kernel, grid_spec=pltpu.PrefetchScalarGridSpe...  23.8 us
  transfers between devices with their start and end apart: 68, of which 22 were waited for; matrix products, arithmetic and copies ran while one was open for 15% of the time, Pallas kernels for 29%

profile of v5, /device:TPU:0, one launch (start us, length us, event | category | flops | bytes accessed | tf_op | source)
XLA Modules:
  0.0 563.8 jit_solution(11089826826602626283)
XLA Ops:
  13.2 6.8 %all-to-all-start = ((bf16[128,8,256]{2,1,0:T(8,128)(2,1)}), bf16[128,8,256]{2,1,0:T(8,128)(2,1)S(1)}, u32[]{:S(2)}, u32[]{:S(2)}) async-start(bf16[128,8,256]{2,1,0:T(8,128)(2,1)} %bitcast.8), calls=%async_computation | async-start | bytes 1048576 | tf_op jit(solution)/shard_map/all_to_all | solution.py:700
  20.5 6.4 %multiply_sine_fusion = (f32[3584,32]{1,0:T(8,128)S(1)}, f32[3584,32]{1,0:T(8,128)S(1)}) fusion(f32[32]{0:T(128)S(1)} %multiply_power_fusion, f32[3584]{0:T(1024)S(1)} %get-tuple-element.285), kind=kLoop, calls=%fused_computation.1 | loop fusion | flops 114688 | bytes 931968 | tf_op jit(solution)/shard_map/sin | solution.py:129
  29.8 5.2 all-to-all-done
  46.5 5.3 all-to-all-start.1
  52.7 10.1 %shard_map.178 = (bf16[8,224,1024]{2,1,0:T(8,128)(2,1)}, bf16[3584,64]{1,0:T(8,128)(2,1)}, bf16[3584,64]{1,0:T(8,128)(2,1)}, bf16[3584,64]{1,0:T(8,128)(2,1)}) custom-call(s32[8]{0:T(128)} %get-tuple-element.288.places, bf16[4,224,1024]{2,1,0:T(8,128)(2,1)} %copy-done.4, bf16[4,224,1024]{2,1,0:T(8,128)(2,1)} %collective-permute-done.7.other, ...), custom_call_target="tpu_custom_call" | custom-call | flops 939524096 | bytes 10485760 | tf_op jit(solution)/shard_map/pallas_call | solution.py:166
  73.4 6.2 %all-to-all-start.2 = ((bf16[16,64,1152]{2,1,0:T(8,128)(2,1)}), bf16[16,64,1152]{2,1,0:T(8,128)(2,1)S(1)}, u32[]{:S(2)}, u32[]{:S(2)}) async-start(bf16[16,64,1152]{2,1,0:T(8,128)(2,1)} %broadcast_in_dim.97), calls=%async_computation.2 | async-start | bytes 4718592 | tf_op jit(solution)/shard_map/all_to_all | solution.py:729
  82.0 10.1 %shard_map.179 = (bf16[8,224,1024]{2,1,0:T(8,128)(2,1)}, bf16[3584,64]{1,0:T(8,128)(2,1)}, bf16[3584,64]{1,0:T(8,128)(2,1)}, bf16[3584,64]{1,0:T(8,128)(2,1)}) custom-call(s32[8]{0:T(128)} %get-tuple-element.289.places, bf16[4,224,1024]{2,1,0:T(8,128)(2,1)} %pad_maximum_fusion.5.mine, ...), custom_call_target="tpu_custom_call", output_to_operand_aliasing={{1}: (7, {}), {2}: (8, {}), {3}: (9, {})} | custom-call | flops 939524096 | bytes 10485760 | tf_op jit(solution)/shard_map/pallas_call | solution.py:166
  99.1 9.5 %collective-permute-done.14.refs_1_ = bf16[2,2,192,1024]{3,2,1,0:T(8,128)(2,1)} collective-permute-done((bf16[2,2,192,1024]{3,2,1,0:T(8,128)(2,1)}, bf16[2,2,192,1024]{3,2,1,0:T(8,128)(2,1)}, u32[]{:S(2)}, u32[]{:S(2)}) %collective-permute-start.14) | collective-permute-done | bytes 1572896 | tf_op jit(solution)/shard_map/ppermute | solution.py:94
  109.9 19.4 %shard_map.180 = (bf16[16,64,224]{2,1,0:T(8,128)(2,1)}, f32[64,3584]{1,0:T(8,128)}, f32[1,3584]{1,0:T(1,128)}) custom-call(bf16[3584,64]{1,0:T(8,128)(2,1)} %get-tuple-element.146.q_ref, bf16[3584,64]{1,0:T(8,128)(2,1)} %get-tuple-element.147.k_ref, bf16[3584,64]{1,0:T(8,128)(2,1)} %get-tuple-element.148.v_ref, s32[1,3584]{1,0:T(1,128)} %compare_select_fusion.begin_ref), custom_call_target="tpu_custom_call" | custom-call | flops 7247757312 | bytes 4194304 | tf_op jit(solution)/shard_map/pallas_call | solution.py:300
  143.8 5.7 %all-to-all-start.3 = ((bf16[16,64,224]{2,1,0:T(8,128)(2,1)}), bf16[16,64,224]{2,1,0:T(8,128)(2,1)S(1)}, u32[]{:S(2)}, u32[]{:S(2)}) async-start(bf16[16,64,224]{2,1,0:T(8,128)(2,1)} %get-tuple-element.153), calls=%async_computation.3 | async-start | bytes 1048576 | tf_op jit(solution)/shard_map/all_to_all | solution.py:749
  150.3 19.0 %all-to-all-done.3.att_ref = bf16[16,64,224]{2,1,0:T(8,128)(2,1)S(1)} async-done(((bf16[16,64,224]{2,1,0:T(8,128)(2,1)}), bf16[16,64,224]{2,1,0:T(8,128)(2,1)S(1)}, u32[]{:S(2)}, u32[]{:S(2)}) %all-to-all-start.3) | async-done | bytes 458784 | tf_op jit(solution)/shard_map/all_to_all | solution.py:749
  182.9 5.7 %collective-permute-done.21 = bf16[224,1024]{1,0:T(8,128)(2,1)S(1)} collective-permute-done((bf16[224,1024]{1,0:T(8,128)(2,1)}, bf16[224,1024]{1,0:T(8,128)(2,1)S(1)}, u32[]{:S(2)}, u32[]{:S(2)}) %collective-permute-start.21) | collective-permute-done | bytes 458784 | tf_op jit(solution)/shard_map/ppermute | solution.py:52
  191.9 8.6 %collective-permute-done.28 = bf16[224,1024]{1,0:T(8,128)(2,1)S(1)} collective-permute-done((bf16[224,1024]{1,0:T(8,128)(2,1)}, bf16[224,1024]{1,0:T(8,128)(2,1)S(1)}, u32[]{:S(2)}, u32[]{:S(2)}) %collective-permute-start.28) | collective-permute-done | bytes 458784 | tf_op jit(solution)/shard_map/ppermute | solution.py:52
  209.4 24.3 %shard_map.182 = (bf16[4,256,1024]{2,1,0:T(8,128)(2,1)}, bf16[4,256,1024]{2,1,0:T(8,128)(2,1)}, bf16[8,224,1024]{2,1,0:T(8,128)(2,1)}, bf16[8,224,1024]{2,1,0:T(...) custom-call(s32[9]{0:T(128)} %stack.163.own_ref, ...), custom_call_target="tpu_custom_call" | custom-call | flops 15032385536 | bytes 25165824 | tf_op jit(solution)/shard_map/pallas_call | solution.py:495
  248.4 24.4 %shard_map.183 = (bf16[4,256,1024]{2,1,0:T(8,128)(2,1)}, bf16[4,256,1024]{2,1,0:T(8,128)(2,1)}, bf16[8,224,1024]{2,1,0:T(8,128)(2,1)}, bf16[8,224,1024]{2,1,0:T(...) custom-call(s32[9]{0:T(128)} %stack.163.own_ref, ...), custom_call_target="tpu_custom_call", output_to_operand_aliasing={{2}: (13, {}), {3}: (14, {}), {4}: (15, {}), {5}: (16, {}),... | custom-call | flops 15032385536 | bytes 25165824 | tf_op jit(solution)/shard_map/pallas_call | solution.py:495
  273.9 8.6 %collective-permute-done.36 = bf16[4,256,1024]{2,1,0:T(8,128)(2,1)S(1)} collective-permute-done((bf16[4,256,1024]{2,1,0:T(8,128)(2,1)}, bf16[4,256,1024]{2,1,0:T(8,128)(2,1)S(1)}, u32[]{:S(2)}, u32[]{:S(2)}) %collective-permute-start.36) | collective-permute-done | bytes 2097184 | tf_op jit(solution)/shard_map/ppermute | solution.py:56
  289.4 16.6 %shard_map.184 = bf16[4,2,2,192,1024]{4,3,2,1,0:T(8,128)(2,1)} custom-call(s32[4]{0:T(128)} %and_select_fusion.order, bf16[2,1152,1024]{2,1,0:T(8,128)(2,1)} %get-tuple-element.200.x_ref, bf16[2,1152,1024]{2,1,0:T(8,128)(2,1)} %get-tuple-element.201.dh_ref, bf16[2,1152,512]{2,1,0:T(8,128)(2,1)} %get-tuple-element.202.act_ref, ...), custom_call_target="tpu_custom_call" | custom-call | flops 8589934592 | bytes 14680064 | tf_op jit(solution)/shard_map/pallas_call | solution.py:552
  306.0 8.0 %collective-permute-done.38 = bf16[256,1024]{1,0:T(8,128)(2,1)} collective-permute-done((bf16[256,1024]{1,0:T(8,128)(2,1)}, bf16[256,1024]{1,0:T(8,128)(2,1)}, u32[]{:S(2)}, u32[]{:S(2)}) %collective-permute-start.38) | collective-permute-done | bytes 524320 | tf_op jit(solution)/shard_map/ppermute | solution.py:52
  318.9 12.5 %collective-permute-done.41.crossed = bf16[256,1024]{1,0:T(8,128)(2,1)} collective-permute-done((bf16[256,1024]{1,0:T(8,128)(2,1)S(1)}, bf16[256,1024]{1,0:T(8,128)(2,1)}, u32[]{:S(2)}, u32[]{:S(2)}) %collective-permute-start.41) | collective-permute-done | bytes 524320 | tf_op jit(solution)/shard_map/ppermute | solution.py:52
  331.4 5.8 %shard_map.185 = (f32[224,1024]{1,0:T(8,128)}, bf16[224,1024]{1,0:T(8,128)(2,1)}, bf16[32,224]{1,0:T(8,128)(2,1)}, bf16[224,1024]{1,0:T(8,128)(2,1)}, bf16[16,64,224]{2,1,0:T(8,128)(2,1)}) custom-call(bf16[256,1024]{1,0:T(8,128)(2,1)} %get-tuple-element.194.t0, bf16[256,1024]{1,0:T(8,128)(2,1)} %collective-permute-done.33.t1, ...), custom_call_target="tpu_custom_call" | custom-call | flops 469762048 | bytes 8388608 | tf_op jit(solution)/shard_map/pallas_call | solution.py:626
  342.8 5.0 fusion.12
  367.2 28.2 %all-to-all-done.4.g_ref = bf16[16,64,224]{2,1,0:T(8,128)(2,1)} async-done(((bf16[16,64,224]{2,1,0:T(8,128)(2,1)}), bf16[16,64,224]{2,1,0:T(8,128)(2,1)}, u32[]{:S(2)}, u32[]{:S(2)}) %all-to-all-start.4) | async-done | bytes 458784 | tf_op jit(solution)/shard_map/all_to_all | solution.py:782
  399.0 4.5 all-to-all-start.5
  403.5 27.0 %shard_map.187 = (f32[3584,64]{1,0:T(8,128)}, f32[3584,64]{1,0:T(8,128)}, f32[3584,64]{1,0:T(8,128)}) custom-call(bf16[3584,64]{1,0:T(8,128)(2,1)} %get-tuple-element.146.q_ref, bf16[3584,64]{1,0:T(8,128)(2,1)} %get-tuple-element.147.k_ref, bf16[3584,64]{1,0:T(8,128)(2,1)} %get-tuple-element.148.v_ref, bf16[16,64,224]{2,1,0:T(8,128)(2,1)} %all-to-all-done.4.g_ref, ...), custom_call_target="tpu_custom_call" | custom-call | flops 18119393280 | bytes 8388608 | tf_op jit(solution)/shard_map/pallas_call | solution.py:362
  430.5 15.0 %collective-permute-done.47 = bf16[2,2,192,1024]{3,2,1,0:T(8,128)(2,1)} collective-permute-done((bf16[2,2,192,1024]{3,2,1,0:T(8,128)(2,1)}, bf16[2,2,192,1024]{3,2,1,0:T(8,128)(2,1)}, u32[]{:S(2)}, u32[]{:S(2)}) %collective-permute-start.47) | collective-permute-done | bytes 1572896 | tf_op jit(solution)/shard_map/ppermute | solution.py:94
  448.5 11.7 %shard_map.188 = (bf16[4,224,1024]{2,1,0:T(8,128)(2,1)}, bf16[4,224,1024]{2,1,0:T(8,128)(2,1)}, f32[1024,256]{1,0:T(8,128)}) custom-call(s32[8]{0:T(128)} %get-tuple-element.289.places, bf16[8,224,1024]{2,1,0:T(8,128)(2,1)} %get-tuple-element.151.normed, f32[3584,64]{1,0:T(8,128)} %get-tuple-element.231.dq, f32[3584,64]{1,0:T(8,128)} %get-tuple-element.232.dk, ...), custom_call_target="tpu_custom_call" | custom-call | flops 1879048192 | bytes 12582912 | tf_op jit(solution)/shard_map/pallas_call | solution.py:216
  463.1 12.1 %shard_map.189 = (bf16[4,224,1024]{2,1,0:T(8,128)(2,1)}, bf16[4,224,1024]{2,1,0:T(8,128)(2,1)}, f32[1024,256]{1,0:T(8,128)}) custom-call(s32[8]{0:T(128)} %get-tuple-element.288.places, bf16[8,224,1024]{2,1,0:T(8,128)(2,1)} %get-tuple-element.230.normed, f32[3584,64]{1,0:T(8,128)} %get-tuple-element.231.dq, f32[3584,64]{1,0:T(8,128)} %get-tuple-element.232.dk, ...), custom_call_target="tpu_custom_call" | custom-call | flops 1879048192 | bytes 12582912 | tf_op jit(solution)/shard_map/pallas_call | solution.py:216
  500.4 5.5 all-to-all-done.7
  505.8 6.8 %all-to-all-start.6 = ((bf16[128,8,256]{2,1,0:T(8,128)(2,1)}), bf16[128,8,256]{2,1,0:T(8,128)(2,1)S(1)}, u32[]{:S(2)}, u32[]{:S(2)}) async-start(bf16[128,8,256]{2,1,0:T(8,128)(2,1)} %convert_bitcast_fusion), calls=%async_computation.6 | async-start | bytes 1048576 | tf_op jit(solution)/shard_map/all_to_all | solution.py:807
  514.6 8.0 %collective-permute-done.55 = bf16[224,1024]{1,0:T(8,128)(2,1)S(1)} collective-permute-done((bf16[224,1024]{1,0:T(8,128)(2,1)}, bf16[224,1024]{1,0:T(8,128)(2,1)S(1)}, u32[]{:S(2)}, u32[]{:S(2)}) %collective-permute-start.55) | collective-permute-done | bytes 458784 | tf_op jit(solution)/shard_map/ppermute | solution.py:52
  541.6 9.8 %collective-permute-done.51 = bf16[224,1024]{1,0:T(8,128)(2,1)} collective-permute-done((bf16[224,1024]{1,0:T(8,128)(2,1)}, bf16[224,1024]{1,0:T(8,128)(2,1)}, u32[]{:S(2)}, u32[]{:S(2)}) %collective-permute-start.51) | collective-permute-done | bytes 458784 | tf_op jit(solution)/shard_map/ppermute | solution.py:52
  551.4 9.0 %collective-permute-done.52 = bf16[224,1024]{1,0:T(8,128)(2,1)} collective-permute-done((bf16[224,1024]{1,0:T(8,128)(2,1)}, bf16[224,1024]{1,0:T(8,128)(2,1)}, u32[]{:S(2)}, u32[]{:S(2)}) %collective-permute-start.52) | collective-permute-done | bytes 458784 | tf_op jit(solution)/shard_map/ppermute | solution.py:52
  (295 shorter events, 201.6 us)
Async XLA Ops:
  0.7 35.1 %collective-permute-start = (bf16[224,1024]{1,0:T(8,128)(2,1)}, bf16[224,1024]{1,0:T(8,128)(2,1)S(1)}, u32[]{:S(2)}, u32[]{:S(2)}) collective-permute-start(bf16[224,1024]{1,0:T(8,128)(2,1)} %bitcast.206), channel_id=1, source_target_pairs={{0,64},{8,72},{16,80},{24,88},{32,96},{40,104},{48,112},{56,120},{... | collective-permute-start | bytes 1376264 | tf_op jit(solution)/shard_map/ppermute | solution.py:52
  3.8 32.0 %collective-permute-start.4 = (bf16[224,1024]{1,0:T(8,128)(2,1)}, bf16[224,1024]{1,0:T(8,128)(2,1)S(1)}, u32[]{:S(2)}, u32[]{:S(2)}) collective-permute-start(bf16[224,1024]{1,0:T(8,128)(2,1)} %bitcast.207), channel_id=1, source_target_pairs={{0,16},{8,24},{16,32},{24,40},{32,48},{40,56},{48,0},{56,8},{64,80... | collective-permute-start | bytes 1376264 | tf_op jit(solution)/shard_map/ppermute | solution.py:52
  5.8 30.0 %collective-permute-start.5 = (bf16[224,1024]{1,0:T(8,128)(2,1)}, bf16[224,1024]{1,0:T(8,128)(2,1)S(1)}, u32[]{:S(2)}, u32[]{:S(2)}) collective-permute-start(bf16[224,1024]{1,0:T(8,128)(2,1)} %bitcast.208), channel_id=1, source_target_pairs={{0,48},{8,56},{16,0},{24,8},{32,16},{40,24},{48,32},{56,40},{64,11... | collective-permute-start | bytes 1376264 | tf_op jit(solution)/shard_map/ppermute | solution.py:52
  70.1 38.4 %collective-permute-start.14 = (bf16[2,2,192,1024]{3,2,1,0:T(8,128)(2,1)}, bf16[2,2,192,1024]{3,2,1,0:T(8,128)(2,1)}, u32[]{:S(2)}, u32[]{:S(2)}) collective-permute-start(bf16[2,2,192,1024]{3,2,1,0:T(8,128)(2,1)} %pad_maximum_fusion.8.refs_0_), channel_id=1, source_target_pairs={{0,2},{1,3},{2,4},{3,5},{4,6},{5,7},{6,0},{7,1},{8,10},{9,11},{10,... | collective-permute-start | bytes 4718600 | tf_op jit(solution)/shard_map/ppermute | solution.py:94
  73.4 56.0 %all-to-all-start.2 = ((bf16[16,64,1152]{2,1,0:T(8,128)(2,1)}), bf16[16,64,1152]{2,1,0:T(8,128)(2,1)S(1)}, u32[]{:S(2)}, u32[]{:S(2)}) async-start(bf16[16,64,1152]{2,1,0:T(8,128)(2,1)} %broadcast_in_dim.97), calls=%async_computation.2 | async-start | bytes 4718592 | tf_op jit(solution)/shard_map/all_to_all | solution.py:729
  79.6 49.7 %collective-permute-start.15 = (bf16[2,2,192,1024]{3,2,1,0:T(8,128)(2,1)}, bf16[2,2,192,1024]{3,2,1,0:T(8,128)(2,1)}, u32[]{:S(2)}, u32[]{:S(2)}) collective-permute-start(bf16[2,2,192,1024]{3,2,1,0:T(8,128)(2,1)} %pad_maximum_fusion.8.refs_0_), channel_id=1, source_target_pairs={{0,6},{1,7},{2,0},{3,1},{4,2},{5,3},{6,4},{7,5},{8,14},{9,15},{10,... | collective-permute-start | bytes 4718600 | tf_op jit(solution)/shard_map/ppermute | solution.py:94
  92.1 37.3 %collective-permute-start.10 = (bf16[240,1024]{1,0:T(8,128)(2,1)S(1)}, bf16[240,1024]{1,0:T(8,128)(2,1)S(1)}, u32[]{:S(2)}, u32[]{:S(2)}) collective-permute-start(bf16[240,1024]{1,0:T(8,128)(2,1)S(1)} %fusion.32), channel_id=1, source_target_pairs={{0,48},{8,56},{16,0},{24,8},{32,16},{40,24},{48,32},{56,40},{64,11... | collective-permute-start | bytes 1474568 | tf_op jit(solution)/shard_map/ppermute | solution.py:52
  95.2 34.1 %collective-permute-start.11 = (bf16[240,1024]{1,0:T(8,128)(2,1)S(1)}, bf16[240,1024]{1,0:T(8,128)(2,1)}, u32[]{:S(2)}, u32[]{:S(2)}) collective-permute-start(bf16[240,1024]{1,0:T(8,128)(2,1)S(1)} %fusion.32), channel_id=1, source_target_pairs={{0,32},{8,40},{16,48},{24,56},{32,0},{40,8},{48,16},{56,24},{64,96... | collective-permute-start | bytes 1474568 | tf_op jit(solution)/shard_map/ppermute | solution.py:52
  96.1 33.3 %collective-permute-start.12 = (bf16[240,1024]{1,0:T(8,128)(2,1)S(1)}, bf16[240,1024]{1,0:T(8,128)(2,1)}, u32[]{:S(2)}, u32[]{:S(2)}) collective-permute-start(bf16[240,1024]{1,0:T(8,128)(2,1)S(1)} %fusion.32), channel_id=1, source_target_pairs={{0,64},{8,72},{16,80},{24,88},{32,96},{40,104},{48,112},{56,120},{... | collective-permute-start | bytes 1474568 | tf_op jit(solution)/shard_map/ppermute | solution.py:52
  132.9 40.9 %collective-permute-start.19 = (bf16[2,192,1024]{2,1,0:T(8,128)(2,1)}, bf16[2,192,1024]{2,1,0:T(8,128)(2,1)}, u32[]{:S(2)}, u32[]{:S(2)}) collective-permute-start(bf16[2,192,1024]{2,1,0:T(8,128)(2,1)} %slice_bitcast_fusion.14), channel_id=1, source_target_pairs={{0,2},{1,3},{2,4},{3,5},{4,6},{5,7},{6,0},{7,1},{8,10},{9,11},{10,... | collective-permute-start | bytes 2359304 | tf_op jit(solution)/shard_map/ppermute | solution.py:94
  136.5 37.3 %collective-permute-start.20 = (bf16[2,192,1024]{2,1,0:T(8,128)(2,1)}, bf16[2,192,1024]{2,1,0:T(8,128)(2,1)}, u32[]{:S(2)}, u32[]{:S(2)}) collective-permute-start(bf16[2,192,1024]{2,1,0:T(8,128)(2,1)} %slice_bitcast_fusion.13), channel_id=1, source_target_pairs={{0,6},{1,7},{2,0},{3,1},{4,2},{5,3},{6,4},{7,5},{8,14},{9,15},{10,... | collective-permute-start | bytes 2359304 | tf_op jit(solution)/shard_map/ppermute | solution.py:94
  138.2 35.6 %collective-permute-start.16 = (bf16[240,1024]{1,0:T(8,128)(2,1)}, bf16[240,1024]{1,0:T(8,128)(2,1)}, u32[]{:S(2)}, u32[]{:S(2)}) collective-permute-start(bf16[240,1024]{1,0:T(8,128)(2,1)} %collective-permute-done.12), channel_id=1, source_target_pairs={{0,16},{8,24},{16,32},{24,40},{32,48},{40,56},{48,0},{56,8},{64,80... | collective-permute-start | bytes 1474568 | tf_op jit(solution)/shard_map/ppermute | solution.py:52
  140.2 33.6 %collective-permute-start.17 = (bf16[240,1024]{1,0:T(8,128)(2,1)}, bf16[240,1024]{1,0:T(8,128)(2,1)}, u32[]{:S(2)}, u32[]{:S(2)}) collective-permute-start(bf16[240,1024]{1,0:T(8,128)(2,1)} %collective-permute-done.12), channel_id=1, source_target_pairs={{0,48},{8,56},{16,0},{24,8},{32,16},{40,24},{48,32},{56,40},{64,11... | collective-permute-start | bytes 1474568 | tf_op jit(solution)/shard_map/ppermute | solution.py:52
  142.3 31.5 %collective-permute-start.18 = (bf16[240,1024]{1,0:T(8,128)(2,1)}, bf16[240,1024]{1,0:T(8,128)(2,1)}, u32[]{:S(2)}, u32[]{:S(2)}) collective-permute-start(bf16[240,1024]{1,0:T(8,128)(2,1)} %collective-permute-done.12), channel_id=1, source_target_pairs={{0,32},{8,40},{16,48},{24,56},{32,0},{40,8},{48,16},{56,24},{64,96... | collective-permute-start | bytes 1474568 | tf_op jit(solution)/shard_map/ppermute | solution.py:52
  205.2 31.0 %collective-permute-start.22 = (bf16[224,1024]{1,0:T(8,128)(2,1)S(1)}, bf16[224,1024]{1,0:T(8,128)(2,1)S(1)}, u32[]{:S(2)}, u32[]{:S(2)}) collective-permute-start(bf16[224,1024]{1,0:T(8,128)(2,1)S(1)} %collective-permute-done.21), channel_id=1, source_target_pairs={{0,16},{8,24},{16,32},{24,40},{32,48},{40,56},{48,0},{56,8},{64,80... | collective-permute-start | bytes 1376264 | tf_op jit(solution)/shard_map/ppermute | solution.py:52
  206.5 29.7 %collective-permute-start.23 = (bf16[224,1024]{1,0:T(8,128)(2,1)S(1)}, bf16[224,1024]{1,0:T(8,128)(2,1)}, u32[]{:S(2)}, u32[]{:S(2)}) collective-permute-start(bf16[224,1024]{1,0:T(8,128)(2,1)S(1)} %collective-permute-done.21), channel_id=1, source_target_pairs={{0,48},{8,56},{16,0},{24,8},{32,16},{40,24},{48,32},{56,40},{64,11... | collective-permute-start | bytes 1376264 | tf_op jit(solution)/shard_map/ppermute | solution.py:52
  241.1 31.7 %collective-permute-start.33 = (bf16[256,1024]{1,0:T(8,128)(2,1)}, bf16[256,1024]{1,0:T(8,128)(2,1)}, u32[]{:S(2)}, u32[]{:S(2)}) collective-permute-start(bf16[256,1024]{1,0:T(8,128)(2,1)} %get-tuple-element.272), channel_id=1, source_target_pairs={{0,48},{8,56},{16,0},{24,8},{32,16},{40,24},{48,32},{56,40},{64,11... | collective-permute-start | bytes 1572872 | tf_op jit(solution)/shard_map/ppermute | solution.py:52
  243.1 29.7 %collective-permute-start.34 = (bf16[256,1024]{1,0:T(8,128)(2,1)}, bf16[256,1024]{1,0:T(8,128)(2,1)}, u32[]{:S(2)}, u32[]{:S(2)}) collective-permute-start(bf16[256,1024]{1,0:T(8,128)(2,1)} %get-tuple-element.271), channel_id=1, source_target_pairs={{0,16},{8,24},{16,32},{24,40},{32,48},{40,56},{48,0},{56,8},{64,80... | collective-permute-start | bytes 1572872 | tf_op jit(solution)/shard_map/ppermute | solution.py:52
  272.8 41.3 %collective-permute-start.40 = (bf16[8,224,1024]{2,1,0:T(8,128)(2,1)}, bf16[8,224,1024]{2,1,0:T(8,128)(2,1)S(1)}, u32[]{:S(2)}, u32[]{:S(2)}) collective-permute-start(bf16[8,224,1024]{2,1,0:T(8,128)(2,1)} %get-tuple-element.204), channel_id=1, source_target_pairs={{0,8},{8,0},{16,24},{24,16},{32,40},{40,32},{48,56},{56,48},{64,72... | collective-permute-start | bytes 11010056 | tf_op jit(solution)/shard_map/ppermute | solution.py:56
  347.8 82.7 %collective-permute-start.44 = (bf16[2,224,1024]{2,1,0:T(8,128)(2,1)}, bf16[2,224,1024]{2,1,0:T(8,128)(2,1)}, u32[]{:S(2)}, u32[]{:S(2)}) collective-permute-start(bf16[2,224,1024]{2,1,0:T(8,128)(2,1)} %get-tuple-element.258), channel_id=1, source_target_pairs={{0,48},{8,56},{16,0},{24,8},{32,16},{40,24},{48,32},{56,40},{64,11... | collective-permute-start | bytes 2752520 | tf_op jit(solution)/shard_map/ppermute | solution.py:52
  349.1 81.4 %collective-permute-start.45 = (bf16[2,224,1024]{2,1,0:T(8,128)(2,1)}, bf16[2,224,1024]{2,1,0:T(8,128)(2,1)}, u32[]{:S(2)}, u32[]{:S(2)}) collective-permute-start(bf16[2,224,1024]{2,1,0:T(8,128)(2,1)} %get-tuple-element.257), channel_id=1, source_target_pairs={{0,16},{8,24},{16,32},{24,40},{32,48},{40,56},{48,0},{56,8},{64,80... | collective-permute-start | bytes 2752520 | tf_op jit(solution)/shard_map/ppermute | solution.py:52
  349.8 80.7 %collective-permute-start.46 = (bf16[2,224,1024]{2,1,0:T(8,128)(2,1)}, bf16[2,224,1024]{2,1,0:T(8,128)(2,1)}, u32[]{:S(2)}, u32[]{:S(2)}) collective-permute-start(bf16[2,224,1024]{2,1,0:T(8,128)(2,1)} %get-tuple-element.256), channel_id=1, source_target_pairs={{0,32},{8,40},{16,48},{24,56},{32,0},{40,8},{48,16},{56,24},{64,96... | collective-permute-start | bytes 2752520 | tf_op jit(solution)/shard_map/ppermute | solution.py:52
  351.4 43.9 %all-to-all-start.4 = ((bf16[16,64,224]{2,1,0:T(8,128)(2,1)}), bf16[16,64,224]{2,1,0:T(8,128)(2,1)}, u32[]{:S(2)}, u32[]{:S(2)}) async-start(bf16[16,64,224]{2,1,0:T(8,128)(2,1)} %get-tuple-element.209), calls=%async_computation.4 | async-start | bytes 1048576 | tf_op jit(solution)/shard_map/all_to_all | solution.py:782
  395.3 50.2 %collective-permute-start.47 = (bf16[2,2,192,1024]{3,2,1,0:T(8,128)(2,1)}, bf16[2,2,192,1024]{3,2,1,0:T(8,128)(2,1)}, u32[]{:S(2)}, u32[]{:S(2)}) collective-permute-start(bf16[2,2,192,1024]{3,2,1,0:T(8,128)(2,1)} %pad_maximum_fusion.9), channel_id=1, source_target_pairs={{0,6},{1,7},{2,0},{3,1},{4,2},{5,3},{6,4},{7,5},{8,14},{9,15},{10,... | collective-permute-start | bytes 4718600 | tf_op jit(solution)/shard_map/ppermute | solution.py:94
  397.1 51.4 %collective-permute-start.48 = (bf16[2,2,192,1024]{3,2,1,0:T(8,128)(2,1)}, bf16[2,2,192,1024]{3,2,1,0:T(8,128)(2,1)}, u32[]{:S(2)}, u32[]{:S(2)}) collective-permute-start(bf16[2,2,192,1024]{3,2,1,0:T(8,128)(2,1)} %pad_maximum_fusion.10), channel_id=1, source_target_pairs={{0,2},{1,3},{2,4},{3,5},{4,6},{5,7},{6,0},{7,1},{8,10},{9,11},{10,... | collective-permute-start | bytes 4718600 | tf_op jit(solution)/shard_map/ppermute | solution.py:94
  399.0 78.4 %all-to-all-start.5 = ((bf16[16,8,8,1152]{3,2,0,1:T(8,128)(2,1)}), bf16[16,8,8,1152]{3,2,0,1:T(8,128)(2,1)S(1)}, u32[]{:S(2)}, u32[]{:S(2)}) async-start(bf16[16,8,8,1152]{3,2,0,1:T(8,128)(2,1)} %copy.146), calls=%async_computation.5 | async-start | bytes 4718592 | tf_op jit(solution)/shard_map/all_to_all | solution.py:790
  477.5 57.4 %collective-permute-start.50 = (bf16[4,224,1024]{2,1,0:T(8,128)(2,1)}, bf16[4,224,1024]{2,1,0:T(8,128)(2,1)}, u32[]{:S(2)}, u32[]{:S(2)}) collective-permute-start(bf16[4,224,1024]{2,1,0:T(8,128)(2,1)} %get-tuple-element.241), channel_id=1, source_target_pairs={{0,8},{8,0},{16,24},{24,16},{32,40},{40,32},{48,56},{56,48},{64,72... | collective-permute-start | bytes 5505032 | tf_op jit(solution)/shard_map/ppermute | solution.py:56
  483.0 48.6 %collective-permute-start.59 = (bf16[2,192,1024]{2,1,0:T(8,128)(2,1)}, bf16[2,192,1024]{2,1,0:T(8,128)(2,1)}, u32[]{:S(2)}, u32[]{:S(2)}) collective-permute-start(bf16[2,192,1024]{2,1,0:T(8,128)(2,1)} %dynamic-slice_bitcast_fusion), channel_id=1, source_target_pairs={{0,1},{1,0},{2,3},{3,2},{4,5},{5,4},{6,7},{7,6},{8,9},{9,8},{10,11... | collective-permute-start | bytes 2359304 | tf_op jit(solution)/shard_map/ppermute | solution.py:94
  492.3 30.3 %collective-permute-start.55 = (bf16[224,1024]{1,0:T(8,128)(2,1)}, bf16[224,1024]{1,0:T(8,128)(2,1)S(1)}, u32[]{:S(2)}, u32[]{:S(2)}) collective-permute-start(bf16[224,1024]{1,0:T(8,128)(2,1)} %get-tuple-element.277), channel_id=1, source_target_pairs={{0,48},{8,56},{16,0},{24,8},{32,16},{40,24},{48,32},{56,40},{64,11... | collective-permute-start | bytes 1376264 | tf_op jit(solution)/shard_map/ppermute | solution.py:52
  495.4 30.6 %collective-permute-start.56 = (bf16[224,1024]{1,0:T(8,128)(2,1)}, bf16[224,1024]{1,0:T(8,128)(2,1)S(1)}, u32[]{:S(2)}, u32[]{:S(2)}) collective-permute-start(bf16[224,1024]{1,0:T(8,128)(2,1)} %get-tuple-element.279), channel_id=1, source_target_pairs={{0,16},{8,24},{16,32},{24,40},{32,48},{40,56},{48,0},{56,8},{64,80... | collective-permute-start | bytes 1376264 | tf_op jit(solution)/shard_map/ppermute | solution.py:52
  495.4 30.6 %collective-permute-start.57 = (bf16[224,1024]{1,0:T(8,128)(2,1)S(1)}, bf16[224,1024]{1,0:T(8,128)(2,1)}, u32[]{:S(2)}, u32[]{:S(2)}) collective-permute-start(bf16[224,1024]{1,0:T(8,128)(2,1)S(1)} %get-tuple-element.278), channel_id=1, source_target_pairs={{0,32},{8,40},{16,48},{24,56},{32,0},{40,8},{48,16},{56,24},{64,96... | collective-permute-start | bytes 1376264 | tf_op jit(solution)/shard_map/ppermute | solution.py:52
  505.8 34.6 %all-to-all-start.6 = ((bf16[128,8,256]{2,1,0:T(8,128)(2,1)}), bf16[128,8,256]{2,1,0:T(8,128)(2,1)S(1)}, u32[]{:S(2)}, u32[]{:S(2)}) async-start(bf16[128,8,256]{2,1,0:T(8,128)(2,1)} %convert_bitcast_fusion), calls=%async_computation.6 | async-start | bytes 1048576 | tf_op jit(solution)/shard_map/all_to_all | solution.py:807
  (78 other events, 1103.3 us)

commit v6 on v5

--- a/solution.py
+++ b/solution.py
@@ -84,14 +84,22 @@
 
 
 def sum_along_z(mine, other):
-    got = swap_cores(other)
-    parts = [add_low(mine[i], got[i]) for i in range(4)]
+    return send_along_z(chip_parts(mine, swap_cores(other)))
+
+
+def chip_parts(mine, got):
+    return [add_low(mine[i], got[i]) for i in range(4)]
+
+
+def send_along_z(parts):
     return [parts[0]] + [send(parts[i], 0, -b) for i, b in ((1, 1), (2, 3), (3, 2))]
 
 
-def send_w(rows, a, b):
-    pairs = [(y * 2 + x, ((y + b) % 4) * 2 + (x ^ a)) for y in range(4) for x in range(2)]
-    return lax.ppermute(rows, "wshard", pairs)
+def swap_x(rows):
+    return lax.ppermute(rows, "wshard", [(w, w ^ 1) for w in range(8)])
+
+
+ALONG_Y = [[y * 2 + x for y in range(4)] for x in range(2)]
 
 
 def tie(*values):
@@ -122,15 +130,12 @@
     return position, jnp.where(inside, PROMPT + begin, 0)
 
 
-def rotary_tables(position):
+def rotary_table(position):
     half_dim = HEAD_DIM // 2
     inverse = rope_base ** (-(jnp.arange(half_dim, dtype=f32) * 2.0) / HEAD_DIM)
     angles = position[:, None] * inverse[None, :]
     cosine, sine = jnp.cos(angles), jnp.sin(angles)
-    return (
-        jnp.concatenate([cosine, cosine], axis=-1),
-        jnp.concatenate([sine, sine], axis=-1),
-    )
+    return jnp.concatenate([cosine, cosine, sine, sine], axis=-1)
 
 
 def turn(values):
@@ -143,99 +148,118 @@
     return jnp.concatenate([values[:, half_dim:], -values[:, :half_dim]], axis=-1)
 
 
-def project_kernel(places, mine, other, w, gain, cosine, sine, *refs):
-    del places
-    normed_ref, q_ref, k_ref, v_ref = refs[-4:]
-    rows = jnp.where(pl.program_id(1) == 0, mine[0], other[0])
-    values = rows.astype(f32)
-    normed = (values * inverse_rms(values) * gain[...]).astype(bf16)
-    normed_ref[0] = normed
-    projected = jnp.dot(normed, w[...], preferred_element_type=f32)
-    c, s = cosine[...], sine[...]
-    q, k, v = projected[:, :64], projected[:, 64:128], projected[:, 128:192]
-    q_ref[...] = ((q * c + turn(q) * s).astype(bf16).astype(f32) * HEAD_DIM**-0.5).astype(bf16)
-    k_ref[...] = (k * c + turn(k) * s).astype(bf16)
-    v_ref[...] = v.astype(bf16)
-
-
-def project(places, gathered, w, gain, cosine, sine, before):
-    chip = pl.BlockSpec((1, TOK, WIDTH), lambda j, k, p: (j, 0, 0))
-    whole = lambda shape: pl.BlockSpec(shape, lambda j, k, p: (0,) * len(shape))
-    at = pl.BlockSpec((TOK, HEAD_DIM), lambda j, k, p: (p[2 * j + k], 0))
-    table = jax.ShapeDtypeStruct((GROUP, HEAD_DIM), bf16)
+def project_kernel(places, mine, other, w, gain, table, *refs):
+    out = refs[-1]
+    j = pl.program_id(0)
+
+    if len(refs) > 1:
+
+        @pl.when(j == 0)
+        def _():
+            out[...] = refs[0][...]
+
+    for k, ref in enumerate((mine, other)):
+        at = pl.ds(pl.multiple_of(places[2 * j + k] * TOK, TOK), TOK)
+        rows = ref[0].astype(f32)
+        normed = (rows * inverse_rms(rows) * gain[...]).astype(bf16)
+        projected = jnp.dot(normed, w[...], preferred_element_type=f32)
+        c, s = table[at, :HEAD_DIM], table[at, HEAD_DIM:]
+        q, k, v = projected[:, :64], projected[:, 64:128], projected[:, 128:]
+        q = (q * c + turn(q) * s).astype(bf16).astype(f32) * HEAD_DIM**-0.5
+        out[at, :] = jnp.concatenate([q, k * c + turn(k) * s, v], axis=1).astype(bf16)
+
+
+def project(places, gathered, w, gain, table, before):
+    chip = pl.BlockSpec((1, TOK, WIDTH), lambda j, p: (j, 0, 0))
+    whole = lambda *shape: pl.BlockSpec(shape, lambda j, p: (0,) * len(shape))
     return pl.pallas_call(
         project_kernel,
         grid_spec=pltpu.PrefetchScalarGridSpec(
             num_scalar_prefetch=1,
-            grid=(4, 2),
-            in_specs=[chip, chip, whole((WIDTH, 256)), whole((1, WIDTH)), at, at]
-            + [pl.BlockSpec(memory_space=pl.ANY)] * len(before),
-            out_specs=[pl.BlockSpec((1, TOK, WIDTH), lambda j, k, p: (2 * j + k, 0, 0)), at, at, at],
-        ),
-        out_shape=[jax.ShapeDtypeStruct((8, TOK, WIDTH), bf16), table, table, table],
-        input_output_aliases={7 + i: 1 + i for i in range(len(before))},
+            grid=(4,),
+            in_specs=[chip, chip, whole(WIDTH, 256), whole(1, WIDTH), whole(GROUP, 128)]
+            + [whole(GROUP, 256)] * len(before),
+            out_specs=whole(GROUP, 256),
+        ),
+        out_shape=jax.ShapeDtypeStruct((GROUP, 256), bf16),
         compiler_params=pltpu.CompilerParams(vmem_limit_bytes=VMEM_LIMIT),
         cost_estimate=pl.CostEstimate(
             flops=2 * 8 * TOK * WIDTH * 256, bytes_accessed=10 << 20, transcendentals=0
         ),
-    )(places, *gathered, w, gain, cosine, sine, *before)
-
-
-def project_back_kernel(places, normed, dq, dk, dv, w, cosine, sine, *refs):
+    )(places, *gathered, w, gain, table, *before)
+
+
+def project_back_kernel(places, first, second, w, mine, other):
     del places
-    mine, other, grad = refs[-3:]
-    first = (pl.program_id(0) == 0) & (pl.program_id(1) == 0)
-
-    @pl.when(first)
-    def _():
-        grad[...] = jnp.zeros_like(grad) if len(refs) == 3 else refs[0][...]
-
-    c, s = cosine[...], sine[...]
-    q = dq[...].astype(bf16).astype(f32)
-    k = dk[...].astype(bf16).astype(f32)
-    projected = jnp.concatenate(
-        [q * c + turn_back(q * s), k * c + turn_back(k * s), dv[...], jnp.zeros_like(q)], axis=1
-    ).astype(bf16)
-    grad[...] += lax.dot_general(normed[0], projected, TN, preferred_element_type=f32)
-    part = lax.dot_general(projected, w[...], NT, preferred_element_type=f32).astype(bf16)
-
-    @pl.when(pl.program_id(1) == 0)
-    def _():
-        mine[0] = part
-
-    @pl.when(pl.program_id(1) == 1)
-    def _():
-        other[0] = part
-
-
-def project_back(places, normed, grads, w, cosine, sine, before):
-    chip = pl.BlockSpec((1, TOK, WIDTH), lambda j, k, p: (j, 0, 0))
-    whole = lambda shape: pl.BlockSpec(shape, lambda j, k, p: (0,) * len(shape))
-    at = pl.BlockSpec((TOK, HEAD_DIM), lambda j, k, p: (p[2 * j + k], 0))
+    mine[0] = lax.dot_general(first[...], w[...], NT, preferred_element_type=f32).astype(bf16)
+    other[0] = lax.dot_general(second[...], w[...], NT, preferred_element_type=f32).astype(bf16)
+
+
+def project_back(places, projected_grad, w):
+    chip = pl.BlockSpec((1, TOK, WIDTH), lambda j, p: (j, 0, 0))
+    at = lambda k: pl.BlockSpec((TOK, 256), lambda j, p: (p[2 * j + k], 0))
     part = jax.ShapeDtypeStruct((4, TOK, WIDTH), bf16)
     return pl.pallas_call(
         project_back_kernel,
         grid_spec=pltpu.PrefetchScalarGridSpec(
             num_scalar_prefetch=1,
-            grid=(4, 2),
-            in_specs=[
-                pl.BlockSpec((1, TOK, WIDTH), lambda j, k, p: (2 * j + k, 0, 0)),
-                at,
-                at,
-                at,
-                whole((WIDTH, 256)),
-                at,
-                at,
-            ]
-            + [whole((WIDTH, 256))] * len(before),
-            out_specs=[chip, chip, whole((WIDTH, 256))],
-        ),
-        out_shape=[part, part, jax.ShapeDtypeStruct((WIDTH, 256), f32)],
+            grid=(4,),
+            in_specs=[at(0), at(1), pl.BlockSpec((WIDTH, 256), lambda j, p: (0, 0))],
+            out_specs=[chip, chip],
+        ),
+        out_shape=[part, part],
         compiler_params=pltpu.CompilerParams(vmem_limit_bytes=VMEM_LIMIT),
         cost_estimate=pl.CostEstimate(
-            flops=4 * 8 * TOK * WIDTH * 256, bytes_accessed=12 << 20, transcendentals=0
-        ),
-    )(places, normed, *grads, w, cosine, sine, *before)
+            flops=2 * 8 * TOK * WIDTH * 256, bytes_accessed=5 << 20, transcendentals=0
+        ),
+    )(places, projected_grad, projected_grad, w)
+
+
+def head_grad_kernel(places, near_mine, near_other, far_mine, far_other, gain, first, second, out, total):
+    del places
+    j = pl.program_id(0)
+
+    @pl.when(j == 0)
+    def _():
+        total[...] = jnp.zeros_like(total)
+
+    for near, far, projected in ((near_mine, far_mine, first), (near_other, far_other, second)):
+        rows = jnp.where(j < 4, near[0], far[0]).astype(f32)
+        normed = (rows * inverse_rms(rows) * gain[...]).astype(bf16)
+        total[...] += lax.dot_general(normed, projected[...], TN, preferred_element_type=f32)
+
+    @pl.when(j == 7)
+    def _():
+        out[...] = total[...].astype(bf16)
+
+
+def head_weight_grad(places, near, far, gain, projected_grad):
+    near_chip = pl.BlockSpec((1, TOK, WIDTH), lambda j, p: (jnp.minimum(j, 3), 0, 0))
+    far_chip = pl.BlockSpec((1, TOK, WIDTH), lambda j, p: (jnp.maximum(j - 4, 0), 0, 0))
+    at = lambda k: pl.BlockSpec((TOK, 256), lambda j, p: (p[2 * j + k], 0))
+    return pl.pallas_call(
+        head_grad_kernel,
+        grid_spec=pltpu.PrefetchScalarGridSpec(
+            num_scalar_prefetch=1,
+            grid=(8,),
+            in_specs=[
+                near_chip,
+                near_chip,
+                far_chip,
+                far_chip,
+                pl.BlockSpec((1, WIDTH), lambda j, p: (0, 0)),
+                at(0),
+                at(1),
+            ],
+            out_specs=pl.BlockSpec((WIDTH, 256), lambda j, p: (0, 0)),
+            scratch_shapes=[pltpu.VMEM((WIDTH, 256), f32)],
+        ),
+        out_shape=jax.ShapeDtypeStruct((WIDTH, 256), bf16),
+        compiler_params=pltpu.CompilerParams(vmem_limit_bytes=VMEM_LIMIT),
+        cost_estimate=pl.CostEstimate(
+            flops=2 * 16 * TOK * WIDTH * 256, bytes_accessed=10 << 20, transcendentals=0
+        ),
+    )(places, *near, *far, gain, projected_grad, projected_grad)
 
 
 def tile_mask(scores, key_start, query_start, begin):
@@ -249,21 +273,23 @@
     return jnp.where(i > first, i - 1, i), jnp.minimum(i, first)
 
 
-def attend_kernel(q_ref, k_ref, v_ref, begin_ref, o_ref, ot_ref, lse_ref, vt):
+def attend_kernel(qkv_ref, begin_ref, o_ref, ot_ref, lse_ref, keys, vt):
     i = pl.program_id(0)
+    here = pl.ds(pl.multiple_of(i * BLOCK, BLOCK), BLOCK)
 
     @pl.when(i == 0)
     def _():
-        vt[...] = v_ref[...].T
-
-    q = q_ref[...]
+        keys[...] = qkv_ref[:, 64:128]
+        vt[...] = qkv_ref[:, 128:192].T
+
+    q = qkv_ref[here, :64]
     begin = begin_ref[...]
 
     def tile(j, carry, masked, n=1):
         peak, total, out = carry
         start = pl.multiple_of(j * BLOCK, BLOCK)
         at = pl.ds(start, n * BLOCK)
-        s = lax.dot_general(k_ref[at, :], q, NT, preferred_element_type=f32)
+        s = lax.dot_general(keys[at, :], q, NT, preferred_element_type=f32)
         if masked:
             s = tile_mask(s, start, i * BLOCK, begin)
         higher = jnp.maximum(peak, jnp.max(s, axis=0, keepdims=True))
@@ -284,7 +310,7 @@
     pairs = shared // 2
     carry = lax.fori_loop(0, pairs, lambda j, c: tile(2 * j, c, False, 2), carry)
     peak, total, out = lax.fori_loop(2 * pairs, shared, lambda j, c: tile(j, c, False), carry)
-    ot_ref[:, pl.ds(pl.multiple_of(i * BLOCK, BLOCK), BLOCK)] = out * (1.0 / total)
+    ot_ref[:, here] = out * (1.0 / total)
     lse_ref[...] = peak + jnp.log(total)
 
     @pl.when(i == GROUP // BLOCK - 1)
@@ -293,41 +319,48 @@
             o_ref[b] = ot_ref[:, b * TOK : (b + 1) * TOK].astype(bf16)
 
 
-def attend(q, k, v, begin):
+def attend(qkv, begin):
     whole = lambda *shape: pl.BlockSpec(shape, lambda i: (0,) * len(shape))
-    rows = pl.BlockSpec((BLOCK, HEAD_DIM), lambda i: (i, 0))
     cols = lambda n: pl.BlockSpec((n, BLOCK), lambda i: (0, i))
     return pl.pallas_call(
         attend_kernel,
         grid=(GROUP // BLOCK,),
-        in_specs=[rows, whole(GROUP, HEAD_DIM), whole(GROUP, HEAD_DIM), cols(1)],
+        in_specs=[whole(GROUP, 256), cols(1)],
         out_specs=[whole(16, HEAD_DIM, TOK), whole(HEAD_DIM, GROUP), cols(1)],
         out_shape=[
             jax.ShapeDtypeStruct((16, HEAD_DIM, TOK), bf16),
             jax.ShapeDtypeStruct((HEAD_DIM, GROUP), f32),
             jax.ShapeDtypeStruct((1, GROUP), f32),
         ],
-        scratch_shapes=[pltpu.VMEM((HEAD_DIM, GROUP), bf16)],
+        scratch_shapes=[
+            pltpu.VMEM((GROUP, HEAD_DIM), bf16),
+            pltpu.VMEM((HEAD_DIM, GROUP), bf16),
+        ],
         compiler_params=pltpu.CompilerParams(vmem_limit_bytes=VMEM_LIMIT),
         cost_estimate=pl.CostEstimate(
             flops=2 * 27 * BLOCK * BLOCK * 512, bytes_accessed=4 << 20, transcendentals=27 * BLOCK * BLOCK
         ),
-    )(q, k, v, begin)
-
-
-def attend_back_kernel(q_ref, k_ref, v_ref, g_ref, ot_ref, lse_ref, begin_ref, dq_ref, dk_ref, dv_ref, kt, gt):
+    )(qkv, begin)
+
+
+def attend_back_kernel(
+    qkv_ref, g_ref, ot_ref, lse_ref, begin_ref, table, out_ref, keys, values, kt, gt, dq, dk, dv
+):
     i = pl.program_id(0)
+    here = pl.ds(pl.multiple_of(i * BLOCK, BLOCK), BLOCK)
 
     @pl.when(i == 0)
     def _():
-        dk_ref[...] = jnp.zeros_like(dk_ref)
-        dv_ref[...] = jnp.zeros_like(dv_ref)
-        kt[...] = k_ref[...].T
+        dk[...] = jnp.zeros_like(dk)
+        dv[...] = jnp.zeros_like(dv)
+        keys[...] = qkv_ref[:, 64:128]
+        values[...] = qkv_ref[:, 128:192]
+        kt[...] = qkv_ref[:, 64:128].T
         for b in range(16):
             gt[:, b * TOK : (b + 1) * TOK] = g_ref[b]
 
-    q = q_ref[...]
-    g = gt[:, pl.ds(pl.multiple_of(i * BLOCK, BLOCK), BLOCK)]
+    q = qkv_ref[here, :64]
+    g = gt[:, here]
     begin = begin_ref[...]
     lse = lse_ref[...]
     inner = jnp.sum(g.astype(f32) * ot_ref[...], axis=0, keepdims=True)
@@ -335,64 +368,84 @@
     def tile(j, dq, masked, n=1):
         start = pl.multiple_of(j * BLOCK, BLOCK)
         at = pl.ds(start, n * BLOCK)
-        s = lax.dot_general(k_ref[at, :], q, NT, preferred_element_type=f32)
+        s = lax.dot_general(keys[at, :], q, NT, preferred_element_type=f32)
         if masked:
             s = tile_mask(s, start, i * BLOCK, begin)
         p = jnp.exp(s - lse)
-        dp = jnp.dot(v_ref[at, :], g, preferred_element_type=f32)
+        dp = jnp.dot(values[at, :], g, preferred_element_type=f32)
         ds = (p * (dp - inner)).astype(bf16)
-        dv_ref[at, :] += lax.dot_general(p.astype(bf16), g, NT, preferred_element_type=f32)
-        dk_ref[at, :] += jnp.dot(ds, q, preferred_element_type=f32)
+        dv[at, :] += lax.dot_general(p.astype(bf16), g, NT, preferred_element_type=f32)
+        dk[at, :] += jnp.dot(ds, q, preferred_element_type=f32)
         return dq + jnp.dot(kt[:, at], ds, preferred_element_type=f32)
 
-    dq = tile(i, jnp.zeros((HEAD_DIM, BLOCK), f32), True)
+    dqt = tile(i, jnp.zeros((HEAD_DIM, BLOCK), f32), True)
     window, shared = key_ranges(i)
-    dq = lax.fori_loop(window, i, lambda j, c: tile(j, c, True), dq)
+    dqt = lax.fori_loop(window, i, lambda j, c: tile(j, c, True), dqt)
     pairs = shared // 2
-    dq = lax.fori_loop(0, pairs, lambda j, c: tile(2 * j, c, False, 2), dq)
-    dq = lax.fori_loop(2 * pairs, shared, lambda j, c: tile(j, c, False), dq)
-    dq_ref[...] = dq.T * HEAD_DIM**-0.5
-
-
-def attend_back(q, k, v, g, ot, lse, begin):
+    dqt = lax.fori_loop(0, pairs, lambda j, c: tile(2 * j, c, False, 2), dqt)
+    dqt = lax.fori_loop(2 * pairs, shared, lambda j, c: tile(j, c, False), dqt)
+    dq[here, :] = dqt.T * HEAD_DIM**-0.5
+
+    @pl.when(i == GROUP // BLOCK - 1)
+    def _():
+        def back(b, _):
+            at = pl.ds(pl.multiple_of(b * BLOCK, BLOCK), BLOCK)
+            c, s = table[at, :HEAD_DIM], table[at, HEAD_DIM:]
+            q, k = dq[at, :].astype(bf16).astype(f32), dk[at, :].astype(bf16).astype(f32)
+            parts = [q * c + turn_back(q * s), k * c + turn_back(k * s), dv[at, :], jnp.zeros_like(q)]
+            out_ref[at, :] = jnp.concatenate(parts, axis=1).astype(bf16)
+            return 0
+
+        lax.fori_loop(0, GROUP // BLOCK, back, 0)
+
+
+def attend_back(qkv, g, ot, lse, begin, table):
     whole = lambda *shape: pl.BlockSpec(shape, lambda i: (0,) * len(shape))
-    rows = pl.BlockSpec((BLOCK, HEAD_DIM), lambda i: (i, 0))
     cols = lambda n: pl.BlockSpec((n, BLOCK), lambda i: (0, i))
-    out = jax.ShapeDtypeStruct((GROUP, HEAD_DIM), f32)
     return pl.pallas_call(
         attend_back_kernel,
         grid=(GROUP // BLOCK,),
-        in_specs=[rows, whole(GROUP, HEAD_DIM), whole(GROUP, HEAD_DIM), whole(16, HEAD_DIM, TOK), cols(HEAD_DIM), cols(1), cols(1)],
-        out_specs=[rows, whole(GROUP, HEAD_DIM), whole(GROUP, HEAD_DIM)],
-        out_shape=[out, out, out],
-        scratch_shapes=[pltpu.VMEM((HEAD_DIM, GROUP), bf16), pltpu.VMEM((HEAD_DIM, GROUP), bf16)],
+        in_specs=[
+            whole(GROUP, 256),
+            whole(16, HEAD_DIM, TOK),
+            cols(HEAD_DIM),
+            cols(1),
+            cols(1),
+            whole(GROUP, 128),
+        ],
+        out_specs=whole(GROUP, 256),
+        out_shape=jax.ShapeDtypeStruct((GROUP, 256), bf16),
+        scratch_shapes=[
+            pltpu.VMEM((GROUP, HEAD_DIM), bf16),
+            pltpu.VMEM((GROUP, HEAD_DIM), bf16),
+            pltpu.VMEM((HEAD_DIM, GROUP), bf16),
+            pltpu.VMEM((HEAD_DIM, GROUP), bf16),
+            pltpu.VMEM((GROUP, HEAD_DIM), f32),
+            pltpu.VMEM((GROUP, HEAD_DIM), f32),
+            pltpu.VMEM((GROUP, HEAD_DIM), f32),
+        ],
         compiler_params=pltpu.CompilerParams(vmem_limit_bytes=VMEM_LIMIT),
         cost_estimate=pl.CostEstimate(
             flops=5 * 27 * BLOCK * BLOCK * 512, bytes_accessed=8 << 20, transcendentals=27 * BLOCK * BLOCK
         ),
-    )(q, k, v, g, ot, lse, begin)
-
-
-SHARDS = [(0, 0, 0), (0, 1, 1), (1, 0, 2), (1, 1, 3), (2, 0, 6), (2, 1, 7), (3, None, 4), (4, None, 5)]
-N_SHARDS = 5
+    )(qkv, g, ot, lse, begin, table)
 
 
 def experts_kernel(
-    own_ref, ffn_mine, ffn_other, g_mine, g_other, routes_mine, routes_other, router_ref, *refs
+    own_ref, ffn_mine, ffn_other, g_mine, g_other, routes_mine, routes_other, router_ref, own_w, across_w, *refs
 ):
-    shards = refs[:N_SHARDS]
     routed_mine, routed_other, moved_mine, moved_other = refs[-10:-6]
     x_ref, dh_ref, act_ref, dy_ref, w_ref, sem = refs[-6:]
     own = own_ref[0]
 
     @pl.when(pl.program_id(0) == 0)
     def _():
-        copies = []
-        for n, (shard, a, r) in enumerate(SHARDS):
-            source = shards[shard] if a is None else shards[shard].at[a]
-            for e in range(2):
-                place = own_ref[1 + r]
-                copies.append(pltpu.make_async_copy(source.at[e], w_ref.at[e, place], sem.at[n, e]))
+        copies = [
+            pltpu.make_async_copy(shards.at[y, e], w_ref.at[e, 2 * y + (own_ref[1] ^ a)], sem.at[a, y, e])
+            for a, shards in enumerate((own_w, across_w))
+            for y in range(4)
+            for e in range(2)
+        ]
         for copy in copies:
             copy.start()
         for copy in copies:
@@ -506,7 +559,7 @@
                 routes,
                 whole((EXPERTS, WIDTH)),
             ]
-            + [pl.BlockSpec(memory_space=pl.ANY)] * (N_SHARDS + len(before)),
+            + [pl.BlockSpec(memory_space=pl.ANY)] * (2 + len(before)),
             out_specs=[
                 summed,
                 summed,
@@ -519,7 +572,7 @@
             ],
             scratch_shapes=[
                 pltpu.VMEM((2, 8, 192, 1024), bf16),
-                pltpu.SemaphoreType.DMA((8, 2)),
+                pltpu.SemaphoreType.DMA((2, 4, 2)),
             ],
         ),
         out_shape=[
@@ -532,7 +585,7 @@
             keep(FF),
             keep(WIDTH),
         ],
-        input_output_aliases={8 + N_SHARDS + i: 2 + i for i in range(len(before))},
+        input_output_aliases={10 + i: 2 + i for i in range(len(before))},
         compiler_params=pltpu.CompilerParams(vmem_limit_bytes=VMEM_LIMIT),
         cost_estimate=pl.CostEstimate(
             flops=14 << 30, bytes_accessed=24 << 20, transcendentals=8 * SLOTS * 2 * FF
@@ -540,32 +593,28 @@
     )(own, *ffn, *grads, *grads, router, *weights, *before)
 
 
-def expert_grads_kernel(order, x_ref, dh_ref, act_ref, dy_ref, out_ref):
-    del order
+def expert_grads_kernel(x_ref, dh_ref, act_ref, dy_ref, out_ref):
     up = lax.dot_general(x_ref[0], dh_ref[0], TN, preferred_element_type=f32)
     down = lax.dot_general(act_ref[0], dy_ref[0], TN, preferred_element_type=f32)
     out_ref[0, :, 0, :128, :] = up.astype(bf16).reshape(2, 128, 2 * FF)
     out_ref[0, :, 0, 128:, :] = down.astype(bf16).reshape(2, 64, WIDTH)
 
 
-def expert_weight_grads(order, x, dh, act, dy):
+def expert_weight_grads(x, dh, act, dy):
     return pl.pallas_call(
         expert_grads_kernel,
-        grid_spec=pltpu.PrefetchScalarGridSpec(
-            num_scalar_prefetch=1,
-            grid=(2, 4),
-            in_specs=[
-                pl.BlockSpec((1, ALL_ROWS, 256), lambda e, i, o: (e, 0, i)),
-                pl.BlockSpec((1, ALL_ROWS, 2 * FF), lambda e, i, o: (e, 0, 0)),
-                pl.BlockSpec((1, ALL_ROWS, 128), lambda e, i, o: (e, 0, i)),
-                pl.BlockSpec((1, ALL_ROWS, WIDTH), lambda e, i, o: (e, 0, 0)),
-            ],
-            out_specs=pl.BlockSpec((1, 2, 1, 192, 1024), lambda e, i, o: (o[i], 0, e, 0, 0)),
-        ),
+        grid=(2, 4),
+        in_specs=[
+            pl.BlockSpec((1, ALL_ROWS, 256), lambda e, i: (e, 0, i)),
+            pl.BlockSpec((1, ALL_ROWS, 2 * FF), lambda e, i: (e, 0, 0)),
+            pl.BlockSpec((1, ALL_ROWS, 128), lambda e, i: (e, 0, i)),
+            pl.BlockSpec((1, ALL_ROWS, WIDTH), lambda e, i: (e, 0, 0)),
+        ],
+        out_specs=pl.BlockSpec((1, 2, 1, 192, 1024), lambda e, i: (i, 0, e, 0, 0)),
         out_shape=jax.ShapeDtypeStruct((4, 2, 2, 192, 1024), bf16),
         compiler_params=pltpu.CompilerParams(vmem_limit_bytes=VMEM_LIMIT),
         cost_estimate=pl.CostEstimate(flops=8 << 30, bytes_accessed=14 << 20, transcendentals=0),
-    )(order, x, dh, act, dy)
+    )(x, dh, act, dy)
 
 
 def hidden_kernel(att_ref, w_ref, rows_ref, gain_ref, hidden_ref, normed_ref):
@@ -683,7 +732,7 @@
 
     position, begin = group_layout(cont_lengths[0])
     begin = begin[None]
-    cosine, sine = rotary_tables(position.astype(f32))
+    table = rotary_table(position.astype(f32))
     kv_heads = lambda start: jnp.repeat(
         w_qkv[:, start : start + kv_width].reshape(8, KV_HEADS, HEAD_DIM), 2, axis=1
     )
@@ -702,19 +751,15 @@
     head_weights = jnp.where(jnp.arange(256)[None] < 192, head_weights, 0.0).astype(bf16)
 
     rows_near, rows_across = gather_near(rows)
-    rows_near, _, cosine, sine, head_weights = tie(
-        rows_near, rows_across, cosine, sine, head_weights
-    )
+    rows_near, _, table, head_weights = tie(rows_near, rows_across, table, head_weights)
     rows_near, rows_far = both_cores(rows_near), gather_far(rows_across)
 
-    w_index = lax.axis_index("wshard")
-    own_y, own_x = w_index // 2, w_index % 2
+    own_x = lax.axis_index("wshard") % 2
     expert_rows = jnp.concatenate([w_gate_up, w_down], axis=1)
-    expert_pair = jnp.stack([expert_rows, send_w(expert_rows, 1, 0)])
-    pair_before, pair_after = send_w(expert_pair, 0, 1), send_w(expert_pair, 0, -1)
-    w_places = [((own_y - b) % 4) * 2 + (own_x ^ a) for b in range(4) for a in range(2)]
-
-    normed_near, *qkv = project(places[:8], rows_near, head_weights, gain_attn, cosine, sine, ())
+    along_y = lambda t: lax.all_gather(t, "wshard", axis_index_groups=ALONG_Y, axis=0)
+    experts, expert_rows = along_y(expert_rows), swap_x(expert_rows)
+
+    qkv = project(places[:8], rows_near, head_weights, gain_attn, table, ())
     shared = jnp.concatenate(
         [w_out, w_router, norm_ffn[:, None], jnp.zeros((8, 95), bf16)], axis=1
     )
@@ -722,97 +767,91 @@
     shared = lax.all_to_all(
         jnp.broadcast_to(shared[None], (8, 8, 1152)), "wshard", 0, 0, tiled=True
     ).reshape(64, 1152)
-    rows_far, normed_near, shared = tie(rows_far, normed_near, shared)
+    routes_rows = jnp.pad(routes[0].T.astype(bf16), ((0, 8), (0, WIDTH - TOK)))
+    upstream_rows = jnp.concatenate([cotangent[0], routes_rows], axis=0)
+    rows_far, qkv, shared, upstream_rows, expert_rows = tie(
+        rows_far, qkv, shared, upstream_rows, expert_rows
+    )
+    experts = [experts, along_y(expert_rows)]
     rows_far = both_cores(rows_far)
-    normed_far, q, k, v = project(places[8:], rows_far, head_weights, gain_attn, cosine, sine, qkv)
+    grad_near = [upstream_rows] + [send(upstream_rows, 0, b) for b in (1, 3, 2)]
+    qkv = project(places[8:], rows_far, head_weights, gain_attn, table, (qkv,))
 
     shared = lax.all_to_all(
         jnp.broadcast_to(shared[None], (16, 64, 1152)), "seq", 0, 0, tiled=True
     ).reshape(WIDTH, 1152)
     router_t = shared[:, WIDTH : WIDTH + EXPERTS].T
     gain_ffn = shared[:, WIDTH + EXPERTS].astype(f32)[None]
-    routes_rows = jnp.pad(routes[0].T.astype(bf16), ((0, 8), (0, WIDTH - TOK)))
-    upstream_rows, _ = tie(jnp.concatenate([cotangent[0], routes_rows], axis=0), normed_far)
-    grad_near, grad_across = gather_near(upstream_rows)
-    attended_head, attended_t, lse = attend(q, k, v, begin)
-    attended_head, shared, grad_near, grad_across, pair_before, pair_after = tie(
-        attended_head, shared, grad_near, grad_across, pair_before, pair_after
-    )
-    grad_near, grad_far = both_cores(grad_near), gather_far(grad_across)
-    experts = (
-        expert_pair,
-        pair_before,
-        pair_after,
-        send_w(pair_before[0], 0, 1),
-        send_w(pair_after[1], 0, -1),
-    )
+    attended_head, attended_t, lse = attend(qkv, begin)
+    attended_head, shared, grad_near = tie(attended_head, shared, grad_near)
+    grad_near = jnp.stack(grad_near)
+    grad_far = send(grad_near, 1, 0)
     attended = lax.all_to_all(attended_head, "seq", 0, 0, tiled=True)
     hidden, normed_ffn = hidden_of(attended, shared, rows, gain_ffn)
-    normed_ffn, grad_far, experts = tie(normed_ffn, grad_far, experts)
-    grad_far = both_cores(grad_far)
+    grad_near = (grad_near, swap_cores(grad_near))
 
     ffn_near, ffn_across = gather_near(normed_ffn)
-    ffn_near, _ = tie(ffn_near, ffn_across)
+    ffn_near, _, grad_far = tie(ffn_near, ffn_across, grad_far)
     ffn_near, ffn_far = both_cores(ffn_near), gather_far(ffn_across)
-    own = jnp.stack([seq_index * 2] + w_places)
+    own = jnp.stack([seq_index * 2, own_x])
     near = run_experts(0, own, ffn_near, grad_near, experts, router_t, ())
     near_terms = sum_along_z(*near[:2])
     ffn_far = both_cores(ffn_far)
+    grad_far = (grad_far, swap_cores(grad_far))
     far = run_experts(1, own, ffn_far, grad_far, experts, router_t, near[2:])
     far, near_terms = tie(far, near_terms)
     moved, saved = far[2:4], far[4:]
-    far_terms = sum_along_z(*far[:2])
-    along = jnp.arange(4, dtype=i32)
-    expert_grads = expert_weight_grads((own_y - along) % 4, *saved)
-    moved_other = swap_cores(moved[1])
+    far_other, moved_other = tie(swap_cores(far[1]), moved[1])
+    far_terms = send_along_z(chip_parts(far[0], far_other))
+    expert_grads = expert_weight_grads(*saved)
+    moved_other = swap_cores(moved_other)
     far_terms, expert_grads, moved_other = tie(far_terms, expert_grads, moved_other)
     crossed = send(add_low(*far_terms), 1, 0)
     by_x = [t.reshape(2, 4, TOK, WIDTH) for t in (moved[0], moved_other)]
     moved_parts = [add_low(by_x[0][:, i], by_x[1][:, i]) for i in range(4)]
-    moved_terms = [moved_parts[0]] + [
-        send(moved_parts[i], 0, -b) for i, b in ((1, 1), (2, 3), (3, 2))
-    ]
+    crossed, moved_parts = tie(crossed, moved_parts)
 
     expert_range = jnp.arange(EXPERTS, dtype=i32)
     chosen_here = jnp.any(routes[0].T[None] == expert_range[:, None, None], axis=1).astype(f32)
     hidden_grad, branch_grad, logit_grad, scaled_grad, attended_grad = hidden_back(
         near_terms, crossed, hidden, normed_ffn, chosen_here, router_t, cotangent[0], gain_ffn, shared
     )
-    branch_grad, expert_grads = tie(branch_grad, expert_grads)
+    expert_grads = lax.psum_scatter(
+        expert_grads.reshape(8, 2, 192, 1024),
+        "wshard",
+        axis_index_groups=ALONG_Y,
+        scatter_dimension=0,
+        tiled=True,
+    )
     head_grad = lax.all_to_all(attended_grad, "seq", 0, 0, tiled=True)
     shared_grads = shared_weight_grads(attended, branch_grad, normed_ffn, logit_grad, scaled_grad)
-
-    far_down, far_up = send_w(expert_grads[2, 0], 0, -1), send_w(expert_grads[2, 1], 0, 1)
-    below = jnp.stack([add_low(expert_grads[1, 0], far_down), expert_grads[1, 1]])
-    above = jnp.stack([expert_grads[3, 0], add_low(expert_grads[3, 1], far_up)])
-    head_grad, shared_grads, below, above = tie(head_grad, shared_grads, below, above)
-    expert_terms = (expert_grads[0], send_w(below, 0, -1), send_w(above, 0, 1))
+    head_grad, shared_grads, moved_parts = tie(head_grad, shared_grads, moved_parts)
+    moved_terms = [moved_parts[0]] + [
+        send(moved_parts[i], 0, -b) for i, b in ((1, 1), (2, 3), (3, 2))
+    ]
+
     shared_grads = lax.all_to_all(
         shared_grads.reshape(16, 8, 8, 1152), "wshard", 1, 1, tiled=True
     )
-    grads = attend_back(q, k, v, head_grad, attended_t, lse, begin)
-    grads, moved_terms, expert_terms = tie(grads, moved_terms, expert_terms)
+    projected_grad = attend_back(qkv, head_grad, attended_t, lse, begin, table)
+    far_part = project_back(places[8:], projected_grad, head_weights)
+    far_part, shared_grads, moved_terms = tie(far_part, shared_grads, moved_terms)
+    far_parts = chip_parts(far_part[0], swap_cores(far_part[1]))
+    near_part = project_back(places[:8], projected_grad, head_weights)
+    near_part, expert_grads = tie(near_part, expert_grads)
+    far_parts, projected_grad = tie(far_parts, projected_grad)
+    far_terms = send_along_z(far_parts)
+    near_terms = sum_along_z(*near_part)
     moved_crossed = send(add_low(*[t[1] for t in moved_terms]), 1, 0)
-    *far_part, grad_head = project_back(
-        places[8:], normed_far, grads, head_weights, cosine, sine, ()
-    )
-    far_terms = sum_along_z(*far_part)
-    *near_part, grad_head = project_back(
-        places[:8], normed_near, grads, head_weights, cosine, sine, (grad_head,)
-    )
-    near_part, moved_crossed, shared_grads = tie(near_part, moved_crossed, shared_grads)
-    near_terms = sum_along_z(*near_part)
     shared_grads = jnp.sum(shared_grads.astype(f32), axis=1).astype(bf16)
     shared_grads = lax.all_to_all(shared_grads, "seq", 0, 0, tiled=True)
-    grad_heads = lax.all_to_all(
-        grad_head.astype(bf16).reshape(128, 8, 256), BOTH, 0, 0, tiled=True
-    )
+    grad_head = head_weight_grad(places, rows_near, rows_far, gain_attn, projected_grad)
+    grad_heads = lax.all_to_all(grad_head.reshape(128, 8, 256), BOTH, 0, 0, tiled=True)
     crossed = send(add_low(*far_terms), 1, 0)
-    crossed, grad_heads = tie(crossed, grad_heads)
-    expert_grads = add_low(*expert_terms)
+    crossed, near_terms, grad_heads = tie(crossed, near_terms, grad_heads)
     kept = lax.dynamic_index_in_dim(expert_grads, own_x, 0, keepdims=False)
     sent = lax.dynamic_index_in_dim(expert_grads, 1 - own_x, 0, keepdims=False)
-    expert_grads = kept.astype(f32) + send_w(sent, 1, 0).astype(f32)
+    expert_grads = kept.astype(f32) + swap_x(sent).astype(f32)
     total = lambda terms: sum([t.astype(f32) for t in terms])
     output = (hidden + total([t[0] for t in moved_terms] + [moved_crossed])).astype(bf16)
     normed_grad = total(near_terms + [crossed])

time: 575 us -> 523 us (0.910)
  waiting for transfers between devices: 169 us -> 147 us
  other arithmetic: 70.7 us -> 57 us
  local copies, waits for them, and re-layouts: 34.6 us -> 21.3 us
  between operations: 1.63 us -> 14.8 us
  starting transfers between devices: 119 us -> 106 us
    all_to_all x1, waiting for transfers between devices: 19 us -> 45.9 us  [local(): attended = lax.all_to_all(attended_head, 'seq', 0, 0, tiled=True)]
    ppermute x10 -> x2, waiting for transfers between devices: 27.5 us -> 6.77 us  [swap_x(): return lax.ppermute(rows, 'wshard', [(w, w ^ 1) for w in range(8)])]
    all_to_all x1, waiting for transfers between devices: 28.2 us -> 8.48 us  [local(): head_grad = lax.all_to_all(attended_grad, 'seq', 0, 0, tiled=True)]
    pallas_call x3 -> x4, Pallas kernels: 62.9 us -> 77.7 us  [the longest x1 31 us: attend_back(): pl.pallas_call(attend_back_kernel, grid=(GROUP // BLOCK,), in_specs=[whol...]
    pallas_call x2, Pallas kernels: 23.8 us -> 10.8 us  [project_back(): pl.pallas_call(project_back_kernel, grid_spec=pltpu.PrefetchScalarGridSpe...]
    ppermute x10 -> x2, starting transfers between devices: 11.4 us -> 1.69 us  [swap_x(): return lax.ppermute(rows, 'wshard', [(w, w ^ 1) for w in range(8)])]
    squeeze x3 -> x0, local copies, waits for them, and re-layouts: 6.84 us -> none  [the longest x1 2.68 us: local(): expert_terms = (expert_grads[0], send_w(below, 0, -1), send_w(above, 0, 1))]
    cos x0 -> x1, other arithmetic: none -> 6.39 us  [rotary_table(): cosine, sine = (jnp.cos(angles), jnp.sin(angles))]
  transfers between devices with their start and end apart: 68 -> 60, of which waited for: 22 -> 20; matrix products, arithmetic and copies ran while one was open for 15% -> 14% of each run, Pallas kernels for 29% -> 33%
where the time goes in v6:
time: 523 us; the launch traced here: 513 us
  Pallas kernels  167 us (32%)
  waiting for transfers between devices  147 us (28%)
  starting transfers between devices  106 us (20%)
  other arithmetic  57 us (11%)
  local copies, waits for them, and re-layouts  21.3 us (4%)
  between operations  14.8 us (3%)
    ppermute x36, waiting for transfers between devices, send(): return lax.ppermute(rows, 'seq', shift_perm(a, b))  67.3 us
    ppermute x36, starting transfers between devices, send(): return lax.ppermute(rows, 'seq', shift_perm(a, b))  58.2 us
    pallas_call x2, Pallas kernels, run_experts(): pl.pallas_call(experts_kernel, grid_spec=pltpu.PrefetchScalarGridSpec(num...  48.7 us
    all_to_all x1, waiting for transfers between devices, local(): attended = lax.all_to_all(attended_head, 'seq', 0, 0, tiled=True)  45.9 us
    pallas_call x1, Pallas kernels, attend_back(): pl.pallas_call(attend_back_kernel, grid=(GROUP // BLOCK,), in_specs=[whol...  31 us
    convert_element_type x7, other arithmetic, add_low(): return sum([t.astype(f32) for t in terms]).astype(bf16)  20.9 us
    pallas_call x1, Pallas kernels, attend(): pl.pallas_call(attend_kernel, grid=(GROUP // BLOCK,), in_specs=[whole(GRO...  19.9 us
    pallas_call x2, Pallas kernels, project(): pl.pallas_call(project_kernel, grid_spec=pltpu.PrefetchScalarGridSpec(num...  16.5 us
  transfers between devices with their start and end apart: 60, of which 20 were waited for; matrix products, arithmetic and copies ran while one was open for 14% of the time, Pallas kernels for 33%

profile of v6, /device:TPU:0, one launch (start us, length us, event | category | flops | bytes accessed | tf_op | source)
XLA Modules:
  0.0 512.8 jit_solution(5074070503572778445)
XLA Ops:
  19.8 6.8 %all-to-all-start = ((bf16[128,8,256]{2,1,0:T(8,128)(2,1)}), bf16[128,8,256]{2,1,0:T(8,128)(2,1)S(1)}, u32[]{:S(2)}, u32[]{:S(2)}) async-start(bf16[128,8,256]{2,1,0:T(8,128)(2,1)} %bitcast.8), calls=%async_computation | async-start | bytes 1048576 | tf_op jit(solution)/shard_map/all_to_all | solution.py:749
  28.7 6.4 %multiply_cosine_fusion = (f32[3584,32]{1,0:T(8,128)S(1)}, f32[3584,32]{1,0:T(8,128)S(1)}) fusion(f32[3584]{0:T(1024)S(1)} %get-tuple-element.254, f32[32]{0:T(128)S(1)} %multiply_power_fusion), kind=kLoop, calls=%fused_computation.1 | loop fusion | flops 114688 | bytes 931968 | tf_op jit(solution)/shard_map/cos | solution.py:137
  51.2 5.2 %all-to-all-start.1 = ((bf16[8,8,1152]{2,1,0:T(8,128)(2,1)}), bf16[8,8,1152]{2,1,0:T(8,128)(2,1)S(1)}, u32[]{:S(2)}, u32[]{:S(2)}) async-start(bf16[8,8,1152]{2,1,0:T(8,128)(2,1)} %broadcast_in_dim.96), calls=%async_computation.1 | async-start | bytes 294912 | tf_op jit(solution)/shard_map/all_to_all | solution.py:767
  57.3 8.0 %shard_map.178.refs_0_ = bf16[3584,256]{1,0:T(8,128)(2,1)} custom-call(s32[8]{0:T(128)} %get-tuple-element.257.places, bf16[4,224,1024]{2,1,0:T(8,128)(2,1)} %copy-done.1, bf16[4,224,1024]{2,1,0:T(8,128)(2,1)} %collective-permute-done.7.other.near_other, bf16[1024,256]{1,0:T(8,128)(2,1)} %broadcast_select_fusion.w, f32[1,1024]{1,0:T(1,128)} %bitcast.189, ...), custom_call_target="tpu_custom_call" | custom-call | flops 939524096 | bytes 10485760 | tf_op jit(solution)/shard_map/pallas_call | solution.py:175
  65.2 3.9 all-to-all-done.1
  74.4 5.8 %all-to-all-start.2 = ((bf16[16,64,1152]{2,1,0:T(8,128)(2,1)}), bf16[16,64,1152]{2,1,0:T(8,128)(2,1)S(1)}, u32[]{:S(2)}, u32[]{:S(2)}) async-start(bf16[16,64,1152]{2,1,0:T(8,128)(2,1)} %broadcast_in_dim.97), calls=%async_computation.2 | async-start | bytes 4718592 | tf_op jit(solution)/shard_map/all_to_all | solution.py:780
  86.3 8.6 %shard_map.179.qkv_ref = bf16[3584,256]{1,0:T(8,128)(2,1)} custom-call(s32[8]{0:T(128)} %get-tuple-element.258.places, bf16[4,224,1024]{2,1,0:T(8,128)(2,1)} %pad_maximum_fusion.3.mine.far_mine, bf16[4,224,1024]{2,1,0:T(8,128)(2,1)} %collective-permute-done.9.other.far_other, bf16[1024,256]{1,0:T(8,128)(2,1)} %broadcast_select_fusion.w, ...), custom_call_target="tpu_custom_call" | custom-call | flops 939524096 | bytes 10485760 | tf_op jit(solution)/shard_map/pallas_call | solution.py:175
  94.9 19.9 %shard_map.180 = (bf16[16,64,224]{2,1,0:T(8,128)(2,1)}, f32[64,3584]{1,0:T(8,128)}, f32[1,3584]{1,0:T(1,128)}) custom-call(bf16[3584,256]{1,0:T(8,128)(2,1)} %shard_map.179.qkv_ref, s32[1,3584]{1,0:T(1,128)} %compare_select_fusion.begin_ref), custom_call_target="tpu_custom_call" | custom-call | flops 7247757312 | bytes 4194304 | tf_op jit(solution)/shard_map/pallas_call | solution.py:325
  114.8 5.6 %collective-permute-done.10 = bf16[240,1024]{1,0:T(8,128)(2,1)S(1)} collective-permute-done((bf16[240,1024]{1,0:T(8,128)(2,1)S(1)}, bf16[240,1024]{1,0:T(8,128)(2,1)S(1)}, u32[]{:S(2)}, u32[]{:S(2)}) %collective-permute-start.10) | collective-permute-done | bytes 491552 | tf_op jit(solution)/shard_map/ppermute | solution.py:52
  122.7 8.6 %collective-permute-done.12 = bf16[240,1024]{1,0:T(8,128)(2,1)} collective-permute-done((bf16[240,1024]{1,0:T(8,128)(2,1)S(1)}, bf16[240,1024]{1,0:T(8,128)(2,1)}, u32[]{:S(2)}, u32[]{:S(2)}) %collective-permute-start.12) | collective-permute-done | bytes 491552 | tf_op jit(solution)/shard_map/ppermute | solution.py:52
  137.7 5.5 %all-to-all-start.3 = ((bf16[16,64,224]{2,1,0:T(8,128)(2,1)}), bf16[16,64,224]{2,1,0:T(8,128)(2,1)S(1)}, u32[]{:S(2)}, u32[]{:S(2)}) async-start(bf16[16,64,224]{2,1,0:T(8,128)(2,1)} %get-tuple-element.132), calls=%async_computation.3 | async-start | bytes 1048576 | tf_op jit(solution)/shard_map/all_to_all | solution.py:789
  144.1 45.9 %all-to-all-done.3.att_ref = bf16[16,64,224]{2,1,0:T(8,128)(2,1)S(1)} async-done(((bf16[16,64,224]{2,1,0:T(8,128)(2,1)}), bf16[16,64,224]{2,1,0:T(8,128)(2,1)S(1)}, u32[]{:S(2)}, u32[]{:S(2)}) %all-to-all-start.3) | async-done | bytes 458784 | tf_op jit(solution)/shard_map/all_to_all | solution.py:789
  200.9 6.6 %collective-permute-done.13 = bf16[224,1024]{1,0:T(8,128)(2,1)S(1)} collective-permute-done((bf16[224,1024]{1,0:T(8,128)(2,1)}, bf16[224,1024]{1,0:T(8,128)(2,1)S(1)}, u32[]{:S(2)}, u32[]{:S(2)}) %collective-permute-start.13) | collective-permute-done | bytes 458784 | tf_op jit(solution)/shard_map/ppermute | solution.py:52
  207.5 12.5 %collective-permute-done.18 = bf16[224,1024]{1,0:T(8,128)(2,1)S(1)} collective-permute-done((bf16[224,1024]{1,0:T(8,128)(2,1)}, bf16[224,1024]{1,0:T(8,128)(2,1)S(1)}, u32[]{:S(2)}, u32[]{:S(2)}) %collective-permute-start.18) | collective-permute-done | bytes 458784 | tf_op jit(solution)/shard_map/ppermute | solution.py:52
  228.6 24.2 %shard_map.182 = (bf16[4,256,1024]{2,1,0:T(8,128)(2,1)}, bf16[4,256,1024]{2,1,0:T(8,128)(2,1)}, bf16[8,224,1024]{2,1,0:T(8,128)(2,1)}, bf16[8,224,1024]{2,1,0:T(...) custom-call(s32[2]{0:T(128)} %pad_add_fusion.own_ref, ...), custom_call_target="tpu_custom_call" | custom-call | flops 15032385536 | bytes 25165824 | tf_op jit(solution)/shard_map/pallas_call | solution.py:548
  255.0 4.3 collective-permute-done.25
  267.0 24.4 %shard_map.183 = (bf16[4,256,1024]{2,1,0:T(8,128)(2,1)}, bf16[4,256,1024]{2,1,0:T(8,128)(2,1)}, bf16[8,224,1024]{2,1,0:T(8,128)(2,1)}, bf16[8,224,1024]{2,1,0:T(...) custom-call(s32[2]{0:T(128)} %pad_add_fusion.own_ref, ...), custom_call_target="tpu_custom_call", output_to_operand_aliasing={{2}: (10, {}), {3}: (11, {}), {4}: (12, {}), {5}: (13, {}),... | custom-call | flops 15032385536 | bytes 25165824 | tf_op jit(solution)/shard_map/pallas_call | solution.py:548
  291.6 4.4 collective-permute-done.29
  302.8 15.9 %shard_map.184 = bf16[4,2,2,192,1024]{4,3,2,1,0:T(8,128)(2,1)} custom-call(bf16[2,1152,1024]{2,1,0:T(8,128)(2,1)} %get-tuple-element.170.x_ref, bf16[2,1152,1024]{2,1,0:T(8,128)(2,1)} %get-tuple-element.171.dh_ref, bf16[2,1152,512]{2,1,0:T(8,128)(2,1)} %get-tuple-element.172.act_ref, bf16[2,1152,1024]{2,1,0:T(8,128)(2,1)} %get-tuple-element.173.dy_ref), custom_call_target="tpu_custom_call" | custom-call | flops 8589934592 | bytes 14680064 | tf_op jit(solution)/shard_map/pallas_call | solution.py:604
  318.7 8.9 %collective-permute-done.31 = bf16[256,1024]{1,0:T(8,128)(2,1)S(1)} collective-permute-done((bf16[256,1024]{1,0:T(8,128)(2,1)S(1)}, bf16[256,1024]{1,0:T(8,128)(2,1)S(1)}, u32[]{:S(2)}, u32[]{:S(2)}) %collective-permute-start.31) | collective-permute-done | bytes 524320 | tf_op jit(solution)/shard_map/ppermute | solution.py:52
  329.3 6.1 %fusion.10 = (bf16[2,224,1024]{2,1,0:T(8,128)(2,1)}, bf16[2,224,1024]{2,1,0:T(8,128)(2,1)}, bf16[2,224,1024]{2,1,0:T(8,128)(2,1)}, bf16[2,224,1024]{2,1,0:T(8,128)(2,1)S(1)}) fusion(bf16[2,4,224,1024]{3,2,1,0:T(8,128)(2,1)} %bitcast.50, bf16[2,4,224,1024]{3,2,1,0:T(8,128)(2,1)} %bitcast.171), kind=kLoop, calls=%fused_computation.37 | loop fusion | flops 7340032 | bytes 11010048 | tf_op jit(solution)/shard_map/convert_element_type | solution.py:83
  335.5 7.4 %collective-permute-done.34.crossed = bf16[256,1024]{1,0:T(8,128)(2,1)S(1)} collective-permute-done((bf16[256,1024]{1,0:T(8,128)(2,1)S(1)}, bf16[256,1024]{1,0:T(8,128)(2,1)S(1)}, u32[]{:S(2)}, u32[]{:S(2)}) %collective-permute-start.34) | collective-permute-done | bytes 524320 | tf_op jit(solution)/shard_map/ppermute | solution.py:52
  343.7 5.8 %shard_map.185 = (f32[224,1024]{1,0:T(8,128)}, bf16[224,1024]{1,0:T(8,128)(2,1)}, bf16[32,224]{1,0:T(8,128)(2,1)}, bf16[224,1024]{1,0:T(8,128)(2,1)}, bf16[16,64,224]{2,1,0:T(8,128)(2,1)}) custom-call(bf16[256,1024]{1,0:T(8,128)(2,1)} %get-tuple-element.162.t0, bf16[256,1024]{1,0:T(8,128)(2,1)} %copy-done.13, bf16[256,1024]{1,0:T(8,128)(2,1)} %copy-done.14, ...), custom_call_target="tpu_custom_call" | custom-call | flops 469762048 | bytes 8388608 | tf_op jit(solution)/shard_map/pallas_call | solution.py:675
  356.9 8.5 %all-to-all-done.4.g_ref = bf16[16,64,224]{2,1,0:T(8,128)(2,1)S(1)} async-done(((bf16[16,64,224]{2,1,0:T(8,128)(2,1)}), bf16[16,64,224]{2,1,0:T(8,128)(2,1)S(1)}, u32[]{:S(2)}, u32[]{:S(2)}) %all-to-all-start.4) | async-done | bytes 458784 | tf_op jit(solution)/shard_map/all_to_all | solution.py:826
  369.0 4.8 all-to-all-start.5
  376.4 31.0 %shard_map.187.first.second = bf16[3584,256]{1,0:T(8,128)(2,1)} custom-call(bf16[3584,256]{1,0:T(8,128)(2,1)} %shard_map.179.qkv_ref, bf16[16,64,224]{2,1,0:T(8,128)(2,1)} %copy-done.18, f32[64,3584]{1,0:T(8,128)} %get-tuple-element.191.ot_ref, f32[1,3584]{1,0:T(1,128)} %get-tuple-element.192.lse_ref, s32[1,3584]{1,0:T(1,128)} %compare_select_fusion.begin_ref, ...), custom_call_target="tpu_custom_call" | custom-call | flops 18119393280 | bytes 8388608 | tf_op jit(solution)/shard_map/pallas_call | solution.py:405
  407.4 5.4 %shard_map.188 = (bf16[4,224,1024]{2,1,0:T(8,128)(2,1)}, bf16[4,224,1024]{2,1,0:T(8,128)(2,1)}) custom-call(s32[8]{0:T(128)} %get-tuple-element.258.places, bf16[3584,256]{1,0:T(8,128)(2,1)} %shard_map.187.first.second, bf16[3584,256]{1,0:T(8,128)(2,1)} %shard_map.187.first.second, bf16[1024,256]{1,0:T(8,128)(2,1)} %broadcast_select_fusion.w), custom_call_target="tpu_custom_call" | custom-call | flops 939524096 | bytes 5242880 | tf_op jit(solution)/shard_map/pallas_call | solution.py:202
  418.3 5.5 %shard_map.189 = (bf16[4,224,1024]{2,1,0:T(8,128)(2,1)}, bf16[4,224,1024]{2,1,0:T(8,128)(2,1)}) custom-call(s32[8]{0:T(128)} %get-tuple-element.257.places, bf16[3584,256]{1,0:T(8,128)(2,1)} %shard_map.187.first.second, bf16[3584,256]{1,0:T(8,128)(2,1)} %shard_map.187.first.second, bf16[1024,256]{1,0:T(8,128)(2,1)} %broadcast_select_fusion.w), custom_call_target="tpu_custom_call" | custom-call | flops 939524096 | bytes 5242880 | tf_op jit(solution)/shard_map/pallas_call | solution.py:202
  445.7 10.9 %shard_map.190 = bf16[1024,256]{1,0:T(8,128)(2,1)} custom-call(s32[16]{0:T(128)} %copy-done.27, bf16[4,224,1024]{2,1,0:T(8,128)(2,1)} %copy-done.1, bf16[4,224,1024]{2,1,0:T(8,128)(2,1)} %collective-permute-done.7.other.near_other, bf16[4,224,1024]{2,1,0:T(8,128)(2,1)} %pad_maximum_fusion.3.mine.far_mine, ...), custom_call_target="tpu_custom_call" | custom-call | flops 1879048192 | bytes 10485760 | tf_op jit(solution)/shard_map/pallas_call | solution.py:240
  456.6 8.1 %all-to-all-start.6 = ((bf16[128,8,256]{2,1,0:T(8,128)(2,1)}), bf16[128,8,256]{2,1,0:T(8,128)(2,1)S(1)}, u32[]{:S(2)}, u32[]{:S(2)}) async-start(bf16[128,8,256]{2,1,0:T(8,128)(2,1)} %bitcast.173), calls=%async_computation.7 | async-start | bytes 1048576 | tf_op jit(solution)/shard_map/all_to_all | solution.py:849
  482.1 6.8 %collective-permute-done.48 = bf16[2,192,1024]{2,1,0:T(8,128)(2,1)S(1)} collective-permute-done((bf16[2,192,1024]{2,1,0:T(8,128)(2,1)S(1)}, bf16[2,192,1024]{2,1,0:T(8,128)(2,1)S(1)}, u32[]{:S(2)}, u32[]{:S(2)}) %collective-permute-start.48) | collective-permute-done | bytes 786464 | tf_op jit(solution)/shard_map/ppermute | solution.py:99
  491.1 8.7 %collective-permute-done.43 = bf16[224,1024]{1,0:T(8,128)(2,1)S(1)} collective-permute-done((bf16[224,1024]{1,0:T(8,128)(2,1)}, bf16[224,1024]{1,0:T(8,128)(2,1)S(1)}, u32[]{:S(2)}, u32[]{:S(2)}) %collective-permute-start.43) | collective-permute-done | bytes 458784 | tf_op jit(solution)/shard_map/ppermute | solution.py:52
  (253 shorter events, 157.6 us)
Async XLA Ops:
  7.2 35.1 %collective-permute-start = (bf16[224,1024]{1,0:T(8,128)(2,1)}, bf16[224,1024]{1,0:T(8,128)(2,1)S(1)}, u32[]{:S(2)}, u32[]{:S(2)}) collective-permute-start(bf16[224,1024]{1,0:T(8,128)(2,1)} %bitcast.164), channel_id=1, source_target_pairs={{0,64},{8,72},{16,80},{24,88},{32,96},{40,104},{48,112},{56,120},{... | collective-permute-start | bytes 1376264 | tf_op jit(solution)/shard_map/ppermute | solution.py:52
  10.4 32.0 %collective-permute-start.4 = (bf16[224,1024]{1,0:T(8,128)(2,1)}, bf16[224,1024]{1,0:T(8,128)(2,1)}, u32[]{:S(2)}, u32[]{:S(2)}) collective-permute-start(bf16[224,1024]{1,0:T(8,128)(2,1)} %bitcast.165), channel_id=1, source_target_pairs={{0,16},{8,24},{16,32},{24,40},{32,48},{40,56},{48,0},{56,8},{64,80... | collective-permute-start | bytes 1376264 | tf_op jit(solution)/shard_map/ppermute | solution.py:52
  12.3 30.0 %collective-permute-start.5 = (bf16[224,1024]{1,0:T(8,128)(2,1)}, bf16[224,1024]{1,0:T(8,128)(2,1)}, u32[]{:S(2)}, u32[]{:S(2)}) collective-permute-start(bf16[224,1024]{1,0:T(8,128)(2,1)} %bitcast.166), channel_id=1, source_target_pairs={{0,48},{8,56},{16,0},{24,8},{32,16},{40,24},{48,32},{56,40},{64,11... | collective-permute-start | bytes 1376264 | tf_op jit(solution)/shard_map/ppermute | solution.py:52
  14.4 27.9 %collective-permute-start.6 = (bf16[224,1024]{1,0:T(8,128)(2,1)}, bf16[224,1024]{1,0:T(8,128)(2,1)}, u32[]{:S(2)}, u32[]{:S(2)}) collective-permute-start(bf16[224,1024]{1,0:T(8,128)(2,1)} %bitcast.167), channel_id=1, source_target_pairs={{0,32},{8,40},{16,48},{24,56},{32,0},{40,8},{48,16},{56,24},{64,96... | collective-permute-start | bytes 1376264 | tf_op jit(solution)/shard_map/ppermute | solution.py:52
  26.6 202.0 %all-gather.5.cloned.1.call-start = ((), (), s32[]{:S(2)}) async-start(), calls=%async_computation.10 | async-start | bytes 3932160 | tf_op jit(solution)/shard_map/all_gather | solution.py:759
  74.4 57.0 %all-to-all-start.2 = ((bf16[16,64,1152]{2,1,0:T(8,128)(2,1)}), bf16[16,64,1152]{2,1,0:T(8,128)(2,1)S(1)}, u32[]{:S(2)}, u32[]{:S(2)}) async-start(bf16[16,64,1152]{2,1,0:T(8,128)(2,1)} %broadcast_in_dim.97), calls=%async_computation.2 | async-start | bytes 4718592 | tf_op jit(solution)/shard_map/all_to_all | solution.py:780
  80.2 148.4 %all-gather.7.cloned.1.call-start = ((), (), s32[]{:S(2)}) async-start(), calls=%async_computation.11 | async-start | bytes 3932160 | tf_op jit(solution)/shard_map/all_gather | solution.py:759
  80.8 39.6 %collective-permute-start.10 = (bf16[240,1024]{1,0:T(8,128)(2,1)S(1)}, bf16[240,1024]{1,0:T(8,128)(2,1)S(1)}, u32[]{:S(2)}, u32[]{:S(2)}) collective-permute-start(bf16[240,1024]{1,0:T(8,128)(2,1)S(1)} %fusion.21), channel_id=1, source_target_pairs={{0,16},{8,24},{16,32},{24,40},{32,48},{40,56},{48,0},{56,8},{64,80... | collective-permute-start | bytes 1474568 | tf_op jit(solution)/shard_map/ppermute | solution.py:52
  82.8 40.0 %collective-permute-start.11 = (bf16[240,1024]{1,0:T(8,128)(2,1)S(1)}, bf16[240,1024]{1,0:T(8,128)(2,1)}, u32[]{:S(2)}, u32[]{:S(2)}) collective-permute-start(bf16[240,1024]{1,0:T(8,128)(2,1)S(1)} %fusion.21), channel_id=1, source_target_pairs={{0,48},{8,56},{16,0},{24,8},{32,16},{40,24},{48,32},{56,40},{64,11... | collective-permute-start | bytes 1474568 | tf_op jit(solution)/shard_map/ppermute | solution.py:52
  84.1 47.3 %collective-permute-start.12 = (bf16[240,1024]{1,0:T(8,128)(2,1)S(1)}, bf16[240,1024]{1,0:T(8,128)(2,1)}, u32[]{:S(2)}, u32[]{:S(2)}) collective-permute-start(bf16[240,1024]{1,0:T(8,128)(2,1)S(1)} %fusion.21), channel_id=1, source_target_pairs={{0,32},{8,40},{16,48},{24,56},{32,0},{40,8},{48,16},{56,24},{64,96... | collective-permute-start | bytes 1474568 | tf_op jit(solution)/shard_map/ppermute | solution.py:52
  134.8 85.2 %collective-permute-start.21 = (bf16[4,240,1024]{2,1,0:T(8,128)(2,1)}, bf16[4,240,1024]{2,1,0:T(8,128)(2,1)}, u32[]{:S(2)}, u32[]{:S(2)}) collective-permute-start(bf16[4,240,1024]{2,1,0:T(8,128)(2,1)} %pad_maximum_fusion.g_mine.routes_mine), channel_id=1, source_target_pairs={{0,64},{8,72},{16,80},{24,88},{32,96},{40,104},{48,112},{56,120},{... | collective-permute-start | bytes 5898248 | tf_op jit(solution)/shard_map/ppermute | solution.py:52
  137.7 52.3 %all-to-all-start.3 = ((bf16[16,64,224]{2,1,0:T(8,128)(2,1)}), bf16[16,64,224]{2,1,0:T(8,128)(2,1)S(1)}, u32[]{:S(2)}, u32[]{:S(2)}) async-start(bf16[16,64,224]{2,1,0:T(8,128)(2,1)} %get-tuple-element.132), calls=%async_computation.3 | async-start | bytes 1048576 | tf_op jit(solution)/shard_map/all_to_all | solution.py:789
  143.2 280.5 %reduce-scatter.2.cloned.1.call-start = ((), (), s32[]{:S(2)}) async-start(), calls=%async_computation.9 | async-start | bytes 7864320 | tf_op jit(solution)/shard_map/reduce_scatter | solution.py:819
  224.2 29.3 %collective-permute-start.14 = (bf16[224,1024]{1,0:T(8,128)(2,1)S(1)}, bf16[224,1024]{1,0:T(8,128)(2,1)S(1)}, u32[]{:S(2)}, u32[]{:S(2)}) collective-permute-start(bf16[224,1024]{1,0:T(8,128)(2,1)S(1)} %collective-permute-done.13), channel_id=1, source_target_pairs={{0,16},{8,24},{16,32},{24,40},{32,48},{40,56},{48,0},{56,8},{64,80... | collective-permute-start | bytes 1376264 | tf_op jit(solution)/shard_map/ppermute | solution.py:52
  225.1 28.4 %collective-permute-start.15 = (bf16[224,1024]{1,0:T(8,128)(2,1)S(1)}, bf16[224,1024]{1,0:T(8,128)(2,1)S(1)}, u32[]{:S(2)}, u32[]{:S(2)}) collective-permute-start(bf16[224,1024]{1,0:T(8,128)(2,1)S(1)} %collective-permute-done.13), channel_id=1, source_target_pairs={{0,48},{8,56},{16,0},{24,8},{32,16},{40,24},{48,32},{56,40},{64,11... | collective-permute-start | bytes 1376264 | tf_op jit(solution)/shard_map/ppermute | solution.py:52
  261.3 30.2 %collective-permute-start.26 = (bf16[256,1024]{1,0:T(8,128)(2,1)}, bf16[256,1024]{1,0:T(8,128)(2,1)S(1)}, u32[]{:S(2)}, u32[]{:S(2)}) collective-permute-start(bf16[256,1024]{1,0:T(8,128)(2,1)} %get-tuple-element.239), channel_id=1, source_target_pairs={{0,48},{8,56},{16,0},{24,8},{32,16},{40,24},{48,32},{56,40},{64,11... | collective-permute-start | bytes 1572872 | tf_op jit(solution)/shard_map/ppermute | solution.py:52
  262.4 29.1 %collective-permute-start.27 = (bf16[256,1024]{1,0:T(8,128)(2,1)}, bf16[256,1024]{1,0:T(8,128)(2,1)S(1)}, u32[]{:S(2)}, u32[]{:S(2)}) collective-permute-start(bf16[256,1024]{1,0:T(8,128)(2,1)} %get-tuple-element.238), channel_id=1, source_target_pairs={{0,16},{8,24},{16,32},{24,40},{32,48},{40,56},{48,0},{56,8},{64,80... | collective-permute-start | bytes 1572872 | tf_op jit(solution)/shard_map/ppermute | solution.py:52
  263.3 28.2 %collective-permute-start.28 = (bf16[256,1024]{1,0:T(8,128)(2,1)S(1)}, bf16[256,1024]{1,0:T(8,128)(2,1)S(1)}, u32[]{:S(2)}, u32[]{:S(2)}) collective-permute-start(bf16[256,1024]{1,0:T(8,128)(2,1)S(1)} %get-tuple-element.237), channel_id=1, source_target_pairs={{0,32},{8,40},{16,48},{24,56},{32,0},{40,8},{48,16},{56,24},{64,96... | collective-permute-start | bytes 1572872 | tf_op jit(solution)/shard_map/ppermute | solution.py:52
  296.0 31.6 %collective-permute-start.33 = (bf16[8,224,1024]{2,1,0:T(8,128)(2,1)}, bf16[8,224,1024]{2,1,0:T(8,128)(2,1)}, u32[]{:S(2)}, u32[]{:S(2)}) collective-permute-start(bf16[8,224,1024]{2,1,0:T(8,128)(2,1)} %get-tuple-element.174), channel_id=1, source_target_pairs={{0,8},{8,0},{16,24},{24,16},{32,40},{40,32},{48,56},{56,48},{64,72... | collective-permute-start | bytes 11010056 | tf_op jit(solution)/shard_map/ppermute | solution.py:56
  301.3 26.4 %collective-permute-start.31 = (bf16[256,1024]{1,0:T(8,128)(2,1)S(1)}, bf16[256,1024]{1,0:T(8,128)(2,1)S(1)}, u32[]{:S(2)}, u32[]{:S(2)}) collective-permute-start(bf16[256,1024]{1,0:T(8,128)(2,1)S(1)} %get-tuple-element.234), channel_id=1, source_target_pairs={{0,16},{8,24},{16,32},{24,40},{32,48},{40,56},{48,0},{56,8},{64,80... | collective-permute-start | bytes 1572872 | tf_op jit(solution)/shard_map/ppermute | solution.py:52
  301.6 26.1 %collective-permute-start.32 = (bf16[256,1024]{1,0:T(8,128)(2,1)S(1)}, bf16[256,1024]{1,0:T(8,128)(2,1)S(1)}, u32[]{:S(2)}, u32[]{:S(2)}) collective-permute-start(bf16[256,1024]{1,0:T(8,128)(2,1)S(1)} %get-tuple-element.233), channel_id=1, source_target_pairs={{0,32},{8,40},{16,48},{24,56},{32,0},{40,8},{48,16},{56,24},{64,96... | collective-permute-start | bytes 1572872 | tf_op jit(solution)/shard_map/ppermute | solution.py:52
  369.0 49.0 %all-to-all-start.5 = ((bf16[16,8,8,1152]{3,2,0,1:T(8,128)(2,1)}), bf16[16,8,8,1152]{3,2,0,1:T(8,128)(2,1)S(1)}, u32[]{:S(2)}, u32[]{:S(2)}) async-start(bf16[16,8,8,1152]{3,2,0,1:T(8,128)(2,1)} %copy.161), calls=%async_computation.5 | async-start | bytes 4718592 | tf_op jit(solution)/shard_map/all_to_all | solution.py:833
  373.9 40.8 %collective-permute-start.35 = (bf16[2,224,1024]{2,1,0:T(8,128)(2,1)}, bf16[2,224,1024]{2,1,0:T(8,128)(2,1)}, u32[]{:S(2)}, u32[]{:S(2)}) collective-permute-start(bf16[2,224,1024]{2,1,0:T(8,128)(2,1)} %get-tuple-element.197), channel_id=1, source_target_pairs={{0,48},{8,56},{16,0},{24,8},{32,16},{40,24},{48,32},{56,40},{64,11... | collective-permute-start | bytes 2752520 | tf_op jit(solution)/shard_map/ppermute | solution.py:52
  374.9 43.1 %collective-permute-start.36 = (bf16[2,224,1024]{2,1,0:T(8,128)(2,1)}, bf16[2,224,1024]{2,1,0:T(8,128)(2,1)}, u32[]{:S(2)}, u32[]{:S(2)}) collective-permute-start(bf16[2,224,1024]{2,1,0:T(8,128)(2,1)} %get-tuple-element.198), channel_id=1, source_target_pairs={{0,16},{8,24},{16,32},{24,40},{32,48},{40,56},{48,0},{56,8},{64,80... | collective-permute-start | bytes 2752520 | tf_op jit(solution)/shard_map/ppermute | solution.py:52
  375.9 42.1 %collective-permute-start.37 = (bf16[2,224,1024]{2,1,0:T(8,128)(2,1)}, bf16[2,224,1024]{2,1,0:T(8,128)(2,1)}, u32[]{:S(2)}, u32[]{:S(2)}) collective-permute-start(bf16[2,224,1024]{2,1,0:T(8,128)(2,1)} %get-tuple-element.199), channel_id=1, source_target_pairs={{0,32},{8,40},{16,48},{24,56},{32,0},{40,8},{48,16},{56,24},{64,96... | collective-permute-start | bytes 2752520 | tf_op jit(solution)/shard_map/ppermute | solution.py:52
  423.7 47.2 %collective-permute-start.44 = (bf16[4,224,1024]{2,1,0:T(8,128)(2,1)}, bf16[4,224,1024]{2,1,0:T(8,128)(2,1)}, u32[]{:S(2)}, u32[]{:S(2)}) collective-permute-start(bf16[4,224,1024]{2,1,0:T(8,128)(2,1)} %get-tuple-element.215), channel_id=1, source_target_pairs={{0,8},{8,0},{16,24},{24,16},{32,40},{40,32},{48,56},{56,48},{64,72... | collective-permute-start | bytes 5505032 | tf_op jit(solution)/shard_map/ppermute | solution.py:56
  426.6 50.8 %collective-permute-start.38 = (bf16[224,1024]{1,0:T(8,128)(2,1)}, bf16[224,1024]{1,0:T(8,128)(2,1)}, u32[]{:S(2)}, u32[]{:S(2)}) collective-permute-start(bf16[224,1024]{1,0:T(8,128)(2,1)} %fusion.22), channel_id=1, source_target_pairs={{0,64},{8,72},{16,80},{24,88},{32,96},{40,104},{48,112},{56,120},{... | collective-permute-start | bytes 1376264 | tf_op jit(solution)/shard_map/ppermute | solution.py:52
  436.3 28.5 %collective-permute-start.40 = (bf16[224,1024]{1,0:T(8,128)(2,1)}, bf16[224,1024]{1,0:T(8,128)(2,1)}, u32[]{:S(2)}, u32[]{:S(2)}) collective-permute-start(bf16[224,1024]{1,0:T(8,128)(2,1)} %get-tuple-element.208), channel_id=1, source_target_pairs={{0,48},{8,56},{16,0},{24,8},{32,16},{40,24},{48,32},{56,40},{64,11... | collective-permute-start | bytes 1376264 | tf_op jit(solution)/shard_map/ppermute | solution.py:52
  439.4 26.4 %collective-permute-start.41 = (bf16[224,1024]{1,0:T(8,128)(2,1)}, bf16[224,1024]{1,0:T(8,128)(2,1)}, u32[]{:S(2)}, u32[]{:S(2)}) collective-permute-start(bf16[224,1024]{1,0:T(8,128)(2,1)} %get-tuple-element.209), channel_id=1, source_target_pairs={{0,16},{8,24},{16,32},{24,40},{32,48},{40,56},{48,0},{56,8},{64,80... | collective-permute-start | bytes 1376264 | tf_op jit(solution)/shard_map/ppermute | solution.py:52
  439.4 26.4 %collective-permute-start.42 = (bf16[224,1024]{1,0:T(8,128)(2,1)}, bf16[224,1024]{1,0:T(8,128)(2,1)}, u32[]{:S(2)}, u32[]{:S(2)}) collective-permute-start(bf16[224,1024]{1,0:T(8,128)(2,1)} %get-tuple-element.210), channel_id=1, source_target_pairs={{0,32},{8,40},{16,48},{24,56},{32,0},{40,8},{48,16},{56,24},{64,96... | collective-permute-start | bytes 1376264 | tf_op jit(solution)/shard_map/ppermute | solution.py:52
  456.6 34.5 %all-to-all-start.6 = ((bf16[128,8,256]{2,1,0:T(8,128)(2,1)}), bf16[128,8,256]{2,1,0:T(8,128)(2,1)S(1)}, u32[]{:S(2)}, u32[]{:S(2)}) async-start(bf16[128,8,256]{2,1,0:T(8,128)(2,1)} %bitcast.173), calls=%async_computation.7 | async-start | bytes 1048576 | tf_op jit(solution)/shard_map/all_to_all | solution.py:849
  468.2 31.6 %collective-permute-start.43 = (bf16[224,1024]{1,0:T(8,128)(2,1)}, bf16[224,1024]{1,0:T(8,128)(2,1)S(1)}, u32[]{:S(2)}, u32[]{:S(2)}) collective-permute-start(bf16[224,1024]{1,0:T(8,128)(2,1)} %add_convert_fusion.17), channel_id=1, source_target_pairs={{0,64},{8,72},{16,80},{24,88},{32,96},{40,104},{48,112},{56,120},{... | collective-permute-start | bytes 1376264 | tf_op jit(solution)/shard_map/ppermute | solution.py:52
  (61 other events, 780.9 us)
Sparse Core Ops, SparseCore 0:
  29.1 42.2 all-gather.4
  86.4 39.6 all-gather.6
  327.8 82.0 reduce-scatter.1

commit v7 on v6

--- a/solution.py
+++ b/solution.py
@@ -132,10 +132,9 @@
 
 def rotary_table(position):
     half_dim = HEAD_DIM // 2
-    inverse = rope_base ** (-(jnp.arange(half_dim, dtype=f32) * 2.0) / HEAD_DIM)
-    angles = position[:, None] * inverse[None, :]
-    cosine, sine = jnp.cos(angles), jnp.sin(angles)
-    return jnp.concatenate([cosine, cosine, sine, sine], axis=-1)
+    inverse = rope_base ** (-((jnp.arange(2 * HEAD_DIM) % half_dim).astype(f32) * 2.0) / HEAD_DIM)
+    back = jnp.where(jnp.arange(2 * HEAD_DIM) < HEAD_DIM, 0.0, 0.5 * jnp.pi).astype(f32)
+    return jnp.cos(position[:, None] * inverse[None, :] - back[None, :])
 
 
 def turn(values):
@@ -689,21 +688,25 @@
 
 
 def shared_grads_kernel(att_ref, branch_ref, normed_ref, logit_ref, scaled_ref, out_ref):
-    att = att_ref[...].reshape(WIDTH, TOK)
-    out_ref[:, :WIDTH] = jnp.dot(att, branch_ref[...], preferred_element_type=f32).astype(bf16)
     over_tokens = (((0,), (1,)), ((), ()))
     logit = jnp.concatenate([logit_ref[...], jnp.zeros((96, TOK), bf16)], axis=0)
     ones = (lax.broadcasted_iota(i32, (128, TOK), 0) == EXPERTS).astype(f32).astype(bf16)
-    out_ref[:, WIDTH:] = (
+    att = att_ref[...].reshape(WIDTH, TOK)
+    grads = [
+        jnp.dot(att, branch_ref[...], preferred_element_type=f32),
         lax.dot_general(normed_ref[...], logit, over_tokens, preferred_element_type=f32)
-        + lax.dot_general(scaled_ref[...], ones, over_tokens, preferred_element_type=f32)
-    ).astype(bf16)
+        + lax.dot_general(scaled_ref[...], ones, over_tokens, preferred_element_type=f32),
+    ]
+    for w in range(8):
+        for part, at in zip(grads, (slice(0, WIDTH), slice(WIDTH, None))):
+            rows = [part[s * 64 + w * 8 : s * 64 + w * 8 + 8] for s in range(16)]
+            out_ref[w, :, at] = jnp.concatenate(rows, axis=0).astype(bf16)
 
 
 def shared_weight_grads(att, branch, normed, logit_grad, scaled):
     return pl.pallas_call(
         shared_grads_kernel,
-        out_shape=jax.ShapeDtypeStruct((WIDTH, 1152), bf16),
+        out_shape=jax.ShapeDtypeStruct((8, 128, 1152), bf16),
         compiler_params=pltpu.CompilerParams(vmem_limit_bytes=VMEM_LIMIT),
         cost_estimate=pl.CostEstimate(
             flops=2 * TOK * WIDTH * 1280, bytes_accessed=5 << 20, transcendentals=0
@@ -763,30 +766,26 @@
     shared = jnp.concatenate(
         [w_out, w_router, norm_ffn[:, None], jnp.zeros((8, 95), bf16)], axis=1
     )
-    shared, _ = tie(shared, head_weights)
+    shared, qkv = tie(shared, qkv)
     shared = lax.all_to_all(
-        jnp.broadcast_to(shared[None], (8, 8, 1152)), "wshard", 0, 0, tiled=True
-    ).reshape(64, 1152)
+        jnp.broadcast_to(shared[None], (128, 8, 1152)), BOTH, 0, 0, tiled=True
+    ).reshape(WIDTH, 1152)
     routes_rows = jnp.pad(routes[0].T.astype(bf16), ((0, 8), (0, WIDTH - TOK)))
     upstream_rows = jnp.concatenate([cotangent[0], routes_rows], axis=0)
-    rows_far, qkv, shared, upstream_rows, expert_rows = tie(
-        rows_far, qkv, shared, upstream_rows, expert_rows
-    )
+    rows_far, qkv, upstream_rows, expert_rows = tie(rows_far, qkv, upstream_rows, expert_rows)
     experts = [experts, along_y(expert_rows)]
     rows_far = both_cores(rows_far)
     grad_near = [upstream_rows] + [send(upstream_rows, 0, b) for b in (1, 3, 2)]
     qkv = project(places[8:], rows_far, head_weights, gain_attn, table, (qkv,))
 
-    shared = lax.all_to_all(
-        jnp.broadcast_to(shared[None], (16, 64, 1152)), "seq", 0, 0, tiled=True
-    ).reshape(WIDTH, 1152)
     router_t = shared[:, WIDTH : WIDTH + EXPERTS].T
     gain_ffn = shared[:, WIDTH + EXPERTS].astype(f32)[None]
     attended_head, attended_t, lse = attend(qkv, begin)
-    attended_head, shared, grad_near = tie(attended_head, shared, grad_near)
+    attended_head, shared = tie(attended_head, shared)
+    attended = lax.all_to_all(attended_head, "seq", 0, 0, tiled=True)
+    attended, grad_near = tie(attended, grad_near)
     grad_near = jnp.stack(grad_near)
     grad_far = send(grad_near, 1, 0)
-    attended = lax.all_to_all(attended_head, "seq", 0, 0, tiled=True)
     hidden, normed_ffn = hidden_of(attended, shared, rows, gain_ffn)
     grad_near = (grad_near, swap_cores(grad_near))
 
@@ -830,20 +829,22 @@
         send(moved_parts[i], 0, -b) for i, b in ((1, 1), (2, 3), (3, 2))
     ]
 
-    shared_grads = lax.all_to_all(
-        shared_grads.reshape(16, 8, 8, 1152), "wshard", 1, 1, tiled=True
-    )
+    shared_grads = lax.all_to_all(shared_grads, "wshard", 0, 0, tiled=True)
     projected_grad = attend_back(qkv, head_grad, attended_t, lse, begin, table)
     far_part = project_back(places[8:], projected_grad, head_weights)
     far_part, shared_grads, moved_terms = tie(far_part, shared_grads, moved_terms)
     far_parts = chip_parts(far_part[0], swap_cores(far_part[1]))
     near_part = project_back(places[:8], projected_grad, head_weights)
     near_part, expert_grads = tie(near_part, expert_grads)
-    far_parts, projected_grad = tie(far_parts, projected_grad)
+    far_parts, projected_grad, shared_grads, moved_terms, expert_grads = tie(
+        far_parts, projected_grad, shared_grads, moved_terms, expert_grads
+    )
     far_terms = send_along_z(far_parts)
-    near_terms = sum_along_z(*near_part)
+    near_parts = chip_parts(near_part[0], swap_cores(near_part[1]))
+    near_parts, projected_grad = tie(near_parts, projected_grad)
+    near_terms = send_along_z(near_parts)
     moved_crossed = send(add_low(*[t[1] for t in moved_terms]), 1, 0)
-    shared_grads = jnp.sum(shared_grads.astype(f32), axis=1).astype(bf16)
+    shared_grads = jnp.sum(shared_grads.astype(f32), axis=0).astype(bf16).reshape(16, 8, 1152)
     shared_grads = lax.all_to_all(shared_grads, "seq", 0, 0, tiled=True)
     grad_head = head_weight_grad(places, rows_near, rows_far, gain_attn, projected_grad)
     grad_heads = lax.all_to_all(grad_head.reshape(128, 8, 256), BOTH, 0, 0, tiled=True)

time: 523 us -> 514 us (0.983)
    all_to_all x1, waiting for transfers between devices: 45.9 us -> 2.2 us  [local(): attended = lax.all_to_all(attended_head, 'seq', 0, 0, tiled=True)]
    ppermute x36, waiting for transfers between devices: 67.3 us -> 100 us  [send(): return lax.ppermute(rows, 'seq', shift_perm(a, b))]
    all_to_all x1, waiting for transfers between devices: 1.99 us -> 15.6 us  [local(): shared_grads = lax.all_to_all(shared_grads, 'seq', 0, 0, tiled=True)]
    all_to_all x3 -> x2, starting transfers between devices: 15.8 us -> 13.7 us  [the longest x1 9 us: local(): lax.all_to_all(jnp.broadcast_to(shared[None], (128, 8, 1152)), BOTH, 0, 0...]
  transfers between devices with their start and end apart: 60 -> 59, of which waited for: 20 -> 18; matrix products, arithmetic and copies ran while one was open for 14% -> 13% of each run, Pallas kernels for 33% -> 33%
where the time goes in v7:
time: 514 us; the launch traced here: 506 us
  Pallas kernels  167 us (32%)
  waiting for transfers between devices  146 us (28%)
  starting transfers between devices  102 us (20%)
  other arithmetic  56.5 us (11%)
  local copies, waits for them, and re-layouts  18.7 us (4%)
  between operations  14.8 us (3%)
    ppermute x36, waiting for transfers between devices, send(): return lax.ppermute(rows, 'seq', shift_perm(a, b))  100 us
    ppermute x36, starting transfers between devices, send(): return lax.ppermute(rows, 'seq', shift_perm(a, b))  54.6 us
    pallas_call x2, Pallas kernels, run_experts(): pl.pallas_call(experts_kernel, grid_spec=pltpu.PrefetchScalarGridSpec(num...  48.4 us
    pallas_call x1, Pallas kernels, attend_back(): pl.pallas_call(attend_back_kernel, grid=(GROUP // BLOCK,), in_specs=[whol...  31 us
    convert_element_type x7, other arithmetic, add_low(): return sum([t.astype(f32) for t in terms]).astype(bf16)  21.2 us
    pallas_call x1, Pallas kernels, attend(): pl.pallas_call(attend_kernel, grid=(GROUP // BLOCK,), in_specs=[whole(GRO...  19.9 us
    pallas_call x2, Pallas kernels, project(): pl.pallas_call(project_kernel, grid_spec=pltpu.PrefetchScalarGridSpec(num...  16.5 us
    pallas_call x1, Pallas kernels, expert_weight_grads(): pl.pallas_call(expert_grads_kernel, grid=(2, 4), in_specs=[pl.BlockSpec((...  15.9 us
  transfers between devices with their start and end apart: 59, of which 18 were waited for; matrix products, arithmetic and copies ran while one was open for 13% of the time, Pallas kernels for 33%

profile of v7, /device:TPU:0, one launch (start us, length us, event | category | flops | bytes accessed | tf_op | source)
XLA Modules:
  0.0 505.6 jit_solution(15223672142446327725)
XLA Ops:
  19.8 6.8 %all-to-all-start = ((bf16[128,8,256]{2,1,0:T(8,128)(2,1)}), bf16[128,8,256]{2,1,0:T(8,128)(2,1)S(1)}, u32[]{:S(2)}, u32[]{:S(2)}) async-start(bf16[128,8,256]{2,1,0:T(8,128)(2,1)} %bitcast.9), calls=%async_computation | async-start | bytes 1048576 | tf_op jit(solution)/shard_map/all_to_all | solution.py:752
  28.7 7.7 %subtract_cosine_fusion.table = f32[3584,128]{1,0:T(8,128)} fusion(f32[128]{0:T(128)S(1)} %get-tuple-element.281, f32[128]{0:T(128)S(1)} %get-tuple-element.282, f32[3584]{0:T(1024)S(1)} %get-tuple-element.276), kind=kLoop, calls=%fused_computation.9 | loop fusion | flops 917504 | bytes 1850368 | tf_op jit(solution)/shard_map/cos | solution.py:137
  36.4 5.1 %all-to-all-done = bf16[128,8,256]{2,1,0:T(8,128)(2,1)S(1)} async-done(((bf16[128,8,256]{2,1,0:T(8,128)(2,1)}), bf16[128,8,256]{2,1,0:T(8,128)(2,1)S(1)}, u32[]{:S(2)}, u32[]{:S(2)}) %all-to-all-start) | async-done | bytes 524320 | tf_op jit(solution)/shard_map/all_to_all | solution.py:752
  51.5 8.0 %shard_map.178.refs_0_ = bf16[3584,256]{1,0:T(8,128)(2,1)} custom-call(s32[8]{0:T(128)} %get-tuple-element.279.places, bf16[4,224,1024]{2,1,0:T(8,128)(2,1)} %copy-done.1, bf16[4,224,1024]{2,1,0:T(8,128)(2,1)} %collective-permute-done.7.other.near_other, bf16[1024,256]{1,0:T(8,128)(2,1)} %broadcast_select_fusion.w, f32[1,1024]{1,0:T(1,128)} %bitcast.188, ...), custom_call_target="tpu_custom_call" | custom-call | flops 939524096 | bytes 10485760 | tf_op jit(solution)/shard_map/pallas_call | solution.py:174
  59.4 6.0 %collective-permute-done.8 = bf16[2,192,1024]{2,1,0:T(8,128)(2,1)} collective-permute-done((bf16[2,192,1024]{2,1,0:T(8,128)(2,1)}, bf16[2,192,1024]{2,1,0:T(8,128)(2,1)}, u32[]{:S(2)}, u32[]{:S(2)}) %collective-permute-start.8) | collective-permute-done | bytes 786464 | tf_op jit(solution)/shard_map/ppermute | solution.py:99
  74.3 9.0 %all-to-all-start.1 = ((bf16[128,8,1152]{2,1,0:T(8,128)(2,1)}), bf16[128,8,1152]{2,1,0:T(8,128)(2,1)S(1)}, u32[]{:S(2)}, u32[]{:S(2)}) async-start(bf16[128,8,1152]{2,1,0:T(8,128)(2,1)} %broadcast_in_dim.101), calls=%async_computation.1 | async-start | bytes 4718592 | tf_op jit(solution)/shard_map/all_to_all | solution.py:770
  89.1 8.6 %shard_map.179.qkv_ref = bf16[3584,256]{1,0:T(8,128)(2,1)} custom-call(s32[8]{0:T(128)} %get-tuple-element.280.places, bf16[4,224,1024]{2,1,0:T(8,128)(2,1)} %pad_maximum_fusion.2.mine.far_mine, bf16[4,224,1024]{2,1,0:T(8,128)(2,1)} %collective-permute-done.9.other.far_other, bf16[1024,256]{1,0:T(8,128)(2,1)} %broadcast_select_fusion.w, ...), custom_call_target="tpu_custom_call" | custom-call | flops 939524096 | bytes 10485760 | tf_op jit(solution)/shard_map/pallas_call | solution.py:174
  97.6 19.9 %shard_map.180 = (bf16[16,64,224]{2,1,0:T(8,128)(2,1)}, f32[64,3584]{1,0:T(8,128)}, f32[1,3584]{1,0:T(1,128)}) custom-call(bf16[3584,256]{1,0:T(8,128)(2,1)} %shard_map.179.qkv_ref, s32[1,3584]{1,0:T(1,128)} %compare_select_fusion.begin_ref), custom_call_target="tpu_custom_call" | custom-call | flops 7247757312 | bytes 4194304 | tf_op jit(solution)/shard_map/pallas_call | solution.py:324
  117.6 5.1 %all-to-all-start.2 = ((bf16[16,64,224]{2,1,0:T(8,128)(2,1)}), bf16[16,64,224]{2,1,0:T(8,128)(2,1)S(1)}, u32[]{:S(2)}, u32[]{:S(2)}) async-start(bf16[16,64,224]{2,1,0:T(8,128)(2,1)} %get-tuple-element.143), calls=%async_computation.2 | async-start | bytes 1048576 | tf_op jit(solution)/shard_map/all_to_all | solution.py:785
  122.9 13.4 %collective-permute-done.12 = bf16[240,1024]{1,0:T(8,128)(2,1)} collective-permute-done((bf16[240,1024]{1,0:T(8,128)(2,1)S(1)}, bf16[240,1024]{1,0:T(8,128)(2,1)}, u32[]{:S(2)}, u32[]{:S(2)}) %collective-permute-start.12) | collective-permute-done | bytes 491552 | tf_op jit(solution)/shard_map/ppermute | solution.py:52
  153.2 44.8 %collective-permute-done.13 = bf16[224,1024]{1,0:T(8,128)(2,1)S(1)} collective-permute-done((bf16[224,1024]{1,0:T(8,128)(2,1)}, bf16[224,1024]{1,0:T(8,128)(2,1)S(1)}, u32[]{:S(2)}, u32[]{:S(2)}) %collective-permute-start.13) | collective-permute-done | bytes 458784 | tf_op jit(solution)/shard_map/ppermute | solution.py:52
  206.2 24.2 %shard_map.182 = (bf16[4,256,1024]{2,1,0:T(8,128)(2,1)}, bf16[4,256,1024]{2,1,0:T(8,128)(2,1)}, bf16[8,224,1024]{2,1,0:T(8,128)(2,1)}, bf16[8,224,1024]{2,1,0:T(...) custom-call(s32[2]{0:T(128)} %pad_add_fusion.own_ref, ...), custom_call_target="tpu_custom_call" | custom-call | flops 15032385536 | bytes 25165824 | tf_op jit(solution)/shard_map/pallas_call | solution.py:547
  232.6 4.3 collective-permute-done.25
  245.3 24.2 %shard_map.183 = (bf16[4,256,1024]{2,1,0:T(8,128)(2,1)}, bf16[4,256,1024]{2,1,0:T(8,128)(2,1)}, bf16[8,224,1024]{2,1,0:T(8,128)(2,1)}, bf16[8,224,1024]{2,1,0:T(...) custom-call(s32[2]{0:T(128)} %pad_add_fusion.own_ref, ...), custom_call_target="tpu_custom_call", output_to_operand_aliasing={{2}: (10, {}), {3}: (11, {}), {4}: (12, {}), {5}: (13, {}),... | custom-call | flops 15032385536 | bytes 25165824 | tf_op jit(solution)/shard_map/pallas_call | solution.py:547
  269.7 4.4 collective-permute-done.29
  280.6 15.9 %shard_map.184 = bf16[4,2,2,192,1024]{4,3,2,1,0:T(8,128)(2,1)} custom-call(bf16[2,1152,1024]{2,1,0:T(8,128)(2,1)} %get-tuple-element.183.x_ref, bf16[2,1152,1024]{2,1,0:T(8,128)(2,1)} %get-tuple-element.184.dh_ref, bf16[2,1152,512]{2,1,0:T(8,128)(2,1)} %get-tuple-element.185.act_ref, bf16[2,1152,1024]{2,1,0:T(8,128)(2,1)} %get-tuple-element.186.dy_ref), custom_call_target="tpu_custom_call" | custom-call | flops 8589934592 | bytes 14680064 | tf_op jit(solution)/shard_map/pallas_call | solution.py:603
  296.4 8.1 %collective-permute-done.31 = bf16[256,1024]{1,0:T(8,128)(2,1)S(1)} collective-permute-done((bf16[256,1024]{1,0:T(8,128)(2,1)S(1)}, bf16[256,1024]{1,0:T(8,128)(2,1)S(1)}, u32[]{:S(2)}, u32[]{:S(2)}) %collective-permute-start.31) | collective-permute-done | bytes 524320 | tf_op jit(solution)/shard_map/ppermute | solution.py:52
  309.0 6.2 %fusion.10 = (bf16[2,224,1024]{2,1,0:T(8,128)(2,1)}, bf16[2,224,1024]{2,1,0:T(8,128)(2,1)}, bf16[2,224,1024]{2,1,0:T(8,128)(2,1)}, bf16[2,224,1024]{2,1,0:T(8,128)(2,1)S(1)}) fusion(bf16[2,4,224,1024]{3,2,1,0:T(8,128)(2,1)} %bitcast.49, bf16[2,4,224,1024]{3,2,1,0:T(8,128)(2,1)} %bitcast.169), kind=kLoop, calls=%fused_computation.35 | loop fusion | flops 7340032 | bytes 11010048 | tf_op jit(solution)/shard_map/convert_element_type | solution.py:83
  315.2 4.4 collective-permute-done.34.crossed
  320.4 5.9 %shard_map.185 = (f32[224,1024]{1,0:T(8,128)}, bf16[224,1024]{1,0:T(8,128)(2,1)}, bf16[32,224]{1,0:T(8,128)(2,1)}, bf16[224,1024]{1,0:T(8,128)(2,1)}, bf16[16,64,224]{2,1,0:T(8,128)(2,1)}) custom-call(bf16[256,1024]{1,0:T(8,128)(2,1)} %get-tuple-element.175.t0, bf16[256,1024]{1,0:T(8,128)(2,1)} %copy-done.18, bf16[256,1024]{1,0:T(8,128)(2,1)} %copy-done.19, ...), custom_call_target="tpu_custom_call" | custom-call | flops 469762048 | bytes 8388608 | tf_op jit(solution)/shard_map/pallas_call | solution.py:674
  326.2 5.7 %all-to-all-start.3 = ((bf16[16,64,224]{2,1,0:T(8,128)(2,1)}), bf16[16,64,224]{2,1,0:T(8,128)(2,1)S(1)}, u32[]{:S(2)}, u32[]{:S(2)}) async-start(bf16[16,64,224]{2,1,0:T(8,128)(2,1)} %get-tuple-element.195), calls=%async_computation.3 | async-start | bytes 1048576 | tf_op jit(solution)/shard_map/all_to_all | solution.py:825
  335.9 8.4 %all-to-all-done.3.g_ref = bf16[16,64,224]{2,1,0:T(8,128)(2,1)S(1)} async-done(((bf16[16,64,224]{2,1,0:T(8,128)(2,1)}), bf16[16,64,224]{2,1,0:T(8,128)(2,1)S(1)}, u32[]{:S(2)}, u32[]{:S(2)}) %all-to-all-start.3) | async-done | bytes 458784 | tf_op jit(solution)/shard_map/all_to_all | solution.py:825
  345.1 4.7 all-to-all-start.4
  352.3 31.0 %shard_map.187.first.second = bf16[3584,256]{1,0:T(8,128)(2,1)} custom-call(bf16[3584,256]{1,0:T(8,128)(2,1)} %shard_map.179.qkv_ref, bf16[16,64,224]{2,1,0:T(8,128)(2,1)} %copy-done.23, f32[64,3584]{1,0:T(8,128)} %get-tuple-element.204.ot_ref, f32[1,3584]{1,0:T(1,128)} %get-tuple-element.205.lse_ref, s32[1,3584]{1,0:T(1,128)} %compare_select_fusion.begin_ref, ...), custom_call_target="tpu_custom_call" | custom-call | flops 18119393280 | bytes 8388608 | tf_op jit(solution)/shard_map/pallas_call | solution.py:404
  383.3 5.4 %shard_map.188 = (bf16[4,224,1024]{2,1,0:T(8,128)(2,1)}, bf16[4,224,1024]{2,1,0:T(8,128)(2,1)}) custom-call(s32[8]{0:T(128)} %get-tuple-element.280.places, bf16[3584,256]{1,0:T(8,128)(2,1)} %shard_map.187.first.second, bf16[3584,256]{1,0:T(8,128)(2,1)} %shard_map.187.first.second, bf16[1024,256]{1,0:T(8,128)(2,1)} %broadcast_select_fusion.w), custom_call_target="tpu_custom_call" | custom-call | flops 939524096 | bytes 5242880 | tf_op jit(solution)/shard_map/pallas_call | solution.py:201
  394.2 5.5 %shard_map.189 = (bf16[4,224,1024]{2,1,0:T(8,128)(2,1)}, bf16[4,224,1024]{2,1,0:T(8,128)(2,1)}) custom-call(s32[8]{0:T(128)} %get-tuple-element.279.places, bf16[3584,256]{1,0:T(8,128)(2,1)} %shard_map.187.first.second, bf16[3584,256]{1,0:T(8,128)(2,1)} %shard_map.187.first.second, bf16[1024,256]{1,0:T(8,128)(2,1)} %broadcast_select_fusion.w), custom_call_target="tpu_custom_call" | custom-call | flops 939524096 | bytes 5242880 | tf_op jit(solution)/shard_map/pallas_call | solution.py:201
  400.2 4.0 fusion.25
  410.5 4.8 all-to-all-start.6
  417.8 15.6 %all-to-all-done.6 = bf16[16,8,1152]{2,1,0:T(8,128)(2,1)S(1)} async-done(((bf16[16,8,1152]{2,1,0:T(8,128)(2,1)}), bf16[16,8,1152]{2,1,0:T(8,128)(2,1)S(1)}, u32[]{:S(2)}, u32[]{:S(2)}) %all-to-all-start.6) | async-done | bytes 294944 | tf_op jit(solution)/shard_map/all_to_all | solution.py:848
  444.4 10.9 %shard_map.190 = bf16[1024,256]{1,0:T(8,128)(2,1)} custom-call(s32[16]{0:T(128)} %copy-done.34, bf16[4,224,1024]{2,1,0:T(8,128)(2,1)} %copy-done.1, bf16[4,224,1024]{2,1,0:T(8,128)(2,1)} %collective-permute-done.7.other.near_other, bf16[4,224,1024]{2,1,0:T(8,128)(2,1)} %pad_maximum_fusion.2.mine.far_mine, ...), custom_call_target="tpu_custom_call" | custom-call | flops 1879048192 | bytes 10485760 | tf_op jit(solution)/shard_map/pallas_call | solution.py:239
  455.3 6.8 %all-to-all-start.5 = ((bf16[128,8,256]{2,1,0:T(8,128)(2,1)}), bf16[128,8,256]{2,1,0:T(8,128)(2,1)S(1)}, u32[]{:S(2)}, u32[]{:S(2)}) async-start(bf16[128,8,256]{2,1,0:T(8,128)(2,1)} %bitcast.171), calls=%async_computation.6 | async-start | bytes 1048576 | tf_op jit(solution)/shard_map/all_to_all | solution.py:850
  473.0 16.2 %collective-permute-done.45 = bf16[224,1024]{1,0:T(8,128)(2,1)S(1)} collective-permute-done((bf16[224,1024]{1,0:T(8,128)(2,1)}, bf16[224,1024]{1,0:T(8,128)(2,1)S(1)}, u32[]{:S(2)}, u32[]{:S(2)}) %collective-permute-start.45) | collective-permute-done | bytes 458784 | tf_op jit(solution)/shard_map/ppermute | solution.py:52
  (262 shorter events, 139.9 us)
Async XLA Ops:
  7.2 35.1 %collective-permute-start = (bf16[224,1024]{1,0:T(8,128)(2,1)}, bf16[224,1024]{1,0:T(8,128)(2,1)S(1)}, u32[]{:S(2)}, u32[]{:S(2)}) collective-permute-start(bf16[224,1024]{1,0:T(8,128)(2,1)} %bitcast.162), channel_id=1, source_target_pairs={{0,64},{8,72},{16,80},{24,88},{32,96},{40,104},{48,112},{56,120},{... | collective-permute-start | bytes 1376264 | tf_op jit(solution)/shard_map/ppermute | solution.py:52
  10.4 32.0 %collective-permute-start.4 = (bf16[224,1024]{1,0:T(8,128)(2,1)}, bf16[224,1024]{1,0:T(8,128)(2,1)S(1)}, u32[]{:S(2)}, u32[]{:S(2)}) collective-permute-start(bf16[224,1024]{1,0:T(8,128)(2,1)} %bitcast.163), channel_id=1, source_target_pairs={{0,16},{8,24},{16,32},{24,40},{32,48},{40,56},{48,0},{56,8},{64,80... | collective-permute-start | bytes 1376264 | tf_op jit(solution)/shard_map/ppermute | solution.py:52
  12.3 30.1 %collective-permute-start.5 = (bf16[224,1024]{1,0:T(8,128)(2,1)}, bf16[224,1024]{1,0:T(8,128)(2,1)S(1)}, u32[]{:S(2)}, u32[]{:S(2)}) collective-permute-start(bf16[224,1024]{1,0:T(8,128)(2,1)} %bitcast.164), channel_id=1, source_target_pairs={{0,48},{8,56},{16,0},{24,8},{32,16},{40,24},{48,32},{56,40},{64,11... | collective-permute-start | bytes 1376264 | tf_op jit(solution)/shard_map/ppermute | solution.py:52
  26.6 179.6 %all-gather.5.cloned.1.call-start = ((), (), s32[]{:S(2)}) async-start(), calls=%async_computation.9 | async-start | bytes 3932160 | tf_op jit(solution)/shard_map/all_gather | solution.py:762
  74.3 43.3 %all-to-all-start.1 = ((bf16[128,8,1152]{2,1,0:T(8,128)(2,1)}), bf16[128,8,1152]{2,1,0:T(8,128)(2,1)S(1)}, u32[]{:S(2)}, u32[]{:S(2)}) async-start(bf16[128,8,1152]{2,1,0:T(8,128)(2,1)} %broadcast_in_dim.101), calls=%async_computation.1 | async-start | bytes 4718592 | tf_op jit(solution)/shard_map/all_to_all | solution.py:770
  83.3 122.9 %all-gather.7.cloned.1.call-start = ((), (), s32[]{:S(2)}) async-start(), calls=%async_computation.10 | async-start | bytes 3932160 | tf_op jit(solution)/shard_map/all_gather | solution.py:762
  83.9 38.9 %collective-permute-start.10 = (bf16[240,1024]{1,0:T(8,128)(2,1)S(1)}, bf16[240,1024]{1,0:T(8,128)(2,1)}, u32[]{:S(2)}, u32[]{:S(2)}) collective-permute-start(bf16[240,1024]{1,0:T(8,128)(2,1)S(1)} %fusion.21), channel_id=1, source_target_pairs={{0,16},{8,24},{16,32},{24,40},{32,48},{40,56},{48,0},{56,8},{64,80... | collective-permute-start | bytes 1474568 | tf_op jit(solution)/shard_map/ppermute | solution.py:52
  85.0 37.9 %collective-permute-start.11 = (bf16[240,1024]{1,0:T(8,128)(2,1)S(1)}, bf16[240,1024]{1,0:T(8,128)(2,1)}, u32[]{:S(2)}, u32[]{:S(2)}) collective-permute-start(bf16[240,1024]{1,0:T(8,128)(2,1)S(1)} %fusion.21), channel_id=1, source_target_pairs={{0,48},{8,56},{16,0},{24,8},{32,16},{40,24},{48,32},{56,40},{64,11... | collective-permute-start | bytes 1474568 | tf_op jit(solution)/shard_map/ppermute | solution.py:52
  87.2 49.1 %collective-permute-start.12 = (bf16[240,1024]{1,0:T(8,128)(2,1)S(1)}, bf16[240,1024]{1,0:T(8,128)(2,1)}, u32[]{:S(2)}, u32[]{:S(2)}) collective-permute-start(bf16[240,1024]{1,0:T(8,128)(2,1)S(1)} %fusion.21), channel_id=1, source_target_pairs={{0,32},{8,40},{16,48},{24,56},{32,0},{40,8},{48,16},{56,24},{64,96... | collective-permute-start | bytes 1474568 | tf_op jit(solution)/shard_map/ppermute | solution.py:52
  122.7 277.0 %reduce-scatter.2.cloned.1.call-start = ((), (), s32[]{:S(2)}) async-start(), calls=%async_computation.8 | async-start | bytes 7864320 | tf_op jit(solution)/shard_map/reduce_scatter | solution.py:818
  141.6 56.4 %collective-permute-start.21 = (bf16[4,240,1024]{2,1,0:T(8,128)(2,1)}, bf16[4,240,1024]{2,1,0:T(8,128)(2,1)}, u32[]{:S(2)}, u32[]{:S(2)}) collective-permute-start(bf16[4,240,1024]{2,1,0:T(8,128)(2,1)} %pad_maximum_fusion.g_mine.routes_mine), channel_id=1, source_target_pairs={{0,64},{8,72},{16,80},{24,88},{32,96},{40,104},{48,112},{56,120},{... | collective-permute-start | bytes 5898248 | tf_op jit(solution)/shard_map/ppermute | solution.py:52
  149.0 48.9 %collective-permute-start.13 = (bf16[224,1024]{1,0:T(8,128)(2,1)}, bf16[224,1024]{1,0:T(8,128)(2,1)S(1)}, u32[]{:S(2)}, u32[]{:S(2)}) collective-permute-start(bf16[224,1024]{1,0:T(8,128)(2,1)} %get-tuple-element.155.normed_ref), channel_id=1, source_target_pairs={{0,64},{8,72},{16,80},{24,88},{32,96},{40,104},{48,112},{56,120},{... | collective-permute-start | bytes 1376264 | tf_op jit(solution)/shard_map/ppermute | solution.py:52
  149.6 48.4 %collective-permute-start.18 = (bf16[224,1024]{1,0:T(8,128)(2,1)}, bf16[224,1024]{1,0:T(8,128)(2,1)S(1)}, u32[]{:S(2)}, u32[]{:S(2)}) collective-permute-start(bf16[224,1024]{1,0:T(8,128)(2,1)} %get-tuple-element.155.normed_ref), channel_id=1, source_target_pairs={{0,16},{8,24},{16,32},{24,40},{32,48},{40,56},{48,0},{56,8},{64,80... | collective-permute-start | bytes 1376264 | tf_op jit(solution)/shard_map/ppermute | solution.py:52
  150.5 47.5 %collective-permute-start.19 = (bf16[224,1024]{1,0:T(8,128)(2,1)}, bf16[224,1024]{1,0:T(8,128)(2,1)S(1)}, u32[]{:S(2)}, u32[]{:S(2)}) collective-permute-start(bf16[224,1024]{1,0:T(8,128)(2,1)} %get-tuple-element.155.normed_ref), channel_id=1, source_target_pairs={{0,48},{8,56},{16,0},{24,8},{32,16},{40,24},{48,32},{56,40},{64,11... | collective-permute-start | bytes 1376264 | tf_op jit(solution)/shard_map/ppermute | solution.py:52
  152.8 45.2 %collective-permute-start.20 = (bf16[224,1024]{1,0:T(8,128)(2,1)}, bf16[224,1024]{1,0:T(8,128)(2,1)S(1)}, u32[]{:S(2)}, u32[]{:S(2)}) collective-permute-start(bf16[224,1024]{1,0:T(8,128)(2,1)} %get-tuple-element.155.normed_ref), channel_id=1, source_target_pairs={{0,32},{8,40},{16,48},{24,56},{32,0},{40,8},{48,16},{56,24},{64,96... | collective-permute-start | bytes 1376264 | tf_op jit(solution)/shard_map/ppermute | solution.py:52
  202.1 28.9 %collective-permute-start.14 = (bf16[224,1024]{1,0:T(8,128)(2,1)S(1)}, bf16[224,1024]{1,0:T(8,128)(2,1)S(1)}, u32[]{:S(2)}, u32[]{:S(2)}) collective-permute-start(bf16[224,1024]{1,0:T(8,128)(2,1)S(1)} %collective-permute-done.13), channel_id=1, source_target_pairs={{0,16},{8,24},{16,32},{24,40},{32,48},{40,56},{48,0},{56,8},{64,80... | collective-permute-start | bytes 1376264 | tf_op jit(solution)/shard_map/ppermute | solution.py:52
  238.8 30.7 %collective-permute-start.26 = (bf16[256,1024]{1,0:T(8,128)(2,1)}, bf16[256,1024]{1,0:T(8,128)(2,1)S(1)}, u32[]{:S(2)}, u32[]{:S(2)}) collective-permute-start(bf16[256,1024]{1,0:T(8,128)(2,1)} %get-tuple-element.263), channel_id=1, source_target_pairs={{0,48},{8,56},{16,0},{24,8},{32,16},{40,24},{48,32},{56,40},{64,11... | collective-permute-start | bytes 1572872 | tf_op jit(solution)/shard_map/ppermute | solution.py:52
  240.7 28.8 %collective-permute-start.27 = (bf16[256,1024]{1,0:T(8,128)(2,1)}, bf16[256,1024]{1,0:T(8,128)(2,1)S(1)}, u32[]{:S(2)}, u32[]{:S(2)}) collective-permute-start(bf16[256,1024]{1,0:T(8,128)(2,1)} %get-tuple-element.262), channel_id=1, source_target_pairs={{0,16},{8,24},{16,32},{24,40},{32,48},{40,56},{48,0},{56,8},{64,80... | collective-permute-start | bytes 1572872 | tf_op jit(solution)/shard_map/ppermute | solution.py:52
  240.8 28.8 %collective-permute-start.28 = (bf16[256,1024]{1,0:T(8,128)(2,1)S(1)}, bf16[256,1024]{1,0:T(8,128)(2,1)S(1)}, u32[]{:S(2)}, u32[]{:S(2)}) collective-permute-start(bf16[256,1024]{1,0:T(8,128)(2,1)S(1)} %get-tuple-element.261), channel_id=1, source_target_pairs={{0,32},{8,40},{16,48},{24,56},{32,0},{40,8},{48,16},{56,24},{64,96... | collective-permute-start | bytes 1572872 | tf_op jit(solution)/shard_map/ppermute | solution.py:52
  274.1 30.5 %collective-permute-start.33 = (bf16[8,224,1024]{2,1,0:T(8,128)(2,1)}, bf16[8,224,1024]{2,1,0:T(8,128)(2,1)}, u32[]{:S(2)}, u32[]{:S(2)}) collective-permute-start(bf16[8,224,1024]{2,1,0:T(8,128)(2,1)} %get-tuple-element.187), channel_id=1, source_target_pairs={{0,8},{8,0},{16,24},{24,16},{32,40},{40,32},{48,56},{56,48},{64,72... | collective-permute-start | bytes 11010056 | tf_op jit(solution)/shard_map/ppermute | solution.py:56
  345.1 48.9 %all-to-all-start.4 = ((bf16[8,128,1152]{2,1,0:T(8,128)(2,1)}), bf16[8,128,1152]{2,1,0:T(8,128)(2,1)S(1)}, u32[]{:S(2)}, u32[]{:S(2)}) async-start(bf16[8,128,1152]{2,1,0:T(8,128)(2,1)} %shard_map.186), calls=%async_computation.4 | async-start | bytes 4718592 | tf_op jit(solution)/shard_map/all_to_all | solution.py:832
  349.8 40.8 %collective-permute-start.35 = (bf16[2,224,1024]{2,1,0:T(8,128)(2,1)}, bf16[2,224,1024]{2,1,0:T(8,128)(2,1)}, u32[]{:S(2)}, u32[]{:S(2)}) collective-permute-start(bf16[2,224,1024]{2,1,0:T(8,128)(2,1)} %get-tuple-element.210), channel_id=1, source_target_pairs={{0,48},{8,56},{16,0},{24,8},{32,16},{40,24},{48,32},{56,40},{64,11... | collective-permute-start | bytes 2752520 | tf_op jit(solution)/shard_map/ppermute | solution.py:52
  350.8 43.2 %collective-permute-start.36 = (bf16[2,224,1024]{2,1,0:T(8,128)(2,1)}, bf16[2,224,1024]{2,1,0:T(8,128)(2,1)}, u32[]{:S(2)}, u32[]{:S(2)}) collective-permute-start(bf16[2,224,1024]{2,1,0:T(8,128)(2,1)} %get-tuple-element.211), channel_id=1, source_target_pairs={{0,16},{8,24},{16,32},{24,40},{32,48},{40,56},{48,0},{56,8},{64,80... | collective-permute-start | bytes 2752520 | tf_op jit(solution)/shard_map/ppermute | solution.py:52
  351.8 42.1 %collective-permute-start.37 = (bf16[2,224,1024]{2,1,0:T(8,128)(2,1)}, bf16[2,224,1024]{2,1,0:T(8,128)(2,1)}, u32[]{:S(2)}, u32[]{:S(2)}) collective-permute-start(bf16[2,224,1024]{2,1,0:T(8,128)(2,1)} %get-tuple-element.212), channel_id=1, source_target_pairs={{0,32},{8,40},{16,48},{24,56},{32,0},{40,8},{48,16},{56,24},{64,96... | collective-permute-start | bytes 2752520 | tf_op jit(solution)/shard_map/ppermute | solution.py:52
  399.7 41.6 %collective-permute-start.44 = (bf16[4,224,1024]{2,1,0:T(8,128)(2,1)}, bf16[4,224,1024]{2,1,0:T(8,128)(2,1)}, u32[]{:S(2)}, u32[]{:S(2)}) collective-permute-start(bf16[4,224,1024]{2,1,0:T(8,128)(2,1)} %get-tuple-element.234), channel_id=1, source_target_pairs={{0,8},{8,0},{16,24},{24,16},{32,40},{40,32},{48,56},{56,48},{64,72... | collective-permute-start | bytes 5505032 | tf_op jit(solution)/shard_map/ppermute | solution.py:56
  405.1 64.7 %collective-permute-start.48 = (bf16[2,192,1024]{2,1,0:T(8,128)(2,1)}, bf16[2,192,1024]{2,1,0:T(8,128)(2,1)}, u32[]{:S(2)}, u32[]{:S(2)}) collective-permute-start(bf16[2,192,1024]{2,1,0:T(8,128)(2,1)} %dynamic-slice_bitcast_fusion), channel_id=1, source_target_pairs={{0,1},{1,0},{2,3},{3,2},{4,5},{5,4},{6,7},{7,6},{8,9},{9,8},{10,11... | collective-permute-start | bytes 2359304 | tf_op jit(solution)/shard_map/ppermute | solution.py:99
  406.8 28.5 %collective-permute-start.40 = (bf16[224,1024]{1,0:T(8,128)(2,1)}, bf16[224,1024]{1,0:T(8,128)(2,1)}, u32[]{:S(2)}, u32[]{:S(2)}) collective-permute-start(bf16[224,1024]{1,0:T(8,128)(2,1)} %get-tuple-element.230), channel_id=1, source_target_pairs={{0,48},{8,56},{16,0},{24,8},{32,16},{40,24},{48,32},{56,40},{64,11... | collective-permute-start | bytes 1376264 | tf_op jit(solution)/shard_map/ppermute | solution.py:52
  407.2 28.9 %collective-permute-start.41 = (bf16[224,1024]{1,0:T(8,128)(2,1)}, bf16[224,1024]{1,0:T(8,128)(2,1)}, u32[]{:S(2)}, u32[]{:S(2)}) collective-permute-start(bf16[224,1024]{1,0:T(8,128)(2,1)} %get-tuple-element.231), channel_id=1, source_target_pairs={{0,16},{8,24},{16,32},{24,40},{32,48},{40,56},{48,0},{56,8},{64,80... | collective-permute-start | bytes 1376264 | tf_op jit(solution)/shard_map/ppermute | solution.py:52
  435.3 29.7 %collective-permute-start.39 = (bf16[224,1024]{1,0:T(8,128)(2,1)}, bf16[224,1024]{1,0:T(8,128)(2,1)}, u32[]{:S(2)}, u32[]{:S(2)}) collective-permute-start(bf16[224,1024]{1,0:T(8,128)(2,1)} %fusion.26), channel_id=1, source_target_pairs={{0,64},{8,72},{16,80},{24,88},{32,96},{40,104},{48,112},{56,120},{... | collective-permute-start | bytes 1376264 | tf_op jit(solution)/shard_map/ppermute | solution.py:52
  438.5 34.5 %collective-permute-start.43 = (bf16[224,1024]{1,0:T(8,128)(2,1)}, bf16[224,1024]{1,0:T(8,128)(2,1)S(1)}, u32[]{:S(2)}, u32[]{:S(2)}) collective-permute-start(bf16[224,1024]{1,0:T(8,128)(2,1)} %add_convert_fusion.17), channel_id=1, source_target_pairs={{0,64},{8,72},{16,80},{24,88},{32,96},{40,104},{48,112},{56,120},{... | collective-permute-start | bytes 1376264 | tf_op jit(solution)/shard_map/ppermute | solution.py:52
  455.3 37.9 %all-to-all-start.5 = ((bf16[128,8,256]{2,1,0:T(8,128)(2,1)}), bf16[128,8,256]{2,1,0:T(8,128)(2,1)S(1)}, u32[]{:S(2)}, u32[]{:S(2)}) async-start(bf16[128,8,256]{2,1,0:T(8,128)(2,1)} %bitcast.171), calls=%async_computation.6 | async-start | bytes 1048576 | tf_op jit(solution)/shard_map/all_to_all | solution.py:850
  465.0 28.2 %collective-permute-start.47 = (bf16[224,1024]{1,0:T(8,128)(2,1)}, bf16[224,1024]{1,0:T(8,128)(2,1)}, u32[]{:S(2)}, u32[]{:S(2)}) collective-permute-start(bf16[224,1024]{1,0:T(8,128)(2,1)} %get-tuple-element.239), channel_id=1, source_target_pairs={{0,32},{8,40},{16,48},{24,56},{32,0},{40,8},{48,16},{56,24},{64,96... | collective-permute-start | bytes 1376264 | tf_op jit(solution)/shard_map/ppermute | solution.py:52
  (67 other events, 863.5 us)
Sparse Core Ops, SparseCore 0:
  29.1 40.6 all-gather.4
  89.2 47.6 all-gather.6
  304.7 89.3 reduce-scatter.1

commit v8 on v7

--- a/solution.py
+++ b/solution.py
@@ -772,31 +772,33 @@
     ).reshape(WIDTH, 1152)
     routes_rows = jnp.pad(routes[0].T.astype(bf16), ((0, 8), (0, WIDTH - TOK)))
     upstream_rows = jnp.concatenate([cotangent[0], routes_rows], axis=0)
-    rows_far, qkv, upstream_rows, expert_rows = tie(rows_far, qkv, upstream_rows, expert_rows)
-    experts = [experts, along_y(expert_rows)]
+    grad_across = send(upstream_rows, 1, 0)
+    rows_far, qkv, upstream_rows, grad_across = tie(rows_far, qkv, upstream_rows, grad_across)
     rows_far = both_cores(rows_far)
     grad_near = [upstream_rows] + [send(upstream_rows, 0, b) for b in (1, 3, 2)]
     qkv = project(places[8:], rows_far, head_weights, gain_attn, table, (qkv,))
 
     router_t = shared[:, WIDTH : WIDTH + EXPERTS].T
     gain_ffn = shared[:, WIDTH + EXPERTS].astype(f32)[None]
+    grad_far = [grad_across, send(grad_across, 0, 1), send(grad_across, 0, 3)]
     attended_head, attended_t, lse = attend(qkv, begin)
+    grad_across, expert_rows, _ = tie(grad_across, expert_rows, attended_head)
+    experts = [experts, along_y(expert_rows)]
+    grad_far = grad_far + [send(grad_across, 0, 2)]
     attended_head, shared = tie(attended_head, shared)
     attended = lax.all_to_all(attended_head, "seq", 0, 0, tiled=True)
-    attended, grad_near = tie(attended, grad_near)
-    grad_near = jnp.stack(grad_near)
-    grad_far = send(grad_near, 1, 0)
+    attended, grad_near, grad_far = tie(attended, grad_near, grad_far)
     hidden, normed_ffn = hidden_of(attended, shared, rows, gain_ffn)
-    grad_near = (grad_near, swap_cores(grad_near))
 
     ffn_near, ffn_across = gather_near(normed_ffn)
-    ffn_near, _, grad_far = tie(ffn_near, ffn_across, grad_far)
+    ffn_near, _ = tie(ffn_near, ffn_across)
     ffn_near, ffn_far = both_cores(ffn_near), gather_far(ffn_across)
+    grad_near = both_cores(grad_near)
     own = jnp.stack([seq_index * 2, own_x])
     near = run_experts(0, own, ffn_near, grad_near, experts, router_t, ())
     near_terms = sum_along_z(*near[:2])
     ffn_far = both_cores(ffn_far)
-    grad_far = (grad_far, swap_cores(grad_far))
+    grad_far = both_cores(grad_far)
     far = run_experts(1, own, ffn_far, grad_far, experts, router_t, near[2:])
     far, near_terms = tie(far, near_terms)
     moved, saved = far[2:4], far[4:]
@@ -841,12 +843,12 @@
     )
     far_terms = send_along_z(far_parts)
     near_parts = chip_parts(near_part[0], swap_cores(near_part[1]))
-    near_parts, projected_grad = tie(near_parts, projected_grad)
-    near_terms = send_along_z(near_parts)
     moved_crossed = send(add_low(*[t[1] for t in moved_terms]), 1, 0)
     shared_grads = jnp.sum(shared_grads.astype(f32), axis=0).astype(bf16).reshape(16, 8, 1152)
     shared_grads = lax.all_to_all(shared_grads, "seq", 0, 0, tiled=True)
     grad_head = head_weight_grad(places, rows_near, rows_far, gain_attn, projected_grad)
+    far_terms, near_parts, grad_head = tie(far_terms, near_parts, grad_head)
+    near_terms = send_along_z(near_parts)
     grad_heads = lax.all_to_all(grad_head.reshape(128, 8, 256), BOTH, 0, 0, tiled=True)
     crossed = send(add_low(*far_terms), 1, 0)
     crossed, near_terms, grad_heads = tie(crossed, near_terms, grad_heads)

time: 514 us -> 494 us (0.961)
  waiting for transfers between devices: 146 us -> 123 us
    all_to_all x1, waiting for transfers between devices: 15.6 us -> 4.64 us  [local(): shared_grads = lax.all_to_all(shared_grads, 'seq', 0, 0, tiled=True)]
    ppermute x2, waiting for transfers between devices: 5.96 us -> 0.01 us  [swap_x(): return lax.ppermute(rows, 'wshard', [(w, w ^ 1) for w in range(8)])]
    another operation x4 -> x6, other arithmetic: 6.9 us -> 10.3 us  [both_cores(): mine = jnp.stack(parts)]
    ppermute x36 -> x39, waiting for transfers between devices: 100 us -> 97.6 us  [send(): return lax.ppermute(rows, 'seq', shift_perm(a, b))]
    ppermute x36 -> x39, starting transfers between devices: 54.6 us -> 55.8 us  [send(): return lax.ppermute(rows, 'seq', shift_perm(a, b))]
  transfers between devices with their start and end apart: 59 -> 62, of which waited for: 18 -> 22; matrix products, arithmetic and copies ran while one was open for 13% -> 13% of each run, Pallas kernels for 33% -> 34%
where the time goes in v8:
time: 494 us; the launch traced here: 485 us
  Pallas kernels  167 us (34%)
  waiting for transfers between devices  123 us (25%)
  starting transfers between devices  103 us (21%)
  other arithmetic  57.4 us (12%)
  local copies, waits for them, and re-layouts  19.9 us (4%)
  between operations  14.9 us (3%)
    ppermute x39, waiting for transfers between devices, send(): return lax.ppermute(rows, 'seq', shift_perm(a, b))  97.6 us
    ppermute x39, starting transfers between devices, send(): return lax.ppermute(rows, 'seq', shift_perm(a, b))  55.8 us
    pallas_call x2, Pallas kernels, run_experts(): pl.pallas_call(experts_kernel, grid_spec=pltpu.PrefetchScalarGridSpec(num...  48.6 us
    pallas_call x1, Pallas kernels, attend_back(): pl.pallas_call(attend_back_kernel, grid=(GROUP // BLOCK,), in_specs=[whol...  31 us
    convert_element_type x7, other arithmetic, add_low(): return sum([t.astype(f32) for t in terms]).astype(bf16)  21.3 us
    pallas_call x1, Pallas kernels, attend(): pl.pallas_call(attend_kernel, grid=(GROUP // BLOCK,), in_specs=[whole(GRO...  19.8 us
    pallas_call x2, Pallas kernels, project(): pl.pallas_call(project_kernel, grid_spec=pltpu.PrefetchScalarGridSpec(num...  16.6 us
    pallas_call x1, Pallas kernels, expert_weight_grads(): pl.pallas_call(expert_grads_kernel, grid=(2, 4), in_specs=[pl.BlockSpec((...  15.9 us
  transfers between devices with their start and end apart: 62, of which 22 were waited for; matrix products, arithmetic and copies ran while one was open for 13% of the time, Pallas kernels for 34%

profile of v8, /device:TPU:0, one launch (start us, length us, event | category | flops | bytes accessed | tf_op | source)
XLA Modules:
  0.0 485.1 jit_solution(7892319251231858923)
XLA Ops:
  19.8 6.8 %all-to-all-start = ((bf16[128,8,256]{2,1,0:T(8,128)(2,1)}), bf16[128,8,256]{2,1,0:T(8,128)(2,1)S(1)}, u32[]{:S(2)}, u32[]{:S(2)}) async-start(bf16[128,8,256]{2,1,0:T(8,128)(2,1)} %bitcast.9), calls=%async_computation | async-start | bytes 1048576 | tf_op jit(solution)/shard_map/all_to_all | solution.py:752
  28.1 7.7 %subtract_cosine_fusion.table = f32[3584,128]{1,0:T(8,128)} fusion(f32[128]{0:T(128)S(1)} %get-tuple-element.299, f32[128]{0:T(128)S(1)} %get-tuple-element.300, f32[3584]{0:T(1024)S(1)} %get-tuple-element.294), kind=kLoop, calls=%fused_computation.10 | loop fusion | flops 917504 | bytes 1850368 | tf_op jit(solution)/shard_map/cos | solution.py:137
  35.8 5.7 %all-to-all-done = bf16[128,8,256]{2,1,0:T(8,128)(2,1)S(1)} async-done(((bf16[128,8,256]{2,1,0:T(8,128)(2,1)}), bf16[128,8,256]{2,1,0:T(8,128)(2,1)S(1)}, u32[]{:S(2)}, u32[]{:S(2)}) %all-to-all-start) | async-done | bytes 524320 | tf_op jit(solution)/shard_map/all_to_all | solution.py:752
  50.9 8.0 %shard_map.178.refs_0_ = bf16[3584,256]{1,0:T(8,128)(2,1)} custom-call(s32[8]{0:T(128)} %get-tuple-element.297.places, bf16[4,224,1024]{2,1,0:T(8,128)(2,1)} %copy-done.1, bf16[4,224,1024]{2,1,0:T(8,128)(2,1)} %collective-permute-done.7.other.near_other, bf16[1024,256]{1,0:T(8,128)(2,1)} %broadcast_select_fusion.w, f32[1,1024]{1,0:T(1,128)} %bitcast.190, ...), custom_call_target="tpu_custom_call" | custom-call | flops 939524096 | bytes 10485760 | tf_op jit(solution)/shard_map/pallas_call | solution.py:174
  60.3 8.4 %collective-permute-done.2 = bf16[224,1024]{1,0:T(8,128)(2,1)} collective-permute-done((bf16[224,1024]{1,0:T(8,128)(2,1)}, bf16[224,1024]{1,0:T(8,128)(2,1)}, u32[]{:S(2)}, u32[]{:S(2)}) %collective-permute-start.2) | collective-permute-done | bytes 458784 | tf_op jit(solution)/shard_map/ppermute | solution.py:52
  75.9 9.7 %all-to-all-start.1 = ((bf16[128,8,1152]{2,1,0:T(8,128)(2,1)}), bf16[128,8,1152]{2,1,0:T(8,128)(2,1)S(1)}, u32[]{:S(2)}, u32[]{:S(2)}) async-start(bf16[128,8,1152]{2,1,0:T(8,128)(2,1)} %broadcast_in_dim.101), calls=%async_computation.1 | async-start | bytes 4718592 | tf_op jit(solution)/shard_map/all_to_all | solution.py:770
  85.9 8.6 %shard_map.179.qkv_ref = bf16[3584,256]{1,0:T(8,128)(2,1)} custom-call(s32[8]{0:T(128)} %get-tuple-element.298.places, bf16[4,224,1024]{2,1,0:T(8,128)(2,1)} %pad_maximum_fusion.3.mine.far_mine, bf16[4,224,1024]{2,1,0:T(8,128)(2,1)} %collective-permute-done.9.other.far_other, bf16[1024,256]{1,0:T(8,128)(2,1)} %broadcast_select_fusion.w, ...), custom_call_target="tpu_custom_call" | custom-call | flops 939524096 | bytes 10485760 | tf_op jit(solution)/shard_map/pallas_call | solution.py:174
  94.6 19.8 %shard_map.180 = (bf16[16,64,224]{2,1,0:T(8,128)(2,1)}, f32[64,3584]{1,0:T(8,128)}, f32[1,3584]{1,0:T(1,128)}) custom-call(bf16[3584,256]{1,0:T(8,128)(2,1)} %shard_map.179.qkv_ref, s32[1,3584]{1,0:T(1,128)} %compare_select_fusion.begin_ref), custom_call_target="tpu_custom_call" | custom-call | flops 7247757312 | bytes 4194304 | tf_op jit(solution)/shard_map/pallas_call | solution.py:324
  122.6 19.3 %collective-permute-done.10 = bf16[240,1024]{1,0:T(8,128)(2,1)S(1)} collective-permute-done((bf16[240,1024]{1,0:T(8,128)(2,1)}, bf16[240,1024]{1,0:T(8,128)(2,1)S(1)}, u32[]{:S(2)}, u32[]{:S(2)}) %collective-permute-start.10) | collective-permute-done | bytes 491552 | tf_op jit(solution)/shard_map/ppermute | solution.py:52
  142.6 4.9 %all-to-all-start.2 = ((bf16[16,64,224]{2,1,0:T(8,128)(2,1)}), bf16[16,64,224]{2,1,0:T(8,128)(2,1)S(1)}, u32[]{:S(2)}, u32[]{:S(2)}) async-start(bf16[16,64,224]{2,1,0:T(8,128)(2,1)} %get-tuple-element.152), calls=%async_computation.2 | async-start | bytes 1048576 | tf_op jit(solution)/shard_map/all_to_all | solution.py:789
  152.2 13.6 %collective-permute-done.16 = bf16[240,1024]{1,0:T(8,128)(2,1)} collective-permute-done((bf16[240,1024]{1,0:T(8,128)(2,1)}, bf16[240,1024]{1,0:T(8,128)(2,1)}, u32[]{:S(2)}, u32[]{:S(2)}) %collective-permute-start.16) | collective-permute-done | bytes 491552 | tf_op jit(solution)/shard_map/ppermute | solution.py:52
  180.5 6.2 %collective-permute-done.17 = bf16[224,1024]{1,0:T(8,128)(2,1)S(1)} collective-permute-done((bf16[224,1024]{1,0:T(8,128)(2,1)}, bf16[224,1024]{1,0:T(8,128)(2,1)S(1)}, u32[]{:S(2)}, u32[]{:S(2)}) %collective-permute-start.17) | collective-permute-done | bytes 458784 | tf_op jit(solution)/shard_map/ppermute | solution.py:52
  188.9 9.2 %collective-permute-done.24 = bf16[224,1024]{1,0:T(8,128)(2,1)S(1)} collective-permute-done((bf16[224,1024]{1,0:T(8,128)(2,1)}, bf16[224,1024]{1,0:T(8,128)(2,1)S(1)}, u32[]{:S(2)}, u32[]{:S(2)}) %collective-permute-start.24) | collective-permute-done | bytes 458784 | tf_op jit(solution)/shard_map/ppermute | solution.py:52
  207.4 24.3 %shard_map.182 = (bf16[4,256,1024]{2,1,0:T(8,128)(2,1)}, bf16[4,256,1024]{2,1,0:T(8,128)(2,1)}, bf16[8,224,1024]{2,1,0:T(8,128)(2,1)}, bf16[8,224,1024]{2,1,0:T(...) custom-call(s32[2]{0:T(128)} %pad_add_fusion.own_ref, ...), custom_call_target="tpu_custom_call" | custom-call | flops 15032385536 | bytes 25165824 | tf_op jit(solution)/shard_map/pallas_call | solution.py:547
  245.6 24.3 %shard_map.183 = (bf16[4,256,1024]{2,1,0:T(8,128)(2,1)}, bf16[4,256,1024]{2,1,0:T(8,128)(2,1)}, bf16[8,224,1024]{2,1,0:T(8,128)(2,1)}, bf16[8,224,1024]{2,1,0:T(...) custom-call(s32[2]{0:T(128)} %pad_add_fusion.own_ref, ...), custom_call_target="tpu_custom_call", output_to_operand_aliasing={{2}: (10, {}), {3}: (11, {}), {4}: (12, {}), {5}: (13, {}),... | custom-call | flops 15032385536 | bytes 25165824 | tf_op jit(solution)/shard_map/pallas_call | solution.py:547
  270.0 4.4 collective-permute-done.32
  281.1 15.9 %shard_map.184 = bf16[4,2,2,192,1024]{4,3,2,1,0:T(8,128)(2,1)} custom-call(bf16[2,1152,1024]{2,1,0:T(8,128)(2,1)} %get-tuple-element.197.x_ref, bf16[2,1152,1024]{2,1,0:T(8,128)(2,1)} %get-tuple-element.198.dh_ref, bf16[2,1152,512]{2,1,0:T(8,128)(2,1)} %get-tuple-element.199.act_ref, bf16[2,1152,1024]{2,1,0:T(8,128)(2,1)} %get-tuple-element.200.dy_ref), custom_call_target="tpu_custom_call" | custom-call | flops 8589934592 | bytes 14680064 | tf_op jit(solution)/shard_map/pallas_call | solution.py:603
  297.0 8.5 %collective-permute-done.34 = bf16[256,1024]{1,0:T(8,128)(2,1)S(1)} collective-permute-done((bf16[256,1024]{1,0:T(8,128)(2,1)S(1)}, bf16[256,1024]{1,0:T(8,128)(2,1)S(1)}, u32[]{:S(2)}, u32[]{:S(2)}) %collective-permute-start.34) | collective-permute-done | bytes 524320 | tf_op jit(solution)/shard_map/ppermute | solution.py:52
  307.7 6.2 %fusion.10 = (bf16[2,224,1024]{2,1,0:T(8,128)(2,1)}, bf16[2,224,1024]{2,1,0:T(8,128)(2,1)}, bf16[2,224,1024]{2,1,0:T(8,128)(2,1)}, bf16[2,224,1024]{2,1,0:T(8,128)(2,1)S(1)}) fusion(bf16[2,4,224,1024]{3,2,1,0:T(8,128)(2,1)} %bitcast.53, bf16[2,4,224,1024]{3,2,1,0:T(8,128)(2,1)} %bitcast.173), kind=kLoop, calls=%fused_computation.36 | loop fusion | flops 7340032 | bytes 11010048 | tf_op jit(solution)/shard_map/convert_element_type | solution.py:83
  314.0 6.2 %collective-permute-done.37.crossed = bf16[256,1024]{1,0:T(8,128)(2,1)S(1)} collective-permute-done((bf16[256,1024]{1,0:T(8,128)(2,1)S(1)}, bf16[256,1024]{1,0:T(8,128)(2,1)S(1)}, u32[]{:S(2)}, u32[]{:S(2)}) %collective-permute-start.37) | collective-permute-done | bytes 524320 | tf_op jit(solution)/shard_map/ppermute | solution.py:52
  320.9 5.8 %shard_map.185 = (f32[224,1024]{1,0:T(8,128)}, bf16[224,1024]{1,0:T(8,128)(2,1)}, bf16[32,224]{1,0:T(8,128)(2,1)}, bf16[224,1024]{1,0:T(8,128)(2,1)}, bf16[16,64,224]{2,1,0:T(8,128)(2,1)}) custom-call(bf16[256,1024]{1,0:T(8,128)(2,1)} %get-tuple-element.189.t0, bf16[256,1024]{1,0:T(8,128)(2,1)} %copy-done.21, bf16[256,1024]{1,0:T(8,128)(2,1)} %copy-done.22, ...), custom_call_target="tpu_custom_call" | custom-call | flops 469762048 | bytes 8388608 | tf_op jit(solution)/shard_map/pallas_call | solution.py:674
  334.2 8.4 %all-to-all-done.3.g_ref = bf16[16,64,224]{2,1,0:T(8,128)(2,1)S(1)} async-done(((bf16[16,64,224]{2,1,0:T(8,128)(2,1)}), bf16[16,64,224]{2,1,0:T(8,128)(2,1)S(1)}, u32[]{:S(2)}, u32[]{:S(2)}) %all-to-all-start.3) | async-done | bytes 458784 | tf_op jit(solution)/shard_map/all_to_all | solution.py:827
  343.4 4.3 all-to-all-start.4
  350.2 31.0 %shard_map.187.first.second = bf16[3584,256]{1,0:T(8,128)(2,1)} custom-call(bf16[3584,256]{1,0:T(8,128)(2,1)} %shard_map.179.qkv_ref, bf16[16,64,224]{2,1,0:T(8,128)(2,1)} %copy-done.26, f32[64,3584]{1,0:T(8,128)} %get-tuple-element.218.ot_ref, f32[1,3584]{1,0:T(1,128)} %get-tuple-element.219.lse_ref, s32[1,3584]{1,0:T(1,128)} %compare_select_fusion.begin_ref, ...), custom_call_target="tpu_custom_call" | custom-call | flops 18119393280 | bytes 8388608 | tf_op jit(solution)/shard_map/pallas_call | solution.py:404
  381.2 5.4 %shard_map.188 = (bf16[4,224,1024]{2,1,0:T(8,128)(2,1)}, bf16[4,224,1024]{2,1,0:T(8,128)(2,1)}) custom-call(s32[8]{0:T(128)} %get-tuple-element.298.places, bf16[3584,256]{1,0:T(8,128)(2,1)} %shard_map.187.first.second, bf16[3584,256]{1,0:T(8,128)(2,1)} %shard_map.187.first.second, bf16[1024,256]{1,0:T(8,128)(2,1)} %broadcast_select_fusion.w), custom_call_target="tpu_custom_call" | custom-call | flops 939524096 | bytes 5242880 | tf_op jit(solution)/shard_map/pallas_call | solution.py:201
  392.1 5.4 %shard_map.189 = (bf16[4,224,1024]{2,1,0:T(8,128)(2,1)}, bf16[4,224,1024]{2,1,0:T(8,128)(2,1)}) custom-call(s32[8]{0:T(128)} %get-tuple-element.297.places, bf16[3584,256]{1,0:T(8,128)(2,1)} %shard_map.187.first.second, bf16[3584,256]{1,0:T(8,128)(2,1)} %shard_map.187.first.second, bf16[1024,256]{1,0:T(8,128)(2,1)} %broadcast_select_fusion.w), custom_call_target="tpu_custom_call" | custom-call | flops 939524096 | bytes 5242880 | tf_op jit(solution)/shard_map/pallas_call | solution.py:201
  398.0 4.0 fusion.25
  408.4 4.9 %all-to-all-start.6 = ((bf16[16,8,1152]{2,1,0:T(8,128)(2,1)}), bf16[16,8,1152]{2,1,0:T(8,128)(2,1)S(1)}, u32[]{:S(2)}, u32[]{:S(2)}) async-start(bf16[16,8,1152]{2,1,0:T(8,128)(2,1)} %bitcast.178), calls=%async_computation.7 | async-start | bytes 589824 | tf_op jit(solution)/shard_map/all_to_all | solution.py:848
  413.3 10.8 %shard_map.190 = bf16[1024,256]{1,0:T(8,128)(2,1)} custom-call(s32[16]{0:T(128)} %copy-done.39, bf16[4,224,1024]{2,1,0:T(8,128)(2,1)} %copy-done.1, bf16[4,224,1024]{2,1,0:T(8,128)(2,1)} %collective-permute-done.7.other.near_other, bf16[4,224,1024]{2,1,0:T(8,128)(2,1)} %pad_maximum_fusion.3.mine.far_mine, ...), custom_call_target="tpu_custom_call" | custom-call | flops 1879048192 | bytes 10485760 | tf_op jit(solution)/shard_map/pallas_call | solution.py:239
  426.5 4.6 all-to-all-done.6
  444.3 7.4 %all-to-all-start.5 = ((bf16[128,8,256]{2,1,0:T(8,128)(2,1)}), bf16[128,8,256]{2,1,0:T(8,128)(2,1)S(1)}, u32[]{:S(2)}, u32[]{:S(2)}) async-start(bf16[128,8,256]{2,1,0:T(8,128)(2,1)} %bitcast.71), calls=%async_computation.6 | async-start | bytes 1048576 | tf_op jit(solution)/shard_map/all_to_all | solution.py:852
  460.7 11.8 %collective-permute-done.49 = bf16[224,1024]{1,0:T(8,128)(2,1)} collective-permute-done((bf16[224,1024]{1,0:T(8,128)(2,1)}, bf16[224,1024]{1,0:T(8,128)(2,1)}, u32[]{:S(2)}, u32[]{:S(2)}) %collective-permute-start.49) | collective-permute-done | bytes 458784 | tf_op jit(solution)/shard_map/ppermute | solution.py:52
  (281 shorter events, 148.7 us)
Async XLA Ops:
  7.2 35.1 %collective-permute-start = (bf16[224,1024]{1,0:T(8,128)(2,1)}, bf16[224,1024]{1,0:T(8,128)(2,1)S(1)}, u32[]{:S(2)}, u32[]{:S(2)}) collective-permute-start(bf16[224,1024]{1,0:T(8,128)(2,1)} %bitcast.166), channel_id=1, source_target_pairs={{0,64},{8,72},{16,80},{24,88},{32,96},{40,104},{48,112},{56,120},{... | collective-permute-start | bytes 1376264 | tf_op jit(solution)/shard_map/ppermute | solution.py:52
  10.4 32.0 %collective-permute-start.4 = (bf16[224,1024]{1,0:T(8,128)(2,1)}, bf16[224,1024]{1,0:T(8,128)(2,1)S(1)}, u32[]{:S(2)}, u32[]{:S(2)}) collective-permute-start(bf16[224,1024]{1,0:T(8,128)(2,1)} %bitcast.167), channel_id=1, source_target_pairs={{0,16},{8,24},{16,32},{24,40},{32,48},{40,56},{48,0},{56,8},{64,80... | collective-permute-start | bytes 1376264 | tf_op jit(solution)/shard_map/ppermute | solution.py:52
  12.3 30.0 %collective-permute-start.5 = (bf16[224,1024]{1,0:T(8,128)(2,1)}, bf16[224,1024]{1,0:T(8,128)(2,1)}, u32[]{:S(2)}, u32[]{:S(2)}) collective-permute-start(bf16[224,1024]{1,0:T(8,128)(2,1)} %bitcast.168), channel_id=1, source_target_pairs={{0,48},{8,56},{16,0},{24,8},{32,16},{40,24},{48,32},{56,40},{64,11... | collective-permute-start | bytes 1376264 | tf_op jit(solution)/shard_map/ppermute | solution.py:52
  14.4 27.9 %collective-permute-start.6 = (bf16[224,1024]{1,0:T(8,128)(2,1)}, bf16[224,1024]{1,0:T(8,128)(2,1)}, u32[]{:S(2)}, u32[]{:S(2)}) collective-permute-start(bf16[224,1024]{1,0:T(8,128)(2,1)} %bitcast.169), channel_id=1, source_target_pairs={{0,32},{8,40},{16,48},{24,56},{32,0},{40,8},{48,16},{56,24},{64,96... | collective-permute-start | bytes 1376264 | tf_op jit(solution)/shard_map/ppermute | solution.py:52
  26.6 180.8 %all-gather.5.cloned.1.call-start = ((), (), s32[]{:S(2)}) async-start(), calls=%async_computation.9 | async-start | bytes 3932160 | tf_op jit(solution)/shard_map/all_gather | solution.py:762
  72.3 42.0 %collective-permute-start.15 = (bf16[2,192,1024]{2,1,0:T(8,128)(2,1)S(1)}, bf16[2,192,1024]{2,1,0:T(8,128)(2,1)}, u32[]{:S(2)}, u32[]{:S(2)}) collective-permute-start(bf16[2,192,1024]{2,1,0:T(8,128)(2,1)S(1)} %copy-done.8), channel_id=1, source_target_pairs={{0,1},{1,0},{2,3},{3,2},{4,5},{5,4},{6,7},{7,6},{8,9},{9,8},{10,11... | collective-permute-start | bytes 2359304 | tf_op jit(solution)/shard_map/ppermute | solution.py:99
  75.9 66.7 %all-to-all-start.1 = ((bf16[128,8,1152]{2,1,0:T(8,128)(2,1)}), bf16[128,8,1152]{2,1,0:T(8,128)(2,1)S(1)}, u32[]{:S(2)}, u32[]{:S(2)}) async-start(bf16[128,8,1152]{2,1,0:T(8,128)(2,1)} %broadcast_in_dim.101), calls=%async_computation.1 | async-start | bytes 4718592 | tf_op jit(solution)/shard_map/all_to_all | solution.py:770
  85.7 121.7 %all-gather.7.cloned.1.call-start = ((), (), s32[]{:S(2)}) async-start(), calls=%async_computation.10 | async-start | bytes 3932160 | tf_op jit(solution)/shard_map/all_gather | solution.py:762
  114.4 27.5 %collective-permute-start.10 = (bf16[240,1024]{1,0:T(8,128)(2,1)}, bf16[240,1024]{1,0:T(8,128)(2,1)S(1)}, u32[]{:S(2)}, u32[]{:S(2)}) collective-permute-start(bf16[240,1024]{1,0:T(8,128)(2,1)} %copy-done.12), channel_id=1, source_target_pairs={{0,16},{8,24},{16,32},{24,40},{32,48},{40,56},{48,0},{56,8},{64,80... | collective-permute-start | bytes 1474568 | tf_op jit(solution)/shard_map/ppermute | solution.py:52
  115.5 33.0 %collective-permute-start.11 = (bf16[240,1024]{1,0:T(8,128)(2,1)}, bf16[240,1024]{1,0:T(8,128)(2,1)}, u32[]{:S(2)}, u32[]{:S(2)}) collective-permute-start(bf16[240,1024]{1,0:T(8,128)(2,1)} %copy-done.12), channel_id=1, source_target_pairs={{0,48},{8,56},{16,0},{24,8},{32,16},{40,24},{48,32},{56,40},{64,11... | collective-permute-start | bytes 1474568 | tf_op jit(solution)/shard_map/ppermute | solution.py:52
  117.7 30.8 %collective-permute-start.12 = (bf16[240,1024]{1,0:T(8,128)(2,1)}, bf16[240,1024]{1,0:T(8,128)(2,1)}, u32[]{:S(2)}, u32[]{:S(2)}) collective-permute-start(bf16[240,1024]{1,0:T(8,128)(2,1)} %copy-done.12), channel_id=1, source_target_pairs={{0,32},{8,40},{16,48},{24,56},{32,0},{40,8},{48,16},{56,24},{64,96... | collective-permute-start | bytes 1474568 | tf_op jit(solution)/shard_map/ppermute | solution.py:52
  119.3 32.4 %collective-permute-start.13 = (bf16[240,1024]{1,0:T(8,128)(2,1)}, bf16[240,1024]{1,0:T(8,128)(2,1)}, u32[]{:S(2)}, u32[]{:S(2)}) collective-permute-start(bf16[240,1024]{1,0:T(8,128)(2,1)} %copy-done.27), channel_id=1, source_target_pairs={{0,16},{8,24},{16,32},{24,40},{32,48},{40,56},{48,0},{56,8},{64,80... | collective-permute-start | bytes 1474568 | tf_op jit(solution)/shard_map/ppermute | solution.py:52
  120.2 32.1 %collective-permute-start.14 = (bf16[240,1024]{1,0:T(8,128)(2,1)}, bf16[240,1024]{1,0:T(8,128)(2,1)}, u32[]{:S(2)}, u32[]{:S(2)}) collective-permute-start(bf16[240,1024]{1,0:T(8,128)(2,1)} %copy-done.27), channel_id=1, source_target_pairs={{0,48},{8,56},{16,0},{24,8},{32,16},{40,24},{48,32},{56,40},{64,11... | collective-permute-start | bytes 1474568 | tf_op jit(solution)/shard_map/ppermute | solution.py:52
  147.6 249.9 %reduce-scatter.2.cloned.1.call-start = ((), (), s32[]{:S(2)}) async-start(), calls=%async_computation.8 | async-start | bytes 7864320 | tf_op jit(solution)/shard_map/reduce_scatter | solution.py:820
  203.1 30.9 %collective-permute-start.18 = (bf16[224,1024]{1,0:T(8,128)(2,1)S(1)}, bf16[224,1024]{1,0:T(8,128)(2,1)S(1)}, u32[]{:S(2)}, u32[]{:S(2)}) collective-permute-start(bf16[224,1024]{1,0:T(8,128)(2,1)S(1)} %collective-permute-done.17), channel_id=1, source_target_pairs={{0,16},{8,24},{16,32},{24,40},{32,48},{40,56},{48,0},{56,8},{64,80... | collective-permute-start | bytes 1376264 | tf_op jit(solution)/shard_map/ppermute | solution.py:52
  204.2 29.7 %collective-permute-start.19 = (bf16[224,1024]{1,0:T(8,128)(2,1)S(1)}, bf16[224,1024]{1,0:T(8,128)(2,1)}, u32[]{:S(2)}, u32[]{:S(2)}) collective-permute-start(bf16[224,1024]{1,0:T(8,128)(2,1)S(1)} %collective-permute-done.17), channel_id=1, source_target_pairs={{0,48},{8,56},{16,0},{24,8},{32,16},{40,24},{48,32},{56,40},{64,11... | collective-permute-start | bytes 1376264 | tf_op jit(solution)/shard_map/ppermute | solution.py:52
  206.3 27.7 %collective-permute-start.20 = (bf16[224,1024]{1,0:T(8,128)(2,1)S(1)}, bf16[224,1024]{1,0:T(8,128)(2,1)}, u32[]{:S(2)}, u32[]{:S(2)}) collective-permute-start(bf16[224,1024]{1,0:T(8,128)(2,1)S(1)} %collective-permute-done.17), channel_id=1, source_target_pairs={{0,32},{8,40},{16,48},{24,56},{32,0},{40,8},{48,16},{56,24},{64,96... | collective-permute-start | bytes 1376264 | tf_op jit(solution)/shard_map/ppermute | solution.py:52
  238.0 31.8 %collective-permute-start.29 = (bf16[256,1024]{1,0:T(8,128)(2,1)}, bf16[256,1024]{1,0:T(8,128)(2,1)S(1)}, u32[]{:S(2)}, u32[]{:S(2)}) collective-permute-start(bf16[256,1024]{1,0:T(8,128)(2,1)} %get-tuple-element.281), channel_id=1, source_target_pairs={{0,48},{8,56},{16,0},{24,8},{32,16},{40,24},{48,32},{56,40},{64,11... | collective-permute-start | bytes 1572872 | tf_op jit(solution)/shard_map/ppermute | solution.py:52
  240.0 29.9 %collective-permute-start.30 = (bf16[256,1024]{1,0:T(8,128)(2,1)}, bf16[256,1024]{1,0:T(8,128)(2,1)S(1)}, u32[]{:S(2)}, u32[]{:S(2)}) collective-permute-start(bf16[256,1024]{1,0:T(8,128)(2,1)} %get-tuple-element.280), channel_id=1, source_target_pairs={{0,16},{8,24},{16,32},{24,40},{32,48},{40,56},{48,0},{56,8},{64,80... | collective-permute-start | bytes 1572872 | tf_op jit(solution)/shard_map/ppermute | solution.py:52
  240.1 29.8 %collective-permute-start.31 = (bf16[256,1024]{1,0:T(8,128)(2,1)S(1)}, bf16[256,1024]{1,0:T(8,128)(2,1)S(1)}, u32[]{:S(2)}, u32[]{:S(2)}) collective-permute-start(bf16[256,1024]{1,0:T(8,128)(2,1)S(1)} %get-tuple-element.279), channel_id=1, source_target_pairs={{0,32},{8,40},{16,48},{24,56},{32,0},{40,8},{48,16},{56,24},{64,96... | collective-permute-start | bytes 1572872 | tf_op jit(solution)/shard_map/ppermute | solution.py:52
  274.4 31.1 %collective-permute-start.36 = (bf16[8,224,1024]{2,1,0:T(8,128)(2,1)}, bf16[8,224,1024]{2,1,0:T(8,128)(2,1)}, u32[]{:S(2)}, u32[]{:S(2)}) collective-permute-start(bf16[8,224,1024]{2,1,0:T(8,128)(2,1)} %get-tuple-element.201), channel_id=1, source_target_pairs={{0,8},{8,0},{16,24},{24,16},{32,40},{40,32},{48,56},{56,48},{64,72... | collective-permute-start | bytes 11010056 | tf_op jit(solution)/shard_map/ppermute | solution.py:56
  343.4 48.5 %all-to-all-start.4 = ((bf16[8,128,1152]{2,1,0:T(8,128)(2,1)}), bf16[8,128,1152]{2,1,0:T(8,128)(2,1)S(1)}, u32[]{:S(2)}, u32[]{:S(2)}) async-start(bf16[8,128,1152]{2,1,0:T(8,128)(2,1)} %shard_map.186), calls=%async_computation.4 | async-start | bytes 4718592 | tf_op jit(solution)/shard_map/all_to_all | solution.py:834
  347.7 40.8 %collective-permute-start.38 = (bf16[2,224,1024]{2,1,0:T(8,128)(2,1)}, bf16[2,224,1024]{2,1,0:T(8,128)(2,1)}, u32[]{:S(2)}, u32[]{:S(2)}) collective-permute-start(bf16[2,224,1024]{2,1,0:T(8,128)(2,1)} %get-tuple-element.224), channel_id=1, source_target_pairs={{0,48},{8,56},{16,0},{24,8},{32,16},{40,24},{48,32},{56,40},{64,11... | collective-permute-start | bytes 2752520 | tf_op jit(solution)/shard_map/ppermute | solution.py:52
  348.7 43.2 %collective-permute-start.39 = (bf16[2,224,1024]{2,1,0:T(8,128)(2,1)}, bf16[2,224,1024]{2,1,0:T(8,128)(2,1)}, u32[]{:S(2)}, u32[]{:S(2)}) collective-permute-start(bf16[2,224,1024]{2,1,0:T(8,128)(2,1)} %get-tuple-element.225), channel_id=1, source_target_pairs={{0,16},{8,24},{16,32},{24,40},{32,48},{40,56},{48,0},{56,8},{64,80... | collective-permute-start | bytes 2752520 | tf_op jit(solution)/shard_map/ppermute | solution.py:52
  349.7 42.1 %collective-permute-start.40 = (bf16[2,224,1024]{2,1,0:T(8,128)(2,1)}, bf16[2,224,1024]{2,1,0:T(8,128)(2,1)}, u32[]{:S(2)}, u32[]{:S(2)}) collective-permute-start(bf16[2,224,1024]{2,1,0:T(8,128)(2,1)} %get-tuple-element.226), channel_id=1, source_target_pairs={{0,32},{8,40},{16,48},{24,56},{32,0},{40,8},{48,16},{56,24},{64,96... | collective-permute-start | bytes 2752520 | tf_op jit(solution)/shard_map/ppermute | solution.py:52
  397.5 35.6 %collective-permute-start.46 = (bf16[4,224,1024]{2,1,0:T(8,128)(2,1)}, bf16[4,224,1024]{2,1,0:T(8,128)(2,1)}, u32[]{:S(2)}, u32[]{:S(2)}) collective-permute-start(bf16[4,224,1024]{2,1,0:T(8,128)(2,1)} %get-tuple-element.248), channel_id=1, source_target_pairs={{0,8},{8,0},{16,24},{24,16},{32,40},{40,32},{48,56},{56,48},{64,72... | collective-permute-start | bytes 5505032 | tf_op jit(solution)/shard_map/ppermute | solution.py:56
  402.9 54.4 %collective-permute-start.51 = (bf16[2,192,1024]{2,1,0:T(8,128)(2,1)}, bf16[2,192,1024]{2,1,0:T(8,128)(2,1)}, u32[]{:S(2)}, u32[]{:S(2)}) collective-permute-start(bf16[2,192,1024]{2,1,0:T(8,128)(2,1)} %dynamic-slice_bitcast_fusion), channel_id=1, source_target_pairs={{0,1},{1,0},{2,3},{3,2},{4,5},{5,4},{6,7},{7,6},{8,9},{9,8},{10,11... | collective-permute-start | bytes 2359304 | tf_op jit(solution)/shard_map/ppermute | solution.py:99
  404.7 32.9 %collective-permute-start.43 = (bf16[224,1024]{1,0:T(8,128)(2,1)}, bf16[224,1024]{1,0:T(8,128)(2,1)}, u32[]{:S(2)}, u32[]{:S(2)}) collective-permute-start(bf16[224,1024]{1,0:T(8,128)(2,1)} %get-tuple-element.244), channel_id=1, source_target_pairs={{0,48},{8,56},{16,0},{24,8},{32,16},{40,24},{48,32},{56,40},{64,11... | collective-permute-start | bytes 1376264 | tf_op jit(solution)/shard_map/ppermute | solution.py:52
  405.1 32.5 %collective-permute-start.44 = (bf16[224,1024]{1,0:T(8,128)(2,1)}, bf16[224,1024]{1,0:T(8,128)(2,1)}, u32[]{:S(2)}, u32[]{:S(2)}) collective-permute-start(bf16[224,1024]{1,0:T(8,128)(2,1)} %get-tuple-element.245), channel_id=1, source_target_pairs={{0,16},{8,24},{16,32},{24,40},{32,48},{40,56},{48,0},{56,8},{64,80... | collective-permute-start | bytes 1376264 | tf_op jit(solution)/shard_map/ppermute | solution.py:52
  406.7 30.9 %collective-permute-start.45 = (bf16[224,1024]{1,0:T(8,128)(2,1)}, bf16[224,1024]{1,0:T(8,128)(2,1)}, u32[]{:S(2)}, u32[]{:S(2)}) collective-permute-start(bf16[224,1024]{1,0:T(8,128)(2,1)} %get-tuple-element.246), channel_id=1, source_target_pairs={{0,32},{8,40},{16,48},{24,56},{32,0},{40,8},{48,16},{56,24},{64,96... | collective-permute-start | bytes 1376264 | tf_op jit(solution)/shard_map/ppermute | solution.py:52
  443.7 28.7 %collective-permute-start.49 = (bf16[224,1024]{1,0:T(8,128)(2,1)}, bf16[224,1024]{1,0:T(8,128)(2,1)}, u32[]{:S(2)}, u32[]{:S(2)}) collective-permute-start(bf16[224,1024]{1,0:T(8,128)(2,1)} %get-tuple-element.256), channel_id=1, source_target_pairs={{0,16},{8,24},{16,32},{24,40},{32,48},{40,56},{48,0},{56,8},{64,80... | collective-permute-start | bytes 1376264 | tf_op jit(solution)/shard_map/ppermute | solution.py:52
  444.3 28.1 %all-to-all-start.5 = ((bf16[128,8,256]{2,1,0:T(8,128)(2,1)}), bf16[128,8,256]{2,1,0:T(8,128)(2,1)S(1)}, u32[]{:S(2)}, u32[]{:S(2)}) async-start(bf16[128,8,256]{2,1,0:T(8,128)(2,1)} %bitcast.71), calls=%async_computation.6 | async-start | bytes 1048576 | tf_op jit(solution)/shard_map/all_to_all | solution.py:852
  (76 other events, 923.1 us)
Sparse Core Ops, SparseCore 0:
  29.1 40.6 all-gather.4
  114.5 40.6 all-gather.6
  305.6 85.5 reduce-scatter.1

commit v9 on v8

--- a/solution.py
+++ b/solution.py
@@ -437,18 +437,19 @@
     x_ref, dh_ref, act_ref, dy_ref, w_ref, sem = refs[-6:]
     own = own_ref[0]
 
-    @pl.when(pl.program_id(0) == 0)
-    def _():
-        copies = [
+    copies = [
+        [
             pltpu.make_async_copy(shards.at[y, e], w_ref.at[e, 2 * y + (own_ref[1] ^ a)], sem.at[a, y, e])
             for a, shards in enumerate((own_w, across_w))
             for y in range(4)
-            for e in range(2)
         ]
-        for copy in copies:
+        for e in range(2)
+    ]
+
+    @pl.when(pl.program_id(0) == 0)
+    def _():
+        for copy in copies[0] + copies[1]:
             copy.start()
-        for copy in copies:
-            copy.wait()
 
     expert_rows = lax.broadcasted_iota(i32, (EXPERTS, TOK), 0)
     slot_rows = lax.broadcasted_iota(i32, (SLOTS, TOK), 0).astype(f32)
@@ -483,13 +484,20 @@
             gate_rows[e].append(
                 jnp.sum(jnp.where(expert_rows == own + e, gates, 0.0), axis=0, keepdims=True)
             )
-            pick = (slots[e : e + 1] == slot_rows).astype(f32)
-            picks[e].append(pick)
-            low = pick.astype(bf16)
-            picked_rows[e].append(jnp.dot(low, rows, preferred_element_type=f32))
-            picked_grads[e].append(jnp.dot(low, grads, preferred_element_type=f32))
+            picks[e].append((slots[e : e + 1] == slot_rows).astype(f32))
+        low = jnp.concatenate([picks[0][-1], picks[1][-1]], axis=0).astype(bf16)
+        for source, kept in ((rows, picked_rows), (grads, picked_grads)):
+            both = jnp.dot(low, source, preferred_element_type=f32)
+            kept[0].append(both[:SLOTS])
+            kept[1].append(both[SLOTS:])
     moved, routed = [], []
     for e in range(2):
+
+        @pl.when(pl.program_id(0) == 0)
+        def _():
+            for copy in copies[e]:
+                copy.wait()
+
         w_gate_up = w_ref[e, :, :128, :].reshape(WIDTH, 2 * FF)
         w_down = w_ref[e, :, 128:, :].reshape(FF, WIDTH)
         x = jnp.concatenate(picked_rows[e], axis=0).astype(bf16)
@@ -539,7 +547,7 @@
     pair = pl.BlockSpec((2, TOK, WIDTH), lambda i, o: (i, 0, 0))
     pair_of_all = pl.BlockSpec((2, TOK, WIDTH), lambda i, o: (i + 2 * half, 0, 0))
     whole = lambda shape: pl.BlockSpec(shape, lambda i, o: (0,) * len(shape))
-    routes = pl.BlockSpec((2, 16, 256), lambda i, o: (i, TOK // 16, 0))
+    routes = pl.BlockSpec((2, 16, 256), lambda i, o: (i + 2 * half, TOK // 16, 0))
     summed = pl.BlockSpec((2, PAY, WIDTH), lambda i, o: (i, 0, 0))
     kept = lambda n: pl.BlockSpec((2, STEP_ROWS, n), lambda i, o: (0, i + 2 * half, 0))
     part = jax.ShapeDtypeStruct((4, PAY, WIDTH), bf16)
@@ -552,8 +560,8 @@
             in_specs=[
                 pair,
                 pair,
-                pair,
-                pair,
+                pair_of_all,
+                pair_of_all,
                 routes,
                 routes,
                 whole((EXPERTS, WIDTH)),
@@ -773,7 +781,10 @@
     routes_rows = jnp.pad(routes[0].T.astype(bf16), ((0, 8), (0, WIDTH - TOK)))
     upstream_rows = jnp.concatenate([cotangent[0], routes_rows], axis=0)
     grad_across = send(upstream_rows, 1, 0)
-    rows_far, qkv, upstream_rows, grad_across = tie(rows_far, qkv, upstream_rows, grad_across)
+    rows_far, qkv, upstream_rows, grad_across, expert_rows = tie(
+        rows_far, qkv, upstream_rows, grad_across, expert_rows
+    )
+    experts = [experts, along_y(expert_rows)]
     rows_far = both_cores(rows_far)
     grad_near = [upstream_rows] + [send(upstream_rows, 0, b) for b in (1, 3, 2)]
     qkv = project(places[8:], rows_far, head_weights, gain_attn, table, (qkv,))
@@ -782,8 +793,7 @@
     gain_ffn = shared[:, WIDTH + EXPERTS].astype(f32)[None]
     grad_far = [grad_across, send(grad_across, 0, 1), send(grad_across, 0, 3)]
     attended_head, attended_t, lse = attend(qkv, begin)
-    grad_across, expert_rows, _ = tie(grad_across, expert_rows, attended_head)
-    experts = [experts, along_y(expert_rows)]
+    grad_across, _ = tie(grad_across, attended_head)
     grad_far = grad_far + [send(grad_across, 0, 2)]
     attended_head, shared = tie(attended_head, shared)
     attended = lax.all_to_all(attended_head, "seq", 0, 0, tiled=True)
@@ -791,15 +801,14 @@
     hidden, normed_ffn = hidden_of(attended, shared, rows, gain_ffn)
 
     ffn_near, ffn_across = gather_near(normed_ffn)
-    ffn_near, _ = tie(ffn_near, ffn_across)
+    grad_all = both_cores(grad_near + grad_far)
+    ffn_near, _, grad_all = tie(ffn_near, ffn_across, grad_all)
     ffn_near, ffn_far = both_cores(ffn_near), gather_far(ffn_across)
-    grad_near = both_cores(grad_near)
     own = jnp.stack([seq_index * 2, own_x])
-    near = run_experts(0, own, ffn_near, grad_near, experts, router_t, ())
+    near = run_experts(0, own, ffn_near, grad_all, experts, router_t, ())
     near_terms = sum_along_z(*near[:2])
     ffn_far = both_cores(ffn_far)
-    grad_far = both_cores(grad_far)
-    far = run_experts(1, own, ffn_far, grad_far, experts, router_t, near[2:])
+    far = run_experts(1, own, ffn_far, grad_all, experts, router_t, near[2:])
     far, near_terms = tie(far, near_terms)
     moved, saved = far[2:4], far[4:]
     far_other, moved_other = tie(swap_cores(far[1]), moved[1])

time: 494 us -> 503 us (1.018)
  the two profiles are of different devices: /device:TPU:0 before, /device:TPU:1 now
where the time goes in v9:
time: 503 us; the launch traced here: 494 us
  Pallas kernels  162 us (32%)
  starting transfers between devices  117 us (23%)
  waiting for transfers between devices  113 us (22%)
  other arithmetic  55.7 us (11%)
  local copies, waits for them, and re-layouts  30.5 us (6%)
  between operations  14.8 us (3%)
    ppermute x39, waiting for transfers between devices, send(): return lax.ppermute(rows, 'seq', shift_perm(a, b))  82.4 us
    ppermute x39, starting transfers between devices, send(): return lax.ppermute(rows, 'seq', shift_perm(a, b))  53.1 us
    pallas_call x2, Pallas kernels, run_experts(): pl.pallas_call(experts_kernel, grid_spec=pltpu.PrefetchScalarGridSpec(num...  43.9 us
    pallas_call x1, Pallas kernels, attend_back(): pl.pallas_call(attend_back_kernel, grid=(GROUP // BLOCK,), in_specs=[whol...  31 us
    convert_element_type x7, other arithmetic, add_low(): return sum([t.astype(f32) for t in terms]).astype(bf16)  21.2 us
    pallas_call x1, Pallas kernels, attend(): pl.pallas_call(attend_kernel, grid=(GROUP // BLOCK,), in_specs=[whole(GRO...  19.8 us
    pallas_call x2, Pallas kernels, project(): pl.pallas_call(project_kernel, grid_spec=pltpu.PrefetchScalarGridSpec(num...  16.6 us
    unnamed x84, local copies, waits for them, and re-layouts  16.2 us
  transfers between devices with their start and end apart: 61, of which 17 were waited for; matrix products, arithmetic and copies ran while one was open for 15% of the time, Pallas kernels for 33%

profile of v9, /device:TPU:1, one launch (start us, length us, event | category | flops | bytes accessed | tf_op | source)
XLA Modules:
  0.0 493.6 jit_solution(3350900674999543898)
XLA Ops:
  19.4 7.5 %all-to-all-start = ((bf16[128,8,256]{2,1,0:T(8,128)(2,1)}), bf16[128,8,256]{2,1,0:T(8,128)(2,1)S(1)}, u32[]{:S(2)}, u32[]{:S(2)}) async-start(bf16[128,8,256]{2,1,0:T(8,128)(2,1)} %bitcast.9), calls=%async_computation | async-start | bytes 1048576 | tf_op jit(solution)/shard_map/all_to_all | solution.py:760
  27.4 7.7 %subtract_cosine_fusion.table = f32[3584,128]{1,0:T(8,128)} fusion(f32[128]{0:T(128)S(1)} %get-tuple-element.303, f32[128]{0:T(128)S(1)} %get-tuple-element.304, f32[3584]{0:T(1024)S(1)} %get-tuple-element.298), kind=kLoop, calls=%fused_computation.8 | loop fusion | flops 917504 | bytes 1850368 | tf_op jit(solution)/shard_map/cos | solution.py:137
  35.1 7.3 %all-to-all-done = bf16[128,8,256]{2,1,0:T(8,128)(2,1)S(1)} async-done(((bf16[128,8,256]{2,1,0:T(8,128)(2,1)}), bf16[128,8,256]{2,1,0:T(8,128)(2,1)S(1)}, u32[]{:S(2)}, u32[]{:S(2)}) %all-to-all-start) | async-done | bytes 524320 | tf_op jit(solution)/shard_map/all_to_all | solution.py:760
  55.1 8.0 %shard_map.178.refs_0_ = bf16[3584,256]{1,0:T(8,128)(2,1)} custom-call(s32[8]{0:T(128)} %get-tuple-element.301.places, bf16[4,224,1024]{2,1,0:T(8,128)(2,1)} %copy-done.1, bf16[4,224,1024]{2,1,0:T(8,128)(2,1)} %collective-permute-done.7.other.near_other, bf16[1024,256]{1,0:T(8,128)(2,1)} %broadcast_select_fusion.w, f32[1,1024]{1,0:T(1,128)} %bitcast.198, ...), custom_call_target="tpu_custom_call" | custom-call | flops 939524096 | bytes 10485760 | tf_op jit(solution)/shard_map/pallas_call | solution.py:174
  63.1 13.8 %collective-permute-done.8 = bf16[240,1024]{1,0:T(8,128)(2,1)} collective-permute-done((bf16[240,1024]{1,0:T(8,128)(2,1)}, bf16[240,1024]{1,0:T(8,128)(2,1)}, u32[]{:S(2)}, u32[]{:S(2)}) %collective-permute-start.8) | collective-permute-done | bytes 491552 | tf_op jit(solution)/shard_map/ppermute | solution.py:52
  82.1 6.9 %all-to-all-start.1 = ((bf16[128,8,1152]{2,1,0:T(8,128)(2,1)}), bf16[128,8,1152]{2,1,0:T(8,128)(2,1)S(1)}, u32[]{:S(2)}, u32[]{:S(2)}) async-start(bf16[128,8,1152]{2,1,0:T(8,128)(2,1)} %broadcast_in_dim.101), calls=%async_computation.1 | async-start | bytes 4718592 | tf_op jit(solution)/shard_map/all_to_all | solution.py:778
  98.0 8.6 %shard_map.179.qkv_ref = bf16[3584,256]{1,0:T(8,128)(2,1)} custom-call(s32[8]{0:T(128)} %get-tuple-element.302.places, bf16[4,224,1024]{2,1,0:T(8,128)(2,1)} %pad_maximum_fusion.1.mine.far_mine, bf16[4,224,1024]{2,1,0:T(8,128)(2,1)} %collective-permute-done.10.other.far_other, bf16[1024,256]{1,0:T(8,128)(2,1)} %broadcast_select_fusion.w, ...), custom_call_target="tpu_custom_call" | custom-call | flops 939524096 | bytes 10485760 | tf_op jit(solution)/shard_map/pallas_call | solution.py:174
  106.6 19.8 %shard_map.180 = (bf16[16,64,224]{2,1,0:T(8,128)(2,1)}, f32[64,3584]{1,0:T(8,128)}, f32[1,3584]{1,0:T(1,128)}) custom-call(bf16[3584,256]{1,0:T(8,128)(2,1)} %shard_map.179.qkv_ref, s32[1,3584]{1,0:T(1,128)} %compare_select_fusion.begin_ref), custom_call_target="tpu_custom_call" | custom-call | flops 7247757312 | bytes 4194304 | tf_op jit(solution)/shard_map/pallas_call | solution.py:324
  129.0 15.4 %all-to-all-start.2 = ((bf16[16,64,224]{2,1,0:T(8,128)(2,1)}), bf16[16,64,224]{2,1,0:T(8,128)(2,1)S(1)}, u32[]{:S(2)}, u32[]{:S(2)}) async-start(bf16[16,64,224]{2,1,0:T(8,128)(2,1)} %get-tuple-element.154), calls=%async_computation.2 | async-start | bytes 1048576 | tf_op jit(solution)/shard_map/all_to_all | solution.py:799
  144.5 5.3 %collective-permute-done.14 = bf16[240,1024]{1,0:T(8,128)(2,1)} collective-permute-done((bf16[240,1024]{1,0:T(8,128)(2,1)}, bf16[240,1024]{1,0:T(8,128)(2,1)}, u32[]{:S(2)}, u32[]{:S(2)}) %collective-permute-start.14) | collective-permute-done | bytes 491552 | tf_op jit(solution)/shard_map/ppermute | solution.py:52
  149.8 14.0 %collective-permute-done.16 = bf16[240,1024]{1,0:T(8,128)(2,1)} collective-permute-done((bf16[240,1024]{1,0:T(8,128)(2,1)}, bf16[240,1024]{1,0:T(8,128)(2,1)}, u32[]{:S(2)}, u32[]{:S(2)}) %collective-permute-start.16) | collective-permute-done | bytes 491552 | tf_op jit(solution)/shard_map/ppermute | solution.py:52
  190.4 8.3 %collective-permute-done.17 = bf16[224,1024]{1,0:T(8,128)(2,1)S(1)} collective-permute-done((bf16[224,1024]{1,0:T(8,128)(2,1)}, bf16[224,1024]{1,0:T(8,128)(2,1)S(1)}, u32[]{:S(2)}, u32[]{:S(2)}) %collective-permute-start.17) | collective-permute-done | bytes 458784 | tf_op jit(solution)/shard_map/ppermute | solution.py:52
  198.7 12.2 %collective-permute-done.22 = bf16[224,1024]{1,0:T(8,128)(2,1)S(1)} collective-permute-done((bf16[224,1024]{1,0:T(8,128)(2,1)}, bf16[224,1024]{1,0:T(8,128)(2,1)S(1)}, u32[]{:S(2)}, u32[]{:S(2)}) %collective-permute-start.22) | collective-permute-done | bytes 458784 | tf_op jit(solution)/shard_map/ppermute | solution.py:52
  219.9 21.9 %shard_map.182 = (bf16[4,256,1024]{2,1,0:T(8,128)(2,1)}, bf16[4,256,1024]{2,1,0:T(8,128)(2,1)}, bf16[8,224,1024]{2,1,0:T(8,128)(2,1)}, bf16[8,224,1024]{2,1,0:T(...) custom-call(s32[2]{0:T(128)} %pad_add_fusion.own_ref, ...), custom_call_target="tpu_custom_call" | custom-call | flops 15032385536 | bytes 25165824 | tf_op jit(solution)/shard_map/pallas_call | solution.py:555
  253.4 22.0 %shard_map.183 = (bf16[4,256,1024]{2,1,0:T(8,128)(2,1)}, bf16[4,256,1024]{2,1,0:T(8,128)(2,1)}, bf16[8,224,1024]{2,1,0:T(8,128)(2,1)}, bf16[8,224,1024]{2,1,0:T(...) custom-call(s32[2]{0:T(128)} %pad_add_fusion.own_ref, ...), custom_call_target="tpu_custom_call", output_to_operand_aliasing={{2}: (10, {}), {3}: (11, {}), {4}: (12, {}), {5}: (13, {}),... | custom-call | flops 15032385536 | bytes 25165824 | tf_op jit(solution)/shard_map/pallas_call | solution.py:555
  277.2 4.0 collective-permute-done.31
  287.7 15.9 %shard_map.184 = bf16[4,2,2,192,1024]{4,3,2,1,0:T(8,128)(2,1)} custom-call(bf16[2,1152,1024]{2,1,0:T(8,128)(2,1)} %get-tuple-element.201.x_ref, bf16[2,1152,1024]{2,1,0:T(8,128)(2,1)} %get-tuple-element.202.dh_ref, bf16[2,1152,512]{2,1,0:T(8,128)(2,1)} %get-tuple-element.203.act_ref, bf16[2,1152,1024]{2,1,0:T(8,128)(2,1)} %get-tuple-element.204.dy_ref), custom_call_target="tpu_custom_call" | custom-call | flops 8589934592 | bytes 14680064 | tf_op jit(solution)/shard_map/pallas_call | solution.py:611
  303.6 7.3 %collective-permute-done.34 = bf16[256,1024]{1,0:T(8,128)(2,1)S(1)} collective-permute-done((bf16[256,1024]{1,0:T(8,128)(2,1)S(1)}, bf16[256,1024]{1,0:T(8,128)(2,1)S(1)}, u32[]{:S(2)}, u32[]{:S(2)}) %collective-permute-start.34) | collective-permute-done | bytes 524320 | tf_op jit(solution)/shard_map/ppermute | solution.py:52
  315.0 6.2 %fusion.10 = (bf16[2,224,1024]{2,1,0:T(8,128)(2,1)}, bf16[2,224,1024]{2,1,0:T(8,128)(2,1)}, bf16[2,224,1024]{2,1,0:T(8,128)(2,1)}, bf16[2,224,1024]{2,1,0:T(8,128)(2,1)S(1)}) fusion(bf16[2,4,224,1024]{3,2,1,0:T(8,128)(2,1)} %bitcast.53, bf16[2,4,224,1024]{3,2,1,0:T(8,128)(2,1)} %bitcast.181), kind=kLoop, calls=%fused_computation.34 | loop fusion | flops 7340032 | bytes 11010048 | tf_op jit(solution)/shard_map/convert_element_type | solution.py:83
  325.5 5.8 %shard_map.185 = (f32[224,1024]{1,0:T(8,128)}, bf16[224,1024]{1,0:T(8,128)(2,1)}, bf16[32,224]{1,0:T(8,128)(2,1)}, bf16[224,1024]{1,0:T(8,128)(2,1)}, bf16[16,64,224]{2,1,0:T(8,128)(2,1)}) custom-call(bf16[256,1024]{1,0:T(8,128)(2,1)} %get-tuple-element.193.t0, bf16[256,1024]{1,0:T(8,128)(2,1)} %copy-done.15, bf16[256,1024]{1,0:T(8,128)(2,1)} %copy-done.16, ...), custom_call_target="tpu_custom_call" | custom-call | flops 469762048 | bytes 8388608 | tf_op jit(solution)/shard_map/pallas_call | solution.py:682
  331.3 8.1 %all-to-all-start.3 = ((bf16[16,64,224]{2,1,0:T(8,128)(2,1)}), bf16[16,64,224]{2,1,0:T(8,128)(2,1)S(1)}, u32[]{:S(2)}, u32[]{:S(2)}) async-start(bf16[16,64,224]{2,1,0:T(8,128)(2,1)} %get-tuple-element.213), calls=%async_computation.3 | async-start | bytes 1048576 | tf_op jit(solution)/shard_map/all_to_all | solution.py:836
  339.4 4.0 shard_map.186
  343.4 7.3 %all-to-all-done.3.g_ref = bf16[16,64,224]{2,1,0:T(8,128)(2,1)S(1)} async-done(((bf16[16,64,224]{2,1,0:T(8,128)(2,1)}), bf16[16,64,224]{2,1,0:T(8,128)(2,1)S(1)}, u32[]{:S(2)}, u32[]{:S(2)}) %all-to-all-start.3) | async-done | bytes 458784 | tf_op jit(solution)/shard_map/all_to_all | solution.py:836
  358.2 31.0 %shard_map.187.first.second = bf16[3584,256]{1,0:T(8,128)(2,1)} custom-call(bf16[3584,256]{1,0:T(8,128)(2,1)} %shard_map.179.qkv_ref, bf16[16,64,224]{2,1,0:T(8,128)(2,1)} %copy-done.20, f32[64,3584]{1,0:T(8,128)} %get-tuple-element.222.ot_ref, f32[1,3584]{1,0:T(1,128)} %get-tuple-element.223.lse_ref, s32[1,3584]{1,0:T(1,128)} %compare_select_fusion.begin_ref, ...), custom_call_target="tpu_custom_call" | custom-call | flops 18119393280 | bytes 8388608 | tf_op jit(solution)/shard_map/pallas_call | solution.py:404
  389.2 5.4 %shard_map.188 = (bf16[4,224,1024]{2,1,0:T(8,128)(2,1)}, bf16[4,224,1024]{2,1,0:T(8,128)(2,1)}) custom-call(s32[8]{0:T(128)} %get-tuple-element.302.places, bf16[3584,256]{1,0:T(8,128)(2,1)} %shard_map.187.first.second, bf16[3584,256]{1,0:T(8,128)(2,1)} %shard_map.187.first.second, bf16[1024,256]{1,0:T(8,128)(2,1)} %broadcast_select_fusion.w), custom_call_target="tpu_custom_call" | custom-call | flops 939524096 | bytes 5242880 | tf_op jit(solution)/shard_map/pallas_call | solution.py:201
  394.6 4.9 collective-permute-done.38
  401.1 5.5 %shard_map.189 = (bf16[4,224,1024]{2,1,0:T(8,128)(2,1)}, bf16[4,224,1024]{2,1,0:T(8,128)(2,1)}) custom-call(s32[8]{0:T(128)} %get-tuple-element.301.places, bf16[3584,256]{1,0:T(8,128)(2,1)} %shard_map.187.first.second, bf16[3584,256]{1,0:T(8,128)(2,1)} %shard_map.187.first.second, bf16[1024,256]{1,0:T(8,128)(2,1)} %broadcast_select_fusion.w), custom_call_target="tpu_custom_call" | custom-call | flops 939524096 | bytes 5242880 | tf_op jit(solution)/shard_map/pallas_call | solution.py:201
  415.7 5.8 %all-to-all-start.6 = ((bf16[16,8,1152]{2,1,0:T(8,128)(2,1)}), bf16[16,8,1152]{2,1,0:T(8,128)(2,1)S(1)}, u32[]{:S(2)}, u32[]{:S(2)}) async-start(bf16[16,8,1152]{2,1,0:T(8,128)(2,1)} %bitcast.185), calls=%async_computation.7 | async-start | bytes 589824 | tf_op jit(solution)/shard_map/all_to_all | solution.py:857
  421.5 10.7 %shard_map.190 = bf16[1024,256]{1,0:T(8,128)(2,1)} custom-call(s32[16]{0:T(128)} %copy-done.31, bf16[4,224,1024]{2,1,0:T(8,128)(2,1)} %copy-done.1, bf16[4,224,1024]{2,1,0:T(8,128)(2,1)} %collective-permute-done.7.other.near_other, bf16[4,224,1024]{2,1,0:T(8,128)(2,1)} %pad_maximum_fusion.1.mine.far_mine, ...), custom_call_target="tpu_custom_call" | custom-call | flops 1879048192 | bytes 10485760 | tf_op jit(solution)/shard_map/pallas_call | solution.py:239
  434.7 4.9 all-to-all-done.6
  451.7 7.5 %all-to-all-start.5 = ((bf16[128,8,256]{2,1,0:T(8,128)(2,1)}), bf16[128,8,256]{2,1,0:T(8,128)(2,1)S(1)}, u32[]{:S(2)}, u32[]{:S(2)}) async-start(bf16[128,8,256]{2,1,0:T(8,128)(2,1)} %bitcast.71), calls=%async_computation.6 | async-start | bytes 1048576 | tf_op jit(solution)/shard_map/all_to_all | solution.py:861
  468.5 10.8 %collective-permute-done.49 = bf16[224,1024]{1,0:T(8,128)(2,1)} collective-permute-done((bf16[224,1024]{1,0:T(8,128)(2,1)}, bf16[224,1024]{1,0:T(8,128)(2,1)}, u32[]{:S(2)}, u32[]{:S(2)}) %collective-permute-start.49) | collective-permute-done | bytes 458784 | tf_op jit(solution)/shard_map/ppermute | solution.py:52
  (267 shorter events, 154.9 us)
Async XLA Ops:
  7.2 36.0 %collective-permute-start = (bf16[224,1024]{1,0:T(8,128)(2,1)}, bf16[224,1024]{1,0:T(8,128)(2,1)S(1)}, u32[]{:S(2)}, u32[]{:S(2)}) collective-permute-start(bf16[224,1024]{1,0:T(8,128)(2,1)} %bitcast.174), channel_id=1, source_target_pairs={{0,64},{8,72},{16,80},{24,88},{32,96},{40,104},{48,112},{56,120},{... | collective-permute-start | bytes 1376264 | tf_op jit(solution)/shard_map/ppermute | solution.py:52
  10.8 32.4 %collective-permute-start.4 = (bf16[224,1024]{1,0:T(8,128)(2,1)}, bf16[224,1024]{1,0:T(8,128)(2,1)S(1)}, u32[]{:S(2)}, u32[]{:S(2)}) collective-permute-start(bf16[224,1024]{1,0:T(8,128)(2,1)} %bitcast.175), channel_id=1, source_target_pairs={{0,16},{8,24},{16,32},{24,40},{32,48},{40,56},{48,0},{56,8},{64,80... | collective-permute-start | bytes 1376264 | tf_op jit(solution)/shard_map/ppermute | solution.py:52
  12.5 30.8 %collective-permute-start.5 = (bf16[224,1024]{1,0:T(8,128)(2,1)}, bf16[224,1024]{1,0:T(8,128)(2,1)S(1)}, u32[]{:S(2)}, u32[]{:S(2)}) collective-permute-start(bf16[224,1024]{1,0:T(8,128)(2,1)} %bitcast.176), channel_id=1, source_target_pairs={{0,48},{8,56},{16,0},{24,8},{32,16},{40,24},{48,32},{56,40},{64,11... | collective-permute-start | bytes 1376264 | tf_op jit(solution)/shard_map/ppermute | solution.py:52
  14.6 28.7 %collective-permute-start.6 = (bf16[224,1024]{1,0:T(8,128)(2,1)}, bf16[224,1024]{1,0:T(8,128)(2,1)S(1)}, u32[]{:S(2)}, u32[]{:S(2)}) collective-permute-start(bf16[224,1024]{1,0:T(8,128)(2,1)} %bitcast.177), channel_id=1, source_target_pairs={{0,32},{8,40},{16,48},{24,56},{32,0},{40,8},{48,16},{56,24},{64,96... | collective-permute-start | bytes 1376264 | tf_op jit(solution)/shard_map/ppermute | solution.py:52
  46.5 30.4 %collective-permute-start.9 = (bf16[2,192,1024]{2,1,0:T(8,128)(2,1)S(1)}, bf16[2,192,1024]{2,1,0:T(8,128)(2,1)}, u32[]{:S(2)}, u32[]{:S(2)}) collective-permute-start(bf16[2,192,1024]{2,1,0:T(8,128)(2,1)S(1)} %constant_dynamic-update-slice_fusion), channel_id=1, source_target_pairs={{0,1},{1,0},{2,3},{3,2},{4,5},{5,4},{6,7},{7,6},{8,9},{9,8},{10,11... | collective-permute-start | bytes 2359304 | tf_op jit(solution)/shard_map/ppermute | solution.py:99
  48.8 28.2 %collective-permute-start.8 = (bf16[240,1024]{1,0:T(8,128)(2,1)}, bf16[240,1024]{1,0:T(8,128)(2,1)}, u32[]{:S(2)}, u32[]{:S(2)}) collective-permute-start(bf16[240,1024]{1,0:T(8,128)(2,1)} %fusion.21), channel_id=1, source_target_pairs={{0,64},{8,72},{16,80},{24,88},{32,96},{40,104},{48,112},{56,120},{... | collective-permute-start | bytes 1474568 | tf_op jit(solution)/shard_map/ppermute | solution.py:52
  50.5 26.4 %collective-permute-start.1 = (bf16[224,1024]{1,0:T(8,128)(2,1)}, bf16[224,1024]{1,0:T(8,128)(2,1)}, u32[]{:S(2)}, u32[]{:S(2)}) collective-permute-start(bf16[224,1024]{1,0:T(8,128)(2,1)} %copy-done.21), channel_id=1, source_target_pairs={{0,16},{8,24},{16,32},{24,40},{32,48},{40,56},{48,0},{56,8},{64,80... | collective-permute-start | bytes 1376264 | tf_op jit(solution)/shard_map/ppermute | solution.py:52
  82.1 46.9 %all-to-all-start.1 = ((bf16[128,8,1152]{2,1,0:T(8,128)(2,1)}), bf16[128,8,1152]{2,1,0:T(8,128)(2,1)S(1)}, u32[]{:S(2)}, u32[]{:S(2)}) async-start(bf16[128,8,1152]{2,1,0:T(8,128)(2,1)} %broadcast_in_dim.101), calls=%async_computation.1 | async-start | bytes 4718592 | tf_op jit(solution)/shard_map/all_to_all | solution.py:778
  89.0 130.9 %all-gather.5.cloned.1.call-start = ((), (), s32[]{:S(2)}) async-start(), calls=%async_computation.9 | async-start | bytes 3932160 | tf_op jit(solution)/shard_map/all_gather | solution.py:770
  90.4 38.4 %collective-permute-start.11 = (bf16[240,1024]{1,0:T(8,128)(2,1)}, bf16[240,1024]{1,0:T(8,128)(2,1)S(1)}, u32[]{:S(2)}, u32[]{:S(2)}) collective-permute-start(bf16[240,1024]{1,0:T(8,128)(2,1)} %fusion.21), channel_id=1, source_target_pairs={{0,16},{8,24},{16,32},{24,40},{32,48},{40,56},{48,0},{56,8},{64,80... | collective-permute-start | bytes 1474568 | tf_op jit(solution)/shard_map/ppermute | solution.py:52
  91.9 52.6 %collective-permute-start.12 = (bf16[240,1024]{1,0:T(8,128)(2,1)}, bf16[240,1024]{1,0:T(8,128)(2,1)}, u32[]{:S(2)}, u32[]{:S(2)}) collective-permute-start(bf16[240,1024]{1,0:T(8,128)(2,1)} %fusion.21), channel_id=1, source_target_pairs={{0,48},{8,56},{16,0},{24,8},{32,16},{40,24},{48,32},{56,40},{64,11... | collective-permute-start | bytes 1474568 | tf_op jit(solution)/shard_map/ppermute | solution.py:52
  93.6 50.9 %collective-permute-start.13 = (bf16[240,1024]{1,0:T(8,128)(2,1)}, bf16[240,1024]{1,0:T(8,128)(2,1)}, u32[]{:S(2)}, u32[]{:S(2)}) collective-permute-start(bf16[240,1024]{1,0:T(8,128)(2,1)} %fusion.21), channel_id=1, source_target_pairs={{0,32},{8,40},{16,48},{24,56},{32,0},{40,8},{48,16},{56,24},{64,96... | collective-permute-start | bytes 1474568 | tf_op jit(solution)/shard_map/ppermute | solution.py:52
  95.1 54.7 %collective-permute-start.14 = (bf16[240,1024]{1,0:T(8,128)(2,1)}, bf16[240,1024]{1,0:T(8,128)(2,1)}, u32[]{:S(2)}, u32[]{:S(2)}) collective-permute-start(bf16[240,1024]{1,0:T(8,128)(2,1)} %collective-permute-done.8), channel_id=1, source_target_pairs={{0,16},{8,24},{16,32},{24,40},{32,48},{40,56},{48,0},{56,8},{64,80... | collective-permute-start | bytes 1474568 | tf_op jit(solution)/shard_map/ppermute | solution.py:52
  95.7 54.1 %collective-permute-start.15 = (bf16[240,1024]{1,0:T(8,128)(2,1)}, bf16[240,1024]{1,0:T(8,128)(2,1)}, u32[]{:S(2)}, u32[]{:S(2)}) collective-permute-start(bf16[240,1024]{1,0:T(8,128)(2,1)} %collective-permute-done.8), channel_id=1, source_target_pairs={{0,48},{8,56},{16,0},{24,8},{32,16},{40,24},{48,32},{56,40},{64,11... | collective-permute-start | bytes 1474568 | tf_op jit(solution)/shard_map/ppermute | solution.py:52
  128.7 35.1 %collective-permute-start.16 = (bf16[240,1024]{1,0:T(8,128)(2,1)}, bf16[240,1024]{1,0:T(8,128)(2,1)}, u32[]{:S(2)}, u32[]{:S(2)}) collective-permute-start(bf16[240,1024]{1,0:T(8,128)(2,1)} %collective-permute-done.8), channel_id=1, source_target_pairs={{0,32},{8,40},{16,48},{24,56},{32,0},{40,8},{48,16},{56,24},{64,96... | collective-permute-start | bytes 1474568 | tf_op jit(solution)/shard_map/ppermute | solution.py:52
  129.0 36.8 %all-to-all-start.2 = ((bf16[16,64,224]{2,1,0:T(8,128)(2,1)}), bf16[16,64,224]{2,1,0:T(8,128)(2,1)S(1)}, u32[]{:S(2)}, u32[]{:S(2)}) async-start(bf16[16,64,224]{2,1,0:T(8,128)(2,1)} %get-tuple-element.154), calls=%async_computation.2 | async-start | bytes 1048576 | tf_op jit(solution)/shard_map/all_to_all | solution.py:799
  144.4 75.5 %all-gather.7.cloned.1.call-start = ((), (), s32[]{:S(2)}) async-start(), calls=%async_computation.10 | async-start | bytes 3932160 | tf_op jit(solution)/shard_map/all_gather | solution.py:770
  179.9 30.9 %collective-permute-start.25 = (bf16[8,240,1024]{2,1,0:T(8,128)(2,1)}, bf16[8,240,1024]{2,1,0:T(8,128)(2,1)}, u32[]{:S(2)}, u32[]{:S(2)}) collective-permute-start(bf16[8,240,1024]{2,1,0:T(8,128)(2,1)} %bitcast_dynamic-update-slice_fusion.g_mine.routes_mine), channel_id=1, source_target_pairs={{0,8},{8,0},{16,24},{24,16},{32,40},{40,32},{48,56},{56,48},{64,72... | collective-permute-start | bytes 11796488 | tf_op jit(solution)/shard_map/ppermute | solution.py:56
  180.4 226.2 %reduce-scatter.2.cloned.1.call-start = ((), (), s32[]{:S(2)}) async-start(), calls=%async_computation.8 | async-start | bytes 7864320 | tf_op jit(solution)/shard_map/reduce_scatter | solution.py:829
  215.7 26.9 %collective-permute-start.18 = (bf16[224,1024]{1,0:T(8,128)(2,1)S(1)}, bf16[224,1024]{1,0:T(8,128)(2,1)S(1)}, u32[]{:S(2)}, u32[]{:S(2)}) collective-permute-start(bf16[224,1024]{1,0:T(8,128)(2,1)S(1)} %collective-permute-done.17), channel_id=1, source_target_pairs={{0,16},{8,24},{16,32},{24,40},{32,48},{40,56},{48,0},{56,8},{64,80... | collective-permute-start | bytes 1376264 | tf_op jit(solution)/shard_map/ppermute | solution.py:52
  248.4 27.0 %collective-permute-start.28 = (bf16[256,1024]{1,0:T(8,128)(2,1)}, bf16[256,1024]{1,0:T(8,128)(2,1)S(1)}, u32[]{:S(2)}, u32[]{:S(2)}) collective-permute-start(bf16[256,1024]{1,0:T(8,128)(2,1)} %get-tuple-element.285), channel_id=1, source_target_pairs={{0,48},{8,56},{16,0},{24,8},{32,16},{40,24},{48,32},{56,40},{64,11... | collective-permute-start | bytes 1572872 | tf_op jit(solution)/shard_map/ppermute | solution.py:52
  281.2 29.7 %collective-permute-start.35 = (bf16[8,224,1024]{2,1,0:T(8,128)(2,1)}, bf16[8,224,1024]{2,1,0:T(8,128)(2,1)}, u32[]{:S(2)}, u32[]{:S(2)}) collective-permute-start(bf16[8,224,1024]{2,1,0:T(8,128)(2,1)} %get-tuple-element.205), channel_id=1, source_target_pairs={{0,8},{8,0},{16,24},{24,16},{32,40},{40,32},{48,56},{56,48},{64,72... | collective-permute-start | bytes 11010056 | tf_op jit(solution)/shard_map/ppermute | solution.py:56
  351.6 48.0 %all-to-all-start.4 = ((bf16[8,128,1152]{2,1,0:T(8,128)(2,1)}), bf16[8,128,1152]{2,1,0:T(8,128)(2,1)S(1)}, u32[]{:S(2)}, u32[]{:S(2)}) async-start(bf16[8,128,1152]{2,1,0:T(8,128)(2,1)} %shard_map.186), calls=%async_computation.4 | async-start | bytes 4718592 | tf_op jit(solution)/shard_map/all_to_all | solution.py:843
  355.2 39.5 %collective-permute-start.37 = (bf16[2,224,1024]{2,1,0:T(8,128)(2,1)}, bf16[2,224,1024]{2,1,0:T(8,128)(2,1)}, u32[]{:S(2)}, u32[]{:S(2)}) collective-permute-start(bf16[2,224,1024]{2,1,0:T(8,128)(2,1)} %get-tuple-element.228), channel_id=1, source_target_pairs={{0,48},{8,56},{16,0},{24,8},{32,16},{40,24},{48,32},{56,40},{64,11... | collective-permute-start | bytes 2752520 | tf_op jit(solution)/shard_map/ppermute | solution.py:52
  356.9 42.6 %collective-permute-start.38 = (bf16[2,224,1024]{2,1,0:T(8,128)(2,1)}, bf16[2,224,1024]{2,1,0:T(8,128)(2,1)}, u32[]{:S(2)}, u32[]{:S(2)}) collective-permute-start(bf16[2,224,1024]{2,1,0:T(8,128)(2,1)} %get-tuple-element.229), channel_id=1, source_target_pairs={{0,16},{8,24},{16,32},{24,40},{32,48},{40,56},{48,0},{56,8},{64,80... | collective-permute-start | bytes 2752520 | tf_op jit(solution)/shard_map/ppermute | solution.py:52
  356.9 42.6 %collective-permute-start.39 = (bf16[2,224,1024]{2,1,0:T(8,128)(2,1)}, bf16[2,224,1024]{2,1,0:T(8,128)(2,1)}, u32[]{:S(2)}, u32[]{:S(2)}) collective-permute-start(bf16[2,224,1024]{2,1,0:T(8,128)(2,1)} %get-tuple-element.230), channel_id=1, source_target_pairs={{0,32},{8,40},{16,48},{24,56},{32,0},{40,8},{48,16},{56,24},{64,96... | collective-permute-start | bytes 2752520 | tf_op jit(solution)/shard_map/ppermute | solution.py:52
  406.6 35.1 %collective-permute-start.45 = (bf16[4,224,1024]{2,1,0:T(8,128)(2,1)}, bf16[4,224,1024]{2,1,0:T(8,128)(2,1)}, u32[]{:S(2)}, u32[]{:S(2)}) collective-permute-start(bf16[4,224,1024]{2,1,0:T(8,128)(2,1)} %get-tuple-element.252), channel_id=1, source_target_pairs={{0,8},{8,0},{16,24},{24,16},{32,40},{40,32},{48,56},{56,48},{64,72... | collective-permute-start | bytes 5505032 | tf_op jit(solution)/shard_map/ppermute | solution.py:56
  411.5 53.7 %collective-permute-start.50 = (bf16[2,192,1024]{2,1,0:T(8,128)(2,1)}, bf16[2,192,1024]{2,1,0:T(8,128)(2,1)}, u32[]{:S(2)}, u32[]{:S(2)}) collective-permute-start(bf16[2,192,1024]{2,1,0:T(8,128)(2,1)} %dynamic-slice_bitcast_fusion), channel_id=1, source_target_pairs={{0,1},{1,0},{2,3},{3,2},{4,5},{5,4},{6,7},{7,6},{8,9},{9,8},{10,11... | collective-permute-start | bytes 2359304 | tf_op jit(solution)/shard_map/ppermute | solution.py:99
  412.8 32.2 %collective-permute-start.42 = (bf16[224,1024]{1,0:T(8,128)(2,1)}, bf16[224,1024]{1,0:T(8,128)(2,1)}, u32[]{:S(2)}, u32[]{:S(2)}) collective-permute-start(bf16[224,1024]{1,0:T(8,128)(2,1)} %get-tuple-element.248), channel_id=1, source_target_pairs={{0,48},{8,56},{16,0},{24,8},{32,16},{40,24},{48,32},{56,40},{64,11... | collective-permute-start | bytes 1376264 | tf_op jit(solution)/shard_map/ppermute | solution.py:52
  412.9 32.1 %collective-permute-start.43 = (bf16[224,1024]{1,0:T(8,128)(2,1)}, bf16[224,1024]{1,0:T(8,128)(2,1)}, u32[]{:S(2)}, u32[]{:S(2)}) collective-permute-start(bf16[224,1024]{1,0:T(8,128)(2,1)} %get-tuple-element.249), channel_id=1, source_target_pairs={{0,16},{8,24},{16,32},{24,40},{32,48},{40,56},{48,0},{56,8},{64,80... | collective-permute-start | bytes 1376264 | tf_op jit(solution)/shard_map/ppermute | solution.py:52
  414.3 30.8 %collective-permute-start.44 = (bf16[224,1024]{1,0:T(8,128)(2,1)}, bf16[224,1024]{1,0:T(8,128)(2,1)}, u32[]{:S(2)}, u32[]{:S(2)}) collective-permute-start(bf16[224,1024]{1,0:T(8,128)(2,1)} %get-tuple-element.250), channel_id=1, source_target_pairs={{0,32},{8,40},{16,48},{24,56},{32,0},{40,8},{48,16},{56,24},{64,96... | collective-permute-start | bytes 1376264 | tf_op jit(solution)/shard_map/ppermute | solution.py:52
  451.7 29.3 %all-to-all-start.5 = ((bf16[128,8,256]{2,1,0:T(8,128)(2,1)}), bf16[128,8,256]{2,1,0:T(8,128)(2,1)S(1)}, u32[]{:S(2)}, u32[]{:S(2)}) async-start(bf16[128,8,256]{2,1,0:T(8,128)(2,1)} %bitcast.71), calls=%async_computation.6 | async-start | bytes 1048576 | tf_op jit(solution)/shard_map/all_to_all | solution.py:861
  (66 other events, 868.2 us)
Sparse Core Ops, SparseCore 0:
  91.5 51.5 all-gather.4
  180.5 38.4 all-gather.6
  311.1 88.1 reduce-scatter.1

commit v10 on v9

--- a/solution.py
+++ b/solution.py
@@ -547,7 +547,7 @@
     pair = pl.BlockSpec((2, TOK, WIDTH), lambda i, o: (i, 0, 0))
     pair_of_all = pl.BlockSpec((2, TOK, WIDTH), lambda i, o: (i + 2 * half, 0, 0))
     whole = lambda shape: pl.BlockSpec(shape, lambda i, o: (0,) * len(shape))
-    routes = pl.BlockSpec((2, 16, 256), lambda i, o: (i + 2 * half, TOK // 16, 0))
+    routes = pl.BlockSpec((2, 16, 256), lambda i, o: (i, TOK // 16, 0))
     summed = pl.BlockSpec((2, PAY, WIDTH), lambda i, o: (i, 0, 0))
     kept = lambda n: pl.BlockSpec((2, STEP_ROWS, n), lambda i, o: (0, i + 2 * half, 0))
     part = jax.ShapeDtypeStruct((4, PAY, WIDTH), bf16)
@@ -560,8 +560,8 @@
             in_specs=[
                 pair,
                 pair,
-                pair_of_all,
-                pair_of_all,
+                pair,
+                pair,
                 routes,
                 routes,
                 whole((EXPERTS, WIDTH)),
@@ -780,10 +780,7 @@
     ).reshape(WIDTH, 1152)
     routes_rows = jnp.pad(routes[0].T.astype(bf16), ((0, 8), (0, WIDTH - TOK)))
     upstream_rows = jnp.concatenate([cotangent[0], routes_rows], axis=0)
-    grad_across = send(upstream_rows, 1, 0)
-    rows_far, qkv, upstream_rows, grad_across, expert_rows = tie(
-        rows_far, qkv, upstream_rows, grad_across, expert_rows
-    )
+    rows_far, qkv, upstream_rows, expert_rows = tie(rows_far, qkv, upstream_rows, expert_rows)
     experts = [experts, along_y(expert_rows)]
     rows_far = both_cores(rows_far)
     grad_near = [upstream_rows] + [send(upstream_rows, 0, b) for b in (1, 3, 2)]
@@ -791,24 +788,24 @@
 
     router_t = shared[:, WIDTH : WIDTH + EXPERTS].T
     gain_ffn = shared[:, WIDTH + EXPERTS].astype(f32)[None]
-    grad_far = [grad_across, send(grad_across, 0, 1), send(grad_across, 0, 3)]
     attended_head, attended_t, lse = attend(qkv, begin)
-    grad_across, _ = tie(grad_across, attended_head)
-    grad_far = grad_far + [send(grad_across, 0, 2)]
     attended_head, shared = tie(attended_head, shared)
     attended = lax.all_to_all(attended_head, "seq", 0, 0, tiled=True)
-    attended, grad_near, grad_far = tie(attended, grad_near, grad_far)
+    attended, grad_near = tie(attended, grad_near)
+    grad_near = jnp.stack(grad_near)
     hidden, normed_ffn = hidden_of(attended, shared, rows, gain_ffn)
-
     ffn_near, ffn_across = gather_near(normed_ffn)
-    grad_all = both_cores(grad_near + grad_far)
-    ffn_near, _, grad_all = tie(ffn_near, ffn_across, grad_all)
+    ffn_near, _ = tie(ffn_near, ffn_across)
+    grad_near_mine, _ = tie(grad_near, ffn_across)
+    grad_far = send(grad_near_mine, 1, 0)
+    grad_near = (grad_near, swap_cores(grad_near))
     ffn_near, ffn_far = both_cores(ffn_near), gather_far(ffn_across)
     own = jnp.stack([seq_index * 2, own_x])
-    near = run_experts(0, own, ffn_near, grad_all, experts, router_t, ())
+    near = run_experts(0, own, ffn_near, grad_near, experts, router_t, ())
     near_terms = sum_along_z(*near[:2])
     ffn_far = both_cores(ffn_far)
-    far = run_experts(1, own, ffn_far, grad_all, experts, router_t, near[2:])
+    grad_far = (grad_far, swap_cores(grad_far))
+    far = run_experts(1, own, ffn_far, grad_far, experts, router_t, near[2:])
     far, near_terms = tie(far, near_terms)
     moved, saved = far[2:4], far[4:]
     far_other, moved_other = tie(swap_cores(far[1]), moved[1])
@@ -860,7 +857,9 @@
     near_terms = send_along_z(near_parts)
     grad_heads = lax.all_to_all(grad_head.reshape(128, 8, 256), BOTH, 0, 0, tiled=True)
     crossed = send(add_low(*far_terms), 1, 0)
-    crossed, near_terms, grad_heads = tie(crossed, near_terms, grad_heads)
+    crossed, near_terms, grad_heads, shared_grads = tie(
+        crossed, near_terms, grad_heads, shared_grads
+    )
     kept = lax.dynamic_index_in_dim(expert_grads, own_x, 0, keepdims=False)
     sent = lax.dynamic_index_in_dim(expert_grads, 1 - own_x, 0, keepdims=False)
     expert_grads = kept.astype(f32) + swap_x(sent).astype(f32)

time: 503 us -> 476 us (0.946)
  local copies, waits for them, and re-layouts: 30.5 us -> 20.1 us
  starting transfers between devices: 117 us -> 107 us
  waiting for transfers between devices: 113 us -> 107 us
    unnamed x84 -> x85, local copies, waits for them, and re-layouts: 16.2 us -> 6.94 us
    all_to_all x1, starting transfers between devices: 15.4 us -> 6.36 us  [local(): attended = lax.all_to_all(attended_head, 'seq', 0, 0, tiled=True)]
    ppermute x39 -> x36, waiting for transfers between devices: 82.4 us -> 75.2 us  [send(): return lax.ppermute(rows, 'seq', shift_perm(a, b))]
    ppermute x2, waiting for transfers between devices: 0.01 us -> 6.26 us  [swap_x(): return lax.ppermute(rows, 'wshard', [(w, w ^ 1) for w in range(8)])]
    ppermute x39 -> x36, starting transfers between devices: 53.1 us -> 47.4 us  [send(): return lax.ppermute(rows, 'seq', shift_perm(a, b))]
    ppermute x10 -> x11, starting transfers between devices: 7.67 us -> 10.2 us  [swap_cores(): return lax.ppermute(rows, 'seq', CORE_PERM)]
  transfers between devices with their start and end apart: 61 -> 59, of which waited for: 17 -> 18; matrix products, arithmetic and copies ran while one was open for 15% -> 13% of each run, Pallas kernels for 33% -> 35%
where the time goes in v10:
time: 476 us; the launch traced here: 467 us
  Pallas kernels  162 us (34%)
  starting transfers between devices  107 us (22%)
  waiting for transfers between devices  107 us (22%)
  other arithmetic  56.2 us (12%)
  local copies, waits for them, and re-layouts  20.1 us (4%)
  between operations  14.8 us (3%)
    ppermute x36, waiting for transfers between devices, send(): return lax.ppermute(rows, 'seq', shift_perm(a, b))  75.2 us
    ppermute x36, starting transfers between devices, send(): return lax.ppermute(rows, 'seq', shift_perm(a, b))  47.4 us
    pallas_call x2, Pallas kernels, run_experts(): pl.pallas_call(experts_kernel, grid_spec=pltpu.PrefetchScalarGridSpec(num...  43.9 us
    pallas_call x1, Pallas kernels, attend_back(): pl.pallas_call(attend_back_kernel, grid=(GROUP // BLOCK,), in_specs=[whol...  31 us
    convert_element_type x7, other arithmetic, add_low(): return sum([t.astype(f32) for t in terms]).astype(bf16)  21.2 us
    pallas_call x1, Pallas kernels, attend(): pl.pallas_call(attend_kernel, grid=(GROUP // BLOCK,), in_specs=[whole(GRO...  19.9 us
    pallas_call x2, Pallas kernels, project(): pl.pallas_call(project_kernel, grid_spec=pltpu.PrefetchScalarGridSpec(num...  16.6 us
    pallas_call x1, Pallas kernels, expert_weight_grads(): pl.pallas_call(expert_grads_kernel, grid=(2, 4), in_specs=[pl.BlockSpec((...  15.9 us
  transfers between devices with their start and end apart: 59, of which 18 were waited for; matrix products, arithmetic and copies ran while one was open for 13% of the time, Pallas kernels for 35%

profile of v10, /device:TPU:1, one launch (start us, length us, event | category | flops | bytes accessed | tf_op | source)
XLA Modules:
  0.0 467.3 jit_solution(18409629374422780813)
XLA Ops:
  19.4 7.5 %all-to-all-start = ((bf16[128,8,256]{2,1,0:T(8,128)(2,1)}), bf16[128,8,256]{2,1,0:T(8,128)(2,1)S(1)}, u32[]{:S(2)}, u32[]{:S(2)}) async-start(bf16[128,8,256]{2,1,0:T(8,128)(2,1)} %bitcast.9), calls=%async_computation | async-start | bytes 1048576 | tf_op jit(solution)/shard_map/all_to_all | solution.py:760
  29.0 7.7 %subtract_cosine_fusion.table = f32[3584,128]{1,0:T(8,128)} fusion(f32[128]{0:T(128)S(1)} %get-tuple-element.291, f32[128]{0:T(128)S(1)} %get-tuple-element.292, f32[3584]{0:T(1024)S(1)} %get-tuple-element.286), kind=kLoop, calls=%fused_computation.9 | loop fusion | flops 917504 | bytes 1850368 | tf_op jit(solution)/shard_map/cos | solution.py:137
  36.7 5.7 %all-to-all-done = bf16[128,8,256]{2,1,0:T(8,128)(2,1)S(1)} async-done(((bf16[128,8,256]{2,1,0:T(8,128)(2,1)}), bf16[128,8,256]{2,1,0:T(8,128)(2,1)S(1)}, u32[]{:S(2)}, u32[]{:S(2)}) %all-to-all-start) | async-done | bytes 524320 | tf_op jit(solution)/shard_map/all_to_all | solution.py:760
  51.8 8.0 %shard_map.178.refs_0_ = bf16[3584,256]{1,0:T(8,128)(2,1)} custom-call(s32[8]{0:T(128)} %get-tuple-element.289.places, bf16[4,224,1024]{2,1,0:T(8,128)(2,1)} %copy-done.1, bf16[4,224,1024]{2,1,0:T(8,128)(2,1)} %collective-permute-done.7.other.near_other, bf16[1024,256]{1,0:T(8,128)(2,1)} %broadcast_select_fusion.w, f32[1,1024]{1,0:T(1,128)} %bitcast.188, ...), custom_call_target="tpu_custom_call" | custom-call | flops 939524096 | bytes 10485760 | tf_op jit(solution)/shard_map/pallas_call | solution.py:174
  59.8 6.3 %collective-permute-done.8 = bf16[2,192,1024]{2,1,0:T(8,128)(2,1)} collective-permute-done((bf16[2,192,1024]{2,1,0:T(8,128)(2,1)}, bf16[2,192,1024]{2,1,0:T(8,128)(2,1)}, u32[]{:S(2)}, u32[]{:S(2)}) %collective-permute-start.8) | collective-permute-done | bytes 786464 | tf_op jit(solution)/shard_map/ppermute | solution.py:99
  75.8 7.9 %all-to-all-start.1 = ((bf16[128,8,1152]{2,1,0:T(8,128)(2,1)}), bf16[128,8,1152]{2,1,0:T(8,128)(2,1)S(1)}, u32[]{:S(2)}, u32[]{:S(2)}) async-start(bf16[128,8,1152]{2,1,0:T(8,128)(2,1)} %broadcast_in_dim.101), calls=%async_computation.1 | async-start | bytes 4718592 | tf_op jit(solution)/shard_map/all_to_all | solution.py:778
  90.0 8.6 %shard_map.179.qkv_ref = bf16[3584,256]{1,0:T(8,128)(2,1)} custom-call(s32[8]{0:T(128)} %get-tuple-element.290.places, bf16[4,224,1024]{2,1,0:T(8,128)(2,1)} %pad_maximum_fusion.2.mine.far_mine, bf16[4,224,1024]{2,1,0:T(8,128)(2,1)} %collective-permute-done.9.other.far_other, bf16[1024,256]{1,0:T(8,128)(2,1)} %broadcast_select_fusion.w, ...), custom_call_target="tpu_custom_call" | custom-call | flops 939524096 | bytes 10485760 | tf_op jit(solution)/shard_map/pallas_call | solution.py:174
  98.6 19.9 %shard_map.180 = (bf16[16,64,224]{2,1,0:T(8,128)(2,1)}, f32[64,3584]{1,0:T(8,128)}, f32[1,3584]{1,0:T(1,128)}) custom-call(bf16[3584,256]{1,0:T(8,128)(2,1)} %shard_map.179.qkv_ref, s32[1,3584]{1,0:T(1,128)} %compare_select_fusion.begin_ref), custom_call_target="tpu_custom_call" | custom-call | flops 7247757312 | bytes 4194304 | tf_op jit(solution)/shard_map/pallas_call | solution.py:324
  118.5 6.4 %all-to-all-start.2 = ((bf16[16,64,224]{2,1,0:T(8,128)(2,1)}), bf16[16,64,224]{2,1,0:T(8,128)(2,1)S(1)}, u32[]{:S(2)}, u32[]{:S(2)}) async-start(bf16[16,64,224]{2,1,0:T(8,128)(2,1)} %get-tuple-element.148), calls=%async_computation.2 | async-start | bytes 1048576 | tf_op jit(solution)/shard_map/all_to_all | solution.py:793
  125.8 10.9 %collective-permute-done.12 = bf16[240,1024]{1,0:T(8,128)(2,1)} collective-permute-done((bf16[240,1024]{1,0:T(8,128)(2,1)S(1)}, bf16[240,1024]{1,0:T(8,128)(2,1)}, u32[]{:S(2)}, u32[]{:S(2)}) %collective-permute-start.12) | collective-permute-done | bytes 491552 | tf_op jit(solution)/shard_map/ppermute | solution.py:52
  152.5 5.3 %collective-permute-done.13 = bf16[224,1024]{1,0:T(8,128)(2,1)S(1)} collective-permute-done((bf16[224,1024]{1,0:T(8,128)(2,1)}, bf16[224,1024]{1,0:T(8,128)(2,1)S(1)}, u32[]{:S(2)}, u32[]{:S(2)}) %collective-permute-start.13) | collective-permute-done | bytes 458784 | tf_op jit(solution)/shard_map/ppermute | solution.py:52
  159.7 9.7 %collective-permute-done.22 = bf16[224,1024]{1,0:T(8,128)(2,1)S(1)} collective-permute-done((bf16[224,1024]{1,0:T(8,128)(2,1)}, bf16[224,1024]{1,0:T(8,128)(2,1)S(1)}, u32[]{:S(2)}, u32[]{:S(2)}) %collective-permute-start.22) | collective-permute-done | bytes 458784 | tf_op jit(solution)/shard_map/ppermute | solution.py:52
  179.6 21.9 %shard_map.182 = (bf16[4,256,1024]{2,1,0:T(8,128)(2,1)}, bf16[4,256,1024]{2,1,0:T(8,128)(2,1)}, bf16[8,224,1024]{2,1,0:T(8,128)(2,1)}, bf16[8,224,1024]{2,1,0:T(...) custom-call(s32[2]{0:T(128)} %pad_add_fusion.own_ref, ...), custom_call_target="tpu_custom_call" | custom-call | flops 15032385536 | bytes 25165824 | tf_op jit(solution)/shard_map/pallas_call | solution.py:555
  202.4 16.7 %collective-permute-done.18.g_mine.routes_mine = bf16[4,240,1024]{2,1,0:T(8,128)(2,1)} collective-permute-done((bf16[4,240,1024]{2,1,0:T(8,128)(2,1)S(1)}, bf16[4,240,1024]{2,1,0:T(8,128)(2,1)}, u32[]{:S(2)}, u32[]{:S(2)}) %collective-permute-start.18) | collective-permute-done | bytes 1966112 | tf_op jit(solution)/shard_map/ppermute | solution.py:52
  230.0 22.0 %shard_map.183 = (bf16[4,256,1024]{2,1,0:T(8,128)(2,1)}, bf16[4,256,1024]{2,1,0:T(8,128)(2,1)}, bf16[8,224,1024]{2,1,0:T(8,128)(2,1)}, bf16[8,224,1024]{2,1,0:T(...) custom-call(s32[2]{0:T(128)} %pad_add_fusion.own_ref, ...), custom_call_target="tpu_custom_call", output_to_operand_aliasing={{2}: (10, {}), {3}: (11, {}), {4}: (12, {}), {5}: (13, {}),... | custom-call | flops 15032385536 | bytes 25165824 | tf_op jit(solution)/shard_map/pallas_call | solution.py:555
  264.9 15.9 %shard_map.184 = bf16[4,2,2,192,1024]{4,3,2,1,0:T(8,128)(2,1)} custom-call(bf16[2,1152,1024]{2,1,0:T(8,128)(2,1)} %get-tuple-element.188.x_ref, bf16[2,1152,1024]{2,1,0:T(8,128)(2,1)} %get-tuple-element.189.dh_ref, bf16[2,1152,512]{2,1,0:T(8,128)(2,1)} %get-tuple-element.190.act_ref, bf16[2,1152,1024]{2,1,0:T(8,128)(2,1)} %get-tuple-element.191.dy_ref), custom_call_target="tpu_custom_call" | custom-call | flops 8589934592 | bytes 14680064 | tf_op jit(solution)/shard_map/pallas_call | solution.py:611
  280.8 7.3 %collective-permute-done.32 = bf16[256,1024]{1,0:T(8,128)(2,1)S(1)} collective-permute-done((bf16[256,1024]{1,0:T(8,128)(2,1)S(1)}, bf16[256,1024]{1,0:T(8,128)(2,1)S(1)}, u32[]{:S(2)}, u32[]{:S(2)}) %collective-permute-start.32) | collective-permute-done | bytes 524320 | tf_op jit(solution)/shard_map/ppermute | solution.py:52
  290.0 6.1 %fusion.10 = (bf16[2,224,1024]{2,1,0:T(8,128)(2,1)}, bf16[2,224,1024]{2,1,0:T(8,128)(2,1)}, bf16[2,224,1024]{2,1,0:T(8,128)(2,1)}, bf16[2,224,1024]{2,1,0:T(8,128)(2,1)S(1)}) fusion(bf16[2,4,224,1024]{3,2,1,0:T(8,128)(2,1)} %bitcast.49, bf16[2,4,224,1024]{3,2,1,0:T(8,128)(2,1)} %bitcast.169), kind=kLoop, calls=%fused_computation.35 | loop fusion | flops 7340032 | bytes 11010048 | tf_op jit(solution)/shard_map/convert_element_type | solution.py:83
  296.1 6.5 %collective-permute-done.34.crossed = bf16[256,1024]{1,0:T(8,128)(2,1)S(1)} collective-permute-done((bf16[256,1024]{1,0:T(8,128)(2,1)S(1)}, bf16[256,1024]{1,0:T(8,128)(2,1)S(1)}, u32[]{:S(2)}, u32[]{:S(2)}) %collective-permute-start.34) | collective-permute-done | bytes 524320 | tf_op jit(solution)/shard_map/ppermute | solution.py:52
  303.4 5.9 %shard_map.185 = (f32[224,1024]{1,0:T(8,128)}, bf16[224,1024]{1,0:T(8,128)(2,1)}, bf16[32,224]{1,0:T(8,128)(2,1)}, bf16[224,1024]{1,0:T(8,128)(2,1)}, bf16[16,64,224]{2,1,0:T(8,128)(2,1)}) custom-call(bf16[256,1024]{1,0:T(8,128)(2,1)} %get-tuple-element.180.t0, bf16[256,1024]{1,0:T(8,128)(2,1)} %copy-done.16, bf16[256,1024]{1,0:T(8,128)(2,1)} %copy-done.17, ...), custom_call_target="tpu_custom_call" | custom-call | flops 469762048 | bytes 8388608 | tf_op jit(solution)/shard_map/pallas_call | solution.py:682
  309.4 5.2 %all-to-all-start.3 = ((bf16[16,64,224]{2,1,0:T(8,128)(2,1)}), bf16[16,64,224]{2,1,0:T(8,128)(2,1)S(1)}, u32[]{:S(2)}, u32[]{:S(2)}) async-start(bf16[16,64,224]{2,1,0:T(8,128)(2,1)} %get-tuple-element.200), calls=%async_computation.3 | async-start | bytes 1048576 | tf_op jit(solution)/shard_map/all_to_all | solution.py:833
  318.5 7.5 %all-to-all-done.3.g_ref = bf16[16,64,224]{2,1,0:T(8,128)(2,1)S(1)} async-done(((bf16[16,64,224]{2,1,0:T(8,128)(2,1)}), bf16[16,64,224]{2,1,0:T(8,128)(2,1)S(1)}, u32[]{:S(2)}, u32[]{:S(2)}) %all-to-all-start.3) | async-done | bytes 458784 | tf_op jit(solution)/shard_map/all_to_all | solution.py:833
  326.8 4.7 all-to-all-start.4
  334.4 31.0 %shard_map.187.first.second = bf16[3584,256]{1,0:T(8,128)(2,1)} custom-call(bf16[3584,256]{1,0:T(8,128)(2,1)} %shard_map.179.qkv_ref, bf16[16,64,224]{2,1,0:T(8,128)(2,1)} %copy-done.21, f32[64,3584]{1,0:T(8,128)} %get-tuple-element.209.ot_ref, f32[1,3584]{1,0:T(1,128)} %get-tuple-element.210.lse_ref, s32[1,3584]{1,0:T(1,128)} %compare_select_fusion.begin_ref, ...), custom_call_target="tpu_custom_call" | custom-call | flops 18119393280 | bytes 8388608 | tf_op jit(solution)/shard_map/pallas_call | solution.py:404
  365.4 5.4 %shard_map.188 = (bf16[4,224,1024]{2,1,0:T(8,128)(2,1)}, bf16[4,224,1024]{2,1,0:T(8,128)(2,1)}) custom-call(s32[8]{0:T(128)} %get-tuple-element.290.places, bf16[3584,256]{1,0:T(8,128)(2,1)} %shard_map.187.first.second, bf16[3584,256]{1,0:T(8,128)(2,1)} %shard_map.187.first.second, bf16[1024,256]{1,0:T(8,128)(2,1)} %broadcast_select_fusion.w), custom_call_target="tpu_custom_call" | custom-call | flops 939524096 | bytes 5242880 | tf_op jit(solution)/shard_map/pallas_call | solution.py:201
  370.8 4.6 collective-permute-done.36
  377.3 5.4 %shard_map.189 = (bf16[4,224,1024]{2,1,0:T(8,128)(2,1)}, bf16[4,224,1024]{2,1,0:T(8,128)(2,1)}) custom-call(s32[8]{0:T(128)} %get-tuple-element.289.places, bf16[3584,256]{1,0:T(8,128)(2,1)} %shard_map.187.first.second, bf16[3584,256]{1,0:T(8,128)(2,1)} %shard_map.187.first.second, bf16[1024,256]{1,0:T(8,128)(2,1)} %broadcast_select_fusion.w), custom_call_target="tpu_custom_call" | custom-call | flops 939524096 | bytes 5242880 | tf_op jit(solution)/shard_map/pallas_call | solution.py:201
  392.1 6.4 %all-to-all-start.6 = ((bf16[16,8,1152]{2,1,0:T(8,128)(2,1)}), bf16[16,8,1152]{2,1,0:T(8,128)(2,1)}, u32[]{:S(2)}, u32[]{:S(2)}) async-start(bf16[16,8,1152]{2,1,0:T(8,128)(2,1)} %bitcast.174), calls=%async_computation.7 | async-start | bytes 589824 | tf_op jit(solution)/shard_map/all_to_all | solution.py:854
  400.1 10.9 %shard_map.190 = bf16[1024,256]{1,0:T(8,128)(2,1)} custom-call(s32[16]{0:T(128)} %copy-done.35, bf16[4,224,1024]{2,1,0:T(8,128)(2,1)} %copy-done.1, bf16[4,224,1024]{2,1,0:T(8,128)(2,1)} %collective-permute-done.7.other.near_other, bf16[4,224,1024]{2,1,0:T(8,128)(2,1)} %pad_maximum_fusion.2.mine.far_mine, ...), custom_call_target="tpu_custom_call" | custom-call | flops 1879048192 | bytes 10485760 | tf_op jit(solution)/shard_map/pallas_call | solution.py:239
  427.4 9.0 %all-to-all-start.5 = ((bf16[128,8,256]{2,1,0:T(8,128)(2,1)}), bf16[128,8,256]{2,1,0:T(8,128)(2,1)S(1)}, u32[]{:S(2)}, u32[]{:S(2)}) async-start(bf16[128,8,256]{2,1,0:T(8,128)(2,1)} %bitcast.67), calls=%async_computation.6 | async-start | bytes 1048576 | tf_op jit(solution)/shard_map/all_to_all | solution.py:858
  442.5 4.6 collective-permute-done.47
  447.2 4.5 all-to-all-done.5
  (264 shorter events, 147.1 us)
Async XLA Ops:
  7.2 36.0 %collective-permute-start = (bf16[224,1024]{1,0:T(8,128)(2,1)}, bf16[224,1024]{1,0:T(8,128)(2,1)S(1)}, u32[]{:S(2)}, u32[]{:S(2)}) collective-permute-start(bf16[224,1024]{1,0:T(8,128)(2,1)} %bitcast.162), channel_id=1, source_target_pairs={{0,64},{8,72},{16,80},{24,88},{32,96},{40,104},{48,112},{56,120},{... | collective-permute-start | bytes 1376264 | tf_op jit(solution)/shard_map/ppermute | solution.py:52
  10.8 32.4 %collective-permute-start.4 = (bf16[224,1024]{1,0:T(8,128)(2,1)}, bf16[224,1024]{1,0:T(8,128)(2,1)S(1)}, u32[]{:S(2)}, u32[]{:S(2)}) collective-permute-start(bf16[224,1024]{1,0:T(8,128)(2,1)} %bitcast.163), channel_id=1, source_target_pairs={{0,16},{8,24},{16,32},{24,40},{32,48},{40,56},{48,0},{56,8},{64,80... | collective-permute-start | bytes 1376264 | tf_op jit(solution)/shard_map/ppermute | solution.py:52
  12.5 30.8 %collective-permute-start.5 = (bf16[224,1024]{1,0:T(8,128)(2,1)}, bf16[224,1024]{1,0:T(8,128)(2,1)S(1)}, u32[]{:S(2)}, u32[]{:S(2)}) collective-permute-start(bf16[224,1024]{1,0:T(8,128)(2,1)} %bitcast.164), channel_id=1, source_target_pairs={{0,48},{8,56},{16,0},{24,8},{32,16},{40,24},{48,32},{56,40},{64,11... | collective-permute-start | bytes 1376264 | tf_op jit(solution)/shard_map/ppermute | solution.py:52
  14.6 28.7 %collective-permute-start.6 = (bf16[224,1024]{1,0:T(8,128)(2,1)}, bf16[224,1024]{1,0:T(8,128)(2,1)S(1)}, u32[]{:S(2)}, u32[]{:S(2)}) collective-permute-start(bf16[224,1024]{1,0:T(8,128)(2,1)} %bitcast.165), channel_id=1, source_target_pairs={{0,32},{8,40},{16,48},{24,56},{32,0},{40,8},{48,16},{56,24},{64,96... | collective-permute-start | bytes 1376264 | tf_op jit(solution)/shard_map/ppermute | solution.py:52
  26.9 152.7 %all-gather.5.cloned.1.call-start = ((), (), s32[]{:S(2)}) async-start(), calls=%async_computation.9 | async-start | bytes 3932160 | tf_op jit(solution)/shard_map/all_gather | solution.py:770
  75.8 42.7 %all-to-all-start.1 = ((bf16[128,8,1152]{2,1,0:T(8,128)(2,1)}), bf16[128,8,1152]{2,1,0:T(8,128)(2,1)S(1)}, u32[]{:S(2)}, u32[]{:S(2)}) async-start(bf16[128,8,1152]{2,1,0:T(8,128)(2,1)} %broadcast_in_dim.101), calls=%async_computation.1 | async-start | bytes 4718592 | tf_op jit(solution)/shard_map/all_to_all | solution.py:778
  83.7 95.9 %all-gather.7.cloned.1.call-start = ((), (), s32[]{:S(2)}) async-start(), calls=%async_computation.10 | async-start | bytes 3932160 | tf_op jit(solution)/shard_map/all_gather | solution.py:770
  85.1 40.7 %collective-permute-start.10 = (bf16[240,1024]{1,0:T(8,128)(2,1)S(1)}, bf16[240,1024]{1,0:T(8,128)(2,1)}, u32[]{:S(2)}, u32[]{:S(2)}) collective-permute-start(bf16[240,1024]{1,0:T(8,128)(2,1)S(1)} %fusion.21), channel_id=1, source_target_pairs={{0,16},{8,24},{16,32},{24,40},{32,48},{40,56},{48,0},{56,8},{64,80... | collective-permute-start | bytes 1474568 | tf_op jit(solution)/shard_map/ppermute | solution.py:52
  86.6 39.2 %collective-permute-start.11 = (bf16[240,1024]{1,0:T(8,128)(2,1)S(1)}, bf16[240,1024]{1,0:T(8,128)(2,1)}, u32[]{:S(2)}, u32[]{:S(2)}) collective-permute-start(bf16[240,1024]{1,0:T(8,128)(2,1)S(1)} %fusion.21), channel_id=1, source_target_pairs={{0,48},{8,56},{16,0},{24,8},{32,16},{40,24},{48,32},{56,40},{64,11... | collective-permute-start | bytes 1474568 | tf_op jit(solution)/shard_map/ppermute | solution.py:52
  88.4 48.4 %collective-permute-start.12 = (bf16[240,1024]{1,0:T(8,128)(2,1)S(1)}, bf16[240,1024]{1,0:T(8,128)(2,1)}, u32[]{:S(2)}, u32[]{:S(2)}) collective-permute-start(bf16[240,1024]{1,0:T(8,128)(2,1)S(1)} %fusion.21), channel_id=1, source_target_pairs={{0,32},{8,40},{16,48},{24,56},{32,0},{40,8},{48,16},{56,24},{64,96... | collective-permute-start | bytes 1474568 | tf_op jit(solution)/shard_map/ppermute | solution.py:52
  124.9 257.8 %reduce-scatter.2.cloned.1.call-start = ((), (), s32[]{:S(2)}) async-start(), calls=%async_computation.8 | async-start | bytes 7864320 | tf_op jit(solution)/shard_map/reduce_scatter | solution.py:826
  151.2 26.8 %collective-permute-start.24 = (bf16[4,240,1024]{2,1,0:T(8,128)(2,1)S(1)}, bf16[4,240,1024]{2,1,0:T(8,128)(2,1)}, u32[]{:S(2)}, u32[]{:S(2)}) collective-permute-start(bf16[4,240,1024]{2,1,0:T(8,128)(2,1)S(1)} %pad_maximum_fusion.g_mine.routes_mine), channel_id=1, source_target_pairs={{0,8},{8,0},{16,24},{24,16},{32,40},{40,32},{48,56},{56,48},{64,72... | collective-permute-start | bytes 5898248 | tf_op jit(solution)/shard_map/ppermute | solution.py:56
  173.1 46.1 %collective-permute-start.18 = (bf16[4,240,1024]{2,1,0:T(8,128)(2,1)S(1)}, bf16[4,240,1024]{2,1,0:T(8,128)(2,1)}, u32[]{:S(2)}, u32[]{:S(2)}) collective-permute-start(bf16[4,240,1024]{2,1,0:T(8,128)(2,1)S(1)} %pad_maximum_fusion.g_mine.routes_mine), channel_id=1, source_target_pairs={{0,64},{8,72},{16,80},{24,88},{32,96},{40,104},{48,112},{56,120},{... | collective-permute-start | bytes 5898248 | tf_op jit(solution)/shard_map/ppermute | solution.py:52
  175.4 44.6 %collective-permute-start.14 = (bf16[224,1024]{1,0:T(8,128)(2,1)S(1)}, bf16[224,1024]{1,0:T(8,128)(2,1)S(1)}, u32[]{:S(2)}, u32[]{:S(2)}) collective-permute-start(bf16[224,1024]{1,0:T(8,128)(2,1)S(1)} %collective-permute-done.13), channel_id=1, source_target_pairs={{0,16},{8,24},{16,32},{24,40},{32,48},{40,56},{48,0},{56,8},{64,80... | collective-permute-start | bytes 1376264 | tf_op jit(solution)/shard_map/ppermute | solution.py:52
  176.0 44.0 %collective-permute-start.15 = (bf16[224,1024]{1,0:T(8,128)(2,1)S(1)}, bf16[224,1024]{1,0:T(8,128)(2,1)S(1)}, u32[]{:S(2)}, u32[]{:S(2)}) collective-permute-start(bf16[224,1024]{1,0:T(8,128)(2,1)S(1)} %collective-permute-done.13), channel_id=1, source_target_pairs={{0,48},{8,56},{16,0},{24,8},{32,16},{40,24},{48,32},{56,40},{64,11... | collective-permute-start | bytes 1376264 | tf_op jit(solution)/shard_map/ppermute | solution.py:52
  178.1 41.9 %collective-permute-start.16 = (bf16[224,1024]{1,0:T(8,128)(2,1)S(1)}, bf16[224,1024]{1,0:T(8,128)(2,1)}, u32[]{:S(2)}, u32[]{:S(2)}) collective-permute-start(bf16[224,1024]{1,0:T(8,128)(2,1)S(1)} %collective-permute-done.13), channel_id=1, source_target_pairs={{0,32},{8,40},{16,48},{24,56},{32,0},{40,8},{48,16},{56,24},{64,96... | collective-permute-start | bytes 1376264 | tf_op jit(solution)/shard_map/ppermute | solution.py:52
  224.8 27.3 %collective-permute-start.26 = (bf16[256,1024]{1,0:T(8,128)(2,1)}, bf16[256,1024]{1,0:T(8,128)(2,1)S(1)}, u32[]{:S(2)}, u32[]{:S(2)}) collective-permute-start(bf16[256,1024]{1,0:T(8,128)(2,1)} %get-tuple-element.273), channel_id=1, source_target_pairs={{0,48},{8,56},{16,0},{24,8},{32,16},{40,24},{48,32},{56,40},{64,11... | collective-permute-start | bytes 1572872 | tf_op jit(solution)/shard_map/ppermute | solution.py:52
  227.5 25.6 %collective-permute-start.27 = (bf16[256,1024]{1,0:T(8,128)(2,1)}, bf16[256,1024]{1,0:T(8,128)(2,1)S(1)}, u32[]{:S(2)}, u32[]{:S(2)}) collective-permute-start(bf16[256,1024]{1,0:T(8,128)(2,1)} %get-tuple-element.272), channel_id=1, source_target_pairs={{0,16},{8,24},{16,32},{24,40},{32,48},{40,56},{48,0},{56,8},{64,80... | collective-permute-start | bytes 1572872 | tf_op jit(solution)/shard_map/ppermute | solution.py:52
  227.5 25.6 %collective-permute-start.28 = (bf16[256,1024]{1,0:T(8,128)(2,1)S(1)}, bf16[256,1024]{1,0:T(8,128)(2,1)S(1)}, u32[]{:S(2)}, u32[]{:S(2)}) collective-permute-start(bf16[256,1024]{1,0:T(8,128)(2,1)S(1)} %get-tuple-element.271), channel_id=1, source_target_pairs={{0,32},{8,40},{16,48},{24,56},{32,0},{40,8},{48,16},{56,24},{64,96... | collective-permute-start | bytes 1572872 | tf_op jit(solution)/shard_map/ppermute | solution.py:52
  258.5 29.6 %collective-permute-start.33 = (bf16[8,224,1024]{2,1,0:T(8,128)(2,1)}, bf16[8,224,1024]{2,1,0:T(8,128)(2,1)}, u32[]{:S(2)}, u32[]{:S(2)}) collective-permute-start(bf16[8,224,1024]{2,1,0:T(8,128)(2,1)} %get-tuple-element.192), channel_id=1, source_target_pairs={{0,8},{8,0},{16,24},{24,16},{32,40},{40,32},{48,56},{56,48},{64,72... | collective-permute-start | bytes 11010056 | tf_op jit(solution)/shard_map/ppermute | solution.py:56
  263.7 24.3 %collective-permute-start.32 = (bf16[256,1024]{1,0:T(8,128)(2,1)S(1)}, bf16[256,1024]{1,0:T(8,128)(2,1)S(1)}, u32[]{:S(2)}, u32[]{:S(2)}) collective-permute-start(bf16[256,1024]{1,0:T(8,128)(2,1)S(1)} %get-tuple-element.267), channel_id=1, source_target_pairs={{0,32},{8,40},{16,48},{24,56},{32,0},{40,8},{48,16},{56,24},{64,96... | collective-permute-start | bytes 1572872 | tf_op jit(solution)/shard_map/ppermute | solution.py:52
  326.8 48.6 %all-to-all-start.4 = ((bf16[8,128,1152]{2,1,0:T(8,128)(2,1)}), bf16[8,128,1152]{2,1,0:T(8,128)(2,1)S(1)}, u32[]{:S(2)}, u32[]{:S(2)}) async-start(bf16[8,128,1152]{2,1,0:T(8,128)(2,1)} %shard_map.186), calls=%async_computation.4 | async-start | bytes 4718592 | tf_op jit(solution)/shard_map/all_to_all | solution.py:840
  331.5 39.4 %collective-permute-start.35 = (bf16[2,224,1024]{2,1,0:T(8,128)(2,1)}, bf16[2,224,1024]{2,1,0:T(8,128)(2,1)}, u32[]{:S(2)}, u32[]{:S(2)}) collective-permute-start(bf16[2,224,1024]{2,1,0:T(8,128)(2,1)} %get-tuple-element.215), channel_id=1, source_target_pairs={{0,48},{8,56},{16,0},{24,8},{32,16},{40,24},{48,32},{56,40},{64,11... | collective-permute-start | bytes 2752520 | tf_op jit(solution)/shard_map/ppermute | solution.py:52
  333.1 42.3 %collective-permute-start.36 = (bf16[2,224,1024]{2,1,0:T(8,128)(2,1)}, bf16[2,224,1024]{2,1,0:T(8,128)(2,1)}, u32[]{:S(2)}, u32[]{:S(2)}) collective-permute-start(bf16[2,224,1024]{2,1,0:T(8,128)(2,1)} %get-tuple-element.216), channel_id=1, source_target_pairs={{0,16},{8,24},{16,32},{24,40},{32,48},{40,56},{48,0},{56,8},{64,80... | collective-permute-start | bytes 2752520 | tf_op jit(solution)/shard_map/ppermute | solution.py:52
  333.1 42.3 %collective-permute-start.37 = (bf16[2,224,1024]{2,1,0:T(8,128)(2,1)}, bf16[2,224,1024]{2,1,0:T(8,128)(2,1)}, u32[]{:S(2)}, u32[]{:S(2)}) collective-permute-start(bf16[2,224,1024]{2,1,0:T(8,128)(2,1)} %get-tuple-element.217), channel_id=1, source_target_pairs={{0,32},{8,40},{16,48},{24,56},{32,0},{40,8},{48,16},{56,24},{64,96... | collective-permute-start | bytes 2752520 | tf_op jit(solution)/shard_map/ppermute | solution.py:52
  382.7 28.3 %collective-permute-start.43 = (bf16[4,224,1024]{2,1,0:T(8,128)(2,1)}, bf16[4,224,1024]{2,1,0:T(8,128)(2,1)}, u32[]{:S(2)}, u32[]{:S(2)}) collective-permute-start(bf16[4,224,1024]{2,1,0:T(8,128)(2,1)} %get-tuple-element.239), channel_id=1, source_target_pairs={{0,8},{8,0},{16,24},{24,16},{32,40},{40,32},{48,56},{56,48},{64,72... | collective-permute-start | bytes 5505032 | tf_op jit(solution)/shard_map/ppermute | solution.py:56
  387.7 51.6 %collective-permute-start.48 = (bf16[2,192,1024]{2,1,0:T(8,128)(2,1)}, bf16[2,192,1024]{2,1,0:T(8,128)(2,1)}, u32[]{:S(2)}, u32[]{:S(2)}) collective-permute-start(bf16[2,192,1024]{2,1,0:T(8,128)(2,1)} %dynamic-slice_bitcast_fusion), channel_id=1, source_target_pairs={{0,1},{1,0},{2,3},{3,2},{4,5},{5,4},{6,7},{7,6},{8,9},{9,8},{10,11... | collective-permute-start | bytes 2359304 | tf_op jit(solution)/shard_map/ppermute | solution.py:99
  389.1 28.0 %collective-permute-start.40 = (bf16[224,1024]{1,0:T(8,128)(2,1)}, bf16[224,1024]{1,0:T(8,128)(2,1)}, u32[]{:S(2)}, u32[]{:S(2)}) collective-permute-start(bf16[224,1024]{1,0:T(8,128)(2,1)} %get-tuple-element.235), channel_id=1, source_target_pairs={{0,48},{8,56},{16,0},{24,8},{32,16},{40,24},{48,32},{56,40},{64,11... | collective-permute-start | bytes 1376264 | tf_op jit(solution)/shard_map/ppermute | solution.py:52
  389.3 27.9 %collective-permute-start.41 = (bf16[224,1024]{1,0:T(8,128)(2,1)}, bf16[224,1024]{1,0:T(8,128)(2,1)}, u32[]{:S(2)}, u32[]{:S(2)}) collective-permute-start(bf16[224,1024]{1,0:T(8,128)(2,1)} %get-tuple-element.236), channel_id=1, source_target_pairs={{0,16},{8,24},{16,32},{24,40},{32,48},{40,56},{48,0},{56,8},{64,80... | collective-permute-start | bytes 1376264 | tf_op jit(solution)/shard_map/ppermute | solution.py:52
  390.6 26.6 %collective-permute-start.42 = (bf16[224,1024]{1,0:T(8,128)(2,1)}, bf16[224,1024]{1,0:T(8,128)(2,1)}, u32[]{:S(2)}, u32[]{:S(2)}) collective-permute-start(bf16[224,1024]{1,0:T(8,128)(2,1)} %get-tuple-element.237), channel_id=1, source_target_pairs={{0,32},{8,40},{16,48},{24,56},{32,0},{40,8},{48,16},{56,24},{64,96... | collective-permute-start | bytes 1376264 | tf_op jit(solution)/shard_map/ppermute | solution.py:52
  392.1 35.3 %all-to-all-start.6 = ((bf16[16,8,1152]{2,1,0:T(8,128)(2,1)}), bf16[16,8,1152]{2,1,0:T(8,128)(2,1)}, u32[]{:S(2)}, u32[]{:S(2)}) async-start(bf16[16,8,1152]{2,1,0:T(8,128)(2,1)} %bitcast.174), calls=%async_computation.7 | async-start | bytes 589824 | tf_op jit(solution)/shard_map/all_to_all | solution.py:854
  427.4 24.3 %all-to-all-start.5 = ((bf16[128,8,256]{2,1,0:T(8,128)(2,1)}), bf16[128,8,256]{2,1,0:T(8,128)(2,1)S(1)}, u32[]{:S(2)}, u32[]{:S(2)}) async-start(bf16[128,8,256]{2,1,0:T(8,128)(2,1)} %bitcast.67), calls=%async_computation.6 | async-start | bytes 1048576 | tf_op jit(solution)/shard_map/all_to_all | solution.py:858
  (68 other events, 770.9 us)
Sparse Core Ops, SparseCore 0:
  29.4 41.0 all-gather.4
  86.2 51.5 all-gather.6
  288.2 87.6 reduce-scatter.1

commit v11 on v10

--- a/solution.py
+++ b/solution.py
@@ -841,31 +841,50 @@
     projected_grad = attend_back(qkv, head_grad, attended_t, lse, begin, table)
     far_part = project_back(places[8:], projected_grad, head_weights)
     far_part, shared_grads, moved_terms = tie(far_part, shared_grads, moved_terms)
-    far_parts = chip_parts(far_part[0], swap_cores(far_part[1]))
     near_part = project_back(places[:8], projected_grad, head_weights)
-    near_part, expert_grads = tie(near_part, expert_grads)
-    far_parts, projected_grad, shared_grads, moved_terms, expert_grads = tie(
-        far_parts, projected_grad, shared_grads, moved_terms, expert_grads
-    )
-    far_terms = send_along_z(far_parts)
-    near_parts = chip_parts(near_part[0], swap_cores(near_part[1]))
-    moved_crossed = send(add_low(*[t[1] for t in moved_terms]), 1, 0)
     shared_grads = jnp.sum(shared_grads.astype(f32), axis=0).astype(bf16).reshape(16, 8, 1152)
+    upper, lower = slice(0, TOK // 2), slice(TOK // 2, TOK)
+    far_got, near_got = swap_cores(far_part[1]), swap_cores(near_part[1])
+    far_upper = add_low(far_part[0][:, upper], far_got[:, upper])
+    lower_parts = [
+        jnp.stack(
+            [
+                add_low(near_part[0][i, lower], near_got[i, lower]),
+                add_low(far_part[0][i, lower], far_got[i, lower]),
+            ]
+        )
+        for i in range(4)
+    ]
+    far_upper, lower_parts, projected_grad, shared_grads = tie(
+        far_upper, lower_parts, projected_grad, shared_grads
+    )
+    far_upper = send(far_upper, 1, 0)
+    lower_terms = [lower_parts[0]] + [
+        send(lower_parts[i], 0, -b) for i, b in ((1, 1), (2, 3), (3, 2))
+    ]
     shared_grads = lax.all_to_all(shared_grads, "seq", 0, 0, tiled=True)
     grad_head = head_weight_grad(places, rows_near, rows_far, gain_attn, projected_grad)
-    far_terms, near_parts, grad_head = tie(far_terms, near_parts, grad_head)
-    near_terms = send_along_z(near_parts)
+    far_upper, lower_terms, moved_terms, expert_grads = tie(
+        far_upper, lower_terms, moved_terms, expert_grads
+    )
     grad_heads = lax.all_to_all(grad_head.reshape(128, 8, 256), BOTH, 0, 0, tiled=True)
-    crossed = send(add_low(*far_terms), 1, 0)
-    crossed, near_terms, grad_heads, shared_grads = tie(
-        crossed, near_terms, grad_heads, shared_grads
-    )
+    crossed = send(add_low(*[t[1] for t in lower_terms]), 1, 0)
+    upper_parts = [
+        add_low(near_part[0][i, upper], near_got[i, upper], far_upper[i]) for i in range(4)
+    ]
+    upper_terms = [upper_parts[0]] + [
+        send(upper_parts[i], 0, -b) for i, b in ((1, 1), (2, 3), (3, 2))
+    ]
+    moved_crossed = send(add_low(*[t[1] for t in moved_terms]), 1, 0)
+    crossed, grad_heads = tie(crossed, grad_heads)
     kept = lax.dynamic_index_in_dim(expert_grads, own_x, 0, keepdims=False)
     sent = lax.dynamic_index_in_dim(expert_grads, 1 - own_x, 0, keepdims=False)
     expert_grads = kept.astype(f32) + swap_x(sent).astype(f32)
     total = lambda terms: sum([t.astype(f32) for t in terms])
     output = (hidden + total([t[0] for t in moved_terms] + [moved_crossed])).astype(bf16)
-    normed_grad = total(near_terms + [crossed])
+    normed_grad = jnp.concatenate(
+        [total(upper_terms), total([t[0] for t in lower_terms] + [crossed])], axis=0
+    )
     shared_grads = jnp.sum(shared_grads.astype(f32), axis=0)
     grad_heads = jnp.sum(grad_heads.reshape(16, 8, 8, 256).astype(f32), axis=1).transpose(1, 0, 2)
     kv_sum = lambda start: jnp.sum(

time: 476 us -> 491 us (1.032)
  the two profiles are of different devices: /device:TPU:1 before, /device:TPU:0 now
where the time goes in v11:
time: 491 us; the launch traced here: 482 us
  Pallas kernels  162 us (33%)
  waiting for transfers between devices  120 us (24%)
  starting transfers between devices  104 us (21%)
  other arithmetic  59.8 us (12%)
  local copies, waits for them, and re-layouts  21 us (4%)
  between operations  14.9 us (3%)
    ppermute x37, waiting for transfers between devices, send(): return lax.ppermute(rows, 'seq', shift_perm(a, b))  86.6 us
    ppermute x37, starting transfers between devices, send(): return lax.ppermute(rows, 'seq', shift_perm(a, b))  57.8 us
    pallas_call x2, Pallas kernels, run_experts(): pl.pallas_call(experts_kernel, grid_spec=pltpu.PrefetchScalarGridSpec(num...  44 us
    pallas_call x1, Pallas kernels, attend_back(): pl.pallas_call(attend_back_kernel, grid=(GROUP // BLOCK,), in_specs=[whol...  31 us
    convert_element_type x8, other arithmetic, add_low(): return sum([t.astype(f32) for t in terms]).astype(bf16)  21.3 us
    pallas_call x1, Pallas kernels, attend(): pl.pallas_call(attend_kernel, grid=(GROUP // BLOCK,), in_specs=[whole(GRO...  19.8 us
    pallas_call x2, Pallas kernels, project(): pl.pallas_call(project_kernel, grid_spec=pltpu.PrefetchScalarGridSpec(num...  16.6 us
    pallas_call x1, Pallas kernels, expert_weight_grads(): pl.pallas_call(expert_grads_kernel, grid=(2, 4), in_specs=[pl.BlockSpec((...  15.9 us
  transfers between devices with their start and end apart: 60, of which 17 were waited for; matrix products, arithmetic and copies ran while one was open for 15% of the time, Pallas kernels for 34%

profile of v11, /device:TPU:0, one launch (start us, length us, event | category | flops | bytes accessed | tf_op | source)
XLA Modules:
  0.0 481.9 jit_solution(5052599192894266131)
XLA Ops:
  19.8 6.8 %all-to-all-start = ((bf16[128,8,256]{2,1,0:T(8,128)(2,1)}), bf16[128,8,256]{2,1,0:T(8,128)(2,1)S(1)}, u32[]{:S(2)}, u32[]{:S(2)}) async-start(bf16[128,8,256]{2,1,0:T(8,128)(2,1)} %bitcast.9), calls=%async_computation | async-start | bytes 1048576 | tf_op jit(solution)/shard_map/all_to_all | solution.py:760
  28.7 7.7 %subtract_cosine_fusion.table = f32[3584,128]{1,0:T(8,128)} fusion(f32[128]{0:T(128)S(1)} %get-tuple-element.272, f32[128]{0:T(128)S(1)} %get-tuple-element.273, f32[3584]{0:T(1024)S(1)} %get-tuple-element.267), kind=kLoop, calls=%fused_computation.10 | loop fusion | flops 917504 | bytes 1850368 | tf_op jit(solution)/shard_map/cos | solution.py:137
  36.4 5.1 %all-to-all-done = bf16[128,8,256]{2,1,0:T(8,128)(2,1)S(1)} async-done(((bf16[128,8,256]{2,1,0:T(8,128)(2,1)}), bf16[128,8,256]{2,1,0:T(8,128)(2,1)S(1)}, u32[]{:S(2)}, u32[]{:S(2)}) %all-to-all-start) | async-done | bytes 524320 | tf_op jit(solution)/shard_map/all_to_all | solution.py:760
  51.6 8.0 %shard_map.178.refs_0_ = bf16[3584,256]{1,0:T(8,128)(2,1)} custom-call(s32[8]{0:T(128)} %get-tuple-element.270.places, bf16[4,224,1024]{2,1,0:T(8,128)(2,1)} %copy-done.1, bf16[4,224,1024]{2,1,0:T(8,128)(2,1)} %collective-permute-done.7.other.near_other, bf16[1024,256]{1,0:T(8,128)(2,1)} %broadcast_select_fusion.w, f32[1,1024]{1,0:T(1,128)} %bitcast.187, ...), custom_call_target="tpu_custom_call" | custom-call | flops 939524096 | bytes 10485760 | tf_op jit(solution)/shard_map/pallas_call | solution.py:174
  59.6 6.0 %collective-permute-done.8 = bf16[2,192,1024]{2,1,0:T(8,128)(2,1)} collective-permute-done((bf16[2,192,1024]{2,1,0:T(8,128)(2,1)}, bf16[2,192,1024]{2,1,0:T(8,128)(2,1)}, u32[]{:S(2)}, u32[]{:S(2)}) %collective-permute-start.8) | collective-permute-done | bytes 786464 | tf_op jit(solution)/shard_map/ppermute | solution.py:99
  74.4 9.0 %all-to-all-start.1 = ((bf16[128,8,1152]{2,1,0:T(8,128)(2,1)}), bf16[128,8,1152]{2,1,0:T(8,128)(2,1)S(1)}, u32[]{:S(2)}, u32[]{:S(2)}) async-start(bf16[128,8,1152]{2,1,0:T(8,128)(2,1)} %broadcast_in_dim.101), calls=%async_computation.1 | async-start | bytes 4718592 | tf_op jit(solution)/shard_map/all_to_all | solution.py:778
  89.8 8.6 %shard_map.179.qkv_ref = bf16[3584,256]{1,0:T(8,128)(2,1)} custom-call(s32[8]{0:T(128)} %get-tuple-element.271.places, bf16[4,224,1024]{2,1,0:T(8,128)(2,1)} %pad_maximum_fusion.2.mine.far_mine, bf16[4,224,1024]{2,1,0:T(8,128)(2,1)} %collective-permute-done.9.other.far_other, bf16[1024,256]{1,0:T(8,128)(2,1)} %broadcast_select_fusion.w, ...), custom_call_target="tpu_custom_call" | custom-call | flops 939524096 | bytes 10485760 | tf_op jit(solution)/shard_map/pallas_call | solution.py:174
  98.4 19.8 %shard_map.180 = (bf16[16,64,224]{2,1,0:T(8,128)(2,1)}, f32[64,3584]{1,0:T(8,128)}, f32[1,3584]{1,0:T(1,128)}) custom-call(bf16[3584,256]{1,0:T(8,128)(2,1)} %shard_map.179.qkv_ref, s32[1,3584]{1,0:T(1,128)} %compare_select_fusion.begin_ref), custom_call_target="tpu_custom_call" | custom-call | flops 7247757312 | bytes 4194304 | tf_op jit(solution)/shard_map/pallas_call | solution.py:324
  118.2 5.3 %all-to-all-start.2 = ((bf16[16,64,224]{2,1,0:T(8,128)(2,1)}), bf16[16,64,224]{2,1,0:T(8,128)(2,1)S(1)}, u32[]{:S(2)}, u32[]{:S(2)}) async-start(bf16[16,64,224]{2,1,0:T(8,128)(2,1)} %get-tuple-element.137), calls=%async_computation.2 | async-start | bytes 1048576 | tf_op jit(solution)/shard_map/all_to_all | solution.py:793
  124.4 12.0 %collective-permute-done.12 = bf16[240,1024]{1,0:T(8,128)(2,1)} collective-permute-done((bf16[240,1024]{1,0:T(8,128)(2,1)S(1)}, bf16[240,1024]{1,0:T(8,128)(2,1)}, u32[]{:S(2)}, u32[]{:S(2)}) %collective-permute-start.12) | collective-permute-done | bytes 491552 | tf_op jit(solution)/shard_map/ppermute | solution.py:52
  151.0 6.5 %collective-permute-done.13 = bf16[224,1024]{1,0:T(8,128)(2,1)S(1)} collective-permute-done((bf16[224,1024]{1,0:T(8,128)(2,1)}, bf16[224,1024]{1,0:T(8,128)(2,1)S(1)}, u32[]{:S(2)}, u32[]{:S(2)}) %collective-permute-start.13) | collective-permute-done | bytes 458784 | tf_op jit(solution)/shard_map/ppermute | solution.py:52
  157.6 12.0 %collective-permute-done.20 = bf16[224,1024]{1,0:T(8,128)(2,1)S(1)} collective-permute-done((bf16[224,1024]{1,0:T(8,128)(2,1)}, bf16[224,1024]{1,0:T(8,128)(2,1)S(1)}, u32[]{:S(2)}, u32[]{:S(2)}) %collective-permute-start.20) | collective-permute-done | bytes 458784 | tf_op jit(solution)/shard_map/ppermute | solution.py:52
  178.9 21.9 %shard_map.182 = (bf16[4,256,1024]{2,1,0:T(8,128)(2,1)}, bf16[4,256,1024]{2,1,0:T(8,128)(2,1)}, bf16[8,224,1024]{2,1,0:T(8,128)(2,1)}, bf16[8,224,1024]{2,1,0:T(...) custom-call(s32[2]{0:T(128)} %pad_add_fusion.own_ref, ...), custom_call_target="tpu_custom_call" | custom-call | flops 15032385536 | bytes 25165824 | tf_op jit(solution)/shard_map/pallas_call | solution.py:555
  200.9 17.5 %collective-permute-done.18.g_mine.routes_mine = bf16[4,240,1024]{2,1,0:T(8,128)(2,1)} collective-permute-done((bf16[4,240,1024]{2,1,0:T(8,128)(2,1)S(1)}, bf16[4,240,1024]{2,1,0:T(8,128)(2,1)}, u32[]{:S(2)}, u32[]{:S(2)}) %collective-permute-start.18) | collective-permute-done | bytes 1966112 | tf_op jit(solution)/shard_map/ppermute | solution.py:52
  229.4 22.1 %shard_map.183 = (bf16[4,256,1024]{2,1,0:T(8,128)(2,1)}, bf16[4,256,1024]{2,1,0:T(8,128)(2,1)}, bf16[8,224,1024]{2,1,0:T(8,128)(2,1)}, bf16[8,224,1024]{2,1,0:T(...) custom-call(s32[2]{0:T(128)} %pad_add_fusion.own_ref, ...), custom_call_target="tpu_custom_call", output_to_operand_aliasing={{2}: (10, {}), {3}: (11, {}), {4}: (12, {}), {5}: (13, {}),... | custom-call | flops 15032385536 | bytes 25165824 | tf_op jit(solution)/shard_map/pallas_call | solution.py:555
  253.0 4.4 collective-permute-done.29
  264.2 15.9 %shard_map.184 = bf16[4,2,2,192,1024]{4,3,2,1,0:T(8,128)(2,1)} custom-call(bf16[2,1152,1024]{2,1,0:T(8,128)(2,1)} %get-tuple-element.177.x_ref, bf16[2,1152,1024]{2,1,0:T(8,128)(2,1)} %get-tuple-element.178.dh_ref, bf16[2,1152,512]{2,1,0:T(8,128)(2,1)} %get-tuple-element.179.act_ref, bf16[2,1152,1024]{2,1,0:T(8,128)(2,1)} %get-tuple-element.180.dy_ref), custom_call_target="tpu_custom_call" | custom-call | flops 8589934592 | bytes 14680064 | tf_op jit(solution)/shard_map/pallas_call | solution.py:611
  280.1 7.6 %collective-permute-done.32 = bf16[256,1024]{1,0:T(8,128)(2,1)S(1)} collective-permute-done((bf16[256,1024]{1,0:T(8,128)(2,1)S(1)}, bf16[256,1024]{1,0:T(8,128)(2,1)S(1)}, u32[]{:S(2)}, u32[]{:S(2)}) %collective-permute-start.32) | collective-permute-done | bytes 524320 | tf_op jit(solution)/shard_map/ppermute | solution.py:52
  289.9 6.1 %fusion.10 = (bf16[2,224,1024]{2,1,0:T(8,128)(2,1)}, bf16[2,224,1024]{2,1,0:T(8,128)(2,1)}, bf16[2,224,1024]{2,1,0:T(8,128)(2,1)}, bf16[2,224,1024]{2,1,0:T(8,128)(2,1)S(1)}) fusion(bf16[2,4,224,1024]{3,2,1,0:T(8,128)(2,1)} %bitcast.49, bf16[2,4,224,1024]{3,2,1,0:T(8,128)(2,1)} %bitcast.168), kind=kLoop, calls=%fused_computation.36 | loop fusion | flops 7340032 | bytes 11010048 | tf_op jit(solution)/shard_map/convert_element_type | solution.py:83
  296.0 7.2 %collective-permute-done.34.crossed = bf16[256,1024]{1,0:T(8,128)(2,1)S(1)} collective-permute-done((bf16[256,1024]{1,0:T(8,128)(2,1)S(1)}, bf16[256,1024]{1,0:T(8,128)(2,1)S(1)}, u32[]{:S(2)}, u32[]{:S(2)}) %collective-permute-start.34) | collective-permute-done | bytes 524320 | tf_op jit(solution)/shard_map/ppermute | solution.py:52
  304.0 5.8 %shard_map.185 = (f32[224,1024]{1,0:T(8,128)}, bf16[224,1024]{1,0:T(8,128)(2,1)}, bf16[32,224]{1,0:T(8,128)(2,1)}, bf16[224,1024]{1,0:T(8,128)(2,1)}, bf16[16,64,224]{2,1,0:T(8,128)(2,1)}) custom-call(bf16[256,1024]{1,0:T(8,128)(2,1)} %get-tuple-element.169.t0, bf16[256,1024]{1,0:T(8,128)(2,1)} %copy-done.17, bf16[256,1024]{1,0:T(8,128)(2,1)} %copy-done.18, ...), custom_call_target="tpu_custom_call" | custom-call | flops 469762048 | bytes 8388608 | tf_op jit(solution)/shard_map/pallas_call | solution.py:682
  317.3 8.4 %all-to-all-done.3.g_ref = bf16[16,64,224]{2,1,0:T(8,128)(2,1)S(1)} async-done(((bf16[16,64,224]{2,1,0:T(8,128)(2,1)}), bf16[16,64,224]{2,1,0:T(8,128)(2,1)S(1)}, u32[]{:S(2)}, u32[]{:S(2)}) %all-to-all-start.3) | async-done | bytes 458784 | tf_op jit(solution)/shard_map/all_to_all | solution.py:833
  326.6 4.9 %all-to-all-start.4 = ((bf16[8,128,1152]{2,1,0:T(8,128)(2,1)}), bf16[8,128,1152]{2,1,0:T(8,128)(2,1)S(1)}, u32[]{:S(2)}, u32[]{:S(2)}) async-start(bf16[8,128,1152]{2,1,0:T(8,128)(2,1)} %shard_map.186), calls=%async_computation.4 | async-start | bytes 4718592 | tf_op jit(solution)/shard_map/all_to_all | solution.py:840
  334.0 31.0 %shard_map.187.first.second = bf16[3584,256]{1,0:T(8,128)(2,1)} custom-call(bf16[3584,256]{1,0:T(8,128)(2,1)} %shard_map.179.qkv_ref, bf16[16,64,224]{2,1,0:T(8,128)(2,1)} %copy-done.22, f32[64,3584]{1,0:T(8,128)} %get-tuple-element.198.ot_ref, f32[1,3584]{1,0:T(1,128)} %get-tuple-element.199.lse_ref, s32[1,3584]{1,0:T(1,128)} %compare_select_fusion.begin_ref, ...), custom_call_target="tpu_custom_call" | custom-call | flops 18119393280 | bytes 8388608 | tf_op jit(solution)/shard_map/pallas_call | solution.py:404
  364.9 5.4 %shard_map.189 = (bf16[4,224,1024]{2,1,0:T(8,128)(2,1)}, bf16[4,224,1024]{2,1,0:T(8,128)(2,1)}) custom-call(s32[8]{0:T(128)} %get-tuple-element.270.places, bf16[3584,256]{1,0:T(8,128)(2,1)} %shard_map.187.first.second, bf16[3584,256]{1,0:T(8,128)(2,1)} %shard_map.187.first.second, bf16[1024,256]{1,0:T(8,128)(2,1)} %broadcast_select_fusion.w), custom_call_target="tpu_custom_call" | custom-call | flops 939524096 | bytes 5242880 | tf_op jit(solution)/shard_map/pallas_call | solution.py:201
  370.6 5.4 %shard_map.188 = (bf16[4,224,1024]{2,1,0:T(8,128)(2,1)}, bf16[4,224,1024]{2,1,0:T(8,128)(2,1)}) custom-call(s32[8]{0:T(128)} %get-tuple-element.271.places, bf16[3584,256]{1,0:T(8,128)(2,1)} %shard_map.187.first.second, bf16[3584,256]{1,0:T(8,128)(2,1)} %shard_map.187.first.second, bf16[1024,256]{1,0:T(8,128)(2,1)} %broadcast_select_fusion.w), custom_call_target="tpu_custom_call" | custom-call | flops 939524096 | bytes 5242880 | tf_op jit(solution)/shard_map/pallas_call | solution.py:201
  389.5 5.3 %all-to-all-start.6 = ((bf16[16,8,1152]{2,1,0:T(8,128)(2,1)}), bf16[16,8,1152]{2,1,0:T(8,128)(2,1)S(1)}, u32[]{:S(2)}, u32[]{:S(2)}) async-start(bf16[16,8,1152]{2,1,0:T(8,128)(2,1)} %bitcast.55), calls=%async_computation.7 | async-start | bytes 589824 | tf_op jit(solution)/shard_map/all_to_all | solution.py:865
  400.3 10.8 %shard_map.190 = bf16[1024,256]{1,0:T(8,128)(2,1)} custom-call(s32[16]{0:T(128)} %copy-done.37, bf16[4,224,1024]{2,1,0:T(8,128)(2,1)} %copy-done.1, bf16[4,224,1024]{2,1,0:T(8,128)(2,1)} %collective-permute-done.7.other.near_other, bf16[4,224,1024]{2,1,0:T(8,128)(2,1)} %pad_maximum_fusion.2.mine.far_mine, ...), custom_call_target="tpu_custom_call" | custom-call | flops 1879048192 | bytes 10485760 | tf_op jit(solution)/shard_map/pallas_call | solution.py:239
  411.0 5.9 %all-to-all-done.6 = bf16[16,8,1152]{2,1,0:T(8,128)(2,1)S(1)} async-done(((bf16[16,8,1152]{2,1,0:T(8,128)(2,1)}), bf16[16,8,1152]{2,1,0:T(8,128)(2,1)S(1)}, u32[]{:S(2)}, u32[]{:S(2)}) %all-to-all-start.6) | async-done | bytes 294944 | tf_op jit(solution)/shard_map/all_to_all | solution.py:865
  416.9 8.0 %all-to-all-start.5 = ((bf16[128,8,256]{2,1,0:T(8,128)(2,1)}), bf16[128,8,256]{2,1,0:T(8,128)(2,1)S(1)}, u32[]{:S(2)}, u32[]{:S(2)}) async-start(bf16[128,8,256]{2,1,0:T(8,128)(2,1)} %bitcast.170), calls=%async_computation.6 | async-start | bytes 1048576 | tf_op jit(solution)/shard_map/all_to_all | solution.py:870
  444.4 11.0 %collective-permute-done.48 = bf16[112,1024]{1,0:T(8,128)(2,1)S(1)} collective-permute-done((bf16[112,1024]{1,0:T(8,128)(2,1)S(1)}, bf16[112,1024]{1,0:T(8,128)(2,1)S(1)}, u32[]{:S(2)}, u32[]{:S(2)}) %collective-permute-start.48) | collective-permute-done | bytes 229408 | tf_op jit(solution)/shard_map/ppermute | solution.py:52
  462.0 6.9 %collective-permute-done.44 = bf16[224,1024]{1,0:T(8,128)(2,1)} collective-permute-done((bf16[224,1024]{1,0:T(8,128)(2,1)}, bf16[224,1024]{1,0:T(8,128)(2,1)}, u32[]{:S(2)}, u32[]{:S(2)}) %collective-permute-start.44) | collective-permute-done | bytes 458784 | tf_op jit(solution)/shard_map/ppermute | solution.py:52
  (278 shorter events, 148.8 us)
Async XLA Ops:
  7.2 35.1 %collective-permute-start = (bf16[224,1024]{1,0:T(8,128)(2,1)}, bf16[224,1024]{1,0:T(8,128)(2,1)S(1)}, u32[]{:S(2)}, u32[]{:S(2)}) collective-permute-start(bf16[224,1024]{1,0:T(8,128)(2,1)} %bitcast.161), channel_id=1, source_target_pairs={{0,64},{8,72},{16,80},{24,88},{32,96},{40,104},{48,112},{56,120},{... | collective-permute-start | bytes 1376264 | tf_op jit(solution)/shard_map/ppermute | solution.py:52
  10.4 32.0 %collective-permute-start.4 = (bf16[224,1024]{1,0:T(8,128)(2,1)}, bf16[224,1024]{1,0:T(8,128)(2,1)S(1)}, u32[]{:S(2)}, u32[]{:S(2)}) collective-permute-start(bf16[224,1024]{1,0:T(8,128)(2,1)} %bitcast.162), channel_id=1, source_target_pairs={{0,16},{8,24},{16,32},{24,40},{32,48},{40,56},{48,0},{56,8},{64,80... | collective-permute-start | bytes 1376264 | tf_op jit(solution)/shard_map/ppermute | solution.py:52
  12.3 30.1 %collective-permute-start.5 = (bf16[224,1024]{1,0:T(8,128)(2,1)}, bf16[224,1024]{1,0:T(8,128)(2,1)S(1)}, u32[]{:S(2)}, u32[]{:S(2)}) collective-permute-start(bf16[224,1024]{1,0:T(8,128)(2,1)} %bitcast.163), channel_id=1, source_target_pairs={{0,48},{8,56},{16,0},{24,8},{32,16},{40,24},{48,32},{56,40},{64,11... | collective-permute-start | bytes 1376264 | tf_op jit(solution)/shard_map/ppermute | solution.py:52
  14.4 28.0 %collective-permute-start.6 = (bf16[224,1024]{1,0:T(8,128)(2,1)}, bf16[224,1024]{1,0:T(8,128)(2,1)S(1)}, u32[]{:S(2)}, u32[]{:S(2)}) collective-permute-start(bf16[224,1024]{1,0:T(8,128)(2,1)} %bitcast.164), channel_id=1, source_target_pairs={{0,32},{8,40},{16,48},{24,56},{32,0},{40,8},{48,16},{56,24},{64,96... | collective-permute-start | bytes 1376264 | tf_op jit(solution)/shard_map/ppermute | solution.py:52
  26.6 152.4 %all-gather.5.cloned.1.call-start = ((), (), s32[]{:S(2)}) async-start(), calls=%async_computation.9 | async-start | bytes 3932160 | tf_op jit(solution)/shard_map/all_gather | solution.py:770
  74.4 43.8 %all-to-all-start.1 = ((bf16[128,8,1152]{2,1,0:T(8,128)(2,1)}), bf16[128,8,1152]{2,1,0:T(8,128)(2,1)S(1)}, u32[]{:S(2)}, u32[]{:S(2)}) async-start(bf16[128,8,1152]{2,1,0:T(8,128)(2,1)} %broadcast_in_dim.101), calls=%async_computation.1 | async-start | bytes 4718592 | tf_op jit(solution)/shard_map/all_to_all | solution.py:778
  83.4 95.6 %all-gather.7.cloned.1.call-start = ((), (), s32[]{:S(2)}) async-start(), calls=%async_computation.10 | async-start | bytes 3932160 | tf_op jit(solution)/shard_map/all_gather | solution.py:770
  84.7 39.7 %collective-permute-start.10 = (bf16[240,1024]{1,0:T(8,128)(2,1)S(1)}, bf16[240,1024]{1,0:T(8,128)(2,1)}, u32[]{:S(2)}, u32[]{:S(2)}) collective-permute-start(bf16[240,1024]{1,0:T(8,128)(2,1)S(1)} %fusion.21), channel_id=1, source_target_pairs={{0,16},{8,24},{16,32},{24,40},{32,48},{40,56},{48,0},{56,8},{64,80... | collective-permute-start | bytes 1474568 | tf_op jit(solution)/shard_map/ppermute | solution.py:52
  85.8 38.6 %collective-permute-start.11 = (bf16[240,1024]{1,0:T(8,128)(2,1)S(1)}, bf16[240,1024]{1,0:T(8,128)(2,1)}, u32[]{:S(2)}, u32[]{:S(2)}) collective-permute-start(bf16[240,1024]{1,0:T(8,128)(2,1)S(1)} %fusion.21), channel_id=1, source_target_pairs={{0,48},{8,56},{16,0},{24,8},{32,16},{40,24},{48,32},{56,40},{64,11... | collective-permute-start | bytes 1474568 | tf_op jit(solution)/shard_map/ppermute | solution.py:52
  87.9 48.5 %collective-permute-start.12 = (bf16[240,1024]{1,0:T(8,128)(2,1)S(1)}, bf16[240,1024]{1,0:T(8,128)(2,1)}, u32[]{:S(2)}, u32[]{:S(2)}) collective-permute-start(bf16[240,1024]{1,0:T(8,128)(2,1)S(1)} %fusion.21), channel_id=1, source_target_pairs={{0,32},{8,40},{16,48},{24,56},{32,0},{40,8},{48,16},{56,24},{64,96... | collective-permute-start | bytes 1474568 | tf_op jit(solution)/shard_map/ppermute | solution.py:52
  123.5 303.4 %reduce-scatter.2.cloned.1.call-start = ((), (), s32[]{:S(2)}) async-start(), calls=%async_computation.8 | async-start | bytes 7864320 | tf_op jit(solution)/shard_map/reduce_scatter | solution.py:826
  150.9 26.4 %collective-permute-start.24 = (bf16[4,240,1024]{2,1,0:T(8,128)(2,1)S(1)}, bf16[4,240,1024]{2,1,0:T(8,128)(2,1)}, u32[]{:S(2)}, u32[]{:S(2)}) collective-permute-start(bf16[4,240,1024]{2,1,0:T(8,128)(2,1)S(1)} %pad_maximum_fusion.g_mine.routes_mine), channel_id=1, source_target_pairs={{0,8},{8,0},{16,24},{24,16},{32,40},{40,32},{48,56},{56,48},{64,72... | collective-permute-start | bytes 5898248 | tf_op jit(solution)/shard_map/ppermute | solution.py:56
  171.6 46.8 %collective-permute-start.18 = (bf16[4,240,1024]{2,1,0:T(8,128)(2,1)S(1)}, bf16[4,240,1024]{2,1,0:T(8,128)(2,1)}, u32[]{:S(2)}, u32[]{:S(2)}) collective-permute-start(bf16[4,240,1024]{2,1,0:T(8,128)(2,1)S(1)} %pad_maximum_fusion.g_mine.routes_mine), channel_id=1, source_target_pairs={{0,64},{8,72},{16,80},{24,88},{32,96},{40,104},{48,112},{56,120},{... | collective-permute-start | bytes 5898248 | tf_op jit(solution)/shard_map/ppermute | solution.py:52
  174.1 44.3 %collective-permute-start.14 = (bf16[224,1024]{1,0:T(8,128)(2,1)S(1)}, bf16[224,1024]{1,0:T(8,128)(2,1)S(1)}, u32[]{:S(2)}, u32[]{:S(2)}) collective-permute-start(bf16[224,1024]{1,0:T(8,128)(2,1)S(1)} %collective-permute-done.13), channel_id=1, source_target_pairs={{0,16},{8,24},{16,32},{24,40},{32,48},{40,56},{48,0},{56,8},{64,80... | collective-permute-start | bytes 1376264 | tf_op jit(solution)/shard_map/ppermute | solution.py:52
  175.0 43.4 %collective-permute-start.15 = (bf16[224,1024]{1,0:T(8,128)(2,1)S(1)}, bf16[224,1024]{1,0:T(8,128)(2,1)S(1)}, u32[]{:S(2)}, u32[]{:S(2)}) collective-permute-start(bf16[224,1024]{1,0:T(8,128)(2,1)S(1)} %collective-permute-done.13), channel_id=1, source_target_pairs={{0,48},{8,56},{16,0},{24,8},{32,16},{40,24},{48,32},{56,40},{64,11... | collective-permute-start | bytes 1376264 | tf_op jit(solution)/shard_map/ppermute | solution.py:52
  177.4 41.1 %collective-permute-start.16 = (bf16[224,1024]{1,0:T(8,128)(2,1)S(1)}, bf16[224,1024]{1,0:T(8,128)(2,1)}, u32[]{:S(2)}, u32[]{:S(2)}) collective-permute-start(bf16[224,1024]{1,0:T(8,128)(2,1)S(1)} %collective-permute-done.13), channel_id=1, source_target_pairs={{0,32},{8,40},{16,48},{24,56},{32,0},{40,8},{48,16},{56,24},{64,96... | collective-permute-start | bytes 1376264 | tf_op jit(solution)/shard_map/ppermute | solution.py:52
  223.6 27.9 %collective-permute-start.26 = (bf16[256,1024]{1,0:T(8,128)(2,1)}, bf16[256,1024]{1,0:T(8,128)(2,1)S(1)}, u32[]{:S(2)}, u32[]{:S(2)}) collective-permute-start(bf16[256,1024]{1,0:T(8,128)(2,1)} %get-tuple-element.254), channel_id=1, source_target_pairs={{0,48},{8,56},{16,0},{24,8},{32,16},{40,24},{48,32},{56,40},{64,11... | collective-permute-start | bytes 1572872 | tf_op jit(solution)/shard_map/ppermute | solution.py:52
  226.5 26.4 %collective-permute-start.27 = (bf16[256,1024]{1,0:T(8,128)(2,1)}, bf16[256,1024]{1,0:T(8,128)(2,1)S(1)}, u32[]{:S(2)}, u32[]{:S(2)}) collective-permute-start(bf16[256,1024]{1,0:T(8,128)(2,1)} %get-tuple-element.253), channel_id=1, source_target_pairs={{0,16},{8,24},{16,32},{24,40},{32,48},{40,56},{48,0},{56,8},{64,80... | collective-permute-start | bytes 1572872 | tf_op jit(solution)/shard_map/ppermute | solution.py:52
  226.5 26.4 %collective-permute-start.28 = (bf16[256,1024]{1,0:T(8,128)(2,1)S(1)}, bf16[256,1024]{1,0:T(8,128)(2,1)S(1)}, u32[]{:S(2)}, u32[]{:S(2)}) collective-permute-start(bf16[256,1024]{1,0:T(8,128)(2,1)S(1)} %get-tuple-element.252), channel_id=1, source_target_pairs={{0,32},{8,40},{16,48},{24,56},{32,0},{40,8},{48,16},{56,24},{64,96... | collective-permute-start | bytes 1572872 | tf_op jit(solution)/shard_map/ppermute | solution.py:52
  257.4 30.3 %collective-permute-start.33 = (bf16[8,224,1024]{2,1,0:T(8,128)(2,1)}, bf16[8,224,1024]{2,1,0:T(8,128)(2,1)}, u32[]{:S(2)}, u32[]{:S(2)}) collective-permute-start(bf16[8,224,1024]{2,1,0:T(8,128)(2,1)} %get-tuple-element.181), channel_id=1, source_target_pairs={{0,8},{8,0},{16,24},{24,16},{32,40},{40,32},{48,56},{56,48},{64,72... | collective-permute-start | bytes 11010056 | tf_op jit(solution)/shard_map/ppermute | solution.py:56
  263.0 24.7 %collective-permute-start.32 = (bf16[256,1024]{1,0:T(8,128)(2,1)S(1)}, bf16[256,1024]{1,0:T(8,128)(2,1)S(1)}, u32[]{:S(2)}, u32[]{:S(2)}) collective-permute-start(bf16[256,1024]{1,0:T(8,128)(2,1)S(1)} %get-tuple-element.248), channel_id=1, source_target_pairs={{0,32},{8,40},{16,48},{24,56},{32,0},{40,8},{48,16},{56,24},{64,96... | collective-permute-start | bytes 1572872 | tf_op jit(solution)/shard_map/ppermute | solution.py:52
  326.6 49.5 %all-to-all-start.4 = ((bf16[8,128,1152]{2,1,0:T(8,128)(2,1)}), bf16[8,128,1152]{2,1,0:T(8,128)(2,1)S(1)}, u32[]{:S(2)}, u32[]{:S(2)}) async-start(bf16[8,128,1152]{2,1,0:T(8,128)(2,1)} %shard_map.186), calls=%async_computation.4 | async-start | bytes 4718592 | tf_op jit(solution)/shard_map/all_to_all | solution.py:840
  331.4 44.6 %collective-permute-start.35 = (bf16[2,224,1024]{2,1,0:T(8,128)(2,1)}, bf16[2,224,1024]{2,1,0:T(8,128)(2,1)}, u32[]{:S(2)}, u32[]{:S(2)}) collective-permute-start(bf16[2,224,1024]{2,1,0:T(8,128)(2,1)} %get-tuple-element.204), channel_id=1, source_target_pairs={{0,48},{8,56},{16,0},{24,8},{32,16},{40,24},{48,32},{56,40},{64,11... | collective-permute-start | bytes 2752520 | tf_op jit(solution)/shard_map/ppermute | solution.py:52
  332.4 43.6 %collective-permute-start.36 = (bf16[2,224,1024]{2,1,0:T(8,128)(2,1)}, bf16[2,224,1024]{2,1,0:T(8,128)(2,1)}, u32[]{:S(2)}, u32[]{:S(2)}) collective-permute-start(bf16[2,224,1024]{2,1,0:T(8,128)(2,1)} %get-tuple-element.205), channel_id=1, source_target_pairs={{0,16},{8,24},{16,32},{24,40},{32,48},{40,56},{48,0},{56,8},{64,80... | collective-permute-start | bytes 2752520 | tf_op jit(solution)/shard_map/ppermute | solution.py:52
  333.5 42.6 %collective-permute-start.37 = (bf16[2,224,1024]{2,1,0:T(8,128)(2,1)}, bf16[2,224,1024]{2,1,0:T(8,128)(2,1)}, u32[]{:S(2)}, u32[]{:S(2)}) collective-permute-start(bf16[2,224,1024]{2,1,0:T(8,128)(2,1)} %get-tuple-element.206), channel_id=1, source_target_pairs={{0,32},{8,40},{16,48},{24,56},{32,0},{40,8},{48,16},{56,24},{64,96... | collective-permute-start | bytes 2752520 | tf_op jit(solution)/shard_map/ppermute | solution.py:52
  387.4 39.5 %collective-permute-start.40 = (bf16[4,112,1024]{2,1,0:T(8,128)(2,1)}, bf16[4,112,1024]{2,1,0:T(8,128)(2,1)S(1)}, u32[]{:S(2)}, u32[]{:S(2)}) collective-permute-start(bf16[4,112,1024]{2,1,0:T(8,128)(2,1)} %add_convert_fusion), channel_id=1, source_target_pairs={{0,64},{8,72},{16,80},{24,88},{32,96},{40,104},{48,112},{56,120},{... | collective-permute-start | bytes 2752520 | tf_op jit(solution)/shard_map/ppermute | solution.py:52
  389.5 27.4 %all-to-all-start.6 = ((bf16[16,8,1152]{2,1,0:T(8,128)(2,1)}), bf16[16,8,1152]{2,1,0:T(8,128)(2,1)S(1)}, u32[]{:S(2)}, u32[]{:S(2)}) async-start(bf16[16,8,1152]{2,1,0:T(8,128)(2,1)} %bitcast.55), calls=%async_computation.7 | async-start | bytes 589824 | tf_op jit(solution)/shard_map/all_to_all | solution.py:865
  394.8 32.1 %collective-permute-start.41 = (bf16[2,112,1024]{2,1,0:T(8,128)(2,1)}, bf16[2,112,1024]{2,1,0:T(8,128)(2,1)}, u32[]{:S(2)}, u32[]{:S(2)}) collective-permute-start(bf16[2,112,1024]{2,1,0:T(8,128)(2,1)} %pad_maximum_fusion.6), channel_id=1, source_target_pairs={{0,48},{8,56},{16,0},{24,8},{32,16},{40,24},{48,32},{56,40},{64,11... | collective-permute-start | bytes 1376264 | tf_op jit(solution)/shard_map/ppermute | solution.py:52
  398.0 28.9 %collective-permute-start.42 = (bf16[2,112,1024]{2,1,0:T(8,128)(2,1)}, bf16[2,112,1024]{2,1,0:T(8,128)(2,1)}, u32[]{:S(2)}, u32[]{:S(2)}) collective-permute-start(bf16[2,112,1024]{2,1,0:T(8,128)(2,1)} %pad_maximum_fusion.7), channel_id=1, source_target_pairs={{0,16},{8,24},{16,32},{24,40},{32,48},{40,56},{48,0},{56,8},{64,80... | collective-permute-start | bytes 1376264 | tf_op jit(solution)/shard_map/ppermute | solution.py:52
  398.0 28.9 %collective-permute-start.43 = (bf16[2,112,1024]{2,1,0:T(8,128)(2,1)}, bf16[2,112,1024]{2,1,0:T(8,128)(2,1)}, u32[]{:S(2)}, u32[]{:S(2)}) collective-permute-start(bf16[2,112,1024]{2,1,0:T(8,128)(2,1)} %pad_maximum_fusion.8), channel_id=1, source_target_pairs={{0,32},{8,40},{16,48},{24,56},{32,0},{40,8},{48,16},{56,24},{64,96... | collective-permute-start | bytes 1376264 | tf_op jit(solution)/shard_map/ppermute | solution.py:52
  416.9 39.3 %all-to-all-start.5 = ((bf16[128,8,256]{2,1,0:T(8,128)(2,1)}), bf16[128,8,256]{2,1,0:T(8,128)(2,1)S(1)}, u32[]{:S(2)}, u32[]{:S(2)}) async-start(bf16[128,8,256]{2,1,0:T(8,128)(2,1)} %bitcast.170), calls=%async_computation.6 | async-start | bytes 1048576 | tf_op jit(solution)/shard_map/all_to_all | solution.py:870
  429.0 42.6 %collective-permute-start.49 = (bf16[2,192,1024]{2,1,0:T(8,128)(2,1)}, bf16[2,192,1024]{2,1,0:T(8,128)(2,1)}, u32[]{:S(2)}, u32[]{:S(2)}) collective-permute-start(bf16[2,192,1024]{2,1,0:T(8,128)(2,1)} %dynamic-slice_bitcast_fusion), channel_id=1, source_target_pairs={{0,1},{1,0},{2,3},{3,2},{4,5},{5,4},{6,7},{7,6},{8,9},{9,8},{10,11... | collective-permute-start | bytes 2359304 | tf_op jit(solution)/shard_map/ppermute | solution.py:99
  (71 other events, 741.0 us)
Sparse Core Ops, SparseCore 0:
  29.1 40.6 all-gather.4
  85.9 50.9 all-gather.6
  287.8 87.2 reduce-scatter.1

commit v12 on v10

--- a/solution.py
+++ b/solution.py
@@ -761,9 +761,10 @@
     gain_attn = head_weights[:, 192].astype(f32)[None]
     head_weights = jnp.where(jnp.arange(256)[None] < 192, head_weights, 0.0).astype(bf16)
 
-    rows_near, rows_across = gather_near(rows)
-    rows_near, _, table, head_weights = tie(rows_near, rows_across, table, head_weights)
-    rows_near, rows_far = both_cores(rows_near), gather_far(rows_across)
+    rows_near = [rows] + [send(rows, 0, b) for b in (1, 3, 2)]
+    rows_near, table, head_weights = tie(rows_near, table, head_weights)
+    rows_near = both_cores(rows_near)
+    rows_far = send(rows_near[0], 1, 0)
 
     own_x = lax.axis_index("wshard") % 2
     expert_rows = jnp.concatenate([w_gate_up, w_down], axis=1)
@@ -780,31 +781,33 @@
     ).reshape(WIDTH, 1152)
     routes_rows = jnp.pad(routes[0].T.astype(bf16), ((0, 8), (0, WIDTH - TOK)))
     upstream_rows = jnp.concatenate([cotangent[0], routes_rows], axis=0)
-    rows_far, qkv, upstream_rows, expert_rows = tie(rows_far, qkv, upstream_rows, expert_rows)
-    experts = [experts, along_y(expert_rows)]
-    rows_far = both_cores(rows_far)
+    upstream_rows, _ = tie(upstream_rows, rows_near[0])
     grad_near = [upstream_rows] + [send(upstream_rows, 0, b) for b in (1, 3, 2)]
+    rows_far, qkv, grad_near, upstream_rows = tie(rows_far, qkv, grad_near, upstream_rows)
+    grad_across = send(upstream_rows, 1, 0)
+    rows_far = (rows_far, swap_cores(rows_far))
     qkv = project(places[8:], rows_far, head_weights, gain_attn, table, (qkv,))
+    qkv, grad_across = tie(qkv, grad_across)
+    grad_far = gather_far(grad_across)
 
     router_t = shared[:, WIDTH : WIDTH + EXPERTS].T
     gain_ffn = shared[:, WIDTH + EXPERTS].astype(f32)[None]
     attended_head, attended_t, lse = attend(qkv, begin)
-    attended_head, shared = tie(attended_head, shared)
+    attended_head, shared, expert_rows = tie(attended_head, shared, expert_rows)
+    experts = [experts, along_y(expert_rows)]
     attended = lax.all_to_all(attended_head, "seq", 0, 0, tiled=True)
-    attended, grad_near = tie(attended, grad_near)
-    grad_near = jnp.stack(grad_near)
     hidden, normed_ffn = hidden_of(attended, shared, rows, gain_ffn)
+    normed_ffn, grad_far = tie(normed_ffn, grad_far)
+
     ffn_near, ffn_across = gather_near(normed_ffn)
     ffn_near, _ = tie(ffn_near, ffn_across)
-    grad_near_mine, _ = tie(grad_near, ffn_across)
-    grad_far = send(grad_near_mine, 1, 0)
-    grad_near = (grad_near, swap_cores(grad_near))
+    grad_near = both_cores(grad_near)
     ffn_near, ffn_far = both_cores(ffn_near), gather_far(ffn_across)
     own = jnp.stack([seq_index * 2, own_x])
     near = run_experts(0, own, ffn_near, grad_near, experts, router_t, ())
     near_terms = sum_along_z(*near[:2])
     ffn_far = both_cores(ffn_far)
-    grad_far = (grad_far, swap_cores(grad_far))
+    grad_far = both_cores(grad_far)
     far = run_experts(1, own, ffn_far, grad_far, experts, router_t, near[2:])
     far, near_terms = tie(far, near_terms)
     moved, saved = far[2:4], far[4:]

time: 476 us -> 523 us (1.099)
  the two profiles are of different devices: /device:TPU:1 before, /device:TPU:0 now
where the time goes in v12:
time: 523 us; the launch traced here: 514 us
  Pallas kernels  163 us (31%)
  waiting for transfers between devices  156 us (30%)
  starting transfers between devices  106 us (20%)
  other arithmetic  54.8 us (10%)
  local copies, waits for them, and re-layouts  19.3 us (4%)
  between operations  14.9 us (3%)
    ppermute x36, waiting for transfers between devices, send(): return lax.ppermute(rows, 'seq', shift_perm(a, b))  118 us
    ppermute x36, starting transfers between devices, send(): return lax.ppermute(rows, 'seq', shift_perm(a, b))  57 us
    pallas_call x2, Pallas kernels, run_experts(): pl.pallas_call(experts_kernel, grid_spec=pltpu.PrefetchScalarGridSpec(num...  44.1 us
    pallas_call x1, Pallas kernels, attend_back(): pl.pallas_call(attend_back_kernel, grid=(GROUP // BLOCK,), in_specs=[whol...  31 us
    convert_element_type x7, other arithmetic, add_low(): return sum([t.astype(f32) for t in terms]).astype(bf16)  21.2 us
    all_to_all x1, waiting for transfers between devices, local(): attended = lax.all_to_all(attended_head, 'seq', 0, 0, tiled=True)  21 us
    pallas_call x1, Pallas kernels, attend(): pl.pallas_call(attend_kernel, grid=(GROUP // BLOCK,), in_specs=[whole(GRO...  19.9 us
    pallas_call x2, Pallas kernels, project(): pl.pallas_call(project_kernel, grid_spec=pltpu.PrefetchScalarGridSpec(num...  16.6 us
  transfers between devices with their start and end apart: 59, of which 19 were waited for; matrix products, arithmetic and copies ran while one was open for 11% of the time, Pallas kernels for 32%

profile of v12, /device:TPU:0, one launch (start us, length us, event | category | flops | bytes accessed | tf_op | source)
XLA Modules:
  0.0 513.9 jit_solution(1644932667547720913)
XLA Ops:
  16.7 8.8 %all-to-all-start = ((bf16[128,8,256]{2,1,0:T(8,128)(2,1)}), bf16[128,8,256]{2,1,0:T(8,128)(2,1)S(1)}, u32[]{:S(2)}, u32[]{:S(2)}) async-start(bf16[128,8,256]{2,1,0:T(8,128)(2,1)} %bitcast.8), calls=%async_computation | async-start | bytes 1048576 | tf_op jit(solution)/shard_map/all_to_all | solution.py:760
  27.0 7.7 %subtract_cosine_fusion.table = f32[3584,128]{1,0:T(8,128)} fusion(f32[128]{0:T(128)S(1)} %get-tuple-element.297, f32[128]{0:T(128)S(1)} %get-tuple-element.298, f32[3584]{0:T(1024)S(1)} %get-tuple-element.292), kind=kLoop, calls=%fused_computation.9 | loop fusion | flops 917504 | bytes 1850368 | tf_op jit(solution)/shard_map/cos | solution.py:137
  34.7 4.3 all-to-all-done
  50.9 7.9 %shard_map.178.refs_0_ = bf16[3584,256]{1,0:T(8,128)(2,1)} custom-call(s32[8]{0:T(128)} %get-tuple-element.295.places, bf16[4,224,1024]{2,1,0:T(8,128)(2,1)} %copy-done.1, bf16[4,224,1024]{2,1,0:T(8,128)(2,1)} %collective-permute-done.4.other.near_other, bf16[1024,256]{1,0:T(8,128)(2,1)} %broadcast_select_fusion.w, f32[1,1024]{1,0:T(1,128)} %bitcast.185, ...), custom_call_target="tpu_custom_call" | custom-call | flops 939524096 | bytes 10485760 | tf_op jit(solution)/shard_map/pallas_call | solution.py:174
  60.6 9.2 %collective-permute-done.6 = bf16[240,1024]{1,0:T(8,128)(2,1)} collective-permute-done((bf16[240,1024]{1,0:T(8,128)(2,1)S(1)}, bf16[240,1024]{1,0:T(8,128)(2,1)}, u32[]{:S(2)}, u32[]{:S(2)}) %collective-permute-start.6) | collective-permute-done | bytes 491552 | tf_op jit(solution)/shard_map/ppermute | solution.py:52
  70.7 15.8 %collective-permute-done.3.mine.far_mine = bf16[4,224,1024]{2,1,0:T(8,128)(2,1)} collective-permute-done((bf16[4,224,1024]{2,1,0:T(8,128)(2,1)S(1)}, bf16[4,224,1024]{2,1,0:T(8,128)(2,1)}, u32[]{:S(2)}, u32[]{:S(2)}) %collective-permute-start.3) | collective-permute-done | bytes 1835040 | tf_op jit(solution)/shard_map/ppermute | solution.py:52
  88.2 8.8 %all-to-all-start.1 = ((bf16[128,8,1152]{2,1,0:T(8,128)(2,1)}), bf16[128,8,1152]{2,1,0:T(8,128)(2,1)S(1)}, u32[]{:S(2)}, u32[]{:S(2)}) async-start(bf16[128,8,1152]{2,1,0:T(8,128)(2,1)} %broadcast_in_dim.101), calls=%async_computation.1 | async-start | bytes 4718592 | tf_op jit(solution)/shard_map/all_to_all | solution.py:779
  101.6 8.6 %shard_map.179.qkv_ref = bf16[3584,256]{1,0:T(8,128)(2,1)} custom-call(s32[8]{0:T(128)} %get-tuple-element.296.places, bf16[4,224,1024]{2,1,0:T(8,128)(2,1)} %collective-permute-done.3.mine.far_mine, bf16[4,224,1024]{2,1,0:T(8,128)(2,1)} %collective-permute-done.8.other.far_other, bf16[1024,256]{1,0:T(8,128)(2,1)} %broadcast_select_fusion.w, ...), custom_call_target="tpu_custom_call" | custom-call | flops 939524096 | bytes 10485760 | tf_op jit(solution)/shard_map/pallas_call | solution.py:174
  110.2 42.3 %collective-permute-done.9 = bf16[240,1024]{1,0:T(8,128)(2,1)S(1)} collective-permute-done((bf16[240,1024]{1,0:T(8,128)(2,1)}, bf16[240,1024]{1,0:T(8,128)(2,1)S(1)}, u32[]{:S(2)}, u32[]{:S(2)}) %collective-permute-start.9) | collective-permute-done | bytes 491552 | tf_op jit(solution)/shard_map/ppermute | solution.py:52
  152.5 19.9 %shard_map.180 = (bf16[16,64,224]{2,1,0:T(8,128)(2,1)}, f32[64,3584]{1,0:T(8,128)}, f32[1,3584]{1,0:T(1,128)}) custom-call(bf16[3584,256]{1,0:T(8,128)(2,1)} %shard_map.179.qkv_ref, s32[1,3584]{1,0:T(1,128)} %compare_select_fusion.begin_ref), custom_call_target="tpu_custom_call" | custom-call | flops 7247757312 | bytes 4194304 | tf_op jit(solution)/shard_map/pallas_call | solution.py:324
  182.4 21.0 %all-to-all-done.2.att_ref = bf16[16,64,224]{2,1,0:T(8,128)(2,1)S(1)} async-done(((bf16[16,64,224]{2,1,0:T(8,128)(2,1)}), bf16[16,64,224]{2,1,0:T(8,128)(2,1)S(1)}, u32[]{:S(2)}, u32[]{:S(2)}) %all-to-all-start.2) | async-done | bytes 458784 | tf_op jit(solution)/shard_map/all_to_all | solution.py:798
  214.2 8.4 %collective-permute-done.14 = bf16[224,1024]{1,0:T(8,128)(2,1)S(1)} collective-permute-done((bf16[224,1024]{1,0:T(8,128)(2,1)}, bf16[224,1024]{1,0:T(8,128)(2,1)S(1)}, u32[]{:S(2)}, u32[]{:S(2)}) %collective-permute-start.14) | collective-permute-done | bytes 458784 | tf_op jit(solution)/shard_map/ppermute | solution.py:52
  223.2 10.0 %collective-permute-done.22 = bf16[224,1024]{1,0:T(8,128)(2,1)S(1)} collective-permute-done((bf16[224,1024]{1,0:T(8,128)(2,1)}, bf16[224,1024]{1,0:T(8,128)(2,1)S(1)}, u32[]{:S(2)}, u32[]{:S(2)}) %collective-permute-start.22) | collective-permute-done | bytes 458784 | tf_op jit(solution)/shard_map/ppermute | solution.py:52
  241.2 22.0 %shard_map.182 = (bf16[4,256,1024]{2,1,0:T(8,128)(2,1)}, bf16[4,256,1024]{2,1,0:T(8,128)(2,1)}, bf16[8,224,1024]{2,1,0:T(8,128)(2,1)}, bf16[8,224,1024]{2,1,0:T(...) custom-call(s32[2]{0:T(128)} %pad_add_fusion.own_ref, ...), custom_call_target="tpu_custom_call" | custom-call | flops 15032385536 | bytes 25165824 | tf_op jit(solution)/shard_map/pallas_call | solution.py:555
  277.3 22.1 %shard_map.183 = (bf16[4,256,1024]{2,1,0:T(8,128)(2,1)}, bf16[4,256,1024]{2,1,0:T(8,128)(2,1)}, bf16[8,224,1024]{2,1,0:T(8,128)(2,1)}, bf16[8,224,1024]{2,1,0:T(...) custom-call(s32[2]{0:T(128)} %pad_add_fusion.own_ref, ...), custom_call_target="tpu_custom_call", output_to_operand_aliasing={{2}: (10, {}), {3}: (11, {}), {4}: (12, {}), {5}: (13, {}),... | custom-call | flops 15032385536 | bytes 25165824 | tf_op jit(solution)/shard_map/pallas_call | solution.py:555
  299.6 4.4 collective-permute-done.29
  310.6 15.9 %shard_map.184 = bf16[4,2,2,192,1024]{4,3,2,1,0:T(8,128)(2,1)} custom-call(bf16[2,1152,1024]{2,1,0:T(8,128)(2,1)} %get-tuple-element.194.x_ref, bf16[2,1152,1024]{2,1,0:T(8,128)(2,1)} %get-tuple-element.195.dh_ref, bf16[2,1152,512]{2,1,0:T(8,128)(2,1)} %get-tuple-element.196.act_ref, bf16[2,1152,1024]{2,1,0:T(8,128)(2,1)} %get-tuple-element.197.dy_ref), custom_call_target="tpu_custom_call" | custom-call | flops 8589934592 | bytes 14680064 | tf_op jit(solution)/shard_map/pallas_call | solution.py:611
  326.5 8.2 %collective-permute-done.31 = bf16[256,1024]{1,0:T(8,128)(2,1)S(1)} collective-permute-done((bf16[256,1024]{1,0:T(8,128)(2,1)S(1)}, bf16[256,1024]{1,0:T(8,128)(2,1)S(1)}, u32[]{:S(2)}, u32[]{:S(2)}) %collective-permute-start.31) | collective-permute-done | bytes 524320 | tf_op jit(solution)/shard_map/ppermute | solution.py:52
  339.1 6.2 %fusion.10 = (bf16[2,224,1024]{2,1,0:T(8,128)(2,1)}, bf16[2,224,1024]{2,1,0:T(8,128)(2,1)}, bf16[2,224,1024]{2,1,0:T(8,128)(2,1)}, bf16[2,224,1024]{2,1,0:T(8,128)(2,1)S(1)}) fusion(bf16[2,4,224,1024]{3,2,1,0:T(8,128)(2,1)} %bitcast.49, bf16[2,4,224,1024]{3,2,1,0:T(8,128)(2,1)} %bitcast.168), kind=kLoop, calls=%fused_computation.35 | loop fusion | flops 7340032 | bytes 11010048 | tf_op jit(solution)/shard_map/convert_element_type | solution.py:83
  345.3 4.3 collective-permute-done.34.crossed
  350.5 5.9 %shard_map.185 = (f32[224,1024]{1,0:T(8,128)}, bf16[224,1024]{1,0:T(8,128)(2,1)}, bf16[32,224]{1,0:T(8,128)(2,1)}, bf16[224,1024]{1,0:T(8,128)(2,1)}, bf16[16,64,224]{2,1,0:T(8,128)(2,1)}) custom-call(bf16[256,1024]{1,0:T(8,128)(2,1)} %get-tuple-element.186.t0, bf16[256,1024]{1,0:T(8,128)(2,1)} %copy-done.21, bf16[256,1024]{1,0:T(8,128)(2,1)} %copy-done.22, ...), custom_call_target="tpu_custom_call" | custom-call | flops 469762048 | bytes 8388608 | tf_op jit(solution)/shard_map/pallas_call | solution.py:682
  356.4 5.4 %all-to-all-start.3 = ((bf16[16,64,224]{2,1,0:T(8,128)(2,1)}), bf16[16,64,224]{2,1,0:T(8,128)(2,1)S(1)}, u32[]{:S(2)}, u32[]{:S(2)}) async-start(bf16[16,64,224]{2,1,0:T(8,128)(2,1)} %get-tuple-element.206), calls=%async_computation.3 | async-start | bytes 1048576 | tf_op jit(solution)/shard_map/all_to_all | solution.py:836
  365.6 8.4 %all-to-all-done.3.g_ref = bf16[16,64,224]{2,1,0:T(8,128)(2,1)S(1)} async-done(((bf16[16,64,224]{2,1,0:T(8,128)(2,1)}), bf16[16,64,224]{2,1,0:T(8,128)(2,1)S(1)}, u32[]{:S(2)}, u32[]{:S(2)}) %all-to-all-start.3) | async-done | bytes 458784 | tf_op jit(solution)/shard_map/all_to_all | solution.py:836
  374.9 4.3 all-to-all-start.4
  381.7 31.0 %shard_map.187.first.second = bf16[3584,256]{1,0:T(8,128)(2,1)} custom-call(bf16[3584,256]{1,0:T(8,128)(2,1)} %shard_map.179.qkv_ref, bf16[16,64,224]{2,1,0:T(8,128)(2,1)} %copy-done.26, f32[64,3584]{1,0:T(8,128)} %get-tuple-element.215.ot_ref, f32[1,3584]{1,0:T(1,128)} %get-tuple-element.216.lse_ref, s32[1,3584]{1,0:T(1,128)} %compare_select_fusion.begin_ref, ...), custom_call_target="tpu_custom_call" | custom-call | flops 18119393280 | bytes 8388608 | tf_op jit(solution)/shard_map/pallas_call | solution.py:404
  412.7 5.4 %shard_map.188 = (bf16[4,224,1024]{2,1,0:T(8,128)(2,1)}, bf16[4,224,1024]{2,1,0:T(8,128)(2,1)}) custom-call(s32[8]{0:T(128)} %get-tuple-element.296.places, bf16[3584,256]{1,0:T(8,128)(2,1)} %shard_map.187.first.second, bf16[3584,256]{1,0:T(8,128)(2,1)} %shard_map.187.first.second, bf16[1024,256]{1,0:T(8,128)(2,1)} %broadcast_select_fusion.w), custom_call_target="tpu_custom_call" | custom-call | flops 939524096 | bytes 5242880 | tf_op jit(solution)/shard_map/pallas_call | solution.py:201
  423.6 5.4 %shard_map.189 = (bf16[4,224,1024]{2,1,0:T(8,128)(2,1)}, bf16[4,224,1024]{2,1,0:T(8,128)(2,1)}) custom-call(s32[8]{0:T(128)} %get-tuple-element.295.places, bf16[3584,256]{1,0:T(8,128)(2,1)} %shard_map.187.first.second, bf16[3584,256]{1,0:T(8,128)(2,1)} %shard_map.187.first.second, bf16[1024,256]{1,0:T(8,128)(2,1)} %broadcast_select_fusion.w), custom_call_target="tpu_custom_call" | custom-call | flops 939524096 | bytes 5242880 | tf_op jit(solution)/shard_map/pallas_call | solution.py:201
  429.5 3.9 fusion.25
  439.9 4.9 all-to-all-start.6
  446.4 10.9 %shard_map.190 = bf16[1024,256]{1,0:T(8,128)(2,1)} custom-call(s32[16]{0:T(128)} %copy-done.39, bf16[4,224,1024]{2,1,0:T(8,128)(2,1)} %copy-done.1, bf16[4,224,1024]{2,1,0:T(8,128)(2,1)} %collective-permute-done.4.other.near_other, bf16[4,224,1024]{2,1,0:T(8,128)(2,1)} %collective-permute-done.3.mine.far_mine, ...), custom_call_target="tpu_custom_call" | custom-call | flops 1879048192 | bytes 10485760 | tf_op jit(solution)/shard_map/pallas_call | solution.py:239
  475.8 7.9 %all-to-all-start.5 = ((bf16[128,8,256]{2,1,0:T(8,128)(2,1)}), bf16[128,8,256]{2,1,0:T(8,128)(2,1)S(1)}, u32[]{:S(2)}, u32[]{:S(2)}) async-start(bf16[128,8,256]{2,1,0:T(8,128)(2,1)} %bitcast.67), calls=%async_computation.6 | async-start | bytes 1048576 | tf_op jit(solution)/shard_map/all_to_all | solution.py:861
  489.8 5.1 collective-permute-done.45
  (274 shorter events, 144.5 us)
Async XLA Ops:
  7.2 32.7 %collective-permute-start = (bf16[224,1024]{1,0:T(8,128)(2,1)}, bf16[224,1024]{1,0:T(8,128)(2,1)S(1)}, u32[]{:S(2)}, u32[]{:S(2)}) collective-permute-start(bf16[224,1024]{1,0:T(8,128)(2,1)} %bitcast.162), channel_id=1, source_target_pairs={{0,16},{8,24},{16,32},{24,40},{32,48},{40,56},{48,0},{56,8},{64,80... | collective-permute-start | bytes 1376264 | tf_op jit(solution)/shard_map/ppermute | solution.py:52
  9.3 30.6 %collective-permute-start.1 = (bf16[224,1024]{1,0:T(8,128)(2,1)}, bf16[224,1024]{1,0:T(8,128)(2,1)S(1)}, u32[]{:S(2)}, u32[]{:S(2)}) collective-permute-start(bf16[224,1024]{1,0:T(8,128)(2,1)} %bitcast.163), channel_id=1, source_target_pairs={{0,48},{8,56},{16,0},{24,8},{32,16},{40,24},{48,32},{56,40},{64,11... | collective-permute-start | bytes 1376264 | tf_op jit(solution)/shard_map/ppermute | solution.py:52
  11.5 28.4 %collective-permute-start.2 = (bf16[224,1024]{1,0:T(8,128)(2,1)}, bf16[224,1024]{1,0:T(8,128)(2,1)}, u32[]{:S(2)}, u32[]{:S(2)}) collective-permute-start(bf16[224,1024]{1,0:T(8,128)(2,1)} %bitcast.164), channel_id=1, source_target_pairs={{0,32},{8,40},{16,48},{24,56},{32,0},{40,8},{48,16},{56,24},{64,96... | collective-permute-start | bytes 1376264 | tf_op jit(solution)/shard_map/ppermute | solution.py:52
  25.5 215.6 %all-gather.5.cloned.1.call-start = ((), (), s32[]{:S(2)}) async-start(), calls=%async_computation.9 | async-start | bytes 3932160 | tf_op jit(solution)/shard_map/all_gather | solution.py:771
  42.5 44.0 %collective-permute-start.3 = (bf16[4,224,1024]{2,1,0:T(8,128)(2,1)S(1)}, bf16[4,224,1024]{2,1,0:T(8,128)(2,1)}, u32[]{:S(2)}, u32[]{:S(2)}) collective-permute-start(bf16[4,224,1024]{2,1,0:T(8,128)(2,1)S(1)} %pad_maximum_fusion.2.mine.near_mine), channel_id=1, source_target_pairs={{0,64},{8,72},{16,80},{24,88},{32,96},{40,104},{48,112},{56,120},{... | collective-permute-start | bytes 5505032 | tf_op jit(solution)/shard_map/ppermute | solution.py:52
  88.2 84.3 %all-to-all-start.1 = ((bf16[128,8,1152]{2,1,0:T(8,128)(2,1)}), bf16[128,8,1152]{2,1,0:T(8,128)(2,1)S(1)}, u32[]{:S(2)}, u32[]{:S(2)}) async-start(bf16[128,8,1152]{2,1,0:T(8,128)(2,1)} %broadcast_in_dim.101), calls=%async_computation.1 | async-start | bytes 4718592 | tf_op jit(solution)/shard_map/all_to_all | solution.py:779
  97.0 144.1 %all-gather.7.cloned.1.call-start = ((), (), s32[]{:S(2)}) async-start(), calls=%async_computation.10 | async-start | bytes 3932160 | tf_op jit(solution)/shard_map/all_gather | solution.py:771
  97.1 75.4 %collective-permute-start.10 = (bf16[2,192,1024]{2,1,0:T(8,128)(2,1)S(1)}, bf16[2,192,1024]{2,1,0:T(8,128)(2,1)}, u32[]{:S(2)}, u32[]{:S(2)}) collective-permute-start(bf16[2,192,1024]{2,1,0:T(8,128)(2,1)S(1)} %copy-done.8), channel_id=1, source_target_pairs={{0,1},{1,0},{2,3},{3,2},{4,5},{5,4},{6,7},{7,6},{8,9},{9,8},{10,11... | collective-permute-start | bytes 2359304 | tf_op jit(solution)/shard_map/ppermute | solution.py:99
  98.1 54.4 %collective-permute-start.9 = (bf16[240,1024]{1,0:T(8,128)(2,1)}, bf16[240,1024]{1,0:T(8,128)(2,1)S(1)}, u32[]{:S(2)}, u32[]{:S(2)}) collective-permute-start(bf16[240,1024]{1,0:T(8,128)(2,1)} %copy-done.12), channel_id=1, source_target_pairs={{0,64},{8,72},{16,80},{24,88},{32,96},{40,104},{48,112},{56,120},{... | collective-permute-start | bytes 1474568 | tf_op jit(solution)/shard_map/ppermute | solution.py:52
  172.5 35.4 %collective-permute-start.11 = (bf16[240,1024]{1,0:T(8,128)(2,1)}, bf16[240,1024]{1,0:T(8,128)(2,1)}, u32[]{:S(2)}, u32[]{:S(2)}) collective-permute-start(bf16[240,1024]{1,0:T(8,128)(2,1)} %copy-done.27), channel_id=1, source_target_pairs={{0,16},{8,24},{16,32},{24,40},{32,48},{40,56},{48,0},{56,8},{64,80... | collective-permute-start | bytes 1474568 | tf_op jit(solution)/shard_map/ppermute | solution.py:52
  174.2 33.8 %collective-permute-start.12 = (bf16[240,1024]{1,0:T(8,128)(2,1)}, bf16[240,1024]{1,0:T(8,128)(2,1)}, u32[]{:S(2)}, u32[]{:S(2)}) collective-permute-start(bf16[240,1024]{1,0:T(8,128)(2,1)} %copy-done.27), channel_id=1, source_target_pairs={{0,48},{8,56},{16,0},{24,8},{32,16},{40,24},{48,32},{56,40},{64,11... | collective-permute-start | bytes 1474568 | tf_op jit(solution)/shard_map/ppermute | solution.py:52
  176.0 31.9 %collective-permute-start.13 = (bf16[240,1024]{1,0:T(8,128)(2,1)}, bf16[240,1024]{1,0:T(8,128)(2,1)}, u32[]{:S(2)}, u32[]{:S(2)}) collective-permute-start(bf16[240,1024]{1,0:T(8,128)(2,1)} %copy-done.27), channel_id=1, source_target_pairs={{0,32},{8,40},{16,48},{24,56},{32,0},{40,8},{48,16},{56,24},{64,96... | collective-permute-start | bytes 1474568 | tf_op jit(solution)/shard_map/ppermute | solution.py:52
  181.6 247.4 %reduce-scatter.2.cloned.1.call-start = ((), (), s32[]{:S(2)}) async-start(), calls=%async_computation.8 | async-start | bytes 7864320 | tf_op jit(solution)/shard_map/reduce_scatter | solution.py:829
  214.1 27.0 %collective-permute-start.24 = (bf16[4,240,1024]{2,1,0:T(8,128)(2,1)S(1)}, bf16[4,240,1024]{2,1,0:T(8,128)(2,1)}, u32[]{:S(2)}, u32[]{:S(2)}) collective-permute-start(bf16[4,240,1024]{2,1,0:T(8,128)(2,1)S(1)} %pad_maximum_fusion.1.g_mine.routes_mine), channel_id=1, source_target_pairs={{0,8},{8,0},{16,24},{24,16},{32,40},{40,32},{48,56},{56,48},{64,72... | collective-permute-start | bytes 5898248 | tf_op jit(solution)/shard_map/ppermute | solution.py:56
  237.1 28.3 %collective-permute-start.15 = (bf16[224,1024]{1,0:T(8,128)(2,1)S(1)}, bf16[224,1024]{1,0:T(8,128)(2,1)S(1)}, u32[]{:S(2)}, u32[]{:S(2)}) collective-permute-start(bf16[224,1024]{1,0:T(8,128)(2,1)S(1)} %collective-permute-done.14), channel_id=1, source_target_pairs={{0,16},{8,24},{16,32},{24,40},{32,48},{40,56},{48,0},{56,8},{64,80... | collective-permute-start | bytes 1376264 | tf_op jit(solution)/shard_map/ppermute | solution.py:52
  238.2 27.2 %collective-permute-start.16 = (bf16[224,1024]{1,0:T(8,128)(2,1)S(1)}, bf16[224,1024]{1,0:T(8,128)(2,1)}, u32[]{:S(2)}, u32[]{:S(2)}) collective-permute-start(bf16[224,1024]{1,0:T(8,128)(2,1)S(1)} %collective-permute-done.14), channel_id=1, source_target_pairs={{0,48},{8,56},{16,0},{24,8},{32,16},{40,24},{48,32},{56,40},{64,11... | collective-permute-start | bytes 1376264 | tf_op jit(solution)/shard_map/ppermute | solution.py:52
  269.5 29.9 %collective-permute-start.26 = (bf16[256,1024]{1,0:T(8,128)(2,1)}, bf16[256,1024]{1,0:T(8,128)(2,1)S(1)}, u32[]{:S(2)}, u32[]{:S(2)}) collective-permute-start(bf16[256,1024]{1,0:T(8,128)(2,1)} %get-tuple-element.279), channel_id=1, source_target_pairs={{0,48},{8,56},{16,0},{24,8},{32,16},{40,24},{48,32},{56,40},{64,11... | collective-permute-start | bytes 1572872 | tf_op jit(solution)/shard_map/ppermute | solution.py:52
  271.7 27.7 %collective-permute-start.27 = (bf16[256,1024]{1,0:T(8,128)(2,1)}, bf16[256,1024]{1,0:T(8,128)(2,1)S(1)}, u32[]{:S(2)}, u32[]{:S(2)}) collective-permute-start(bf16[256,1024]{1,0:T(8,128)(2,1)} %get-tuple-element.278), channel_id=1, source_target_pairs={{0,16},{8,24},{16,32},{24,40},{32,48},{40,56},{48,0},{56,8},{64,80... | collective-permute-start | bytes 1572872 | tf_op jit(solution)/shard_map/ppermute | solution.py:52
  271.7 27.7 %collective-permute-start.28 = (bf16[256,1024]{1,0:T(8,128)(2,1)S(1)}, bf16[256,1024]{1,0:T(8,128)(2,1)S(1)}, u32[]{:S(2)}, u32[]{:S(2)}) collective-permute-start(bf16[256,1024]{1,0:T(8,128)(2,1)S(1)} %get-tuple-element.277), channel_id=1, source_target_pairs={{0,32},{8,40},{16,48},{24,56},{32,0},{40,8},{48,16},{56,24},{64,96... | collective-permute-start | bytes 1572872 | tf_op jit(solution)/shard_map/ppermute | solution.py:52
  303.9 30.8 %collective-permute-start.33 = (bf16[8,224,1024]{2,1,0:T(8,128)(2,1)}, bf16[8,224,1024]{2,1,0:T(8,128)(2,1)}, u32[]{:S(2)}, u32[]{:S(2)}) collective-permute-start(bf16[8,224,1024]{2,1,0:T(8,128)(2,1)} %get-tuple-element.198), channel_id=1, source_target_pairs={{0,8},{8,0},{16,24},{24,16},{32,40},{40,32},{48,56},{56,48},{64,72... | collective-permute-start | bytes 11010056 | tf_op jit(solution)/shard_map/ppermute | solution.py:56
  308.4 26.4 %collective-permute-start.31 = (bf16[256,1024]{1,0:T(8,128)(2,1)S(1)}, bf16[256,1024]{1,0:T(8,128)(2,1)S(1)}, u32[]{:S(2)}, u32[]{:S(2)}) collective-permute-start(bf16[256,1024]{1,0:T(8,128)(2,1)S(1)} %get-tuple-element.274), channel_id=1, source_target_pairs={{0,16},{8,24},{16,32},{24,40},{32,48},{40,56},{48,0},{56,8},{64,80... | collective-permute-start | bytes 1572872 | tf_op jit(solution)/shard_map/ppermute | solution.py:52
  374.9 48.5 %all-to-all-start.4 = ((bf16[8,128,1152]{2,1,0:T(8,128)(2,1)}), bf16[8,128,1152]{2,1,0:T(8,128)(2,1)S(1)}, u32[]{:S(2)}, u32[]{:S(2)}) async-start(bf16[8,128,1152]{2,1,0:T(8,128)(2,1)} %shard_map.186), calls=%async_computation.4 | async-start | bytes 4718592 | tf_op jit(solution)/shard_map/all_to_all | solution.py:843
  379.2 40.8 %collective-permute-start.35 = (bf16[2,224,1024]{2,1,0:T(8,128)(2,1)}, bf16[2,224,1024]{2,1,0:T(8,128)(2,1)}, u32[]{:S(2)}, u32[]{:S(2)}) collective-permute-start(bf16[2,224,1024]{2,1,0:T(8,128)(2,1)} %get-tuple-element.221), channel_id=1, source_target_pairs={{0,48},{8,56},{16,0},{24,8},{32,16},{40,24},{48,32},{56,40},{64,11... | collective-permute-start | bytes 2752520 | tf_op jit(solution)/shard_map/ppermute | solution.py:52
  380.2 43.2 %collective-permute-start.36 = (bf16[2,224,1024]{2,1,0:T(8,128)(2,1)}, bf16[2,224,1024]{2,1,0:T(8,128)(2,1)}, u32[]{:S(2)}, u32[]{:S(2)}) collective-permute-start(bf16[2,224,1024]{2,1,0:T(8,128)(2,1)} %get-tuple-element.222), channel_id=1, source_target_pairs={{0,16},{8,24},{16,32},{24,40},{32,48},{40,56},{48,0},{56,8},{64,80... | collective-permute-start | bytes 2752520 | tf_op jit(solution)/shard_map/ppermute | solution.py:52
  381.2 42.1 %collective-permute-start.37 = (bf16[2,224,1024]{2,1,0:T(8,128)(2,1)}, bf16[2,224,1024]{2,1,0:T(8,128)(2,1)}, u32[]{:S(2)}, u32[]{:S(2)}) collective-permute-start(bf16[2,224,1024]{2,1,0:T(8,128)(2,1)} %get-tuple-element.223), channel_id=1, source_target_pairs={{0,32},{8,40},{16,48},{24,56},{32,0},{40,8},{48,16},{56,24},{64,96... | collective-permute-start | bytes 2752520 | tf_op jit(solution)/shard_map/ppermute | solution.py:52
  429.0 28.3 %collective-permute-start.43 = (bf16[4,224,1024]{2,1,0:T(8,128)(2,1)}, bf16[4,224,1024]{2,1,0:T(8,128)(2,1)}, u32[]{:S(2)}, u32[]{:S(2)}) collective-permute-start(bf16[4,224,1024]{2,1,0:T(8,128)(2,1)} %get-tuple-element.245), channel_id=1, source_target_pairs={{0,8},{8,0},{16,24},{24,16},{32,40},{40,32},{48,56},{56,48},{64,72... | collective-permute-start | bytes 5505032 | tf_op jit(solution)/shard_map/ppermute | solution.py:56
  434.4 52.1 %collective-permute-start.48 = (bf16[2,192,1024]{2,1,0:T(8,128)(2,1)}, bf16[2,192,1024]{2,1,0:T(8,128)(2,1)}, u32[]{:S(2)}, u32[]{:S(2)}) collective-permute-start(bf16[2,192,1024]{2,1,0:T(8,128)(2,1)} %dynamic-slice_bitcast_fusion), channel_id=1, source_target_pairs={{0,1},{1,0},{2,3},{3,2},{4,5},{5,4},{6,7},{7,6},{8,9},{9,8},{10,11... | collective-permute-start | bytes 2359304 | tf_op jit(solution)/shard_map/ppermute | solution.py:99
  436.1 27.8 %collective-permute-start.40 = (bf16[224,1024]{1,0:T(8,128)(2,1)}, bf16[224,1024]{1,0:T(8,128)(2,1)}, u32[]{:S(2)}, u32[]{:S(2)}) collective-permute-start(bf16[224,1024]{1,0:T(8,128)(2,1)} %get-tuple-element.241), channel_id=1, source_target_pairs={{0,48},{8,56},{16,0},{24,8},{32,16},{40,24},{48,32},{56,40},{64,11... | collective-permute-start | bytes 1376264 | tf_op jit(solution)/shard_map/ppermute | solution.py:52
  436.6 27.3 %collective-permute-start.41 = (bf16[224,1024]{1,0:T(8,128)(2,1)}, bf16[224,1024]{1,0:T(8,128)(2,1)}, u32[]{:S(2)}, u32[]{:S(2)}) collective-permute-start(bf16[224,1024]{1,0:T(8,128)(2,1)} %get-tuple-element.242), channel_id=1, source_target_pairs={{0,16},{8,24},{16,32},{24,40},{32,48},{40,56},{48,0},{56,8},{64,80... | collective-permute-start | bytes 1376264 | tf_op jit(solution)/shard_map/ppermute | solution.py:52
  439.9 35.9 %all-to-all-start.6 = ((bf16[16,8,1152]{2,1,0:T(8,128)(2,1)}), bf16[16,8,1152]{2,1,0:T(8,128)(2,1)}, u32[]{:S(2)}, u32[]{:S(2)}) async-start(bf16[16,8,1152]{2,1,0:T(8,128)(2,1)} %bitcast.173), calls=%async_computation.7 | async-start | bytes 589824 | tf_op jit(solution)/shard_map/all_to_all | solution.py:857
  466.6 28.3 %collective-permute-start.45 = (bf16[224,1024]{1,0:T(8,128)(2,1)}, bf16[224,1024]{1,0:T(8,128)(2,1)}, u32[]{:S(2)}, u32[]{:S(2)}) collective-permute-start(bf16[224,1024]{1,0:T(8,128)(2,1)} %get-tuple-element.252), channel_id=1, source_target_pairs={{0,48},{8,56},{16,0},{24,8},{32,16},{40,24},{48,32},{56,40},{64,11... | collective-permute-start | bytes 1376264 | tf_op jit(solution)/shard_map/ppermute | solution.py:52
  469.6 28.6 %collective-permute-start.46 = (bf16[224,1024]{1,0:T(8,128)(2,1)}, bf16[224,1024]{1,0:T(8,128)(2,1)}, u32[]{:S(2)}, u32[]{:S(2)}) collective-permute-start(bf16[224,1024]{1,0:T(8,128)(2,1)} %get-tuple-element.253), channel_id=1, source_target_pairs={{0,16},{8,24},{16,32},{24,40},{32,48},{40,56},{48,0},{56,8},{64,80... | collective-permute-start | bytes 1376264 | tf_op jit(solution)/shard_map/ppermute | solution.py:52
  (73 other events, 914.5 us)
Sparse Core Ops, SparseCore 0:
  28.0 40.6 all-gather.4
  172.6 39.3 all-gather.6
  334.9 88.5 reduce-scatter.1

commit v13 on v10

--- a/solution.py
+++ b/solution.py
@@ -793,17 +793,19 @@
     attended = lax.all_to_all(attended_head, "seq", 0, 0, tiled=True)
     attended, grad_near = tie(attended, grad_near)
     grad_near = jnp.stack(grad_near)
+    grad_far = [send(grad_near[:2], 1, 0)]
     hidden, normed_ffn = hidden_of(attended, shared, rows, gain_ffn)
     ffn_near, ffn_across = gather_near(normed_ffn)
-    ffn_near, _ = tie(ffn_near, ffn_across)
     grad_near_mine, _ = tie(grad_near, ffn_across)
-    grad_far = send(grad_near_mine, 1, 0)
+    ffn_near, _, grad_far[0] = tie(ffn_near, ffn_across, grad_far[0])
+    grad_far.append(send(grad_near_mine[2:], 1, 0))
     grad_near = (grad_near, swap_cores(grad_near))
     ffn_near, ffn_far = both_cores(ffn_near), gather_far(ffn_across)
     own = jnp.stack([seq_index * 2, own_x])
     near = run_experts(0, own, ffn_near, grad_near, experts, router_t, ())
     near_terms = sum_along_z(*near[:2])
     ffn_far = both_cores(ffn_far)
+    grad_far = jnp.concatenate(grad_far, axis=0)
     grad_far = (grad_far, swap_cores(grad_far))
     far = run_experts(1, own, ffn_far, grad_far, experts, router_t, near[2:])
     far, near_terms = tie(far, near_terms)
@@ -840,21 +842,22 @@
     shared_grads = lax.all_to_all(shared_grads, "wshard", 0, 0, tiled=True)
     projected_grad = attend_back(qkv, head_grad, attended_t, lse, begin, table)
     far_part = project_back(places[8:], projected_grad, head_weights)
-    far_part, shared_grads, moved_terms = tie(far_part, shared_grads, moved_terms)
     far_parts = chip_parts(far_part[0], swap_cores(far_part[1]))
     near_part = project_back(places[:8], projected_grad, head_weights)
-    near_part, expert_grads = tie(near_part, expert_grads)
-    far_parts, projected_grad, shared_grads, moved_terms, expert_grads = tie(
-        far_parts, projected_grad, shared_grads, moved_terms, expert_grads
+    near_part, expert_grads, shared_grads, moved_terms = tie(
+        near_part, expert_grads, shared_grads, moved_terms
+    )
+    near_parts = chip_parts(near_part[0], swap_cores(near_part[1]))
+    far_parts, near_parts, projected_grad, shared_grads, moved_terms = tie(
+        far_parts, near_parts, projected_grad, shared_grads, moved_terms
     )
     far_terms = send_along_z(far_parts)
-    near_parts = chip_parts(near_part[0], swap_cores(near_part[1]))
     moved_crossed = send(add_low(*[t[1] for t in moved_terms]), 1, 0)
     shared_grads = jnp.sum(shared_grads.astype(f32), axis=0).astype(bf16).reshape(16, 8, 1152)
     shared_grads = lax.all_to_all(shared_grads, "seq", 0, 0, tiled=True)
     grad_head = head_weight_grad(places, rows_near, rows_far, gain_attn, projected_grad)
-    far_terms, near_parts, grad_head = tie(far_terms, near_parts, grad_head)
     near_terms = send_along_z(near_parts)
+    far_terms, grad_head, expert_grads = tie(far_terms, grad_head, expert_grads)
     grad_heads = lax.all_to_all(grad_head.reshape(128, 8, 256), BOTH, 0, 0, tiled=True)
     crossed = send(add_low(*far_terms), 1, 0)
     crossed, near_terms, grad_heads, shared_grads = tie(

time: 476 us -> 482 us (1.013)
  the two profiles are of different devices: /device:TPU:1 before, /device:TPU:0 now
where the time goes in v13:
time: 482 us; the launch traced here: 473 us
  Pallas kernels  162 us (34%)
  starting transfers between devices  118 us (24%)
  waiting for transfers between devices  96.9 us (20%)
  other arithmetic  58.1 us (12%)
  local copies, waits for them, and re-layouts  22.1 us (5%)
  between operations  14.9 us (3%)
    ppermute x37, waiting for transfers between devices, send(): return lax.ppermute(rows, 'seq', shift_perm(a, b))  62.1 us
    ppermute x37, starting transfers between devices, send(): return lax.ppermute(rows, 'seq', shift_perm(a, b))  61.3 us
    pallas_call x2, Pallas kernels, run_experts(): pl.pallas_call(experts_kernel, grid_spec=pltpu.PrefetchScalarGridSpec(num...  44 us
    pallas_call x1, Pallas kernels, attend_back(): pl.pallas_call(attend_back_kernel, grid=(GROUP // BLOCK,), in_specs=[whol...  31 us
    convert_element_type x7, other arithmetic, add_low(): return sum([t.astype(f32) for t in terms]).astype(bf16)  20 us
    pallas_call x1, Pallas kernels, attend(): pl.pallas_call(attend_kernel, grid=(GROUP // BLOCK,), in_specs=[whole(GRO...  19.8 us
    all_to_all x1, starting transfers between devices, local(): lax.all_to_all(grad_head.reshape(128, 8, 256), BOTH, 0, 0, tiled=True)  17.4 us
    pallas_call x2, Pallas kernels, project(): pl.pallas_call(project_kernel, grid_spec=pltpu.PrefetchScalarGridSpec(num...  16.6 us
  transfers between devices with their start and end apart: 60, of which 15 were waited for; matrix products, arithmetic and copies ran while one was open for 15% of the time, Pallas kernels for 34%

profile of v13, /device:TPU:0, one launch (start us, length us, event | category | flops | bytes accessed | tf_op | source)
XLA Modules:
  0.0 472.6 jit_solution(16841632722353913470)
XLA Ops:
  19.8 6.8 %all-to-all-start = ((bf16[128,8,256]{2,1,0:T(8,128)(2,1)}), bf16[128,8,256]{2,1,0:T(8,128)(2,1)S(1)}, u32[]{:S(2)}, u32[]{:S(2)}) async-start(bf16[128,8,256]{2,1,0:T(8,128)(2,1)} %bitcast.9), calls=%async_computation | async-start | bytes 1048576 | tf_op jit(solution)/shard_map/all_to_all | solution.py:760
  28.7 7.7 %subtract_cosine_fusion.table = f32[3584,128]{1,0:T(8,128)} fusion(f32[128]{0:T(128)S(1)} %get-tuple-element.289, f32[128]{0:T(128)S(1)} %get-tuple-element.290, f32[3584]{0:T(1024)S(1)} %get-tuple-element.284), kind=kLoop, calls=%fused_computation.9 | loop fusion | flops 917504 | bytes 1850368 | tf_op jit(solution)/shard_map/cos | solution.py:137
  36.4 5.1 %all-to-all-done = bf16[128,8,256]{2,1,0:T(8,128)(2,1)S(1)} async-done(((bf16[128,8,256]{2,1,0:T(8,128)(2,1)}), bf16[128,8,256]{2,1,0:T(8,128)(2,1)S(1)}, u32[]{:S(2)}, u32[]{:S(2)}) %all-to-all-start) | async-done | bytes 524320 | tf_op jit(solution)/shard_map/all_to_all | solution.py:760
  51.6 8.0 %shard_map.178.refs_0_ = bf16[3584,256]{1,0:T(8,128)(2,1)} custom-call(s32[8]{0:T(128)} %get-tuple-element.287.places, bf16[4,224,1024]{2,1,0:T(8,128)(2,1)} %copy-done.1, bf16[4,224,1024]{2,1,0:T(8,128)(2,1)} %collective-permute-done.7.other.near_other, bf16[1024,256]{1,0:T(8,128)(2,1)} %broadcast_select_fusion.w, f32[1,1024]{1,0:T(1,128)} %bitcast.188, ...), custom_call_target="tpu_custom_call" | custom-call | flops 939524096 | bytes 10485760 | tf_op jit(solution)/shard_map/pallas_call | solution.py:174
  59.5 6.0 %collective-permute-done.8 = bf16[2,192,1024]{2,1,0:T(8,128)(2,1)} collective-permute-done((bf16[2,192,1024]{2,1,0:T(8,128)(2,1)}, bf16[2,192,1024]{2,1,0:T(8,128)(2,1)}, u32[]{:S(2)}, u32[]{:S(2)}) %collective-permute-start.8) | collective-permute-done | bytes 786464 | tf_op jit(solution)/shard_map/ppermute | solution.py:99
  74.3 9.0 %all-to-all-start.1 = ((bf16[128,8,1152]{2,1,0:T(8,128)(2,1)}), bf16[128,8,1152]{2,1,0:T(8,128)(2,1)S(1)}, u32[]{:S(2)}, u32[]{:S(2)}) async-start(bf16[128,8,1152]{2,1,0:T(8,128)(2,1)} %broadcast_in_dim.101), calls=%async_computation.1 | async-start | bytes 4718592 | tf_op jit(solution)/shard_map/all_to_all | solution.py:778
  89.7 8.7 %shard_map.179.qkv_ref = bf16[3584,256]{1,0:T(8,128)(2,1)} custom-call(s32[8]{0:T(128)} %get-tuple-element.288.places, bf16[4,224,1024]{2,1,0:T(8,128)(2,1)} %pad_maximum_fusion.2.mine.far_mine, bf16[4,224,1024]{2,1,0:T(8,128)(2,1)} %collective-permute-done.9.other.far_other, bf16[1024,256]{1,0:T(8,128)(2,1)} %broadcast_select_fusion.w, ...), custom_call_target="tpu_custom_call" | custom-call | flops 939524096 | bytes 10485760 | tf_op jit(solution)/shard_map/pallas_call | solution.py:174
  98.4 19.8 %shard_map.180 = (bf16[16,64,224]{2,1,0:T(8,128)(2,1)}, f32[64,3584]{1,0:T(8,128)}, f32[1,3584]{1,0:T(1,128)}) custom-call(bf16[3584,256]{1,0:T(8,128)(2,1)} %shard_map.179.qkv_ref, s32[1,3584]{1,0:T(1,128)} %compare_select_fusion.begin_ref), custom_call_target="tpu_custom_call" | custom-call | flops 7247757312 | bytes 4194304 | tf_op jit(solution)/shard_map/pallas_call | solution.py:324
  118.2 5.3 %all-to-all-start.2 = ((bf16[16,64,224]{2,1,0:T(8,128)(2,1)}), bf16[16,64,224]{2,1,0:T(8,128)(2,1)S(1)}, u32[]{:S(2)}, u32[]{:S(2)}) async-start(bf16[16,64,224]{2,1,0:T(8,128)(2,1)} %get-tuple-element.147), calls=%async_computation.2 | async-start | bytes 1048576 | tf_op jit(solution)/shard_map/all_to_all | solution.py:793
  123.6 12.8 %collective-permute-done.12 = bf16[240,1024]{1,0:T(8,128)(2,1)} collective-permute-done((bf16[240,1024]{1,0:T(8,128)(2,1)S(1)}, bf16[240,1024]{1,0:T(8,128)(2,1)}, u32[]{:S(2)}, u32[]{:S(2)}) %collective-permute-start.12) | collective-permute-done | bytes 491552 | tf_op jit(solution)/shard_map/ppermute | solution.py:52
  154.0 22.4 %collective-permute-done.13 = bf16[224,1024]{1,0:T(8,128)(2,1)S(1)} collective-permute-done((bf16[224,1024]{1,0:T(8,128)(2,1)}, bf16[224,1024]{1,0:T(8,128)(2,1)S(1)}, u32[]{:S(2)}, u32[]{:S(2)}) %collective-permute-start.13) | collective-permute-done | bytes 458784 | tf_op jit(solution)/shard_map/ppermute | solution.py:52
  188.4 21.9 %shard_map.182 = (bf16[4,256,1024]{2,1,0:T(8,128)(2,1)}, bf16[4,256,1024]{2,1,0:T(8,128)(2,1)}, bf16[8,224,1024]{2,1,0:T(8,128)(2,1)}, bf16[8,224,1024]{2,1,0:T(...) custom-call(s32[2]{0:T(128)} %pad_add_fusion.own_ref, ...), custom_call_target="tpu_custom_call" | custom-call | flops 15032385536 | bytes 25165824 | tf_op jit(solution)/shard_map/pallas_call | solution.py:555
  223.7 22.1 %shard_map.183 = (bf16[4,256,1024]{2,1,0:T(8,128)(2,1)}, bf16[4,256,1024]{2,1,0:T(8,128)(2,1)}, bf16[8,224,1024]{2,1,0:T(8,128)(2,1)}, bf16[8,224,1024]{2,1,0:T(...) custom-call(s32[2]{0:T(128)} %pad_add_fusion.own_ref, ...), custom_call_target="tpu_custom_call", output_to_operand_aliasing={{2}: (10, {}), {3}: (11, {}), {4}: (12, {}), {5}: (13, {}),... | custom-call | flops 15032385536 | bytes 25165824 | tf_op jit(solution)/shard_map/pallas_call | solution.py:555
  246.0 4.4 collective-permute-done.30
  257.1 15.9 %shard_map.184 = bf16[4,2,2,192,1024]{4,3,2,1,0:T(8,128)(2,1)} custom-call(bf16[2,1152,1024]{2,1,0:T(8,128)(2,1)} %get-tuple-element.188.x_ref, bf16[2,1152,1024]{2,1,0:T(8,128)(2,1)} %get-tuple-element.189.dh_ref, bf16[2,1152,512]{2,1,0:T(8,128)(2,1)} %get-tuple-element.190.act_ref, bf16[2,1152,1024]{2,1,0:T(8,128)(2,1)} %get-tuple-element.191.dy_ref), custom_call_target="tpu_custom_call" | custom-call | flops 8589934592 | bytes 14680064 | tf_op jit(solution)/shard_map/pallas_call | solution.py:611
  273.0 7.8 %collective-permute-done.32 = bf16[256,1024]{1,0:T(8,128)(2,1)S(1)} collective-permute-done((bf16[256,1024]{1,0:T(8,128)(2,1)S(1)}, bf16[256,1024]{1,0:T(8,128)(2,1)S(1)}, u32[]{:S(2)}, u32[]{:S(2)}) %collective-permute-start.32) | collective-permute-done | bytes 524320 | tf_op jit(solution)/shard_map/ppermute | solution.py:52
  283.1 6.5 %fusion.10 = (bf16[2,224,1024]{2,1,0:T(8,128)(2,1)}, bf16[2,224,1024]{2,1,0:T(8,128)(2,1)}, bf16[2,224,1024]{2,1,0:T(8,128)(2,1)}, bf16[2,224,1024]{2,1,0:T(8,128)(2,1)}) fusion(bf16[2,4,224,1024]{3,2,1,0:T(8,128)(2,1)} %bitcast.49, bf16[2,4,224,1024]{3,2,1,0:T(8,128)(2,1)} %bitcast.171), kind=kLoop, calls=%fused_computation.36 | loop fusion | flops 7340032 | bytes 11010048 | tf_op jit(solution)/shard_map/convert_element_type | solution.py:83
  289.5 6.0 %collective-permute-done.35.crossed = bf16[256,1024]{1,0:T(8,128)(2,1)S(1)} collective-permute-done((bf16[256,1024]{1,0:T(8,128)(2,1)S(1)}, bf16[256,1024]{1,0:T(8,128)(2,1)S(1)}, u32[]{:S(2)}, u32[]{:S(2)}) %collective-permute-start.35) | collective-permute-done | bytes 524320 | tf_op jit(solution)/shard_map/ppermute | solution.py:52
  296.3 5.8 %shard_map.185 = (f32[224,1024]{1,0:T(8,128)}, bf16[224,1024]{1,0:T(8,128)(2,1)}, bf16[32,224]{1,0:T(8,128)(2,1)}, bf16[224,1024]{1,0:T(8,128)(2,1)}, bf16[16,64,224]{2,1,0:T(8,128)(2,1)}) custom-call(bf16[256,1024]{1,0:T(8,128)(2,1)} %get-tuple-element.180.t0, bf16[256,1024]{1,0:T(8,128)(2,1)} %copy-done.17, bf16[256,1024]{1,0:T(8,128)(2,1)} %copy-done.18, ...), custom_call_target="tpu_custom_call" | custom-call | flops 469762048 | bytes 8388608 | tf_op jit(solution)/shard_map/pallas_call | solution.py:682
  302.2 3.8 all-to-all-start.3
  306.0 3.9 shard_map.186
  309.9 8.4 %all-to-all-done.3.g_ref = bf16[16,64,224]{2,1,0:T(8,128)(2,1)S(1)} async-done(((bf16[16,64,224]{2,1,0:T(8,128)(2,1)}), bf16[16,64,224]{2,1,0:T(8,128)(2,1)S(1)}, u32[]{:S(2)}, u32[]{:S(2)}) %all-to-all-start.3) | async-done | bytes 458784 | tf_op jit(solution)/shard_map/all_to_all | solution.py:835
  320.8 5.1 %all-to-all-start.4 = ((bf16[8,128,1152]{2,1,0:T(8,128)(2,1)}), bf16[8,128,1152]{2,1,0:T(8,128)(2,1)S(1)}, u32[]{:S(2)}, u32[]{:S(2)}) async-start(bf16[8,128,1152]{2,1,0:T(8,128)(2,1)} %shard_map.186), calls=%async_computation.5 | async-start | bytes 4718592 | tf_op jit(solution)/shard_map/all_to_all | solution.py:842
  325.9 31.0 %shard_map.187.first.second = bf16[3584,256]{1,0:T(8,128)(2,1)} custom-call(bf16[3584,256]{1,0:T(8,128)(2,1)} %shard_map.179.qkv_ref, bf16[16,64,224]{2,1,0:T(8,128)(2,1)} %copy-done.22, f32[64,3584]{1,0:T(8,128)} %get-tuple-element.209.ot_ref, f32[1,3584]{1,0:T(1,128)} %get-tuple-element.210.lse_ref, s32[1,3584]{1,0:T(1,128)} %compare_select_fusion.begin_ref, ...), custom_call_target="tpu_custom_call" | custom-call | flops 18119393280 | bytes 8388608 | tf_op jit(solution)/shard_map/pallas_call | solution.py:404
  356.9 5.4 %shard_map.188 = (bf16[4,224,1024]{2,1,0:T(8,128)(2,1)}, bf16[4,224,1024]{2,1,0:T(8,128)(2,1)}) custom-call(s32[8]{0:T(128)} %get-tuple-element.288.places, bf16[3584,256]{1,0:T(8,128)(2,1)} %shard_map.187.first.second, bf16[3584,256]{1,0:T(8,128)(2,1)} %shard_map.187.first.second, bf16[1024,256]{1,0:T(8,128)(2,1)} %broadcast_select_fusion.w), custom_call_target="tpu_custom_call" | custom-call | flops 939524096 | bytes 5242880 | tf_op jit(solution)/shard_map/pallas_call | solution.py:201
  362.6 5.5 %shard_map.189 = (bf16[4,224,1024]{2,1,0:T(8,128)(2,1)}, bf16[4,224,1024]{2,1,0:T(8,128)(2,1)}) custom-call(s32[8]{0:T(128)} %get-tuple-element.287.places, bf16[3584,256]{1,0:T(8,128)(2,1)} %shard_map.187.first.second, bf16[3584,256]{1,0:T(8,128)(2,1)} %shard_map.187.first.second, bf16[1024,256]{1,0:T(8,128)(2,1)} %broadcast_select_fusion.w), custom_call_target="tpu_custom_call" | custom-call | flops 939524096 | bytes 5242880 | tf_op jit(solution)/shard_map/pallas_call | solution.py:201
  368.7 3.8 fusion.25
  382.7 5.4 %all-to-all-start.6 = ((bf16[16,8,1152]{2,1,0:T(8,128)(2,1)}), bf16[16,8,1152]{2,1,0:T(8,128)(2,1)S(1)}, u32[]{:S(2)}, u32[]{:S(2)}) async-start(bf16[16,8,1152]{2,1,0:T(8,128)(2,1)} %bitcast.68), calls=%async_computation.7 | async-start | bytes 589824 | tf_op jit(solution)/shard_map/all_to_all | solution.py:857
  394.0 10.8 %shard_map.190 = bf16[1024,256]{1,0:T(8,128)(2,1)} custom-call(s32[16]{0:T(128)} %copy-done.35, bf16[4,224,1024]{2,1,0:T(8,128)(2,1)} %copy-done.1, bf16[4,224,1024]{2,1,0:T(8,128)(2,1)} %collective-permute-done.7.other.near_other, bf16[4,224,1024]{2,1,0:T(8,128)(2,1)} %pad_maximum_fusion.2.mine.far_mine, ...), custom_call_target="tpu_custom_call" | custom-call | flops 1879048192 | bytes 10485760 | tf_op jit(solution)/shard_map/pallas_call | solution.py:239
  411.3 17.4 %all-to-all-start.5 = ((bf16[128,8,256]{2,1,0:T(8,128)(2,1)}), bf16[128,8,256]{2,1,0:T(8,128)(2,1)S(1)}, u32[]{:S(2)}, u32[]{:S(2)}) async-start(bf16[128,8,256]{2,1,0:T(8,128)(2,1)} %bitcast.173), calls=%async_computation.6 | async-start | bytes 1048576 | tf_op jit(solution)/shard_map/all_to_all | solution.py:861
  439.0 8.5 %collective-permute-done.45 = bf16[224,1024]{1,0:T(8,128)(2,1)} collective-permute-done((bf16[224,1024]{1,0:T(8,128)(2,1)}, bf16[224,1024]{1,0:T(8,128)(2,1)}, u32[]{:S(2)}, u32[]{:S(2)}) %collective-permute-start.45) | collective-permute-done | bytes 458784 | tf_op jit(solution)/shard_map/ppermute | solution.py:52
  456.5 5.8 %collective-permute-done.49 = bf16[2,192,1024]{2,1,0:T(8,128)(2,1)} collective-permute-done((bf16[2,192,1024]{2,1,0:T(8,128)(2,1)}, bf16[2,192,1024]{2,1,0:T(8,128)(2,1)}, u32[]{:S(2)}, u32[]{:S(2)}) %collective-permute-start.49) | collective-permute-done | bytes 786464 | tf_op jit(solution)/shard_map/ppermute | solution.py:99
  (272 shorter events, 141.0 us)
Async XLA Ops:
  7.2 35.1 %collective-permute-start = (bf16[224,1024]{1,0:T(8,128)(2,1)}, bf16[224,1024]{1,0:T(8,128)(2,1)S(1)}, u32[]{:S(2)}, u32[]{:S(2)}) collective-permute-start(bf16[224,1024]{1,0:T(8,128)(2,1)} %bitcast.162), channel_id=1, source_target_pairs={{0,64},{8,72},{16,80},{24,88},{32,96},{40,104},{48,112},{56,120},{... | collective-permute-start | bytes 1376264 | tf_op jit(solution)/shard_map/ppermute | solution.py:52
  10.4 32.0 %collective-permute-start.4 = (bf16[224,1024]{1,0:T(8,128)(2,1)}, bf16[224,1024]{1,0:T(8,128)(2,1)S(1)}, u32[]{:S(2)}, u32[]{:S(2)}) collective-permute-start(bf16[224,1024]{1,0:T(8,128)(2,1)} %bitcast.163), channel_id=1, source_target_pairs={{0,16},{8,24},{16,32},{24,40},{32,48},{40,56},{48,0},{56,8},{64,80... | collective-permute-start | bytes 1376264 | tf_op jit(solution)/shard_map/ppermute | solution.py:52
  12.3 30.1 %collective-permute-start.5 = (bf16[224,1024]{1,0:T(8,128)(2,1)}, bf16[224,1024]{1,0:T(8,128)(2,1)S(1)}, u32[]{:S(2)}, u32[]{:S(2)}) collective-permute-start(bf16[224,1024]{1,0:T(8,128)(2,1)} %bitcast.164), channel_id=1, source_target_pairs={{0,48},{8,56},{16,0},{24,8},{32,16},{40,24},{48,32},{56,40},{64,11... | collective-permute-start | bytes 1376264 | tf_op jit(solution)/shard_map/ppermute | solution.py:52
  14.4 28.0 %collective-permute-start.6 = (bf16[224,1024]{1,0:T(8,128)(2,1)}, bf16[224,1024]{1,0:T(8,128)(2,1)S(1)}, u32[]{:S(2)}, u32[]{:S(2)}) collective-permute-start(bf16[224,1024]{1,0:T(8,128)(2,1)} %bitcast.165), channel_id=1, source_target_pairs={{0,32},{8,40},{16,48},{24,56},{32,0},{40,8},{48,16},{56,24},{64,96... | collective-permute-start | bytes 1376264 | tf_op jit(solution)/shard_map/ppermute | solution.py:52
  26.6 161.8 %all-gather.5.cloned.1.call-start = ((), (), s32[]{:S(2)}) async-start(), calls=%async_computation.9 | async-start | bytes 3932160 | tf_op jit(solution)/shard_map/all_gather | solution.py:770
  74.3 43.9 %all-to-all-start.1 = ((bf16[128,8,1152]{2,1,0:T(8,128)(2,1)}), bf16[128,8,1152]{2,1,0:T(8,128)(2,1)S(1)}, u32[]{:S(2)}, u32[]{:S(2)}) async-start(bf16[128,8,1152]{2,1,0:T(8,128)(2,1)} %broadcast_in_dim.101), calls=%async_computation.1 | async-start | bytes 4718592 | tf_op jit(solution)/shard_map/all_to_all | solution.py:778
  83.3 105.1 %all-gather.7.cloned.1.call-start = ((), (), s32[]{:S(2)}) async-start(), calls=%async_computation.10 | async-start | bytes 3932160 | tf_op jit(solution)/shard_map/all_gather | solution.py:770
  84.7 39.0 %collective-permute-start.10 = (bf16[240,1024]{1,0:T(8,128)(2,1)S(1)}, bf16[240,1024]{1,0:T(8,128)(2,1)}, u32[]{:S(2)}, u32[]{:S(2)}) collective-permute-start(bf16[240,1024]{1,0:T(8,128)(2,1)S(1)} %fusion.21), channel_id=1, source_target_pairs={{0,16},{8,24},{16,32},{24,40},{32,48},{40,56},{48,0},{56,8},{64,80... | collective-permute-start | bytes 1474568 | tf_op jit(solution)/shard_map/ppermute | solution.py:52
  85.7 37.9 %collective-permute-start.11 = (bf16[240,1024]{1,0:T(8,128)(2,1)S(1)}, bf16[240,1024]{1,0:T(8,128)(2,1)}, u32[]{:S(2)}, u32[]{:S(2)}) collective-permute-start(bf16[240,1024]{1,0:T(8,128)(2,1)S(1)} %fusion.21), channel_id=1, source_target_pairs={{0,48},{8,56},{16,0},{24,8},{32,16},{40,24},{48,32},{56,40},{64,11... | collective-permute-start | bytes 1474568 | tf_op jit(solution)/shard_map/ppermute | solution.py:52
  87.9 48.5 %collective-permute-start.12 = (bf16[240,1024]{1,0:T(8,128)(2,1)S(1)}, bf16[240,1024]{1,0:T(8,128)(2,1)}, u32[]{:S(2)}, u32[]{:S(2)}) collective-permute-start(bf16[240,1024]{1,0:T(8,128)(2,1)S(1)} %fusion.21), channel_id=1, source_target_pairs={{0,32},{8,40},{16,48},{24,56},{32,0},{40,8},{48,16},{56,24},{64,96... | collective-permute-start | bytes 1474568 | tf_op jit(solution)/shard_map/ppermute | solution.py:52
  123.6 244.6 %reduce-scatter.2.cloned.1.call-start = ((), (), s32[]{:S(2)}) async-start(), calls=%async_computation.8 | async-start | bytes 7864320 | tf_op jit(solution)/shard_map/reduce_scatter | solution.py:828
  141.1 35.3 %collective-permute-start.21 = (bf16[2,240,1024]{2,1,0:T(8,128)(2,1)}, bf16[2,240,1024]{2,1,0:T(8,128)(2,1)}, u32[]{:S(2)}, u32[]{:S(2)}) collective-permute-start(bf16[2,240,1024]{2,1,0:T(8,128)(2,1)} %pad_maximum_fusion.5), channel_id=1, source_target_pairs={{0,64},{8,72},{16,80},{24,88},{32,96},{40,104},{48,112},{56,120},{... | collective-permute-start | bytes 2949128 | tf_op jit(solution)/shard_map/ppermute | solution.py:52
  148.2 28.2 %collective-permute-start.13 = (bf16[224,1024]{1,0:T(8,128)(2,1)}, bf16[224,1024]{1,0:T(8,128)(2,1)S(1)}, u32[]{:S(2)}, u32[]{:S(2)}) collective-permute-start(bf16[224,1024]{1,0:T(8,128)(2,1)} %get-tuple-element.160.normed_ref), channel_id=1, source_target_pairs={{0,64},{8,72},{16,80},{24,88},{32,96},{40,104},{48,112},{56,120},{... | collective-permute-start | bytes 1376264 | tf_op jit(solution)/shard_map/ppermute | solution.py:52
  149.1 27.3 %collective-permute-start.18 = (bf16[224,1024]{1,0:T(8,128)(2,1)}, bf16[224,1024]{1,0:T(8,128)(2,1)S(1)}, u32[]{:S(2)}, u32[]{:S(2)}) collective-permute-start(bf16[224,1024]{1,0:T(8,128)(2,1)} %get-tuple-element.160.normed_ref), channel_id=1, source_target_pairs={{0,16},{8,24},{16,32},{24,40},{32,48},{40,56},{48,0},{56,8},{64,80... | collective-permute-start | bytes 1376264 | tf_op jit(solution)/shard_map/ppermute | solution.py:52
  181.7 30.0 %collective-permute-start.22 = (bf16[2,240,1024]{2,1,0:T(8,128)(2,1)}, bf16[2,240,1024]{2,1,0:T(8,128)(2,1)S(1)}, u32[]{:S(2)}, u32[]{:S(2)}) collective-permute-start(bf16[2,240,1024]{2,1,0:T(8,128)(2,1)} %slice.206), channel_id=1, source_target_pairs={{0,64},{8,72},{16,80},{24,88},{32,96},{40,104},{48,112},{56,120},{... | collective-permute-start | bytes 2949128 | tf_op jit(solution)/shard_map/ppermute | solution.py:52
  184.4 27.9 %collective-permute-start.14 = (bf16[224,1024]{1,0:T(8,128)(2,1)S(1)}, bf16[224,1024]{1,0:T(8,128)(2,1)}, u32[]{:S(2)}, u32[]{:S(2)}) collective-permute-start(bf16[224,1024]{1,0:T(8,128)(2,1)S(1)} %collective-permute-done.13), channel_id=1, source_target_pairs={{0,16},{8,24},{16,32},{24,40},{32,48},{40,56},{48,0},{56,8},{64,80... | collective-permute-start | bytes 1376264 | tf_op jit(solution)/shard_map/ppermute | solution.py:52
  216.6 29.2 %collective-permute-start.27 = (bf16[256,1024]{1,0:T(8,128)(2,1)}, bf16[256,1024]{1,0:T(8,128)(2,1)S(1)}, u32[]{:S(2)}, u32[]{:S(2)}) collective-permute-start(bf16[256,1024]{1,0:T(8,128)(2,1)} %get-tuple-element.271), channel_id=1, source_target_pairs={{0,48},{8,56},{16,0},{24,8},{32,16},{40,24},{48,32},{56,40},{64,11... | collective-permute-start | bytes 1572872 | tf_op jit(solution)/shard_map/ppermute | solution.py:52
  218.5 27.3 %collective-permute-start.28 = (bf16[256,1024]{1,0:T(8,128)(2,1)}, bf16[256,1024]{1,0:T(8,128)(2,1)S(1)}, u32[]{:S(2)}, u32[]{:S(2)}) collective-permute-start(bf16[256,1024]{1,0:T(8,128)(2,1)} %get-tuple-element.270), channel_id=1, source_target_pairs={{0,16},{8,24},{16,32},{24,40},{32,48},{40,56},{48,0},{56,8},{64,80... | collective-permute-start | bytes 1572872 | tf_op jit(solution)/shard_map/ppermute | solution.py:52
  250.3 30.5 %collective-permute-start.34 = (bf16[8,224,1024]{2,1,0:T(8,128)(2,1)}, bf16[8,224,1024]{2,1,0:T(8,128)(2,1)}, u32[]{:S(2)}, u32[]{:S(2)}) collective-permute-start(bf16[8,224,1024]{2,1,0:T(8,128)(2,1)} %get-tuple-element.192), channel_id=1, source_target_pairs={{0,8},{8,0},{16,24},{24,16},{32,40},{40,32},{48,56},{56,48},{64,72... | collective-permute-start | bytes 11010056 | tf_op jit(solution)/shard_map/ppermute | solution.py:56
  318.4 49.7 %collective-permute-start.37 = (bf16[2,224,1024]{2,1,0:T(8,128)(2,1)}, bf16[2,224,1024]{2,1,0:T(8,128)(2,1)}, u32[]{:S(2)}, u32[]{:S(2)}) collective-permute-start(bf16[2,224,1024]{2,1,0:T(8,128)(2,1)} %get-tuple-element.218), channel_id=1, source_target_pairs={{0,48},{8,56},{16,0},{24,8},{32,16},{40,24},{48,32},{56,40},{64,11... | collective-permute-start | bytes 2752520 | tf_op jit(solution)/shard_map/ppermute | solution.py:52
  319.4 48.7 %collective-permute-start.38 = (bf16[2,224,1024]{2,1,0:T(8,128)(2,1)}, bf16[2,224,1024]{2,1,0:T(8,128)(2,1)}, u32[]{:S(2)}, u32[]{:S(2)}) collective-permute-start(bf16[2,224,1024]{2,1,0:T(8,128)(2,1)} %get-tuple-element.219), channel_id=1, source_target_pairs={{0,16},{8,24},{16,32},{24,40},{32,48},{40,56},{48,0},{56,8},{64,80... | collective-permute-start | bytes 2752520 | tf_op jit(solution)/shard_map/ppermute | solution.py:52
  320.4 47.7 %collective-permute-start.39 = (bf16[2,224,1024]{2,1,0:T(8,128)(2,1)}, bf16[2,224,1024]{2,1,0:T(8,128)(2,1)}, u32[]{:S(2)}, u32[]{:S(2)}) collective-permute-start(bf16[2,224,1024]{2,1,0:T(8,128)(2,1)} %get-tuple-element.220), channel_id=1, source_target_pairs={{0,32},{8,40},{16,48},{24,56},{32,0},{40,8},{48,16},{56,24},{64,96... | collective-permute-start | bytes 2752520 | tf_op jit(solution)/shard_map/ppermute | solution.py:52
  320.8 47.3 %all-to-all-start.4 = ((bf16[8,128,1152]{2,1,0:T(8,128)(2,1)}), bf16[8,128,1152]{2,1,0:T(8,128)(2,1)S(1)}, u32[]{:S(2)}, u32[]{:S(2)}) async-start(bf16[8,128,1152]{2,1,0:T(8,128)(2,1)} %shard_map.186), calls=%async_computation.5 | async-start | bytes 4718592 | tf_op jit(solution)/shard_map/all_to_all | solution.py:842
  374.2 30.5 %collective-permute-start.42 = (bf16[224,1024]{1,0:T(8,128)(2,1)}, bf16[224,1024]{1,0:T(8,128)(2,1)}, u32[]{:S(2)}, u32[]{:S(2)}) collective-permute-start(bf16[224,1024]{1,0:T(8,128)(2,1)} %get-tuple-element.234), channel_id=1, source_target_pairs={{0,48},{8,56},{16,0},{24,8},{32,16},{40,24},{48,32},{56,40},{64,11... | collective-permute-start | bytes 1376264 | tf_op jit(solution)/shard_map/ppermute | solution.py:52
  376.5 29.8 %collective-permute-start.43 = (bf16[224,1024]{1,0:T(8,128)(2,1)}, bf16[224,1024]{1,0:T(8,128)(2,1)}, u32[]{:S(2)}, u32[]{:S(2)}) collective-permute-start(bf16[224,1024]{1,0:T(8,128)(2,1)} %get-tuple-element.235), channel_id=1, source_target_pairs={{0,16},{8,24},{16,32},{24,40},{32,48},{40,56},{48,0},{56,8},{64,80... | collective-permute-start | bytes 1376264 | tf_op jit(solution)/shard_map/ppermute | solution.py:52
  376.8 32.1 %collective-permute-start.44 = (bf16[224,1024]{1,0:T(8,128)(2,1)S(1)}, bf16[224,1024]{1,0:T(8,128)(2,1)}, u32[]{:S(2)}, u32[]{:S(2)}) collective-permute-start(bf16[224,1024]{1,0:T(8,128)(2,1)S(1)} %get-tuple-element.236), channel_id=1, source_target_pairs={{0,32},{8,40},{16,48},{24,56},{32,0},{40,8},{48,16},{56,24},{64,96... | collective-permute-start | bytes 1376264 | tf_op jit(solution)/shard_map/ppermute | solution.py:52
  379.3 59.6 %collective-permute-start.46 = (bf16[224,1024]{1,0:T(8,128)(2,1)}, bf16[224,1024]{1,0:T(8,128)(2,1)}, u32[]{:S(2)}, u32[]{:S(2)}) collective-permute-start(bf16[224,1024]{1,0:T(8,128)(2,1)} %get-tuple-element.244), channel_id=1, source_target_pairs={{0,48},{8,56},{16,0},{24,8},{32,16},{40,24},{48,32},{56,40},{64,11... | collective-permute-start | bytes 1376264 | tf_op jit(solution)/shard_map/ppermute | solution.py:52
  382.7 27.9 %all-to-all-start.6 = ((bf16[16,8,1152]{2,1,0:T(8,128)(2,1)}), bf16[16,8,1152]{2,1,0:T(8,128)(2,1)S(1)}, u32[]{:S(2)}, u32[]{:S(2)}) async-start(bf16[16,8,1152]{2,1,0:T(8,128)(2,1)} %bitcast.68), calls=%async_computation.7 | async-start | bytes 589824 | tf_op jit(solution)/shard_map/all_to_all | solution.py:857
  390.6 45.2 %collective-permute-start.41 = (bf16[224,1024]{1,0:T(8,128)(2,1)}, bf16[224,1024]{1,0:T(8,128)(2,1)}, u32[]{:S(2)}, u32[]{:S(2)}) collective-permute-start(bf16[224,1024]{1,0:T(8,128)(2,1)} %fusion.30), channel_id=1, source_target_pairs={{0,64},{8,72},{16,80},{24,88},{32,96},{40,104},{48,112},{56,120},{... | collective-permute-start | bytes 1376264 | tf_op jit(solution)/shard_map/ppermute | solution.py:52
  404.7 34.2 %collective-permute-start.47 = (bf16[224,1024]{1,0:T(8,128)(2,1)}, bf16[224,1024]{1,0:T(8,128)(2,1)}, u32[]{:S(2)}, u32[]{:S(2)}) collective-permute-start(bf16[224,1024]{1,0:T(8,128)(2,1)} %get-tuple-element.245), channel_id=1, source_target_pairs={{0,16},{8,24},{16,32},{24,40},{32,48},{40,56},{48,0},{56,8},{64,80... | collective-permute-start | bytes 1376264 | tf_op jit(solution)/shard_map/ppermute | solution.py:52
  406.3 32.7 %collective-permute-start.48 = (bf16[224,1024]{1,0:T(8,128)(2,1)}, bf16[224,1024]{1,0:T(8,128)(2,1)}, u32[]{:S(2)}, u32[]{:S(2)}) collective-permute-start(bf16[224,1024]{1,0:T(8,128)(2,1)} %get-tuple-element.246), channel_id=1, source_target_pairs={{0,32},{8,40},{16,48},{24,56},{32,0},{40,8},{48,16},{56,24},{64,96... | collective-permute-start | bytes 1376264 | tf_op jit(solution)/shard_map/ppermute | solution.py:52
  411.3 36.2 %all-to-all-start.5 = ((bf16[128,8,256]{2,1,0:T(8,128)(2,1)}), bf16[128,8,256]{2,1,0:T(8,128)(2,1)S(1)}, u32[]{:S(2)}, u32[]{:S(2)}) async-start(bf16[128,8,256]{2,1,0:T(8,128)(2,1)} %bitcast.173), calls=%async_computation.6 | async-start | bytes 1048576 | tf_op jit(solution)/shard_map/all_to_all | solution.py:861
  (70 other events, 845.9 us)
Sparse Core Ops, SparseCore 0:
  29.1 40.6 all-gather.4
  85.8 50.9 all-gather.6
  281.0 85.6 reduce-scatter.1

commit v14 on v13

--- a/solution.py
+++ b/solution.py
@@ -19,6 +19,7 @@
 ALL_ROWS = 16 * SLOTS
 BLOCK = 512
 VMEM_LIMIT = 60 << 20
+LAST = TOK + 16
 PAY = TOK + 32
 
 norm_eps = 1e-06
@@ -188,22 +189,32 @@
     )(places, *gathered, w, gain, table, *before)
 
 
-def project_back_kernel(places, first, second, w, mine, other):
+def project_back_kernel(places, first, second, w, first_shared, second_shared, mine, other):
     del places
-    mine[0] = lax.dot_general(first[...], w[...], NT, preferred_element_type=f32).astype(bf16)
-    other[0] = lax.dot_general(second[...], w[...], NT, preferred_element_type=f32).astype(bf16)
-
-
-def project_back(places, projected_grad, w):
-    chip = pl.BlockSpec((1, TOK, WIDTH), lambda j, p: (j, 0, 0))
-    at = lambda k: pl.BlockSpec((TOK, 256), lambda j, p: (p[2 * j + k], 0))
-    part = jax.ShapeDtypeStruct((4, TOK, WIDTH), bf16)
+    for projected, shared, out in ((first, first_shared, mine), (second, second_shared, other)):
+        out[0, :TOK, :] = lax.dot_general(
+            projected[...], w[...], NT, preferred_element_type=f32
+        ).astype(bf16)
+        rest = jnp.concatenate([shared[:, WIDTH:], jnp.zeros((8, WIDTH - 128), f32)], axis=1)
+        out[0, TOK:, :] = jnp.concatenate([shared[:, :WIDTH], rest], axis=0).astype(bf16)
+
+
+def project_back(places, projected_grad, w, shared):
+    chip = pl.BlockSpec((1, LAST, WIDTH), lambda j, p: (j, 0, 0))
+    at = lambda k, rows, n: pl.BlockSpec((rows, n), lambda j, p: (p[2 * j + k], 0))
+    part = jax.ShapeDtypeStruct((4, LAST, WIDTH), bf16)
     return pl.pallas_call(
         project_back_kernel,
         grid_spec=pltpu.PrefetchScalarGridSpec(
             num_scalar_prefetch=1,
             grid=(4,),
-            in_specs=[at(0), at(1), pl.BlockSpec((WIDTH, 256), lambda j, p: (0, 0))],
+            in_specs=[
+                at(0, TOK, 256),
+                at(1, TOK, 256),
+                pl.BlockSpec((WIDTH, 256), lambda j, p: (0, 0)),
+                at(0, 8, 1152),
+                at(1, 8, 1152),
+            ],
             out_specs=[chip, chip],
         ),
         out_shape=[part, part],
@@ -211,7 +222,7 @@
         cost_estimate=pl.CostEstimate(
             flops=2 * 8 * TOK * WIDTH * 256, bytes_accessed=5 << 20, transcendentals=0
         ),
-    )(places, projected_grad, projected_grad, w)
+    )(places, projected_grad, projected_grad, w, shared, shared)
 
 
 def head_grad_kernel(places, near_mine, near_other, far_mine, far_other, gain, first, second, out, total):
@@ -841,35 +852,29 @@
 
     shared_grads = lax.all_to_all(shared_grads, "wshard", 0, 0, tiled=True)
     projected_grad = attend_back(qkv, head_grad, attended_t, lse, begin, table)
-    far_part = project_back(places[8:], projected_grad, head_weights)
+    shared_grads = jnp.sum(shared_grads.astype(f32), axis=0)
+    far_part = project_back(places[8:], projected_grad, head_weights, shared_grads)
+    near_part = project_back(places[:8], projected_grad, head_weights, shared_grads)
     far_parts = chip_parts(far_part[0], swap_cores(far_part[1]))
-    near_part = project_back(places[:8], projected_grad, head_weights)
-    near_part, expert_grads, shared_grads, moved_terms = tie(
-        near_part, expert_grads, shared_grads, moved_terms
-    )
+    near_part, moved_terms, expert_grads = tie(near_part, moved_terms, expert_grads)
     near_parts = chip_parts(near_part[0], swap_cores(near_part[1]))
-    far_parts, near_parts, projected_grad, shared_grads, moved_terms = tie(
-        far_parts, near_parts, projected_grad, shared_grads, moved_terms
+    far_parts, near_parts, projected_grad, moved_terms, expert_grads = tie(
+        far_parts, near_parts, projected_grad, moved_terms, expert_grads
     )
     far_terms = send_along_z(far_parts)
+    near_terms = send_along_z(near_parts)
     moved_crossed = send(add_low(*[t[1] for t in moved_terms]), 1, 0)
-    shared_grads = jnp.sum(shared_grads.astype(f32), axis=0).astype(bf16).reshape(16, 8, 1152)
-    shared_grads = lax.all_to_all(shared_grads, "seq", 0, 0, tiled=True)
     grad_head = head_weight_grad(places, rows_near, rows_far, gain_attn, projected_grad)
-    near_terms = send_along_z(near_parts)
-    far_terms, grad_head, expert_grads = tie(far_terms, grad_head, expert_grads)
     grad_heads = lax.all_to_all(grad_head.reshape(128, 8, 256), BOTH, 0, 0, tiled=True)
     crossed = send(add_low(*far_terms), 1, 0)
-    crossed, near_terms, grad_heads, shared_grads = tie(
-        crossed, near_terms, grad_heads, shared_grads
-    )
+    crossed, near_terms, grad_heads = tie(crossed, near_terms, grad_heads)
     kept = lax.dynamic_index_in_dim(expert_grads, own_x, 0, keepdims=False)
     sent = lax.dynamic_index_in_dim(expert_grads, 1 - own_x, 0, keepdims=False)
     expert_grads = kept.astype(f32) + swap_x(sent).astype(f32)
     total = lambda terms: sum([t.astype(f32) for t in terms])
     output = (hidden + total([t[0] for t in moved_terms] + [moved_crossed])).astype(bf16)
-    normed_grad = total(near_terms + [crossed])
-    shared_grads = jnp.sum(shared_grads.astype(f32), axis=0)
+    last_sum = total(near_terms + [crossed])
+    normed_grad, shared_grads = last_sum[:TOK], last_sum[TOK:]
     grad_heads = jnp.sum(grad_heads.reshape(16, 8, 8, 256).astype(f32), axis=1).transpose(1, 0, 2)
     kv_sum = lambda start: jnp.sum(
         grad_heads[:, :, start : start + HEAD_DIM].reshape(8, KV_HEADS, 2, HEAD_DIM), axis=2
@@ -886,9 +891,9 @@
         grad_input[None],
         grad_norm_attn,
         grad_qkv,
-        shared_grads[:, :WIDTH],
-        shared_grads[:, WIDTH : WIDTH + EXPERTS],
-        shared_grads[:, WIDTH + EXPERTS],
+        shared_grads[:8],
+        shared_grads[8:, :EXPERTS],
+        shared_grads[8:, EXPERTS],
         expert_grads[:, :128],
         expert_grads[:, 128:],
     )

time: 482 us -> 470 us (0.975)
  starting transfers between devices: 118 us -> 96 us
  waiting for transfers between devices: 96.9 us -> 108 us
    all_to_all x1, starting transfers between devices: 17.4 us -> 5.78 us  [local(): lax.all_to_all(grad_head.reshape(128, 8, 256), BOTH, 0, 0, tiled=True)]
    ppermute x37, waiting for transfers between devices: 62.1 us -> 71.4 us  [send(): return lax.ppermute(rows, 'seq', shift_perm(a, b))]
    all_to_all x1, waiting for transfers between devices: 0.01 us -> 9.01 us  [local(): shared_grads = lax.all_to_all(shared_grads, 'wshard', 0, 0, tiled=True)]
    ppermute x37, starting transfers between devices: 61.3 us -> 55.2 us  [send(): return lax.ppermute(rows, 'seq', shift_perm(a, b))]
    ppermute x2, waiting for transfers between devices: 11.8 us -> 5.95 us  [swap_x(): return lax.ppermute(rows, 'wshard', [(w, w ^ 1) for w in range(8)])]
    all_to_all x1 -> x0, starting transfers between devices: 5.37 us -> none  [local(): shared_grads = lax.all_to_all(shared_grads, 'seq', 0, 0, tiled=True)]
  transfers between devices with their start and end apart: 60 -> 59, of which waited for: 15 -> 17; matrix products, arithmetic and copies ran while one was open for 15% -> 14% of each run, Pallas kernels for 34% -> 35%
where the time goes in v14:
time: 470 us; the launch traced here: 461 us
  Pallas kernels  163 us (35%)
  waiting for transfers between devices  108 us (23%)
  starting transfers between devices  96 us (20%)
  other arithmetic  56.3 us (12%)
  local copies, waits for them, and re-layouts  22.5 us (5%)
  between operations  14.9 us (3%)
    ppermute x37, waiting for transfers between devices, send(): return lax.ppermute(rows, 'seq', shift_perm(a, b))  71.4 us
    ppermute x37, starting transfers between devices, send(): return lax.ppermute(rows, 'seq', shift_perm(a, b))  55.2 us
    pallas_call x2, Pallas kernels, run_experts(): pl.pallas_call(experts_kernel, grid_spec=pltpu.PrefetchScalarGridSpec(num...  44 us
    pallas_call x1, Pallas kernels, attend_back(): pl.pallas_call(attend_back_kernel, grid=(GROUP // BLOCK,), in_specs=[whol...  31.1 us
    convert_element_type x7, other arithmetic, add_low(): return sum([t.astype(f32) for t in terms]).astype(bf16)  20.8 us
    pallas_call x1, Pallas kernels, attend(): pl.pallas_call(attend_kernel, grid=(GROUP // BLOCK,), in_specs=[whole(GRO...  19.8 us
    pallas_call x2, Pallas kernels, project(): pl.pallas_call(project_kernel, grid_spec=pltpu.PrefetchScalarGridSpec(num...  16.7 us
    pallas_call x1, Pallas kernels, expert_weight_grads(): pl.pallas_call(expert_grads_kernel, grid=(2, 4), in_specs=[pl.BlockSpec((...  15.9 us
  transfers between devices with their start and end apart: 59, of which 17 were waited for; matrix products, arithmetic and copies ran while one was open for 14% of the time, Pallas kernels for 35%

profile of v14, /device:TPU:0, one launch (start us, length us, event | category | flops | bytes accessed | tf_op | source)
XLA Modules:
  0.0 461.1 jit_solution(2161436952380721907)
XLA Ops:
  19.8 6.8 %all-to-all-start = ((bf16[128,8,256]{2,1,0:T(8,128)(2,1)}), bf16[128,8,256]{2,1,0:T(8,128)(2,1)S(1)}, u32[]{:S(2)}, u32[]{:S(2)}) async-start(bf16[128,8,256]{2,1,0:T(8,128)(2,1)} %bitcast.9), calls=%async_computation | async-start | bytes 1048576 | tf_op jit(solution)/shard_map/all_to_all | solution.py:771
  28.7 7.7 %subtract_cosine_fusion.table = f32[3584,128]{1,0:T(8,128)} fusion(f32[128]{0:T(128)S(1)} %get-tuple-element.273, f32[128]{0:T(128)S(1)} %get-tuple-element.274, f32[3584]{0:T(1024)S(1)} %get-tuple-element.268), kind=kLoop, calls=%fused_computation.10 | loop fusion | flops 917504 | bytes 1850368 | tf_op jit(solution)/shard_map/cos | solution.py:138
  36.4 5.1 %all-to-all-done = bf16[128,8,256]{2,1,0:T(8,128)(2,1)S(1)} async-done(((bf16[128,8,256]{2,1,0:T(8,128)(2,1)}), bf16[128,8,256]{2,1,0:T(8,128)(2,1)S(1)}, u32[]{:S(2)}, u32[]{:S(2)}) %all-to-all-start) | async-done | bytes 524320 | tf_op jit(solution)/shard_map/all_to_all | solution.py:771
  51.6 8.0 %shard_map.178.refs_0_ = bf16[3584,256]{1,0:T(8,128)(2,1)} custom-call(s32[8]{0:T(128)} %get-tuple-element.271.places, bf16[4,224,1024]{2,1,0:T(8,128)(2,1)} %copy-done.1, bf16[4,224,1024]{2,1,0:T(8,128)(2,1)} %collective-permute-done.7.other.near_other, bf16[1024,256]{1,0:T(8,128)(2,1)} %broadcast_select_fusion.w, f32[1,1024]{1,0:T(1,128)} %bitcast.187, ...), custom_call_target="tpu_custom_call" | custom-call | flops 939524096 | bytes 10485760 | tf_op jit(solution)/shard_map/pallas_call | solution.py:175
  59.6 5.9 %collective-permute-done.8 = bf16[2,192,1024]{2,1,0:T(8,128)(2,1)} collective-permute-done((bf16[2,192,1024]{2,1,0:T(8,128)(2,1)}, bf16[2,192,1024]{2,1,0:T(8,128)(2,1)}, u32[]{:S(2)}, u32[]{:S(2)}) %collective-permute-start.8) | collective-permute-done | bytes 786464 | tf_op jit(solution)/shard_map/ppermute | solution.py:100
  65.5 3.8 collective-permute-done.2
  74.3 9.0 %all-to-all-start.1 = ((bf16[128,8,1152]{2,1,0:T(8,128)(2,1)}), bf16[128,8,1152]{2,1,0:T(8,128)(2,1)S(1)}, u32[]{:S(2)}, u32[]{:S(2)}) async-start(bf16[128,8,1152]{2,1,0:T(8,128)(2,1)} %broadcast_in_dim.101), calls=%async_computation.1 | async-start | bytes 4718592 | tf_op jit(solution)/shard_map/all_to_all | solution.py:789
  89.7 8.7 %shard_map.179.qkv_ref = bf16[3584,256]{1,0:T(8,128)(2,1)} custom-call(s32[8]{0:T(128)} %get-tuple-element.272.places, bf16[4,224,1024]{2,1,0:T(8,128)(2,1)} %pad_maximum_fusion.2.mine.far_mine, bf16[4,224,1024]{2,1,0:T(8,128)(2,1)} %collective-permute-done.9.other.far_other, bf16[1024,256]{1,0:T(8,128)(2,1)} %broadcast_select_fusion.w, ...), custom_call_target="tpu_custom_call" | custom-call | flops 939524096 | bytes 10485760 | tf_op jit(solution)/shard_map/pallas_call | solution.py:175
  98.5 19.8 %shard_map.180 = (bf16[16,64,224]{2,1,0:T(8,128)(2,1)}, f32[64,3584]{1,0:T(8,128)}, f32[1,3584]{1,0:T(1,128)}) custom-call(bf16[3584,256]{1,0:T(8,128)(2,1)} %shard_map.179.qkv_ref, s32[1,3584]{1,0:T(1,128)} %compare_select_fusion.begin_ref), custom_call_target="tpu_custom_call" | custom-call | flops 7247757312 | bytes 4194304 | tf_op jit(solution)/shard_map/pallas_call | solution.py:335
  118.3 5.3 %all-to-all-start.2 = ((bf16[16,64,224]{2,1,0:T(8,128)(2,1)}), bf16[16,64,224]{2,1,0:T(8,128)(2,1)S(1)}, u32[]{:S(2)}, u32[]{:S(2)}) async-start(bf16[16,64,224]{2,1,0:T(8,128)(2,1)} %get-tuple-element.139), calls=%async_computation.2 | async-start | bytes 1048576 | tf_op jit(solution)/shard_map/all_to_all | solution.py:804
  123.6 12.8 %collective-permute-done.12 = bf16[240,1024]{1,0:T(8,128)(2,1)} collective-permute-done((bf16[240,1024]{1,0:T(8,128)(2,1)S(1)}, bf16[240,1024]{1,0:T(8,128)(2,1)}, u32[]{:S(2)}, u32[]{:S(2)}) %collective-permute-start.12) | collective-permute-done | bytes 491552 | tf_op jit(solution)/shard_map/ppermute | solution.py:53
  144.6 3.6 shard_map.181
  154.0 22.4 %collective-permute-done.13 = bf16[224,1024]{1,0:T(8,128)(2,1)S(1)} collective-permute-done((bf16[224,1024]{1,0:T(8,128)(2,1)}, bf16[224,1024]{1,0:T(8,128)(2,1)S(1)}, u32[]{:S(2)}, u32[]{:S(2)}) %collective-permute-start.13) | collective-permute-done | bytes 458784 | tf_op jit(solution)/shard_map/ppermute | solution.py:53
  188.5 21.9 %shard_map.182 = (bf16[4,256,1024]{2,1,0:T(8,128)(2,1)}, bf16[4,256,1024]{2,1,0:T(8,128)(2,1)}, bf16[8,224,1024]{2,1,0:T(8,128)(2,1)}, bf16[8,224,1024]{2,1,0:T(...) custom-call(s32[2]{0:T(128)} %pad_add_fusion.own_ref, ...), custom_call_target="tpu_custom_call" | custom-call | flops 15032385536 | bytes 25165824 | tf_op jit(solution)/shard_map/pallas_call | solution.py:566
  223.8 22.1 %shard_map.183 = (bf16[4,256,1024]{2,1,0:T(8,128)(2,1)}, bf16[4,256,1024]{2,1,0:T(8,128)(2,1)}, bf16[8,224,1024]{2,1,0:T(8,128)(2,1)}, bf16[8,224,1024]{2,1,0:T(...) custom-call(s32[2]{0:T(128)} %pad_add_fusion.own_ref, ...), custom_call_target="tpu_custom_call", output_to_operand_aliasing={{2}: (10, {}), {3}: (11, {}), {4}: (12, {}), {5}: (13, {}),... | custom-call | flops 15032385536 | bytes 25165824 | tf_op jit(solution)/shard_map/pallas_call | solution.py:566
  246.1 4.4 collective-permute-done.30
  257.2 15.9 %shard_map.184 = bf16[4,2,2,192,1024]{4,3,2,1,0:T(8,128)(2,1)} custom-call(bf16[2,1152,1024]{2,1,0:T(8,128)(2,1)} %get-tuple-element.180.x_ref, bf16[2,1152,1024]{2,1,0:T(8,128)(2,1)} %get-tuple-element.181.dh_ref, bf16[2,1152,512]{2,1,0:T(8,128)(2,1)} %get-tuple-element.182.act_ref, bf16[2,1152,1024]{2,1,0:T(8,128)(2,1)} %get-tuple-element.183.dy_ref), custom_call_target="tpu_custom_call" | custom-call | flops 8589934592 | bytes 14680064 | tf_op jit(solution)/shard_map/pallas_call | solution.py:622
  273.1 7.9 %collective-permute-done.32 = bf16[256,1024]{1,0:T(8,128)(2,1)S(1)} collective-permute-done((bf16[256,1024]{1,0:T(8,128)(2,1)S(1)}, bf16[256,1024]{1,0:T(8,128)(2,1)S(1)}, u32[]{:S(2)}, u32[]{:S(2)}) %collective-permute-start.32) | collective-permute-done | bytes 524320 | tf_op jit(solution)/shard_map/ppermute | solution.py:53
  283.2 6.2 %fusion.10 = (bf16[2,224,1024]{2,1,0:T(8,128)(2,1)}, bf16[2,224,1024]{2,1,0:T(8,128)(2,1)}, bf16[2,224,1024]{2,1,0:T(8,128)(2,1)}, bf16[2,224,1024]{2,1,0:T(8,128)(2,1)S(1)}) fusion(bf16[2,4,224,1024]{3,2,1,0:T(8,128)(2,1)} %bitcast.49, bf16[2,4,224,1024]{3,2,1,0:T(8,128)(2,1)} %bitcast.170), kind=kLoop, calls=%fused_computation.47 | loop fusion | flops 7340032 | bytes 11010048 | tf_op jit(solution)/shard_map/convert_element_type | solution.py:84
  289.4 6.3 %collective-permute-done.35.crossed = bf16[256,1024]{1,0:T(8,128)(2,1)S(1)} collective-permute-done((bf16[256,1024]{1,0:T(8,128)(2,1)S(1)}, bf16[256,1024]{1,0:T(8,128)(2,1)S(1)}, u32[]{:S(2)}, u32[]{:S(2)}) %collective-permute-start.35) | collective-permute-done | bytes 524320 | tf_op jit(solution)/shard_map/ppermute | solution.py:53
  296.4 5.8 %shard_map.185 = (f32[224,1024]{1,0:T(8,128)}, bf16[224,1024]{1,0:T(8,128)(2,1)}, bf16[32,224]{1,0:T(8,128)(2,1)}, bf16[224,1024]{1,0:T(8,128)(2,1)}, bf16[16,64,224]{2,1,0:T(8,128)(2,1)}) custom-call(bf16[256,1024]{1,0:T(8,128)(2,1)} %get-tuple-element.172.t0, bf16[256,1024]{1,0:T(8,128)(2,1)} %copy-done.16, bf16[256,1024]{1,0:T(8,128)(2,1)} %copy-done.17, ...), custom_call_target="tpu_custom_call" | custom-call | flops 469762048 | bytes 8388608 | tf_op jit(solution)/shard_map/pallas_call | solution.py:693
  302.3 3.8 all-to-all-start.3
  306.1 3.9 shard_map.186
  310.0 8.4 %all-to-all-done.3.g_ref = bf16[16,64,224]{2,1,0:T(8,128)(2,1)S(1)} async-done(((bf16[16,64,224]{2,1,0:T(8,128)(2,1)}), bf16[16,64,224]{2,1,0:T(8,128)(2,1)S(1)}, u32[]{:S(2)}, u32[]{:S(2)}) %all-to-all-start.3) | async-done | bytes 458784 | tf_op jit(solution)/shard_map/all_to_all | solution.py:846
  319.3 5.1 %all-to-all-start.4 = ((bf16[8,128,1152]{2,1,0:T(8,128)(2,1)}), bf16[8,128,1152]{2,1,0:T(8,128)(2,1)S(1)}, u32[]{:S(2)}, u32[]{:S(2)}) async-start(bf16[8,128,1152]{2,1,0:T(8,128)(2,1)} %shard_map.186), calls=%async_computation.4 | async-start | bytes 4718592 | tf_op jit(solution)/shard_map/all_to_all | solution.py:853
  326.9 31.1 %shard_map.187.first.second = bf16[3584,256]{1,0:T(8,128)(2,1)} custom-call(bf16[3584,256]{1,0:T(8,128)(2,1)} %shard_map.179.qkv_ref, bf16[16,64,224]{2,1,0:T(8,128)(2,1)} %copy-done.21, f32[64,3584]{1,0:T(8,128)} %get-tuple-element.201.ot_ref, f32[1,3584]{1,0:T(1,128)} %get-tuple-element.202.lse_ref, s32[1,3584]{1,0:T(1,128)} %compare_select_fusion.begin_ref, ...), custom_call_target="tpu_custom_call" | custom-call | flops 18119393280 | bytes 8388608 | tf_op jit(solution)/shard_map/pallas_call | solution.py:415
  358.0 9.0 %all-to-all-done.4 = bf16[8,128,1152]{2,1,0:T(8,128)(2,1)S(1)} async-done(((bf16[8,128,1152]{2,1,0:T(8,128)(2,1)}), bf16[8,128,1152]{2,1,0:T(8,128)(2,1)S(1)}, u32[]{:S(2)}, u32[]{:S(2)}) %all-to-all-start.4) | async-done | bytes 2359328 | tf_op jit(solution)/shard_map/all_to_all | solution.py:853
  368.1 5.7 %shard_map.188 = (bf16[4,240,1024]{2,1,0:T(8,128)(2,1)}, bf16[4,240,1024]{2,1,0:T(8,128)(2,1)}) custom-call(s32[8]{0:T(128)} %get-tuple-element.272.places, bf16[3584,256]{1,0:T(8,128)(2,1)} %shard_map.187.first.second, bf16[3584,256]{1,0:T(8,128)(2,1)} %shard_map.187.first.second, bf16[1024,256]{1,0:T(8,128)(2,1)} %broadcast_select_fusion.w, ...), custom_call_target="tpu_custom_call" | custom-call | flops 939524096 | bytes 5242880 | tf_op jit(solution)/shard_map/pallas_call | solution.py:206
  374.1 5.9 %shard_map.189 = (bf16[4,240,1024]{2,1,0:T(8,128)(2,1)}, bf16[4,240,1024]{2,1,0:T(8,128)(2,1)}) custom-call(s32[8]{0:T(128)} %get-tuple-element.271.places, bf16[3584,256]{1,0:T(8,128)(2,1)} %shard_map.187.first.second, bf16[3584,256]{1,0:T(8,128)(2,1)} %shard_map.187.first.second, bf16[1024,256]{1,0:T(8,128)(2,1)} %broadcast_select_fusion.w, ...), custom_call_target="tpu_custom_call" | custom-call | flops 939524096 | bytes 5242880 | tf_op jit(solution)/shard_map/pallas_call | solution.py:206
  397.4 10.8 %shard_map.190 = bf16[1024,256]{1,0:T(8,128)(2,1)} custom-call(s32[16]{0:T(128)} %copy-done.37, bf16[4,224,1024]{2,1,0:T(8,128)(2,1)} %copy-done.1, bf16[4,224,1024]{2,1,0:T(8,128)(2,1)} %collective-permute-done.7.other.near_other, bf16[4,224,1024]{2,1,0:T(8,128)(2,1)} %pad_maximum_fusion.2.mine.far_mine, ...), custom_call_target="tpu_custom_call" | custom-call | flops 1879048192 | bytes 10485760 | tf_op jit(solution)/shard_map/pallas_call | solution.py:250
  408.1 5.8 %all-to-all-start.5 = ((bf16[128,8,256]{2,1,0:T(8,128)(2,1)}), bf16[128,8,256]{2,1,0:T(8,128)(2,1)S(1)}, u32[]{:S(2)}, u32[]{:S(2)}) async-start(bf16[128,8,256]{2,1,0:T(8,128)(2,1)} %bitcast.172), calls=%async_computation.6 | async-start | bytes 1048576 | tf_op jit(solution)/shard_map/all_to_all | solution.py:868
  430.9 12.0 %collective-permute-done.46 = bf16[240,1024]{1,0:T(8,128)(2,1)S(1)} collective-permute-done((bf16[240,1024]{1,0:T(8,128)(2,1)}, bf16[240,1024]{1,0:T(8,128)(2,1)S(1)}, u32[]{:S(2)}, u32[]{:S(2)}) %collective-permute-start.46) | collective-permute-done | bytes 491552 | tf_op jit(solution)/shard_map/ppermute | solution.py:53
  (274 shorter events, 135.5 us)
Async XLA Ops:
  7.2 35.1 %collective-permute-start = (bf16[224,1024]{1,0:T(8,128)(2,1)}, bf16[224,1024]{1,0:T(8,128)(2,1)S(1)}, u32[]{:S(2)}, u32[]{:S(2)}) collective-permute-start(bf16[224,1024]{1,0:T(8,128)(2,1)} %bitcast.161), channel_id=1, source_target_pairs={{0,64},{8,72},{16,80},{24,88},{32,96},{40,104},{48,112},{56,120},{... | collective-permute-start | bytes 1376264 | tf_op jit(solution)/shard_map/ppermute | solution.py:53
  10.4 32.0 %collective-permute-start.4 = (bf16[224,1024]{1,0:T(8,128)(2,1)}, bf16[224,1024]{1,0:T(8,128)(2,1)S(1)}, u32[]{:S(2)}, u32[]{:S(2)}) collective-permute-start(bf16[224,1024]{1,0:T(8,128)(2,1)} %bitcast.162), channel_id=1, source_target_pairs={{0,16},{8,24},{16,32},{24,40},{32,48},{40,56},{48,0},{56,8},{64,80... | collective-permute-start | bytes 1376264 | tf_op jit(solution)/shard_map/ppermute | solution.py:53
  12.3 30.1 %collective-permute-start.5 = (bf16[224,1024]{1,0:T(8,128)(2,1)}, bf16[224,1024]{1,0:T(8,128)(2,1)S(1)}, u32[]{:S(2)}, u32[]{:S(2)}) collective-permute-start(bf16[224,1024]{1,0:T(8,128)(2,1)} %bitcast.163), channel_id=1, source_target_pairs={{0,48},{8,56},{16,0},{24,8},{32,16},{40,24},{48,32},{56,40},{64,11... | collective-permute-start | bytes 1376264 | tf_op jit(solution)/shard_map/ppermute | solution.py:53
  14.4 28.0 %collective-permute-start.6 = (bf16[224,1024]{1,0:T(8,128)(2,1)}, bf16[224,1024]{1,0:T(8,128)(2,1)S(1)}, u32[]{:S(2)}, u32[]{:S(2)}) collective-permute-start(bf16[224,1024]{1,0:T(8,128)(2,1)} %bitcast.164), channel_id=1, source_target_pairs={{0,32},{8,40},{16,48},{24,56},{32,0},{40,8},{48,16},{56,24},{64,96... | collective-permute-start | bytes 1376264 | tf_op jit(solution)/shard_map/ppermute | solution.py:53
  26.6 161.9 %all-gather.5.cloned.1.call-start = ((), (), s32[]{:S(2)}) async-start(), calls=%async_computation.8 | async-start | bytes 3932160 | tf_op jit(solution)/shard_map/all_gather | solution.py:781
  74.3 43.9 %all-to-all-start.1 = ((bf16[128,8,1152]{2,1,0:T(8,128)(2,1)}), bf16[128,8,1152]{2,1,0:T(8,128)(2,1)S(1)}, u32[]{:S(2)}, u32[]{:S(2)}) async-start(bf16[128,8,1152]{2,1,0:T(8,128)(2,1)} %broadcast_in_dim.101), calls=%async_computation.1 | async-start | bytes 4718592 | tf_op jit(solution)/shard_map/all_to_all | solution.py:789
  83.3 105.2 %all-gather.7.cloned.1.call-start = ((), (), s32[]{:S(2)}) async-start(), calls=%async_computation.9 | async-start | bytes 3932160 | tf_op jit(solution)/shard_map/all_gather | solution.py:781
  84.7 39.0 %collective-permute-start.10 = (bf16[240,1024]{1,0:T(8,128)(2,1)S(1)}, bf16[240,1024]{1,0:T(8,128)(2,1)}, u32[]{:S(2)}, u32[]{:S(2)}) collective-permute-start(bf16[240,1024]{1,0:T(8,128)(2,1)S(1)} %fusion.21), channel_id=1, source_target_pairs={{0,16},{8,24},{16,32},{24,40},{32,48},{40,56},{48,0},{56,8},{64,80... | collective-permute-start | bytes 1474568 | tf_op jit(solution)/shard_map/ppermute | solution.py:53
  85.7 37.9 %collective-permute-start.11 = (bf16[240,1024]{1,0:T(8,128)(2,1)S(1)}, bf16[240,1024]{1,0:T(8,128)(2,1)}, u32[]{:S(2)}, u32[]{:S(2)}) collective-permute-start(bf16[240,1024]{1,0:T(8,128)(2,1)S(1)} %fusion.21), channel_id=1, source_target_pairs={{0,48},{8,56},{16,0},{24,8},{32,16},{40,24},{48,32},{56,40},{64,11... | collective-permute-start | bytes 1474568 | tf_op jit(solution)/shard_map/ppermute | solution.py:53
  87.9 48.5 %collective-permute-start.12 = (bf16[240,1024]{1,0:T(8,128)(2,1)S(1)}, bf16[240,1024]{1,0:T(8,128)(2,1)}, u32[]{:S(2)}, u32[]{:S(2)}) collective-permute-start(bf16[240,1024]{1,0:T(8,128)(2,1)S(1)} %fusion.21), channel_id=1, source_target_pairs={{0,32},{8,40},{16,48},{24,56},{32,0},{40,8},{48,16},{56,24},{64,96... | collective-permute-start | bytes 1474568 | tf_op jit(solution)/shard_map/ppermute | solution.py:53
  123.6 256.4 %reduce-scatter.2.cloned.1.call-start = ((), (), s32[]{:S(2)}) async-start(), calls=%async_computation.7 | async-start | bytes 7864320 | tf_op jit(solution)/shard_map/reduce_scatter | solution.py:839
  141.1 35.3 %collective-permute-start.21 = (bf16[2,240,1024]{2,1,0:T(8,128)(2,1)}, bf16[2,240,1024]{2,1,0:T(8,128)(2,1)}, u32[]{:S(2)}, u32[]{:S(2)}) collective-permute-start(bf16[2,240,1024]{2,1,0:T(8,128)(2,1)} %pad_maximum_fusion.5), channel_id=1, source_target_pairs={{0,64},{8,72},{16,80},{24,88},{32,96},{40,104},{48,112},{56,120},{... | collective-permute-start | bytes 2949128 | tf_op jit(solution)/shard_map/ppermute | solution.py:53
  148.2 28.2 %collective-permute-start.13 = (bf16[224,1024]{1,0:T(8,128)(2,1)}, bf16[224,1024]{1,0:T(8,128)(2,1)S(1)}, u32[]{:S(2)}, u32[]{:S(2)}) collective-permute-start(bf16[224,1024]{1,0:T(8,128)(2,1)} %get-tuple-element.152.normed_ref), channel_id=1, source_target_pairs={{0,64},{8,72},{16,80},{24,88},{32,96},{40,104},{48,112},{56,120},{... | collective-permute-start | bytes 1376264 | tf_op jit(solution)/shard_map/ppermute | solution.py:53
  149.1 27.3 %collective-permute-start.18 = (bf16[224,1024]{1,0:T(8,128)(2,1)}, bf16[224,1024]{1,0:T(8,128)(2,1)S(1)}, u32[]{:S(2)}, u32[]{:S(2)}) collective-permute-start(bf16[224,1024]{1,0:T(8,128)(2,1)} %get-tuple-element.152.normed_ref), channel_id=1, source_target_pairs={{0,16},{8,24},{16,32},{24,40},{32,48},{40,56},{48,0},{56,8},{64,80... | collective-permute-start | bytes 1376264 | tf_op jit(solution)/shard_map/ppermute | solution.py:53
  181.8 30.0 %collective-permute-start.22 = (bf16[2,240,1024]{2,1,0:T(8,128)(2,1)}, bf16[2,240,1024]{2,1,0:T(8,128)(2,1)S(1)}, u32[]{:S(2)}, u32[]{:S(2)}) collective-permute-start(bf16[2,240,1024]{2,1,0:T(8,128)(2,1)} %slice.213), channel_id=1, source_target_pairs={{0,64},{8,72},{16,80},{24,88},{32,96},{40,104},{48,112},{56,120},{... | collective-permute-start | bytes 2949128 | tf_op jit(solution)/shard_map/ppermute | solution.py:53
  184.5 27.9 %collective-permute-start.14 = (bf16[224,1024]{1,0:T(8,128)(2,1)S(1)}, bf16[224,1024]{1,0:T(8,128)(2,1)}, u32[]{:S(2)}, u32[]{:S(2)}) collective-permute-start(bf16[224,1024]{1,0:T(8,128)(2,1)S(1)} %collective-permute-done.13), channel_id=1, source_target_pairs={{0,16},{8,24},{16,32},{24,40},{32,48},{40,56},{48,0},{56,8},{64,80... | collective-permute-start | bytes 1376264 | tf_op jit(solution)/shard_map/ppermute | solution.py:53
  216.7 29.2 %collective-permute-start.27 = (bf16[256,1024]{1,0:T(8,128)(2,1)}, bf16[256,1024]{1,0:T(8,128)(2,1)S(1)}, u32[]{:S(2)}, u32[]{:S(2)}) collective-permute-start(bf16[256,1024]{1,0:T(8,128)(2,1)} %get-tuple-element.255), channel_id=1, source_target_pairs={{0,48},{8,56},{16,0},{24,8},{32,16},{40,24},{48,32},{56,40},{64,11... | collective-permute-start | bytes 1572872 | tf_op jit(solution)/shard_map/ppermute | solution.py:53
  218.7 27.3 %collective-permute-start.28 = (bf16[256,1024]{1,0:T(8,128)(2,1)}, bf16[256,1024]{1,0:T(8,128)(2,1)S(1)}, u32[]{:S(2)}, u32[]{:S(2)}) collective-permute-start(bf16[256,1024]{1,0:T(8,128)(2,1)} %get-tuple-element.254), channel_id=1, source_target_pairs={{0,16},{8,24},{16,32},{24,40},{32,48},{40,56},{48,0},{56,8},{64,80... | collective-permute-start | bytes 1572872 | tf_op jit(solution)/shard_map/ppermute | solution.py:53
  218.7 27.2 %collective-permute-start.29 = (bf16[256,1024]{1,0:T(8,128)(2,1)S(1)}, bf16[256,1024]{1,0:T(8,128)(2,1)S(1)}, u32[]{:S(2)}, u32[]{:S(2)}) collective-permute-start(bf16[256,1024]{1,0:T(8,128)(2,1)S(1)} %get-tuple-element.253), channel_id=1, source_target_pairs={{0,32},{8,40},{16,48},{24,56},{32,0},{40,8},{48,16},{56,24},{64,96... | collective-permute-start | bytes 1572872 | tf_op jit(solution)/shard_map/ppermute | solution.py:53
  250.4 30.5 %collective-permute-start.34 = (bf16[8,224,1024]{2,1,0:T(8,128)(2,1)}, bf16[8,224,1024]{2,1,0:T(8,128)(2,1)}, u32[]{:S(2)}, u32[]{:S(2)}) collective-permute-start(bf16[8,224,1024]{2,1,0:T(8,128)(2,1)} %get-tuple-element.184), channel_id=1, source_target_pairs={{0,8},{8,0},{16,24},{24,16},{32,40},{40,32},{48,56},{56,48},{64,72... | collective-permute-start | bytes 11010056 | tf_op jit(solution)/shard_map/ppermute | solution.py:57
  319.3 47.7 %all-to-all-start.4 = ((bf16[8,128,1152]{2,1,0:T(8,128)(2,1)}), bf16[8,128,1152]{2,1,0:T(8,128)(2,1)S(1)}, u32[]{:S(2)}, u32[]{:S(2)}) async-start(bf16[8,128,1152]{2,1,0:T(8,128)(2,1)} %shard_map.186), calls=%async_computation.4 | async-start | bytes 4718592 | tf_op jit(solution)/shard_map/all_to_all | solution.py:853
  324.4 55.6 %collective-permute-start.37 = (bf16[2,224,1024]{2,1,0:T(8,128)(2,1)}, bf16[2,224,1024]{2,1,0:T(8,128)(2,1)}, u32[]{:S(2)}, u32[]{:S(2)}) collective-permute-start(bf16[2,224,1024]{2,1,0:T(8,128)(2,1)} %get-tuple-element.209), channel_id=1, source_target_pairs={{0,48},{8,56},{16,0},{24,8},{32,16},{40,24},{48,32},{56,40},{64,11... | collective-permute-start | bytes 2752520 | tf_op jit(solution)/shard_map/ppermute | solution.py:53
  325.4 54.6 %collective-permute-start.38 = (bf16[2,224,1024]{2,1,0:T(8,128)(2,1)}, bf16[2,224,1024]{2,1,0:T(8,128)(2,1)}, u32[]{:S(2)}, u32[]{:S(2)}) collective-permute-start(bf16[2,224,1024]{2,1,0:T(8,128)(2,1)} %get-tuple-element.210), channel_id=1, source_target_pairs={{0,16},{8,24},{16,32},{24,40},{32,48},{40,56},{48,0},{56,8},{64,80... | collective-permute-start | bytes 2752520 | tf_op jit(solution)/shard_map/ppermute | solution.py:53
  326.4 53.6 %collective-permute-start.39 = (bf16[2,224,1024]{2,1,0:T(8,128)(2,1)}, bf16[2,224,1024]{2,1,0:T(8,128)(2,1)}, u32[]{:S(2)}, u32[]{:S(2)}) collective-permute-start(bf16[2,224,1024]{2,1,0:T(8,128)(2,1)} %get-tuple-element.211), channel_id=1, source_target_pairs={{0,32},{8,40},{16,48},{24,56},{32,0},{40,8},{48,16},{56,24},{64,96... | collective-permute-start | bytes 2752520 | tf_op jit(solution)/shard_map/ppermute | solution.py:53
  389.0 27.8 %collective-permute-start.43 = (bf16[240,1024]{1,0:T(8,128)(2,1)}, bf16[240,1024]{1,0:T(8,128)(2,1)}, u32[]{:S(2)}, u32[]{:S(2)}) collective-permute-start(bf16[240,1024]{1,0:T(8,128)(2,1)} %get-tuple-element.227), channel_id=1, source_target_pairs={{0,16},{8,24},{16,32},{24,40},{32,48},{40,56},{48,0},{56,8},{64,80... | collective-permute-start | bytes 1474568 | tf_op jit(solution)/shard_map/ppermute | solution.py:53
  389.7 27.2 %collective-permute-start.44 = (bf16[240,1024]{1,0:T(8,128)(2,1)}, bf16[240,1024]{1,0:T(8,128)(2,1)}, u32[]{:S(2)}, u32[]{:S(2)}) collective-permute-start(bf16[240,1024]{1,0:T(8,128)(2,1)} %get-tuple-element.228), channel_id=1, source_target_pairs={{0,32},{8,40},{16,48},{24,56},{32,0},{40,8},{48,16},{56,24},{64,96... | collective-permute-start | bytes 1474568 | tf_op jit(solution)/shard_map/ppermute | solution.py:53
  391.4 36.2 %collective-permute-start.49 = (bf16[2,192,1024]{2,1,0:T(8,128)(2,1)}, bf16[2,192,1024]{2,1,0:T(8,128)(2,1)}, u32[]{:S(2)}, u32[]{:S(2)}) collective-permute-start(bf16[2,192,1024]{2,1,0:T(8,128)(2,1)} %dynamic-slice_bitcast_fusion), channel_id=1, source_target_pairs={{0,1},{1,0},{2,3},{3,2},{4,5},{5,4},{6,7},{7,6},{8,9},{9,8},{10,11... | collective-permute-start | bytes 2359304 | tf_op jit(solution)/shard_map/ppermute | solution.py:100
  395.2 28.4 %collective-permute-start.41 = (bf16[224,1024]{1,0:T(8,128)(2,1)}, bf16[224,1024]{1,0:T(8,128)(2,1)}, u32[]{:S(2)}, u32[]{:S(2)}) collective-permute-start(bf16[224,1024]{1,0:T(8,128)(2,1)} %fusion.30), channel_id=1, source_target_pairs={{0,64},{8,72},{16,80},{24,88},{32,96},{40,104},{48,112},{56,120},{... | collective-permute-start | bytes 1376264 | tf_op jit(solution)/shard_map/ppermute | solution.py:53
  408.1 38.8 %all-to-all-start.5 = ((bf16[128,8,256]{2,1,0:T(8,128)(2,1)}), bf16[128,8,256]{2,1,0:T(8,128)(2,1)S(1)}, u32[]{:S(2)}, u32[]{:S(2)}) async-start(bf16[128,8,256]{2,1,0:T(8,128)(2,1)} %bitcast.172), calls=%async_computation.6 | async-start | bytes 1048576 | tf_op jit(solution)/shard_map/all_to_all | solution.py:868
  413.9 29.0 %collective-permute-start.46 = (bf16[240,1024]{1,0:T(8,128)(2,1)}, bf16[240,1024]{1,0:T(8,128)(2,1)S(1)}, u32[]{:S(2)}, u32[]{:S(2)}) collective-permute-start(bf16[240,1024]{1,0:T(8,128)(2,1)} %get-tuple-element.230), channel_id=1, source_target_pairs={{0,48},{8,56},{16,0},{24,8},{32,16},{40,24},{48,32},{56,40},{64,11... | collective-permute-start | bytes 1474568 | tf_op jit(solution)/shard_map/ppermute | solution.py:53
  416.8 29.3 %collective-permute-start.47 = (bf16[240,1024]{1,0:T(8,128)(2,1)}, bf16[240,1024]{1,0:T(8,128)(2,1)S(1)}, u32[]{:S(2)}, u32[]{:S(2)}) collective-permute-start(bf16[240,1024]{1,0:T(8,128)(2,1)} %get-tuple-element.231), channel_id=1, source_target_pairs={{0,16},{8,24},{16,32},{24,40},{32,48},{40,56},{48,0},{56,8},{64,80... | collective-permute-start | bytes 1474568 | tf_op jit(solution)/shard_map/ppermute | solution.py:53
  416.8 30.1 %collective-permute-start.48 = (bf16[240,1024]{1,0:T(8,128)(2,1)}, bf16[240,1024]{1,0:T(8,128)(2,1)}, u32[]{:S(2)}, u32[]{:S(2)}) collective-permute-start(bf16[240,1024]{1,0:T(8,128)(2,1)} %get-tuple-element.232), channel_id=1, source_target_pairs={{0,32},{8,40},{16,48},{24,56},{32,0},{40,8},{48,16},{56,24},{64,96... | collective-permute-start | bytes 1474568 | tf_op jit(solution)/shard_map/ppermute | solution.py:53
  (71 other events, 766.0 us)
Sparse Core Ops, SparseCore 0:
  29.1 40.6 all-gather.4
  85.8 50.9 all-gather.6
  281.1 87.1 reduce-scatter.1

commit v15 on v14

--- a/solution.py
+++ b/solution.py
@@ -441,10 +441,30 @@
     )(qkv, g, ot, lse, begin, table)
 
 
+def up_to():
+    return (
+        lax.broadcasted_iota(i32, (TOK, TOK), 0) <= lax.broadcasted_iota(i32, (TOK, TOK), 1)
+    ).astype(f32).astype(bf16)
+
+
+def slots_of(routes, own, upto):
+    named = [jnp.max((routes == own + e).astype(f32), axis=0, keepdims=True) for e in range(2)]
+    named = jnp.concatenate(named + [jnp.zeros((6, TOK), f32)], axis=0)
+    rank = jnp.dot(named.astype(bf16), upto, preferred_element_type=f32)
+    return jnp.where(named > 0, rank - 1.0, -1.0)
+
+
+def back_to_tokens(slot_cols):
+    columns = lax.broadcasted_iota(i32, (TOK, 2 * SLOTS), 1).astype(f32)
+    first, second = slot_cols[:, 0:1], slot_cols[:, 1:2]
+    back = (columns == first) | ((columns == second + SLOTS) & (second >= 0))
+    return back.astype(f32).astype(bf16)
+
+
 def experts_kernel(
     own_ref, ffn_mine, ffn_other, g_mine, g_other, routes_mine, routes_other, router_ref, own_w, across_w, *refs
 ):
-    routed_mine, routed_other, moved_mine, moved_other = refs[-10:-6]
+    routed_mine, routed_other, z_ref = refs[-9:-6]
     x_ref, dh_ref, act_ref, dy_ref, w_ref, sem = refs[-6:]
     own = own_ref[0]
 
@@ -464,9 +484,7 @@
 
     expert_rows = lax.broadcasted_iota(i32, (EXPERTS, TOK), 0)
     slot_rows = lax.broadcasted_iota(i32, (SLOTS, TOK), 0).astype(f32)
-    upto = (
-        lax.broadcasted_iota(i32, (TOK, TOK), 0) <= lax.broadcasted_iota(i32, (TOK, TOK), 1)
-    ).astype(f32).astype(bf16)
+    upto = up_to()
     slot_cols = []
     gate_grads = [jnp.zeros((EXPERTS, WIDTH), f32) for _ in range(4)]
     payload_rows = lax.broadcasted_iota(i32, (EXPERTS, WIDTH), 0)
@@ -482,10 +500,7 @@
         chosen = expert_rows == routes[0:1]
         for j in range(1, 8):
             chosen = chosen | (expert_rows == routes[j : j + 1])
-        named = [jnp.max((routes == own + e).astype(f32), axis=0, keepdims=True) for e in range(2)]
-        named = jnp.concatenate(named + [jnp.zeros((6, TOK), f32)], axis=0)
-        rank = jnp.dot(named.astype(bf16), upto, preferred_element_type=f32)
-        slots = jnp.where(named > 0, rank - 1.0, -1.0)
+        slots = slots_of(routes, own, upto)
         slot_cols.append(slots.T)
         logits = lax.dot_general(router_ref[...], rows, NT, preferred_element_type=f32)
         peak = jnp.max(jnp.where(chosen, logits, masked_score), axis=0, keepdims=True)
@@ -542,21 +557,50 @@
             gate_grads[b] = gate_grads[b] + jnp.where(payload_rows == own + e, wide, 0.0)
         moved.append(gate * returned)
         routed.append(lax.dot_general(dh, w_gate_up, NT, preferred_element_type=f32))
-    columns = lax.broadcasted_iota(i32, (TOK, 2 * SLOTS), 1).astype(f32)
-    outs = [(routed_mine, moved_mine, 0), (routed_other, moved_other, 0), (routed_mine, moved_mine, 1), (routed_other, moved_other, 1)]
-    for b, (routed_ref, moved_ref, n) in enumerate(outs):
-        first, second = slot_cols[b][:, 0:1], slot_cols[b][:, 1:2]
-        back = ((columns == first) | ((columns == second + SLOTS) & (second >= 0))).astype(f32).astype(bf16)
+    outs = [(routed_mine, 0), (routed_other, 0), (routed_mine, 1), (routed_other, 1)]
+    for b, (routed_ref, n) in enumerate(outs):
         at = slice(b * SLOTS, (b + 1) * SLOTS)
-        for terms, ref in ((routed, routed_ref), (moved, moved_ref)):
-            joined = jnp.concatenate([terms[0][at], terms[1][at]], axis=0).astype(bf16)
-            ref[n, :TOK, :] = jnp.dot(back, joined, preferred_element_type=f32).astype(bf16)
+        joined = jnp.concatenate([routed[0][at], routed[1][at]], axis=0).astype(bf16)
+        back = back_to_tokens(slot_cols[b])
+        routed_ref[n, :TOK, :] = jnp.dot(back, joined, preferred_element_type=f32).astype(bf16)
         routed_ref[n, TOK:, :] = gate_grads[b].astype(bf16)
+        z_ref[b] = jnp.concatenate([moved[0][at], moved[1][at]], axis=0).astype(bf16)
+
+
+def moved_kernel(own_ref, routes_mine, routes_other, z_ref, moved_mine, moved_other):
+    upto = up_to()
+    outs = [(routes_mine, moved_mine, 0), (routes_other, moved_other, 0)]
+    outs = outs + [(*refs_of[:2], 1) for refs_of in outs]
+    for b, (routes_ref, moved_ref, n) in enumerate(outs):
+        routes = routes_ref[n][:8, :TOK].astype(f32).astype(i32)
+        back = back_to_tokens(slots_of(routes, own_ref[0], upto).T)
+        moved_ref[n] = jnp.dot(back, z_ref[b], preferred_element_type=f32).astype(bf16)
+
+
+def moved_rows(half, own, grads, z):
+    routes = pl.BlockSpec((2, 16, 256), lambda i, o: (i, TOK // 16, 0))
+    pair = pl.BlockSpec((2, TOK, WIDTH), lambda i, o: (i, 0, 0))
+    part = jax.ShapeDtypeStruct((4, TOK, WIDTH), bf16)
+    return pl.pallas_call(
+        moved_kernel,
+        grid_spec=pltpu.PrefetchScalarGridSpec(
+            num_scalar_prefetch=1,
+            grid=(2,),
+            in_specs=[
+                routes,
+                routes,
+                pl.BlockSpec((4, 2 * SLOTS, WIDTH), lambda i, o: (i + 2 * half, 0, 0)),
+            ],
+            out_specs=[pair, pair],
+        ),
+        out_shape=[part, part],
+        compiler_params=pltpu.CompilerParams(vmem_limit_bytes=VMEM_LIMIT),
+        cost_estimate=pl.CostEstimate(flops=1 << 30, bytes_accessed=6 << 20, transcendentals=0),
+    )(own, *grads, z)
 
 
 def run_experts(half, own, ffn, grads, weights, router, before):
     pair = pl.BlockSpec((2, TOK, WIDTH), lambda i, o: (i, 0, 0))
-    pair_of_all = pl.BlockSpec((2, TOK, WIDTH), lambda i, o: (i + 2 * half, 0, 0))
     whole = lambda shape: pl.BlockSpec(shape, lambda i, o: (0,) * len(shape))
     routes = pl.BlockSpec((2, 16, 256), lambda i, o: (i, TOK // 16, 0))
     summed = pl.BlockSpec((2, PAY, WIDTH), lambda i, o: (i, 0, 0))
@@ -581,8 +625,7 @@
             out_specs=[
                 summed,
                 summed,
-                pair_of_all,
-                pair_of_all,
+                pl.BlockSpec((4, 2 * SLOTS, WIDTH), lambda i, o: (i + 2 * half, 0, 0)),
                 kept(WIDTH),
                 kept(2 * FF),
                 kept(FF),
@@ -596,8 +639,7 @@
         out_shape=[
             part,
             part,
-            jax.ShapeDtypeStruct((8, TOK, WIDTH), bf16),
-            jax.ShapeDtypeStruct((8, TOK, WIDTH), bf16),
+            jax.ShapeDtypeStruct((16, 2 * SLOTS, WIDTH), bf16),
             keep(WIDTH),
             keep(2 * FF),
             keep(FF),
@@ -804,12 +846,12 @@
     attended = lax.all_to_all(attended_head, "seq", 0, 0, tiled=True)
     attended, grad_near = tie(attended, grad_near)
     grad_near = jnp.stack(grad_near)
-    grad_far = [send(grad_near[:2], 1, 0)]
+    grad_far = [send(grad_near[:1], 1, 0)]
     hidden, normed_ffn = hidden_of(attended, shared, rows, gain_ffn)
     ffn_near, ffn_across = gather_near(normed_ffn)
     grad_near_mine, _ = tie(grad_near, ffn_across)
     ffn_near, _, grad_far[0] = tie(ffn_near, ffn_across, grad_far[0])
-    grad_far.append(send(grad_near_mine[2:], 1, 0))
+    grad_far.append(send(grad_near_mine[1:], 1, 0))
     grad_near = (grad_near, swap_cores(grad_near))
     ffn_near, ffn_far = both_cores(ffn_near), gather_far(ffn_across)
     own = jnp.stack([seq_index * 2, own_x])
@@ -820,15 +862,21 @@
     grad_far = (grad_far, swap_cores(grad_far))
     far = run_experts(1, own, ffn_far, grad_far, experts, router_t, near[2:])
     far, near_terms = tie(far, near_terms)
-    moved, saved = far[2:4], far[4:]
-    far_other, moved_other = tie(swap_cores(far[1]), moved[1])
+    moved, saved = far[2], far[3:]
+    far_other, moved = tie(swap_cores(far[1]), moved)
     far_terms = send_along_z(chip_parts(far[0], far_other))
     expert_grads = expert_weight_grads(*saved)
-    moved_other = swap_cores(moved_other)
-    far_terms, expert_grads, moved_other = tie(far_terms, expert_grads, moved_other)
+    moved_near = moved_rows(0, own, grad_near, moved)
+    moved_far = moved_rows(1, own, grad_far, moved)
+    far_terms, expert_grads, moved_near, moved_far = tie(
+        far_terms, expert_grads, moved_near, moved_far
+    )
     crossed = send(add_low(*far_terms), 1, 0)
-    by_x = [t.reshape(2, 4, TOK, WIDTH) for t in (moved[0], moved_other)]
-    moved_parts = [add_low(by_x[0][:, i], by_x[1][:, i]) for i in range(4)]
+    near_got, far_got = swap_cores(moved_near[1]), swap_cores(moved_far[1])
+    moved_parts = [
+        jnp.stack([add_low(moved_near[0][i], near_got[i]), add_low(moved_far[0][i], far_got[i])])
+        for i in range(4)
+    ]
     crossed, moved_parts = tie(crossed, moved_parts)
 
     expert_range = jnp.arange(EXPERTS, dtype=i32)

time: 470 us -> 480 us (1.021)
  Pallas kernels: 163 us -> 177 us
    pallas_call x0 -> x2, Pallas kernels: none -> 15.2 us  [moved_rows(): pl.pallas_call(moved_kernel, grid_spec=pltpu.PrefetchScalarGridSpec(num_s...]
    convert_element_type x7 -> x8, other arithmetic: 20.8 us -> 15.8 us  [add_low(): return sum([t.astype(f32) for t in terms]).astype(bf16)]
  transfers between devices with their start and end apart: 59 -> 60, of which waited for: 17 -> 19; matrix products, arithmetic and copies ran while one was open for 14% -> 12% of each run, Pallas kernels for 35% -> 37%
where the time goes in v15:
time: 480 us; the launch traced here: 472 us
  Pallas kernels  177 us (37%)
  waiting for transfers between devices  104 us (22%)
  starting transfers between devices  99.9 us (21%)
  other arithmetic  53.2 us (11%)
  local copies, waits for them, and re-layouts  22.9 us (5%)
  between operations  14.6 us (3%)
    ppermute x37, waiting for transfers between devices, send(): return lax.ppermute(rows, 'seq', shift_perm(a, b))  68.9 us
    ppermute x37, starting transfers between devices, send(): return lax.ppermute(rows, 'seq', shift_perm(a, b))  58.5 us
    pallas_call x2, Pallas kernels, run_experts(): pl.pallas_call(experts_kernel, grid_spec=pltpu.PrefetchScalarGridSpec(num...  42.3 us
    pallas_call x1, Pallas kernels, attend_back(): pl.pallas_call(attend_back_kernel, grid=(GROUP // BLOCK,), in_specs=[whol...  31.1 us
    pallas_call x1, Pallas kernels, attend(): pl.pallas_call(attend_kernel, grid=(GROUP // BLOCK,), in_specs=[whole(GRO...  19.8 us
    pallas_call x2, Pallas kernels, project(): pl.pallas_call(project_kernel, grid_spec=pltpu.PrefetchScalarGridSpec(num...  16.7 us
    pallas_call x1, Pallas kernels, expert_weight_grads(): pl.pallas_call(expert_grads_kernel, grid=(2, 4), in_specs=[pl.BlockSpec((...  15.9 us
    convert_element_type x8, other arithmetic, add_low(): return sum([t.astype(f32) for t in terms]).astype(bf16)  15.8 us
  transfers between devices with their start and end apart: 60, of which 19 were waited for; matrix products, arithmetic and copies ran while one was open for 12% of the time, Pallas kernels for 37%

profile of v15, /device:TPU:0, one launch (start us, length us, event | category | flops | bytes accessed | tf_op | source)
XLA Modules:
  0.0 471.5 jit_solution(3045017557970157958)
XLA Ops:
  19.8 6.8 %all-to-all-start = ((bf16[128,8,256]{2,1,0:T(8,128)(2,1)}), bf16[128,8,256]{2,1,0:T(8,128)(2,1)S(1)}, u32[]{:S(2)}, u32[]{:S(2)}) async-start(bf16[128,8,256]{2,1,0:T(8,128)(2,1)} %bitcast.9), calls=%async_computation | async-start | bytes 1048576 | tf_op jit(solution)/shard_map/all_to_all | solution.py:813
  28.7 7.7 %subtract_cosine_fusion.table = f32[3584,128]{1,0:T(8,128)} fusion(f32[128]{0:T(128)S(1)} %get-tuple-element.285, f32[128]{0:T(128)S(1)} %get-tuple-element.286, f32[3584]{0:T(1024)S(1)} %get-tuple-element.280), kind=kLoop, calls=%fused_computation.6 | loop fusion | flops 917504 | bytes 1850368 | tf_op jit(solution)/shard_map/cos | solution.py:138
  36.4 5.1 %all-to-all-done = bf16[128,8,256]{2,1,0:T(8,128)(2,1)S(1)} async-done(((bf16[128,8,256]{2,1,0:T(8,128)(2,1)}), bf16[128,8,256]{2,1,0:T(8,128)(2,1)S(1)}, u32[]{:S(2)}, u32[]{:S(2)}) %all-to-all-start) | async-done | bytes 524320 | tf_op jit(solution)/shard_map/all_to_all | solution.py:813
  52.2 8.0 %shard_map.178.refs_0_ = bf16[3584,256]{1,0:T(8,128)(2,1)} custom-call(s32[8]{0:T(128)} %get-tuple-element.283.places, bf16[4,224,1024]{2,1,0:T(8,128)(2,1)} %copy-done.1, bf16[4,224,1024]{2,1,0:T(8,128)(2,1)} %collective-permute-done.7.other.near_other, bf16[1024,256]{1,0:T(8,128)(2,1)} %broadcast_select_fusion.w, f32[1,1024]{1,0:T(1,128)} %bitcast.143, ...), custom_call_target="tpu_custom_call" | custom-call | flops 939524096 | bytes 10485760 | tf_op jit(solution)/shard_map/pallas_call | solution.py:175
  60.2 4.9 %collective-permute-done.8 = bf16[2,192,1024]{2,1,0:T(8,128)(2,1)} collective-permute-done((bf16[2,192,1024]{2,1,0:T(8,128)(2,1)}, bf16[2,192,1024]{2,1,0:T(8,128)(2,1)}, u32[]{:S(2)}, u32[]{:S(2)}) %collective-permute-start.8) | collective-permute-done | bytes 786464 | tf_op jit(solution)/shard_map/ppermute | solution.py:100
  65.1 4.8 %collective-permute-done.2 = bf16[224,1024]{1,0:T(8,128)(2,1)} collective-permute-done((bf16[224,1024]{1,0:T(8,128)(2,1)}, bf16[224,1024]{1,0:T(8,128)(2,1)}, u32[]{:S(2)}, u32[]{:S(2)}) %collective-permute-start.2) | collective-permute-done | bytes 458784 | tf_op jit(solution)/shard_map/ppermute | solution.py:53
  74.9 9.0 %all-to-all-start.1 = ((bf16[128,8,1152]{2,1,0:T(8,128)(2,1)}), bf16[128,8,1152]{2,1,0:T(8,128)(2,1)S(1)}, u32[]{:S(2)}, u32[]{:S(2)}) async-start(bf16[128,8,1152]{2,1,0:T(8,128)(2,1)} %broadcast_in_dim.101), calls=%async_computation.1 | async-start | bytes 4718592 | tf_op jit(solution)/shard_map/all_to_all | solution.py:831
  90.4 8.7 %shard_map.179.qkv_ref = bf16[3584,256]{1,0:T(8,128)(2,1)} custom-call(s32[8]{0:T(128)} %get-tuple-element.284.places, bf16[4,224,1024]{2,1,0:T(8,128)(2,1)} %pad_maximum_fusion.2.mine.far_mine, bf16[4,224,1024]{2,1,0:T(8,128)(2,1)} %collective-permute-done.9.other.far_other, bf16[1024,256]{1,0:T(8,128)(2,1)} %broadcast_select_fusion.w, ...), custom_call_target="tpu_custom_call" | custom-call | flops 939524096 | bytes 10485760 | tf_op jit(solution)/shard_map/pallas_call | solution.py:175
  99.1 19.8 %shard_map.180 = (bf16[16,64,224]{2,1,0:T(8,128)(2,1)}, f32[64,3584]{1,0:T(8,128)}, f32[1,3584]{1,0:T(1,128)}) custom-call(bf16[3584,256]{1,0:T(8,128)(2,1)} %shard_map.179.qkv_ref, s32[1,3584]{1,0:T(1,128)} %compare_select_fusion.begin_ref), custom_call_target="tpu_custom_call" | custom-call | flops 7247757312 | bytes 4194304 | tf_op jit(solution)/shard_map/pallas_call | solution.py:335
  118.9 5.3 %all-to-all-start.2 = ((bf16[16,64,224]{2,1,0:T(8,128)(2,1)}), bf16[16,64,224]{2,1,0:T(8,128)(2,1)S(1)}, u32[]{:S(2)}, u32[]{:S(2)}) async-start(bf16[16,64,224]{2,1,0:T(8,128)(2,1)} %get-tuple-element.143), calls=%async_computation.2 | async-start | bytes 1048576 | tf_op jit(solution)/shard_map/all_to_all | solution.py:846
  125.1 11.9 %collective-permute-done.12 = bf16[240,1024]{1,0:T(8,128)(2,1)} collective-permute-done((bf16[240,1024]{1,0:T(8,128)(2,1)S(1)}, bf16[240,1024]{1,0:T(8,128)(2,1)}, u32[]{:S(2)}, u32[]{:S(2)}) %collective-permute-start.12) | collective-permute-done | bytes 491552 | tf_op jit(solution)/shard_map/ppermute | solution.py:53
  151.6 12.5 %collective-permute-done.13 = bf16[224,1024]{1,0:T(8,128)(2,1)S(1)} collective-permute-done((bf16[224,1024]{1,0:T(8,128)(2,1)}, bf16[224,1024]{1,0:T(8,128)(2,1)S(1)}, u32[]{:S(2)}, u32[]{:S(2)}) %collective-permute-start.13) | collective-permute-done | bytes 458784 | tf_op jit(solution)/shard_map/ppermute | solution.py:53
  164.1 6.1 %collective-permute-done.18 = bf16[224,1024]{1,0:T(8,128)(2,1)S(1)} collective-permute-done((bf16[224,1024]{1,0:T(8,128)(2,1)}, bf16[224,1024]{1,0:T(8,128)(2,1)S(1)}, u32[]{:S(2)}, u32[]{:S(2)}) %collective-permute-start.18) | collective-permute-done | bytes 458784 | tf_op jit(solution)/shard_map/ppermute | solution.py:53
  182.5 21.3 %shard_map.182 = (bf16[4,256,1024]{2,1,0:T(8,128)(2,1)}, bf16[4,256,1024]{2,1,0:T(8,128)(2,1)}, bf16[16,144,1024]{2,1,0:T(8,128)(2,1)}, bf16[2,1152,1024]{2,1,0:...) custom-call(s32[2]{0:T(128)} %pad_add_fusion.own_ref, ...), custom_call_target="tpu_custom_call" | custom-call | flops 15032385536 | bytes 25165824 | tf_op jit(solution)/shard_map/pallas_call | solution.py:610
  203.9 7.6 %collective-permute-done.22 = bf16[3,240,1024]{2,1,0:T(8,128)(2,1)S(1)} collective-permute-done((bf16[3,240,1024]{2,1,0:T(8,128)(2,1)}, bf16[3,240,1024]{2,1,0:T(8,128)(2,1)S(1)}, u32[]{:S(2)}, u32[]{:S(2)}) %collective-permute-start.22) | collective-permute-done | bytes 1474592 | tf_op jit(solution)/shard_map/ppermute | solution.py:53
  224.0 21.0 %shard_map.183 = (bf16[4,256,1024]{2,1,0:T(8,128)(2,1)}, bf16[4,256,1024]{2,1,0:T(8,128)(2,1)}, bf16[16,144,1024]{2,1,0:T(8,128)(2,1)}, bf16[2,1152,1024]{2,1,0:...) custom-call(s32[2]{0:T(128)} %pad_add_fusion.own_ref, ...), custom_call_target="tpu_custom_call", output_to_operand_aliasing={{2}: (10, {}), {3}: (11, {}), {4}: (12, {}), {5}: (13, {}),... | custom-call | flops 15032385536 | bytes 25165824 | tf_op jit(solution)/shard_map/pallas_call | solution.py:610
  246.4 4.4 collective-permute-done.30
  256.9 15.9 %shard_map.184 = bf16[4,2,2,192,1024]{4,3,2,1,0:T(8,128)(2,1)} custom-call(bf16[2,1152,1024]{2,1,0:T(8,128)(2,1)} %get-tuple-element.182.x_ref, bf16[2,1152,1024]{2,1,0:T(8,128)(2,1)} %get-tuple-element.183.dh_ref, bf16[2,1152,512]{2,1,0:T(8,128)(2,1)} %get-tuple-element.184.act_ref, bf16[2,1152,1024]{2,1,0:T(8,128)(2,1)} %get-tuple-element.185.dy_ref), custom_call_target="tpu_custom_call" | custom-call | flops 8589934592 | bytes 14680064 | tf_op jit(solution)/shard_map/pallas_call | solution.py:664
  272.8 7.6 %shard_map.186 = (bf16[4,224,1024]{2,1,0:T(8,128)(2,1)}, bf16[4,224,1024]{2,1,0:T(8,128)(2,1)}) custom-call(s32[2]{0:T(128)} %pad_add_fusion.own_ref, bf16[4,240,1024]{2,1,0:T(8,128)(2,1)} %copy-done.8, bf16[4,240,1024]{2,1,0:T(8,128)(2,1)} %copy-done.10, bf16[16,144,1024]{2,1,0:T(8,128)(2,1)} %get-tuple-element.186.z_ref), custom_call_target="tpu_custom_call" | custom-call | flops 1073741824 | bytes 6291456 | tf_op jit(solution)/shard_map/pallas_call | solution.py:584
  280.5 7.6 %shard_map.185 = (bf16[4,224,1024]{2,1,0:T(8,128)(2,1)}, bf16[4,224,1024]{2,1,0:T(8,128)(2,1)}) custom-call(s32[2]{0:T(128)} %pad_add_fusion.own_ref, bf16[4,240,1024]{2,1,0:T(8,128)(2,1)} %copy-done.2, bf16[4,240,1024]{2,1,0:T(8,128)(2,1)} %collective-permute-done.25.g_other.routes_other, bf16[16,144,1024]{2,1,0:T(8,128)(2,1)} %get-tuple-element.186.z_ref), custom_call_target="tpu_custom_call" | custom-call | flops 1073741824 | bytes 6291456 | tf_op jit(solution)/shard_map/pallas_call | solution.py:584
  298.9 6.4 %collective-permute-done.34.crossed = bf16[256,1024]{1,0:T(8,128)(2,1)S(1)} collective-permute-done((bf16[256,1024]{1,0:T(8,128)(2,1)S(1)}, bf16[256,1024]{1,0:T(8,128)(2,1)S(1)}, u32[]{:S(2)}, u32[]{:S(2)}) %collective-permute-start.34) | collective-permute-done | bytes 524320 | tf_op jit(solution)/shard_map/ppermute | solution.py:53
  306.1 5.8 %shard_map.187 = (f32[224,1024]{1,0:T(8,128)}, bf16[224,1024]{1,0:T(8,128)(2,1)}, bf16[32,224]{1,0:T(8,128)(2,1)}, bf16[224,1024]{1,0:T(8,128)(2,1)}, bf16[16,64,224]{2,1,0:T(8,128)(2,1)}) custom-call(bf16[256,1024]{1,0:T(8,128)(2,1)} %get-tuple-element.174.t0, bf16[256,1024]{1,0:T(8,128)(2,1)} %collective-permute-done.27.t1, ...), custom_call_target="tpu_custom_call" | custom-call | flops 469762048 | bytes 8388608 | tf_op jit(solution)/shard_map/pallas_call | solution.py:735
  311.9 6.0 %all-to-all-start.3 = ((bf16[16,64,224]{2,1,0:T(8,128)(2,1)}), bf16[16,64,224]{2,1,0:T(8,128)(2,1)S(1)}, u32[]{:S(2)}, u32[]{:S(2)}) async-start(bf16[16,64,224]{2,1,0:T(8,128)(2,1)} %get-tuple-element.200), calls=%async_computation.3 | async-start | bytes 1048576 | tf_op jit(solution)/shard_map/all_to_all | solution.py:894
  321.9 8.4 %all-to-all-done.3.g_ref = bf16[16,64,224]{2,1,0:T(8,128)(2,1)S(1)} async-done(((bf16[16,64,224]{2,1,0:T(8,128)(2,1)}), bf16[16,64,224]{2,1,0:T(8,128)(2,1)S(1)}, u32[]{:S(2)}, u32[]{:S(2)}) %all-to-all-start.3) | async-done | bytes 458784 | tf_op jit(solution)/shard_map/all_to_all | solution.py:894
  331.1 4.5 all-to-all-start.4
  338.3 31.1 %shard_map.189.first.second = bf16[3584,256]{1,0:T(8,128)(2,1)} custom-call(bf16[3584,256]{1,0:T(8,128)(2,1)} %shard_map.179.qkv_ref, bf16[16,64,224]{2,1,0:T(8,128)(2,1)} %copy-done.21, f32[64,3584]{1,0:T(8,128)} %get-tuple-element.209.ot_ref, f32[1,3584]{1,0:T(1,128)} %get-tuple-element.210.lse_ref, s32[1,3584]{1,0:T(1,128)} %compare_select_fusion.begin_ref, ...), custom_call_target="tpu_custom_call" | custom-call | flops 18119393280 | bytes 8388608 | tf_op jit(solution)/shard_map/pallas_call | solution.py:415
  369.4 7.2 %all-to-all-done.4 = bf16[8,128,1152]{2,1,0:T(8,128)(2,1)S(1)} async-done(((bf16[8,128,1152]{2,1,0:T(8,128)(2,1)}), bf16[8,128,1152]{2,1,0:T(8,128)(2,1)S(1)}, u32[]{:S(2)}, u32[]{:S(2)}) %all-to-all-start.4) | async-done | bytes 2359328 | tf_op jit(solution)/shard_map/all_to_all | solution.py:901
  377.8 5.7 %shard_map.190 = (bf16[4,240,1024]{2,1,0:T(8,128)(2,1)}, bf16[4,240,1024]{2,1,0:T(8,128)(2,1)}) custom-call(s32[8]{0:T(128)} %get-tuple-element.284.places, bf16[3584,256]{1,0:T(8,128)(2,1)} %shard_map.189.first.second, bf16[3584,256]{1,0:T(8,128)(2,1)} %shard_map.189.first.second, bf16[1024,256]{1,0:T(8,128)(2,1)} %broadcast_select_fusion.w, ...), custom_call_target="tpu_custom_call" | custom-call | flops 939524096 | bytes 5242880 | tf_op jit(solution)/shard_map/pallas_call | solution.py:206
  383.5 5.8 %shard_map.191 = (bf16[4,240,1024]{2,1,0:T(8,128)(2,1)}, bf16[4,240,1024]{2,1,0:T(8,128)(2,1)}) custom-call(s32[8]{0:T(128)} %get-tuple-element.283.places, bf16[3584,256]{1,0:T(8,128)(2,1)} %shard_map.189.first.second, bf16[3584,256]{1,0:T(8,128)(2,1)} %shard_map.189.first.second, bf16[1024,256]{1,0:T(8,128)(2,1)} %broadcast_select_fusion.w, ...), custom_call_target="tpu_custom_call" | custom-call | flops 939524096 | bytes 5242880 | tf_op jit(solution)/shard_map/pallas_call | solution.py:206
  408.1 10.8 %shard_map.192 = bf16[1024,256]{1,0:T(8,128)(2,1)} custom-call(s32[16]{0:T(128)} %copy-done.39, bf16[4,224,1024]{2,1,0:T(8,128)(2,1)} %copy-done.1, bf16[4,224,1024]{2,1,0:T(8,128)(2,1)} %collective-permute-done.7.other.near_other, bf16[4,224,1024]{2,1,0:T(8,128)(2,1)} %pad_maximum_fusion.2.mine.far_mine, ...), custom_call_target="tpu_custom_call" | custom-call | flops 1879048192 | bytes 10485760 | tf_op jit(solution)/shard_map/pallas_call | solution.py:250
  418.8 5.8 %all-to-all-start.5 = ((bf16[128,8,256]{2,1,0:T(8,128)(2,1)}), bf16[128,8,256]{2,1,0:T(8,128)(2,1)S(1)}, u32[]{:S(2)}, u32[]{:S(2)}) async-start(bf16[128,8,256]{2,1,0:T(8,128)(2,1)} %bitcast.127), calls=%async_computation.6 | async-start | bytes 1048576 | tf_op jit(solution)/shard_map/all_to_all | solution.py:916
  441.7 12.0 %collective-permute-done.47 = bf16[240,1024]{1,0:T(8,128)(2,1)S(1)} collective-permute-done((bf16[240,1024]{1,0:T(8,128)(2,1)}, bf16[240,1024]{1,0:T(8,128)(2,1)S(1)}, u32[]{:S(2)}, u32[]{:S(2)}) %collective-permute-start.47) | collective-permute-done | bytes 491552 | tf_op jit(solution)/shard_map/ppermute | solution.py:53
  (284 shorter events, 151.6 us)
Async XLA Ops:
  7.2 35.1 %collective-permute-start = (bf16[224,1024]{1,0:T(8,128)(2,1)}, bf16[224,1024]{1,0:T(8,128)(2,1)S(1)}, u32[]{:S(2)}, u32[]{:S(2)}) collective-permute-start(bf16[224,1024]{1,0:T(8,128)(2,1)} %bitcast.119), channel_id=1, source_target_pairs={{0,64},{8,72},{16,80},{24,88},{32,96},{40,104},{48,112},{56,120},{... | collective-permute-start | bytes 1376264 | tf_op jit(solution)/shard_map/ppermute | solution.py:53
  10.4 32.0 %collective-permute-start.4 = (bf16[224,1024]{1,0:T(8,128)(2,1)}, bf16[224,1024]{1,0:T(8,128)(2,1)S(1)}, u32[]{:S(2)}, u32[]{:S(2)}) collective-permute-start(bf16[224,1024]{1,0:T(8,128)(2,1)} %bitcast.120), channel_id=1, source_target_pairs={{0,16},{8,24},{16,32},{24,40},{32,48},{40,56},{48,0},{56,8},{64,80... | collective-permute-start | bytes 1376264 | tf_op jit(solution)/shard_map/ppermute | solution.py:53
  12.3 30.0 %collective-permute-start.5 = (bf16[224,1024]{1,0:T(8,128)(2,1)}, bf16[224,1024]{1,0:T(8,128)(2,1)S(1)}, u32[]{:S(2)}, u32[]{:S(2)}) collective-permute-start(bf16[224,1024]{1,0:T(8,128)(2,1)} %bitcast.121), channel_id=1, source_target_pairs={{0,48},{8,56},{16,0},{24,8},{32,16},{40,24},{48,32},{56,40},{64,11... | collective-permute-start | bytes 1376264 | tf_op jit(solution)/shard_map/ppermute | solution.py:53
  14.4 27.9 %collective-permute-start.6 = (bf16[224,1024]{1,0:T(8,128)(2,1)}, bf16[224,1024]{1,0:T(8,128)(2,1)}, u32[]{:S(2)}, u32[]{:S(2)}) collective-permute-start(bf16[224,1024]{1,0:T(8,128)(2,1)} %bitcast.122), channel_id=1, source_target_pairs={{0,32},{8,40},{16,48},{24,56},{32,0},{40,8},{48,16},{56,24},{64,96... | collective-permute-start | bytes 1376264 | tf_op jit(solution)/shard_map/ppermute | solution.py:53
  26.6 155.9 %all-gather.5.cloned.1.call-start = ((), (), s32[]{:S(2)}) async-start(), calls=%async_computation.8 | async-start | bytes 3932160 | tf_op jit(solution)/shard_map/all_gather | solution.py:823
  74.9 44.0 %all-to-all-start.1 = ((bf16[128,8,1152]{2,1,0:T(8,128)(2,1)}), bf16[128,8,1152]{2,1,0:T(8,128)(2,1)S(1)}, u32[]{:S(2)}, u32[]{:S(2)}) async-start(bf16[128,8,1152]{2,1,0:T(8,128)(2,1)} %broadcast_in_dim.101), calls=%async_computation.1 | async-start | bytes 4718592 | tf_op jit(solution)/shard_map/all_to_all | solution.py:831
  84.0 98.5 %all-gather.7.cloned.1.call-start = ((), (), s32[]{:S(2)}) async-start(), calls=%async_computation.9 | async-start | bytes 3932160 | tf_op jit(solution)/shard_map/all_gather | solution.py:823
  85.3 39.8 %collective-permute-start.10 = (bf16[240,1024]{1,0:T(8,128)(2,1)S(1)}, bf16[240,1024]{1,0:T(8,128)(2,1)}, u32[]{:S(2)}, u32[]{:S(2)}) collective-permute-start(bf16[240,1024]{1,0:T(8,128)(2,1)S(1)} %fusion.17), channel_id=1, source_target_pairs={{0,16},{8,24},{16,32},{24,40},{32,48},{40,56},{48,0},{56,8},{64,80... | collective-permute-start | bytes 1474568 | tf_op jit(solution)/shard_map/ppermute | solution.py:53
  86.4 38.7 %collective-permute-start.11 = (bf16[240,1024]{1,0:T(8,128)(2,1)S(1)}, bf16[240,1024]{1,0:T(8,128)(2,1)}, u32[]{:S(2)}, u32[]{:S(2)}) collective-permute-start(bf16[240,1024]{1,0:T(8,128)(2,1)S(1)} %fusion.17), channel_id=1, source_target_pairs={{0,48},{8,56},{16,0},{24,8},{32,16},{40,24},{48,32},{56,40},{64,11... | collective-permute-start | bytes 1474568 | tf_op jit(solution)/shard_map/ppermute | solution.py:53
  88.5 48.5 %collective-permute-start.12 = (bf16[240,1024]{1,0:T(8,128)(2,1)S(1)}, bf16[240,1024]{1,0:T(8,128)(2,1)}, u32[]{:S(2)}, u32[]{:S(2)}) collective-permute-start(bf16[240,1024]{1,0:T(8,128)(2,1)S(1)} %fusion.17), channel_id=1, source_target_pairs={{0,32},{8,40},{16,48},{24,56},{32,0},{40,8},{48,16},{56,24},{64,96... | collective-permute-start | bytes 1474568 | tf_op jit(solution)/shard_map/ppermute | solution.py:53
  124.2 265.1 %reduce-scatter.2.cloned.1.call-start = ((), (), s32[]{:S(2)}) async-start(), calls=%async_computation.7 | async-start | bytes 7864320 | tf_op jit(solution)/shard_map/reduce_scatter | solution.py:887
  139.5 30.6 %collective-permute-start.21 = (bf16[1,240,1024]{2,1,0:T(8,128)(2,1)S(1)}, bf16[1,240,1024]{2,1,0:T(8,128)(2,1)S(1)}, u32[]{:S(2)}, u32[]{:S(2)}) collective-permute-start(bf16[1,240,1024]{2,1,0:T(8,128)(2,1)S(1)} %bitcast.128), channel_id=1, source_target_pairs={{0,64},{8,72},{16,80},{24,88},{32,96},{40,104},{48,112},{56,120},{... | collective-permute-start | bytes 1474568 | tf_op jit(solution)/shard_map/ppermute | solution.py:53
  175.2 36.4 %collective-permute-start.22 = (bf16[3,240,1024]{2,1,0:T(8,128)(2,1)}, bf16[3,240,1024]{2,1,0:T(8,128)(2,1)S(1)}, u32[]{:S(2)}, u32[]{:S(2)}) collective-permute-start(bf16[3,240,1024]{2,1,0:T(8,128)(2,1)} %slice.235), channel_id=1, source_target_pairs={{0,64},{8,72},{16,80},{24,88},{32,96},{40,104},{48,112},{56,120},{... | collective-permute-start | bytes 4423688 | tf_op jit(solution)/shard_map/ppermute | solution.py:53
  177.6 34.2 %collective-permute-start.14 = (bf16[224,1024]{1,0:T(8,128)(2,1)}, bf16[224,1024]{1,0:T(8,128)(2,1)}, u32[]{:S(2)}, u32[]{:S(2)}) collective-permute-start(bf16[224,1024]{1,0:T(8,128)(2,1)} %copy-done.29), channel_id=1, source_target_pairs={{0,16},{8,24},{16,32},{24,40},{32,48},{40,56},{48,0},{56,8},{64,80... | collective-permute-start | bytes 1376264 | tf_op jit(solution)/shard_map/ppermute | solution.py:53
  178.5 33.3 %collective-permute-start.15 = (bf16[224,1024]{1,0:T(8,128)(2,1)}, bf16[224,1024]{1,0:T(8,128)(2,1)}, u32[]{:S(2)}, u32[]{:S(2)}) collective-permute-start(bf16[224,1024]{1,0:T(8,128)(2,1)} %copy-done.29), channel_id=1, source_target_pairs={{0,48},{8,56},{16,0},{24,8},{32,16},{40,24},{48,32},{56,40},{64,11... | collective-permute-start | bytes 1376264 | tf_op jit(solution)/shard_map/ppermute | solution.py:53
  180.9 30.9 %collective-permute-start.16 = (bf16[224,1024]{1,0:T(8,128)(2,1)}, bf16[224,1024]{1,0:T(8,128)(2,1)S(1)}, u32[]{:S(2)}, u32[]{:S(2)}) collective-permute-start(bf16[224,1024]{1,0:T(8,128)(2,1)} %copy-done.29), channel_id=1, source_target_pairs={{0,32},{8,40},{16,48},{24,56},{32,0},{40,8},{48,16},{56,24},{64,96... | collective-permute-start | bytes 1376264 | tf_op jit(solution)/shard_map/ppermute | solution.py:53
  216.9 28.1 %collective-permute-start.27 = (bf16[256,1024]{1,0:T(8,128)(2,1)}, bf16[256,1024]{1,0:T(8,128)(2,1)}, u32[]{:S(2)}, u32[]{:S(2)}) collective-permute-start(bf16[256,1024]{1,0:T(8,128)(2,1)} %get-tuple-element.259), channel_id=1, source_target_pairs={{0,48},{8,56},{16,0},{24,8},{32,16},{40,24},{48,32},{56,40},{64,11... | collective-permute-start | bytes 1572872 | tf_op jit(solution)/shard_map/ppermute | solution.py:53
  253.3 34.8 %collective-permute-start.31 = (bf16[256,1024]{1,0:T(8,128)(2,1)S(1)}, bf16[256,1024]{1,0:T(8,128)(2,1)S(1)}, u32[]{:S(2)}, u32[]{:S(2)}) collective-permute-start(bf16[256,1024]{1,0:T(8,128)(2,1)S(1)} %get-tuple-element.255), channel_id=1, source_target_pairs={{0,48},{8,56},{16,0},{24,8},{32,16},{40,24},{48,32},{56,40},{64,11... | collective-permute-start | bytes 1572872 | tf_op jit(solution)/shard_map/ppermute | solution.py:53
  253.9 34.2 %collective-permute-start.32 = (bf16[256,1024]{1,0:T(8,128)(2,1)S(1)}, bf16[256,1024]{1,0:T(8,128)(2,1)S(1)}, u32[]{:S(2)}, u32[]{:S(2)}) collective-permute-start(bf16[256,1024]{1,0:T(8,128)(2,1)S(1)} %get-tuple-element.254), channel_id=1, source_target_pairs={{0,16},{8,24},{16,32},{24,40},{32,48},{40,56},{48,0},{56,8},{64,80... | collective-permute-start | bytes 1572872 | tf_op jit(solution)/shard_map/ppermute | solution.py:53
  255.4 32.7 %collective-permute-start.33 = (bf16[256,1024]{1,0:T(8,128)(2,1)S(1)}, bf16[256,1024]{1,0:T(8,128)(2,1)S(1)}, u32[]{:S(2)}, u32[]{:S(2)}) collective-permute-start(bf16[256,1024]{1,0:T(8,128)(2,1)S(1)} %get-tuple-element.253), channel_id=1, source_target_pairs={{0,32},{8,40},{16,48},{24,56},{32,0},{40,8},{48,16},{56,24},{64,96... | collective-permute-start | bytes 1572872 | tf_op jit(solution)/shard_map/ppermute | solution.py:53
  331.1 45.6 %all-to-all-start.4 = ((bf16[8,128,1152]{2,1,0:T(8,128)(2,1)}), bf16[8,128,1152]{2,1,0:T(8,128)(2,1)S(1)}, u32[]{:S(2)}, u32[]{:S(2)}) async-start(bf16[8,128,1152]{2,1,0:T(8,128)(2,1)} %shard_map.188), calls=%async_computation.4 | async-start | bytes 4718592 | tf_op jit(solution)/shard_map/all_to_all | solution.py:901
  335.5 53.8 %collective-permute-start.38 = (bf16[2,224,1024]{2,1,0:T(8,128)(2,1)}, bf16[2,224,1024]{2,1,0:T(8,128)(2,1)}, u32[]{:S(2)}, u32[]{:S(2)}) collective-permute-start(bf16[2,224,1024]{2,1,0:T(8,128)(2,1)} %pad_maximum_fusion.6), channel_id=1, source_target_pairs={{0,48},{8,56},{16,0},{24,8},{32,16},{40,24},{48,32},{56,40},{64,11... | collective-permute-start | bytes 2752520 | tf_op jit(solution)/shard_map/ppermute | solution.py:53
  336.5 52.8 %collective-permute-start.39 = (bf16[2,224,1024]{2,1,0:T(8,128)(2,1)}, bf16[2,224,1024]{2,1,0:T(8,128)(2,1)}, u32[]{:S(2)}, u32[]{:S(2)}) collective-permute-start(bf16[2,224,1024]{2,1,0:T(8,128)(2,1)} %pad_maximum_fusion.7), channel_id=1, source_target_pairs={{0,16},{8,24},{16,32},{24,40},{32,48},{40,56},{48,0},{56,8},{64,80... | collective-permute-start | bytes 2752520 | tf_op jit(solution)/shard_map/ppermute | solution.py:53
  337.5 51.8 %collective-permute-start.40 = (bf16[2,224,1024]{2,1,0:T(8,128)(2,1)}, bf16[2,224,1024]{2,1,0:T(8,128)(2,1)}, u32[]{:S(2)}, u32[]{:S(2)}) collective-permute-start(bf16[2,224,1024]{2,1,0:T(8,128)(2,1)} %pad_maximum_fusion.8), channel_id=1, source_target_pairs={{0,32},{8,40},{16,48},{24,56},{32,0},{40,8},{48,16},{56,24},{64,96... | collective-permute-start | bytes 2752520 | tf_op jit(solution)/shard_map/ppermute | solution.py:53
  399.8 27.7 %collective-permute-start.44 = (bf16[240,1024]{1,0:T(8,128)(2,1)}, bf16[240,1024]{1,0:T(8,128)(2,1)}, u32[]{:S(2)}, u32[]{:S(2)}) collective-permute-start(bf16[240,1024]{1,0:T(8,128)(2,1)} %get-tuple-element.235), channel_id=1, source_target_pairs={{0,16},{8,24},{16,32},{24,40},{32,48},{40,56},{48,0},{56,8},{64,80... | collective-permute-start | bytes 1474568 | tf_op jit(solution)/shard_map/ppermute | solution.py:53
  399.8 27.7 %collective-permute-start.45 = (bf16[240,1024]{1,0:T(8,128)(2,1)}, bf16[240,1024]{1,0:T(8,128)(2,1)}, u32[]{:S(2)}, u32[]{:S(2)}) collective-permute-start(bf16[240,1024]{1,0:T(8,128)(2,1)} %get-tuple-element.236), channel_id=1, source_target_pairs={{0,32},{8,40},{16,48},{24,56},{32,0},{40,8},{48,16},{56,24},{64,96... | collective-permute-start | bytes 1474568 | tf_op jit(solution)/shard_map/ppermute | solution.py:53
  402.2 36.2 %collective-permute-start.50 = (bf16[2,192,1024]{2,1,0:T(8,128)(2,1)}, bf16[2,192,1024]{2,1,0:T(8,128)(2,1)}, u32[]{:S(2)}, u32[]{:S(2)}) collective-permute-start(bf16[2,192,1024]{2,1,0:T(8,128)(2,1)} %dynamic-slice_bitcast_fusion), channel_id=1, source_target_pairs={{0,1},{1,0},{2,3},{3,2},{4,5},{5,4},{6,7},{7,6},{8,9},{9,8},{10,11... | collective-permute-start | bytes 2359304 | tf_op jit(solution)/shard_map/ppermute | solution.py:100
  406.0 28.3 %collective-permute-start.42 = (bf16[224,1024]{1,0:T(8,128)(2,1)}, bf16[224,1024]{1,0:T(8,128)(2,1)}, u32[]{:S(2)}, u32[]{:S(2)}) collective-permute-start(bf16[224,1024]{1,0:T(8,128)(2,1)} %fusion.26), channel_id=1, source_target_pairs={{0,64},{8,72},{16,80},{24,88},{32,96},{40,104},{48,112},{56,120},{... | collective-permute-start | bytes 1376264 | tf_op jit(solution)/shard_map/ppermute | solution.py:53
  418.8 38.8 %all-to-all-start.5 = ((bf16[128,8,256]{2,1,0:T(8,128)(2,1)}), bf16[128,8,256]{2,1,0:T(8,128)(2,1)S(1)}, u32[]{:S(2)}, u32[]{:S(2)}) async-start(bf16[128,8,256]{2,1,0:T(8,128)(2,1)} %bitcast.127), calls=%async_computation.6 | async-start | bytes 1048576 | tf_op jit(solution)/shard_map/all_to_all | solution.py:916
  424.6 29.0 %collective-permute-start.47 = (bf16[240,1024]{1,0:T(8,128)(2,1)}, bf16[240,1024]{1,0:T(8,128)(2,1)S(1)}, u32[]{:S(2)}, u32[]{:S(2)}) collective-permute-start(bf16[240,1024]{1,0:T(8,128)(2,1)} %get-tuple-element.238), channel_id=1, source_target_pairs={{0,48},{8,56},{16,0},{24,8},{32,16},{40,24},{48,32},{56,40},{64,11... | collective-permute-start | bytes 1474568 | tf_op jit(solution)/shard_map/ppermute | solution.py:53
  427.5 29.3 %collective-permute-start.48 = (bf16[240,1024]{1,0:T(8,128)(2,1)}, bf16[240,1024]{1,0:T(8,128)(2,1)S(1)}, u32[]{:S(2)}, u32[]{:S(2)}) collective-permute-start(bf16[240,1024]{1,0:T(8,128)(2,1)} %get-tuple-element.239), channel_id=1, source_target_pairs={{0,16},{8,24},{16,32},{24,40},{32,48},{40,56},{48,0},{56,8},{64,80... | collective-permute-start | bytes 1474568 | tf_op jit(solution)/shard_map/ppermute | solution.py:53
  427.5 30.1 %collective-permute-start.49 = (bf16[240,1024]{1,0:T(8,128)(2,1)}, bf16[240,1024]{1,0:T(8,128)(2,1)}, u32[]{:S(2)}, u32[]{:S(2)}) collective-permute-start(bf16[240,1024]{1,0:T(8,128)(2,1)} %get-tuple-element.240), channel_id=1, source_target_pairs={{0,32},{8,40},{16,48},{24,56},{32,0},{40,8},{48,16},{56,24},{64,96... | collective-permute-start | bytes 1474568 | tf_op jit(solution)/shard_map/ppermute | solution.py:53
  (73 other events, 767.6 us)
Sparse Core Ops, SparseCore 0:
  29.1 40.6 all-gather.4
  86.5 50.9 all-gather.6
  288.2 88.4 reduce-scatter.1

commit v16 on v14

--- a/solution.py
+++ b/solution.py
@@ -20,6 +20,7 @@
 BLOCK = 512
 VMEM_LIMIT = 60 << 20
 LAST = TOK + 16
+EARLY = 352
 PAY = TOK + 32
 
 norm_eps = 1e-06
@@ -804,19 +805,20 @@
     attended = lax.all_to_all(attended_head, "seq", 0, 0, tiled=True)
     attended, grad_near = tie(attended, grad_near)
     grad_near = jnp.stack(grad_near)
-    grad_far = [send(grad_near[:2], 1, 0)]
+    grad_rows = grad_near.reshape(-1, WIDTH)
+    grad_far = [send(grad_rows[:EARLY], 1, 0)]
     hidden, normed_ffn = hidden_of(attended, shared, rows, gain_ffn)
     ffn_near, ffn_across = gather_near(normed_ffn)
-    grad_near_mine, _ = tie(grad_near, ffn_across)
+    grad_rows, _ = tie(grad_rows, ffn_across)
     ffn_near, _, grad_far[0] = tie(ffn_near, ffn_across, grad_far[0])
-    grad_far.append(send(grad_near_mine[2:], 1, 0))
+    grad_far.append(send(grad_rows[EARLY:], 1, 0))
     grad_near = (grad_near, swap_cores(grad_near))
     ffn_near, ffn_far = both_cores(ffn_near), gather_far(ffn_across)
     own = jnp.stack([seq_index * 2, own_x])
     near = run_experts(0, own, ffn_near, grad_near, experts, router_t, ())
     near_terms = sum_along_z(*near[:2])
     ffn_far = both_cores(ffn_far)
-    grad_far = jnp.concatenate(grad_far, axis=0)
+    grad_far = jnp.concatenate(grad_far, axis=0).reshape(grad_near[0].shape)
     grad_far = (grad_far, swap_cores(grad_far))
     far = run_experts(1, own, ffn_far, grad_far, experts, router_t, near[2:])
     far, near_terms = tie(far, near_terms)
@@ -852,19 +854,20 @@
 
     shared_grads = lax.all_to_all(shared_grads, "wshard", 0, 0, tiled=True)
     projected_grad = attend_back(qkv, head_grad, attended_t, lse, begin, table)
+    grad_head = head_weight_grad(places, rows_near, rows_far, gain_attn, projected_grad)
+    shared_grads, grad_head, projected_grad = tie(shared_grads, grad_head, projected_grad)
     shared_grads = jnp.sum(shared_grads.astype(f32), axis=0)
     far_part = project_back(places[8:], projected_grad, head_weights, shared_grads)
     near_part = project_back(places[:8], projected_grad, head_weights, shared_grads)
     far_parts = chip_parts(far_part[0], swap_cores(far_part[1]))
     near_part, moved_terms, expert_grads = tie(near_part, moved_terms, expert_grads)
     near_parts = chip_parts(near_part[0], swap_cores(near_part[1]))
-    far_parts, near_parts, projected_grad, moved_terms, expert_grads = tie(
-        far_parts, near_parts, projected_grad, moved_terms, expert_grads
+    far_parts, near_parts, grad_head, moved_terms, expert_grads = tie(
+        far_parts, near_parts, grad_head, moved_terms, expert_grads
     )
     far_terms = send_along_z(far_parts)
     near_terms = send_along_z(near_parts)
     moved_crossed = send(add_low(*[t[1] for t in moved_terms]), 1, 0)
-    grad_head = head_weight_grad(places, rows_near, rows_far, gain_attn, projected_grad)
     grad_heads = lax.all_to_all(grad_head.reshape(128, 8, 256), BOTH, 0, 0, tiled=True)
     crossed = send(add_low(*far_terms), 1, 0)
     crossed, near_terms, grad_heads = tie(crossed, near_terms, grad_heads)

time: 470 us -> 469 us (level)
  waiting for transfers between devices: 108 us -> 99 us
  starting transfers between devices: 96 us -> 103 us
    all_to_all x1, waiting for transfers between devices: 9.01 us -> 0.01 us  [local(): shared_grads = lax.all_to_all(shared_grads, 'wshard', 0, 0, tiled=True)]
    ppermute x37, starting transfers between devices: 55.2 us -> 60 us  [send(): return lax.ppermute(rows, 'seq', shift_perm(a, b))]
  transfers between devices with their start and end apart: 59 -> 59, of which waited for: 17 -> 19; matrix products, arithmetic and copies ran while one was open for 14% -> 14% of each run, Pallas kernels for 35% -> 36%
where the time goes in v16:
time: 469 us; the launch traced here: 460 us
  Pallas kernels  163 us (35%)
  starting transfers between devices  103 us (22%)
  waiting for transfers between devices  99 us (21%)
  other arithmetic  57.4 us (12%)
  local copies, waits for them, and re-layouts  22 us (5%)
  between operations  14.9 us (3%)
    ppermute x37, waiting for transfers between devices, send(): return lax.ppermute(rows, 'seq', shift_perm(a, b))  72.4 us
    ppermute x37, starting transfers between devices, send(): return lax.ppermute(rows, 'seq', shift_perm(a, b))  60 us
    pallas_call x2, Pallas kernels, run_experts(): pl.pallas_call(experts_kernel, grid_spec=pltpu.PrefetchScalarGridSpec(num...  44 us
    pallas_call x1, Pallas kernels, attend_back(): pl.pallas_call(attend_back_kernel, grid=(GROUP // BLOCK,), in_specs=[whol...  31.1 us
    convert_element_type x7, other arithmetic, add_low(): return sum([t.astype(f32) for t in terms]).astype(bf16)  20.6 us
    pallas_call x1, Pallas kernels, attend(): pl.pallas_call(attend_kernel, grid=(GROUP // BLOCK,), in_specs=[whole(GRO...  19.8 us
    pallas_call x2, Pallas kernels, project(): pl.pallas_call(project_kernel, grid_spec=pltpu.PrefetchScalarGridSpec(num...  16.7 us
    pallas_call x1, Pallas kernels, expert_weight_grads(): pl.pallas_call(expert_grads_kernel, grid=(2, 4), in_specs=[pl.BlockSpec((...  15.9 us
  transfers between devices with their start and end apart: 59, of which 19 were waited for; matrix products, arithmetic and copies ran while one was open for 14% of the time, Pallas kernels for 36%

profile of v16, /device:TPU:0, one launch (start us, length us, event | category | flops | bytes accessed | tf_op | source)
XLA Modules:
  0.0 459.9 jit_solution(4752938998590517615)
XLA Ops:
  19.8 6.8 %all-to-all-start = ((bf16[128,8,256]{2,1,0:T(8,128)(2,1)}), bf16[128,8,256]{2,1,0:T(8,128)(2,1)S(1)}, u32[]{:S(2)}, u32[]{:S(2)}) async-start(bf16[128,8,256]{2,1,0:T(8,128)(2,1)} %bitcast.9), calls=%async_computation | async-start | bytes 1048576 | tf_op jit(solution)/shard_map/all_to_all | solution.py:772
  28.7 7.7 %subtract_cosine_fusion.table = f32[3584,128]{1,0:T(8,128)} fusion(f32[128]{0:T(128)S(1)} %get-tuple-element.279, f32[128]{0:T(128)S(1)} %get-tuple-element.280, f32[3584]{0:T(1024)S(1)} %get-tuple-element.274), kind=kLoop, calls=%fused_computation.11 | loop fusion | flops 917504 | bytes 1850368 | tf_op jit(solution)/shard_map/cos | solution.py:139
  36.4 5.1 %all-to-all-done = bf16[128,8,256]{2,1,0:T(8,128)(2,1)S(1)} async-done(((bf16[128,8,256]{2,1,0:T(8,128)(2,1)}), bf16[128,8,256]{2,1,0:T(8,128)(2,1)S(1)}, u32[]{:S(2)}, u32[]{:S(2)}) %all-to-all-start) | async-done | bytes 524320 | tf_op jit(solution)/shard_map/all_to_all | solution.py:772
  52.2 8.0 %shard_map.178.refs_0_ = bf16[3584,256]{1,0:T(8,128)(2,1)} custom-call(s32[8]{0:T(128)} %get-tuple-element.277.places, bf16[4,224,1024]{2,1,0:T(8,128)(2,1)} %copy-done.1, bf16[4,224,1024]{2,1,0:T(8,128)(2,1)} %collective-permute-done.7.other.near_other, bf16[1024,256]{1,0:T(8,128)(2,1)} %broadcast_select_fusion.w, f32[1,1024]{1,0:T(1,128)} %bitcast.191, ...), custom_call_target="tpu_custom_call" | custom-call | flops 939524096 | bytes 10485760 | tf_op jit(solution)/shard_map/pallas_call | solution.py:176
  60.2 4.9 %collective-permute-done.8 = bf16[2,192,1024]{2,1,0:T(8,128)(2,1)} collective-permute-done((bf16[2,192,1024]{2,1,0:T(8,128)(2,1)}, bf16[2,192,1024]{2,1,0:T(8,128)(2,1)}, u32[]{:S(2)}, u32[]{:S(2)}) %collective-permute-start.8) | collective-permute-done | bytes 786464 | tf_op jit(solution)/shard_map/ppermute | solution.py:101
  65.1 4.8 %collective-permute-done.2 = bf16[224,1024]{1,0:T(8,128)(2,1)} collective-permute-done((bf16[224,1024]{1,0:T(8,128)(2,1)}, bf16[224,1024]{1,0:T(8,128)(2,1)}, u32[]{:S(2)}, u32[]{:S(2)}) %collective-permute-start.2) | collective-permute-done | bytes 458784 | tf_op jit(solution)/shard_map/ppermute | solution.py:54
  74.9 9.0 %all-to-all-start.1 = ((bf16[128,8,1152]{2,1,0:T(8,128)(2,1)}), bf16[128,8,1152]{2,1,0:T(8,128)(2,1)S(1)}, u32[]{:S(2)}, u32[]{:S(2)}) async-start(bf16[128,8,1152]{2,1,0:T(8,128)(2,1)} %broadcast_in_dim.101), calls=%async_computation.1 | async-start | bytes 4718592 | tf_op jit(solution)/shard_map/all_to_all | solution.py:790
  90.4 8.7 %shard_map.179.qkv_ref = bf16[3584,256]{1,0:T(8,128)(2,1)} custom-call(s32[8]{0:T(128)} %get-tuple-element.278.places, bf16[4,224,1024]{2,1,0:T(8,128)(2,1)} %pad_maximum_fusion.3.mine.far_mine, bf16[4,224,1024]{2,1,0:T(8,128)(2,1)} %collective-permute-done.9.other.far_other, bf16[1024,256]{1,0:T(8,128)(2,1)} %broadcast_select_fusion.w, ...), custom_call_target="tpu_custom_call" | custom-call | flops 939524096 | bytes 10485760 | tf_op jit(solution)/shard_map/pallas_call | solution.py:176
  99.1 19.8 %shard_map.180 = (bf16[16,64,224]{2,1,0:T(8,128)(2,1)}, f32[64,3584]{1,0:T(8,128)}, f32[1,3584]{1,0:T(1,128)}) custom-call(bf16[3584,256]{1,0:T(8,128)(2,1)} %shard_map.179.qkv_ref, s32[1,3584]{1,0:T(1,128)} %compare_select_fusion.begin_ref), custom_call_target="tpu_custom_call" | custom-call | flops 7247757312 | bytes 4194304 | tf_op jit(solution)/shard_map/pallas_call | solution.py:336
  118.9 5.3 %all-to-all-start.2 = ((bf16[16,64,224]{2,1,0:T(8,128)(2,1)}), bf16[16,64,224]{2,1,0:T(8,128)(2,1)S(1)}, u32[]{:S(2)}, u32[]{:S(2)}) async-start(bf16[16,64,224]{2,1,0:T(8,128)(2,1)} %get-tuple-element.142), calls=%async_computation.2 | async-start | bytes 1048576 | tf_op jit(solution)/shard_map/all_to_all | solution.py:805
  124.2 12.8 %collective-permute-done.12 = bf16[240,1024]{1,0:T(8,128)(2,1)} collective-permute-done((bf16[240,1024]{1,0:T(8,128)(2,1)S(1)}, bf16[240,1024]{1,0:T(8,128)(2,1)}, u32[]{:S(2)}, u32[]{:S(2)}) %collective-permute-start.12) | collective-permute-done | bytes 491552 | tf_op jit(solution)/shard_map/ppermute | solution.py:54
  144.9 3.8 shard_map.181
  152.8 18.0 %collective-permute-done.13 = bf16[224,1024]{1,0:T(8,128)(2,1)S(1)} collective-permute-done((bf16[224,1024]{1,0:T(8,128)(2,1)}, bf16[224,1024]{1,0:T(8,128)(2,1)S(1)}, u32[]{:S(2)}, u32[]{:S(2)}) %collective-permute-start.13) | collective-permute-done | bytes 458784 | tf_op jit(solution)/shard_map/ppermute | solution.py:54
  186.3 21.9 %shard_map.182 = (bf16[4,256,1024]{2,1,0:T(8,128)(2,1)}, bf16[4,256,1024]{2,1,0:T(8,128)(2,1)}, bf16[8,224,1024]{2,1,0:T(8,128)(2,1)}, bf16[8,224,1024]{2,1,0:T(...) custom-call(s32[2]{0:T(128)} %pad_add_fusion.own_ref, ...), custom_call_target="tpu_custom_call" | custom-call | flops 15032385536 | bytes 25165824 | tf_op jit(solution)/shard_map/pallas_call | solution.py:567
  223.0 22.1 %shard_map.183 = (bf16[4,256,1024]{2,1,0:T(8,128)(2,1)}, bf16[4,256,1024]{2,1,0:T(8,128)(2,1)}, bf16[8,224,1024]{2,1,0:T(8,128)(2,1)}, bf16[8,224,1024]{2,1,0:T(...) custom-call(s32[2]{0:T(128)} %pad_add_fusion.own_ref, ...), custom_call_target="tpu_custom_call", output_to_operand_aliasing={{2}: (10, {}), {3}: (11, {}), {4}: (12, {}), {5}: (13, {}),... | custom-call | flops 15032385536 | bytes 25165824 | tf_op jit(solution)/shard_map/pallas_call | solution.py:567
  246.1 4.4 collective-permute-done.30
  257.8 15.9 %shard_map.184 = bf16[4,2,2,192,1024]{4,3,2,1,0:T(8,128)(2,1)} custom-call(bf16[2,1152,1024]{2,1,0:T(8,128)(2,1)} %get-tuple-element.183.x_ref, bf16[2,1152,1024]{2,1,0:T(8,128)(2,1)} %get-tuple-element.184.dh_ref, bf16[2,1152,512]{2,1,0:T(8,128)(2,1)} %get-tuple-element.185.act_ref, bf16[2,1152,1024]{2,1,0:T(8,128)(2,1)} %get-tuple-element.186.dy_ref), custom_call_target="tpu_custom_call" | custom-call | flops 8589934592 | bytes 14680064 | tf_op jit(solution)/shard_map/pallas_call | solution.py:623
  273.7 7.6 %collective-permute-done.33 = bf16[256,1024]{1,0:T(8,128)(2,1)S(1)} collective-permute-done((bf16[256,1024]{1,0:T(8,128)(2,1)S(1)}, bf16[256,1024]{1,0:T(8,128)(2,1)S(1)}, u32[]{:S(2)}, u32[]{:S(2)}) %collective-permute-start.33) | collective-permute-done | bytes 524320 | tf_op jit(solution)/shard_map/ppermute | solution.py:54
  285.1 6.1 %fusion.10 = (bf16[2,224,1024]{2,1,0:T(8,128)(2,1)}, bf16[2,224,1024]{2,1,0:T(8,128)(2,1)}, bf16[2,224,1024]{2,1,0:T(8,128)(2,1)}, bf16[2,224,1024]{2,1,0:T(8,128)(2,1)S(1)}) fusion(bf16[2,4,224,1024]{3,2,1,0:T(8,128)(2,1)} %bitcast.51, bf16[2,4,224,1024]{3,2,1,0:T(8,128)(2,1)} %bitcast.172), kind=kLoop, calls=%fused_computation.47 | loop fusion | flops 7340032 | bytes 11010048 | tf_op jit(solution)/shard_map/convert_element_type | solution.py:85
  291.2 5.3 %collective-permute-done.35.crossed = bf16[256,1024]{1,0:T(8,128)(2,1)S(1)} collective-permute-done((bf16[256,1024]{1,0:T(8,128)(2,1)S(1)}, bf16[256,1024]{1,0:T(8,128)(2,1)S(1)}, u32[]{:S(2)}, u32[]{:S(2)}) %collective-permute-start.35) | collective-permute-done | bytes 524320 | tf_op jit(solution)/shard_map/ppermute | solution.py:54
  297.4 5.9 %shard_map.185 = (f32[224,1024]{1,0:T(8,128)}, bf16[224,1024]{1,0:T(8,128)(2,1)}, bf16[32,224]{1,0:T(8,128)(2,1)}, bf16[224,1024]{1,0:T(8,128)(2,1)}, bf16[16,64,224]{2,1,0:T(8,128)(2,1)}) custom-call(bf16[256,1024]{1,0:T(8,128)(2,1)} %get-tuple-element.175.t0, bf16[256,1024]{1,0:T(8,128)(2,1)} %copy-done.16, bf16[256,1024]{1,0:T(8,128)(2,1)} %copy-done.17, ...), custom_call_target="tpu_custom_call" | custom-call | flops 469762048 | bytes 8388608 | tf_op jit(solution)/shard_map/pallas_call | solution.py:694
  303.2 4.8 %all-to-all-start.3 = ((bf16[16,64,224]{2,1,0:T(8,128)(2,1)}), bf16[16,64,224]{2,1,0:T(8,128)(2,1)S(1)}, u32[]{:S(2)}, u32[]{:S(2)}) async-start(bf16[16,64,224]{2,1,0:T(8,128)(2,1)} %get-tuple-element.195), calls=%async_computation.3 | async-start | bytes 1048576 | tf_op jit(solution)/shard_map/all_to_all | solution.py:848
  308.0 3.9 shard_map.186
  312.0 8.4 %all-to-all-done.3.g_ref = bf16[16,64,224]{2,1,0:T(8,128)(2,1)S(1)} async-done(((bf16[16,64,224]{2,1,0:T(8,128)(2,1)}), bf16[16,64,224]{2,1,0:T(8,128)(2,1)S(1)}, u32[]{:S(2)}, u32[]{:S(2)}) %all-to-all-start.3) | async-done | bytes 458784 | tf_op jit(solution)/shard_map/all_to_all | solution.py:848
  321.2 4.7 %all-to-all-start.4 = ((bf16[8,128,1152]{2,1,0:T(8,128)(2,1)}), bf16[8,128,1152]{2,1,0:T(8,128)(2,1)S(1)}, u32[]{:S(2)}, u32[]{:S(2)}) async-start(bf16[8,128,1152]{2,1,0:T(8,128)(2,1)} %shard_map.186), calls=%async_computation.4 | async-start | bytes 4718592 | tf_op jit(solution)/shard_map/all_to_all | solution.py:855
  328.6 31.1 %shard_map.187.first.second = bf16[3584,256]{1,0:T(8,128)(2,1)} custom-call(bf16[3584,256]{1,0:T(8,128)(2,1)} %shard_map.179.qkv_ref, bf16[16,64,224]{2,1,0:T(8,128)(2,1)} %copy-done.21, f32[64,3584]{1,0:T(8,128)} %get-tuple-element.205.ot_ref, f32[1,3584]{1,0:T(1,128)} %get-tuple-element.206.lse_ref, s32[1,3584]{1,0:T(1,128)} %compare_select_fusion.begin_ref, ...), custom_call_target="tpu_custom_call" | custom-call | flops 18119393280 | bytes 8388608 | tf_op jit(solution)/shard_map/pallas_call | solution.py:416
  359.7 10.8 %shard_map.188 = bf16[1024,256]{1,0:T(8,128)(2,1)} custom-call(s32[16]{0:T(128)} %copy-done.37, bf16[4,224,1024]{2,1,0:T(8,128)(2,1)} %copy-done.1, bf16[4,224,1024]{2,1,0:T(8,128)(2,1)} %collective-permute-done.7.other.near_other, bf16[4,224,1024]{2,1,0:T(8,128)(2,1)} %pad_maximum_fusion.3.mine.far_mine, ...), custom_call_target="tpu_custom_call" | custom-call | flops 1879048192 | bytes 10485760 | tf_op jit(solution)/shard_map/pallas_call | solution.py:251
  371.6 5.7 %shard_map.189 = (bf16[4,240,1024]{2,1,0:T(8,128)(2,1)}, bf16[4,240,1024]{2,1,0:T(8,128)(2,1)}) custom-call(s32[8]{0:T(128)} %get-tuple-element.278.places, bf16[3584,256]{1,0:T(8,128)(2,1)} %shard_map.187.first.second, bf16[3584,256]{1,0:T(8,128)(2,1)} %shard_map.187.first.second, bf16[1024,256]{1,0:T(8,128)(2,1)} %broadcast_select_fusion.w, ...), custom_call_target="tpu_custom_call" | custom-call | flops 939524096 | bytes 5242880 | tf_op jit(solution)/shard_map/pallas_call | solution.py:207
  377.3 5.9 %shard_map.190 = (bf16[4,240,1024]{2,1,0:T(8,128)(2,1)}, bf16[4,240,1024]{2,1,0:T(8,128)(2,1)}) custom-call(s32[8]{0:T(128)} %get-tuple-element.277.places, bf16[3584,256]{1,0:T(8,128)(2,1)} %shard_map.187.first.second, bf16[3584,256]{1,0:T(8,128)(2,1)} %shard_map.187.first.second, bf16[1024,256]{1,0:T(8,128)(2,1)} %broadcast_select_fusion.w, ...), custom_call_target="tpu_custom_call" | custom-call | flops 939524096 | bytes 5242880 | tf_op jit(solution)/shard_map/pallas_call | solution.py:207
  402.3 8.5 %all-to-all-start.5 = ((bf16[128,8,256]{2,1,0:T(8,128)(2,1)}), bf16[128,8,256]{2,1,0:T(8,128)(2,1)S(1)}, u32[]{:S(2)}, u32[]{:S(2)}) async-start(bf16[128,8,256]{2,1,0:T(8,128)(2,1)} %bitcast.69), calls=%async_computation.6 | async-start | bytes 1048576 | tf_op jit(solution)/shard_map/all_to_all | solution.py:871
  413.8 6.6 %collective-permute-done.43 = bf16[240,1024]{1,0:T(8,128)(2,1)} collective-permute-done((bf16[240,1024]{1,0:T(8,128)(2,1)}, bf16[240,1024]{1,0:T(8,128)(2,1)}, u32[]{:S(2)}, u32[]{:S(2)}) %collective-permute-start.43) | collective-permute-done | bytes 491552 | tf_op jit(solution)/shard_map/ppermute | solution.py:54
  437.0 7.9 %collective-permute-done.47 = bf16[240,1024]{1,0:T(8,128)(2,1)S(1)} collective-permute-done((bf16[240,1024]{1,0:T(8,128)(2,1)}, bf16[240,1024]{1,0:T(8,128)(2,1)S(1)}, u32[]{:S(2)}, u32[]{:S(2)}) %collective-permute-start.47) | collective-permute-done | bytes 491552 | tf_op jit(solution)/shard_map/ppermute | solution.py:54
  (273 shorter events, 143.0 us)
Async XLA Ops:
  7.2 35.1 %collective-permute-start = (bf16[224,1024]{1,0:T(8,128)(2,1)}, bf16[224,1024]{1,0:T(8,128)(2,1)S(1)}, u32[]{:S(2)}, u32[]{:S(2)}) collective-permute-start(bf16[224,1024]{1,0:T(8,128)(2,1)} %bitcast.165), channel_id=1, source_target_pairs={{0,64},{8,72},{16,80},{24,88},{32,96},{40,104},{48,112},{56,120},{... | collective-permute-start | bytes 1376264 | tf_op jit(solution)/shard_map/ppermute | solution.py:54
  10.4 32.0 %collective-permute-start.4 = (bf16[224,1024]{1,0:T(8,128)(2,1)}, bf16[224,1024]{1,0:T(8,128)(2,1)S(1)}, u32[]{:S(2)}, u32[]{:S(2)}) collective-permute-start(bf16[224,1024]{1,0:T(8,128)(2,1)} %bitcast.166), channel_id=1, source_target_pairs={{0,16},{8,24},{16,32},{24,40},{32,48},{40,56},{48,0},{56,8},{64,80... | collective-permute-start | bytes 1376264 | tf_op jit(solution)/shard_map/ppermute | solution.py:54
  12.3 30.0 %collective-permute-start.5 = (bf16[224,1024]{1,0:T(8,128)(2,1)}, bf16[224,1024]{1,0:T(8,128)(2,1)S(1)}, u32[]{:S(2)}, u32[]{:S(2)}) collective-permute-start(bf16[224,1024]{1,0:T(8,128)(2,1)} %bitcast.167), channel_id=1, source_target_pairs={{0,48},{8,56},{16,0},{24,8},{32,16},{40,24},{48,32},{56,40},{64,11... | collective-permute-start | bytes 1376264 | tf_op jit(solution)/shard_map/ppermute | solution.py:54
  14.4 27.9 %collective-permute-start.6 = (bf16[224,1024]{1,0:T(8,128)(2,1)}, bf16[224,1024]{1,0:T(8,128)(2,1)}, u32[]{:S(2)}, u32[]{:S(2)}) collective-permute-start(bf16[224,1024]{1,0:T(8,128)(2,1)} %bitcast.168), channel_id=1, source_target_pairs={{0,32},{8,40},{16,48},{24,56},{32,0},{40,8},{48,16},{56,24},{64,96... | collective-permute-start | bytes 1376264 | tf_op jit(solution)/shard_map/ppermute | solution.py:54
  26.6 159.8 %all-gather.5.cloned.1.call-start = ((), (), s32[]{:S(2)}) async-start(), calls=%async_computation.8 | async-start | bytes 3932160 | tf_op jit(solution)/shard_map/all_gather | solution.py:782
  74.9 43.9 %all-to-all-start.1 = ((bf16[128,8,1152]{2,1,0:T(8,128)(2,1)}), bf16[128,8,1152]{2,1,0:T(8,128)(2,1)S(1)}, u32[]{:S(2)}, u32[]{:S(2)}) async-start(bf16[128,8,1152]{2,1,0:T(8,128)(2,1)} %broadcast_in_dim.101), calls=%async_computation.1 | async-start | bytes 4718592 | tf_op jit(solution)/shard_map/all_to_all | solution.py:790
  83.9 102.4 %all-gather.7.cloned.1.call-start = ((), (), s32[]{:S(2)}) async-start(), calls=%async_computation.9 | async-start | bytes 3932160 | tf_op jit(solution)/shard_map/all_gather | solution.py:782
  85.3 39.0 %collective-permute-start.10 = (bf16[240,1024]{1,0:T(8,128)(2,1)S(1)}, bf16[240,1024]{1,0:T(8,128)(2,1)}, u32[]{:S(2)}, u32[]{:S(2)}) collective-permute-start(bf16[240,1024]{1,0:T(8,128)(2,1)S(1)} %fusion.21), channel_id=1, source_target_pairs={{0,16},{8,24},{16,32},{24,40},{32,48},{40,56},{48,0},{56,8},{64,80... | collective-permute-start | bytes 1474568 | tf_op jit(solution)/shard_map/ppermute | solution.py:54
  86.4 37.9 %collective-permute-start.11 = (bf16[240,1024]{1,0:T(8,128)(2,1)S(1)}, bf16[240,1024]{1,0:T(8,128)(2,1)}, u32[]{:S(2)}, u32[]{:S(2)}) collective-permute-start(bf16[240,1024]{1,0:T(8,128)(2,1)S(1)} %fusion.21), channel_id=1, source_target_pairs={{0,48},{8,56},{16,0},{24,8},{32,16},{40,24},{48,32},{56,40},{64,11... | collective-permute-start | bytes 1474568 | tf_op jit(solution)/shard_map/ppermute | solution.py:54
  88.5 48.5 %collective-permute-start.12 = (bf16[240,1024]{1,0:T(8,128)(2,1)S(1)}, bf16[240,1024]{1,0:T(8,128)(2,1)}, u32[]{:S(2)}, u32[]{:S(2)}) collective-permute-start(bf16[240,1024]{1,0:T(8,128)(2,1)S(1)} %fusion.21), channel_id=1, source_target_pairs={{0,32},{8,40},{16,48},{24,56},{32,0},{40,8},{48,16},{56,24},{64,96... | collective-permute-start | bytes 1474568 | tf_op jit(solution)/shard_map/ppermute | solution.py:54
  124.2 259.1 %reduce-scatter.2.cloned.1.call-start = ((), (), s32[]{:S(2)}) async-start(), calls=%async_computation.7 | async-start | bytes 7864320 | tf_op jit(solution)/shard_map/reduce_scatter | solution.py:841
  141.3 31.5 %collective-permute-start.21 = (bf16[352,1024]{1,0:T(8,128)(2,1)S(1)}, bf16[352,1024]{1,0:T(8,128)(2,1)}, u32[]{:S(2)}, u32[]{:S(2)}) collective-permute-start(bf16[352,1024]{1,0:T(8,128)(2,1)S(1)} %slice.276), channel_id=1, source_target_pairs={{0,64},{8,72},{16,80},{24,88},{32,96},{40,104},{48,112},{56,120},{... | collective-permute-start | bytes 2162696 | tf_op jit(solution)/shard_map/ppermute | solution.py:54
  178.8 31.5 %collective-permute-start.22 = (bf16[608,1024]{1,0:T(8,128)(2,1)}, bf16[608,1024]{1,0:T(8,128)(2,1)S(1)}, u32[]{:S(2)}, u32[]{:S(2)}) collective-permute-start(bf16[608,1024]{1,0:T(8,128)(2,1)} %slice.215), channel_id=1, source_target_pairs={{0,64},{8,72},{16,80},{24,88},{32,96},{40,104},{48,112},{56,120},{... | collective-permute-start | bytes 3735560 | tf_op jit(solution)/shard_map/ppermute | solution.py:54
  181.5 30.2 %collective-permute-start.14 = (bf16[224,1024]{1,0:T(8,128)(2,1)}, bf16[224,1024]{1,0:T(8,128)(2,1)}, u32[]{:S(2)}, u32[]{:S(2)}) collective-permute-start(bf16[224,1024]{1,0:T(8,128)(2,1)} %copy-done.27), channel_id=1, source_target_pairs={{0,16},{8,24},{16,32},{24,40},{32,48},{40,56},{48,0},{56,8},{64,80... | collective-permute-start | bytes 1376264 | tf_op jit(solution)/shard_map/ppermute | solution.py:54
  182.3 29.3 %collective-permute-start.15 = (bf16[224,1024]{1,0:T(8,128)(2,1)}, bf16[224,1024]{1,0:T(8,128)(2,1)}, u32[]{:S(2)}, u32[]{:S(2)}) collective-permute-start(bf16[224,1024]{1,0:T(8,128)(2,1)} %copy-done.27), channel_id=1, source_target_pairs={{0,48},{8,56},{16,0},{24,8},{32,16},{40,24},{48,32},{56,40},{64,11... | collective-permute-start | bytes 1376264 | tf_op jit(solution)/shard_map/ppermute | solution.py:54
  184.7 27.0 %collective-permute-start.16 = (bf16[224,1024]{1,0:T(8,128)(2,1)}, bf16[224,1024]{1,0:T(8,128)(2,1)S(1)}, u32[]{:S(2)}, u32[]{:S(2)}) collective-permute-start(bf16[224,1024]{1,0:T(8,128)(2,1)} %copy-done.27), channel_id=1, source_target_pairs={{0,32},{8,40},{16,48},{24,56},{32,0},{40,8},{48,16},{56,24},{64,96... | collective-permute-start | bytes 1376264 | tf_op jit(solution)/shard_map/ppermute | solution.py:54
  216.6 28.5 %collective-permute-start.27 = (bf16[256,1024]{1,0:T(8,128)(2,1)}, bf16[256,1024]{1,0:T(8,128)(2,1)S(1)}, u32[]{:S(2)}, u32[]{:S(2)}) collective-permute-start(bf16[256,1024]{1,0:T(8,128)(2,1)} %get-tuple-element.261), channel_id=1, source_target_pairs={{0,48},{8,56},{16,0},{24,8},{32,16},{40,24},{48,32},{56,40},{64,11... | collective-permute-start | bytes 1572872 | tf_op jit(solution)/shard_map/ppermute | solution.py:54
  219.5 26.4 %collective-permute-start.28 = (bf16[256,1024]{1,0:T(8,128)(2,1)}, bf16[256,1024]{1,0:T(8,128)(2,1)S(1)}, u32[]{:S(2)}, u32[]{:S(2)}) collective-permute-start(bf16[256,1024]{1,0:T(8,128)(2,1)} %get-tuple-element.260), channel_id=1, source_target_pairs={{0,16},{8,24},{16,32},{24,40},{32,48},{40,56},{48,0},{56,8},{64,80... | collective-permute-start | bytes 1572872 | tf_op jit(solution)/shard_map/ppermute | solution.py:54
  219.5 26.4 %collective-permute-start.29 = (bf16[256,1024]{1,0:T(8,128)(2,1)S(1)}, bf16[256,1024]{1,0:T(8,128)(2,1)S(1)}, u32[]{:S(2)}, u32[]{:S(2)}) collective-permute-start(bf16[256,1024]{1,0:T(8,128)(2,1)S(1)} %get-tuple-element.259), channel_id=1, source_target_pairs={{0,32},{8,40},{16,48},{24,56},{32,0},{40,8},{48,16},{56,24},{64,96... | collective-permute-start | bytes 1572872 | tf_op jit(solution)/shard_map/ppermute | solution.py:54
  250.4 30.8 %collective-permute-start.34 = (bf16[8,224,1024]{2,1,0:T(8,128)(2,1)}, bf16[8,224,1024]{2,1,0:T(8,128)(2,1)}, u32[]{:S(2)}, u32[]{:S(2)}) collective-permute-start(bf16[8,224,1024]{2,1,0:T(8,128)(2,1)} %get-tuple-element.187), channel_id=1, source_target_pairs={{0,8},{8,0},{16,24},{24,16},{32,40},{40,32},{48,56},{56,48},{64,72... | collective-permute-start | bytes 11010056 | tf_op jit(solution)/shard_map/ppermute | solution.py:58
  255.9 25.3 %collective-permute-start.33 = (bf16[256,1024]{1,0:T(8,128)(2,1)S(1)}, bf16[256,1024]{1,0:T(8,128)(2,1)S(1)}, u32[]{:S(2)}, u32[]{:S(2)}) collective-permute-start(bf16[256,1024]{1,0:T(8,128)(2,1)S(1)} %get-tuple-element.255), channel_id=1, source_target_pairs={{0,32},{8,40},{16,48},{24,56},{32,0},{40,8},{48,16},{56,24},{64,96... | collective-permute-start | bytes 1572872 | tf_op jit(solution)/shard_map/ppermute | solution.py:54
  321.2 49.3 %all-to-all-start.4 = ((bf16[8,128,1152]{2,1,0:T(8,128)(2,1)}), bf16[8,128,1152]{2,1,0:T(8,128)(2,1)S(1)}, u32[]{:S(2)}, u32[]{:S(2)}) async-start(bf16[8,128,1152]{2,1,0:T(8,128)(2,1)} %shard_map.186), calls=%async_computation.4 | async-start | bytes 4718592 | tf_op jit(solution)/shard_map/all_to_all | solution.py:855
  325.9 57.3 %collective-permute-start.37 = (bf16[2,224,1024]{2,1,0:T(8,128)(2,1)}, bf16[2,224,1024]{2,1,0:T(8,128)(2,1)}, u32[]{:S(2)}, u32[]{:S(2)}) collective-permute-start(bf16[2,224,1024]{2,1,0:T(8,128)(2,1)} %get-tuple-element.214), channel_id=1, source_target_pairs={{0,48},{8,56},{16,0},{24,8},{32,16},{40,24},{48,32},{56,40},{64,11... | collective-permute-start | bytes 2752520 | tf_op jit(solution)/shard_map/ppermute | solution.py:54
  326.9 56.3 %collective-permute-start.38 = (bf16[2,224,1024]{2,1,0:T(8,128)(2,1)}, bf16[2,224,1024]{2,1,0:T(8,128)(2,1)}, u32[]{:S(2)}, u32[]{:S(2)}) collective-permute-start(bf16[2,224,1024]{2,1,0:T(8,128)(2,1)} %get-tuple-element.215), channel_id=1, source_target_pairs={{0,16},{8,24},{16,32},{24,40},{32,48},{40,56},{48,0},{56,8},{64,80... | collective-permute-start | bytes 2752520 | tf_op jit(solution)/shard_map/ppermute | solution.py:54
  328.0 55.3 %collective-permute-start.39 = (bf16[2,224,1024]{2,1,0:T(8,128)(2,1)}, bf16[2,224,1024]{2,1,0:T(8,128)(2,1)}, u32[]{:S(2)}, u32[]{:S(2)}) collective-permute-start(bf16[2,224,1024]{2,1,0:T(8,128)(2,1)} %get-tuple-element.216), channel_id=1, source_target_pairs={{0,32},{8,40},{16,48},{24,56},{32,0},{40,8},{48,16},{56,24},{64,96... | collective-permute-start | bytes 2752520 | tf_op jit(solution)/shard_map/ppermute | solution.py:54
  393.1 27.2 %collective-permute-start.43 = (bf16[240,1024]{1,0:T(8,128)(2,1)}, bf16[240,1024]{1,0:T(8,128)(2,1)}, u32[]{:S(2)}, u32[]{:S(2)}) collective-permute-start(bf16[240,1024]{1,0:T(8,128)(2,1)} %get-tuple-element.233), channel_id=1, source_target_pairs={{0,16},{8,24},{16,32},{24,40},{32,48},{40,56},{48,0},{56,8},{64,80... | collective-permute-start | bytes 1474568 | tf_op jit(solution)/shard_map/ppermute | solution.py:54
  393.5 27.0 %collective-permute-start.44 = (bf16[240,1024]{1,0:T(8,128)(2,1)}, bf16[240,1024]{1,0:T(8,128)(2,1)}, u32[]{:S(2)}, u32[]{:S(2)}) collective-permute-start(bf16[240,1024]{1,0:T(8,128)(2,1)} %get-tuple-element.234), channel_id=1, source_target_pairs={{0,32},{8,40},{16,48},{24,56},{32,0},{40,8},{48,16},{56,24},{64,96... | collective-permute-start | bytes 1474568 | tf_op jit(solution)/shard_map/ppermute | solution.py:54
  396.9 36.8 %collective-permute-start.49 = (bf16[2,192,1024]{2,1,0:T(8,128)(2,1)}, bf16[2,192,1024]{2,1,0:T(8,128)(2,1)}, u32[]{:S(2)}, u32[]{:S(2)}) collective-permute-start(bf16[2,192,1024]{2,1,0:T(8,128)(2,1)} %dynamic-slice_bitcast_fusion), channel_id=1, source_target_pairs={{0,1},{1,0},{2,3},{3,2},{4,5},{5,4},{6,7},{7,6},{8,9},{9,8},{10,11... | collective-permute-start | bytes 2359304 | tf_op jit(solution)/shard_map/ppermute | solution.py:101
  401.3 27.2 %collective-permute-start.41 = (bf16[224,1024]{1,0:T(8,128)(2,1)}, bf16[224,1024]{1,0:T(8,128)(2,1)}, u32[]{:S(2)}, u32[]{:S(2)}) collective-permute-start(bf16[224,1024]{1,0:T(8,128)(2,1)} %fusion.30), channel_id=1, source_target_pairs={{0,64},{8,72},{16,80},{24,88},{32,96},{40,104},{48,112},{56,120},{... | collective-permute-start | bytes 1376264 | tf_op jit(solution)/shard_map/ppermute | solution.py:54
  402.3 43.4 %all-to-all-start.5 = ((bf16[128,8,256]{2,1,0:T(8,128)(2,1)}), bf16[128,8,256]{2,1,0:T(8,128)(2,1)S(1)}, u32[]{:S(2)}, u32[]{:S(2)}) async-start(bf16[128,8,256]{2,1,0:T(8,128)(2,1)} %bitcast.69), calls=%async_computation.6 | async-start | bytes 1048576 | tf_op jit(solution)/shard_map/all_to_all | solution.py:871
  410.9 26.1 %collective-permute-start.46 = (bf16[240,1024]{1,0:T(8,128)(2,1)}, bf16[240,1024]{1,0:T(8,128)(2,1)S(1)}, u32[]{:S(2)}, u32[]{:S(2)}) collective-permute-start(bf16[240,1024]{1,0:T(8,128)(2,1)} %get-tuple-element.236), channel_id=1, source_target_pairs={{0,48},{8,56},{16,0},{24,8},{32,16},{40,24},{48,32},{56,40},{64,11... | collective-permute-start | bytes 1474568 | tf_op jit(solution)/shard_map/ppermute | solution.py:54
  420.5 25.2 %collective-permute-start.48 = (bf16[240,1024]{1,0:T(8,128)(2,1)}, bf16[240,1024]{1,0:T(8,128)(2,1)}, u32[]{:S(2)}, u32[]{:S(2)}) collective-permute-start(bf16[240,1024]{1,0:T(8,128)(2,1)} %get-tuple-element.238), channel_id=1, source_target_pairs={{0,32},{8,40},{16,48},{24,56},{32,0},{40,8},{48,16},{56,24},{64,96... | collective-permute-start | bytes 1474568 | tf_op jit(solution)/shard_map/ppermute | solution.py:54
  (71 other events, 738.8 us)
Sparse Core Ops, SparseCore 0:
  29.1 40.6 all-gather.4
  86.4 50.9 all-gather.6
  281.4 89.0 reduce-scatter.1

commit v17 on v16

--- a/solution.py
+++ b/solution.py
@@ -854,20 +854,22 @@
 
     shared_grads = lax.all_to_all(shared_grads, "wshard", 0, 0, tiled=True)
     projected_grad = attend_back(qkv, head_grad, attended_t, lse, begin, table)
-    grad_head = head_weight_grad(places, rows_near, rows_far, gain_attn, projected_grad)
-    shared_grads, grad_head, projected_grad = tie(shared_grads, grad_head, projected_grad)
+    shared_grads, moved_terms = tie(shared_grads, moved_terms)
     shared_grads = jnp.sum(shared_grads.astype(f32), axis=0)
+    moved_crossed = add_low(*[t[1] for t in moved_terms])
+    shared_grads, moved_crossed = tie(shared_grads, moved_crossed)
+    moved_crossed = send(moved_crossed, 1, 0)
     far_part = project_back(places[8:], projected_grad, head_weights, shared_grads)
     near_part = project_back(places[:8], projected_grad, head_weights, shared_grads)
     far_parts = chip_parts(far_part[0], swap_cores(far_part[1]))
-    near_part, moved_terms, expert_grads = tie(near_part, moved_terms, expert_grads)
+    near_part, expert_grads = tie(near_part, expert_grads)
     near_parts = chip_parts(near_part[0], swap_cores(near_part[1]))
-    far_parts, near_parts, grad_head, moved_terms, expert_grads = tie(
-        far_parts, near_parts, grad_head, moved_terms, expert_grads
-    )
-    far_terms = send_along_z(far_parts)
+    far_parts, near_parts, projected_grad, expert_grads = tie(
+        far_parts, near_parts, projected_grad, expert_grads
+    )
+    far_terms, moved_crossed = tie(send_along_z(far_parts), moved_crossed)
     near_terms = send_along_z(near_parts)
-    moved_crossed = send(add_low(*[t[1] for t in moved_terms]), 1, 0)
+    grad_head = head_weight_grad(places, rows_near, rows_far, gain_attn, projected_grad)
     grad_heads = lax.all_to_all(grad_head.reshape(128, 8, 256), BOTH, 0, 0, tiled=True)
     crossed = send(add_low(*far_terms), 1, 0)
     crossed, near_terms, grad_heads = tie(crossed, near_terms, grad_heads)

time: 469 us -> 475 us (1.013)
  waiting for transfers between devices: 99 us -> 106 us
    ppermute x37, waiting for transfers between devices: 72.4 us -> 79.7 us  [send(): return lax.ppermute(rows, 'seq', shift_perm(a, b))]
  transfers between devices with their start and end apart: 59 -> 59, of which waited for: 19 -> 19; matrix products, arithmetic and copies ran while one was open for 14% -> 14% of each run, Pallas kernels for 36% -> 35%
where the time goes in v17:
time: 475 us; the launch traced here: 466 us
  Pallas kernels  163 us (34%)
  waiting for transfers between devices  106 us (22%)
  starting transfers between devices  103 us (22%)
  other arithmetic  56 us (12%)
  local copies, waits for them, and re-layouts  23.1 us (5%)
  between operations  14.8 us (3%)
    ppermute x37, waiting for transfers between devices, send(): return lax.ppermute(rows, 'seq', shift_perm(a, b))  79.7 us
    ppermute x37, starting transfers between devices, send(): return lax.ppermute(rows, 'seq', shift_perm(a, b))  58.5 us
    pallas_call x2, Pallas kernels, run_experts(): pl.pallas_call(experts_kernel, grid_spec=pltpu.PrefetchScalarGridSpec(num...  44 us
    pallas_call x1, Pallas kernels, attend_back(): pl.pallas_call(attend_back_kernel, grid=(GROUP // BLOCK,), in_specs=[whol...  31.1 us
    pallas_call x1, Pallas kernels, attend(): pl.pallas_call(attend_kernel, grid=(GROUP // BLOCK,), in_specs=[whole(GRO...  19.8 us
    convert_element_type x7, other arithmetic, add_low(): return sum([t.astype(f32) for t in terms]).astype(bf16)  19.2 us
    pallas_call x2, Pallas kernels, project(): pl.pallas_call(project_kernel, grid_spec=pltpu.PrefetchScalarGridSpec(num...  16.7 us
    pallas_call x1, Pallas kernels, expert_weight_grads(): pl.pallas_call(expert_grads_kernel, grid=(2, 4), in_specs=[pl.BlockSpec((...  15.9 us
  transfers between devices with their start and end apart: 59, of which 19 were waited for; matrix products, arithmetic and copies ran while one was open for 14% of the time, Pallas kernels for 35%

profile of v17, /device:TPU:0, one launch (start us, length us, event | category | flops | bytes accessed | tf_op | source)
XLA Modules:
  0.0 466.1 jit_solution(14114461858006578014)
XLA Ops:
  19.8 6.8 %all-to-all-start = ((bf16[128,8,256]{2,1,0:T(8,128)(2,1)}), bf16[128,8,256]{2,1,0:T(8,128)(2,1)S(1)}, u32[]{:S(2)}, u32[]{:S(2)}) async-start(bf16[128,8,256]{2,1,0:T(8,128)(2,1)} %bitcast.9), calls=%async_computation | async-start | bytes 1048576 | tf_op jit(solution)/shard_map/all_to_all | solution.py:772
  28.7 7.7 %subtract_cosine_fusion.table = f32[3584,128]{1,0:T(8,128)} fusion(f32[128]{0:T(128)S(1)} %get-tuple-element.281, f32[128]{0:T(128)S(1)} %get-tuple-element.282, f32[3584]{0:T(1024)S(1)} %get-tuple-element.276), kind=kLoop, calls=%fused_computation.11 | loop fusion | flops 917504 | bytes 1850368 | tf_op jit(solution)/shard_map/cos | solution.py:139
  36.4 5.1 %all-to-all-done = bf16[128,8,256]{2,1,0:T(8,128)(2,1)S(1)} async-done(((bf16[128,8,256]{2,1,0:T(8,128)(2,1)}), bf16[128,8,256]{2,1,0:T(8,128)(2,1)S(1)}, u32[]{:S(2)}, u32[]{:S(2)}) %all-to-all-start) | async-done | bytes 524320 | tf_op jit(solution)/shard_map/all_to_all | solution.py:772
  52.2 8.0 %shard_map.178.refs_0_ = bf16[3584,256]{1,0:T(8,128)(2,1)} custom-call(s32[8]{0:T(128)} %get-tuple-element.279.places, bf16[4,224,1024]{2,1,0:T(8,128)(2,1)} %copy-done.1, bf16[4,224,1024]{2,1,0:T(8,128)(2,1)} %collective-permute-done.7.other.near_other, bf16[1024,256]{1,0:T(8,128)(2,1)} %broadcast_select_fusion.w, f32[1,1024]{1,0:T(1,128)} %bitcast.192, ...), custom_call_target="tpu_custom_call" | custom-call | flops 939524096 | bytes 10485760 | tf_op jit(solution)/shard_map/pallas_call | solution.py:176
  60.2 4.9 %collective-permute-done.8 = bf16[2,192,1024]{2,1,0:T(8,128)(2,1)} collective-permute-done((bf16[2,192,1024]{2,1,0:T(8,128)(2,1)}, bf16[2,192,1024]{2,1,0:T(8,128)(2,1)}, u32[]{:S(2)}, u32[]{:S(2)}) %collective-permute-start.8) | collective-permute-done | bytes 786464 | tf_op jit(solution)/shard_map/ppermute | solution.py:101
  65.1 4.8 %collective-permute-done.2 = bf16[224,1024]{1,0:T(8,128)(2,1)} collective-permute-done((bf16[224,1024]{1,0:T(8,128)(2,1)}, bf16[224,1024]{1,0:T(8,128)(2,1)}, u32[]{:S(2)}, u32[]{:S(2)}) %collective-permute-start.2) | collective-permute-done | bytes 458784 | tf_op jit(solution)/shard_map/ppermute | solution.py:54
  74.9 9.0 %all-to-all-start.1 = ((bf16[128,8,1152]{2,1,0:T(8,128)(2,1)}), bf16[128,8,1152]{2,1,0:T(8,128)(2,1)S(1)}, u32[]{:S(2)}, u32[]{:S(2)}) async-start(bf16[128,8,1152]{2,1,0:T(8,128)(2,1)} %broadcast_in_dim.101), calls=%async_computation.1 | async-start | bytes 4718592 | tf_op jit(solution)/shard_map/all_to_all | solution.py:790
  90.3 8.7 %shard_map.179.qkv_ref = bf16[3584,256]{1,0:T(8,128)(2,1)} custom-call(s32[8]{0:T(128)} %get-tuple-element.280.places, bf16[4,224,1024]{2,1,0:T(8,128)(2,1)} %pad_maximum_fusion.3.mine.far_mine, bf16[4,224,1024]{2,1,0:T(8,128)(2,1)} %collective-permute-done.9.other.far_other, bf16[1024,256]{1,0:T(8,128)(2,1)} %broadcast_select_fusion.w, ...), custom_call_target="tpu_custom_call" | custom-call | flops 939524096 | bytes 10485760 | tf_op jit(solution)/shard_map/pallas_call | solution.py:176
  99.1 19.8 %shard_map.180 = (bf16[16,64,224]{2,1,0:T(8,128)(2,1)}, f32[64,3584]{1,0:T(8,128)}, f32[1,3584]{1,0:T(1,128)}) custom-call(bf16[3584,256]{1,0:T(8,128)(2,1)} %shard_map.179.qkv_ref, s32[1,3584]{1,0:T(1,128)} %compare_select_fusion.begin_ref), custom_call_target="tpu_custom_call" | custom-call | flops 7247757312 | bytes 4194304 | tf_op jit(solution)/shard_map/pallas_call | solution.py:336
  118.9 5.3 %all-to-all-start.2 = ((bf16[16,64,224]{2,1,0:T(8,128)(2,1)}), bf16[16,64,224]{2,1,0:T(8,128)(2,1)S(1)}, u32[]{:S(2)}, u32[]{:S(2)}) async-start(bf16[16,64,224]{2,1,0:T(8,128)(2,1)} %get-tuple-element.143), calls=%async_computation.2 | async-start | bytes 1048576 | tf_op jit(solution)/shard_map/all_to_all | solution.py:805
  124.3 12.7 %collective-permute-done.12 = bf16[240,1024]{1,0:T(8,128)(2,1)} collective-permute-done((bf16[240,1024]{1,0:T(8,128)(2,1)S(1)}, bf16[240,1024]{1,0:T(8,128)(2,1)}, u32[]{:S(2)}, u32[]{:S(2)}) %collective-permute-start.12) | collective-permute-done | bytes 491552 | tf_op jit(solution)/shard_map/ppermute | solution.py:54
  144.9 3.8 shard_map.181
  152.8 18.0 %collective-permute-done.13 = bf16[224,1024]{1,0:T(8,128)(2,1)S(1)} collective-permute-done((bf16[224,1024]{1,0:T(8,128)(2,1)}, bf16[224,1024]{1,0:T(8,128)(2,1)S(1)}, u32[]{:S(2)}, u32[]{:S(2)}) %collective-permute-start.13) | collective-permute-done | bytes 458784 | tf_op jit(solution)/shard_map/ppermute | solution.py:54
  186.3 21.9 %shard_map.182 = (bf16[4,256,1024]{2,1,0:T(8,128)(2,1)}, bf16[4,256,1024]{2,1,0:T(8,128)(2,1)}, bf16[8,224,1024]{2,1,0:T(8,128)(2,1)}, bf16[8,224,1024]{2,1,0:T(...) custom-call(s32[2]{0:T(128)} %pad_add_fusion.own_ref, ...), custom_call_target="tpu_custom_call" | custom-call | flops 15032385536 | bytes 25165824 | tf_op jit(solution)/shard_map/pallas_call | solution.py:567
  222.9 22.1 %shard_map.183 = (bf16[4,256,1024]{2,1,0:T(8,128)(2,1)}, bf16[4,256,1024]{2,1,0:T(8,128)(2,1)}, bf16[8,224,1024]{2,1,0:T(8,128)(2,1)}, bf16[8,224,1024]{2,1,0:T(...) custom-call(s32[2]{0:T(128)} %pad_add_fusion.own_ref, ...), custom_call_target="tpu_custom_call", output_to_operand_aliasing={{2}: (10, {}), {3}: (11, {}), {4}: (12, {}), {5}: (13, {}),... | custom-call | flops 15032385536 | bytes 25165824 | tf_op jit(solution)/shard_map/pallas_call | solution.py:567
  246.0 4.4 collective-permute-done.30
  257.8 15.9 %shard_map.184 = bf16[4,2,2,192,1024]{4,3,2,1,0:T(8,128)(2,1)} custom-call(bf16[2,1152,1024]{2,1,0:T(8,128)(2,1)} %get-tuple-element.184.x_ref, bf16[2,1152,1024]{2,1,0:T(8,128)(2,1)} %get-tuple-element.185.dh_ref, bf16[2,1152,512]{2,1,0:T(8,128)(2,1)} %get-tuple-element.186.act_ref, bf16[2,1152,1024]{2,1,0:T(8,128)(2,1)} %get-tuple-element.187.dy_ref), custom_call_target="tpu_custom_call" | custom-call | flops 8589934592 | bytes 14680064 | tf_op jit(solution)/shard_map/pallas_call | solution.py:623
  273.7 7.5 %collective-permute-done.33 = bf16[256,1024]{1,0:T(8,128)(2,1)S(1)} collective-permute-done((bf16[256,1024]{1,0:T(8,128)(2,1)S(1)}, bf16[256,1024]{1,0:T(8,128)(2,1)S(1)}, u32[]{:S(2)}, u32[]{:S(2)}) %collective-permute-start.33) | collective-permute-done | bytes 524320 | tf_op jit(solution)/shard_map/ppermute | solution.py:54
  285.1 6.1 %fusion.10 = (bf16[2,224,1024]{2,1,0:T(8,128)(2,1)}, bf16[2,224,1024]{2,1,0:T(8,128)(2,1)}, bf16[2,224,1024]{2,1,0:T(8,128)(2,1)}, bf16[2,224,1024]{2,1,0:T(8,128)(2,1)S(1)}) fusion(bf16[2,4,224,1024]{3,2,1,0:T(8,128)(2,1)} %bitcast.51, bf16[2,4,224,1024]{3,2,1,0:T(8,128)(2,1)} %bitcast.172), kind=kLoop, calls=%fused_computation.47 | loop fusion | flops 7340032 | bytes 11010048 | tf_op jit(solution)/shard_map/convert_element_type | solution.py:85
  291.2 5.3 %collective-permute-done.35.crossed = bf16[256,1024]{1,0:T(8,128)(2,1)S(1)} collective-permute-done((bf16[256,1024]{1,0:T(8,128)(2,1)S(1)}, bf16[256,1024]{1,0:T(8,128)(2,1)S(1)}, u32[]{:S(2)}, u32[]{:S(2)}) %collective-permute-start.35) | collective-permute-done | bytes 524320 | tf_op jit(solution)/shard_map/ppermute | solution.py:54
  297.4 5.9 %shard_map.185 = (f32[224,1024]{1,0:T(8,128)}, bf16[224,1024]{1,0:T(8,128)(2,1)}, bf16[32,224]{1,0:T(8,128)(2,1)}, bf16[224,1024]{1,0:T(8,128)(2,1)}, bf16[16,64,224]{2,1,0:T(8,128)(2,1)}) custom-call(bf16[256,1024]{1,0:T(8,128)(2,1)} %get-tuple-element.176.t0, bf16[256,1024]{1,0:T(8,128)(2,1)} %copy-done.15, bf16[256,1024]{1,0:T(8,128)(2,1)} %copy-done.16, ...), custom_call_target="tpu_custom_call" | custom-call | flops 469762048 | bytes 8388608 | tf_op jit(solution)/shard_map/pallas_call | solution.py:694
  303.2 4.8 %all-to-all-start.3 = ((bf16[16,64,224]{2,1,0:T(8,128)(2,1)}), bf16[16,64,224]{2,1,0:T(8,128)(2,1)S(1)}, u32[]{:S(2)}, u32[]{:S(2)}) async-start(bf16[16,64,224]{2,1,0:T(8,128)(2,1)} %get-tuple-element.196), calls=%async_computation.3 | async-start | bytes 1048576 | tf_op jit(solution)/shard_map/all_to_all | solution.py:848
  308.1 3.9 shard_map.186
  312.0 8.4 %all-to-all-done.3.g_ref = bf16[16,64,224]{2,1,0:T(8,128)(2,1)S(1)} async-done(((bf16[16,64,224]{2,1,0:T(8,128)(2,1)}), bf16[16,64,224]{2,1,0:T(8,128)(2,1)S(1)}, u32[]{:S(2)}, u32[]{:S(2)}) %all-to-all-start.3) | async-done | bytes 458784 | tf_op jit(solution)/shard_map/all_to_all | solution.py:848
  321.3 4.7 %all-to-all-start.4 = ((bf16[8,128,1152]{2,1,0:T(8,128)(2,1)}), bf16[8,128,1152]{2,1,0:T(8,128)(2,1)S(1)}, u32[]{:S(2)}, u32[]{:S(2)}) async-start(bf16[8,128,1152]{2,1,0:T(8,128)(2,1)} %shard_map.186), calls=%async_computation.4 | async-start | bytes 4718592 | tf_op jit(solution)/shard_map/all_to_all | solution.py:855
  328.7 31.1 %shard_map.187.first.second = bf16[3584,256]{1,0:T(8,128)(2,1)} custom-call(bf16[3584,256]{1,0:T(8,128)(2,1)} %shard_map.179.qkv_ref, bf16[16,64,224]{2,1,0:T(8,128)(2,1)} %copy-done.20, f32[64,3584]{1,0:T(8,128)} %get-tuple-element.214.ot_ref, f32[1,3584]{1,0:T(1,128)} %get-tuple-element.215.lse_ref, s32[1,3584]{1,0:T(1,128)} %compare_select_fusion.begin_ref, ...), custom_call_target="tpu_custom_call" | custom-call | flops 18119393280 | bytes 8388608 | tf_op jit(solution)/shard_map/pallas_call | solution.py:416
  359.8 7.0 %collective-permute-done.36 = bf16[2,224,1024]{2,1,0:T(8,128)(2,1)} collective-permute-done((bf16[2,224,1024]{2,1,0:T(8,128)(2,1)}, bf16[2,224,1024]{2,1,0:T(8,128)(2,1)}, u32[]{:S(2)}, u32[]{:S(2)}) %collective-permute-start.36) | collective-permute-done | bytes 917536 | tf_op jit(solution)/shard_map/ppermute | solution.py:54
  373.6 5.7 %shard_map.188 = (bf16[4,240,1024]{2,1,0:T(8,128)(2,1)}, bf16[4,240,1024]{2,1,0:T(8,128)(2,1)}) custom-call(s32[8]{0:T(128)} %get-tuple-element.280.places, bf16[3584,256]{1,0:T(8,128)(2,1)} %shard_map.187.first.second, bf16[3584,256]{1,0:T(8,128)(2,1)} %shard_map.187.first.second, bf16[1024,256]{1,0:T(8,128)(2,1)} %broadcast_select_fusion.w, ...), custom_call_target="tpu_custom_call" | custom-call | flops 939524096 | bytes 5242880 | tf_op jit(solution)/shard_map/pallas_call | solution.py:207
  379.4 5.9 %shard_map.189 = (bf16[4,240,1024]{2,1,0:T(8,128)(2,1)}, bf16[4,240,1024]{2,1,0:T(8,128)(2,1)}) custom-call(s32[8]{0:T(128)} %get-tuple-element.279.places, bf16[3584,256]{1,0:T(8,128)(2,1)} %shard_map.187.first.second, bf16[3584,256]{1,0:T(8,128)(2,1)} %shard_map.187.first.second, bf16[1024,256]{1,0:T(8,128)(2,1)} %broadcast_select_fusion.w, ...), custom_call_target="tpu_custom_call" | custom-call | flops 939524096 | bytes 5242880 | tf_op jit(solution)/shard_map/pallas_call | solution.py:207
  398.3 10.8 %shard_map.190 = bf16[1024,256]{1,0:T(8,128)(2,1)} custom-call(s32[16]{0:T(128)} %copy-done.36, bf16[4,224,1024]{2,1,0:T(8,128)(2,1)} %copy-done.1, bf16[4,224,1024]{2,1,0:T(8,128)(2,1)} %collective-permute-done.7.other.near_other, bf16[4,224,1024]{2,1,0:T(8,128)(2,1)} %pad_maximum_fusion.3.mine.far_mine, ...), custom_call_target="tpu_custom_call" | custom-call | flops 1879048192 | bytes 10485760 | tf_op jit(solution)/shard_map/pallas_call | solution.py:251
  409.1 10.2 %all-to-all-start.5 = ((bf16[128,8,256]{2,1,0:T(8,128)(2,1)}), bf16[128,8,256]{2,1,0:T(8,128)(2,1)S(1)}, u32[]{:S(2)}, u32[]{:S(2)}) async-start(bf16[128,8,256]{2,1,0:T(8,128)(2,1)} %bitcast.174), calls=%async_computation.6 | async-start | bytes 1048576 | tf_op jit(solution)/shard_map/all_to_all | solution.py:873
  435.7 12.4 %collective-permute-done.46 = bf16[240,1024]{1,0:T(8,128)(2,1)S(1)} collective-permute-done((bf16[240,1024]{1,0:T(8,128)(2,1)}, bf16[240,1024]{1,0:T(8,128)(2,1)S(1)}, u32[]{:S(2)}, u32[]{:S(2)}) %collective-permute-start.46) | collective-permute-done | bytes 491552 | tf_op jit(solution)/shard_map/ppermute | solution.py:54
  (271 shorter events, 142.6 us)
Async XLA Ops:
  7.2 35.1 %collective-permute-start = (bf16[224,1024]{1,0:T(8,128)(2,1)}, bf16[224,1024]{1,0:T(8,128)(2,1)S(1)}, u32[]{:S(2)}, u32[]{:S(2)}) collective-permute-start(bf16[224,1024]{1,0:T(8,128)(2,1)} %bitcast.165), channel_id=1, source_target_pairs={{0,64},{8,72},{16,80},{24,88},{32,96},{40,104},{48,112},{56,120},{... | collective-permute-start | bytes 1376264 | tf_op jit(solution)/shard_map/ppermute | solution.py:54
  10.4 32.0 %collective-permute-start.4 = (bf16[224,1024]{1,0:T(8,128)(2,1)}, bf16[224,1024]{1,0:T(8,128)(2,1)S(1)}, u32[]{:S(2)}, u32[]{:S(2)}) collective-permute-start(bf16[224,1024]{1,0:T(8,128)(2,1)} %bitcast.166), channel_id=1, source_target_pairs={{0,16},{8,24},{16,32},{24,40},{32,48},{40,56},{48,0},{56,8},{64,80... | collective-permute-start | bytes 1376264 | tf_op jit(solution)/shard_map/ppermute | solution.py:54
  12.3 30.0 %collective-permute-start.5 = (bf16[224,1024]{1,0:T(8,128)(2,1)}, bf16[224,1024]{1,0:T(8,128)(2,1)S(1)}, u32[]{:S(2)}, u32[]{:S(2)}) collective-permute-start(bf16[224,1024]{1,0:T(8,128)(2,1)} %bitcast.167), channel_id=1, source_target_pairs={{0,48},{8,56},{16,0},{24,8},{32,16},{40,24},{48,32},{56,40},{64,11... | collective-permute-start | bytes 1376264 | tf_op jit(solution)/shard_map/ppermute | solution.py:54
  14.4 27.9 %collective-permute-start.6 = (bf16[224,1024]{1,0:T(8,128)(2,1)}, bf16[224,1024]{1,0:T(8,128)(2,1)}, u32[]{:S(2)}, u32[]{:S(2)}) collective-permute-start(bf16[224,1024]{1,0:T(8,128)(2,1)} %bitcast.168), channel_id=1, source_target_pairs={{0,32},{8,40},{16,48},{24,56},{32,0},{40,8},{48,16},{56,24},{64,96... | collective-permute-start | bytes 1376264 | tf_op jit(solution)/shard_map/ppermute | solution.py:54
  26.6 159.7 %all-gather.5.cloned.1.call-start = ((), (), s32[]{:S(2)}) async-start(), calls=%async_computation.8 | async-start | bytes 3932160 | tf_op jit(solution)/shard_map/all_gather | solution.py:782
  74.9 43.9 %all-to-all-start.1 = ((bf16[128,8,1152]{2,1,0:T(8,128)(2,1)}), bf16[128,8,1152]{2,1,0:T(8,128)(2,1)S(1)}, u32[]{:S(2)}, u32[]{:S(2)}) async-start(bf16[128,8,1152]{2,1,0:T(8,128)(2,1)} %broadcast_in_dim.101), calls=%async_computation.1 | async-start | bytes 4718592 | tf_op jit(solution)/shard_map/all_to_all | solution.py:790
  83.9 102.4 %all-gather.7.cloned.1.call-start = ((), (), s32[]{:S(2)}) async-start(), calls=%async_computation.9 | async-start | bytes 3932160 | tf_op jit(solution)/shard_map/all_gather | solution.py:782
  85.3 39.0 %collective-permute-start.10 = (bf16[240,1024]{1,0:T(8,128)(2,1)S(1)}, bf16[240,1024]{1,0:T(8,128)(2,1)}, u32[]{:S(2)}, u32[]{:S(2)}) collective-permute-start(bf16[240,1024]{1,0:T(8,128)(2,1)S(1)} %fusion.21), channel_id=1, source_target_pairs={{0,16},{8,24},{16,32},{24,40},{32,48},{40,56},{48,0},{56,8},{64,80... | collective-permute-start | bytes 1474568 | tf_op jit(solution)/shard_map/ppermute | solution.py:54
  86.3 37.9 %collective-permute-start.11 = (bf16[240,1024]{1,0:T(8,128)(2,1)S(1)}, bf16[240,1024]{1,0:T(8,128)(2,1)}, u32[]{:S(2)}, u32[]{:S(2)}) collective-permute-start(bf16[240,1024]{1,0:T(8,128)(2,1)S(1)} %fusion.21), channel_id=1, source_target_pairs={{0,48},{8,56},{16,0},{24,8},{32,16},{40,24},{48,32},{56,40},{64,11... | collective-permute-start | bytes 1474568 | tf_op jit(solution)/shard_map/ppermute | solution.py:54
  88.5 48.5 %collective-permute-start.12 = (bf16[240,1024]{1,0:T(8,128)(2,1)S(1)}, bf16[240,1024]{1,0:T(8,128)(2,1)}, u32[]{:S(2)}, u32[]{:S(2)}) collective-permute-start(bf16[240,1024]{1,0:T(8,128)(2,1)S(1)} %fusion.21), channel_id=1, source_target_pairs={{0,32},{8,40},{16,48},{24,56},{32,0},{40,8},{48,16},{56,24},{64,96... | collective-permute-start | bytes 1474568 | tf_op jit(solution)/shard_map/ppermute | solution.py:54
  124.2 261.1 %reduce-scatter.2.cloned.1.call-start = ((), (), s32[]{:S(2)}) async-start(), calls=%async_computation.7 | async-start | bytes 7864320 | tf_op jit(solution)/shard_map/reduce_scatter | solution.py:841
  141.3 31.5 %collective-permute-start.21 = (bf16[352,1024]{1,0:T(8,128)(2,1)S(1)}, bf16[352,1024]{1,0:T(8,128)(2,1)}, u32[]{:S(2)}, u32[]{:S(2)}) collective-permute-start(bf16[352,1024]{1,0:T(8,128)(2,1)S(1)} %slice.276), channel_id=1, source_target_pairs={{0,64},{8,72},{16,80},{24,88},{32,96},{40,104},{48,112},{56,120},{... | collective-permute-start | bytes 2162696 | tf_op jit(solution)/shard_map/ppermute | solution.py:54
  178.7 31.5 %collective-permute-start.22 = (bf16[608,1024]{1,0:T(8,128)(2,1)}, bf16[608,1024]{1,0:T(8,128)(2,1)S(1)}, u32[]{:S(2)}, u32[]{:S(2)}) collective-permute-start(bf16[608,1024]{1,0:T(8,128)(2,1)} %slice.215), channel_id=1, source_target_pairs={{0,64},{8,72},{16,80},{24,88},{32,96},{40,104},{48,112},{56,120},{... | collective-permute-start | bytes 3735560 | tf_op jit(solution)/shard_map/ppermute | solution.py:54
  181.4 30.2 %collective-permute-start.14 = (bf16[224,1024]{1,0:T(8,128)(2,1)}, bf16[224,1024]{1,0:T(8,128)(2,1)}, u32[]{:S(2)}, u32[]{:S(2)}) collective-permute-start(bf16[224,1024]{1,0:T(8,128)(2,1)} %copy-done.26), channel_id=1, source_target_pairs={{0,16},{8,24},{16,32},{24,40},{32,48},{40,56},{48,0},{56,8},{64,80... | collective-permute-start | bytes 1376264 | tf_op jit(solution)/shard_map/ppermute | solution.py:54
  182.3 29.3 %collective-permute-start.15 = (bf16[224,1024]{1,0:T(8,128)(2,1)}, bf16[224,1024]{1,0:T(8,128)(2,1)}, u32[]{:S(2)}, u32[]{:S(2)}) collective-permute-start(bf16[224,1024]{1,0:T(8,128)(2,1)} %copy-done.26), channel_id=1, source_target_pairs={{0,48},{8,56},{16,0},{24,8},{32,16},{40,24},{48,32},{56,40},{64,11... | collective-permute-start | bytes 1376264 | tf_op jit(solution)/shard_map/ppermute | solution.py:54
  184.7 26.9 %collective-permute-start.16 = (bf16[224,1024]{1,0:T(8,128)(2,1)}, bf16[224,1024]{1,0:T(8,128)(2,1)S(1)}, u32[]{:S(2)}, u32[]{:S(2)}) collective-permute-start(bf16[224,1024]{1,0:T(8,128)(2,1)} %copy-done.26), channel_id=1, source_target_pairs={{0,32},{8,40},{16,48},{24,56},{32,0},{40,8},{48,16},{56,24},{64,96... | collective-permute-start | bytes 1376264 | tf_op jit(solution)/shard_map/ppermute | solution.py:54
  216.5 28.5 %collective-permute-start.27 = (bf16[256,1024]{1,0:T(8,128)(2,1)}, bf16[256,1024]{1,0:T(8,128)(2,1)S(1)}, u32[]{:S(2)}, u32[]{:S(2)}) collective-permute-start(bf16[256,1024]{1,0:T(8,128)(2,1)} %get-tuple-element.263), channel_id=1, source_target_pairs={{0,48},{8,56},{16,0},{24,8},{32,16},{40,24},{48,32},{56,40},{64,11... | collective-permute-start | bytes 1572872 | tf_op jit(solution)/shard_map/ppermute | solution.py:54
  219.5 26.4 %collective-permute-start.28 = (bf16[256,1024]{1,0:T(8,128)(2,1)}, bf16[256,1024]{1,0:T(8,128)(2,1)S(1)}, u32[]{:S(2)}, u32[]{:S(2)}) collective-permute-start(bf16[256,1024]{1,0:T(8,128)(2,1)} %get-tuple-element.262), channel_id=1, source_target_pairs={{0,16},{8,24},{16,32},{24,40},{32,48},{40,56},{48,0},{56,8},{64,80... | collective-permute-start | bytes 1572872 | tf_op jit(solution)/shard_map/ppermute | solution.py:54
  219.5 26.4 %collective-permute-start.29 = (bf16[256,1024]{1,0:T(8,128)(2,1)S(1)}, bf16[256,1024]{1,0:T(8,128)(2,1)S(1)}, u32[]{:S(2)}, u32[]{:S(2)}) collective-permute-start(bf16[256,1024]{1,0:T(8,128)(2,1)S(1)} %get-tuple-element.261), channel_id=1, source_target_pairs={{0,32},{8,40},{16,48},{24,56},{32,0},{40,8},{48,16},{56,24},{64,96... | collective-permute-start | bytes 1572872 | tf_op jit(solution)/shard_map/ppermute | solution.py:54
  250.4 30.8 %collective-permute-start.34 = (bf16[8,224,1024]{2,1,0:T(8,128)(2,1)}, bf16[8,224,1024]{2,1,0:T(8,128)(2,1)}, u32[]{:S(2)}, u32[]{:S(2)}) collective-permute-start(bf16[8,224,1024]{2,1,0:T(8,128)(2,1)} %get-tuple-element.188), channel_id=1, source_target_pairs={{0,8},{8,0},{16,24},{24,16},{32,40},{40,32},{48,56},{56,48},{64,72... | collective-permute-start | bytes 11010056 | tf_op jit(solution)/shard_map/ppermute | solution.py:58
  321.3 48.9 %all-to-all-start.4 = ((bf16[8,128,1152]{2,1,0:T(8,128)(2,1)}), bf16[8,128,1152]{2,1,0:T(8,128)(2,1)S(1)}, u32[]{:S(2)}, u32[]{:S(2)}) async-start(bf16[8,128,1152]{2,1,0:T(8,128)(2,1)} %shard_map.186), calls=%async_computation.4 | async-start | bytes 4718592 | tf_op jit(solution)/shard_map/all_to_all | solution.py:855
  326.0 40.8 %collective-permute-start.36 = (bf16[2,224,1024]{2,1,0:T(8,128)(2,1)}, bf16[2,224,1024]{2,1,0:T(8,128)(2,1)}, u32[]{:S(2)}, u32[]{:S(2)}) collective-permute-start(bf16[2,224,1024]{2,1,0:T(8,128)(2,1)} %get-tuple-element.206), channel_id=1, source_target_pairs={{0,48},{8,56},{16,0},{24,8},{32,16},{40,24},{48,32},{56,40},{64,11... | collective-permute-start | bytes 2752520 | tf_op jit(solution)/shard_map/ppermute | solution.py:54
  326.9 43.2 %collective-permute-start.37 = (bf16[2,224,1024]{2,1,0:T(8,128)(2,1)}, bf16[2,224,1024]{2,1,0:T(8,128)(2,1)}, u32[]{:S(2)}, u32[]{:S(2)}) collective-permute-start(bf16[2,224,1024]{2,1,0:T(8,128)(2,1)} %get-tuple-element.207), channel_id=1, source_target_pairs={{0,16},{8,24},{16,32},{24,40},{32,48},{40,56},{48,0},{56,8},{64,80... | collective-permute-start | bytes 2752520 | tf_op jit(solution)/shard_map/ppermute | solution.py:54
  328.0 42.1 %collective-permute-start.38 = (bf16[2,224,1024]{2,1,0:T(8,128)(2,1)}, bf16[2,224,1024]{2,1,0:T(8,128)(2,1)}, u32[]{:S(2)}, u32[]{:S(2)}) collective-permute-start(bf16[2,224,1024]{2,1,0:T(8,128)(2,1)} %get-tuple-element.208), channel_id=1, source_target_pairs={{0,32},{8,40},{16,48},{24,56},{32,0},{40,8},{48,16},{56,24},{64,96... | collective-permute-start | bytes 2752520 | tf_op jit(solution)/shard_map/ppermute | solution.py:54
  391.2 31.0 %collective-permute-start.41 = (bf16[240,1024]{1,0:T(8,128)(2,1)}, bf16[240,1024]{1,0:T(8,128)(2,1)}, u32[]{:S(2)}, u32[]{:S(2)}) collective-permute-start(bf16[240,1024]{1,0:T(8,128)(2,1)} %get-tuple-element.227), channel_id=1, source_target_pairs={{0,48},{8,56},{16,0},{24,8},{32,16},{40,24},{48,32},{56,40},{64,11... | collective-permute-start | bytes 1474568 | tf_op jit(solution)/shard_map/ppermute | solution.py:54
  391.5 30.7 %collective-permute-start.42 = (bf16[240,1024]{1,0:T(8,128)(2,1)}, bf16[240,1024]{1,0:T(8,128)(2,1)}, u32[]{:S(2)}, u32[]{:S(2)}) collective-permute-start(bf16[240,1024]{1,0:T(8,128)(2,1)} %get-tuple-element.228), channel_id=1, source_target_pairs={{0,16},{8,24},{16,32},{24,40},{32,48},{40,56},{48,0},{56,8},{64,80... | collective-permute-start | bytes 1474568 | tf_op jit(solution)/shard_map/ppermute | solution.py:54
  393.3 31.0 %collective-permute-start.43 = (bf16[240,1024]{1,0:T(8,128)(2,1)}, bf16[240,1024]{1,0:T(8,128)(2,1)}, u32[]{:S(2)}, u32[]{:S(2)}) collective-permute-start(bf16[240,1024]{1,0:T(8,128)(2,1)} %get-tuple-element.229), channel_id=1, source_target_pairs={{0,32},{8,40},{16,48},{24,56},{32,0},{40,8},{48,16},{56,24},{64,96... | collective-permute-start | bytes 1474568 | tf_op jit(solution)/shard_map/ppermute | solution.py:54
  397.2 35.2 %collective-permute-start.49 = (bf16[2,192,1024]{2,1,0:T(8,128)(2,1)}, bf16[2,192,1024]{2,1,0:T(8,128)(2,1)}, u32[]{:S(2)}, u32[]{:S(2)}) collective-permute-start(bf16[2,192,1024]{2,1,0:T(8,128)(2,1)} %dynamic-slice_bitcast_fusion), channel_id=1, source_target_pairs={{0,1},{1,0},{2,3},{3,2},{4,5},{5,4},{6,7},{7,6},{8,9},{9,8},{10,11... | collective-permute-start | bytes 2359304 | tf_op jit(solution)/shard_map/ppermute | solution.py:101
  409.1 42.8 %all-to-all-start.5 = ((bf16[128,8,256]{2,1,0:T(8,128)(2,1)}), bf16[128,8,256]{2,1,0:T(8,128)(2,1)S(1)}, u32[]{:S(2)}, u32[]{:S(2)}) async-start(bf16[128,8,256]{2,1,0:T(8,128)(2,1)} %bitcast.174), calls=%async_computation.6 | async-start | bytes 1048576 | tf_op jit(solution)/shard_map/all_to_all | solution.py:873
  419.3 28.8 %collective-permute-start.46 = (bf16[240,1024]{1,0:T(8,128)(2,1)}, bf16[240,1024]{1,0:T(8,128)(2,1)S(1)}, u32[]{:S(2)}, u32[]{:S(2)}) collective-permute-start(bf16[240,1024]{1,0:T(8,128)(2,1)} %get-tuple-element.238), channel_id=1, source_target_pairs={{0,48},{8,56},{16,0},{24,8},{32,16},{40,24},{48,32},{56,40},{64,11... | collective-permute-start | bytes 1474568 | tf_op jit(solution)/shard_map/ppermute | solution.py:54
  422.2 28.9 %collective-permute-start.47 = (bf16[240,1024]{1,0:T(8,128)(2,1)}, bf16[240,1024]{1,0:T(8,128)(2,1)S(1)}, u32[]{:S(2)}, u32[]{:S(2)}) collective-permute-start(bf16[240,1024]{1,0:T(8,128)(2,1)} %get-tuple-element.239), channel_id=1, source_target_pairs={{0,16},{8,24},{16,32},{24,40},{32,48},{40,56},{48,0},{56,8},{64,80... | collective-permute-start | bytes 1474568 | tf_op jit(solution)/shard_map/ppermute | solution.py:54
  422.2 29.7 %collective-permute-start.48 = (bf16[240,1024]{1,0:T(8,128)(2,1)}, bf16[240,1024]{1,0:T(8,128)(2,1)}, u32[]{:S(2)}, u32[]{:S(2)}) collective-permute-start(bf16[240,1024]{1,0:T(8,128)(2,1)} %get-tuple-element.240), channel_id=1, source_target_pairs={{0,32},{8,40},{16,48},{24,56},{32,0},{40,8},{48,16},{56,24},{64,96... | collective-permute-start | bytes 1474568 | tf_op jit(solution)/shard_map/ppermute | solution.py:54
  (70 other events, 726.3 us)
Sparse Core Ops, SparseCore 0:
  29.1 40.6 all-gather.4
  86.4 50.9 all-gather.6
  281.4 89.0 reduce-scatter.1

commit v18 on v17

--- a/solution.py
+++ b/solution.py
@@ -854,7 +854,10 @@
 
     shared_grads = lax.all_to_all(shared_grads, "wshard", 0, 0, tiled=True)
     projected_grad = attend_back(qkv, head_grad, attended_t, lse, begin, table)
-    shared_grads, moved_terms = tie(shared_grads, moved_terms)
+    grad_head = head_weight_grad(places, rows_near, rows_far, gain_attn, projected_grad)
+    shared_grads, grad_head, projected_grad, moved_terms = tie(
+        shared_grads, grad_head, projected_grad, moved_terms
+    )
     shared_grads = jnp.sum(shared_grads.astype(f32), axis=0)
     moved_crossed = add_low(*[t[1] for t in moved_terms])
     shared_grads, moved_crossed = tie(shared_grads, moved_crossed)
@@ -862,14 +865,12 @@
     far_part = project_back(places[8:], projected_grad, head_weights, shared_grads)
     near_part = project_back(places[:8], projected_grad, head_weights, shared_grads)
     far_parts = chip_parts(far_part[0], swap_cores(far_part[1]))
-    near_part, expert_grads = tie(near_part, expert_grads)
     near_parts = chip_parts(near_part[0], swap_cores(near_part[1]))
-    far_parts, near_parts, projected_grad, expert_grads = tie(
-        far_parts, near_parts, projected_grad, expert_grads
-    )
-    far_terms, moved_crossed = tie(send_along_z(far_parts), moved_crossed)
+    far_parts, near_parts, grad_head = tie(far_parts, near_parts, grad_head)
+    far_terms, moved_crossed, expert_grads = tie(
+        send_along_z(far_parts), moved_crossed, expert_grads
+    )
     near_terms = send_along_z(near_parts)
-    grad_head = head_weight_grad(places, rows_near, rows_far, gain_attn, projected_grad)
     grad_heads = lax.all_to_all(grad_head.reshape(128, 8, 256), BOTH, 0, 0, tiled=True)
     crossed = send(add_low(*far_terms), 1, 0)
     crossed, near_terms, grad_heads = tie(crossed, near_terms, grad_heads)

time: 475 us -> 473 us (level)
  starting transfers between devices: 103 us -> 112 us
  waiting for transfers between devices: 106 us -> 98.4 us
    ppermute x37, waiting for transfers between devices: 79.7 us -> 67.8 us  [send(): return lax.ppermute(rows, 'seq', shift_perm(a, b))]
    ppermute x37, starting transfers between devices: 58.5 us -> 69.4 us  [send(): return lax.ppermute(rows, 'seq', shift_perm(a, b))]
  transfers between devices with their start and end apart: 59 -> 59, of which waited for: 19 -> 20; matrix products, arithmetic and copies ran while one was open for 14% -> 14% of each run, Pallas kernels for 35% -> 35%
where the time goes in v18:
time: 473 us; the launch traced here: 464 us
  Pallas kernels  163 us (34%)
  starting transfers between devices  112 us (24%)
  waiting for transfers between devices  98.4 us (21%)
  other arithmetic  54 us (11%)
  local copies, waits for them, and re-layouts  21.3 us (5%)
  between operations  14.9 us (3%)
    ppermute x37, starting transfers between devices, send(): return lax.ppermute(rows, 'seq', shift_perm(a, b))  69.4 us
    ppermute x37, waiting for transfers between devices, send(): return lax.ppermute(rows, 'seq', shift_perm(a, b))  67.8 us
    pallas_call x2, Pallas kernels, run_experts(): pl.pallas_call(experts_kernel, grid_spec=pltpu.PrefetchScalarGridSpec(num...  44 us
    pallas_call x1, Pallas kernels, attend_back(): pl.pallas_call(attend_back_kernel, grid=(GROUP // BLOCK,), in_specs=[whol...  31.1 us
    pallas_call x1, Pallas kernels, attend(): pl.pallas_call(attend_kernel, grid=(GROUP // BLOCK,), in_specs=[whole(GRO...  19.8 us
    convert_element_type x7, other arithmetic, add_low(): return sum([t.astype(f32) for t in terms]).astype(bf16)  17.8 us
    pallas_call x2, Pallas kernels, project(): pl.pallas_call(project_kernel, grid_spec=pltpu.PrefetchScalarGridSpec(num...  16.7 us
    pallas_call x1, Pallas kernels, expert_weight_grads(): pl.pallas_call(expert_grads_kernel, grid=(2, 4), in_specs=[pl.BlockSpec((...  15.9 us
  transfers between devices with their start and end apart: 59, of which 20 were waited for; matrix products, arithmetic and copies ran while one was open for 14% of the time, Pallas kernels for 35%

profile of v18, /device:TPU:0, one launch (start us, length us, event | category | flops | bytes accessed | tf_op | source)
XLA Modules:
  0.0 463.9 jit_solution(15892298158859355949)
XLA Ops:
  19.8 6.8 %all-to-all-start = ((bf16[128,8,256]{2,1,0:T(8,128)(2,1)}), bf16[128,8,256]{2,1,0:T(8,128)(2,1)S(1)}, u32[]{:S(2)}, u32[]{:S(2)}) async-start(bf16[128,8,256]{2,1,0:T(8,128)(2,1)} %bitcast.9), calls=%async_computation | async-start | bytes 1048576 | tf_op jit(solution)/shard_map/all_to_all | solution.py:772
  28.7 7.7 %subtract_cosine_fusion.table = f32[3584,128]{1,0:T(8,128)} fusion(f32[128]{0:T(128)S(1)} %get-tuple-element.279, f32[128]{0:T(128)S(1)} %get-tuple-element.280, f32[3584]{0:T(1024)S(1)} %get-tuple-element.274), kind=kLoop, calls=%fused_computation.11 | loop fusion | flops 917504 | bytes 1850368 | tf_op jit(solution)/shard_map/cos | solution.py:139
  36.4 5.1 %all-to-all-done = bf16[128,8,256]{2,1,0:T(8,128)(2,1)S(1)} async-done(((bf16[128,8,256]{2,1,0:T(8,128)(2,1)}), bf16[128,8,256]{2,1,0:T(8,128)(2,1)S(1)}, u32[]{:S(2)}, u32[]{:S(2)}) %all-to-all-start) | async-done | bytes 524320 | tf_op jit(solution)/shard_map/all_to_all | solution.py:772
  51.5 8.0 %shard_map.178.refs_0_ = bf16[3584,256]{1,0:T(8,128)(2,1)} custom-call(s32[8]{0:T(128)} %get-tuple-element.277.places, bf16[4,224,1024]{2,1,0:T(8,128)(2,1)} %copy-done.1, bf16[4,224,1024]{2,1,0:T(8,128)(2,1)} %collective-permute-done.7.other.near_other, bf16[1024,256]{1,0:T(8,128)(2,1)} %broadcast_select_fusion.w, f32[1,1024]{1,0:T(1,128)} %bitcast.191, ...), custom_call_target="tpu_custom_call" | custom-call | flops 939524096 | bytes 10485760 | tf_op jit(solution)/shard_map/pallas_call | solution.py:176
  59.4 5.9 %collective-permute-done.8 = bf16[2,192,1024]{2,1,0:T(8,128)(2,1)} collective-permute-done((bf16[2,192,1024]{2,1,0:T(8,128)(2,1)}, bf16[2,192,1024]{2,1,0:T(8,128)(2,1)}, u32[]{:S(2)}, u32[]{:S(2)}) %collective-permute-start.8) | collective-permute-done | bytes 786464 | tf_op jit(solution)/shard_map/ppermute | solution.py:101
  65.4 3.8 collective-permute-done.2
  74.2 9.0 %all-to-all-start.1 = ((bf16[128,8,1152]{2,1,0:T(8,128)(2,1)}), bf16[128,8,1152]{2,1,0:T(8,128)(2,1)S(1)}, u32[]{:S(2)}, u32[]{:S(2)}) async-start(bf16[128,8,1152]{2,1,0:T(8,128)(2,1)} %broadcast_in_dim.101), calls=%async_computation.1 | async-start | bytes 4718592 | tf_op jit(solution)/shard_map/all_to_all | solution.py:790
  89.6 8.7 %shard_map.179.qkv_ref = bf16[3584,256]{1,0:T(8,128)(2,1)} custom-call(s32[8]{0:T(128)} %get-tuple-element.278.places, bf16[4,224,1024]{2,1,0:T(8,128)(2,1)} %pad_maximum_fusion.3.mine.far_mine, bf16[4,224,1024]{2,1,0:T(8,128)(2,1)} %collective-permute-done.9.other.far_other, bf16[1024,256]{1,0:T(8,128)(2,1)} %broadcast_select_fusion.w, ...), custom_call_target="tpu_custom_call" | custom-call | flops 939524096 | bytes 10485760 | tf_op jit(solution)/shard_map/pallas_call | solution.py:176
  98.4 19.8 %shard_map.180 = (bf16[16,64,224]{2,1,0:T(8,128)(2,1)}, f32[64,3584]{1,0:T(8,128)}, f32[1,3584]{1,0:T(1,128)}) custom-call(bf16[3584,256]{1,0:T(8,128)(2,1)} %shard_map.179.qkv_ref, s32[1,3584]{1,0:T(1,128)} %compare_select_fusion.begin_ref), custom_call_target="tpu_custom_call" | custom-call | flops 7247757312 | bytes 4194304 | tf_op jit(solution)/shard_map/pallas_call | solution.py:336
  118.2 5.3 %all-to-all-start.2 = ((bf16[16,64,224]{2,1,0:T(8,128)(2,1)}), bf16[16,64,224]{2,1,0:T(8,128)(2,1)S(1)}, u32[]{:S(2)}, u32[]{:S(2)}) async-start(bf16[16,64,224]{2,1,0:T(8,128)(2,1)} %get-tuple-element.142), calls=%async_computation.2 | async-start | bytes 1048576 | tf_op jit(solution)/shard_map/all_to_all | solution.py:805
  123.5 12.8 %collective-permute-done.12 = bf16[240,1024]{1,0:T(8,128)(2,1)} collective-permute-done((bf16[240,1024]{1,0:T(8,128)(2,1)S(1)}, bf16[240,1024]{1,0:T(8,128)(2,1)}, u32[]{:S(2)}, u32[]{:S(2)}) %collective-permute-start.12) | collective-permute-done | bytes 491552 | tf_op jit(solution)/shard_map/ppermute | solution.py:54
  144.2 3.8 shard_map.181
  152.1 18.0 %collective-permute-done.13 = bf16[224,1024]{1,0:T(8,128)(2,1)S(1)} collective-permute-done((bf16[224,1024]{1,0:T(8,128)(2,1)}, bf16[224,1024]{1,0:T(8,128)(2,1)S(1)}, u32[]{:S(2)}, u32[]{:S(2)}) %collective-permute-start.13) | collective-permute-done | bytes 458784 | tf_op jit(solution)/shard_map/ppermute | solution.py:54
  185.6 21.9 %shard_map.182 = (bf16[4,256,1024]{2,1,0:T(8,128)(2,1)}, bf16[4,256,1024]{2,1,0:T(8,128)(2,1)}, bf16[8,224,1024]{2,1,0:T(8,128)(2,1)}, bf16[8,224,1024]{2,1,0:T(...) custom-call(s32[2]{0:T(128)} %pad_add_fusion.own_ref, ...), custom_call_target="tpu_custom_call" | custom-call | flops 15032385536 | bytes 25165824 | tf_op jit(solution)/shard_map/pallas_call | solution.py:567
  221.6 22.1 %shard_map.183 = (bf16[4,256,1024]{2,1,0:T(8,128)(2,1)}, bf16[4,256,1024]{2,1,0:T(8,128)(2,1)}, bf16[8,224,1024]{2,1,0:T(8,128)(2,1)}, bf16[8,224,1024]{2,1,0:T(...) custom-call(s32[2]{0:T(128)} %pad_add_fusion.own_ref, ...), custom_call_target="tpu_custom_call", output_to_operand_aliasing={{2}: (10, {}), {3}: (11, {}), {4}: (12, {}), {5}: (13, {}),... | custom-call | flops 15032385536 | bytes 25165824 | tf_op jit(solution)/shard_map/pallas_call | solution.py:567
  244.4 4.4 collective-permute-done.30
  255.7 15.9 %shard_map.184 = bf16[4,2,2,192,1024]{4,3,2,1,0:T(8,128)(2,1)} custom-call(bf16[2,1152,1024]{2,1,0:T(8,128)(2,1)} %get-tuple-element.183.x_ref, bf16[2,1152,1024]{2,1,0:T(8,128)(2,1)} %get-tuple-element.184.dh_ref, bf16[2,1152,512]{2,1,0:T(8,128)(2,1)} %get-tuple-element.185.act_ref, bf16[2,1152,1024]{2,1,0:T(8,128)(2,1)} %get-tuple-element.186.dy_ref), custom_call_target="tpu_custom_call" | custom-call | flops 8589934592 | bytes 14680064 | tf_op jit(solution)/shard_map/pallas_call | solution.py:623
  271.6 7.5 %collective-permute-done.33 = bf16[256,1024]{1,0:T(8,128)(2,1)S(1)} collective-permute-done((bf16[256,1024]{1,0:T(8,128)(2,1)S(1)}, bf16[256,1024]{1,0:T(8,128)(2,1)S(1)}, u32[]{:S(2)}, u32[]{:S(2)}) %collective-permute-start.33) | collective-permute-done | bytes 524320 | tf_op jit(solution)/shard_map/ppermute | solution.py:54
  283.0 6.1 %fusion.10 = (bf16[2,224,1024]{2,1,0:T(8,128)(2,1)}, bf16[2,224,1024]{2,1,0:T(8,128)(2,1)}, bf16[2,224,1024]{2,1,0:T(8,128)(2,1)}, bf16[2,224,1024]{2,1,0:T(8,128)(2,1)S(1)}) fusion(bf16[2,4,224,1024]{3,2,1,0:T(8,128)(2,1)} %bitcast.51, bf16[2,4,224,1024]{3,2,1,0:T(8,128)(2,1)} %bitcast.172), kind=kLoop, calls=%fused_computation.47 | loop fusion | flops 7340032 | bytes 11010048 | tf_op jit(solution)/shard_map/convert_element_type | solution.py:85
  289.1 5.3 %collective-permute-done.35.crossed = bf16[256,1024]{1,0:T(8,128)(2,1)S(1)} collective-permute-done((bf16[256,1024]{1,0:T(8,128)(2,1)S(1)}, bf16[256,1024]{1,0:T(8,128)(2,1)S(1)}, u32[]{:S(2)}, u32[]{:S(2)}) %collective-permute-start.35) | collective-permute-done | bytes 524320 | tf_op jit(solution)/shard_map/ppermute | solution.py:54
  295.3 5.9 %shard_map.185 = (f32[224,1024]{1,0:T(8,128)}, bf16[224,1024]{1,0:T(8,128)(2,1)}, bf16[32,224]{1,0:T(8,128)(2,1)}, bf16[224,1024]{1,0:T(8,128)(2,1)}, bf16[16,64,224]{2,1,0:T(8,128)(2,1)}) custom-call(bf16[256,1024]{1,0:T(8,128)(2,1)} %get-tuple-element.175.t0, bf16[256,1024]{1,0:T(8,128)(2,1)} %copy-done.17, bf16[256,1024]{1,0:T(8,128)(2,1)} %copy-done.18, ...), custom_call_target="tpu_custom_call" | custom-call | flops 469762048 | bytes 8388608 | tf_op jit(solution)/shard_map/pallas_call | solution.py:694
  301.1 5.0 %all-to-all-start.3 = ((bf16[16,64,224]{2,1,0:T(8,128)(2,1)}), bf16[16,64,224]{2,1,0:T(8,128)(2,1)S(1)}, u32[]{:S(2)}, u32[]{:S(2)}) async-start(bf16[16,64,224]{2,1,0:T(8,128)(2,1)} %get-tuple-element.195), calls=%async_computation.3 | async-start | bytes 1048576 | tf_op jit(solution)/shard_map/all_to_all | solution.py:848
  306.1 3.9 shard_map.186
  310.1 8.4 %all-to-all-done.3.g_ref = bf16[16,64,224]{2,1,0:T(8,128)(2,1)S(1)} async-done(((bf16[16,64,224]{2,1,0:T(8,128)(2,1)}), bf16[16,64,224]{2,1,0:T(8,128)(2,1)S(1)}, u32[]{:S(2)}, u32[]{:S(2)}) %all-to-all-start.3) | async-done | bytes 458784 | tf_op jit(solution)/shard_map/all_to_all | solution.py:848
  319.3 4.7 %all-to-all-start.4 = ((bf16[8,128,1152]{2,1,0:T(8,128)(2,1)}), bf16[8,128,1152]{2,1,0:T(8,128)(2,1)S(1)}, u32[]{:S(2)}, u32[]{:S(2)}) async-start(bf16[8,128,1152]{2,1,0:T(8,128)(2,1)} %shard_map.186), calls=%async_computation.4 | async-start | bytes 4718592 | tf_op jit(solution)/shard_map/all_to_all | solution.py:855
  326.7 31.1 %shard_map.187.first.second = bf16[3584,256]{1,0:T(8,128)(2,1)} custom-call(bf16[3584,256]{1,0:T(8,128)(2,1)} %shard_map.179.qkv_ref, bf16[16,64,224]{2,1,0:T(8,128)(2,1)} %copy-done.22, f32[64,3584]{1,0:T(8,128)} %get-tuple-element.205.ot_ref, f32[1,3584]{1,0:T(1,128)} %get-tuple-element.206.lse_ref, s32[1,3584]{1,0:T(1,128)} %compare_select_fusion.begin_ref, ...), custom_call_target="tpu_custom_call" | custom-call | flops 18119393280 | bytes 8388608 | tf_op jit(solution)/shard_map/pallas_call | solution.py:416
  357.8 10.8 %shard_map.188 = bf16[1024,256]{1,0:T(8,128)(2,1)} custom-call(s32[16]{0:T(128)} %copy-done.36, bf16[4,224,1024]{2,1,0:T(8,128)(2,1)} %copy-done.1, bf16[4,224,1024]{2,1,0:T(8,128)(2,1)} %collective-permute-done.7.other.near_other, bf16[4,224,1024]{2,1,0:T(8,128)(2,1)} %pad_maximum_fusion.3.mine.far_mine, ...), custom_call_target="tpu_custom_call" | custom-call | flops 1879048192 | bytes 10485760 | tf_op jit(solution)/shard_map/pallas_call | solution.py:251
  372.1 5.7 %shard_map.190 = (bf16[4,240,1024]{2,1,0:T(8,128)(2,1)}, bf16[4,240,1024]{2,1,0:T(8,128)(2,1)}) custom-call(s32[8]{0:T(128)} %get-tuple-element.277.places, bf16[3584,256]{1,0:T(8,128)(2,1)} %shard_map.187.first.second, bf16[3584,256]{1,0:T(8,128)(2,1)} %shard_map.187.first.second, bf16[1024,256]{1,0:T(8,128)(2,1)} %broadcast_select_fusion.w, ...), custom_call_target="tpu_custom_call" | custom-call | flops 939524096 | bytes 5242880 | tf_op jit(solution)/shard_map/pallas_call | solution.py:207
  377.9 5.9 %shard_map.189 = (bf16[4,240,1024]{2,1,0:T(8,128)(2,1)}, bf16[4,240,1024]{2,1,0:T(8,128)(2,1)}) custom-call(s32[8]{0:T(128)} %get-tuple-element.278.places, bf16[3584,256]{1,0:T(8,128)(2,1)} %shard_map.187.first.second, bf16[3584,256]{1,0:T(8,128)(2,1)} %shard_map.187.first.second, bf16[1024,256]{1,0:T(8,128)(2,1)} %broadcast_select_fusion.w, ...), custom_call_target="tpu_custom_call" | custom-call | flops 939524096 | bytes 5242880 | tf_op jit(solution)/shard_map/pallas_call | solution.py:207
  398.0 8.6 %all-to-all-start.5 = ((bf16[128,8,256]{2,1,0:T(8,128)(2,1)}), bf16[128,8,256]{2,1,0:T(8,128)(2,1)S(1)}, u32[]{:S(2)}, u32[]{:S(2)}) async-start(bf16[128,8,256]{2,1,0:T(8,128)(2,1)} %bitcast.69), calls=%async_computation.6 | async-start | bytes 1048576 | tf_op jit(solution)/shard_map/all_to_all | solution.py:874
  409.7 11.9 %collective-permute-start.48 = (bf16[240,1024]{1,0:T(8,128)(2,1)}, bf16[240,1024]{1,0:T(8,128)(2,1)}, u32[]{:S(2)}, u32[]{:S(2)}) collective-permute-start(bf16[240,1024]{1,0:T(8,128)(2,1)} %get-tuple-element.238), channel_id=1, source_target_pairs={{0,32},{8,40},{16,48},{24,56},{32,0},{40,8},{48,16},{56,24},{64,96... | collective-permute-start | bytes 1474568 | tf_op jit(solution)/shard_map/ppermute | solution.py:54
  432.0 11.8 %collective-permute-done.47 = bf16[240,1024]{1,0:T(8,128)(2,1)} collective-permute-done((bf16[240,1024]{1,0:T(8,128)(2,1)}, bf16[240,1024]{1,0:T(8,128)(2,1)}, u32[]{:S(2)}, u32[]{:S(2)}) %collective-permute-start.47) | collective-permute-done | bytes 491552 | tf_op jit(solution)/shard_map/ppermute | solution.py:54
  (271 shorter events, 137.4 us)
Async XLA Ops:
  7.2 35.1 %collective-permute-start = (bf16[224,1024]{1,0:T(8,128)(2,1)}, bf16[224,1024]{1,0:T(8,128)(2,1)S(1)}, u32[]{:S(2)}, u32[]{:S(2)}) collective-permute-start(bf16[224,1024]{1,0:T(8,128)(2,1)} %bitcast.165), channel_id=1, source_target_pairs={{0,64},{8,72},{16,80},{24,88},{32,96},{40,104},{48,112},{56,120},{... | collective-permute-start | bytes 1376264 | tf_op jit(solution)/shard_map/ppermute | solution.py:54
  10.4 32.0 %collective-permute-start.4 = (bf16[224,1024]{1,0:T(8,128)(2,1)}, bf16[224,1024]{1,0:T(8,128)(2,1)S(1)}, u32[]{:S(2)}, u32[]{:S(2)}) collective-permute-start(bf16[224,1024]{1,0:T(8,128)(2,1)} %bitcast.166), channel_id=1, source_target_pairs={{0,16},{8,24},{16,32},{24,40},{32,48},{40,56},{48,0},{56,8},{64,80... | collective-permute-start | bytes 1376264 | tf_op jit(solution)/shard_map/ppermute | solution.py:54
  12.3 30.1 %collective-permute-start.5 = (bf16[224,1024]{1,0:T(8,128)(2,1)}, bf16[224,1024]{1,0:T(8,128)(2,1)S(1)}, u32[]{:S(2)}, u32[]{:S(2)}) collective-permute-start(bf16[224,1024]{1,0:T(8,128)(2,1)} %bitcast.167), channel_id=1, source_target_pairs={{0,48},{8,56},{16,0},{24,8},{32,16},{40,24},{48,32},{56,40},{64,11... | collective-permute-start | bytes 1376264 | tf_op jit(solution)/shard_map/ppermute | solution.py:54
  14.4 28.0 %collective-permute-start.6 = (bf16[224,1024]{1,0:T(8,128)(2,1)}, bf16[224,1024]{1,0:T(8,128)(2,1)}, u32[]{:S(2)}, u32[]{:S(2)}) collective-permute-start(bf16[224,1024]{1,0:T(8,128)(2,1)} %bitcast.168), channel_id=1, source_target_pairs={{0,32},{8,40},{16,48},{24,56},{32,0},{40,8},{48,16},{56,24},{64,96... | collective-permute-start | bytes 1376264 | tf_op jit(solution)/shard_map/ppermute | solution.py:54
  26.6 159.0 %all-gather.5.cloned.1.call-start = ((), (), s32[]{:S(2)}) async-start(), calls=%async_computation.8 | async-start | bytes 3932160 | tf_op jit(solution)/shard_map/all_gather | solution.py:782
  74.2 43.9 %all-to-all-start.1 = ((bf16[128,8,1152]{2,1,0:T(8,128)(2,1)}), bf16[128,8,1152]{2,1,0:T(8,128)(2,1)S(1)}, u32[]{:S(2)}, u32[]{:S(2)}) async-start(bf16[128,8,1152]{2,1,0:T(8,128)(2,1)} %broadcast_in_dim.101), calls=%async_computation.1 | async-start | bytes 4718592 | tf_op jit(solution)/shard_map/all_to_all | solution.py:790
  83.2 102.4 %all-gather.7.cloned.1.call-start = ((), (), s32[]{:S(2)}) async-start(), calls=%async_computation.9 | async-start | bytes 3932160 | tf_op jit(solution)/shard_map/all_gather | solution.py:782
  84.6 39.0 %collective-permute-start.10 = (bf16[240,1024]{1,0:T(8,128)(2,1)S(1)}, bf16[240,1024]{1,0:T(8,128)(2,1)}, u32[]{:S(2)}, u32[]{:S(2)}) collective-permute-start(bf16[240,1024]{1,0:T(8,128)(2,1)S(1)} %fusion.21), channel_id=1, source_target_pairs={{0,16},{8,24},{16,32},{24,40},{32,48},{40,56},{48,0},{56,8},{64,80... | collective-permute-start | bytes 1474568 | tf_op jit(solution)/shard_map/ppermute | solution.py:54
  85.6 37.9 %collective-permute-start.11 = (bf16[240,1024]{1,0:T(8,128)(2,1)S(1)}, bf16[240,1024]{1,0:T(8,128)(2,1)}, u32[]{:S(2)}, u32[]{:S(2)}) collective-permute-start(bf16[240,1024]{1,0:T(8,128)(2,1)S(1)} %fusion.21), channel_id=1, source_target_pairs={{0,48},{8,56},{16,0},{24,8},{32,16},{40,24},{48,32},{56,40},{64,11... | collective-permute-start | bytes 1474568 | tf_op jit(solution)/shard_map/ppermute | solution.py:54
  87.8 48.5 %collective-permute-start.12 = (bf16[240,1024]{1,0:T(8,128)(2,1)S(1)}, bf16[240,1024]{1,0:T(8,128)(2,1)}, u32[]{:S(2)}, u32[]{:S(2)}) collective-permute-start(bf16[240,1024]{1,0:T(8,128)(2,1)S(1)} %fusion.21), channel_id=1, source_target_pairs={{0,32},{8,40},{16,48},{24,56},{32,0},{40,8},{48,16},{56,24},{64,96... | collective-permute-start | bytes 1474568 | tf_op jit(solution)/shard_map/ppermute | solution.py:54
  123.5 299.6 %reduce-scatter.2.cloned.1.call-start = ((), (), s32[]{:S(2)}) async-start(), calls=%async_computation.7 | async-start | bytes 7864320 | tf_op jit(solution)/shard_map/reduce_scatter | solution.py:841
  140.6 31.5 %collective-permute-start.21 = (bf16[352,1024]{1,0:T(8,128)(2,1)S(1)}, bf16[352,1024]{1,0:T(8,128)(2,1)}, u32[]{:S(2)}, u32[]{:S(2)}) collective-permute-start(bf16[352,1024]{1,0:T(8,128)(2,1)S(1)} %slice.276), channel_id=1, source_target_pairs={{0,64},{8,72},{16,80},{24,88},{32,96},{40,104},{48,112},{56,120},{... | collective-permute-start | bytes 2162696 | tf_op jit(solution)/shard_map/ppermute | solution.py:54
  178.0 31.5 %collective-permute-start.22 = (bf16[608,1024]{1,0:T(8,128)(2,1)}, bf16[608,1024]{1,0:T(8,128)(2,1)S(1)}, u32[]{:S(2)}, u32[]{:S(2)}) collective-permute-start(bf16[608,1024]{1,0:T(8,128)(2,1)} %slice.215), channel_id=1, source_target_pairs={{0,64},{8,72},{16,80},{24,88},{32,96},{40,104},{48,112},{56,120},{... | collective-permute-start | bytes 3735560 | tf_op jit(solution)/shard_map/ppermute | solution.py:54
  180.7 30.2 %collective-permute-start.14 = (bf16[224,1024]{1,0:T(8,128)(2,1)}, bf16[224,1024]{1,0:T(8,128)(2,1)}, u32[]{:S(2)}, u32[]{:S(2)}) collective-permute-start(bf16[224,1024]{1,0:T(8,128)(2,1)} %copy-done.26), channel_id=1, source_target_pairs={{0,16},{8,24},{16,32},{24,40},{32,48},{40,56},{48,0},{56,8},{64,80... | collective-permute-start | bytes 1376264 | tf_op jit(solution)/shard_map/ppermute | solution.py:54
  181.6 29.3 %collective-permute-start.15 = (bf16[224,1024]{1,0:T(8,128)(2,1)}, bf16[224,1024]{1,0:T(8,128)(2,1)}, u32[]{:S(2)}, u32[]{:S(2)}) collective-permute-start(bf16[224,1024]{1,0:T(8,128)(2,1)} %copy-done.26), channel_id=1, source_target_pairs={{0,48},{8,56},{16,0},{24,8},{32,16},{40,24},{48,32},{56,40},{64,11... | collective-permute-start | bytes 1376264 | tf_op jit(solution)/shard_map/ppermute | solution.py:54
  184.0 26.9 %collective-permute-start.16 = (bf16[224,1024]{1,0:T(8,128)(2,1)}, bf16[224,1024]{1,0:T(8,128)(2,1)S(1)}, u32[]{:S(2)}, u32[]{:S(2)}) collective-permute-start(bf16[224,1024]{1,0:T(8,128)(2,1)} %copy-done.26), channel_id=1, source_target_pairs={{0,32},{8,40},{16,48},{24,56},{32,0},{40,8},{48,16},{56,24},{64,96... | collective-permute-start | bytes 1376264 | tf_op jit(solution)/shard_map/ppermute | solution.py:54
  215.2 28.5 %collective-permute-start.27 = (bf16[256,1024]{1,0:T(8,128)(2,1)S(1)}, bf16[256,1024]{1,0:T(8,128)(2,1)S(1)}, u32[]{:S(2)}, u32[]{:S(2)}) collective-permute-start(bf16[256,1024]{1,0:T(8,128)(2,1)S(1)} %get-tuple-element.261), channel_id=1, source_target_pairs={{0,48},{8,56},{16,0},{24,8},{32,16},{40,24},{48,32},{56,40},{64,11... | collective-permute-start | bytes 1572872 | tf_op jit(solution)/shard_map/ppermute | solution.py:54
  218.1 26.2 %collective-permute-start.28 = (bf16[256,1024]{1,0:T(8,128)(2,1)S(1)}, bf16[256,1024]{1,0:T(8,128)(2,1)S(1)}, u32[]{:S(2)}, u32[]{:S(2)}) collective-permute-start(bf16[256,1024]{1,0:T(8,128)(2,1)S(1)} %get-tuple-element.260), channel_id=1, source_target_pairs={{0,16},{8,24},{16,32},{24,40},{32,48},{40,56},{48,0},{56,8},{64,80... | collective-permute-start | bytes 1572872 | tf_op jit(solution)/shard_map/ppermute | solution.py:54
  218.2 26.2 %collective-permute-start.29 = (bf16[256,1024]{1,0:T(8,128)(2,1)S(1)}, bf16[256,1024]{1,0:T(8,128)(2,1)S(1)}, u32[]{:S(2)}, u32[]{:S(2)}) collective-permute-start(bf16[256,1024]{1,0:T(8,128)(2,1)S(1)} %get-tuple-element.259), channel_id=1, source_target_pairs={{0,32},{8,40},{16,48},{24,56},{32,0},{40,8},{48,16},{56,24},{64,96... | collective-permute-start | bytes 1572872 | tf_op jit(solution)/shard_map/ppermute | solution.py:54
  248.8 30.3 %collective-permute-start.34 = (bf16[8,224,1024]{2,1,0:T(8,128)(2,1)}, bf16[8,224,1024]{2,1,0:T(8,128)(2,1)}, u32[]{:S(2)}, u32[]{:S(2)}) collective-permute-start(bf16[8,224,1024]{2,1,0:T(8,128)(2,1)} %get-tuple-element.187), channel_id=1, source_target_pairs={{0,8},{8,0},{16,24},{24,16},{32,40},{40,32},{48,56},{56,48},{64,72... | collective-permute-start | bytes 11010056 | tf_op jit(solution)/shard_map/ppermute | solution.py:58
  253.7 25.4 %collective-permute-start.33 = (bf16[256,1024]{1,0:T(8,128)(2,1)S(1)}, bf16[256,1024]{1,0:T(8,128)(2,1)S(1)}, u32[]{:S(2)}, u32[]{:S(2)}) collective-permute-start(bf16[256,1024]{1,0:T(8,128)(2,1)S(1)} %get-tuple-element.255), channel_id=1, source_target_pairs={{0,32},{8,40},{16,48},{24,56},{32,0},{40,8},{48,16},{56,24},{64,96... | collective-permute-start | bytes 1572872 | tf_op jit(solution)/shard_map/ppermute | solution.py:54
  319.3 49.3 %all-to-all-start.4 = ((bf16[8,128,1152]{2,1,0:T(8,128)(2,1)}), bf16[8,128,1152]{2,1,0:T(8,128)(2,1)S(1)}, u32[]{:S(2)}, u32[]{:S(2)}) async-start(bf16[8,128,1152]{2,1,0:T(8,128)(2,1)} %shard_map.186), calls=%async_computation.4 | async-start | bytes 4718592 | tf_op jit(solution)/shard_map/all_to_all | solution.py:855
  324.0 44.6 %collective-permute-start.36 = (bf16[2,224,1024]{2,1,0:T(8,128)(2,1)}, bf16[2,224,1024]{2,1,0:T(8,128)(2,1)}, u32[]{:S(2)}, u32[]{:S(2)}) collective-permute-start(bf16[2,224,1024]{2,1,0:T(8,128)(2,1)} %get-tuple-element.208), channel_id=1, source_target_pairs={{0,48},{8,56},{16,0},{24,8},{32,16},{40,24},{48,32},{56,40},{64,11... | collective-permute-start | bytes 2752520 | tf_op jit(solution)/shard_map/ppermute | solution.py:54
  325.0 43.6 %collective-permute-start.37 = (bf16[2,224,1024]{2,1,0:T(8,128)(2,1)}, bf16[2,224,1024]{2,1,0:T(8,128)(2,1)}, u32[]{:S(2)}, u32[]{:S(2)}) collective-permute-start(bf16[2,224,1024]{2,1,0:T(8,128)(2,1)} %get-tuple-element.209), channel_id=1, source_target_pairs={{0,16},{8,24},{16,32},{24,40},{32,48},{40,56},{48,0},{56,8},{64,80... | collective-permute-start | bytes 2752520 | tf_op jit(solution)/shard_map/ppermute | solution.py:54
  326.1 42.5 %collective-permute-start.38 = (bf16[2,224,1024]{2,1,0:T(8,128)(2,1)}, bf16[2,224,1024]{2,1,0:T(8,128)(2,1)}, u32[]{:S(2)}, u32[]{:S(2)}) collective-permute-start(bf16[2,224,1024]{2,1,0:T(8,128)(2,1)} %get-tuple-element.210), channel_id=1, source_target_pairs={{0,32},{8,40},{16,48},{24,56},{32,0},{40,8},{48,16},{56,24},{64,96... | collective-permute-start | bytes 2752520 | tf_op jit(solution)/shard_map/ppermute | solution.py:54
  391.9 30.4 %collective-permute-start.42 = (bf16[240,1024]{1,0:T(8,128)(2,1)}, bf16[240,1024]{1,0:T(8,128)(2,1)}, u32[]{:S(2)}, u32[]{:S(2)}) collective-permute-start(bf16[240,1024]{1,0:T(8,128)(2,1)} %get-tuple-element.225), channel_id=1, source_target_pairs={{0,16},{8,24},{16,32},{24,40},{32,48},{40,56},{48,0},{56,8},{64,80... | collective-permute-start | bytes 1474568 | tf_op jit(solution)/shard_map/ppermute | solution.py:54
  392.3 30.8 %collective-permute-start.43 = (bf16[240,1024]{1,0:T(8,128)(2,1)}, bf16[240,1024]{1,0:T(8,128)(2,1)}, u32[]{:S(2)}, u32[]{:S(2)}) collective-permute-start(bf16[240,1024]{1,0:T(8,128)(2,1)} %get-tuple-element.226), channel_id=1, source_target_pairs={{0,32},{8,40},{16,48},{24,56},{32,0},{40,8},{48,16},{56,24},{64,96... | collective-permute-start | bytes 1474568 | tf_op jit(solution)/shard_map/ppermute | solution.py:54
  395.9 36.1 %collective-permute-start.46 = (bf16[240,1024]{1,0:T(8,128)(2,1)}, bf16[240,1024]{1,0:T(8,128)(2,1)}, u32[]{:S(2)}, u32[]{:S(2)}) collective-permute-start(bf16[240,1024]{1,0:T(8,128)(2,1)} %get-tuple-element.236), channel_id=1, source_target_pairs={{0,48},{8,56},{16,0},{24,8},{32,16},{40,24},{48,32},{56,40},{64,11... | collective-permute-start | bytes 1474568 | tf_op jit(solution)/shard_map/ppermute | solution.py:54
  398.0 45.9 %all-to-all-start.5 = ((bf16[128,8,256]{2,1,0:T(8,128)(2,1)}), bf16[128,8,256]{2,1,0:T(8,128)(2,1)S(1)}, u32[]{:S(2)}, u32[]{:S(2)}) async-start(bf16[128,8,256]{2,1,0:T(8,128)(2,1)} %bitcast.69), calls=%async_computation.6 | async-start | bytes 1048576 | tf_op jit(solution)/shard_map/all_to_all | solution.py:874
  408.5 35.3 %collective-permute-start.47 = (bf16[240,1024]{1,0:T(8,128)(2,1)}, bf16[240,1024]{1,0:T(8,128)(2,1)}, u32[]{:S(2)}, u32[]{:S(2)}) collective-permute-start(bf16[240,1024]{1,0:T(8,128)(2,1)} %get-tuple-element.237), channel_id=1, source_target_pairs={{0,16},{8,24},{16,32},{24,40},{32,48},{40,56},{48,0},{56,8},{64,80... | collective-permute-start | bytes 1474568 | tf_op jit(solution)/shard_map/ppermute | solution.py:54
  409.7 34.1 %collective-permute-start.48 = (bf16[240,1024]{1,0:T(8,128)(2,1)}, bf16[240,1024]{1,0:T(8,128)(2,1)}, u32[]{:S(2)}, u32[]{:S(2)}) collective-permute-start(bf16[240,1024]{1,0:T(8,128)(2,1)} %get-tuple-element.238), channel_id=1, source_target_pairs={{0,32},{8,40},{16,48},{24,56},{32,0},{40,8},{48,16},{56,24},{64,96... | collective-permute-start | bytes 1474568 | tf_op jit(solution)/shard_map/ppermute | solution.py:54
  428.0 25.7 %collective-permute-start.49 = (bf16[2,192,1024]{2,1,0:T(8,128)(2,1)}, bf16[2,192,1024]{2,1,0:T(8,128)(2,1)}, u32[]{:S(2)}, u32[]{:S(2)}) collective-permute-start(bf16[2,192,1024]{2,1,0:T(8,128)(2,1)} %dynamic-slice_bitcast_fusion), channel_id=1, source_target_pairs={{0,1},{1,0},{2,3},{3,2},{4,5},{5,4},{6,7},{7,6},{8,9},{9,8},{10,11... | collective-permute-start | bytes 2359304 | tf_op jit(solution)/shard_map/ppermute | solution.py:101
  (70 other events, 757.3 us)
Sparse Core Ops, SparseCore 0:
  29.1 40.6 all-gather.4
  85.7 50.9 all-gather.6
  279.3 89.0 reduce-scatter.1

commit v19 on v18

--- a/solution.py
+++ b/solution.py
@@ -864,22 +864,43 @@
     moved_crossed = send(moved_crossed, 1, 0)
     far_part = project_back(places[8:], projected_grad, head_weights, shared_grads)
     near_part = project_back(places[:8], projected_grad, head_weights, shared_grads)
-    far_parts = chip_parts(far_part[0], swap_cores(far_part[1]))
-    near_parts = chip_parts(near_part[0], swap_cores(near_part[1]))
-    far_parts, near_parts, grad_head = tie(far_parts, near_parts, grad_head)
-    far_terms, moved_crossed, expert_grads = tie(
-        send_along_z(far_parts), moved_crossed, expert_grads
-    )
-    near_terms = send_along_z(near_parts)
+    upper, lower = slice(0, TOK // 2), slice(TOK // 2, LAST)
+    far_got, near_got = swap_cores(far_part[1]), swap_cores(near_part[1])
+    far_upper = add_low(far_part[0][:, upper], far_got[:, upper])
+    lower_parts = [
+        jnp.stack(
+            [
+                add_low(near_part[0][i, lower], near_got[i, lower]),
+                add_low(far_part[0][i, lower], far_got[i, lower]),
+            ]
+        )
+        for i in range(4)
+    ]
+    far_upper, lower_parts, grad_head, moved_crossed = tie(
+        far_upper, lower_parts, grad_head, moved_crossed
+    )
+    far_upper = send(far_upper, 1, 0)
+    lower_terms = [lower_parts[0]] + [
+        send(lower_parts[i], 0, -b) for i, b in ((1, 1), (2, 3), (3, 2))
+    ]
     grad_heads = lax.all_to_all(grad_head.reshape(128, 8, 256), BOTH, 0, 0, tiled=True)
-    crossed = send(add_low(*far_terms), 1, 0)
-    crossed, near_terms, grad_heads = tie(crossed, near_terms, grad_heads)
+    far_upper, lower_terms, expert_grads = tie(far_upper, lower_terms, expert_grads)
+    crossed = send(add_low(*[t[1] for t in lower_terms]), 1, 0)
+    upper_parts = [
+        add_low(near_part[0][i, upper], near_got[i, upper], far_upper[i]) for i in range(4)
+    ]
+    upper_terms = [upper_parts[0]] + [
+        send(upper_parts[i], 0, -b) for i, b in ((1, 1), (2, 3), (3, 2))
+    ]
+    crossed, grad_heads = tie(crossed, grad_heads)
     kept = lax.dynamic_index_in_dim(expert_grads, own_x, 0, keepdims=False)
     sent = lax.dynamic_index_in_dim(expert_grads, 1 - own_x, 0, keepdims=False)
     expert_grads = kept.astype(f32) + swap_x(sent).astype(f32)
     total = lambda terms: sum([t.astype(f32) for t in terms])
     output = (hidden + total([t[0] for t in moved_terms] + [moved_crossed])).astype(bf16)
-    last_sum = total(near_terms + [crossed])
+    last_sum = jnp.concatenate(
+        [total(upper_terms), total([t[0] for t in lower_terms] + [crossed])], axis=0
+    )
     normed_grad, shared_grads = last_sum[:TOK], last_sum[TOK:]
     grad_heads = jnp.sum(grad_heads.reshape(16, 8, 8, 256).astype(f32), axis=1).transpose(1, 0, 2)
     kv_sum = lambda start: jnp.sum(

time: 473 us -> 489 us (1.034)
  waiting for transfers between devices: 98.4 us -> 114 us
  starting transfers between devices: 112 us -> 106 us
    ppermute x37 -> x38, waiting for transfers between devices: 67.8 us -> 87.5 us  [send(): return lax.ppermute(rows, 'seq', shift_perm(a, b))]
    ppermute x37 -> x38, starting transfers between devices: 69.4 us -> 61.5 us  [send(): return lax.ppermute(rows, 'seq', shift_perm(a, b))]
    convert_element_type x7 -> x8, other arithmetic: 17.8 us -> 16.3 us  [add_low(): return sum([t.astype(f32) for t in terms]).astype(bf16)]
  transfers between devices with their start and end apart: 59 -> 60, of which waited for: 20 -> 19; matrix products, arithmetic and copies ran while one was open for 14% -> 15% of each run, Pallas kernels for 35% -> 34%
where the time goes in v19:
time: 489 us; the launch traced here: 480 us
  Pallas kernels  163 us (33%)
  waiting for transfers between devices  114 us (23%)
  starting transfers between devices  106 us (22%)
  other arithmetic  57.4 us (12%)
  local copies, waits for them, and re-layouts  25 us (5%)
  between operations  14.9 us (3%)
    ppermute x38, waiting for transfers between devices, send(): return lax.ppermute(rows, 'seq', shift_perm(a, b))  87.5 us
    ppermute x38, starting transfers between devices, send(): return lax.ppermute(rows, 'seq', shift_perm(a, b))  61.5 us
    pallas_call x2, Pallas kernels, run_experts(): pl.pallas_call(experts_kernel, grid_spec=pltpu.PrefetchScalarGridSpec(num...  44 us
    pallas_call x1, Pallas kernels, attend_back(): pl.pallas_call(attend_back_kernel, grid=(GROUP // BLOCK,), in_specs=[whol...  31 us
    pallas_call x1, Pallas kernels, attend(): pl.pallas_call(attend_kernel, grid=(GROUP // BLOCK,), in_specs=[whole(GRO...  19.8 us
    pallas_call x2, Pallas kernels, project(): pl.pallas_call(project_kernel, grid_spec=pltpu.PrefetchScalarGridSpec(num...  16.7 us
    convert_element_type x8, other arithmetic, add_low(): return sum([t.astype(f32) for t in terms]).astype(bf16)  16.3 us
    pallas_call x1, Pallas kernels, expert_weight_grads(): pl.pallas_call(expert_grads_kernel, grid=(2, 4), in_specs=[pl.BlockSpec((...  15.9 us
  transfers between devices with their start and end apart: 60, of which 19 were waited for; matrix products, arithmetic and copies ran while one was open for 15% of the time, Pallas kernels for 34%

profile of v19, /device:TPU:0, one launch (start us, length us, event | category | flops | bytes accessed | tf_op | source)
XLA Modules:
  0.0 480.1 jit_solution(881938819549990018)
XLA Ops:
  19.8 6.8 %all-to-all-start = ((bf16[128,8,256]{2,1,0:T(8,128)(2,1)}), bf16[128,8,256]{2,1,0:T(8,128)(2,1)S(1)}, u32[]{:S(2)}, u32[]{:S(2)}) async-start(bf16[128,8,256]{2,1,0:T(8,128)(2,1)} %bitcast.9), calls=%async_computation | async-start | bytes 1048576 | tf_op jit(solution)/shard_map/all_to_all | solution.py:772
  28.7 7.7 %subtract_cosine_fusion.table = f32[3584,128]{1,0:T(8,128)} fusion(f32[128]{0:T(128)S(1)} %get-tuple-element.270, f32[128]{0:T(128)S(1)} %get-tuple-element.271, f32[3584]{0:T(1024)S(1)} %get-tuple-element.265), kind=kLoop, calls=%fused_computation.12 | loop fusion | flops 917504 | bytes 1850368 | tf_op jit(solution)/shard_map/cos | solution.py:139
  36.4 5.1 %all-to-all-done = bf16[128,8,256]{2,1,0:T(8,128)(2,1)S(1)} async-done(((bf16[128,8,256]{2,1,0:T(8,128)(2,1)}), bf16[128,8,256]{2,1,0:T(8,128)(2,1)S(1)}, u32[]{:S(2)}, u32[]{:S(2)}) %all-to-all-start) | async-done | bytes 524320 | tf_op jit(solution)/shard_map/all_to_all | solution.py:772
  52.2 8.0 %shard_map.178.refs_0_ = bf16[3584,256]{1,0:T(8,128)(2,1)} custom-call(s32[8]{0:T(128)} %get-tuple-element.268.places, bf16[4,224,1024]{2,1,0:T(8,128)(2,1)} %copy-done.1, bf16[4,224,1024]{2,1,0:T(8,128)(2,1)} %collective-permute-done.7.other.near_other, bf16[1024,256]{1,0:T(8,128)(2,1)} %broadcast_select_fusion.w, f32[1,1024]{1,0:T(1,128)} %bitcast.190, ...), custom_call_target="tpu_custom_call" | custom-call | flops 939524096 | bytes 10485760 | tf_op jit(solution)/shard_map/pallas_call | solution.py:176
  60.2 4.9 %collective-permute-done.8 = bf16[2,192,1024]{2,1,0:T(8,128)(2,1)} collective-permute-done((bf16[2,192,1024]{2,1,0:T(8,128)(2,1)}, bf16[2,192,1024]{2,1,0:T(8,128)(2,1)}, u32[]{:S(2)}, u32[]{:S(2)}) %collective-permute-start.8) | collective-permute-done | bytes 786464 | tf_op jit(solution)/shard_map/ppermute | solution.py:101
  65.1 4.8 collective-permute-done.2
  74.9 9.0 %all-to-all-start.1 = ((bf16[128,8,1152]{2,1,0:T(8,128)(2,1)}), bf16[128,8,1152]{2,1,0:T(8,128)(2,1)S(1)}, u32[]{:S(2)}, u32[]{:S(2)}) async-start(bf16[128,8,1152]{2,1,0:T(8,128)(2,1)} %broadcast_in_dim.101), calls=%async_computation.1 | async-start | bytes 4718592 | tf_op jit(solution)/shard_map/all_to_all | solution.py:790
  90.4 8.7 %shard_map.179.qkv_ref = bf16[3584,256]{1,0:T(8,128)(2,1)} custom-call(s32[8]{0:T(128)} %get-tuple-element.269.places, bf16[4,224,1024]{2,1,0:T(8,128)(2,1)} %pad_maximum_fusion.3.mine.far_mine, bf16[4,224,1024]{2,1,0:T(8,128)(2,1)} %collective-permute-done.9.other.far_other, bf16[1024,256]{1,0:T(8,128)(2,1)} %broadcast_select_fusion.w, ...), custom_call_target="tpu_custom_call" | custom-call | flops 939524096 | bytes 10485760 | tf_op jit(solution)/shard_map/pallas_call | solution.py:176
  99.1 19.8 %shard_map.180 = (bf16[16,64,224]{2,1,0:T(8,128)(2,1)}, f32[64,3584]{1,0:T(8,128)}, f32[1,3584]{1,0:T(1,128)}) custom-call(bf16[3584,256]{1,0:T(8,128)(2,1)} %shard_map.179.qkv_ref, s32[1,3584]{1,0:T(1,128)} %compare_select_fusion.begin_ref), custom_call_target="tpu_custom_call" | custom-call | flops 7247757312 | bytes 4194304 | tf_op jit(solution)/shard_map/pallas_call | solution.py:336
  118.9 5.3 %all-to-all-start.2 = ((bf16[16,64,224]{2,1,0:T(8,128)(2,1)}), bf16[16,64,224]{2,1,0:T(8,128)(2,1)S(1)}, u32[]{:S(2)}, u32[]{:S(2)}) async-start(bf16[16,64,224]{2,1,0:T(8,128)(2,1)} %get-tuple-element.136), calls=%async_computation.2 | async-start | bytes 1048576 | tf_op jit(solution)/shard_map/all_to_all | solution.py:805
  124.3 12.8 %collective-permute-done.12 = bf16[240,1024]{1,0:T(8,128)(2,1)} collective-permute-done((bf16[240,1024]{1,0:T(8,128)(2,1)S(1)}, bf16[240,1024]{1,0:T(8,128)(2,1)}, u32[]{:S(2)}, u32[]{:S(2)}) %collective-permute-start.12) | collective-permute-done | bytes 491552 | tf_op jit(solution)/shard_map/ppermute | solution.py:54
  152.8 18.0 %collective-permute-done.13 = bf16[224,1024]{1,0:T(8,128)(2,1)S(1)} collective-permute-done((bf16[224,1024]{1,0:T(8,128)(2,1)}, bf16[224,1024]{1,0:T(8,128)(2,1)S(1)}, u32[]{:S(2)}, u32[]{:S(2)}) %collective-permute-start.13) | collective-permute-done | bytes 458784 | tf_op jit(solution)/shard_map/ppermute | solution.py:54
  186.3 21.9 %shard_map.182 = (bf16[4,256,1024]{2,1,0:T(8,128)(2,1)}, bf16[4,256,1024]{2,1,0:T(8,128)(2,1)}, bf16[8,224,1024]{2,1,0:T(8,128)(2,1)}, bf16[8,224,1024]{2,1,0:T(...) custom-call(s32[2]{0:T(128)} %pad_add_fusion.own_ref, ...), custom_call_target="tpu_custom_call" | custom-call | flops 15032385536 | bytes 25165824 | tf_op jit(solution)/shard_map/pallas_call | solution.py:567
  223.1 22.1 %shard_map.183 = (bf16[4,256,1024]{2,1,0:T(8,128)(2,1)}, bf16[4,256,1024]{2,1,0:T(8,128)(2,1)}, bf16[8,224,1024]{2,1,0:T(8,128)(2,1)}, bf16[8,224,1024]{2,1,0:T(...) custom-call(s32[2]{0:T(128)} %pad_add_fusion.own_ref, ...), custom_call_target="tpu_custom_call", output_to_operand_aliasing={{2}: (10, {}), {3}: (11, {}), {4}: (12, {}), {5}: (13, {}),... | custom-call | flops 15032385536 | bytes 25165824 | tf_op jit(solution)/shard_map/pallas_call | solution.py:567
  246.2 4.4 collective-permute-done.30
  257.1 15.9 %shard_map.184 = bf16[4,2,2,192,1024]{4,3,2,1,0:T(8,128)(2,1)} custom-call(bf16[2,1152,1024]{2,1,0:T(8,128)(2,1)} %get-tuple-element.177.x_ref, bf16[2,1152,1024]{2,1,0:T(8,128)(2,1)} %get-tuple-element.178.dh_ref, bf16[2,1152,512]{2,1,0:T(8,128)(2,1)} %get-tuple-element.179.act_ref, bf16[2,1152,1024]{2,1,0:T(8,128)(2,1)} %get-tuple-element.180.dy_ref), custom_call_target="tpu_custom_call" | custom-call | flops 8589934592 | bytes 14680064 | tf_op jit(solution)/shard_map/pallas_call | solution.py:623
  273.0 7.6 %collective-permute-done.33 = bf16[256,1024]{1,0:T(8,128)(2,1)S(1)} collective-permute-done((bf16[256,1024]{1,0:T(8,128)(2,1)S(1)}, bf16[256,1024]{1,0:T(8,128)(2,1)S(1)}, u32[]{:S(2)}, u32[]{:S(2)}) %collective-permute-start.33) | collective-permute-done | bytes 524320 | tf_op jit(solution)/shard_map/ppermute | solution.py:54
  284.4 6.1 %fusion.10 = (bf16[2,224,1024]{2,1,0:T(8,128)(2,1)}, bf16[2,224,1024]{2,1,0:T(8,128)(2,1)}, bf16[2,224,1024]{2,1,0:T(8,128)(2,1)}, bf16[2,224,1024]{2,1,0:T(8,128)(2,1)S(1)}) fusion(bf16[2,4,224,1024]{3,2,1,0:T(8,128)(2,1)} %bitcast.51, bf16[2,4,224,1024]{3,2,1,0:T(8,128)(2,1)} %bitcast.171), kind=kLoop, calls=%fused_computation.38 | loop fusion | flops 7340032 | bytes 11010048 | tf_op jit(solution)/shard_map/convert_element_type | solution.py:85
  290.5 5.3 %collective-permute-done.35.crossed = bf16[256,1024]{1,0:T(8,128)(2,1)S(1)} collective-permute-done((bf16[256,1024]{1,0:T(8,128)(2,1)S(1)}, bf16[256,1024]{1,0:T(8,128)(2,1)S(1)}, u32[]{:S(2)}, u32[]{:S(2)}) %collective-permute-start.35) | collective-permute-done | bytes 524320 | tf_op jit(solution)/shard_map/ppermute | solution.py:54
  296.6 5.9 %shard_map.185 = (f32[224,1024]{1,0:T(8,128)}, bf16[224,1024]{1,0:T(8,128)(2,1)}, bf16[32,224]{1,0:T(8,128)(2,1)}, bf16[224,1024]{1,0:T(8,128)(2,1)}, bf16[16,64,224]{2,1,0:T(8,128)(2,1)}) custom-call(bf16[256,1024]{1,0:T(8,128)(2,1)} %get-tuple-element.169.t0, bf16[256,1024]{1,0:T(8,128)(2,1)} %collective-permute-done.27.t1, ...), custom_call_target="tpu_custom_call" | custom-call | flops 469762048 | bytes 8388608 | tf_op jit(solution)/shard_map/pallas_call | solution.py:694
  302.5 4.7 all-to-all-start.3
  307.3 3.9 shard_map.186
  311.2 8.4 %all-to-all-done.3.g_ref = bf16[16,64,224]{2,1,0:T(8,128)(2,1)S(1)} async-done(((bf16[16,64,224]{2,1,0:T(8,128)(2,1)}), bf16[16,64,224]{2,1,0:T(8,128)(2,1)S(1)}, u32[]{:S(2)}, u32[]{:S(2)}) %all-to-all-start.3) | async-done | bytes 458784 | tf_op jit(solution)/shard_map/all_to_all | solution.py:848
  320.4 4.7 all-to-all-start.4
  327.9 31.0 %shard_map.187.first.second = bf16[3584,256]{1,0:T(8,128)(2,1)} custom-call(bf16[3584,256]{1,0:T(8,128)(2,1)} %shard_map.179.qkv_ref, bf16[16,64,224]{2,1,0:T(8,128)(2,1)} %copy-done.19, f32[64,3584]{1,0:T(8,128)} %get-tuple-element.199.ot_ref, f32[1,3584]{1,0:T(1,128)} %get-tuple-element.200.lse_ref, s32[1,3584]{1,0:T(1,128)} %compare_select_fusion.begin_ref, ...), custom_call_target="tpu_custom_call" | custom-call | flops 18119393280 | bytes 8388608 | tf_op jit(solution)/shard_map/pallas_call | solution.py:416
  358.9 10.8 %shard_map.188 = bf16[1024,256]{1,0:T(8,128)(2,1)} custom-call(s32[16]{0:T(128)} %copy-done.33, bf16[4,224,1024]{2,1,0:T(8,128)(2,1)} %copy-done.1, bf16[4,224,1024]{2,1,0:T(8,128)(2,1)} %collective-permute-done.7.other.near_other, bf16[4,224,1024]{2,1,0:T(8,128)(2,1)} %pad_maximum_fusion.3.mine.far_mine, ...), custom_call_target="tpu_custom_call" | custom-call | flops 1879048192 | bytes 10485760 | tf_op jit(solution)/shard_map/pallas_call | solution.py:251
  372.5 5.7 %shard_map.190 = (bf16[4,240,1024]{2,1,0:T(8,128)(2,1)}, bf16[4,240,1024]{2,1,0:T(8,128)(2,1)}) custom-call(s32[8]{0:T(128)} %get-tuple-element.268.places, bf16[3584,256]{1,0:T(8,128)(2,1)} %shard_map.187.first.second, bf16[3584,256]{1,0:T(8,128)(2,1)} %shard_map.187.first.second, bf16[1024,256]{1,0:T(8,128)(2,1)} %broadcast_select_fusion.w, ...), custom_call_target="tpu_custom_call" | custom-call | flops 939524096 | bytes 5242880 | tf_op jit(solution)/shard_map/pallas_call | solution.py:207
  378.3 5.8 %shard_map.189 = (bf16[4,240,1024]{2,1,0:T(8,128)(2,1)}, bf16[4,240,1024]{2,1,0:T(8,128)(2,1)}) custom-call(s32[8]{0:T(128)} %get-tuple-element.269.places, bf16[3584,256]{1,0:T(8,128)(2,1)} %shard_map.187.first.second, bf16[3584,256]{1,0:T(8,128)(2,1)} %shard_map.187.first.second, bf16[1024,256]{1,0:T(8,128)(2,1)} %broadcast_select_fusion.w, ...), custom_call_target="tpu_custom_call" | custom-call | flops 939524096 | bytes 5242880 | tf_op jit(solution)/shard_map/pallas_call | solution.py:207
  392.7 5.9 %collective-permute-done.41 = bf16[224,1024]{1,0:T(8,128)(2,1)S(1)} collective-permute-done((bf16[224,1024]{1,0:T(8,128)(2,1)S(1)}, bf16[224,1024]{1,0:T(8,128)(2,1)S(1)}, u32[]{:S(2)}, u32[]{:S(2)}) %collective-permute-start.41) | collective-permute-done | bytes 458784 | tf_op jit(solution)/shard_map/ppermute | solution.py:54
  405.4 9.8 %all-to-all-start.5 = ((bf16[128,8,256]{2,1,0:T(8,128)(2,1)}), bf16[128,8,256]{2,1,0:T(8,128)(2,1)S(1)}, u32[]{:S(2)}, u32[]{:S(2)}) async-start(bf16[128,8,256]{2,1,0:T(8,128)(2,1)} %bitcast.67), calls=%async_computation.6 | async-start | bytes 1048576 | tf_op jit(solution)/shard_map/all_to_all | solution.py:886
  418.0 15.5 %collective-permute-done.44 = bf16[2,128,1024]{2,1,0:T(8,128)(2,1)} collective-permute-done((bf16[2,128,1024]{2,1,0:T(8,128)(2,1)}, bf16[2,128,1024]{2,1,0:T(8,128)(2,1)}, u32[]{:S(2)}, u32[]{:S(2)}) %collective-permute-start.44) | collective-permute-done | bytes 524320 | tf_op jit(solution)/shard_map/ppermute | solution.py:54
  449.5 10.5 %collective-permute-done.49 = bf16[128,1024]{1,0:T(8,128)(2,1)S(1)} collective-permute-done((bf16[128,1024]{1,0:T(8,128)(2,1)S(1)}, bf16[128,1024]{1,0:T(8,128)(2,1)S(1)}, u32[]{:S(2)}, u32[]{:S(2)}) %collective-permute-start.49) | collective-permute-done | bytes 262176 | tf_op jit(solution)/shard_map/ppermute | solution.py:54
  (274 shorter events, 148.3 us)
Async XLA Ops:
  7.2 35.1 %collective-permute-start = (bf16[224,1024]{1,0:T(8,128)(2,1)}, bf16[224,1024]{1,0:T(8,128)(2,1)S(1)}, u32[]{:S(2)}, u32[]{:S(2)}) collective-permute-start(bf16[224,1024]{1,0:T(8,128)(2,1)} %bitcast.164), channel_id=1, source_target_pairs={{0,64},{8,72},{16,80},{24,88},{32,96},{40,104},{48,112},{56,120},{... | collective-permute-start | bytes 1376264 | tf_op jit(solution)/shard_map/ppermute | solution.py:54
  10.4 32.0 %collective-permute-start.4 = (bf16[224,1024]{1,0:T(8,128)(2,1)}, bf16[224,1024]{1,0:T(8,128)(2,1)S(1)}, u32[]{:S(2)}, u32[]{:S(2)}) collective-permute-start(bf16[224,1024]{1,0:T(8,128)(2,1)} %bitcast.165), channel_id=1, source_target_pairs={{0,16},{8,24},{16,32},{24,40},{32,48},{40,56},{48,0},{56,8},{64,80... | collective-permute-start | bytes 1376264 | tf_op jit(solution)/shard_map/ppermute | solution.py:54
  12.3 30.0 %collective-permute-start.5 = (bf16[224,1024]{1,0:T(8,128)(2,1)}, bf16[224,1024]{1,0:T(8,128)(2,1)S(1)}, u32[]{:S(2)}, u32[]{:S(2)}) collective-permute-start(bf16[224,1024]{1,0:T(8,128)(2,1)} %bitcast.166), channel_id=1, source_target_pairs={{0,48},{8,56},{16,0},{24,8},{32,16},{40,24},{48,32},{56,40},{64,11... | collective-permute-start | bytes 1376264 | tf_op jit(solution)/shard_map/ppermute | solution.py:54
  14.4 27.9 %collective-permute-start.6 = (bf16[224,1024]{1,0:T(8,128)(2,1)}, bf16[224,1024]{1,0:T(8,128)(2,1)}, u32[]{:S(2)}, u32[]{:S(2)}) collective-permute-start(bf16[224,1024]{1,0:T(8,128)(2,1)} %bitcast.167), channel_id=1, source_target_pairs={{0,32},{8,40},{16,48},{24,56},{32,0},{40,8},{48,16},{56,24},{64,96... | collective-permute-start | bytes 1376264 | tf_op jit(solution)/shard_map/ppermute | solution.py:54
  26.6 159.7 %all-gather.5.cloned.1.call-start = ((), (), s32[]{:S(2)}) async-start(), calls=%async_computation.8 | async-start | bytes 3932160 | tf_op jit(solution)/shard_map/all_gather | solution.py:782
  74.9 43.9 %all-to-all-start.1 = ((bf16[128,8,1152]{2,1,0:T(8,128)(2,1)}), bf16[128,8,1152]{2,1,0:T(8,128)(2,1)S(1)}, u32[]{:S(2)}, u32[]{:S(2)}) async-start(bf16[128,8,1152]{2,1,0:T(8,128)(2,1)} %broadcast_in_dim.101), calls=%async_computation.1 | async-start | bytes 4718592 | tf_op jit(solution)/shard_map/all_to_all | solution.py:790
  83.9 102.4 %all-gather.7.cloned.1.call-start = ((), (), s32[]{:S(2)}) async-start(), calls=%async_computation.9 | async-start | bytes 3932160 | tf_op jit(solution)/shard_map/all_gather | solution.py:782
  85.3 39.0 %collective-permute-start.10 = (bf16[240,1024]{1,0:T(8,128)(2,1)S(1)}, bf16[240,1024]{1,0:T(8,128)(2,1)}, u32[]{:S(2)}, u32[]{:S(2)}) collective-permute-start(bf16[240,1024]{1,0:T(8,128)(2,1)S(1)} %fusion.22), channel_id=1, source_target_pairs={{0,16},{8,24},{16,32},{24,40},{32,48},{40,56},{48,0},{56,8},{64,80... | collective-permute-start | bytes 1474568 | tf_op jit(solution)/shard_map/ppermute | solution.py:54
  86.4 37.9 %collective-permute-start.11 = (bf16[240,1024]{1,0:T(8,128)(2,1)S(1)}, bf16[240,1024]{1,0:T(8,128)(2,1)}, u32[]{:S(2)}, u32[]{:S(2)}) collective-permute-start(bf16[240,1024]{1,0:T(8,128)(2,1)S(1)} %fusion.22), channel_id=1, source_target_pairs={{0,48},{8,56},{16,0},{24,8},{32,16},{40,24},{48,32},{56,40},{64,11... | collective-permute-start | bytes 1474568 | tf_op jit(solution)/shard_map/ppermute | solution.py:54
  88.5 48.5 %collective-permute-start.12 = (bf16[240,1024]{1,0:T(8,128)(2,1)S(1)}, bf16[240,1024]{1,0:T(8,128)(2,1)}, u32[]{:S(2)}, u32[]{:S(2)}) collective-permute-start(bf16[240,1024]{1,0:T(8,128)(2,1)S(1)} %fusion.22), channel_id=1, source_target_pairs={{0,32},{8,40},{16,48},{24,56},{32,0},{40,8},{48,16},{56,24},{64,96... | collective-permute-start | bytes 1474568 | tf_op jit(solution)/shard_map/ppermute | solution.py:54
  124.2 309.3 %reduce-scatter.2.cloned.1.call-start = ((), (), s32[]{:S(2)}) async-start(), calls=%async_computation.7 | async-start | bytes 7864320 | tf_op jit(solution)/shard_map/reduce_scatter | solution.py:841
  141.3 31.5 %collective-permute-start.21 = (bf16[352,1024]{1,0:T(8,128)(2,1)S(1)}, bf16[352,1024]{1,0:T(8,128)(2,1)}, u32[]{:S(2)}, u32[]{:S(2)}) collective-permute-start(bf16[352,1024]{1,0:T(8,128)(2,1)S(1)} %slice.364), channel_id=1, source_target_pairs={{0,64},{8,72},{16,80},{24,88},{32,96},{40,104},{48,112},{56,120},{... | collective-permute-start | bytes 2162696 | tf_op jit(solution)/shard_map/ppermute | solution.py:54
  149.5 23.2 %collective-permute-start.18 = (bf16[224,1024]{1,0:T(8,128)(2,1)}, bf16[224,1024]{1,0:T(8,128)(2,1)S(1)}, u32[]{:S(2)}, u32[]{:S(2)}) collective-permute-start(bf16[224,1024]{1,0:T(8,128)(2,1)} %get-tuple-element.149.normed_ref), channel_id=1, source_target_pairs={{0,16},{8,24},{16,32},{24,40},{32,48},{40,56},{48,0},{56,8},{64,80... | collective-permute-start | bytes 1376264 | tf_op jit(solution)/shard_map/ppermute | solution.py:54
  150.1 22.6 %collective-permute-start.19 = (bf16[224,1024]{1,0:T(8,128)(2,1)}, bf16[224,1024]{1,0:T(8,128)(2,1)S(1)}, u32[]{:S(2)}, u32[]{:S(2)}) collective-permute-start(bf16[224,1024]{1,0:T(8,128)(2,1)} %get-tuple-element.149.normed_ref), channel_id=1, source_target_pairs={{0,48},{8,56},{16,0},{24,8},{32,16},{40,24},{48,32},{56,40},{64,11... | collective-permute-start | bytes 1376264 | tf_op jit(solution)/shard_map/ppermute | solution.py:54
  178.7 31.5 %collective-permute-start.22 = (bf16[608,1024]{1,0:T(8,128)(2,1)}, bf16[608,1024]{1,0:T(8,128)(2,1)S(1)}, u32[]{:S(2)}, u32[]{:S(2)}) collective-permute-start(bf16[608,1024]{1,0:T(8,128)(2,1)} %slice.281), channel_id=1, source_target_pairs={{0,64},{8,72},{16,80},{24,88},{32,96},{40,104},{48,112},{56,120},{... | collective-permute-start | bytes 3735560 | tf_op jit(solution)/shard_map/ppermute | solution.py:54
  181.4 30.2 %collective-permute-start.14 = (bf16[224,1024]{1,0:T(8,128)(2,1)}, bf16[224,1024]{1,0:T(8,128)(2,1)}, u32[]{:S(2)}, u32[]{:S(2)}) collective-permute-start(bf16[224,1024]{1,0:T(8,128)(2,1)} %copy-done.22), channel_id=1, source_target_pairs={{0,16},{8,24},{16,32},{24,40},{32,48},{40,56},{48,0},{56,8},{64,80... | collective-permute-start | bytes 1376264 | tf_op jit(solution)/shard_map/ppermute | solution.py:54
  182.3 29.3 %collective-permute-start.15 = (bf16[224,1024]{1,0:T(8,128)(2,1)}, bf16[224,1024]{1,0:T(8,128)(2,1)}, u32[]{:S(2)}, u32[]{:S(2)}) collective-permute-start(bf16[224,1024]{1,0:T(8,128)(2,1)} %copy-done.22), channel_id=1, source_target_pairs={{0,48},{8,56},{16,0},{24,8},{32,16},{40,24},{48,32},{56,40},{64,11... | collective-permute-start | bytes 1376264 | tf_op jit(solution)/shard_map/ppermute | solution.py:54
  184.7 27.0 %collective-permute-start.16 = (bf16[224,1024]{1,0:T(8,128)(2,1)}, bf16[224,1024]{1,0:T(8,128)(2,1)S(1)}, u32[]{:S(2)}, u32[]{:S(2)}) collective-permute-start(bf16[224,1024]{1,0:T(8,128)(2,1)} %copy-done.22), channel_id=1, source_target_pairs={{0,32},{8,40},{16,48},{24,56},{32,0},{40,8},{48,16},{56,24},{64,96... | collective-permute-start | bytes 1376264 | tf_op jit(solution)/shard_map/ppermute | solution.py:54
  216.7 28.5 %collective-permute-start.27 = (bf16[256,1024]{1,0:T(8,128)(2,1)}, bf16[256,1024]{1,0:T(8,128)(2,1)}, u32[]{:S(2)}, u32[]{:S(2)}) collective-permute-start(bf16[256,1024]{1,0:T(8,128)(2,1)} %get-tuple-element.252), channel_id=1, source_target_pairs={{0,48},{8,56},{16,0},{24,8},{32,16},{40,24},{48,32},{56,40},{64,11... | collective-permute-start | bytes 1572872 | tf_op jit(solution)/shard_map/ppermute | solution.py:54
  219.7 26.5 %collective-permute-start.28 = (bf16[256,1024]{1,0:T(8,128)(2,1)}, bf16[256,1024]{1,0:T(8,128)(2,1)}, u32[]{:S(2)}, u32[]{:S(2)}) collective-permute-start(bf16[256,1024]{1,0:T(8,128)(2,1)} %get-tuple-element.251), channel_id=1, source_target_pairs={{0,16},{8,24},{16,32},{24,40},{32,48},{40,56},{48,0},{56,8},{64,80... | collective-permute-start | bytes 1572872 | tf_op jit(solution)/shard_map/ppermute | solution.py:54
  219.7 26.5 %collective-permute-start.29 = (bf16[256,1024]{1,0:T(8,128)(2,1)}, bf16[256,1024]{1,0:T(8,128)(2,1)}, u32[]{:S(2)}, u32[]{:S(2)}) collective-permute-start(bf16[256,1024]{1,0:T(8,128)(2,1)} %get-tuple-element.250), channel_id=1, source_target_pairs={{0,32},{8,40},{16,48},{24,56},{32,0},{40,8},{48,16},{56,24},{64,96... | collective-permute-start | bytes 1572872 | tf_op jit(solution)/shard_map/ppermute | solution.py:54
  250.6 29.9 %collective-permute-start.34 = (bf16[8,224,1024]{2,1,0:T(8,128)(2,1)}, bf16[8,224,1024]{2,1,0:T(8,128)(2,1)}, u32[]{:S(2)}, u32[]{:S(2)}) collective-permute-start(bf16[8,224,1024]{2,1,0:T(8,128)(2,1)} %get-tuple-element.181), channel_id=1, source_target_pairs={{0,8},{8,0},{16,24},{24,16},{32,40},{40,32},{48,56},{56,48},{64,72... | collective-permute-start | bytes 11010056 | tf_op jit(solution)/shard_map/ppermute | solution.py:58
  255.3 25.2 %collective-permute-start.33 = (bf16[256,1024]{1,0:T(8,128)(2,1)S(1)}, bf16[256,1024]{1,0:T(8,128)(2,1)S(1)}, u32[]{:S(2)}, u32[]{:S(2)}) collective-permute-start(bf16[256,1024]{1,0:T(8,128)(2,1)S(1)} %get-tuple-element.246), channel_id=1, source_target_pairs={{0,32},{8,40},{16,48},{24,56},{32,0},{40,8},{48,16},{56,24},{64,96... | collective-permute-start | bytes 1572872 | tf_op jit(solution)/shard_map/ppermute | solution.py:54
  320.4 49.3 %all-to-all-start.4 = ((bf16[8,128,1152]{2,1,0:T(8,128)(2,1)}), bf16[8,128,1152]{2,1,0:T(8,128)(2,1)S(1)}, u32[]{:S(2)}, u32[]{:S(2)}) async-start(bf16[8,128,1152]{2,1,0:T(8,128)(2,1)} %shard_map.186), calls=%async_computation.4 | async-start | bytes 4718592 | tf_op jit(solution)/shard_map/all_to_all | solution.py:855
  325.2 44.6 %collective-permute-start.36 = (bf16[2,224,1024]{2,1,0:T(8,128)(2,1)}, bf16[2,224,1024]{2,1,0:T(8,128)(2,1)}, u32[]{:S(2)}, u32[]{:S(2)}) collective-permute-start(bf16[2,224,1024]{2,1,0:T(8,128)(2,1)} %get-tuple-element.202), channel_id=1, source_target_pairs={{0,48},{8,56},{16,0},{24,8},{32,16},{40,24},{48,32},{56,40},{64,11... | collective-permute-start | bytes 2752520 | tf_op jit(solution)/shard_map/ppermute | solution.py:54
  326.1 43.6 %collective-permute-start.37 = (bf16[2,224,1024]{2,1,0:T(8,128)(2,1)}, bf16[2,224,1024]{2,1,0:T(8,128)(2,1)}, u32[]{:S(2)}, u32[]{:S(2)}) collective-permute-start(bf16[2,224,1024]{2,1,0:T(8,128)(2,1)} %get-tuple-element.203), channel_id=1, source_target_pairs={{0,16},{8,24},{16,32},{24,40},{32,48},{40,56},{48,0},{56,8},{64,80... | collective-permute-start | bytes 2752520 | tf_op jit(solution)/shard_map/ppermute | solution.py:54
  327.2 42.6 %collective-permute-start.38 = (bf16[2,224,1024]{2,1,0:T(8,128)(2,1)}, bf16[2,224,1024]{2,1,0:T(8,128)(2,1)}, u32[]{:S(2)}, u32[]{:S(2)}) collective-permute-start(bf16[2,224,1024]{2,1,0:T(8,128)(2,1)} %get-tuple-element.204), channel_id=1, source_target_pairs={{0,32},{8,40},{16,48},{24,56},{32,0},{40,8},{48,16},{56,24},{64,96... | collective-permute-start | bytes 2752520 | tf_op jit(solution)/shard_map/ppermute | solution.py:54
  399.3 34.1 %collective-permute-start.42 = (bf16[4,112,1024]{2,1,0:T(8,128)(2,1)}, bf16[4,112,1024]{2,1,0:T(8,128)(2,1)}, u32[]{:S(2)}, u32[]{:S(2)}) collective-permute-start(bf16[4,112,1024]{2,1,0:T(8,128)(2,1)} %add_convert_fusion), channel_id=1, source_target_pairs={{0,64},{8,72},{16,80},{24,88},{32,96},{40,104},{48,112},{56,120},{... | collective-permute-start | bytes 2752520 | tf_op jit(solution)/shard_map/ppermute | solution.py:54
  402.6 30.8 %collective-permute-start.44 = (bf16[2,128,1024]{2,1,0:T(8,128)(2,1)}, bf16[2,128,1024]{2,1,0:T(8,128)(2,1)}, u32[]{:S(2)}, u32[]{:S(2)}) collective-permute-start(bf16[2,128,1024]{2,1,0:T(8,128)(2,1)} %pad_maximum_fusion.9), channel_id=1, source_target_pairs={{0,16},{8,24},{16,32},{24,40},{32,48},{40,56},{48,0},{56,8},{64,80... | collective-permute-start | bytes 1572872 | tf_op jit(solution)/shard_map/ppermute | solution.py:54
  403.2 30.2 %collective-permute-start.45 = (bf16[2,128,1024]{2,1,0:T(8,128)(2,1)}, bf16[2,128,1024]{2,1,0:T(8,128)(2,1)}, u32[]{:S(2)}, u32[]{:S(2)}) collective-permute-start(bf16[2,128,1024]{2,1,0:T(8,128)(2,1)} %pad_maximum_fusion.10), channel_id=1, source_target_pairs={{0,32},{8,40},{16,48},{24,56},{32,0},{40,8},{48,16},{56,24},{64,96... | collective-permute-start | bytes 1572872 | tf_op jit(solution)/shard_map/ppermute | solution.py:54
  405.4 44.0 %all-to-all-start.5 = ((bf16[128,8,256]{2,1,0:T(8,128)(2,1)}), bf16[128,8,256]{2,1,0:T(8,128)(2,1)S(1)}, u32[]{:S(2)}, u32[]{:S(2)}) async-start(bf16[128,8,256]{2,1,0:T(8,128)(2,1)} %bitcast.67), calls=%async_computation.6 | async-start | bytes 1048576 | tf_op jit(solution)/shard_map/all_to_all | solution.py:886
  434.7 35.1 %collective-permute-start.50 = (bf16[2,192,1024]{2,1,0:T(8,128)(2,1)S(1)}, bf16[2,192,1024]{2,1,0:T(8,128)(2,1)}, u32[]{:S(2)}, u32[]{:S(2)}) collective-permute-start(bf16[2,192,1024]{2,1,0:T(8,128)(2,1)S(1)} %dynamic-slice_bitcast_fusion), channel_id=1, source_target_pairs={{0,1},{1,0},{2,3},{3,2},{4,5},{5,4},{6,7},{7,6},{8,9},{9,8},{10,11... | collective-permute-start | bytes 2359304 | tf_op jit(solution)/shard_map/ppermute | solution.py:101
  (68 other events, 752.8 us)
Sparse Core Ops, SparseCore 0:
  29.1 40.6 all-gather.4
  86.4 50.9 all-gather.6
  280.7 89.0 reduce-scatter.1

commit v20 on v14

--- a/solution.py
+++ b/solution.py
@@ -856,12 +856,12 @@
     far_part = project_back(places[8:], projected_grad, head_weights, shared_grads)
     near_part = project_back(places[:8], projected_grad, head_weights, shared_grads)
     far_parts = chip_parts(far_part[0], swap_cores(far_part[1]))
-    near_part, moved_terms, expert_grads = tie(near_part, moved_terms, expert_grads)
+    near_part, moved_terms = tie(near_part, moved_terms)
     near_parts = chip_parts(near_part[0], swap_cores(near_part[1]))
-    far_parts, near_parts, projected_grad, moved_terms, expert_grads = tie(
-        far_parts, near_parts, projected_grad, moved_terms, expert_grads
-    )
-    far_terms = send_along_z(far_parts)
+    far_parts, near_parts, projected_grad, moved_terms = tie(
+        far_parts, near_parts, projected_grad, moved_terms
+    )
+    far_terms, expert_grads = tie(send_along_z(far_parts), expert_grads)
     near_terms = send_along_z(near_parts)
     moved_crossed = send(add_low(*[t[1] for t in moved_terms]), 1, 0)
     grad_head = head_weight_grad(places, rows_near, rows_far, gain_attn, projected_grad)

time: 470 us -> 466 us (level)
  transfers between devices with their start and end apart: 59 -> 59, of which waited for: 17 -> 16; matrix products, arithmetic and copies ran while one was open for 14% -> 14% of each run, Pallas kernels for 35% -> 36%
where the time goes in v20:
time: 466 us; the launch traced here: 457 us
  Pallas kernels  163 us (35%)
  waiting for transfers between devices  109 us (23%)
  starting transfers between devices  97.3 us (21%)
  other arithmetic  52.9 us (11%)
  local copies, waits for them, and re-layouts  20.2 us (4%)
  between operations  14.9 us (3%)
    ppermute x37, waiting for transfers between devices, send(): return lax.ppermute(rows, 'seq', shift_perm(a, b))  71.8 us
    ppermute x37, starting transfers between devices, send(): return lax.ppermute(rows, 'seq', shift_perm(a, b))  56.9 us
    pallas_call x2, Pallas kernels, run_experts(): pl.pallas_call(experts_kernel, grid_spec=pltpu.PrefetchScalarGridSpec(num...  44 us
    pallas_call x1, Pallas kernels, attend_back(): pl.pallas_call(attend_back_kernel, grid=(GROUP // BLOCK,), in_specs=[whol...  31.1 us
    pallas_call x1, Pallas kernels, attend(): pl.pallas_call(attend_kernel, grid=(GROUP // BLOCK,), in_specs=[whole(GRO...  19.8 us
    convert_element_type x7, other arithmetic, add_low(): return sum([t.astype(f32) for t in terms]).astype(bf16)  18.4 us
    pallas_call x2, Pallas kernels, project(): pl.pallas_call(project_kernel, grid_spec=pltpu.PrefetchScalarGridSpec(num...  16.7 us
    pallas_call x1, Pallas kernels, expert_weight_grads(): pl.pallas_call(expert_grads_kernel, grid=(2, 4), in_specs=[pl.BlockSpec((...  15.9 us
  transfers between devices with their start and end apart: 59, of which 16 were waited for; matrix products, arithmetic and copies ran while one was open for 14% of the time, Pallas kernels for 36%

profile of v20, /device:TPU:0, one launch (start us, length us, event | category | flops | bytes accessed | tf_op | source)
XLA Modules:
  0.0 457.0 jit_solution(15044724086027186236)
XLA Ops:
  19.8 6.8 %all-to-all-start = ((bf16[128,8,256]{2,1,0:T(8,128)(2,1)}), bf16[128,8,256]{2,1,0:T(8,128)(2,1)S(1)}, u32[]{:S(2)}, u32[]{:S(2)}) async-start(bf16[128,8,256]{2,1,0:T(8,128)(2,1)} %bitcast.9), calls=%async_computation | async-start | bytes 1048576 | tf_op jit(solution)/shard_map/all_to_all | solution.py:771
  28.7 7.7 %subtract_cosine_fusion.table = f32[3584,128]{1,0:T(8,128)} fusion(f32[128]{0:T(128)S(1)} %get-tuple-element.279, f32[128]{0:T(128)S(1)} %get-tuple-element.280, f32[3584]{0:T(1024)S(1)} %get-tuple-element.274), kind=kLoop, calls=%fused_computation.10 | loop fusion | flops 917504 | bytes 1850368 | tf_op jit(solution)/shard_map/cos | solution.py:138
  36.4 5.1 %all-to-all-done = bf16[128,8,256]{2,1,0:T(8,128)(2,1)S(1)} async-done(((bf16[128,8,256]{2,1,0:T(8,128)(2,1)}), bf16[128,8,256]{2,1,0:T(8,128)(2,1)S(1)}, u32[]{:S(2)}, u32[]{:S(2)}) %all-to-all-start) | async-done | bytes 524320 | tf_op jit(solution)/shard_map/all_to_all | solution.py:771
  51.6 8.0 %shard_map.178.refs_0_ = bf16[3584,256]{1,0:T(8,128)(2,1)} custom-call(s32[8]{0:T(128)} %get-tuple-element.277.places, bf16[4,224,1024]{2,1,0:T(8,128)(2,1)} %copy-done.1, bf16[4,224,1024]{2,1,0:T(8,128)(2,1)} %collective-permute-done.7.other.near_other, bf16[1024,256]{1,0:T(8,128)(2,1)} %broadcast_select_fusion.w, f32[1,1024]{1,0:T(1,128)} %bitcast.187, ...), custom_call_target="tpu_custom_call" | custom-call | flops 939524096 | bytes 10485760 | tf_op jit(solution)/shard_map/pallas_call | solution.py:175
  59.6 6.0 %collective-permute-done.8 = bf16[2,192,1024]{2,1,0:T(8,128)(2,1)} collective-permute-done((bf16[2,192,1024]{2,1,0:T(8,128)(2,1)}, bf16[2,192,1024]{2,1,0:T(8,128)(2,1)}, u32[]{:S(2)}, u32[]{:S(2)}) %collective-permute-start.8) | collective-permute-done | bytes 786464 | tf_op jit(solution)/shard_map/ppermute | solution.py:100
  65.5 3.8 collective-permute-done.2
  74.3 9.0 %all-to-all-start.1 = ((bf16[128,8,1152]{2,1,0:T(8,128)(2,1)}), bf16[128,8,1152]{2,1,0:T(8,128)(2,1)S(1)}, u32[]{:S(2)}, u32[]{:S(2)}) async-start(bf16[128,8,1152]{2,1,0:T(8,128)(2,1)} %broadcast_in_dim.101), calls=%async_computation.1 | async-start | bytes 4718592 | tf_op jit(solution)/shard_map/all_to_all | solution.py:789
  89.7 8.7 %shard_map.179.qkv_ref = bf16[3584,256]{1,0:T(8,128)(2,1)} custom-call(s32[8]{0:T(128)} %get-tuple-element.278.places, bf16[4,224,1024]{2,1,0:T(8,128)(2,1)} %pad_maximum_fusion.2.mine.far_mine, bf16[4,224,1024]{2,1,0:T(8,128)(2,1)} %collective-permute-done.9.other.far_other, bf16[1024,256]{1,0:T(8,128)(2,1)} %broadcast_select_fusion.w, ...), custom_call_target="tpu_custom_call" | custom-call | flops 939524096 | bytes 10485760 | tf_op jit(solution)/shard_map/pallas_call | solution.py:175
  98.4 19.8 %shard_map.180 = (bf16[16,64,224]{2,1,0:T(8,128)(2,1)}, f32[64,3584]{1,0:T(8,128)}, f32[1,3584]{1,0:T(1,128)}) custom-call(bf16[3584,256]{1,0:T(8,128)(2,1)} %shard_map.179.qkv_ref, s32[1,3584]{1,0:T(1,128)} %compare_select_fusion.begin_ref), custom_call_target="tpu_custom_call" | custom-call | flops 7247757312 | bytes 4194304 | tf_op jit(solution)/shard_map/pallas_call | solution.py:335
  118.2 5.3 %all-to-all-start.2 = ((bf16[16,64,224]{2,1,0:T(8,128)(2,1)}), bf16[16,64,224]{2,1,0:T(8,128)(2,1)S(1)}, u32[]{:S(2)}, u32[]{:S(2)}) async-start(bf16[16,64,224]{2,1,0:T(8,128)(2,1)} %get-tuple-element.142), calls=%async_computation.2 | async-start | bytes 1048576 | tf_op jit(solution)/shard_map/all_to_all | solution.py:804
  123.6 12.8 %collective-permute-done.12 = bf16[240,1024]{1,0:T(8,128)(2,1)} collective-permute-done((bf16[240,1024]{1,0:T(8,128)(2,1)S(1)}, bf16[240,1024]{1,0:T(8,128)(2,1)}, u32[]{:S(2)}, u32[]{:S(2)}) %collective-permute-start.12) | collective-permute-done | bytes 491552 | tf_op jit(solution)/shard_map/ppermute | solution.py:53
  144.6 3.6 shard_map.181
  154.0 22.4 %collective-permute-done.13 = bf16[224,1024]{1,0:T(8,128)(2,1)S(1)} collective-permute-done((bf16[224,1024]{1,0:T(8,128)(2,1)}, bf16[224,1024]{1,0:T(8,128)(2,1)S(1)}, u32[]{:S(2)}, u32[]{:S(2)}) %collective-permute-start.13) | collective-permute-done | bytes 458784 | tf_op jit(solution)/shard_map/ppermute | solution.py:53
  188.4 21.9 %shard_map.182 = (bf16[4,256,1024]{2,1,0:T(8,128)(2,1)}, bf16[4,256,1024]{2,1,0:T(8,128)(2,1)}, bf16[8,224,1024]{2,1,0:T(8,128)(2,1)}, bf16[8,224,1024]{2,1,0:T(...) custom-call(s32[2]{0:T(128)} %pad_add_fusion.own_ref, ...), custom_call_target="tpu_custom_call" | custom-call | flops 15032385536 | bytes 25165824 | tf_op jit(solution)/shard_map/pallas_call | solution.py:566
  223.7 22.1 %shard_map.183 = (bf16[4,256,1024]{2,1,0:T(8,128)(2,1)}, bf16[4,256,1024]{2,1,0:T(8,128)(2,1)}, bf16[8,224,1024]{2,1,0:T(8,128)(2,1)}, bf16[8,224,1024]{2,1,0:T(...) custom-call(s32[2]{0:T(128)} %pad_add_fusion.own_ref, ...), custom_call_target="tpu_custom_call", output_to_operand_aliasing={{2}: (10, {}), {3}: (11, {}), {4}: (12, {}), {5}: (13, {}),... | custom-call | flops 15032385536 | bytes 25165824 | tf_op jit(solution)/shard_map/pallas_call | solution.py:566
  245.9 4.4 collective-permute-done.30
  256.3 15.9 %shard_map.184 = bf16[4,2,2,192,1024]{4,3,2,1,0:T(8,128)(2,1)} custom-call(bf16[2,1152,1024]{2,1,0:T(8,128)(2,1)} %get-tuple-element.183.x_ref, bf16[2,1152,1024]{2,1,0:T(8,128)(2,1)} %get-tuple-element.184.dh_ref, bf16[2,1152,512]{2,1,0:T(8,128)(2,1)} %get-tuple-element.185.act_ref, bf16[2,1152,1024]{2,1,0:T(8,128)(2,1)} %get-tuple-element.186.dy_ref), custom_call_target="tpu_custom_call" | custom-call | flops 8589934592 | bytes 14680064 | tf_op jit(solution)/shard_map/pallas_call | solution.py:622
  272.2 7.8 %collective-permute-done.32 = bf16[256,1024]{1,0:T(8,128)(2,1)S(1)} collective-permute-done((bf16[256,1024]{1,0:T(8,128)(2,1)S(1)}, bf16[256,1024]{1,0:T(8,128)(2,1)S(1)}, u32[]{:S(2)}, u32[]{:S(2)}) %collective-permute-start.32) | collective-permute-done | bytes 524320 | tf_op jit(solution)/shard_map/ppermute | solution.py:53
  282.2 6.1 %fusion.10 = (bf16[2,224,1024]{2,1,0:T(8,128)(2,1)}, bf16[2,224,1024]{2,1,0:T(8,128)(2,1)}, bf16[2,224,1024]{2,1,0:T(8,128)(2,1)}, bf16[2,224,1024]{2,1,0:T(8,128)(2,1)S(1)}) fusion(bf16[2,4,224,1024]{3,2,1,0:T(8,128)(2,1)} %bitcast.49, bf16[2,4,224,1024]{3,2,1,0:T(8,128)(2,1)} %bitcast.170), kind=kLoop, calls=%fused_computation.47 | loop fusion | flops 7340032 | bytes 11010048 | tf_op jit(solution)/shard_map/convert_element_type | solution.py:84
  288.4 6.3 %collective-permute-done.35.crossed = bf16[256,1024]{1,0:T(8,128)(2,1)S(1)} collective-permute-done((bf16[256,1024]{1,0:T(8,128)(2,1)S(1)}, bf16[256,1024]{1,0:T(8,128)(2,1)S(1)}, u32[]{:S(2)}, u32[]{:S(2)}) %collective-permute-start.35) | collective-permute-done | bytes 524320 | tf_op jit(solution)/shard_map/ppermute | solution.py:53
  295.5 5.8 %shard_map.185 = (f32[224,1024]{1,0:T(8,128)}, bf16[224,1024]{1,0:T(8,128)(2,1)}, bf16[32,224]{1,0:T(8,128)(2,1)}, bf16[224,1024]{1,0:T(8,128)(2,1)}, bf16[16,64,224]{2,1,0:T(8,128)(2,1)}) custom-call(bf16[256,1024]{1,0:T(8,128)(2,1)} %get-tuple-element.175.t0, bf16[256,1024]{1,0:T(8,128)(2,1)} %copy-done.16, bf16[256,1024]{1,0:T(8,128)(2,1)} %copy-done.17, ...), custom_call_target="tpu_custom_call" | custom-call | flops 469762048 | bytes 8388608 | tf_op jit(solution)/shard_map/pallas_call | solution.py:693
  301.4 3.8 all-to-all-start.3
  305.2 3.9 shard_map.186
  309.1 8.4 %all-to-all-done.3.g_ref = bf16[16,64,224]{2,1,0:T(8,128)(2,1)S(1)} async-done(((bf16[16,64,224]{2,1,0:T(8,128)(2,1)}), bf16[16,64,224]{2,1,0:T(8,128)(2,1)S(1)}, u32[]{:S(2)}, u32[]{:S(2)}) %all-to-all-start.3) | async-done | bytes 458784 | tf_op jit(solution)/shard_map/all_to_all | solution.py:846
  318.4 5.1 %all-to-all-start.4 = ((bf16[8,128,1152]{2,1,0:T(8,128)(2,1)}), bf16[8,128,1152]{2,1,0:T(8,128)(2,1)S(1)}, u32[]{:S(2)}, u32[]{:S(2)}) async-start(bf16[8,128,1152]{2,1,0:T(8,128)(2,1)} %shard_map.186), calls=%async_computation.4 | async-start | bytes 4718592 | tf_op jit(solution)/shard_map/all_to_all | solution.py:853
  326.0 31.1 %shard_map.187.first.second = bf16[3584,256]{1,0:T(8,128)(2,1)} custom-call(bf16[3584,256]{1,0:T(8,128)(2,1)} %shard_map.179.qkv_ref, bf16[16,64,224]{2,1,0:T(8,128)(2,1)} %copy-done.21, f32[64,3584]{1,0:T(8,128)} %get-tuple-element.204.ot_ref, f32[1,3584]{1,0:T(1,128)} %get-tuple-element.205.lse_ref, s32[1,3584]{1,0:T(1,128)} %compare_select_fusion.begin_ref, ...), custom_call_target="tpu_custom_call" | custom-call | flops 18119393280 | bytes 8388608 | tf_op jit(solution)/shard_map/pallas_call | solution.py:415
  357.0 9.0 %all-to-all-done.4 = bf16[8,128,1152]{2,1,0:T(8,128)(2,1)S(1)} async-done(((bf16[8,128,1152]{2,1,0:T(8,128)(2,1)}), bf16[8,128,1152]{2,1,0:T(8,128)(2,1)S(1)}, u32[]{:S(2)}, u32[]{:S(2)}) %all-to-all-start.4) | async-done | bytes 2359328 | tf_op jit(solution)/shard_map/all_to_all | solution.py:853
  367.2 5.7 %shard_map.189 = (bf16[4,240,1024]{2,1,0:T(8,128)(2,1)}, bf16[4,240,1024]{2,1,0:T(8,128)(2,1)}) custom-call(s32[8]{0:T(128)} %get-tuple-element.277.places, bf16[3584,256]{1,0:T(8,128)(2,1)} %shard_map.187.first.second, bf16[3584,256]{1,0:T(8,128)(2,1)} %shard_map.187.first.second, bf16[1024,256]{1,0:T(8,128)(2,1)} %broadcast_select_fusion.w, ...), custom_call_target="tpu_custom_call" | custom-call | flops 939524096 | bytes 5242880 | tf_op jit(solution)/shard_map/pallas_call | solution.py:206
  373.3 5.9 %shard_map.188 = (bf16[4,240,1024]{2,1,0:T(8,128)(2,1)}, bf16[4,240,1024]{2,1,0:T(8,128)(2,1)}) custom-call(s32[8]{0:T(128)} %get-tuple-element.278.places, bf16[3584,256]{1,0:T(8,128)(2,1)} %shard_map.187.first.second, bf16[3584,256]{1,0:T(8,128)(2,1)} %shard_map.187.first.second, bf16[1024,256]{1,0:T(8,128)(2,1)} %broadcast_select_fusion.w, ...), custom_call_target="tpu_custom_call" | custom-call | flops 939524096 | bytes 5242880 | tf_op jit(solution)/shard_map/pallas_call | solution.py:206
  392.5 10.8 %shard_map.190 = bf16[1024,256]{1,0:T(8,128)(2,1)} custom-call(s32[16]{0:T(128)} %copy-done.34, bf16[4,224,1024]{2,1,0:T(8,128)(2,1)} %copy-done.1, bf16[4,224,1024]{2,1,0:T(8,128)(2,1)} %collective-permute-done.7.other.near_other, bf16[4,224,1024]{2,1,0:T(8,128)(2,1)} %pad_maximum_fusion.2.mine.far_mine, ...), custom_call_target="tpu_custom_call" | custom-call | flops 1879048192 | bytes 10485760 | tf_op jit(solution)/shard_map/pallas_call | solution.py:250
  403.3 6.2 %all-to-all-start.5 = ((bf16[128,8,256]{2,1,0:T(8,128)(2,1)}), bf16[128,8,256]{2,1,0:T(8,128)(2,1)S(1)}, u32[]{:S(2)}, u32[]{:S(2)}) async-start(bf16[128,8,256]{2,1,0:T(8,128)(2,1)} %bitcast.172), calls=%async_computation.6 | async-start | bytes 1048576 | tf_op jit(solution)/shard_map/all_to_all | solution.py:868
  423.3 14.6 %collective-permute-done.46 = bf16[240,1024]{1,0:T(8,128)(2,1)} collective-permute-done((bf16[240,1024]{1,0:T(8,128)(2,1)}, bf16[240,1024]{1,0:T(8,128)(2,1)}, u32[]{:S(2)}, u32[]{:S(2)}) %collective-permute-start.46) | collective-permute-done | bytes 491552 | tf_op jit(solution)/shard_map/ppermute | solution.py:53
  (268 shorter events, 128.4 us)
Async XLA Ops:
  7.2 35.1 %collective-permute-start = (bf16[224,1024]{1,0:T(8,128)(2,1)}, bf16[224,1024]{1,0:T(8,128)(2,1)S(1)}, u32[]{:S(2)}, u32[]{:S(2)}) collective-permute-start(bf16[224,1024]{1,0:T(8,128)(2,1)} %bitcast.161), channel_id=1, source_target_pairs={{0,64},{8,72},{16,80},{24,88},{32,96},{40,104},{48,112},{56,120},{... | collective-permute-start | bytes 1376264 | tf_op jit(solution)/shard_map/ppermute | solution.py:53
  10.4 32.0 %collective-permute-start.4 = (bf16[224,1024]{1,0:T(8,128)(2,1)}, bf16[224,1024]{1,0:T(8,128)(2,1)S(1)}, u32[]{:S(2)}, u32[]{:S(2)}) collective-permute-start(bf16[224,1024]{1,0:T(8,128)(2,1)} %bitcast.162), channel_id=1, source_target_pairs={{0,16},{8,24},{16,32},{24,40},{32,48},{40,56},{48,0},{56,8},{64,80... | collective-permute-start | bytes 1376264 | tf_op jit(solution)/shard_map/ppermute | solution.py:53
  12.3 30.1 %collective-permute-start.5 = (bf16[224,1024]{1,0:T(8,128)(2,1)}, bf16[224,1024]{1,0:T(8,128)(2,1)S(1)}, u32[]{:S(2)}, u32[]{:S(2)}) collective-permute-start(bf16[224,1024]{1,0:T(8,128)(2,1)} %bitcast.163), channel_id=1, source_target_pairs={{0,48},{8,56},{16,0},{24,8},{32,16},{40,24},{48,32},{56,40},{64,11... | collective-permute-start | bytes 1376264 | tf_op jit(solution)/shard_map/ppermute | solution.py:53
  14.4 28.0 %collective-permute-start.6 = (bf16[224,1024]{1,0:T(8,128)(2,1)}, bf16[224,1024]{1,0:T(8,128)(2,1)S(1)}, u32[]{:S(2)}, u32[]{:S(2)}) collective-permute-start(bf16[224,1024]{1,0:T(8,128)(2,1)} %bitcast.164), channel_id=1, source_target_pairs={{0,32},{8,40},{16,48},{24,56},{32,0},{40,8},{48,16},{56,24},{64,96... | collective-permute-start | bytes 1376264 | tf_op jit(solution)/shard_map/ppermute | solution.py:53
  26.6 161.8 %all-gather.5.cloned.1.call-start = ((), (), s32[]{:S(2)}) async-start(), calls=%async_computation.8 | async-start | bytes 3932160 | tf_op jit(solution)/shard_map/all_gather | solution.py:781
  74.3 43.9 %all-to-all-start.1 = ((bf16[128,8,1152]{2,1,0:T(8,128)(2,1)}), bf16[128,8,1152]{2,1,0:T(8,128)(2,1)S(1)}, u32[]{:S(2)}, u32[]{:S(2)}) async-start(bf16[128,8,1152]{2,1,0:T(8,128)(2,1)} %broadcast_in_dim.101), calls=%async_computation.1 | async-start | bytes 4718592 | tf_op jit(solution)/shard_map/all_to_all | solution.py:789
  83.3 105.1 %all-gather.7.cloned.1.call-start = ((), (), s32[]{:S(2)}) async-start(), calls=%async_computation.9 | async-start | bytes 3932160 | tf_op jit(solution)/shard_map/all_gather | solution.py:781
  84.7 39.0 %collective-permute-start.10 = (bf16[240,1024]{1,0:T(8,128)(2,1)S(1)}, bf16[240,1024]{1,0:T(8,128)(2,1)}, u32[]{:S(2)}, u32[]{:S(2)}) collective-permute-start(bf16[240,1024]{1,0:T(8,128)(2,1)S(1)} %fusion.21), channel_id=1, source_target_pairs={{0,16},{8,24},{16,32},{24,40},{32,48},{40,56},{48,0},{56,8},{64,80... | collective-permute-start | bytes 1474568 | tf_op jit(solution)/shard_map/ppermute | solution.py:53
  85.7 37.9 %collective-permute-start.11 = (bf16[240,1024]{1,0:T(8,128)(2,1)S(1)}, bf16[240,1024]{1,0:T(8,128)(2,1)}, u32[]{:S(2)}, u32[]{:S(2)}) collective-permute-start(bf16[240,1024]{1,0:T(8,128)(2,1)S(1)} %fusion.21), channel_id=1, source_target_pairs={{0,48},{8,56},{16,0},{24,8},{32,16},{40,24},{48,32},{56,40},{64,11... | collective-permute-start | bytes 1474568 | tf_op jit(solution)/shard_map/ppermute | solution.py:53
  87.9 48.5 %collective-permute-start.12 = (bf16[240,1024]{1,0:T(8,128)(2,1)S(1)}, bf16[240,1024]{1,0:T(8,128)(2,1)}, u32[]{:S(2)}, u32[]{:S(2)}) collective-permute-start(bf16[240,1024]{1,0:T(8,128)(2,1)S(1)} %fusion.21), channel_id=1, source_target_pairs={{0,32},{8,40},{16,48},{24,56},{32,0},{40,8},{48,16},{56,24},{64,96... | collective-permute-start | bytes 1474568 | tf_op jit(solution)/shard_map/ppermute | solution.py:53
  123.6 290.8 %reduce-scatter.2.cloned.1.call-start = ((), (), s32[]{:S(2)}) async-start(), calls=%async_computation.7 | async-start | bytes 7864320 | tf_op jit(solution)/shard_map/reduce_scatter | solution.py:839
  141.1 35.3 %collective-permute-start.21 = (bf16[2,240,1024]{2,1,0:T(8,128)(2,1)}, bf16[2,240,1024]{2,1,0:T(8,128)(2,1)}, u32[]{:S(2)}, u32[]{:S(2)}) collective-permute-start(bf16[2,240,1024]{2,1,0:T(8,128)(2,1)} %pad_maximum_fusion.5), channel_id=1, source_target_pairs={{0,64},{8,72},{16,80},{24,88},{32,96},{40,104},{48,112},{56,120},{... | collective-permute-start | bytes 2949128 | tf_op jit(solution)/shard_map/ppermute | solution.py:53
  148.2 28.2 %collective-permute-start.13 = (bf16[224,1024]{1,0:T(8,128)(2,1)}, bf16[224,1024]{1,0:T(8,128)(2,1)S(1)}, u32[]{:S(2)}, u32[]{:S(2)}) collective-permute-start(bf16[224,1024]{1,0:T(8,128)(2,1)} %get-tuple-element.155.normed_ref), channel_id=1, source_target_pairs={{0,64},{8,72},{16,80},{24,88},{32,96},{40,104},{48,112},{56,120},{... | collective-permute-start | bytes 1376264 | tf_op jit(solution)/shard_map/ppermute | solution.py:53
  149.1 27.3 %collective-permute-start.18 = (bf16[224,1024]{1,0:T(8,128)(2,1)}, bf16[224,1024]{1,0:T(8,128)(2,1)S(1)}, u32[]{:S(2)}, u32[]{:S(2)}) collective-permute-start(bf16[224,1024]{1,0:T(8,128)(2,1)} %get-tuple-element.155.normed_ref), channel_id=1, source_target_pairs={{0,16},{8,24},{16,32},{24,40},{32,48},{40,56},{48,0},{56,8},{64,80... | collective-permute-start | bytes 1376264 | tf_op jit(solution)/shard_map/ppermute | solution.py:53
  181.7 30.0 %collective-permute-start.22 = (bf16[2,240,1024]{2,1,0:T(8,128)(2,1)}, bf16[2,240,1024]{2,1,0:T(8,128)(2,1)S(1)}, u32[]{:S(2)}, u32[]{:S(2)}) collective-permute-start(bf16[2,240,1024]{2,1,0:T(8,128)(2,1)} %slice.213), channel_id=1, source_target_pairs={{0,64},{8,72},{16,80},{24,88},{32,96},{40,104},{48,112},{56,120},{... | collective-permute-start | bytes 2949128 | tf_op jit(solution)/shard_map/ppermute | solution.py:53
  184.4 27.9 %collective-permute-start.14 = (bf16[224,1024]{1,0:T(8,128)(2,1)S(1)}, bf16[224,1024]{1,0:T(8,128)(2,1)}, u32[]{:S(2)}, u32[]{:S(2)}) collective-permute-start(bf16[224,1024]{1,0:T(8,128)(2,1)S(1)} %collective-permute-done.13), channel_id=1, source_target_pairs={{0,16},{8,24},{16,32},{24,40},{32,48},{40,56},{48,0},{56,8},{64,80... | collective-permute-start | bytes 1376264 | tf_op jit(solution)/shard_map/ppermute | solution.py:53
  185.3 27.0 %collective-permute-start.15 = (bf16[224,1024]{1,0:T(8,128)(2,1)S(1)}, bf16[224,1024]{1,0:T(8,128)(2,1)}, u32[]{:S(2)}, u32[]{:S(2)}) collective-permute-start(bf16[224,1024]{1,0:T(8,128)(2,1)S(1)} %collective-permute-done.13), channel_id=1, source_target_pairs={{0,48},{8,56},{16,0},{24,8},{32,16},{40,24},{48,32},{56,40},{64,11... | collective-permute-start | bytes 1376264 | tf_op jit(solution)/shard_map/ppermute | solution.py:53
  216.5 29.2 %collective-permute-start.27 = (bf16[256,1024]{1,0:T(8,128)(2,1)S(1)}, bf16[256,1024]{1,0:T(8,128)(2,1)S(1)}, u32[]{:S(2)}, u32[]{:S(2)}) collective-permute-start(bf16[256,1024]{1,0:T(8,128)(2,1)S(1)} %get-tuple-element.261), channel_id=1, source_target_pairs={{0,48},{8,56},{16,0},{24,8},{32,16},{40,24},{48,32},{56,40},{64,11... | collective-permute-start | bytes 1572872 | tf_op jit(solution)/shard_map/ppermute | solution.py:53
  218.5 27.3 %collective-permute-start.28 = (bf16[256,1024]{1,0:T(8,128)(2,1)S(1)}, bf16[256,1024]{1,0:T(8,128)(2,1)S(1)}, u32[]{:S(2)}, u32[]{:S(2)}) collective-permute-start(bf16[256,1024]{1,0:T(8,128)(2,1)S(1)} %get-tuple-element.260), channel_id=1, source_target_pairs={{0,16},{8,24},{16,32},{24,40},{32,48},{40,56},{48,0},{56,8},{64,80... | collective-permute-start | bytes 1572872 | tf_op jit(solution)/shard_map/ppermute | solution.py:53
  218.6 27.3 %collective-permute-start.29 = (bf16[256,1024]{1,0:T(8,128)(2,1)S(1)}, bf16[256,1024]{1,0:T(8,128)(2,1)S(1)}, u32[]{:S(2)}, u32[]{:S(2)}) collective-permute-start(bf16[256,1024]{1,0:T(8,128)(2,1)S(1)} %get-tuple-element.259), channel_id=1, source_target_pairs={{0,32},{8,40},{16,48},{24,56},{32,0},{40,8},{48,16},{56,24},{64,96... | collective-permute-start | bytes 1572872 | tf_op jit(solution)/shard_map/ppermute | solution.py:53
  250.3 29.7 %collective-permute-start.34 = (bf16[8,224,1024]{2,1,0:T(8,128)(2,1)}, bf16[8,224,1024]{2,1,0:T(8,128)(2,1)}, u32[]{:S(2)}, u32[]{:S(2)}) collective-permute-start(bf16[8,224,1024]{2,1,0:T(8,128)(2,1)} %get-tuple-element.187), channel_id=1, source_target_pairs={{0,8},{8,0},{16,24},{24,16},{32,40},{40,32},{48,56},{56,48},{64,72... | collective-permute-start | bytes 11010056 | tf_op jit(solution)/shard_map/ppermute | solution.py:57
  318.4 47.7 %all-to-all-start.4 = ((bf16[8,128,1152]{2,1,0:T(8,128)(2,1)}), bf16[8,128,1152]{2,1,0:T(8,128)(2,1)S(1)}, u32[]{:S(2)}, u32[]{:S(2)}) async-start(bf16[8,128,1152]{2,1,0:T(8,128)(2,1)} %shard_map.186), calls=%async_computation.4 | async-start | bytes 4718592 | tf_op jit(solution)/shard_map/all_to_all | solution.py:853
  323.5 49.4 %collective-permute-start.37 = (bf16[2,224,1024]{2,1,0:T(8,128)(2,1)}, bf16[2,224,1024]{2,1,0:T(8,128)(2,1)}, u32[]{:S(2)}, u32[]{:S(2)}) collective-permute-start(bf16[2,224,1024]{2,1,0:T(8,128)(2,1)} %get-tuple-element.212), channel_id=1, source_target_pairs={{0,48},{8,56},{16,0},{24,8},{32,16},{40,24},{48,32},{56,40},{64,11... | collective-permute-start | bytes 2752520 | tf_op jit(solution)/shard_map/ppermute | solution.py:53
  324.4 48.4 %collective-permute-start.38 = (bf16[2,224,1024]{2,1,0:T(8,128)(2,1)}, bf16[2,224,1024]{2,1,0:T(8,128)(2,1)}, u32[]{:S(2)}, u32[]{:S(2)}) collective-permute-start(bf16[2,224,1024]{2,1,0:T(8,128)(2,1)} %get-tuple-element.213), channel_id=1, source_target_pairs={{0,16},{8,24},{16,32},{24,40},{32,48},{40,56},{48,0},{56,8},{64,80... | collective-permute-start | bytes 2752520 | tf_op jit(solution)/shard_map/ppermute | solution.py:53
  325.5 47.4 %collective-permute-start.39 = (bf16[2,224,1024]{2,1,0:T(8,128)(2,1)}, bf16[2,224,1024]{2,1,0:T(8,128)(2,1)}, u32[]{:S(2)}, u32[]{:S(2)}) collective-permute-start(bf16[2,224,1024]{2,1,0:T(8,128)(2,1)} %get-tuple-element.214), channel_id=1, source_target_pairs={{0,32},{8,40},{16,48},{24,56},{32,0},{40,8},{48,16},{56,24},{64,96... | collective-permute-start | bytes 2752520 | tf_op jit(solution)/shard_map/ppermute | solution.py:53
  385.1 27.2 %collective-permute-start.42 = (bf16[240,1024]{1,0:T(8,128)(2,1)}, bf16[240,1024]{1,0:T(8,128)(2,1)}, u32[]{:S(2)}, u32[]{:S(2)}) collective-permute-start(bf16[240,1024]{1,0:T(8,128)(2,1)} %get-tuple-element.227), channel_id=1, source_target_pairs={{0,48},{8,56},{16,0},{24,8},{32,16},{40,24},{48,32},{56,40},{64,11... | collective-permute-start | bytes 1474568 | tf_op jit(solution)/shard_map/ppermute | solution.py:53
  387.2 27.2 %collective-permute-start.44 = (bf16[240,1024]{1,0:T(8,128)(2,1)}, bf16[240,1024]{1,0:T(8,128)(2,1)}, u32[]{:S(2)}, u32[]{:S(2)}) collective-permute-start(bf16[240,1024]{1,0:T(8,128)(2,1)} %get-tuple-element.229), channel_id=1, source_target_pairs={{0,32},{8,40},{16,48},{24,56},{32,0},{40,8},{48,16},{56,24},{64,96... | collective-permute-start | bytes 1474568 | tf_op jit(solution)/shard_map/ppermute | solution.py:53
  390.4 29.5 %collective-permute-start.41 = (bf16[224,1024]{1,0:T(8,128)(2,1)}, bf16[224,1024]{1,0:T(8,128)(2,1)}, u32[]{:S(2)}, u32[]{:S(2)}) collective-permute-start(bf16[224,1024]{1,0:T(8,128)(2,1)} %fusion.30), channel_id=1, source_target_pairs={{0,64},{8,72},{16,80},{24,88},{32,96},{40,104},{48,112},{56,120},{... | collective-permute-start | bytes 1376264 | tf_op jit(solution)/shard_map/ppermute | solution.py:53
  403.3 38.0 %all-to-all-start.5 = ((bf16[128,8,256]{2,1,0:T(8,128)(2,1)}), bf16[128,8,256]{2,1,0:T(8,128)(2,1)S(1)}, u32[]{:S(2)}, u32[]{:S(2)}) async-start(bf16[128,8,256]{2,1,0:T(8,128)(2,1)} %bitcast.172), calls=%async_computation.6 | async-start | bytes 1048576 | tf_op jit(solution)/shard_map/all_to_all | solution.py:868
  409.4 28.5 %collective-permute-start.46 = (bf16[240,1024]{1,0:T(8,128)(2,1)}, bf16[240,1024]{1,0:T(8,128)(2,1)}, u32[]{:S(2)}, u32[]{:S(2)}) collective-permute-start(bf16[240,1024]{1,0:T(8,128)(2,1)} %get-tuple-element.236), channel_id=1, source_target_pairs={{0,48},{8,56},{16,0},{24,8},{32,16},{40,24},{48,32},{56,40},{64,11... | collective-permute-start | bytes 1474568 | tf_op jit(solution)/shard_map/ppermute | solution.py:53
  412.3 28.9 %collective-permute-start.47 = (bf16[240,1024]{1,0:T(8,128)(2,1)}, bf16[240,1024]{1,0:T(8,128)(2,1)}, u32[]{:S(2)}, u32[]{:S(2)}) collective-permute-start(bf16[240,1024]{1,0:T(8,128)(2,1)} %get-tuple-element.237), channel_id=1, source_target_pairs={{0,16},{8,24},{16,32},{24,40},{32,48},{40,56},{48,0},{56,8},{64,80... | collective-permute-start | bytes 1474568 | tf_op jit(solution)/shard_map/ppermute | solution.py:53
  412.3 28.9 %collective-permute-start.48 = (bf16[240,1024]{1,0:T(8,128)(2,1)}, bf16[240,1024]{1,0:T(8,128)(2,1)}, u32[]{:S(2)}, u32[]{:S(2)}) collective-permute-start(bf16[240,1024]{1,0:T(8,128)(2,1)} %get-tuple-element.238), channel_id=1, source_target_pairs={{0,32},{8,40},{16,48},{24,56},{32,0},{40,8},{48,16},{56,24},{64,96... | collective-permute-start | bytes 1474568 | tf_op jit(solution)/shard_map/ppermute | solution.py:53
  (68 other events, 787.0 us)
Sparse Core Ops, SparseCore 0:
  29.1 40.6 all-gather.4
  85.8 50.9 all-gather.6
  280.2 87.0 reduce-scatter.1
